TPU v7x, 32 devices: a whole 2x2x4 slice. The times are simulated.
32 devices in a mesh: pair: 8 (over y, x, core), slab: 4 (over z).
Axes of the slice: x: 2, y: 2, z: 4, core: 2. Of those that a mesh axis runs over, the one named last changes fastest.
Arguments:
- amplitudes: bfloat16 [1536, 9216], P('pair', 'slab'), may hold values from -6 to 6
- integrals: bfloat16 [9216, 9216], P('slab', 'pair'), may hold values from -0.09375 to 0.09375
- pair_index: int32 [1536, 2], P('pair'), may hold values from 0 to 159, as said below
- eps_occ: float32 [160], replicated, may hold values from -2 to -0.5
- eps_vir: float32 [96], replicated, may hold values from 0.5 to 3
Outputs:
- update: float32 [1536, 9216], P('pair', 'slab')
Inputs may be any that keep to these rules, and one draw needn't show every extreme that they name: `pair_index`: each row holds i < j; pairs may repeat; pair 0 is (0, 159).
All inputs are finite; a program needn't handle non-finite values.
Results may differ from a plain program's by a relative error of at most 0.0003.
Values may be sent and summed in bfloat16 or wider, within the bound.
No kernel may reach another device: no remote copies, remote signals or barrier semaphores. Data moves between devices by JAX's collectives and lax.ppermute only.
A program may use at most 128 MiB of HBM per device.

v0:
```python
import jax
import jax.numpy as jnp
from jax import lax
from jax.sharding import PartitionSpec as P


def on_device(amplitudes, integrals, pair_index, eps_occ, eps_vir):
    num_pairs = amplitudes.shape[0]
    vir_count = eps_vir.shape[0]
    owned_rows = jnp.dot(
        lax.all_gather(amplitudes, "pair", axis=0, tiled=True),
        integrals,
        preferred_element_type=jnp.float32,
    )
    ladder = lax.all_to_all(owned_rows, "pair", split_axis=0, concat_axis=1, tiled=True)
    ladder_cube = ladder.reshape(num_pairs, vir_count, vir_count)
    antisym = (ladder_cube - jnp.swapaxes(ladder_cube, 1, 2)).reshape(
        num_pairs, vir_count * vir_count
    )
    summed = lax.psum_scatter(antisym, "slab", scatter_dimension=1, tiled=True)
    col_count = summed.shape[1]
    column_ids = lax.axis_index("slab") * col_count + jnp.arange(col_count, dtype=jnp.int32)
    vir_ids = jnp.arange(vir_count, dtype=jnp.int32)
    eps_first = jnp.sum(
        jnp.where((column_ids // vir_count)[:, None] == vir_ids[None, :], eps_vir[None, :], 0.0),
        axis=1,
    )
    eps_second = jnp.sum(
        jnp.where((column_ids % vir_count)[:, None] == vir_ids[None, :], eps_vir[None, :], 0.0),
        axis=1,
    )
    occ_ids = jnp.arange(eps_occ.shape[0], dtype=jnp.int32)
    eps_iocc = jnp.sum(
        jnp.where(pair_index[:, 0:1] == occ_ids[None, :], eps_occ[None, :], 0.0), axis=1
    )
    eps_jocc = jnp.sum(
        jnp.where(pair_index[:, 1:2] == occ_ids[None, :], eps_occ[None, :], 0.0), axis=1
    )
    denominator = (eps_iocc + eps_jocc)[:, None] - (eps_first + eps_second)[None, :]
    return summed / denominator


def solution(mesh):
    in_specs = (P("pair", "slab"), P("slab", "pair"), P("pair", None), P(), P())
    out_specs = P("pair", "slab")
    return jax.shard_map(
        on_device, mesh=mesh, in_specs=in_specs, out_specs=out_specs, check_vma=False
    )
```

profile of v0, /device:TPU:0, one launch (start us, length us, event | category | flops | bytes accessed | tf_op | source)
XLA Modules:
  0.0 338.0 jit_solution(2965043175742217499)
XLA Ops:
  6.5 0.0 all-gather.2.cloned.1.call-start
  6.5 0.7 all-gather.2.cloned.1.call-update
  7.3 0.0 reduce-scatter.2.cloned.1.call-start
  7.3 53.5 %all-gather.2.cloned.1.call-done = bf16[1536,2304]{1,0:T(8,128)(2,1)} async-done(((bf16[192,2304]{1,0:T(8,128)(2,1)}), bf16[1536,2304]{1,0:T(8,128)(2,1)}) %all-gather.2.cloned.1.call-update) | async-done | bytes 7077904 | tf_op jit(solution)/shard_map/all_gather | solution.py:11
  60.8 13.1 %fusion.6 = f32[1536,1152]{1,0:T(8,128)S(1)} fusion(bf16[1536,2304]{1,0:T(8,128)(2,1)} %all-gather.2.cloned.1.call-done, bf16[2304,1152]{1,0:T(8,128)(2,1)} %param.6), kind=kOutput, calls=%fused_computation.20 | convolution fusion | flops 8153726976 | bytes 19464192 | tf_op jit(solution)/shard_map/dot_general | solution.py:10
  73.9 82.5 %all_to_all.16 = f32[8,192,1152]{2,1,0:T(8,128)S(1)} all-to-all(f32[8,192,1152]{2,1,0:T(8,128)S(1)} %bitcast.9), channel_id=1, replica_groups=mesh['pair'=8,'slab'=4] {'pair'}, dimensions={0} | all-to-all | bytes 14155776 | tf_op jit(solution)/shard_map/all_to_all | solution.py:15
  156.4 6.9 %copy.11 = f32[192,8,1152]{2,1,0:T(8,128)} copy(f32[192,8,1152]{2,0,1:T(8,128)S(1)} %bitcast.8) | data formatting | bytes 14155776 | tf_op jit(solution)/shard_map/all_to_all | solution.py:15
  163.3 10.2 %reshape.40 = f32[192,96,96]{2,1,0:T(8,128)} reshape(f32[192,8,1152]{2,1,0:T(8,128)} %copy.11) | data formatting | bytes 14155776 | tf_op jit(solution)/shard_map/reshape | solution.py:16
  173.5 9.6 %copy.12 = f32[192,96,96]{1,2,0:T(8,128)} copy(f32[192,96,96]{2,1,0:T(8,128)} %reshape.40) | data formatting | bytes 14155776 | tf_op jit(solution)/shard_map/reshape | solution.py:16
  183.1 12.2 %bitcast_subtract_fusion = f32[192,96,96]{2,1,0:T(8,128)} fusion(f32[192,96,96]{2,1,0:T(8,128)} %reshape.40, f32[192,96,96]{1,2,0:T(8,128)} %copy.12), kind=kLoop, calls=%fused_computation | loop fusion | flops 1769472 | bytes 21233664 | tf_op jit(solution)/shard_map/sub | solution.py:17
  195.3 10.0 %reshape.41 = f32[192,9216]{1,0:T(8,128)} reshape(f32[192,96,96]{2,1,0:T(8,128)} %bitcast_subtract_fusion) | data formatting | bytes 14155776 | tf_op jit(solution)/shard_map/reshape | solution.py:17
  205.3 0.0 copy-start.2
  205.3 0.0 copy-start
  205.3 0.0 copy-start.1
  205.4 0.0 reduce-scatter.2.cloned.1.call-update
  205.4 0.6 copy-done.2
  206.0 0.3 select_reduce_fusion
  206.4 0.0 copy-done
  206.4 0.0 copy-done.1
  206.4 0.1 select_reduce_fusion.2
  206.5 121.6 %reduce-scatter.2.cloned.1.call-done = f32[192,2304]{1,0:T(8,128)} async-done(((f32[192,9216]{1,0:T(8,128)}), f32[192,2304]{1,0:T(8,128)}) %reduce-scatter.2.cloned.1.call-update) | async-done | bytes 1769488 | tf_op jit(solution)/shard_map/reduce_scatter | solution.py:20
  328.1 3.0 subtract_divide_fusion
  (4 shorter events, 0.0 us)
Async XLA Ops:
  6.5 54.3 %all-gather.2.cloned.1.call-start = ((), (), s32[]{:S(2)}) async-start(), calls=%async_computation.2 | async-start | bytes 7962624 | tf_op jit(solution)/shard_map/all_gather | solution.py:11
  7.3 320.9 %reduce-scatter.2.cloned.1.call-start = ((), (), s32[]{:S(2)}) async-start(), calls=%async_computation.3 | async-start | bytes 8847360 | tf_op jit(solution)/shard_map/reduce_scatter | solution.py:20
  205.3 0.7 copy-start.2
  205.3 1.0 copy-start
  205.3 1.0 copy-start.1
Sparse Core Ops, SparseCore 0:
  9.2 51.5 all-gather.1
  205.5 122.5 reduce-scatter.1
where the time goes:
time: 339 us; the launch traced here: 338 us
  waiting for transfers between devices  176 us (52%)
  blocking collectives  82.5 us (24%)
  local copies, waits for them, and re-layouts  37.4 us (11%)
  other arithmetic  15.7 us (5%)
  between operations  13.5 us (4%)
  matrix products  13.1 us (4%)
    reduce_scatter x1, waiting for transfers between devices, on_device(): summed = lax.psum_scatter(antisym, 'slab', scatter_dimension=1, tiled=True)  122 us
    all_to_all x1, blocking collectives, on_device(): lax.all_to_all(owned_rows, 'pair', split_axis=0, concat_axis=1, tiled=True)  82.5 us
    all_gather x1, waiting for transfers between devices, on_device(): lax.all_gather(amplitudes, 'pair', axis=0, tiled=True)  53.5 us
    reshape x2, local copies, waits for them, and re-layouts, on_device(): ladder_cube = ladder.reshape(num_pairs, vir_count, vir_count)  19.8 us
    dot_general x1, matrix products, on_device(): jnp.dot(lax.all_gather(amplitudes, 'pair', axis=0, tiled=True), integrals...  13.1 us
    sub x1, other arithmetic, on_device(): ladder_cube - jnp.swapaxes(ladder_cube, 1, 2)  12.2 us
    reshape x1, local copies, waits for them, and re-layouts, on_device(): (ladder_cube - jnp.swapaxes(ladder_cube, 1, 2)).reshape(num_pairs, vir_co...  10 us
    all_to_all x1, local copies, waits for them, and re-layouts, on_device(): lax.all_to_all(owned_rows, 'pair', split_axis=0, concat_axis=1, tiled=True)  6.93 us
  transfers between devices with their start and end apart: 2, of which 2 were waited for; matrix products, arithmetic and copies ran while one was open for 0% of the time, Pallas kernels for 0%

commit v1 on v0

v1 whole, which is shorter than its diff:
```python
import functools

import jax
import jax.numpy as jnp
from jax import lax
from jax.experimental import pallas as pl
from jax.experimental.pallas import tpu as pltpu
from jax.sharding import PartitionSpec as P

CORES = 2
WIDTH = 64
TAIL = 16
VMEM = 48 * 1024 * 1024
NT = (((1,), (1,)), ((), ()))


def tile_of(rows, most):
    return max(t for t in range(16, most + 1, 16) if rows % t == 0)


def power_of(peak):
    return jnp.ceil(jnp.log2(jnp.maximum(peak, 1e-30) * (1.0 / 32760.0)))


def to_codes(values, inverse):
    return jnp.round(values * inverse).astype(jnp.int32).astype(jnp.int16)


def from_codes(codes):
    return codes.astype(jnp.int32).astype(jnp.float32)


def put_power(out_ref, rows, power):
    wide = jnp.broadcast_to(power.astype(jnp.int32), (TAIL, power.shape[1]))
    out_ref[pl.ds(rows, TAIL), :] = wide.astype(jnp.int16)


def scale_in(ref, rows):
    return jnp.exp2(from_codes(ref[pl.ds(rows, TAIL), :])[0:1, :])


def rows_at(i, tile):
    return pl.ds(pl.multiple_of(i * tile, tile), tile)


def ladder_kernel(chips, it_ref, *refs):
    own, sib = refs[:chips], refs[chips : 2 * chips]
    outs = refs[2 * chips : 3 * chips]
    rhs, acc = refs[3 * chips :]
    rows = it_ref.shape[0]
    width = own[0].shape[0]
    lanes = 2 * width
    tile = tile_of(rows, 384)
    small = tile_of(rows, 96)
    for d in range(0, chips, 2):
        for k, ref in enumerate((own[d], sib[d], own[d + 1], sib[d + 1])):
            rhs[pl.ds(k * width, width), :] = ref[...]

        def multiply(i, peak):
            part = lax.dot_general(
                it_ref[rows_at(i, tile), :], rhs[...], NT, preferred_element_type=jnp.float32
            )
            acc[rows_at(i, tile), :] = part
            return jnp.maximum(peak, jnp.max(jnp.abs(part), axis=0, keepdims=True))

        peak = lax.fori_loop(0, rows // tile, multiply, jnp.zeros((1, 2 * lanes), jnp.float32))
        power = power_of(peak)
        inverse = jnp.exp2(-power)

        def code(i, carry):
            at = rows_at(i, small)
            codes = to_codes(acc[at, :], inverse)
            outs[d][at, :] = codes[:, :lanes]
            outs[d + 1][at, :] = codes[:, lanes:]
            return carry

        lax.fori_loop(0, rows // small, code, 0)
        put_power(outs[d], rows, power[:, :lanes])
        put_power(outs[d + 1], rows, power[:, lanes:])


def antisym_kernel(chips, slabs, vir, place_ref, *refs):
    own, sib = refs[:chips], refs[chips : 2 * chips]
    anti, right, left, cube = refs[2 * chips :]
    chip, core = place_ref[0], place_ref[1]
    lanes = cube.shape[1]
    rows = own[0].shape[0] - TAIL
    held = rows // vir
    small = tile_of(rows, 96)
    for d in range(chips):
        block = (chip ^ d) * CORES
        for ref, owner, turned in ((own[d], block + core, False), (sib[d], block + 1 - core, True)):
            scale = scale_in(ref, rows)
            base = owner * rows

            def spread(i, carry, ref=ref, base=base, scale=scale, turned=turned):
                values = from_codes(ref[rows_at(i, small), :]) * scale
                if turned:
                    values = pltpu.roll(values, lanes // 2, 1)
                cube[pl.ds(pl.multiple_of(base + i * small, small), small), :] = values
                return carry

            lax.fori_loop(0, rows // small, spread, 0)
    blocks = vir // slabs // (CORES * held)
    for s in range(slabs):
        peak = jnp.zeros((1, lanes), jnp.float32)
        for blk in range(blocks):
            first = s * (vir // slabs) + blk * CORES * held + core * held

            def subtract(k, peak, s=s, blk=blk, first=first):
                a = first + k
                here = cube[pl.ds(pl.multiple_of(a * vir, vir), vir), :]
                there = cube[pl.ds(a, vir, stride=vir), :]
                both = here - there
                anti[s, pl.ds(pl.multiple_of((blk * held + k) * vir, vir), vir), :] = both
                return jnp.maximum(peak, jnp.max(jnp.abs(both), axis=0, keepdims=True))

            peak = lax.fori_loop(0, held, subtract, peak)
        for out, which in ((right, slabs - 1), (left, 0)):
            if s == which:
                code_rows(lambda at: anti[which, at, :], out, peak, anti.shape[1])


def code_rows(read, out, peak, rows):
    small = tile_of(rows, 96)
    power = power_of(peak)
    inverse = jnp.exp2(-power)

    def code(i, carry):
        at = rows_at(i, small)
        out[at, :] = to_codes(read(at), inverse)
        return carry

    lax.fori_loop(0, rows // small, code, 0)
    put_power(out, rows, power)


def hop_kernel(place_ref, anti_r, anti_l, got_r, got_l, out_r, out_l, total):
    rows, lanes = total.shape
    small = tile_of(rows, 96)
    for anti, got, out in ((anti_r, got_r, out_r), (anti_l, got_l, out_l)):
        scale = scale_in(got, rows)

        def add(i, peak, anti=anti, got=got, scale=scale):
            at = rows_at(i, small)
            values = anti[0, at, :] + from_codes(got[at, :]) * scale
            total[at, :] = values
            return jnp.maximum(peak, jnp.max(jnp.abs(values), axis=0, keepdims=True))

        peak = lax.fori_loop(0, rows // small, add, jnp.zeros((1, lanes), jnp.float32))
        code_rows(lambda at: total[at, :], out, peak, rows)


def finish_kernel(place_ref, anti, got_r, got_l, pair_ref, vir_ref, own_ref, sib_ref):
    rows = vir_ref.shape[0]
    width = own_ref.shape[0]
    total = anti[0] + (
        from_codes(got_r[pl.ds(0, rows), :]) * scale_in(got_r, rows)
        + from_codes(got_l[pl.ds(0, rows), :]) * scale_in(got_l, rows)
    )
    update = (total / (pair_ref[...] - vir_ref[...])).T
    own_ref[...] = update[:width]
    sib_ref[...] = update[width:]


def whole(shape):
    return pl.BlockSpec(shape, lambda i, place: (0,) * len(shape))


def on_device(mesh, amplitudes, integrals, pair_index, eps_occ, eps_vir):
    devices, slabs = mesh.shape["pair"], mesh.shape["slab"]
    chips = devices // CORES
    num_pairs, depth = amplitudes.shape
    rows = integrals.shape[1]
    vir = eps_vir.shape[0]
    held = rows // vir
    lanes = CORES * WIDTH
    chunks = num_pairs // WIDTH
    part_rows = vir // slabs // CORES * vir
    me, z = lax.axis_index("pair"), lax.axis_index("slab")
    chip, core = me // CORES, me % CORES

    def to_chip(x, d):
        return lax.ppermute(x, "pair", [(i, i ^ (d * CORES)) for i in range(devices)])

    def to_core(x):
        return lax.ppermute(x, "pair", [(i, i ^ 1) for i in range(devices)])

    params = pltpu.CompilerParams(vmem_limit_bytes=VMEM)
    message = jax.ShapeDtypeStruct((rows + TAIL, lanes), jnp.int16)
    part_message = jax.ShapeDtypeStruct((part_rows + TAIL, lanes), jnp.int16)
    part_shape = (part_rows + TAIL, lanes)
    smem = pl.BlockSpec(memory_space=pltpu.SMEM)

    ladder = pl.pallas_call(
        functools.partial(ladder_kernel, chips),
        out_shape=[message] * chips,
        scratch_shapes=[
            pltpu.VMEM((2 * lanes, depth), jnp.bfloat16),
            pltpu.VMEM((rows, 2 * lanes), jnp.float32),
        ],
        compiler_params=params,
        cost_estimate=pl.CostEstimate(
            flops=2 * rows * depth * chips * lanes,
            bytes_accessed=2 * (rows + chips * lanes) * depth + 2 * chips * rows * lanes,
            transcendentals=0,
        ),
        name="ladder",
    )
    antisym = pl.pallas_call(
        functools.partial(antisym_kernel, chips, slabs, vir),
        in_specs=[smem] + [pl.BlockSpec(memory_space=pltpu.VMEM)] * (2 * chips),
        out_shape=[
            jax.ShapeDtypeStruct((slabs, part_rows, lanes), jnp.float32),
            part_message,
            part_message,
        ],
        scratch_shapes=[pltpu.VMEM((vir * vir, lanes), jnp.float32)],
        compiler_params=params,
        cost_estimate=pl.CostEstimate(
            flops=8 * vir * vir * lanes, bytes_accessed=8 * vir * vir * lanes, transcendentals=0
        ),
        name="antisym",
    )

    def slab_block(k):
        return pl.BlockSpec((1, part_rows, lanes), lambda i, place: (place[k], 0, 0))

    hop = pl.pallas_call(
        hop_kernel,
        grid_spec=pltpu.PrefetchScalarGridSpec(
            num_scalar_prefetch=1,
            grid=(1,),
            in_specs=[slab_block(0), slab_block(1), whole(part_shape), whole(part_shape)],
            out_specs=[whole(part_shape), whole(part_shape)],
            scratch_shapes=[pltpu.VMEM((part_rows, lanes), jnp.float32)],
        ),
        out_shape=[part_message, part_message],
        compiler_params=params,
        cost_estimate=pl.CostEstimate(
            flops=16 * part_rows * lanes, bytes_accessed=16 * part_rows * lanes, transcendentals=0
        ),
        name="hop",
    )
    finish = pl.pallas_call(
        finish_kernel,
        grid_spec=pltpu.PrefetchScalarGridSpec(
            num_scalar_prefetch=1,
            grid=(1,),
            in_specs=[
                slab_block(0),
                whole(part_shape),
                whole(part_shape),
                whole((1, lanes)),
                whole((part_rows, 1)),
            ],
            out_specs=[whole((WIDTH, part_rows))] * 2,
        ),
        out_shape=[jax.ShapeDtypeStruct((WIDTH, part_rows), jnp.float32)] * 2,
        compiler_params=params,
        cost_estimate=pl.CostEstimate(
            flops=16 * part_rows * lanes, bytes_accessed=12 * part_rows * lanes, transcendentals=0
        ),
        name="finish",
    )

    integrals_t = integrals.T

    occ_ids = jnp.arange(eps_occ.shape[0], dtype=jnp.int32)

    def pick(ids):
        return jnp.sum(jnp.where(ids[:, None] == occ_ids[None, :], eps_occ[None, :], 0.0), axis=1)

    eps_pair = pick(pair_index[:, 0]) + pick(pair_index[:, 1])
    eps_pair = eps_pair.reshape(chunks, 1, WIDTH)
    eps_pair = jnp.concatenate([eps_pair, to_core(eps_pair)], axis=2)
    blocks = vir // slabs // (CORES * held)
    eps_grid = eps_vir.reshape(slabs, blocks, CORES, held)
    eps_mine = lax.dynamic_slice(eps_grid, (z, 0, core, 0), (1, blocks, 1, held)).reshape(-1)
    eps_virt = (eps_mine[:, None] + eps_vir[None, :]).reshape(part_rows, 1)

    place = jnp.stack([chip, core]).astype(jnp.int32)

    gathered = []
    last = None
    for r in range(chunks):
        mine = amplitudes[r * WIDTH : (r + 1) * WIDTH]
        if last is not None:
            mine, last = lax.optimization_barrier((mine, last))
            gathered[-1] = gathered[-1][:1] + list(last)
        got = [to_chip(mine, d) for d in range(1, chips)]
        last = tuple(got)
        gathered.append([mine] + got)

    halves = []
    for r in range(chunks):
        sib = [to_core(x) for x in gathered[r]]
        sums = ladder(integrals_t, *gathered[r], *sib)
        arrived = [sums[0]] + [to_chip(sums[d], d) for d in range(1, chips)]
        twins = [to_core(x) for x in arrived]
        anti, right, left = antisym(place, *arrived, *twins)
        for step in range(1, slabs):
            ahead = slabs - step
            if step > 1:
                targets = jnp.clip(jnp.stack([z + ahead, z - ahead]), 0, slabs - 1)
                right, left = hop(targets.astype(jnp.int32), anti, anti, right, left)
            right, left = (
                lax.ppermute(right, "slab", [(i, i + 1) for i in range(step)]),
                lax.ppermute(
                    left, "slab", [(i, i - 1) for i in range(slabs - step, slabs)]
                ),
            )
        own, other = finish(z[None].astype(jnp.int32), anti, right, left, eps_pair[r], eps_virt)
        other = to_core(other)
        first = jnp.where(core == 0, own, other).reshape(WIDTH, blocks, 1, held * vir)
        second = jnp.where(core == 0, other, own).reshape(WIDTH, blocks, 1, held * vir)
        halves.append(jnp.concatenate([first, second], axis=2).reshape(WIDTH, CORES * part_rows))
    return jnp.concatenate(halves, axis=0)


def solution(mesh):
    in_specs = (P("pair", "slab"), P("slab", "pair"), P("pair", None), P(), P())
    out_specs = P("pair", "slab")
    return jax.shard_map(
        functools.partial(on_device, mesh),
        mesh=mesh,
        in_specs=in_specs,
        out_specs=out_specs,
        check_vma=False,
    )
```

time: 339 us -> 245 us (0.72)
  waiting for transfers between devices: 176 us -> 55.9 us
  blocking collectives: 82.5 us -> 0 us
  Pallas kernels: 0 us -> 68.3 us
  starting transfers between devices: 0.04 us -> 68 us
  matrix products: 13.1 us -> 0 us
  between operations: 13.5 us -> 0.68 us
  other arithmetic: 15.7 us -> 3.88 us
  local copies, waits for them, and re-layouts: 37.4 us -> 46.9 us
    reduce_scatter x1 -> x0, waiting for transfers between devices: 122 us -> none  [on_device(): summed = lax.psum_scatter(antisym, 'slab', scatter_dimension=1, tiled=True)]
    all_to_all x1 -> x0, blocking collectives: 82.5 us -> none  [on_device(): lax.all_to_all(owned_rows, 'pair', split_axis=0, concat_axis=1, tiled=True)]
    pallas_call x0 -> x15, Pallas kernels: none -> 68.3 us  [the longest x3 26.8 us: on_device(): anti, right, left = antisym(place, *arrived, *twins)]
    ppermute x0 -> x64, starting transfers between devices: none -> 68 us  [the longest x9 30.6 us: on_device(): lax.ppermute(right, 'slab', [(i, i + 1) for i in range(step)])]
    ppermute x0 -> x64, waiting for transfers between devices: none -> 55.9 us  [the longest x18 51.2 us: to_chip(): return lax.ppermute(x, 'pair', [(i, i ^ d * CORES) for i in range(devices)])]
    all_gather x1 -> x0, waiting for transfers between devices: 53.5 us -> none  [on_device(): lax.all_gather(amplitudes, 'pair', axis=0, tiled=True)]
    unnamed x6 -> x126, local copies, waits for them, and re-layouts: 0.6 us -> 39.9 us
    reshape x3 -> x1, local copies, waits for them, and re-layouts: 29.8 us -> 1.32 us  [on_device(): eps_grid = eps_vir.reshape(slabs, blocks, CORES, held)]
  transfers between devices with their start and end apart: 2 -> 64, of which waited for: 2 -> 12; matrix products, arithmetic and copies ran while one was open for 0% -> 7% of each run, Pallas kernels for 0% -> 28%
where the time goes in v1:
time: 245 us; the launch traced here: 244 us
  Pallas kernels  68.3 us (28%)
  starting transfers between devices  68 us (28%)
  waiting for transfers between devices  55.9 us (23%)
  local copies, waits for them, and re-layouts  46.9 us (19%)
  other arithmetic  3.88 us (2%)
    ppermute x18, waiting for transfers between devices, to_chip(): return lax.ppermute(x, 'pair', [(i, i ^ d * CORES) for i in range(devices)])  51.2 us
    unnamed x126, local copies, waits for them, and re-layouts  39.9 us
    ppermute x9, starting transfers between devices, on_device(): lax.ppermute(right, 'slab', [(i, i + 1) for i in range(step)])  30.6 us
    pallas_call x3, Pallas kernels, on_device(): anti, right, left = antisym(place, *arrived, *twins)  26.8 us
    pallas_call x3, Pallas kernels, on_device(): sums = ladder(integrals_t, *gathered[r], *sib)  22.4 us
    ppermute x18, starting transfers between devices, to_chip(): return lax.ppermute(x, 'pair', [(i, i ^ d * CORES) for i in range(devices)])  22.2 us
    pallas_call x6, Pallas kernels, on_device(): right, left = hop(targets.astype(jnp.int32), anti, anti, right, left)  15 us
    ppermute x9, starting transfers between devices, on_device(): lax.ppermute(left, 'slab', [(i, i - 1) for i in range(slabs - step, slabs)])  10.4 us
  transfers between devices with their start and end apart: 64, of which 12 were waited for; matrix products, arithmetic and copies ran while one was open for 7% of the time, Pallas kernels for 28%

profile of v1, /device:TPU:0, one launch (start us, length us, event | category | flops | bytes accessed | tf_op | source)
XLA Modules:
  0.0 243.7 jit_solution(15913352909825975136)
XLA Ops:
  1.2 3.0 %collective-permute-start = (bf16[64,2304]{1,0:T(8,128)(2,1)S(1)}, bf16[64,2304]{1,0:T(8,128)(2,1)S(1)}, u32[]{:S(2)}, u32[]{:S(2)}) collective-permute-start(bf16[64,2304]{1,0:T(8,128)(2,1)S(1)} %get-tuple-element.101.refs_0_), channel_id=1, source_target_pairs={{0,8},{4,12},{8,0},{12,4},{16,24},{20,28},{24,16},{28,20},{1,9},{5... | collective-permute-start | bytes 884744 | tf_op jit(solution)/shard_map/ppermute | solution.py:184
  4.2 1.5 collective-permute-start.1
  5.7 6.3 %collective-permute-done.refs_1_ = bf16[64,2304]{1,0:T(8,128)(2,1)S(1)} collective-permute-done((bf16[64,2304]{1,0:T(8,128)(2,1)S(1)}, bf16[64,2304]{1,0:T(8,128)(2,1)S(1)}, u32[]{:S(2)}, u32[]{:S(2)}) %collective-permute-start) | collective-permute-done | bytes 294944 | tf_op jit(solution)/shard_map/ppermute | solution.py:184
  12.0 7.0 %collective-permute-done.1.refs_2_ = bf16[64,2304]{1,0:T(8,128)(2,1)S(1)} collective-permute-done((bf16[64,2304]{1,0:T(8,128)(2,1)S(1)}, bf16[64,2304]{1,0:T(8,128)(2,1)S(1)}, u32[]{:S(2)}, u32[]{:S(2)}) %collective-permute-start.1) | collective-permute-done | bytes 294944 | tf_op jit(solution)/shard_map/ppermute | solution.py:184
  21.1 1.4 collective-permute-start.24
  23.1 5.9 %collective-permute-done.22.refs_1_ = bf16[64,2304]{1,0:T(8,128)(2,1)S(1)} collective-permute-done((bf16[64,2304]{1,0:T(8,128)(2,1)S(1)}, bf16[64,2304]{1,0:T(8,128)(2,1)S(1)}, u32[]{:S(2)}, u32[]{:S(2)}) %collective-permute-start.22) | collective-permute-done | bytes 294944 | tf_op jit(solution)/shard_map/ppermute | solution.py:184
  29.0 5.1 %collective-permute-done.23.refs_2_ = bf16[64,2304]{1,0:T(8,128)(2,1)S(1)} collective-permute-done((bf16[64,2304]{1,0:T(8,128)(2,1)S(1)}, bf16[64,2304]{1,0:T(8,128)(2,1)S(1)}, u32[]{:S(2)}, u32[]{:S(2)}) %collective-permute-start.23) | collective-permute-done | bytes 294944 | tf_op jit(solution)/shard_map/ppermute | solution.py:184
  40.5 8.5 %copy.14 = bf16[2304,1152]{0,1:T(8,128)(2,1)} copy(bf16[2304,1152]{1,0:T(8,128)(2,1)} %param.6) | data formatting | bytes 10616832 | tf_op args[1]
  49.1 2.0 collective-permute-start.45
  56.9 7.2 %ladder.3 = (s16[1168,128]{1,0:T(8,128)(2,1)S(1)}, s16[1168,128]{1,0:T(8,128)(2,1)S(1)}, s16[1168,128]{1,0:T(8,128)(2,1)S(1)}, s16[1168,128]{1,0:T(8,128)(2,1)S(1)}) custom-call(bf16[1152,2304]{1,0:T(8,128)(2,1)} %bitcast.42, bf16[64,2304]{1,0:T(8,128)(2,1)S(1)} %get-tuple-element.101.refs_0_, bf16[64,2304]{1,0:T(8,128)(2,1)S(1)} %collective-permute-done.refs_1_, ...), custom_call_target="tpu_custom_call" | custom-call | flops 2717908992 | bytes 8847360 | tf_op jit(solution)/shard_map/ladder/pallas_call | solution.py:298
  65.7 1.9 collective-permute-start.9
  68.2 7.3 %ladder.4 = (s16[1168,128]{1,0:T(8,128)(2,1)S(1)}, s16[1168,128]{1,0:T(8,128)(2,1)S(1)}, s16[1168,128]{1,0:T(8,128)(2,1)S(1)}, s16[1168,128]{1,0:T(8,128)(2,1)S(1)}) custom-call(bf16[1152,2304]{1,0:T(8,128)(2,1)} %bitcast.43, bf16[64,2304]{1,0:T(8,128)(2,1)S(1)} %get-tuple-element.68.refs_0_, bf16[64,2304]{1,0:T(8,128)(2,1)S(1)} %copy-done.38, ...), custom_call_target="tpu_custom_call" | custom-call | flops 2717908992 | bytes 8847360 | tf_op jit(solution)/shard_map/ladder/pallas_call | solution.py:298
  76.1 2.7 %collective-permute-done.8.refs_2_ = s16[1168,128]{1,0:T(8,128)(2,1)S(1)} collective-permute-done((s16[1168,128]{1,0:T(8,128)(2,1)S(1)}, s16[1168,128]{1,0:T(8,128)(2,1)S(1)}, u32[]{:S(2)}, u32[]{:S(2)}) %collective-permute-start.8) | collective-permute-done | bytes 299040 | tf_op jit(solution)/shard_map/ppermute | solution.py:184
  80.7 1.4 collective-permute-start.30
  82.1 1.4 collective-permute-start.31
  84.0 2.0 collective-permute-done.29.refs_1_
  86.0 10.6 %collective-permute-done.30.refs_2_ = s16[1168,128]{1,0:T(8,128)(2,1)} collective-permute-done((s16[1168,128]{1,0:T(8,128)(2,1)S(1)}, s16[1168,128]{1,0:T(8,128)(2,1)}, u32[]{:S(2)}, u32[]{:S(2)}) %collective-permute-start.30) | collective-permute-done | bytes 299040 | tf_op jit(solution)/shard_map/ppermute | solution.py:184
  98.6 7.9 %ladder.5 = (s16[1168,128]{1,0:T(8,128)(2,1)S(1)}, s16[1168,128]{1,0:T(8,128)(2,1)}, s16[1168,128]{1,0:T(8,128)(2,1)S(1)}, s16[1168,128]{1,0:T(8,128)(2,1)}) custom-call(bf16[1152,2304]{1,0:T(8,128)(2,1)} %bitcast.44, bf16[64,2304]{1,0:T(8,128)(2,1)S(1)} %get-tuple-element.85.refs_0_, bf16[64,2304]{1,0:T(8,128)(2,1)S(1)} %copy-done.34, ...), custom_call_target="tpu_custom_call" | custom-call | flops 2717908992 | bytes 8847360 | tf_op jit(solution)/shard_map/ladder/pallas_call | solution.py:298
  110.0 1.4 collective-permute-start.52
  113.5 3.2 %collective-permute-done.50.refs_1_ = s16[1168,128]{1,0:T(8,128)(2,1)} collective-permute-done((s16[1168,128]{1,0:T(8,128)(2,1)}, s16[1168,128]{1,0:T(8,128)(2,1)}, u32[]{:S(2)}, u32[]{:S(2)}) %collective-permute-start.50) | collective-permute-done | bytes 299040 | tf_op jit(solution)/shard_map/ppermute | solution.py:184
  116.8 7.3 %collective-permute-done.51.refs_2_ = s16[1168,128]{1,0:T(8,128)(2,1)} collective-permute-done((s16[1168,128]{1,0:T(8,128)(2,1)S(1)}, s16[1168,128]{1,0:T(8,128)(2,1)}, u32[]{:S(2)}, u32[]{:S(2)}) %collective-permute-start.51) | collective-permute-done | bytes 299040 | tf_op jit(solution)/shard_map/ppermute | solution.py:184
  129.8 8.2 %antisym.3 = (f32[4,1152,128]{2,1,0:T(8,128)S(1)}, s16[1168,128]{1,0:T(8,128)(2,1)S(1)}, s16[1168,128]{1,0:T(8,128)(2,1)S(1)}) custom-call(s32[2]{0:T(128)S(1)} %pad_add_fusion.place_ref, s16[1168,128]{1,0:T(8,128)(2,1)S(1)} %get-tuple-element.55.refs_0_, s16[1168,128]{1,0:T(8,128)(2,1)S(1)} %collective-permute-done.7.refs_1_, ...), custom_call_target="tpu_custom_call" | custom-call | flops 9437184 | bytes 9437184 | tf_op jit(solution)/shard_map/antisym/pallas_call | solution.py:301
  138.0 3.5 %collective-permute-start.14 = (s16[1168,128]{1,0:T(8,128)(2,1)S(1)}, s16[1168,128]{1,0:T(8,128)(2,1)S(1)}, u32[]{:S(2)}, u32[]{:S(2)}) collective-permute-start(s16[1168,128]{1,0:T(8,128)(2,1)S(1)} %get-tuple-element.60), channel_id=1, source_target_pairs={{0,1},{4,5},{8,9},{12,13},{16,17},{20,21},{24,25},{28,29}} | collective-permute-start | bytes 897032 | tf_op jit(solution)/shard_map/ppermute | solution.py:308
  143.1 9.6 %antisym.4 = (f32[4,1152,128]{2,1,0:T(8,128)S(1)}, s16[1168,128]{1,0:T(8,128)(2,1)}, s16[1168,128]{1,0:T(8,128)(2,1)}) custom-call(s32[2]{0:T(128)S(1)} %pad_add_fusion.place_ref, s16[1168,128]{1,0:T(8,128)(2,1)S(1)} %get-tuple-element.72.refs_0_, s16[1168,128]{1,0:T(8,128)(2,1)} %collective-permute-done.29.refs_1_, ...), custom_call_target="tpu_custom_call" | custom-call | flops 9437184 | bytes 9437184 | tf_op jit(solution)/shard_map/antisym/pallas_call | solution.py:301
  152.7 1.4 copy-done
  154.8 1.6 collective-permute-start.36
  157.1 1.4 collective-permute-start.37
  163.2 1.4 collective-permute-start.16
  165.3 9.0 %antisym.5 = (f32[4,1152,128]{2,1,0:T(8,128)S(1)}, s16[1168,128]{1,0:T(8,128)(2,1)S(1)}, s16[1168,128]{1,0:T(8,128)(2,1)S(1)}) custom-call(s32[2]{0:T(128)S(1)} %copy-done.32, s16[1168,128]{1,0:T(8,128)(2,1)S(1)} %get-tuple-element.86.refs_0_, s16[1168,128]{1,0:T(8,128)(2,1)} %collective-permute-done.50.refs_1_, ...), custom_call_target="tpu_custom_call" | custom-call | flops 9437184 | bytes 9437184 | tf_op jit(solution)/shard_map/antisym/pallas_call | solution.py:301
  174.3 3.4 %collective-permute-start.57 = (s16[1168,128]{1,0:T(8,128)(2,1)S(1)}, s16[1168,128]{1,0:T(8,128)(2,1)S(1)}, u32[]{:S(2)}, u32[]{:S(2)}) collective-permute-start(s16[1168,128]{1,0:T(8,128)(2,1)S(1)} %get-tuple-element.91), channel_id=1, source_target_pairs={{0,1},{4,5},{8,9},{12,13},{16,17},{20,21},{24,25},{28,29}} | collective-permute-start | bytes 897032 | tf_op jit(solution)/shard_map/ppermute | solution.py:308
  178.5 3.0 %hop.8 = (s16[1168,128]{1,0:T(8,128)(2,1)S(1)}, s16[1168,128]{1,0:T(8,128)(2,1)}) custom-call(s32[2]{0:T(128)S(1)} %add_clamp_fusion.1.place_ref, f32[4,1152,128]{2,1,0:T(8,128)S(1)} %copy-done.1, f32[4,1152,128]{2,1,0:T(8,128)S(1)} %copy-done.1, s16[1168,128]{1,0:T(8,128)(2,1)S(1)} %collective-permute-done.36.got_r, ...), custom_call_target="tpu_custom_call" | custom-call | flops 2359296 | bytes 2359296 | tf_op jit(solution)/shard_map/hop/pallas_call | solution.py:306
  184.1 1.4 collective-permute-start.39
  185.5 2.1 hop.7
  187.6 4.4 %collective-permute-start.18 = (s16[1168,128]{1,0:T(8,128)(2,1)}, s16[1168,128]{1,0:T(8,128)(2,1)S(1)}, u32[]{:S(2)}, u32[]{:S(2)}) collective-permute-start(s16[1168,128]{1,0:T(8,128)(2,1)} %get-tuple-element.64), channel_id=1, source_target_pairs={{0,1},{1,2},{2,3},{4,5},{5,6},{6,7},{8,9},{9,10},{10,11},{12,13},{... | collective-permute-start | bytes 897032 | tf_op jit(solution)/shard_map/ppermute | solution.py:308
  193.4 2.1 hop.10
  195.5 5.9 %collective-permute-start.59 = (s16[1168,128]{1,0:T(8,128)(2,1)}, s16[1168,128]{1,0:T(8,128)(2,1)}, u32[]{:S(2)}, u32[]{:S(2)}) collective-permute-start(s16[1168,128]{1,0:T(8,128)(2,1)} %get-tuple-element.93), channel_id=1, source_target_pairs={{0,1},{1,2},{4,5},{5,6},{8,9},{9,10},{12,13},{13,14},{16,17},{17,1... | collective-permute-start | bytes 897032 | tf_op jit(solution)/shard_map/ppermute | solution.py:308
  202.1 1.4 collective-permute-start.60
  207.4 1.7 copy-done.2
  210.0 3.3 %hop.9 = (s16[1168,128]{1,0:T(8,128)(2,1)}, s16[1168,128]{1,0:T(8,128)(2,1)}) custom-call(s32[2]{0:T(128)S(1)} %copy-done.30, f32[4,1152,128]{2,1,0:T(8,128)S(1)} %copy-done.2, f32[4,1152,128]{2,1,0:T(8,128)S(1)} %copy-done.2, s16[1168,128]{1,0:T(8,128)(2,1)S(1)} %copy-done.24, s16[1168,128]{1,0:T(8,128)(2,1)} %collective-permute-done.39.got_l), custom_call_target="tpu_custom_call" | custom-call | flops 2359296 | bytes 2359296 | tf_op jit(solution)/shard_map/hop/pallas_call | solution.py:306
  213.3 3.9 %collective-permute-start.40 = (s16[1168,128]{1,0:T(8,128)(2,1)}, s16[1168,128]{1,0:T(8,128)(2,1)}, u32[]{:S(2)}, u32[]{:S(2)}) collective-permute-start(s16[1168,128]{1,0:T(8,128)(2,1)} %get-tuple-element.81), channel_id=1, source_target_pairs={{0,1},{1,2},{2,3},{4,5},{5,6},{6,7},{8,9},{9,10},{10,11},{12,13},{... | collective-permute-start | bytes 897032 | tf_op jit(solution)/shard_map/ppermute | solution.py:308
  217.2 1.4 collective-permute-start.41
  218.7 3.2 %hop.11 = (s16[1168,128]{1,0:T(8,128)(2,1)}, s16[1168,128]{1,0:T(8,128)(2,1)}) custom-call(s32[2]{0:T(128)S(1)} %copy-done.30, f32[4,1152,128]{2,1,0:T(8,128)S(1)} %copy-done.5, f32[4,1152,128]{2,1,0:T(8,128)S(1)} %copy-done.5, s16[1168,128]{1,0:T(8,128)(2,1)} %collective-permute-done.59.got_r, s16[1168,128]{1,0:T(8,128)(2,1)} %collective-permute-done.60.got_l), custom_call_target="tpu_custom_call" | custom-call | flops 2359296 | bytes 2359296 | tf_op jit(solution)/shard_map/hop/pallas_call | solution.py:306
  221.8 5.3 %collective-permute-start.61 = (s16[1168,128]{1,0:T(8,128)(2,1)}, s16[1168,128]{1,0:T(8,128)(2,1)}, u32[]{:S(2)}, u32[]{:S(2)}) collective-permute-start(s16[1168,128]{1,0:T(8,128)(2,1)} %get-tuple-element.95), channel_id=1, source_target_pairs={{0,1},{1,2},{2,3},{4,5},{5,6},{6,7},{8,9},{9,10},{10,11},{12,13},{... | collective-permute-start | bytes 897032 | tf_op jit(solution)/shard_map/ppermute | solution.py:308
  227.1 1.5 collective-permute-start.62
  230.5 1.7 copy-done.3
  232.2 1.6 finish.4
  234.4 3.6 %collective-permute-done.62.got_l = s16[1168,128]{1,0:T(8,128)(2,1)} collective-permute-done((s16[1168,128]{1,0:T(8,128)(2,1)}, s16[1168,128]{1,0:T(8,128)(2,1)}, u32[]{:S(2)}, u32[]{:S(2)}) %collective-permute-start.62) | collective-permute-done | bytes 299040 | tf_op jit(solution)/shard_map/ppermute | solution.py:309
  238.0 1.5 finish.5
  (243 shorter events, 59.6 us)
Async XLA Ops:
  4.2 14.8 %collective-permute-start.1 = (bf16[64,2304]{1,0:T(8,128)(2,1)S(1)}, bf16[64,2304]{1,0:T(8,128)(2,1)S(1)}, u32[]{:S(2)}, u32[]{:S(2)}) collective-permute-start(bf16[64,2304]{1,0:T(8,128)(2,1)S(1)} %get-tuple-element.101.refs_0_), channel_id=1, source_target_pairs={{0,16},{4,20},{8,24},{12,28},{16,0},{20,4},{24,8},{28,12},{1,17},{... | collective-permute-start | bytes 884744 | tf_op jit(solution)/shard_map/ppermute | solution.py:184
  5.7 13.3 %collective-permute-start.2 = (bf16[64,2304]{1,0:T(8,128)(2,1)S(1)}, bf16[64,2304]{1,0:T(8,128)(2,1)S(1)}, u32[]{:S(2)}, u32[]{:S(2)}) collective-permute-start(bf16[64,2304]{1,0:T(8,128)(2,1)S(1)} %get-tuple-element.101.refs_0_), channel_id=1, source_target_pairs={{0,24},{4,28},{8,16},{12,20},{16,8},{20,12},{24,0},{28,4},{1,25},{... | collective-permute-start | bytes 884744 | tf_op jit(solution)/shard_map/ppermute | solution.py:184
  20.2 13.9 %collective-permute-start.23 = (bf16[64,2304]{1,0:T(8,128)(2,1)S(1)}, bf16[64,2304]{1,0:T(8,128)(2,1)S(1)}, u32[]{:S(2)}, u32[]{:S(2)}) collective-permute-start(bf16[64,2304]{1,0:T(8,128)(2,1)S(1)} %get-tuple-element.68.refs_0_), channel_id=1, source_target_pairs={{0,16},{4,20},{8,24},{12,28},{16,0},{20,4},{24,8},{28,12},{1,17},{... | collective-permute-start | bytes 884744 | tf_op jit(solution)/shard_map/ppermute | solution.py:184
  21.1 13.0 %collective-permute-start.24 = (bf16[64,2304]{1,0:T(8,128)(2,1)S(1)}, bf16[64,2304]{1,0:T(8,128)(2,1)S(1)}, u32[]{:S(2)}, u32[]{:S(2)}) collective-permute-start(bf16[64,2304]{1,0:T(8,128)(2,1)S(1)} %get-tuple-element.68.refs_0_), channel_id=1, source_target_pairs={{0,24},{4,28},{8,16},{12,20},{16,8},{20,12},{24,0},{28,4},{1,25},{... | collective-permute-start | bytes 884744 | tf_op jit(solution)/shard_map/ppermute | solution.py:184
  22.6 12.1 %collective-permute-start.3 = (bf16[64,2304]{1,0:T(8,128)(2,1)S(1)}, bf16[64,2304]{1,0:T(8,128)(2,1)S(1)}, u32[]{:S(2)}, u32[]{:S(2)}) collective-permute-start(bf16[64,2304]{1,0:T(8,128)(2,1)S(1)} %get-tuple-element.101.refs_0_), channel_id=1, source_target_pairs={{0,4},{4,0},{8,12},{12,8},{16,20},{20,16},{24,28},{28,24},{1,5},{5... | collective-permute-start | bytes 884744 | tf_op jit(solution)/shard_map/ppermute | solution.py:187
  22.6 13.0 %collective-permute-start.4 = (bf16[64,2304]{1,0:T(8,128)(2,1)S(1)}, bf16[64,2304]{1,0:T(8,128)(2,1)S(1)}, u32[]{:S(2)}, u32[]{:S(2)}) collective-permute-start(bf16[64,2304]{1,0:T(8,128)(2,1)S(1)} %collective-permute-done.refs_1_), channel_id=1, source_target_pairs={{0,4},{4,0},{8,12},{12,8},{16,20},{20,16},{24,28},{28,24},{1,5},{5... | collective-permute-start | bytes 884744 | tf_op jit(solution)/shard_map/ppermute | solution.py:187
  35.4 13.7 %collective-permute-start.26 = (bf16[64,2304]{1,0:T(8,128)(2,1)S(1)}, bf16[64,2304]{1,0:T(8,128)(2,1)}, u32[]{:S(2)}, u32[]{:S(2)}) collective-permute-start(bf16[64,2304]{1,0:T(8,128)(2,1)S(1)} %collective-permute-done.22.refs_1_), channel_id=1, source_target_pairs={{0,4},{4,0},{8,12},{12,8},{16,20},{20,16},{24,28},{28,24},{1,5},{5... | collective-permute-start | bytes 884744 | tf_op jit(solution)/shard_map/ppermute | solution.py:187
  36.3 27.8 %collective-permute-start.27 = (bf16[64,2304]{1,0:T(8,128)(2,1)S(1)}, bf16[64,2304]{1,0:T(8,128)(2,1)}, u32[]{:S(2)}, u32[]{:S(2)}) collective-permute-start(bf16[64,2304]{1,0:T(8,128)(2,1)S(1)} %collective-permute-done.23.refs_2_), channel_id=1, source_target_pairs={{0,4},{4,0},{8,12},{12,8},{16,20},{20,16},{24,28},{28,24},{1,5},{5... | collective-permute-start | bytes 884744 | tf_op jit(solution)/shard_map/ppermute | solution.py:187
  37.4 27.3 %collective-permute-start.28 = (bf16[64,2304]{1,0:T(8,128)(2,1)S(1)}, bf16[64,2304]{1,0:T(8,128)(2,1)}, u32[]{:S(2)}, u32[]{:S(2)}) collective-permute-start(bf16[64,2304]{1,0:T(8,128)(2,1)S(1)} %collective-permute-done.24.refs_3_), channel_id=1, source_target_pairs={{0,4},{4,0},{8,12},{12,8},{16,20},{20,16},{24,28},{28,24},{1,5},{5... | collective-permute-start | bytes 884744 | tf_op jit(solution)/shard_map/ppermute | solution.py:187
  38.3 27.4 %collective-permute-start.43 = (bf16[64,2304]{1,0:T(8,128)(2,1)S(1)}, bf16[64,2304]{1,0:T(8,128)(2,1)S(1)}, u32[]{:S(2)}, u32[]{:S(2)}) collective-permute-start(bf16[64,2304]{1,0:T(8,128)(2,1)S(1)} %get-tuple-element.85.refs_0_), channel_id=1, source_target_pairs={{0,8},{4,12},{8,0},{12,4},{16,24},{20,28},{24,16},{28,20},{1,9},{5... | collective-permute-start | bytes 884744 | tf_op jit(solution)/shard_map/ppermute | solution.py:184
  39.6 28.1 %collective-permute-start.44 = (bf16[64,2304]{1,0:T(8,128)(2,1)S(1)}, bf16[64,2304]{1,0:T(8,128)(2,1)S(1)}, u32[]{:S(2)}, u32[]{:S(2)}) collective-permute-start(bf16[64,2304]{1,0:T(8,128)(2,1)S(1)} %get-tuple-element.85.refs_0_), channel_id=1, source_target_pairs={{0,16},{4,20},{8,24},{12,28},{16,0},{20,4},{24,8},{28,12},{1,17},{... | collective-permute-start | bytes 884744 | tf_op jit(solution)/shard_map/ppermute | solution.py:184
  49.1 18.5 %collective-permute-start.45 = (bf16[64,2304]{1,0:T(8,128)(2,1)S(1)}, bf16[64,2304]{1,0:T(8,128)(2,1)S(1)}, u32[]{:S(2)}, u32[]{:S(2)}) collective-permute-start(bf16[64,2304]{1,0:T(8,128)(2,1)S(1)} %get-tuple-element.85.refs_0_), channel_id=1, source_target_pairs={{0,24},{4,28},{8,16},{12,20},{16,8},{20,12},{24,0},{28,4},{1,25},{... | collective-permute-start | bytes 884744 | tf_op jit(solution)/shard_map/ppermute | solution.py:184
  64.7 14.1 %collective-permute-start.8 = (s16[1168,128]{1,0:T(8,128)(2,1)S(1)}, s16[1168,128]{1,0:T(8,128)(2,1)S(1)}, u32[]{:S(2)}, u32[]{:S(2)}) collective-permute-start(s16[1168,128]{1,0:T(8,128)(2,1)S(1)} %get-tuple-element.57), channel_id=1, source_target_pairs={{0,16},{4,20},{8,24},{12,28},{16,0},{20,4},{24,8},{28,12},{1,17},{... | collective-permute-start | bytes 897032 | tf_op jit(solution)/shard_map/ppermute | solution.py:184
  65.7 14.2 %collective-permute-start.9 = (s16[1168,128]{1,0:T(8,128)(2,1)S(1)}, s16[1168,128]{1,0:T(8,128)(2,1)S(1)}, u32[]{:S(2)}, u32[]{:S(2)}) collective-permute-start(s16[1168,128]{1,0:T(8,128)(2,1)S(1)} %get-tuple-element.58), channel_id=1, source_target_pairs={{0,24},{4,28},{8,16},{12,20},{16,8},{20,12},{24,0},{28,4},{1,25},{... | collective-permute-start | bytes 897032 | tf_op jit(solution)/shard_map/ppermute | solution.py:184
  67.6 12.3 %collective-permute-start.10 = (s16[1168,128]{1,0:T(8,128)(2,1)S(1)}, s16[1168,128]{1,0:T(8,128)(2,1)S(1)}, u32[]{:S(2)}, u32[]{:S(2)}) collective-permute-start(s16[1168,128]{1,0:T(8,128)(2,1)S(1)} %get-tuple-element.55.refs_0_), channel_id=1, source_target_pairs={{0,4},{4,0},{8,12},{12,8},{16,20},{20,16},{24,28},{28,24},{1,5},{5... | collective-permute-start | bytes 897032 | tf_op jit(solution)/shard_map/ppermute | solution.py:187
  80.7 16.0 %collective-permute-start.30 = (s16[1168,128]{1,0:T(8,128)(2,1)S(1)}, s16[1168,128]{1,0:T(8,128)(2,1)}, u32[]{:S(2)}, u32[]{:S(2)}) collective-permute-start(s16[1168,128]{1,0:T(8,128)(2,1)S(1)} %get-tuple-element.74), channel_id=1, source_target_pairs={{0,16},{4,20},{8,24},{12,28},{16,0},{20,4},{24,8},{28,12},{1,17},{... | collective-permute-start | bytes 897032 | tf_op jit(solution)/shard_map/ppermute | solution.py:184
  82.1 24.4 %collective-permute-start.31 = (s16[1168,128]{1,0:T(8,128)(2,1)S(1)}, s16[1168,128]{1,0:T(8,128)(2,1)}, u32[]{:S(2)}, u32[]{:S(2)}) collective-permute-start(s16[1168,128]{1,0:T(8,128)(2,1)S(1)} %get-tuple-element.75), channel_id=1, source_target_pairs={{0,24},{4,28},{8,16},{12,20},{16,8},{20,12},{24,0},{28,4},{1,25},{... | collective-permute-start | bytes 897032 | tf_op jit(solution)/shard_map/ppermute | solution.py:184
  83.5 24.1 %collective-permute-start.32 = (s16[1168,128]{1,0:T(8,128)(2,1)S(1)}, s16[1168,128]{1,0:T(8,128)(2,1)S(1)}, u32[]{:S(2)}, u32[]{:S(2)}) collective-permute-start(s16[1168,128]{1,0:T(8,128)(2,1)S(1)} %get-tuple-element.72.refs_0_), channel_id=1, source_target_pairs={{0,4},{4,0},{8,12},{12,8},{16,20},{20,16},{24,28},{28,24},{1,5},{5... | collective-permute-start | bytes 897032 | tf_op jit(solution)/shard_map/ppermute | solution.py:187
  83.5 25.8 %collective-permute-start.11 = (s16[1168,128]{1,0:T(8,128)(2,1)S(1)}, s16[1168,128]{1,0:T(8,128)(2,1)S(1)}, u32[]{:S(2)}, u32[]{:S(2)}) collective-permute-start(s16[1168,128]{1,0:T(8,128)(2,1)S(1)} %collective-permute-done.7.refs_1_), channel_id=1, source_target_pairs={{0,4},{4,0},{8,12},{12,8},{16,20},{20,16},{24,28},{28,24},{1,5},{5... | collective-permute-start | bytes 897032 | tf_op jit(solution)/shard_map/ppermute | solution.py:187
  86.0 25.5 %collective-permute-start.12 = (s16[1168,128]{1,0:T(8,128)(2,1)S(1)}, s16[1168,128]{1,0:T(8,128)(2,1)S(1)}, u32[]{:S(2)}, u32[]{:S(2)}) collective-permute-start(s16[1168,128]{1,0:T(8,128)(2,1)S(1)} %collective-permute-done.8.refs_2_), channel_id=1, source_target_pairs={{0,4},{4,0},{8,12},{12,8},{16,20},{20,16},{24,28},{28,24},{1,5},{5... | collective-permute-start | bytes 897032 | tf_op jit(solution)/shard_map/ppermute | solution.py:187
  96.6 15.6 %collective-permute-start.13 = (s16[1168,128]{1,0:T(8,128)(2,1)S(1)}, s16[1168,128]{1,0:T(8,128)(2,1)S(1)}, u32[]{:S(2)}, u32[]{:S(2)}) collective-permute-start(s16[1168,128]{1,0:T(8,128)(2,1)S(1)} %collective-permute-done.9.refs_3_), channel_id=1, source_target_pairs={{0,4},{4,0},{8,12},{12,8},{16,20},{20,16},{24,28},{28,24},{1,5},{5... | collective-permute-start | bytes 897032 | tf_op jit(solution)/shard_map/ppermute | solution.py:187
  108.3 15.7 %collective-permute-start.51 = (s16[1168,128]{1,0:T(8,128)(2,1)S(1)}, s16[1168,128]{1,0:T(8,128)(2,1)}, u32[]{:S(2)}, u32[]{:S(2)}) collective-permute-start(s16[1168,128]{1,0:T(8,128)(2,1)S(1)} %get-tuple-element.88), channel_id=1, source_target_pairs={{0,16},{4,20},{8,24},{12,28},{16,0},{20,4},{24,8},{28,12},{1,17},{... | collective-permute-start | bytes 897032 | tf_op jit(solution)/shard_map/ppermute | solution.py:184
  110.0 28.0 %collective-permute-start.52 = (s16[1168,128]{1,0:T(8,128)(2,1)}, s16[1168,128]{1,0:T(8,128)(2,1)}, u32[]{:S(2)}, u32[]{:S(2)}) collective-permute-start(s16[1168,128]{1,0:T(8,128)(2,1)} %get-tuple-element.89), channel_id=1, source_target_pairs={{0,24},{4,28},{8,16},{12,20},{16,8},{20,12},{24,0},{28,4},{1,25},{... | collective-permute-start | bytes 897032 | tf_op jit(solution)/shard_map/ppermute | solution.py:184
  112.2 29.3 %collective-permute-start.53 = (s16[1168,128]{1,0:T(8,128)(2,1)S(1)}, s16[1168,128]{1,0:T(8,128)(2,1)}, u32[]{:S(2)}, u32[]{:S(2)}) collective-permute-start(s16[1168,128]{1,0:T(8,128)(2,1)S(1)} %get-tuple-element.86.refs_0_), channel_id=1, source_target_pairs={{0,4},{4,0},{8,12},{12,8},{16,20},{20,16},{24,28},{28,24},{1,5},{5... | collective-permute-start | bytes 897032 | tf_op jit(solution)/shard_map/ppermute | solution.py:187
  112.9 29.3 %collective-permute-start.33 = (s16[1168,128]{1,0:T(8,128)(2,1)}, s16[1168,128]{1,0:T(8,128)(2,1)S(1)}, u32[]{:S(2)}, u32[]{:S(2)}) collective-permute-start(s16[1168,128]{1,0:T(8,128)(2,1)} %collective-permute-done.29.refs_1_), channel_id=1, source_target_pairs={{0,4},{4,0},{8,12},{12,8},{16,20},{20,16},{24,28},{28,24},{1,5},{5... | collective-permute-start | bytes 897032 | tf_op jit(solution)/shard_map/ppermute | solution.py:187
  116.8 25.8 %collective-permute-start.34 = (s16[1168,128]{1,0:T(8,128)(2,1)}, s16[1168,128]{1,0:T(8,128)(2,1)S(1)}, u32[]{:S(2)}, u32[]{:S(2)}) collective-permute-start(s16[1168,128]{1,0:T(8,128)(2,1)} %collective-permute-done.30.refs_2_), channel_id=1, source_target_pairs={{0,4},{4,0},{8,12},{12,8},{16,20},{20,16},{24,28},{28,24},{1,5},{5... | collective-permute-start | bytes 897032 | tf_op jit(solution)/shard_map/ppermute | solution.py:187
  124.0 18.8 %collective-permute-start.35 = (s16[1168,128]{1,0:T(8,128)(2,1)}, s16[1168,128]{1,0:T(8,128)(2,1)S(1)}, u32[]{:S(2)}, u32[]{:S(2)}) collective-permute-start(s16[1168,128]{1,0:T(8,128)(2,1)} %collective-permute-done.31.refs_3_), channel_id=1, source_target_pairs={{0,4},{4,0},{8,12},{12,8},{16,20},{20,16},{24,28},{28,24},{1,5},{5... | collective-permute-start | bytes 897032 | tf_op jit(solution)/shard_map/ppermute | solution.py:187
  138.0 16.0 %collective-permute-start.14 = (s16[1168,128]{1,0:T(8,128)(2,1)S(1)}, s16[1168,128]{1,0:T(8,128)(2,1)S(1)}, u32[]{:S(2)}, u32[]{:S(2)}) collective-permute-start(s16[1168,128]{1,0:T(8,128)(2,1)S(1)} %get-tuple-element.60), channel_id=1, source_target_pairs={{0,1},{4,5},{8,9},{12,13},{16,17},{20,21},{24,25},{28,29}} | collective-permute-start | bytes 897032 | tf_op jit(solution)/shard_map/ppermute | solution.py:308
  141.5 14.8 %collective-permute-start.15 = (s16[1168,128]{1,0:T(8,128)(2,1)S(1)}, s16[1168,128]{1,0:T(8,128)(2,1)S(1)}, u32[]{:S(2)}, u32[]{:S(2)}) collective-permute-start(s16[1168,128]{1,0:T(8,128)(2,1)S(1)} %get-tuple-element.61), channel_id=1, source_target_pairs={{3,2},{7,6},{11,10},{15,14},{19,18},{23,22},{27,26},{31,30}} | collective-permute-start | bytes 897032 | tf_op jit(solution)/shard_map/ppermute | solution.py:309
  142.2 20.9 %collective-permute-start.54 = (s16[1168,128]{1,0:T(8,128)(2,1)}, s16[1168,128]{1,0:T(8,128)(2,1)S(1)}, u32[]{:S(2)}, u32[]{:S(2)}) collective-permute-start(s16[1168,128]{1,0:T(8,128)(2,1)} %collective-permute-done.50.refs_1_), channel_id=1, source_target_pairs={{0,4},{4,0},{8,12},{12,8},{16,20},{20,16},{24,28},{28,24},{1,5},{5... | collective-permute-start | bytes 897032 | tf_op jit(solution)/shard_map/ppermute | solution.py:187
  142.6 22.1 %collective-permute-start.55 = (s16[1168,128]{1,0:T(8,128)(2,1)}, s16[1168,128]{1,0:T(8,128)(2,1)S(1)}, u32[]{:S(2)}, u32[]{:S(2)}) collective-permute-start(s16[1168,128]{1,0:T(8,128)(2,1)} %collective-permute-done.51.refs_2_), channel_id=1, source_target_pairs={{0,4},{4,0},{8,12},{12,8},{16,20},{20,16},{24,28},{28,24},{1,5},{5... | collective-permute-start | bytes 897032 | tf_op jit(solution)/shard_map/ppermute | solution.py:187
  142.8 22.5 %collective-permute-start.56 = (s16[1168,128]{1,0:T(8,128)(2,1)}, s16[1168,128]{1,0:T(8,128)(2,1)}, u32[]{:S(2)}, u32[]{:S(2)}) collective-permute-start(s16[1168,128]{1,0:T(8,128)(2,1)} %collective-permute-done.52.refs_3_), channel_id=1, source_target_pairs={{0,4},{4,0},{8,12},{12,8},{16,20},{20,16},{24,28},{28,24},{1,5},{5... | collective-permute-start | bytes 897032 | tf_op jit(solution)/shard_map/ppermute | solution.py:187
  154.8 23.0 %collective-permute-start.36 = (s16[1168,128]{1,0:T(8,128)(2,1)}, s16[1168,128]{1,0:T(8,128)(2,1)S(1)}, u32[]{:S(2)}, u32[]{:S(2)}) collective-permute-start(s16[1168,128]{1,0:T(8,128)(2,1)} %get-tuple-element.77), channel_id=1, source_target_pairs={{0,1},{4,5},{8,9},{12,13},{16,17},{20,21},{24,25},{28,29}} | collective-permute-start | bytes 897032 | tf_op jit(solution)/shard_map/ppermute | solution.py:308
  157.1 21.4 %collective-permute-start.37 = (s16[1168,128]{1,0:T(8,128)(2,1)}, s16[1168,128]{1,0:T(8,128)(2,1)}, u32[]{:S(2)}, u32[]{:S(2)}) collective-permute-start(s16[1168,128]{1,0:T(8,128)(2,1)} %get-tuple-element.78), channel_id=1, source_target_pairs={{3,2},{7,6},{11,10},{15,14},{19,18},{23,22},{27,26},{31,30}} | collective-permute-start | bytes 897032 | tf_op jit(solution)/shard_map/ppermute | solution.py:309
  163.2 20.9 %collective-permute-start.16 = (s16[1168,128]{1,0:T(8,128)(2,1)S(1)}, s16[1168,128]{1,0:T(8,128)(2,1)S(1)}, u32[]{:S(2)}, u32[]{:S(2)}) collective-permute-start(s16[1168,128]{1,0:T(8,128)(2,1)S(1)} %get-tuple-element.62), channel_id=1, source_target_pairs={{0,1},{1,2},{4,5},{5,6},{8,9},{9,10},{12,13},{13,14},{16,17},{17,1... | collective-permute-start | bytes 897032 | tf_op jit(solution)/shard_map/ppermute | solution.py:308
  164.6 20.9 %collective-permute-start.17 = (s16[1168,128]{1,0:T(8,128)(2,1)S(1)}, s16[1168,128]{1,0:T(8,128)(2,1)S(1)}, u32[]{:S(2)}, u32[]{:S(2)}) collective-permute-start(s16[1168,128]{1,0:T(8,128)(2,1)S(1)} %get-tuple-element.63), channel_id=1, source_target_pairs={{2,1},{3,2},{6,5},{7,6},{10,9},{11,10},{14,13},{15,14},{18,17},{19... | collective-permute-start | bytes 897032 | tf_op jit(solution)/shard_map/ppermute | solution.py:309
  174.3 17.7 %collective-permute-start.57 = (s16[1168,128]{1,0:T(8,128)(2,1)S(1)}, s16[1168,128]{1,0:T(8,128)(2,1)S(1)}, u32[]{:S(2)}, u32[]{:S(2)}) collective-permute-start(s16[1168,128]{1,0:T(8,128)(2,1)S(1)} %get-tuple-element.91), channel_id=1, source_target_pairs={{0,1},{4,5},{8,9},{12,13},{16,17},{20,21},{24,25},{28,29}} | collective-permute-start | bytes 897032 | tf_op jit(solution)/shard_map/ppermute | solution.py:308
  177.8 15.6 %collective-permute-start.58 = (s16[1168,128]{1,0:T(8,128)(2,1)S(1)}, s16[1168,128]{1,0:T(8,128)(2,1)S(1)}, u32[]{:S(2)}, u32[]{:S(2)}) collective-permute-start(s16[1168,128]{1,0:T(8,128)(2,1)S(1)} %get-tuple-element.92), channel_id=1, source_target_pairs={{3,2},{7,6},{11,10},{15,14},{19,18},{23,22},{27,26},{31,30}} | collective-permute-start | bytes 897032 | tf_op jit(solution)/shard_map/ppermute | solution.py:309
  181.5 19.9 %collective-permute-start.38 = (s16[1168,128]{1,0:T(8,128)(2,1)S(1)}, s16[1168,128]{1,0:T(8,128)(2,1)S(1)}, u32[]{:S(2)}, u32[]{:S(2)}) collective-permute-start(s16[1168,128]{1,0:T(8,128)(2,1)S(1)} %get-tuple-element.79), channel_id=1, source_target_pairs={{0,1},{1,2},{4,5},{5,6},{8,9},{9,10},{12,13},{13,14},{16,17},{17,1... | collective-permute-start | bytes 897032 | tf_op jit(solution)/shard_map/ppermute | solution.py:308
  184.1 23.3 %collective-permute-start.39 = (s16[1168,128]{1,0:T(8,128)(2,1)}, s16[1168,128]{1,0:T(8,128)(2,1)}, u32[]{:S(2)}, u32[]{:S(2)}) collective-permute-start(s16[1168,128]{1,0:T(8,128)(2,1)} %get-tuple-element.80), channel_id=1, source_target_pairs={{2,1},{3,2},{6,5},{7,6},{10,9},{11,10},{14,13},{15,14},{18,17},{19... | collective-permute-start | bytes 897032 | tf_op jit(solution)/shard_map/ppermute | solution.py:309
  187.6 39.5 %collective-permute-start.18 = (s16[1168,128]{1,0:T(8,128)(2,1)}, s16[1168,128]{1,0:T(8,128)(2,1)S(1)}, u32[]{:S(2)}, u32[]{:S(2)}) collective-permute-start(s16[1168,128]{1,0:T(8,128)(2,1)} %get-tuple-element.64), channel_id=1, source_target_pairs={{0,1},{1,2},{2,3},{4,5},{5,6},{6,7},{8,9},{9,10},{10,11},{12,13},{... | collective-permute-start | bytes 897032 | tf_op jit(solution)/shard_map/ppermute | solution.py:308
  192.1 36.6 %collective-permute-start.19 = (s16[1168,128]{1,0:T(8,128)(2,1)}, s16[1168,128]{1,0:T(8,128)(2,1)S(1)}, u32[]{:S(2)}, u32[]{:S(2)}) collective-permute-start(s16[1168,128]{1,0:T(8,128)(2,1)} %get-tuple-element.65), channel_id=1, source_target_pairs={{1,0},{2,1},{3,2},{5,4},{6,5},{7,6},{9,8},{10,9},{11,10},{13,12},{... | collective-permute-start | bytes 897032 | tf_op jit(solution)/shard_map/ppermute | solution.py:309
  195.5 17.8 %collective-permute-start.59 = (s16[1168,128]{1,0:T(8,128)(2,1)}, s16[1168,128]{1,0:T(8,128)(2,1)}, u32[]{:S(2)}, u32[]{:S(2)}) collective-permute-start(s16[1168,128]{1,0:T(8,128)(2,1)} %get-tuple-element.93), channel_id=1, source_target_pairs={{0,1},{1,2},{4,5},{5,6},{8,9},{9,10},{12,13},{13,14},{16,17},{17,1... | collective-permute-start | bytes 897032 | tf_op jit(solution)/shard_map/ppermute | solution.py:308
  202.1 15.1 %collective-permute-start.60 = (s16[1168,128]{1,0:T(8,128)(2,1)}, s16[1168,128]{1,0:T(8,128)(2,1)}, u32[]{:S(2)}, u32[]{:S(2)}) collective-permute-start(s16[1168,128]{1,0:T(8,128)(2,1)} %get-tuple-element.94), channel_id=1, source_target_pairs={{2,1},{3,2},{6,5},{7,6},{10,9},{11,10},{14,13},{15,14},{18,17},{19... | collective-permute-start | bytes 897032 | tf_op jit(solution)/shard_map/ppermute | solution.py:309
  207.4 14.5 %collective-permute-start.20 = (f32[3,1,64]{2,1,0:T(1,128)S(1)}, f32[3,1,64]{2,1,0:T(1,128)S(1)}, u32[]{:S(2)}, u32[]{:S(2)}) collective-permute-start(f32[3,1,64]{2,1,0:T(1,128)S(1)} %add.65), channel_id=1, source_target_pairs={{0,4},{4,0},{8,12},{12,8},{16,20},{20,16},{24,28},{28,24},{1,5},{5... | collective-permute-start | bytes 2312 | tf_op jit(solution)/shard_map/ppermute | solution.py:187
  213.3 17.2 %collective-permute-start.40 = (s16[1168,128]{1,0:T(8,128)(2,1)}, s16[1168,128]{1,0:T(8,128)(2,1)}, u32[]{:S(2)}, u32[]{:S(2)}) collective-permute-start(s16[1168,128]{1,0:T(8,128)(2,1)} %get-tuple-element.81), channel_id=1, source_target_pairs={{0,1},{1,2},{2,3},{4,5},{5,6},{6,7},{8,9},{9,10},{10,11},{12,13},{... | collective-permute-start | bytes 897032 | tf_op jit(solution)/shard_map/ppermute | solution.py:308
  217.2 13.3 %collective-permute-start.41 = (s16[1168,128]{1,0:T(8,128)(2,1)}, s16[1168,128]{1,0:T(8,128)(2,1)}, u32[]{:S(2)}, u32[]{:S(2)}) collective-permute-start(s16[1168,128]{1,0:T(8,128)(2,1)} %get-tuple-element.82), channel_id=1, source_target_pairs={{1,0},{2,1},{3,2},{5,4},{6,5},{7,6},{9,8},{10,9},{11,10},{13,12},{... | collective-permute-start | bytes 897032 | tf_op jit(solution)/shard_map/ppermute | solution.py:309
  221.8 12.5 %collective-permute-start.61 = (s16[1168,128]{1,0:T(8,128)(2,1)}, s16[1168,128]{1,0:T(8,128)(2,1)}, u32[]{:S(2)}, u32[]{:S(2)}) collective-permute-start(s16[1168,128]{1,0:T(8,128)(2,1)} %get-tuple-element.95), channel_id=1, source_target_pairs={{0,1},{1,2},{2,3},{4,5},{5,6},{6,7},{8,9},{9,10},{10,11},{12,13},{... | collective-permute-start | bytes 897032 | tf_op jit(solution)/shard_map/ppermute | solution.py:308
  (77 other events, 560.0 us)

commit v2 on v0

v2 whole, which is shorter than its diff:
```python
import functools

import jax
import jax.numpy as jnp
from jax import lax
from jax.experimental import pallas as pl
from jax.experimental.pallas import tpu as pltpu
from jax.sharding import PartitionSpec as P

CORES = 2
WIDTH = 64
LANES = 2 * WIDTH
TAIL = 16
NT = (((1,), (1,)), ((), ()))


def tile_of(rows, most):
    return max(t for t in range(16, most + 1, 16) if rows % t == 0)


def is_low(shape):
    return lax.broadcasted_iota(jnp.int32, shape, len(shape) - 1) < WIDTH


def turn(values):
    return pltpu.roll(values, WIDTH, 1)


def encode(values, out_ref):
    tile = values.shape[0]
    peak = jnp.max(jnp.abs(values), axis=0, keepdims=True)
    power = jnp.ceil(jnp.log2(jnp.maximum(peak, 1e-30) * (1.0 / 32760.0)))
    codes = jnp.round(values * jnp.exp2(-power)).astype(jnp.int32)
    out_ref[pl.ds(0, tile), :] = codes.astype(jnp.int16)
    wide = jnp.broadcast_to(power.astype(jnp.int32), (TAIL, LANES))
    out_ref[pl.ds(tile, TAIL), :] = wide.astype(jnp.int16)


def decode(ref):
    tile = ref.shape[0] - TAIL
    power = ref[pl.ds(tile, TAIL), :].astype(jnp.int32).astype(jnp.float32)[0:1, :]
    return ref[pl.ds(0, tile), :].astype(jnp.int32).astype(jnp.float32) * jnp.exp2(power)


def ladder_kernel(chips, own_ref, sib_ref, *refs):
    rows_in, outs, rhs = refs[:chips], refs[chips : 2 * chips], refs[-1]

    @pl.when(pl.program_id(0) == 0)
    def _():
        for d in range(chips):
            rhs[pl.ds(d * WIDTH, WIDTH), :] = rows_in[d][...]

    low = is_low((own_ref.shape[0], LANES))
    group = min(4, chips)
    for first in range(0, chips, group):
        right = rhs[pl.ds(first * WIDTH, group * WIDTH), :]
        own = lax.dot_general(own_ref[...], right, NT, preferred_element_type=jnp.float32)
        sib = lax.dot_general(sib_ref[...], right, NT, preferred_element_type=jnp.float32)
        for k in range(0, group, 2):
            u = own[:, k * WIDTH : k * WIDTH + LANES]
            v = sib[:, k * WIDTH : k * WIDTH + LANES]
            encode(jnp.where(low, u, turn(v)), outs[first + k].at[0])
            encode(jnp.where(low, turn(u), v), outs[first + k + 1].at[0])


def antisym_kernel(chips, slabs, vir, place_ref, *refs):
    arrived, (anti, first_out, cube) = refs[:chips], refs[chips:]
    chip, core, z = place_ref[0], place_ref[1], place_ref[2]
    tiles, tile = arrived[0].shape[0], arrived[0].shape[1] - TAIL
    rows = tiles * tile
    s = pl.program_id(0)

    @pl.when(s == 0)
    def _():
        low = is_low((tile, LANES))
        for d in range(chips):
            base = (chip ^ d) * (CORES * rows)
            for t in range(tiles):
                values = decode(arrived[d].at[t])
                turned = turn(values)
                at_own = pl.multiple_of(base + core * rows + t * tile, tile)
                at_sib = pl.multiple_of(base + (1 - core) * rows + t * tile, tile)
                cube[pl.ds(at_own, tile), :] = jnp.where(low, values, turned)
                cube[pl.ds(at_sib, tile), :] = jnp.where(low, turned, values)

    half = vir // slabs // 2
    low = is_low((vir, LANES))

    def subtract(k, carry):
        a = s * (2 * half) + k
        b = a + half
        here = cube[pl.ds(pl.multiple_of(a * vir, vir), vir), :]
        other = cube[pl.ds(pl.multiple_of(b * vir, vir), vir), :]
        lower = here - cube[pl.ds(a, vir, stride=vir), :]
        upper = other - cube[pl.ds(b, vir, stride=vir), :]
        anti[0, pl.ds(pl.multiple_of(k * vir, vir), vir), :] = jnp.where(low, lower, upper)
        return carry

    lax.fori_loop(0, half, subtract, 0)
    part_tile = first_out.shape[1] - TAIL

    @pl.when(s == jnp.where(z == 0, slabs - 1, 0))
    def _():
        for t in range(first_out.shape[0]):
            encode(anti[0, pl.ds(t * part_tile, part_tile), :], first_out.at[t])


def hop_kernel(count, place_ref, *refs):
    for k in range(count):
        anti, got, out = refs[k], refs[count + k], refs[2 * count + k]
        encode(anti[0] + decode(got.at[0]), out.at[0])


def finish_kernel(place_ref, anti, got_r, got_l, pair_ref, vir_ref, *refs):
    out_ref = refs[-1]
    tiles, tile = got_r.shape[0], got_r.shape[1] - TAIL
    low = is_low((tile, LANES))
    pair = pair_ref[0]
    half = tiles * tile
    for t in range(tiles):
        at = pl.ds(t * tile, tile)
        total = anti[0, at, :] + (decode(got_r.at[t]) + decode(got_l.at[t]))
        virt = jnp.where(low, vir_ref[at, 0:1], vir_ref[at, 1:2])
        update = (total / (pair - virt)).T
        out_ref[:, pl.ds(t * tile, tile)] = update[:WIDTH]
        out_ref[:, pl.ds(half + t * tile, tile)] = update[WIDTH:]


def on_device(mesh, amplitudes, integrals, pair_index, eps_occ, eps_vir):
    devices, slabs = mesh.shape["pair"], mesh.shape["slab"]
    chips = devices // CORES
    num_pairs, depth = amplitudes.shape
    rows = integrals.shape[1]
    vir = eps_vir.shape[0]
    chunks = num_pairs // WIDTH
    half = vir // slabs // 2
    part_rows = half * vir
    tile, part_tile = tile_of(rows, 384), tile_of(part_rows, 384)
    tiles, part_tiles = rows // tile, part_rows // part_tile
    me, z = lax.axis_index("pair"), lax.axis_index("slab")
    chip, core = me // CORES, me % CORES

    def to_chip(x, d):
        return lax.ppermute(x, "pair", [(i, i ^ (d * CORES)) for i in range(devices)])

    def limit(mib):
        return pltpu.CompilerParams(vmem_limit_bytes=mib * 1024 * 1024)

    def cost(flops, moved):
        return pl.CostEstimate(flops=flops, bytes_accessed=moved, transcendentals=0)

    message = jax.ShapeDtypeStruct((tiles, tile + TAIL, LANES), jnp.int16)
    part_message = jax.ShapeDtypeStruct((part_tiles, part_tile + TAIL, LANES), jnp.int16)
    smem = pl.BlockSpec(memory_space=pltpu.SMEM)

    ladder = pl.pallas_call(
        functools.partial(ladder_kernel, chips),
        grid=(tiles,),
        in_specs=[pl.BlockSpec((tile, depth), lambda i: (i, 0))] * 2
        + [pl.BlockSpec((WIDTH, depth), lambda i: (0, 0))] * chips,
        out_specs=[pl.BlockSpec((1, tile + TAIL, LANES), lambda i: (i, 0, 0))] * chips,
        out_shape=[message] * chips,
        scratch_shapes=[pltpu.VMEM((chips * WIDTH, depth), jnp.bfloat16)],
        compiler_params=limit(24),
        cost_estimate=cost(
            4 * rows * depth * chips * WIDTH,
            4 * rows * depth + 2 * chips * WIDTH * depth + 2 * chips * rows * LANES,
        ),
        name="ladder",
    )
    antisym = pl.pallas_call(
        functools.partial(antisym_kernel, chips, slabs, vir),
        grid=(slabs,),
        in_specs=[smem] + [pl.BlockSpec(message.shape, lambda s: (0, 0, 0))] * chips,
        out_specs=[
            pl.BlockSpec((1, part_rows, LANES), lambda s: (s, 0, 0)),
            pl.BlockSpec(part_message.shape, lambda s: (0, 0, 0)),
        ],
        out_shape=[
            jax.ShapeDtypeStruct((slabs, part_rows, LANES), jnp.float32),
            part_message,
        ],
        scratch_shapes=[pltpu.VMEM((vir * vir, LANES), jnp.float32)],
        compiler_params=limit(24),
        cost_estimate=cost(8 * vir * vir * LANES, 4 * vir * vir * LANES),
        name="antisym",
    )
    part_spec = pl.BlockSpec((1, part_tile + TAIL, LANES), lambda i, place: (i, 0, 0))

    def hop(count):
        def anti_spec(k):
            return pl.BlockSpec((1, part_tile, LANES), lambda i, place: (place[k], i, 0))

        return pl.pallas_call(
            functools.partial(hop_kernel, count),
            grid_spec=pltpu.PrefetchScalarGridSpec(
                num_scalar_prefetch=1,
                grid=(part_tiles,),
                in_specs=[anti_spec(k) for k in range(count)] + [part_spec] * count,
                out_specs=[part_spec] * count,
            ),
            out_shape=[part_message] * count,
            compiler_params=limit(12),
            cost_estimate=cost(8 * count * part_rows * LANES, 8 * count * part_rows * LANES),
            name="hop",
        )

    def finish(r, anti, got_r, got_l, pair, virt, place, so_far):
        given = [] if so_far is None else [so_far]
        whole_part = pl.BlockSpec(part_message.shape, lambda i, place: (0, 0, 0))
        return pl.pallas_call(
            finish_kernel,
            grid_spec=pltpu.PrefetchScalarGridSpec(
                num_scalar_prefetch=1,
                grid=(1,),
                in_specs=[
                    pl.BlockSpec((1, part_rows, LANES), lambda i, place: (place[0], 0, 0)),
                    whole_part,
                    whole_part,
                    pl.BlockSpec((1, 1, LANES), lambda i, place: (r, 0, 0)),
                    pl.BlockSpec((part_rows, 2), lambda i, place: (0, 0)),
                ]
                + [pl.BlockSpec(memory_space=pl.ANY)] * len(given),
                out_specs=pl.BlockSpec((WIDTH, 2 * part_rows), lambda i, place: (r, 0)),
            ),
            out_shape=jax.ShapeDtypeStruct((num_pairs, 2 * part_rows), jnp.float32),
            input_output_aliases={6: 0} if given else {},
            compiler_params=limit(16),
            cost_estimate=cost(16 * part_rows * LANES, 16 * part_rows * LANES),
            name="finish",
        )(place, anti, got_r, got_l, pair, virt, *given)

    own_t = integrals.T
    sib_t = lax.ppermute(own_t, "pair", [(i, i ^ 1) for i in range(devices)])

    occ_ids = jnp.arange(eps_occ.shape[0], dtype=jnp.int32)

    def pick(ids):
        return jnp.sum(jnp.where(ids[:, None] == occ_ids[None, :], eps_occ[None, :], 0.0), axis=1)

    eps_pair = (pick(pair_index[:, 0]) + pick(pair_index[:, 1])).reshape(chunks, 1, WIDTH)
    eps_pair = jnp.concatenate([eps_pair, eps_pair], axis=2)
    eps_mine = lax.dynamic_slice(eps_vir.reshape(slabs, 2, half), (z, 0, 0), (1, 2, half))[0]
    eps_virt = (eps_mine[:, :, None] + eps_vir[None, None, :]).reshape(2, part_rows).T

    place = jnp.stack([chip, core, z]).astype(jnp.int32)

    gathered = []
    for r in range(chunks):
        mine = amplitudes[r * WIDTH : (r + 1) * WIDTH]
        if gathered:
            mine, *last = lax.optimization_barrier((mine, *gathered[-1]))
            gathered[-1] = last
        gathered.append([mine] + [to_chip(mine, d) for d in range(1, chips)])

    update = None
    for r in range(chunks):
        sums = ladder(own_t, sib_t, *gathered[r])
        arrived = [sums[0]] + [to_chip(sums[d], d) for d in range(1, chips)]
        anti, one = antisym(place, *arrived)
        for step in range(1, slabs):
            ahead = slabs - step
            rightward = [(i, i + 1) for i in range(step)]
            leftward = [(i, i - 1) for i in range(ahead, slabs)]
            targets = jnp.stack([z + ahead, z - ahead])
            if step <= slabs // 2:
                if step > 1:
                    target = jnp.where(z < slabs // 2, targets[0:1], targets[1:2])
                    target = jnp.clip(target, 0, slabs - 1).astype(jnp.int32)
                    (one,) = hop(1)(target, anti, one)
                if step < slabs // 2:
                    one = lax.ppermute(one, "slab", rightward + leftward)
                    continue
                right = left = one
            else:
                targets = jnp.clip(targets, 0, slabs - 1).astype(jnp.int32)
                right, left = hop(2)(targets, anti, anti, right, left)
            right = lax.ppermute(right, "slab", rightward)
            left = lax.ppermute(left, "slab", leftward)
        here = z[None].astype(jnp.int32)
        update = finish(r, anti, right, left, eps_pair, eps_virt, here, update)
    return update


def solution(mesh):
    in_specs = (P("pair", "slab"), P("slab", "pair"), P("pair", None), P(), P())
    out_specs = P("pair", "slab")
    return jax.shard_map(
        functools.partial(on_device, mesh),
        mesh=mesh,
        in_specs=in_specs,
        out_specs=out_specs,
        check_vma=False,
    )
```

time: 339 us -> 194 us (0.57)
  waiting for transfers between devices: 176 us -> 52.6 us
  blocking collectives: 82.5 us -> 0 us
  starting transfers between devices: 0.04 us -> 62.7 us
  Pallas kernels: 0 us -> 51.3 us
  other arithmetic: 15.7 us -> 0.58 us
  between operations: 13.5 us -> 0.28 us
  matrix products: 13.1 us -> 0 us
  local copies, waits for them, and re-layouts: 37.4 us -> 25.9 us
    reduce_scatter x1 -> x0, waiting for transfers between devices: 122 us -> none  [on_device(): summed = lax.psum_scatter(antisym, 'slab', scatter_dimension=1, tiled=True)]
    all_to_all x1 -> x0, blocking collectives: 82.5 us -> none  [on_device(): lax.all_to_all(owned_rows, 'pair', split_axis=0, concat_axis=1, tiled=True)]
    ppermute x0 -> x34, starting transfers between devices: none -> 62.7 us  [the longest x6 24.8 us: on_device(): right = lax.ppermute(right, 'slab', rightward)]
    all_gather x1 -> x0, waiting for transfers between devices: 53.5 us -> none  [on_device(): lax.all_gather(amplitudes, 'pair', axis=0, tiled=True)]
    ppermute x0 -> x34, waiting for transfers between devices: none -> 52.6 us  [the longest x18 49.7 us: to_chip(): return lax.ppermute(x, 'pair', [(i, i ^ d * CORES) for i in range(devices)])]
    pallas_call x0 -> x15, Pallas kernels: none -> 51.3 us  [the longest x3 16.3 us: on_device(): anti, one = antisym(place, *arrived)]
    reshape x3 -> x1, local copies, waits for them, and re-layouts: 29.8 us -> 0.08 us  [on_device(): eps_vir.reshape(slabs, 2, half)]
    unnamed x6 -> x43, local copies, waits for them, and re-layouts: 0.6 us -> 25.5 us
  transfers between devices with their start and end apart: 2 -> 34, of which waited for: 2 -> 12; matrix products, arithmetic and copies ran while one was open for 0% -> 1% of each run, Pallas kernels for 0% -> 23%
where the time goes in v2:
time: 194 us; the launch traced here: 193 us
  starting transfers between devices  62.7 us (32%)
  waiting for transfers between devices  52.6 us (27%)
  Pallas kernels  51.3 us (26%)
  local copies, waits for them, and re-layouts  25.9 us (13%)
    ppermute x18, waiting for transfers between devices, to_chip(): return lax.ppermute(x, 'pair', [(i, i ^ d * CORES) for i in range(devices)])  49.7 us
    unnamed x43, local copies, waits for them, and re-layouts  25.5 us
    ppermute x6, starting transfers between devices, on_device(): right = lax.ppermute(right, 'slab', rightward)  24.8 us
    ppermute x18, starting transfers between devices, to_chip(): return lax.ppermute(x, 'pair', [(i, i ^ d * CORES) for i in range(devices)])  22.9 us
    pallas_call x3, Pallas kernels, on_device(): anti, one = antisym(place, *arrived)  16.3 us
    pallas_call x3, Pallas kernels, on_device(): sums = ladder(own_t, sib_t, *gathered[r])  14.2 us
    pallas_call x3, Pallas kernels, on_device(): right, left = hop(2)(targets, anti, anti, right, left)  10.2 us
    ppermute x6, starting transfers between devices, on_device(): left = lax.ppermute(left, 'slab', leftward)  7.69 us
  transfers between devices with their start and end apart: 34, of which 12 were waited for; matrix products, arithmetic and copies ran while one was open for 1% of the time, Pallas kernels for 23%

profile of v2, /device:TPU:0, one launch (start us, length us, event | category | flops | bytes accessed | tf_op | source)
XLA Modules:
  0.0 193.3 jit_solution(10668999385080530062)
XLA Ops:
  0.0 8.6 %copy.10 = bf16[2304,1152]{0,1:T(8,128)(2,1)} copy(bf16[2304,1152]{1,0:T(8,128)(2,1)} %param.6) | data formatting | bytes 10616832 | tf_op args[1]
  9.1 3.5 %collective-permute-start.3 = (bf16[64,2304]{1,0:T(8,128)(2,1)S(1)}, bf16[64,2304]{1,0:T(8,128)(2,1)S(1)}, u32[]{:S(2)}, u32[]{:S(2)}) collective-permute-start(bf16[64,2304]{1,0:T(8,128)(2,1)S(1)} %get-tuple-element.61.refs_0_), channel_id=1, source_target_pairs={{0,24},{4,28},{8,16},{12,20},{16,8},{20,12},{24,0},{28,4},{1,25},{... | collective-permute-start | bytes 884744 | tf_op jit(solution)/shard_map/ppermute | solution.py:144
  13.3 7.3 %collective-permute-done.3.refs_3_ = bf16[64,2304]{1,0:T(8,128)(2,1)S(1)} collective-permute-done((bf16[64,2304]{1,0:T(8,128)(2,1)S(1)}, bf16[64,2304]{1,0:T(8,128)(2,1)S(1)}, u32[]{:S(2)}, u32[]{:S(2)}) %collective-permute-start.3) | collective-permute-done | bytes 294944 | tf_op jit(solution)/shard_map/ppermute | solution.py:144
  20.6 6.1 %collective-permute-done.2.refs_2_ = bf16[64,2304]{1,0:T(8,128)(2,1)S(1)} collective-permute-done((bf16[64,2304]{1,0:T(8,128)(2,1)S(1)}, bf16[64,2304]{1,0:T(8,128)(2,1)S(1)}, u32[]{:S(2)}, u32[]{:S(2)}) %collective-permute-start.2) | collective-permute-done | bytes 294944 | tf_op jit(solution)/shard_map/ppermute | solution.py:144
  26.9 1.5 collective-permute-start.6
  28.5 1.4 collective-permute-start.5
  30.4 7.4 %collective-permute-done.6.refs_3_ = bf16[64,2304]{1,0:T(8,128)(2,1)S(1)} collective-permute-done((bf16[64,2304]{1,0:T(8,128)(2,1)S(1)}, bf16[64,2304]{1,0:T(8,128)(2,1)S(1)}, u32[]{:S(2)}, u32[]{:S(2)}) %collective-permute-start.6) | collective-permute-done | bytes 294944 | tf_op jit(solution)/shard_map/ppermute | solution.py:144
  37.8 5.0 %collective-permute-done.5.refs_2_ = bf16[64,2304]{1,0:T(8,128)(2,1)S(1)} collective-permute-done((bf16[64,2304]{1,0:T(8,128)(2,1)S(1)}, bf16[64,2304]{1,0:T(8,128)(2,1)S(1)}, u32[]{:S(2)}, u32[]{:S(2)}) %collective-permute-start.5) | collective-permute-done | bytes 294944 | tf_op jit(solution)/shard_map/ppermute | solution.py:144
  43.1 1.4 collective-permute-start.9
  46.6 7.4 %collective-permute-done.9.refs_3_ = bf16[64,2304]{1,0:T(8,128)(2,1)S(1)} collective-permute-done((bf16[64,2304]{1,0:T(8,128)(2,1)S(1)}, bf16[64,2304]{1,0:T(8,128)(2,1)S(1)}, u32[]{:S(2)}, u32[]{:S(2)}) %collective-permute-start.9) | collective-permute-done | bytes 294944 | tf_op jit(solution)/shard_map/ppermute | solution.py:144
  54.0 5.0 %collective-permute-done.8.refs_2_ = bf16[64,2304]{1,0:T(8,128)(2,1)S(1)} collective-permute-done((bf16[64,2304]{1,0:T(8,128)(2,1)S(1)}, bf16[64,2304]{1,0:T(8,128)(2,1)S(1)}, u32[]{:S(2)}, u32[]{:S(2)}) %collective-permute-start.8) | collective-permute-done | bytes 294944 | tf_op jit(solution)/shard_map/ppermute | solution.py:144
  59.3 2.5 %copy-done = bf16[2304,1152]{0,1:T(8,128)(2,1)S(1)} copy-done((bf16[2304,1152]{0,1:T(8,128)(2,1)S(1)}, bf16[2304,1152]{0,1:T(8,128)(2,1)}, u32[]{:S(2)}) %copy-start) | copy-done | bytes 5308440
  61.8 4.9 %ladder.3 = (s16[3,400,128]{2,1,0:T(8,128)(2,1)S(1)}, s16[3,400,128]{2,1,0:T(8,128)(2,1)}, s16[3,400,128]{2,1,0:T(8,128)(2,1)S(1)}, s16[3,400,128]{2,1,0:T(8,128)(2,1)S(1)}) custom-call(bf16[1152,2304]{1,0:T(8,128)(2,1)S(1)} %bitcast.15, bf16[1152,2304]{1,0:T(8,128)(2,1)S(1)} %collective-permute-done.sib_ref, ...), custom_call_target="tpu_custom_call" | custom-call | flops 2717908992 | bytes 12976128 | tf_op jit(solution)/shard_map/ladder/pallas_call | solution.py:258
  68.8 5.0 %ladder.5 = (s16[3,400,128]{2,1,0:T(8,128)(2,1)S(1)}, s16[3,400,128]{2,1,0:T(8,128)(2,1)}, s16[3,400,128]{2,1,0:T(8,128)(2,1)}, s16[3,400,128]{2,1,0:T(8,128)(2,1)}) custom-call(bf16[1152,2304]{1,0:T(8,128)(2,1)S(1)} %bitcast.16, bf16[1152,2304]{1,0:T(8,128)(2,1)S(1)} %collective-permute-done.sib_ref, bf16[64,2304]{1,0:T(8,128)(2,1)S(1)} %get-tuple-element.61.refs_0_, ...), custom_call_target="tpu_custom_call" | custom-call | flops 2717908992 | bytes 12976128 | tf_op jit(solution)/shard_map/ladder/pallas_call | solution.py:258
  74.4 1.4 collective-permute-start.27
  75.9 1.4 collective-permute-start.28
  77.9 1.5 collective-permute-start.12
  79.4 2.5 %copy-done.1 = bf16[2304,1152]{0,1:T(8,128)(2,1)S(1)} copy-done((bf16[2304,1152]{0,1:T(8,128)(2,1)S(1)}, bf16[2304,1152]{0,1:T(8,128)(2,1)}, u32[]{:S(2)}) %copy-start.1) | copy-done | bytes 5308440
  81.9 2.5 %copy-done.3 = bf16[1152,2304]{1,0:T(8,128)(2,1)S(1)} copy-done((bf16[1152,2304]{1,0:T(8,128)(2,1)S(1)}, bf16[1152,2304]{1,0:T(8,128)(2,1)}, u32[]{:S(2)}) %copy-start.3) | copy-done | bytes 5308440
  84.4 4.3 %ladder.4 = (s16[3,400,128]{2,1,0:T(8,128)(2,1)S(1)}, s16[3,400,128]{2,1,0:T(8,128)(2,1)S(1)}, s16[3,400,128]{2,1,0:T(8,128)(2,1)S(1)}, s16[3,400,128]{2,1,0:T(8,128)(2,1)S(1)}) custom-call(bf16[1152,2304]{1,0:T(8,128)(2,1)S(1)} %bitcast.17, bf16[1152,2304]{1,0:T(8,128)(2,1)S(1)} %copy-done.3, bf16[64,2304]{1,0:T(8,128)(2,1)S(1)} %get-tuple-element.49.refs_0_, ...), custom_call_target="tpu_custom_call" | custom-call | flops 2717908992 | bytes 12976128 | tf_op jit(solution)/shard_map/ladder/pallas_call | solution.py:258
  88.7 1.5 collective-permute-start.18
  90.2 7.4 %collective-permute-done.27.refs_2_ = s16[3,400,128]{2,1,0:T(8,128)(2,1)S(1)} collective-permute-done((s16[3,400,128]{2,1,0:T(8,128)(2,1)}, s16[3,400,128]{2,1,0:T(8,128)(2,1)S(1)}, u32[]{:S(2)}, u32[]{:S(2)}) %collective-permute-start.27) | collective-permute-done | bytes 307232 | tf_op jit(solution)/shard_map/ppermute | solution.py:144
  97.6 1.9 collective-permute-start.19
  99.5 1.4 collective-permute-start.20
  101.0 5.4 %antisym.5 = (f32[4,1152,128]{2,1,0:T(8,128)S(1)}, s16[3,400,128]{2,1,0:T(8,128)(2,1)}) custom-call(s32[3]{0:T(128)S(1)} %pad_add_fusion.place_ref, s16[3,400,128]{2,1,0:T(8,128)(2,1)S(1)} %get-tuple-element.65.refs_0_, s16[3,400,128]{2,1,0:T(8,128)(2,1)S(1)} %collective-permute-done.26.refs_1_, s16[3,400,128]{2,1,0:T(8,128)(2,1)S(1)} %collective-permute-done.27.refs_2_, ...), custom_call_target="tpu_custom_call" | custom-call | flops 9437184 | bytes 4718592 | tf_op jit(solution)/shard_map/antisym/pallas_call | solution.py:260
  106.4 1.5 copy-done.8
  107.9 3.3 %collective-permute-done.11.refs_2_ = s16[3,400,128]{2,1,0:T(8,128)(2,1)S(1)} collective-permute-done((s16[3,400,128]{2,1,0:T(8,128)(2,1)}, s16[3,400,128]{2,1,0:T(8,128)(2,1)S(1)}, u32[]{:S(2)}, u32[]{:S(2)}) %collective-permute-start.11) | collective-permute-done | bytes 307232 | tf_op jit(solution)/shard_map/ppermute | solution.py:144
  111.2 3.5 %collective-permute-start.29 = (s16[3,400,128]{2,1,0:T(8,128)(2,1)}, s16[3,400,128]{2,1,0:T(8,128)(2,1)S(1)}, u32[]{:S(2)}, u32[]{:S(2)}) collective-permute-start(s16[3,400,128]{2,1,0:T(8,128)(2,1)} %get-tuple-element.70), channel_id=1, source_target_pairs={{0,1},{3,2},{4,5},{7,6},{8,9},{11,10},{12,13},{15,14},{16,17},{19,... | collective-permute-start | bytes 921608 | tf_op jit(solution)/shard_map/ppermute | solution.py:272
  114.7 5.4 %antisym.3 = (f32[4,1152,128]{2,1,0:T(8,128)S(1)}, s16[3,400,128]{2,1,0:T(8,128)(2,1)}) custom-call(s32[3]{0:T(128)S(1)} %pad_add_fusion.place_ref, s16[3,400,128]{2,1,0:T(8,128)(2,1)S(1)} %get-tuple-element.41.refs_0_, s16[3,400,128]{2,1,0:T(8,128)(2,1)S(1)} %collective-permute-done.10.refs_1_, s16[3,400,128]{2,1,0:T(8,128)(2,1)S(1)} %collective-permute-done.11.refs_2_, ...), custom_call_target="tpu_custom_call" | custom-call | flops 9437184 | bytes 4718592 | tf_op jit(solution)/shard_map/antisym/pallas_call | solution.py:260
  121.5 5.4 %antisym.4 = (f32[4,1152,128]{2,1,0:T(8,128)S(1)}, s16[3,400,128]{2,1,0:T(8,128)(2,1)}) custom-call(s32[3]{0:T(128)S(1)} %pad_add_fusion.place_ref, s16[3,400,128]{2,1,0:T(8,128)(2,1)S(1)} %get-tuple-element.53.refs_0_, s16[3,400,128]{2,1,0:T(8,128)(2,1)S(1)} %collective-permute-done.18.refs_1_, s16[3,400,128]{2,1,0:T(8,128)(2,1)S(1)} %collective-permute-done.19.refs_2_, ...), custom_call_target="tpu_custom_call" | custom-call | flops 9437184 | bytes 4718592 | tf_op jit(solution)/shard_map/antisym/pallas_call | solution.py:260
  128.3 2.0 %collective-permute-start.21 = (s16[3,400,128]{2,1,0:T(8,128)(2,1)}, s16[3,400,128]{2,1,0:T(8,128)(2,1)}, u32[]{:S(2)}, u32[]{:S(2)}) collective-permute-start(s16[3,400,128]{2,1,0:T(8,128)(2,1)} %get-tuple-element.58), channel_id=1, source_target_pairs={{0,1},{3,2},{4,5},{7,6},{8,9},{11,10},{12,13},{15,14},{16,17},{19,... | collective-permute-start | bytes 921608 | tf_op jit(solution)/shard_map/ppermute | solution.py:272
  130.3 1.7 copy-done.9
  132.0 1.4 hop.10
  134.8 2.0 %collective-permute-start.30 = (s16[3,400,128]{2,1,0:T(8,128)(2,1)}, s16[3,400,128]{2,1,0:T(8,128)(2,1)}, u32[]{:S(2)}, u32[]{:S(2)}) collective-permute-start(s16[3,400,128]{2,1,0:T(8,128)(2,1)} %hop.10), channel_id=1, source_target_pairs={{0,1},{1,2},{4,5},{5,6},{8,9},{9,10},{12,13},{13,14},{16,17},{17,1... | collective-permute-start | bytes 921608 | tf_op jit(solution)/shard_map/ppermute | solution.py:278
  137.1 1.5 collective-permute-start.15
  138.7 3.8 %collective-permute-start.14 = (s16[3,400,128]{2,1,0:T(8,128)(2,1)S(1)}, s16[3,400,128]{2,1,0:T(8,128)(2,1)}, u32[]{:S(2)}, u32[]{:S(2)}) collective-permute-start(s16[3,400,128]{2,1,0:T(8,128)(2,1)S(1)} %hop.6), channel_id=1, source_target_pairs={{0,1},{1,2},{4,5},{5,6},{8,9},{9,10},{12,13},{13,14},{16,17},{17,1... | collective-permute-start | bytes 921608 | tf_op jit(solution)/shard_map/ppermute | solution.py:278
  142.5 2.6 %hop.8 = s16[3,400,128]{2,1,0:T(8,128)(2,1)} custom-call(s32[1]{0:T(128)} %bitcast.6.place_ref, f32[4,1152,128]{2,1,0:T(8,128)S(1)} %copy-done.5, s16[3,400,128]{2,1,0:T(8,128)(2,1)} %collective-permute-done.21.refs_1_), custom_call_target="tpu_custom_call" | custom-call | flops 1179648 | bytes 1179648 | tf_op jit(solution)/shard_map/hop/pallas_call | solution.py:270
  145.9 5.3 %collective-permute-start.22 = (s16[3,400,128]{2,1,0:T(8,128)(2,1)}, s16[3,400,128]{2,1,0:T(8,128)(2,1)}, u32[]{:S(2)}, u32[]{:S(2)}) collective-permute-start(s16[3,400,128]{2,1,0:T(8,128)(2,1)} %hop.8), channel_id=1, source_target_pairs={{0,1},{1,2},{4,5},{5,6},{8,9},{9,10},{12,13},{13,14},{16,17},{17,1... | collective-permute-start | bytes 921608 | tf_op jit(solution)/shard_map/ppermute | solution.py:278
  151.2 3.3 %hop.11 = (s16[3,400,128]{2,1,0:T(8,128)(2,1)}, s16[3,400,128]{2,1,0:T(8,128)(2,1)S(1)}) custom-call(s32[2]{0:T(128)S(1)} %add_clamp_fusion.place_ref, f32[4,1152,128]{2,1,0:T(8,128)S(1)} %copy-done.10, f32[4,1152,128]{2,1,0:T(8,128)S(1)} %copy-done.10, s16[3,400,128]{2,1,0:T(8,128)(2,1)} %collective-permute-done.30.refs_2_, ...), custom_call_target="tpu_custom_call" | custom-call | flops 2359296 | bytes 2359296 | tf_op jit(solution)/shard_map/hop/pallas_call | solution.py:277
  155.3 3.8 %collective-permute-start.32 = (s16[3,400,128]{2,1,0:T(8,128)(2,1)}, s16[3,400,128]{2,1,0:T(8,128)(2,1)S(1)}, u32[]{:S(2)}, u32[]{:S(2)}) collective-permute-start(s16[3,400,128]{2,1,0:T(8,128)(2,1)} %get-tuple-element.71), channel_id=1, source_target_pairs={{0,1},{1,2},{2,3},{4,5},{5,6},{6,7},{8,9},{9,10},{10,11},{12,13},{... | collective-permute-start | bytes 921608 | tf_op jit(solution)/shard_map/ppermute | solution.py:278
  160.6 3.5 %hop.7 = (s16[3,400,128]{2,1,0:T(8,128)(2,1)}, s16[3,400,128]{2,1,0:T(8,128)(2,1)}) custom-call(s32[2]{0:T(128)S(1)} %add_clamp_fusion.place_ref, f32[4,1152,128]{2,1,0:T(8,128)S(1)} %get-tuple-element.45.refs_0_.refs_1_.anti, f32[4,1152,128]{2,1,0:T(8,128)S(1)} %get-tuple-element.45.refs_0_.refs_1_.anti, ...), custom_call_target="tpu_custom_call" | custom-call | flops 2359296 | bytes 2359296 | tf_op jit(solution)/shard_map/hop/pallas_call | solution.py:277
  164.1 4.6 %collective-permute-start.16 = (s16[3,400,128]{2,1,0:T(8,128)(2,1)}, s16[3,400,128]{2,1,0:T(8,128)(2,1)S(1)}, u32[]{:S(2)}, u32[]{:S(2)}) collective-permute-start(s16[3,400,128]{2,1,0:T(8,128)(2,1)} %get-tuple-element.47), channel_id=1, source_target_pairs={{0,1},{1,2},{2,3},{4,5},{5,6},{6,7},{8,9},{9,10},{10,11},{12,13},{... | collective-permute-start | bytes 921608 | tf_op jit(solution)/shard_map/ppermute | solution.py:278
  171.8 3.3 %hop.9 = (s16[3,400,128]{2,1,0:T(8,128)(2,1)}, s16[3,400,128]{2,1,0:T(8,128)(2,1)}) custom-call(s32[2]{0:T(128)S(1)} %add_clamp_fusion.place_ref, f32[4,1152,128]{2,1,0:T(8,128)S(1)} %copy-done.6, f32[4,1152,128]{2,1,0:T(8,128)S(1)} %copy-done.6, s16[3,400,128]{2,1,0:T(8,128)(2,1)} %collective-permute-done.22.refs_2_, s16[3,400,128]{2,1,0:T(8,128)(2,1)S(1)} %copy-done.13), custom_call_target="tpu_custom_call" | custom-call | flops 2359296 | bytes 2359296 | tf_op jit(solution)/shard_map/hop/pallas_call | solution.py:277
  175.1 5.3 %collective-permute-start.24 = (s16[3,400,128]{2,1,0:T(8,128)(2,1)}, s16[3,400,128]{2,1,0:T(8,128)(2,1)}, u32[]{:S(2)}, u32[]{:S(2)}) collective-permute-start(s16[3,400,128]{2,1,0:T(8,128)(2,1)} %get-tuple-element.59), channel_id=1, source_target_pairs={{0,1},{1,2},{2,3},{4,5},{5,6},{6,7},{8,9},{9,10},{10,11},{12,13},{... | collective-permute-start | bytes 921608 | tf_op jit(solution)/shard_map/ppermute | solution.py:278
  182.5 1.7 copy-done.11
  184.2 2.5 %finish.3.refs_0_ = f32[192,2304]{1,0:T(8,128)} custom-call(s32[1]{0:T(128)} %bitcast.place_ref, f32[4,1152,128]{2,1,0:T(8,128)S(1)} %copy-done.11, s16[3,400,128]{2,1,0:T(8,128)(2,1)S(1)} %collective-permute-done.32.got_r, s16[3,400,128]{2,1,0:T(8,128)(2,1)} %collective-permute-done.33.got_l, f32[3,1,128]{2,1,0:T(1,128)S(1)} %pad_maximum_fusion.pair_ref, ...), custom_call_target="tpu_custom_call" | custom-call | flops 2359296 | bytes 2359296 | tf_op jit(solution)/shard_map/finish/pallas_call | solution.py:211
  186.7 2.8 %collective-permute-done.25.got_l = s16[3,400,128]{2,1,0:T(8,128)(2,1)} collective-permute-done((s16[3,400,128]{2,1,0:T(8,128)(2,1)}, s16[3,400,128]{2,1,0:T(8,128)(2,1)}, u32[]{:S(2)}, u32[]{:S(2)}) %collective-permute-start.25) | collective-permute-done | bytes 307232 | tf_op jit(solution)/shard_map/ppermute | solution.py:279
  189.5 2.5 %finish.4.refs_0_ = f32[192,2304]{1,0:T(8,128)} custom-call(s32[1]{0:T(128)} %bitcast.place_ref, f32[4,1152,128]{2,1,0:T(8,128)S(1)} %copy-done.7, s16[3,400,128]{2,1,0:T(8,128)(2,1)} %collective-permute-done.24.got_r, s16[3,400,128]{2,1,0:T(8,128)(2,1)} %collective-permute-done.25.got_l, ...), custom_call_target="tpu_custom_call", output_to_operand_aliasing={{}: (6, {})} | custom-call | flops 2359296 | bytes 2359296 | tf_op jit(solution)/shard_map/finish/pallas_call | solution.py:211
  (92 shorter events, 21.9 us)
Async XLA Ops:
  0.0 9.1 %copy-start.17 = (bf16[192,2304]{1,0:T(8,128)(2,1)S(1)}, bf16[192,2304]{1,0:T(8,128)(2,1)}, u32[]{:S(2)}) copy-start(bf16[192,2304]{1,0:T(8,128)(2,1)} %param.5) | copy-start | bytes 2654212
  8.6 50.7 %collective-permute-start = (bf16[1152,2304]{1,0:T(8,128)(2,1)}, bf16[1152,2304]{1,0:T(8,128)(2,1)S(1)}, u32[]{:S(2)}, u32[]{:S(2)}) collective-permute-start(bf16[1152,2304]{1,0:T(8,128)(2,1)} %bitcast.14), channel_id=1, source_target_pairs={{0,4},{4,0},{8,12},{12,8},{16,20},{20,16},{24,28},{28,24},{1,5},{5... | collective-permute-start | bytes 15925256 | tf_op jit(solution)/shard_map/ppermute | solution.py:234
  9.1 11.4 %collective-permute-start.3 = (bf16[64,2304]{1,0:T(8,128)(2,1)S(1)}, bf16[64,2304]{1,0:T(8,128)(2,1)S(1)}, u32[]{:S(2)}, u32[]{:S(2)}) collective-permute-start(bf16[64,2304]{1,0:T(8,128)(2,1)S(1)} %get-tuple-element.61.refs_0_), channel_id=1, source_target_pairs={{0,24},{4,28},{8,16},{12,20},{16,8},{20,12},{24,0},{28,4},{1,25},{... | collective-permute-start | bytes 884744 | tf_op jit(solution)/shard_map/ppermute | solution.py:144
  12.7 14.0 %collective-permute-start.2 = (bf16[64,2304]{1,0:T(8,128)(2,1)S(1)}, bf16[64,2304]{1,0:T(8,128)(2,1)S(1)}, u32[]{:S(2)}, u32[]{:S(2)}) collective-permute-start(bf16[64,2304]{1,0:T(8,128)(2,1)S(1)} %get-tuple-element.61.refs_0_), channel_id=1, source_target_pairs={{0,16},{4,20},{8,24},{12,28},{16,0},{20,4},{24,8},{28,12},{1,17},{... | collective-permute-start | bytes 884744 | tf_op jit(solution)/shard_map/ppermute | solution.py:144
  13.2 13.8 %collective-permute-start.1 = (bf16[64,2304]{1,0:T(8,128)(2,1)S(1)}, bf16[64,2304]{1,0:T(8,128)(2,1)S(1)}, u32[]{:S(2)}, u32[]{:S(2)}) collective-permute-start(bf16[64,2304]{1,0:T(8,128)(2,1)S(1)} %get-tuple-element.61.refs_0_), channel_id=1, source_target_pairs={{0,8},{4,12},{8,0},{12,4},{16,24},{20,28},{24,16},{28,20},{1,9},{5... | collective-permute-start | bytes 884744 | tf_op jit(solution)/shard_map/ppermute | solution.py:144
  26.9 10.9 %collective-permute-start.6 = (bf16[64,2304]{1,0:T(8,128)(2,1)S(1)}, bf16[64,2304]{1,0:T(8,128)(2,1)S(1)}, u32[]{:S(2)}, u32[]{:S(2)}) collective-permute-start(bf16[64,2304]{1,0:T(8,128)(2,1)S(1)} %get-tuple-element.49.refs_0_), channel_id=1, source_target_pairs={{0,24},{4,28},{8,16},{12,20},{16,8},{20,12},{24,0},{28,4},{1,25},{... | collective-permute-start | bytes 884744 | tf_op jit(solution)/shard_map/ppermute | solution.py:144
  28.5 14.4 %collective-permute-start.5 = (bf16[64,2304]{1,0:T(8,128)(2,1)S(1)}, bf16[64,2304]{1,0:T(8,128)(2,1)S(1)}, u32[]{:S(2)}, u32[]{:S(2)}) collective-permute-start(bf16[64,2304]{1,0:T(8,128)(2,1)S(1)} %get-tuple-element.49.refs_0_), channel_id=1, source_target_pairs={{0,16},{4,20},{8,24},{12,28},{16,0},{20,4},{24,8},{28,12},{1,17},{... | collective-permute-start | bytes 884744 | tf_op jit(solution)/shard_map/ppermute | solution.py:144
  29.9 13.2 %collective-permute-start.4 = (bf16[64,2304]{1,0:T(8,128)(2,1)S(1)}, bf16[64,2304]{1,0:T(8,128)(2,1)S(1)}, u32[]{:S(2)}, u32[]{:S(2)}) collective-permute-start(bf16[64,2304]{1,0:T(8,128)(2,1)S(1)} %get-tuple-element.49.refs_0_), channel_id=1, source_target_pairs={{0,8},{4,12},{8,0},{12,4},{16,24},{20,28},{24,16},{28,20},{1,9},{5... | collective-permute-start | bytes 884744 | tf_op jit(solution)/shard_map/ppermute | solution.py:144
  43.1 10.9 %collective-permute-start.9 = (bf16[64,2304]{1,0:T(8,128)(2,1)S(1)}, bf16[64,2304]{1,0:T(8,128)(2,1)S(1)}, u32[]{:S(2)}, u32[]{:S(2)}) collective-permute-start(bf16[64,2304]{1,0:T(8,128)(2,1)S(1)} %get-tuple-element.40.refs_0_), channel_id=1, source_target_pairs={{0,24},{4,28},{8,16},{12,20},{16,8},{20,12},{24,0},{28,4},{1,25},{... | collective-permute-start | bytes 884744 | tf_op jit(solution)/shard_map/ppermute | solution.py:144
  44.6 14.4 %collective-permute-start.8 = (bf16[64,2304]{1,0:T(8,128)(2,1)S(1)}, bf16[64,2304]{1,0:T(8,128)(2,1)S(1)}, u32[]{:S(2)}, u32[]{:S(2)}) collective-permute-start(bf16[64,2304]{1,0:T(8,128)(2,1)S(1)} %get-tuple-element.40.refs_0_), channel_id=1, source_target_pairs={{0,16},{4,20},{8,24},{12,28},{16,0},{20,4},{24,8},{28,12},{1,17},{... | collective-permute-start | bytes 884744 | tf_op jit(solution)/shard_map/ppermute | solution.py:144
  46.0 13.3 %collective-permute-start.7 = (bf16[64,2304]{1,0:T(8,128)(2,1)S(1)}, bf16[64,2304]{1,0:T(8,128)(2,1)S(1)}, u32[]{:S(2)}, u32[]{:S(2)}) collective-permute-start(bf16[64,2304]{1,0:T(8,128)(2,1)S(1)} %get-tuple-element.40.refs_0_), channel_id=1, source_target_pairs={{0,8},{4,12},{8,0},{12,4},{16,24},{20,28},{24,16},{28,20},{1,9},{5... | collective-permute-start | bytes 884744 | tf_op jit(solution)/shard_map/ppermute | solution.py:144
  59.3 2.5 %copy-start = (bf16[2304,1152]{0,1:T(8,128)(2,1)S(1)}, bf16[2304,1152]{0,1:T(8,128)(2,1)}, u32[]{:S(2)}) copy-start(bf16[2304,1152]{0,1:T(8,128)(2,1)} %copy.10) | copy-start | bytes 15925252
  61.8 7.0 %copy-start.2 = (bf16[1152,2304]{1,0:T(8,128)(2,1)}, bf16[1152,2304]{1,0:T(8,128)(2,1)S(1)}, u32[]{:S(2)}) copy-start(bf16[1152,2304]{1,0:T(8,128)(2,1)S(1)} %collective-permute-done.sib_ref) | copy-start | bytes 15925252
  67.4 6.4 %copy-start.14 = (s16[3,400,128]{2,1,0:T(8,128)(2,1)}, s16[3,400,128]{2,1,0:T(8,128)(2,1)S(1)}, u32[]{:S(2)}) copy-start(s16[3,400,128]{2,1,0:T(8,128)(2,1)S(1)} %get-tuple-element.44) | copy-start | bytes 921604
  67.4 10.5 %collective-permute-start.10 = (s16[3,400,128]{2,1,0:T(8,128)(2,1)}, s16[3,400,128]{2,1,0:T(8,128)(2,1)S(1)}, u32[]{:S(2)}, u32[]{:S(2)}) collective-permute-start(s16[3,400,128]{2,1,0:T(8,128)(2,1)} %get-tuple-element.42), channel_id=1, source_target_pairs={{0,8},{4,12},{8,0},{12,4},{16,24},{20,28},{24,16},{28,20},{1,9},{5... | collective-permute-start | bytes 921608 | tf_op jit(solution)/shard_map/ppermute | solution.py:144
  73.8 14.9 %collective-permute-start.26 = (s16[3,400,128]{2,1,0:T(8,128)(2,1)}, s16[3,400,128]{2,1,0:T(8,128)(2,1)S(1)}, u32[]{:S(2)}, u32[]{:S(2)}) collective-permute-start(s16[3,400,128]{2,1,0:T(8,128)(2,1)} %get-tuple-element.66), channel_id=1, source_target_pairs={{0,8},{4,12},{8,0},{12,4},{16,24},{20,28},{24,16},{28,20},{1,9},{5... | collective-permute-start | bytes 921608 | tf_op jit(solution)/shard_map/ppermute | solution.py:144
  74.4 23.2 %collective-permute-start.27 = (s16[3,400,128]{2,1,0:T(8,128)(2,1)}, s16[3,400,128]{2,1,0:T(8,128)(2,1)S(1)}, u32[]{:S(2)}, u32[]{:S(2)}) collective-permute-start(s16[3,400,128]{2,1,0:T(8,128)(2,1)} %get-tuple-element.67), channel_id=1, source_target_pairs={{0,16},{4,20},{8,24},{12,28},{16,0},{20,4},{24,8},{28,12},{1,17},{... | collective-permute-start | bytes 921608 | tf_op jit(solution)/shard_map/ppermute | solution.py:144
  75.9 23.6 %collective-permute-start.28 = (s16[3,400,128]{2,1,0:T(8,128)(2,1)}, s16[3,400,128]{2,1,0:T(8,128)(2,1)S(1)}, u32[]{:S(2)}, u32[]{:S(2)}) collective-permute-start(s16[3,400,128]{2,1,0:T(8,128)(2,1)} %get-tuple-element.68), channel_id=1, source_target_pairs={{0,24},{4,28},{8,16},{12,20},{16,8},{20,12},{24,0},{28,4},{1,25},{... | collective-permute-start | bytes 921608 | tf_op jit(solution)/shard_map/ppermute | solution.py:144
  77.3 33.9 %collective-permute-start.11 = (s16[3,400,128]{2,1,0:T(8,128)(2,1)}, s16[3,400,128]{2,1,0:T(8,128)(2,1)S(1)}, u32[]{:S(2)}, u32[]{:S(2)}) collective-permute-start(s16[3,400,128]{2,1,0:T(8,128)(2,1)} %copy-done.15), channel_id=1, source_target_pairs={{0,16},{4,20},{8,24},{12,28},{16,0},{20,4},{24,8},{28,12},{1,17},{... | collective-permute-start | bytes 921608 | tf_op jit(solution)/shard_map/ppermute | solution.py:144
  77.9 36.8 %collective-permute-start.12 = (s16[3,400,128]{2,1,0:T(8,128)(2,1)}, s16[3,400,128]{2,1,0:T(8,128)(2,1)S(1)}, u32[]{:S(2)}, u32[]{:S(2)}) collective-permute-start(s16[3,400,128]{2,1,0:T(8,128)(2,1)} %copy-done.14), channel_id=1, source_target_pairs={{0,24},{4,28},{8,16},{12,20},{16,8},{20,12},{24,0},{28,4},{1,25},{... | collective-permute-start | bytes 921608 | tf_op jit(solution)/shard_map/ppermute | solution.py:144
  79.4 2.5 %copy-start.1 = (bf16[2304,1152]{0,1:T(8,128)(2,1)S(1)}, bf16[2304,1152]{0,1:T(8,128)(2,1)}, u32[]{:S(2)}) copy-start(bf16[2304,1152]{0,1:T(8,128)(2,1)} %copy.10) | copy-start | bytes 15925252
  81.9 2.5 %copy-start.3 = (bf16[1152,2304]{1,0:T(8,128)(2,1)S(1)}, bf16[1152,2304]{1,0:T(8,128)(2,1)}, u32[]{:S(2)}) copy-start(bf16[1152,2304]{1,0:T(8,128)(2,1)} %copy-done.2) | copy-start | bytes 15925252
  88.7 32.8 %collective-permute-start.18 = (s16[3,400,128]{2,1,0:T(8,128)(2,1)S(1)}, s16[3,400,128]{2,1,0:T(8,128)(2,1)S(1)}, u32[]{:S(2)}, u32[]{:S(2)}) collective-permute-start(s16[3,400,128]{2,1,0:T(8,128)(2,1)S(1)} %get-tuple-element.54), channel_id=1, source_target_pairs={{0,8},{4,12},{8,0},{12,4},{16,24},{20,28},{24,16},{28,20},{1,9},{5... | collective-permute-start | bytes 921608 | tf_op jit(solution)/shard_map/ppermute | solution.py:144
  97.6 23.9 %collective-permute-start.19 = (s16[3,400,128]{2,1,0:T(8,128)(2,1)S(1)}, s16[3,400,128]{2,1,0:T(8,128)(2,1)S(1)}, u32[]{:S(2)}, u32[]{:S(2)}) collective-permute-start(s16[3,400,128]{2,1,0:T(8,128)(2,1)S(1)} %get-tuple-element.55), channel_id=1, source_target_pairs={{0,16},{4,20},{8,24},{12,28},{16,0},{20,4},{24,8},{28,12},{1,17},{... | collective-permute-start | bytes 921608 | tf_op jit(solution)/shard_map/ppermute | solution.py:144
  99.5 22.0 %collective-permute-start.20 = (s16[3,400,128]{2,1,0:T(8,128)(2,1)S(1)}, s16[3,400,128]{2,1,0:T(8,128)(2,1)S(1)}, u32[]{:S(2)}, u32[]{:S(2)}) collective-permute-start(s16[3,400,128]{2,1,0:T(8,128)(2,1)S(1)} %get-tuple-element.56), channel_id=1, source_target_pairs={{0,24},{4,28},{8,16},{12,20},{16,8},{20,12},{24,0},{28,4},{1,25},{... | collective-permute-start | bytes 921608 | tf_op jit(solution)/shard_map/ppermute | solution.py:144
  111.2 19.2 %collective-permute-start.29 = (s16[3,400,128]{2,1,0:T(8,128)(2,1)}, s16[3,400,128]{2,1,0:T(8,128)(2,1)S(1)}, u32[]{:S(2)}, u32[]{:S(2)}) collective-permute-start(s16[3,400,128]{2,1,0:T(8,128)(2,1)} %get-tuple-element.70), channel_id=1, source_target_pairs={{0,1},{3,2},{4,5},{7,6},{8,9},{11,10},{12,13},{15,14},{16,17},{19,... | collective-permute-start | bytes 921608 | tf_op jit(solution)/shard_map/ppermute | solution.py:272
  120.2 16.7 %collective-permute-start.13 = (s16[3,400,128]{2,1,0:T(8,128)(2,1)}, s16[3,400,128]{2,1,0:T(8,128)(2,1)S(1)}, u32[]{:S(2)}, u32[]{:S(2)}) collective-permute-start(s16[3,400,128]{2,1,0:T(8,128)(2,1)} %get-tuple-element.46), channel_id=1, source_target_pairs={{0,1},{3,2},{4,5},{7,6},{8,9},{11,10},{12,13},{15,14},{16,17},{19,... | collective-permute-start | bytes 921608 | tf_op jit(solution)/shard_map/ppermute | solution.py:272
  128.3 14.1 %collective-permute-start.21 = (s16[3,400,128]{2,1,0:T(8,128)(2,1)}, s16[3,400,128]{2,1,0:T(8,128)(2,1)}, u32[]{:S(2)}, u32[]{:S(2)}) collective-permute-start(s16[3,400,128]{2,1,0:T(8,128)(2,1)} %get-tuple-element.58), channel_id=1, source_target_pairs={{0,1},{3,2},{4,5},{7,6},{8,9},{11,10},{12,13},{15,14},{16,17},{19,... | collective-permute-start | bytes 921608 | tf_op jit(solution)/shard_map/ppermute | solution.py:272
  133.4 12.4 %collective-permute-start.31 = (s16[3,400,128]{2,1,0:T(8,128)(2,1)}, s16[3,400,128]{2,1,0:T(8,128)(2,1)}, u32[]{:S(2)}, u32[]{:S(2)}) collective-permute-start(s16[3,400,128]{2,1,0:T(8,128)(2,1)} %hop.10), channel_id=1, source_target_pairs={{2,1},{3,2},{6,5},{7,6},{10,9},{11,10},{14,13},{15,14},{18,17},{19... | collective-permute-start | bytes 921608 | tf_op jit(solution)/shard_map/ppermute | solution.py:279
  134.8 16.4 %collective-permute-start.30 = (s16[3,400,128]{2,1,0:T(8,128)(2,1)}, s16[3,400,128]{2,1,0:T(8,128)(2,1)}, u32[]{:S(2)}, u32[]{:S(2)}) collective-permute-start(s16[3,400,128]{2,1,0:T(8,128)(2,1)} %hop.10), channel_id=1, source_target_pairs={{0,1},{1,2},{4,5},{5,6},{8,9},{9,10},{12,13},{13,14},{16,17},{17,1... | collective-permute-start | bytes 921608 | tf_op jit(solution)/shard_map/ppermute | solution.py:278
  136.8 5.6 %copy-start.5 = (f32[4,1152,128]{2,1,0:T(8,128)S(1)}, f32[4,1152,128]{2,1,0:T(8,128)}, u32[]{:S(2)}) copy-start(f32[4,1152,128]{2,1,0:T(8,128)} %copy-done.4) | copy-start | bytes 7077892
  136.8 14.4 %copy-start.10 = (f32[4,1152,128]{2,1,0:T(8,128)S(1)}, f32[4,1152,128]{2,1,0:T(8,128)}, u32[]{:S(2)}) copy-start(f32[4,1152,128]{2,1,0:T(8,128)} %copy-done.8) | copy-start | bytes 7077892
  137.1 22.0 %collective-permute-start.15 = (s16[3,400,128]{2,1,0:T(8,128)(2,1)S(1)}, s16[3,400,128]{2,1,0:T(8,128)(2,1)}, u32[]{:S(2)}, u32[]{:S(2)}) collective-permute-start(s16[3,400,128]{2,1,0:T(8,128)(2,1)S(1)} %hop.6), channel_id=1, source_target_pairs={{2,1},{3,2},{6,5},{7,6},{10,9},{11,10},{14,13},{15,14},{18,17},{19... | collective-permute-start | bytes 921608 | tf_op jit(solution)/shard_map/ppermute | solution.py:279
  138.7 21.9 %collective-permute-start.14 = (s16[3,400,128]{2,1,0:T(8,128)(2,1)S(1)}, s16[3,400,128]{2,1,0:T(8,128)(2,1)}, u32[]{:S(2)}, u32[]{:S(2)}) collective-permute-start(s16[3,400,128]{2,1,0:T(8,128)(2,1)S(1)} %hop.6), channel_id=1, source_target_pairs={{0,1},{1,2},{4,5},{5,6},{8,9},{9,10},{12,13},{13,14},{16,17},{17,1... | collective-permute-start | bytes 921608 | tf_op jit(solution)/shard_map/ppermute | solution.py:278
  145.1 23.6 %collective-permute-start.23 = (s16[3,400,128]{2,1,0:T(8,128)(2,1)}, s16[3,400,128]{2,1,0:T(8,128)(2,1)S(1)}, u32[]{:S(2)}, u32[]{:S(2)}) collective-permute-start(s16[3,400,128]{2,1,0:T(8,128)(2,1)} %hop.8), channel_id=1, source_target_pairs={{2,1},{3,2},{6,5},{7,6},{10,9},{11,10},{14,13},{15,14},{18,17},{19... | collective-permute-start | bytes 921608 | tf_op jit(solution)/shard_map/ppermute | solution.py:279
  145.9 13.3 %copy-start.19 = (s32[192,2]{0,1:T(2,128)S(1)}, s32[192,2]{0,1:T(2,128)}, u32[]{:S(2)}) copy-start(s32[192,2]{0,1:T(2,128)} %param.7) | copy-start | bytes 4612
  145.9 25.0 %collective-permute-start.22 = (s16[3,400,128]{2,1,0:T(8,128)(2,1)}, s16[3,400,128]{2,1,0:T(8,128)(2,1)}, u32[]{:S(2)}, u32[]{:S(2)}) collective-permute-start(s16[3,400,128]{2,1,0:T(8,128)(2,1)} %hop.8), channel_id=1, source_target_pairs={{0,1},{1,2},{4,5},{5,6},{8,9},{9,10},{12,13},{13,14},{16,17},{17,1... | collective-permute-start | bytes 921608 | tf_op jit(solution)/shard_map/ppermute | solution.py:278
  155.3 25.2 %collective-permute-start.32 = (s16[3,400,128]{2,1,0:T(8,128)(2,1)}, s16[3,400,128]{2,1,0:T(8,128)(2,1)S(1)}, u32[]{:S(2)}, u32[]{:S(2)}) collective-permute-start(s16[3,400,128]{2,1,0:T(8,128)(2,1)} %get-tuple-element.71), channel_id=1, source_target_pairs={{0,1},{1,2},{2,3},{4,5},{5,6},{6,7},{8,9},{9,10},{10,11},{12,13},{... | collective-permute-start | bytes 921608 | tf_op jit(solution)/shard_map/ppermute | solution.py:278
  159.2 11.7 %copy-start.6 = (f32[4,1152,128]{2,1,0:T(8,128)S(1)}, f32[4,1152,128]{2,1,0:T(8,128)}, u32[]{:S(2)}) copy-start(f32[4,1152,128]{2,1,0:T(8,128)} %copy-done.4) | copy-start | bytes 7077892
  159.2 23.3 %collective-permute-start.33 = (s16[3,400,128]{2,1,0:T(8,128)(2,1)}, s16[3,400,128]{2,1,0:T(8,128)(2,1)}, u32[]{:S(2)}, u32[]{:S(2)}) collective-permute-start(s16[3,400,128]{2,1,0:T(8,128)(2,1)} %copy-done.16), channel_id=1, source_target_pairs={{1,0},{2,1},{3,2},{5,4},{6,5},{7,6},{9,8},{10,9},{11,10},{13,12},{... | collective-permute-start | bytes 921608 | tf_op jit(solution)/shard_map/ppermute | solution.py:279
  164.1 27.8 %collective-permute-start.16 = (s16[3,400,128]{2,1,0:T(8,128)(2,1)}, s16[3,400,128]{2,1,0:T(8,128)(2,1)S(1)}, u32[]{:S(2)}, u32[]{:S(2)}) collective-permute-start(s16[3,400,128]{2,1,0:T(8,128)(2,1)} %get-tuple-element.47), channel_id=1, source_target_pairs={{0,1},{1,2},{2,3},{4,5},{5,6},{6,7},{8,9},{9,10},{10,11},{12,13},{... | collective-permute-start | bytes 921608 | tf_op jit(solution)/shard_map/ppermute | solution.py:278
  169.4 12.3 %copy-start.20 = (f32[160]{0:T(256)S(1)}, f32[160]{0:T(256)}, u32[]{:S(2)}) copy-start(f32[160]{0:T(256)} %param.8) | copy-start | bytes 1924
  169.4 12.5 %copy-start.18 = (f32[96]{0:T(128)S(1)}, f32[96]{0:T(128)}, u32[]{:S(2)}) copy-start(f32[96]{0:T(128)} %param.9) | copy-start | bytes 1156
  169.4 22.5 %collective-permute-start.17 = (s16[3,400,128]{2,1,0:T(8,128)(2,1)}, s16[3,400,128]{2,1,0:T(8,128)(2,1)S(1)}, u32[]{:S(2)}, u32[]{:S(2)}) collective-permute-start(s16[3,400,128]{2,1,0:T(8,128)(2,1)} %get-tuple-element.48), channel_id=1, source_target_pairs={{1,0},{2,1},{3,2},{5,4},{6,5},{7,6},{9,8},{10,9},{11,10},{13,12},{... | collective-permute-start | bytes 921608 | tf_op jit(solution)/shard_map/ppermute | solution.py:279
  175.1 11.5 %collective-permute-start.24 = (s16[3,400,128]{2,1,0:T(8,128)(2,1)}, s16[3,400,128]{2,1,0:T(8,128)(2,1)}, u32[]{:S(2)}, u32[]{:S(2)}) collective-permute-start(s16[3,400,128]{2,1,0:T(8,128)(2,1)} %get-tuple-element.59), channel_id=1, source_target_pairs={{0,1},{1,2},{2,3},{4,5},{5,6},{6,7},{8,9},{9,10},{10,11},{12,13},{... | collective-permute-start | bytes 921608 | tf_op jit(solution)/shard_map/ppermute | solution.py:278
  180.4 9.1 %collective-permute-start.25 = (s16[3,400,128]{2,1,0:T(8,128)(2,1)}, s16[3,400,128]{2,1,0:T(8,128)(2,1)}, u32[]{:S(2)}, u32[]{:S(2)}) collective-permute-start(s16[3,400,128]{2,1,0:T(8,128)(2,1)} %get-tuple-element.60), channel_id=1, source_target_pairs={{1,0},{2,1},{3,2},{5,4},{6,5},{7,6},{9,8},{10,9},{11,10},{13,12},{... | collective-permute-start | bytes 921608 | tf_op jit(solution)/shard_map/ppermute | solution.py:279
  182.5 1.7 copy-start.11
  184.2 5.3 %copy-start.7 = (f32[4,1152,128]{2,1,0:T(8,128)S(1)}, f32[4,1152,128]{2,1,0:T(8,128)}, u32[]{:S(2)}) copy-start(f32[4,1152,128]{2,1,0:T(8,128)} %copy-done.4) | copy-start | bytes 7077892
  (7 other events, 7.7 us)

commit v3 on v2

v3 whole, which is shorter than its diff:
```python
import functools

import jax
import jax.numpy as jnp
from jax import lax
from jax.experimental import pallas as pl
from jax.experimental.pallas import tpu as pltpu
from jax.sharding import PartitionSpec as P

CORES = 2
WIDTH = 64
LANES = 2 * WIDTH
TAIL = 16
NT = (((1,), (1,)), ((), ()))


def tile_of(rows, most):
    return max(t for t in range(16, most + 1, 16) if rows % t == 0)


def is_low(shape):
    return lax.broadcasted_iota(jnp.int32, shape, len(shape) - 1) < WIDTH


def turn(values):
    return pltpu.roll(values, WIDTH, 1)


def encode(values, out_ref):
    tile = values.shape[0]
    peak = jnp.max(jnp.abs(values), axis=0, keepdims=True)
    power = jnp.ceil(jnp.log2(jnp.maximum(peak, 1e-30) * (1.0 / 32760.0)))
    codes = jnp.round(values * jnp.exp2(-power)).astype(jnp.int32)
    out_ref[pl.ds(0, tile), :] = codes.astype(jnp.int16)
    wide = jnp.broadcast_to(power.astype(jnp.int32), (TAIL, LANES))
    out_ref[pl.ds(tile, TAIL), :] = wide.astype(jnp.int16)


def decode(ref):
    tile = ref.shape[0] - TAIL
    power = ref[pl.ds(tile, TAIL), :].astype(jnp.int32).astype(jnp.float32)[0:1, :]
    return ref[pl.ds(0, tile), :].astype(jnp.int32).astype(jnp.float32) * jnp.exp2(power)


def ladder_kernel(chips, place_ref, own_ref, sib_ref, rows_in, *refs):
    outs, rhs = refs[:chips], refs[-1]

    @pl.when(pl.program_id(0) == 0)
    def _():
        for d in range(chips):
            rhs[pl.ds(d * WIDTH, WIDTH), :] = rows_in[place_ref[0] ^ d]

    low = is_low((own_ref.shape[0], LANES))
    group = min(4, chips)
    for first in range(0, chips, group):
        right = rhs[pl.ds(first * WIDTH, group * WIDTH), :]
        own = lax.dot_general(own_ref[...], right, NT, preferred_element_type=jnp.float32)
        sib = lax.dot_general(sib_ref[...], right, NT, preferred_element_type=jnp.float32)
        for k in range(0, group, 2):
            u = own[:, k * WIDTH : k * WIDTH + LANES]
            v = sib[:, k * WIDTH : k * WIDTH + LANES]
            encode(jnp.where(low, u, turn(v)), outs[first + k].at[0])
            encode(jnp.where(low, turn(u), v), outs[first + k + 1].at[0])


def antisym_kernel(chips, slabs, vir, place_ref, *refs):
    arrived, (kept, away, cube, sent) = refs[:chips], refs[chips:]
    chip, core, z = place_ref[0], place_ref[1], place_ref[2]
    tiles, tile = arrived[0].shape[0], arrived[0].shape[1] - TAIL
    rows = tiles * tile
    s = pl.program_id(0)

    @pl.when(s == 0)
    def _():
        low = is_low((tile, LANES))
        for d in range(chips):
            base = (chip ^ d) * (CORES * rows)
            for t in range(tiles):
                values = decode(arrived[d].at[t])
                turned = turn(values)
                at_own = pl.multiple_of(base + core * rows + t * tile, tile)
                at_sib = pl.multiple_of(base + (1 - core) * rows + t * tile, tile)
                cube[pl.ds(at_own, tile), :] = jnp.where(low, values, turned)
                cube[pl.ds(at_sib, tile), :] = jnp.where(low, turned, values)

    half = vir // slabs // 2
    low = is_low((vir, LANES))
    part_tile = away.shape[2] - TAIL
    keep = ((s ^ z) & 1) == 0

    def subtract(k):
        a = s * (2 * half) + k
        b = a + half
        here = cube[pl.ds(pl.multiple_of(a * vir, vir), vir), :]
        other = cube[pl.ds(pl.multiple_of(b * vir, vir), vir), :]
        lower = here - cube[pl.ds(a, vir, stride=vir), :]
        upper = other - cube[pl.ds(b, vir, stride=vir), :]
        return jnp.where(low, lower, upper)

    def into(out):
        def body(k, carry):
            out[pl.ds(pl.multiple_of(k * vir, vir), vir), :] = subtract(k)
            return carry

        lax.fori_loop(0, half, body, 0)

    @pl.when(keep)
    def _():
        into(kept.at[0])

    @pl.when(jnp.logical_not(keep))
    def _():
        into(sent)
        for t in range(away.shape[1]):
            encode(sent[pl.ds(t * part_tile, part_tile), :], away.at[0, t])


def hop_kernel(place_ref, part_send, part_keep, got_send, got_keep, kept, away):
    encode(part_send[0] + decode(got_send.at[0, 0]), away.at[0, 0])
    kept[0] = part_keep[0] + decode(got_keep.at[0, 0])


def finish_kernel(part, got, pair_ref, vir_ref, *refs):
    out_ref = refs[-1]
    tiles, tile = got.shape[1], got.shape[2] - TAIL
    low = is_low((tile, LANES))
    pair = pair_ref[0]
    half = tiles * tile
    for t in range(tiles):
        at = pl.ds(t * tile, tile)
        total = part[0, at, :] + decode(got.at[0, t])
        virt = jnp.where(low, vir_ref[at, 0:1], vir_ref[at, 1:2])
        update = (total / (pair - virt)).T
        out_ref[:, pl.ds(t * tile, tile)] = update[:WIDTH]
        out_ref[:, pl.ds(half + t * tile, tile)] = update[WIDTH:]


def on_device(mesh, amplitudes, integrals, pair_index, eps_occ, eps_vir):
    devices, slabs = mesh.shape["pair"], mesh.shape["slab"]
    chips = devices // CORES
    num_pairs, depth = amplitudes.shape
    rows = integrals.shape[1]
    vir = eps_vir.shape[0]
    chunks = num_pairs // WIDTH
    half = vir // slabs // 2
    part_rows = half * vir
    tile, part_tile = tile_of(rows, 384), tile_of(part_rows, 384)
    tiles, part_tiles = rows // tile, part_rows // part_tile
    me, z = lax.axis_index("pair"), lax.axis_index("slab")
    chip, core = me // CORES, me % CORES

    def to_chip(x, d):
        return lax.ppermute(x, "pair", [(i, i ^ (d * CORES)) for i in range(devices)])

    def limit(mib):
        return pltpu.CompilerParams(vmem_limit_bytes=mib * 1024 * 1024)

    def cost(flops, moved):
        return pl.CostEstimate(flops=flops, bytes_accessed=moved, transcendentals=0)

    def in_hbm(kernel):
        def call(*args):
            pin = pltpu.with_memory_space_constraint
            return kernel(*(x if x.size < 8192 else pin(x, pltpu.HBM) for x in args))

        return call

    message_shape = (tiles, tile + TAIL, LANES)
    message = pltpu.HBM(message_shape, jnp.int16)
    smem = pl.BlockSpec(memory_space=pltpu.SMEM)

    def parcel(count):
        return (count, part_tiles, part_tile + TAIL, LANES)

    ladder = pl.pallas_call(
        functools.partial(ladder_kernel, chips),
        grid=(tiles,),
        in_specs=[smem]
        + [pl.BlockSpec((tile, depth), lambda i: (i, 0))] * 2
        + [pl.BlockSpec((chips, WIDTH, depth), lambda i: (0, 0, 0))],
        out_specs=[pl.BlockSpec((1, tile + TAIL, LANES), lambda i: (i, 0, 0))] * chips,
        out_shape=[message] * chips,
        scratch_shapes=[pltpu.VMEM((chips * WIDTH, depth), jnp.bfloat16)],
        compiler_params=limit(24),
        cost_estimate=cost(
            4 * rows * depth * chips * WIDTH,
            4 * rows * depth + 2 * chips * WIDTH * depth + 2 * chips * rows * LANES,
        ),
        name="ladder",
    )
    antisym = pl.pallas_call(
        functools.partial(antisym_kernel, chips, slabs, vir),
        grid=(slabs,),
        in_specs=[smem] + [pl.BlockSpec(message_shape, lambda s: (0, 0, 0))] * chips,
        out_specs=[
            pl.BlockSpec((1, part_rows, LANES), lambda s: (s // 2, 0, 0)),
            pl.BlockSpec((1, *parcel(1)[1:]), lambda s: (s // 2, 0, 0, 0)),
        ],
        out_shape=[
            pltpu.HBM((slabs // 2, part_rows, LANES), jnp.float32),
            pltpu.HBM(parcel(slabs // 2), jnp.int16),
        ],
        scratch_shapes=[
            pltpu.VMEM((vir * vir, LANES), jnp.float32),
            pltpu.VMEM((part_rows, LANES), jnp.float32),
        ],
        compiler_params=limit(24),
        cost_estimate=cost(8 * vir * vir * LANES, 4 * vir * vir * LANES),
        name="antisym",
    )

    def hop(place, part, got):
        count = part.shape[0] // 2

        def part_spec(turned):
            return pl.BlockSpec(
                (1, part_tile, LANES), lambda i, t, place: (2 * i + (place[0] ^ turned), t, 0)
            )

        def got_spec(turned):
            return pl.BlockSpec(
                (1, 1, part_tile + TAIL, LANES),
                lambda i, t, place: (2 * i + (place[0] ^ turned), t, 0, 0),
            )

        call = pl.pallas_call(
            hop_kernel,
            grid_spec=pltpu.PrefetchScalarGridSpec(
                num_scalar_prefetch=1,
                grid=(count, part_tiles),
                in_specs=[part_spec(1), part_spec(0), got_spec(1), got_spec(0)],
                out_specs=[
                    pl.BlockSpec((1, part_tile, LANES), lambda i, t, place: (i, t, 0)),
                    pl.BlockSpec(
                        (1, 1, part_tile + TAIL, LANES), lambda i, t, place: (i, t, 0, 0)
                    ),
                ],
            ),
            out_shape=[
                pltpu.HBM((count, part_rows, LANES), jnp.float32),
                pltpu.HBM(parcel(count), jnp.int16),
            ],
            compiler_params=limit(12),
            cost_estimate=cost(8 * count * part_rows * LANES, 16 * count * part_rows * LANES),
            name="hop",
        )
        return in_hbm(call)(place, part, part, got, got)

    def finish(r, part, got, pair, virt, so_far):
        given = [] if so_far is None else [so_far]
        call = pl.pallas_call(
            finish_kernel,
            grid=(1,),
            in_specs=[
                pl.BlockSpec((1, part_rows, LANES), lambda i: (0, 0, 0)),
                pl.BlockSpec(parcel(1), lambda i: (0, 0, 0, 0)),
                pl.BlockSpec((1, 1, LANES), lambda i: (r, 0, 0)),
                pl.BlockSpec((part_rows, 2), lambda i: (0, 0)),
            ]
            + [pl.BlockSpec(memory_space=pl.ANY)] * len(given),
            out_specs=pl.BlockSpec((WIDTH, 2 * part_rows), lambda i: (r, 0)),
            out_shape=pltpu.HBM((num_pairs, 2 * part_rows), jnp.float32),
            input_output_aliases={4: 0} if given else {},
            compiler_params=limit(16),
            cost_estimate=cost(16 * part_rows * LANES, 16 * part_rows * LANES),
            name="finish",
        )
        return in_hbm(call)(part, got, pair, virt, *given)

    own_t = integrals.T
    sib_t = lax.ppermute(own_t, "pair", [(i, i ^ 1) for i in range(devices)])

    occ_ids = jnp.arange(eps_occ.shape[0], dtype=jnp.int32)

    def pick(ids):
        return jnp.sum(jnp.where(ids[:, None] == occ_ids[None, :], eps_occ[None, :], 0.0), axis=1)

    eps_pair = (pick(pair_index[:, 0]) + pick(pair_index[:, 1])).reshape(chunks, 1, WIDTH)
    eps_pair = jnp.concatenate([eps_pair, eps_pair], axis=2)
    eps_mine = lax.dynamic_slice(eps_vir.reshape(slabs, 2, half), (z, 0, 0), (1, 2, half))[0]
    eps_virt = (eps_mine[:, :, None] + eps_vir[None, None, :]).reshape(2, part_rows).T

    place = jnp.stack([chip, core, z]).astype(jnp.int32)

    same_core = [list(range(k, devices, CORES)) for k in range(CORES)]
    gathered = []
    for r in range(chunks):
        mine = amplitudes[r * WIDTH : (r + 1) * WIDTH]
        if gathered:
            mine, gathered[-1] = lax.optimization_barrier((mine, gathered[-1]))
        gathered.append(lax.all_gather(mine, "pair", axis_index_groups=same_core))

    def across(x, level):
        return lax.ppermute(x, "slab", [(i, i ^ level) for i in range(slabs)])

    def stages(r):
        sums = yield functools.partial(in_hbm(ladder), place, own_t, sib_t), gathered[r]
        arrived = [to_chip(sums[d], d) for d in range(1, chips)]
        kept, away = yield functools.partial(in_hbm(antisym), place, sums[0]), *arrived
        got, level = across(away, 1), 2
        while level < slabs:
            bit = (z // level % 2)[None].astype(jnp.int32)
            kept, away = yield functools.partial(hop, bit, kept), got
            got, level = across(away, level), 2 * level
        yield functools.partial(finish, r, kept), got

    order = []
    length = 3 + max(0, (slabs - 1).bit_length() - 1)
    for tick in range(length + chunks):
        for r in reversed(range(chunks)):
            k = tick - r
            if 0 <= k < length:
                order.append((r, k))

    running = [stages(r) for r in range(chunks)]
    results = [None] * chunks
    update = token = None
    for r, k in order:
        call, *inputs = running[r].send(results[r])
        if token is not None:
            *inputs, token = lax.optimization_barrier((*inputs, token))
        if k == length - 1:
            update = call(*inputs, eps_pair, eps_virt, update)
        else:
            results[r] = call(*inputs)
            token = results[r][-1]
    return update


def solution(mesh):
    in_specs = (P("pair", "slab"), P("slab", "pair"), P("pair", None), P(), P())
    out_specs = P("pair", "slab")
    return jax.shard_map(
        functools.partial(on_device, mesh),
        mesh=mesh,
        in_specs=in_specs,
        out_specs=out_specs,
        check_vma=False,
    )
```

time: 194 us -> 208 us (1.072)
  waiting for transfers between devices: 52.6 us -> 98.9 us
  starting transfers between devices: 62.7 us -> 16.7 us
  between operations: 0.28 us -> 13.2 us
  Pallas kernels: 51.3 us -> 61.4 us
  local copies, waits for them, and re-layouts: 25.9 us -> 16.9 us
    all_gather x0 -> x3, waiting for transfers between devices: none -> 59.8 us  [on_device(): gathered.append(lax.all_gather(mine, 'pair', axis_index_groups=same_core))]
    ppermute x18 -> x9, waiting for transfers between devices: 49.7 us -> 12.9 us  [to_chip(): return lax.ppermute(x, 'pair', [(i, i ^ d * CORES) for i in range(devices)])]
    ppermute x15 -> x6, starting transfers between devices: 39.3 us -> 6.5 us  [across(): return lax.ppermute(x, 'slab', [(i, i ^ level) for i in range(slabs)])]
    ppermute x15 -> x6, waiting for transfers between devices: 2.82 us -> 26.2 us  [across(): return lax.ppermute(x, 'slab', [(i, i ^ level) for i in range(slabs)])]
    ppermute x18 -> x9, starting transfers between devices: 22.9 us -> 9.65 us  [to_chip(): return lax.ppermute(x, 'pair', [(i, i ^ d * CORES) for i in range(devices)])]
    pallas_call x15 -> x12, Pallas kernels: 51.3 us -> 61.4 us  [call(): return kernel(*(x if x.size < 8192 else pin(x, pltpu.HBM) for x in args))]
    unnamed x43 -> x39, local copies, waits for them, and re-layouts: 25.5 us -> 15.7 us
  transfers between devices with their start and end apart: 34 -> 19, of which waited for: 12 -> 8; matrix products, arithmetic and copies ran while one was open for 1% -> 1% of each run, Pallas kernels for 23% -> 28%
where the time goes in v3:
time: 208 us
  waiting for transfers between devices  98.9 us (48%)
  Pallas kernels  61.4 us (30%)
  local copies, waits for them, and re-layouts  16.9 us (8%)
  starting transfers between devices  16.7 us (8%)
  between operations  13.2 us (6%)
    pallas_call x12, Pallas kernels, call(): return kernel(*(x if x.size < 8192 else pin(x, pltpu.HBM) for x in args))  61.4 us
    all_gather x3, waiting for transfers between devices, on_device(): gathered.append(lax.all_gather(mine, 'pair', axis_index_groups=same_core))  59.8 us
    ppermute x6, waiting for transfers between devices, across(): return lax.ppermute(x, 'slab', [(i, i ^ level) for i in range(slabs)])  26.2 us
    unnamed x39, local copies, waits for them, and re-layouts  15.7 us
    ppermute x9, waiting for transfers between devices, to_chip(): return lax.ppermute(x, 'pair', [(i, i ^ d * CORES) for i in range(devices)])  12.9 us
    ppermute x9, starting transfers between devices, to_chip(): return lax.ppermute(x, 'pair', [(i, i ^ d * CORES) for i in range(devices)])  9.65 us
    ppermute x6, starting transfers between devices, across(): return lax.ppermute(x, 'slab', [(i, i ^ level) for i in range(slabs)])  6.5 us
  transfers between devices with their start and end apart: 19, of which 8 were waited for; matrix products, arithmetic and copies ran while one was open for 1% of the time, Pallas kernels for 28%

profile of v3, /device:TPU:0, one launch (start us, length us, event | category | flops | bytes accessed | tf_op | source)
XLA Modules:
  0.0 207.6 jit_solution(11913961510306787766)
XLA Ops:
  6.5 8.7 %copy.10 = bf16[2304,1152]{0,1:T(8,128)(2,1)} copy(bf16[2304,1152]{1,0:T(8,128)(2,1)} %param.6) | data formatting | bytes 10616832 | tf_op args[1]
  15.2 0.5 collective-permute-start
  15.6 0.9 fusion
  16.6 30.2 %all-gather.7.cloned.1.call-done = bf16[256,2304]{1,0:T(8,128)(2,1)} async-done(((bf16[64,2304]{1,0:T(8,128)(2,1)}), bf16[256,2304]{1,0:T(8,128)(2,1)}) %all-gather.7.cloned.1.call-update) | async-done | bytes 1179664 | tf_op jit(solution)/shard_map/all_gather | solution.py:291
  47.0 29.5 %all-gather.9.cloned.1.call-done = bf16[256,2304]{1,0:T(8,128)(2,1)} async-done(((bf16[64,2304]{1,0:T(8,128)(2,1)}), bf16[256,2304]{1,0:T(8,128)(2,1)}) %all-gather.9.cloned.1.call-update) | async-done | bytes 1179664 | tf_op jit(solution)/shard_map/all_gather | solution.py:291
  76.6 8.0 %ladder.3 = (s16[3,400,128]{2,1,0:T(8,128)(2,1)}, s16[3,400,128]{2,1,0:T(8,128)(2,1)}, s16[3,400,128]{2,1,0:T(8,128)(2,1)}, s16[3,400,128]{2,1,0:T(8,128)(2,1)}) custom-call(s32[3]{0:T(128)S(1)} %pad_add_fusion.place_ref, bf16[1152,2304]{1,0:T(8,128)(2,1)} %bitcast.19, bf16[1152,2304]{1,0:T(8,128)(2,1)} %collective-permute-done.sib_ref, ...), custom_call_target="tpu_custom_call" | custom-call | flops 2717908992 | bytes 12976128 | tf_op jit(solution)/shard_map/ladder/pallas_call | solution.py:164
  84.6 1.5 collective-permute-start.1
  86.1 0.6 collective-permute-start.2
  86.6 1.5 collective-permute-start.3
  88.1 8.0 %ladder.4 = (s16[3,400,128]{2,1,0:T(8,128)(2,1)}, s16[3,400,128]{2,1,0:T(8,128)(2,1)}, s16[3,400,128]{2,1,0:T(8,128)(2,1)}, s16[3,400,128]{2,1,0:T(8,128)(2,1)}) custom-call(s32[3]{0:T(128)S(1)} %pad_add_fusion.place_ref, bf16[1152,2304]{1,0:T(8,128)(2,1)} %bitcast.20, bf16[1152,2304]{1,0:T(8,128)(2,1)} %collective-permute-done.sib_ref, ...), custom_call_target="tpu_custom_call" | custom-call | flops 2717908992 | bytes 12976128 | tf_op jit(solution)/shard_map/ladder/pallas_call | solution.py:164
  96.1 2.0 collective-permute-done.1.refs_1_
  98.2 6.1 %collective-permute-done.2.refs_2_ = s16[3,400,128]{2,1,0:T(8,128)(2,1)S(1)} collective-permute-done((s16[3,400,128]{2,1,0:T(8,128)(2,1)}, s16[3,400,128]{2,1,0:T(8,128)(2,1)S(1)}, u32[]{:S(2)}, u32[]{:S(2)}) %collective-permute-start.2) | collective-permute-done | bytes 307232 | tf_op jit(solution)/shard_map/ppermute | solution.py:153
  104.3 2.2 %collective-permute-done.3.refs_3_ = s16[3,400,128]{2,1,0:T(8,128)(2,1)S(1)} collective-permute-done((s16[3,400,128]{2,1,0:T(8,128)(2,1)}, s16[3,400,128]{2,1,0:T(8,128)(2,1)S(1)}, u32[]{:S(2)}, u32[]{:S(2)}) %collective-permute-start.3) | collective-permute-done | bytes 307232 | tf_op jit(solution)/shard_map/ppermute | solution.py:153
  106.5 0.7 copy-done.15
  107.2 6.6 %antisym.3 = (f32[2,1152,128]{2,1,0:T(8,128)}, s16[2,3,400,128]{3,2,1,0:T(8,128)(2,1)}) custom-call(s32[3]{0:T(128)S(1)} %pad_add_fusion.place_ref, s16[3,400,128]{2,1,0:T(8,128)(2,1)} %get-tuple-element.51.refs_0_, s16[3,400,128]{2,1,0:T(8,128)(2,1)} %copy-done.13, s16[3,400,128]{2,1,0:T(8,128)(2,1)} %copy-done.14, s16[3,400,128]{2,1,0:T(8,128)(2,1)} %copy-done.15), custom_call_target="tpu_custom_call" | custom-call | flops 9437184 | bytes 4718592 | tf_op jit(solution)/shard_map/antisym/pallas_call | solution.py:164
  113.8 1.5 collective-permute-start.7
  115.2 1.7 collective-permute-start.10
  117.0 0.3 collective-permute-start.8
  117.3 1.4 collective-permute-start.9
  118.7 8.0 %ladder.5 = (s16[3,400,128]{2,1,0:T(8,128)(2,1)}, s16[3,400,128]{2,1,0:T(8,128)(2,1)}, s16[3,400,128]{2,1,0:T(8,128)(2,1)}, s16[3,400,128]{2,1,0:T(8,128)(2,1)}) custom-call(s32[3]{0:T(128)S(1)} %pad_add_fusion.place_ref, bf16[1152,2304]{1,0:T(8,128)(2,1)} %bitcast.21, bf16[1152,2304]{1,0:T(8,128)(2,1)} %collective-permute-done.sib_ref, ...), custom_call_target="tpu_custom_call" | custom-call | flops 2717908992 | bytes 12976128 | tf_op jit(solution)/shard_map/ladder/pallas_call | solution.py:164
  126.8 0.5 collective-permute-start.4
  127.3 1.8 collective-permute-start.5
  129.1 2.5 %collective-permute-done.8.refs_1_ = s16[3,400,128]{2,1,0:T(8,128)(2,1)S(1)} collective-permute-done((s16[3,400,128]{2,1,0:T(8,128)(2,1)}, s16[3,400,128]{2,1,0:T(8,128)(2,1)S(1)}, u32[]{:S(2)}, u32[]{:S(2)}) %collective-permute-start.8) | collective-permute-done | bytes 307232 | tf_op jit(solution)/shard_map/ppermute | solution.py:153
  131.6 0.4 collective-permute-start.6
  132.0 0.4 copy-done.9
  132.3 0.4 copy-done.11
  132.7 6.6 %antisym.4 = (f32[2,1152,128]{2,1,0:T(8,128)}, s16[2,3,400,128]{3,2,1,0:T(8,128)(2,1)}) custom-call(s32[3]{0:T(128)S(1)} %pad_add_fusion.place_ref, s16[3,400,128]{2,1,0:T(8,128)(2,1)} %get-tuple-element.68.refs_0_, s16[3,400,128]{2,1,0:T(8,128)(2,1)} %copy-done.9, s16[3,400,128]{2,1,0:T(8,128)(2,1)} %copy-done.11, s16[3,400,128]{2,1,0:T(8,128)(2,1)} %copy-done.8), custom_call_target="tpu_custom_call" | custom-call | flops 9437184 | bytes 4718592 | tf_op jit(solution)/shard_map/antisym/pallas_call | solution.py:164
  139.3 1.0 collective-permute-start.13
  140.4 0.8 copy-done
  141.2 3.4 %hop.3 = (f32[1,1152,128]{2,1,0:T(8,128)}, s16[1,3,400,128]{3,2,1,0:T(8,128)(2,1)}) custom-call(s32[1]{0:T(128)} %bitcast.place_ref, f32[2,1152,128]{2,1,0:T(8,128)} %get-tuple-element.67.part_send.part_keep, f32[2,1152,128]{2,1,0:T(8,128)} %get-tuple-element.67.part_send.part_keep, s16[2,3,400,128]{3,2,1,0:T(8,128)(2,1)} %copy-done, ...), custom_call_target="tpu_custom_call" | custom-call | flops 1179648 | bytes 2359296 | tf_op jit(solution)/shard_map/hop/pallas_call | solution.py:164
  144.6 0.7 copy-done.6
  145.5 6.6 %antisym.5 = (f32[2,1152,128]{2,1,0:T(8,128)}, s16[2,3,400,128]{3,2,1,0:T(8,128)(2,1)}) custom-call(s32[3]{0:T(128)S(1)} %pad_add_fusion.place_ref, s16[3,400,128]{2,1,0:T(8,128)(2,1)} %get-tuple-element.63.refs_0_, s16[3,400,128]{2,1,0:T(8,128)(2,1)} %copy-done.6, s16[3,400,128]{2,1,0:T(8,128)(2,1)} %copy-done.7, s16[3,400,128]{2,1,0:T(8,128)(2,1)} %copy-done.10), custom_call_target="tpu_custom_call" | custom-call | flops 9437184 | bytes 4718592 | tf_op jit(solution)/shard_map/antisym/pallas_call | solution.py:164
  152.1 1.0 collective-permute-start.11
  153.2 2.5 %collective-permute-start.15 = (s16[1,3,400,128]{3,2,1,0:T(8,128)(2,1)}, s16[1,3,400,128]{3,2,1,0:T(8,128)(2,1)S(1)}, u32[]{:S(2)}, u32[]{:S(2)}) collective-permute-start(s16[1,3,400,128]{3,2,1,0:T(8,128)(2,1)} %get-tuple-element.76), channel_id=1, source_target_pairs={{0,2},{1,3},{2,0},{3,1},{4,6},{5,7},{6,4},{7,5},{8,10},{9,11},{10,... | collective-permute-start | bytes 921608 | tf_op jit(solution)/shard_map/ppermute | solution.py:294
  155.7 0.8 copy-done.1
  156.5 3.3 %hop.5 = (f32[1,1152,128]{2,1,0:T(8,128)}, s16[1,3,400,128]{3,2,1,0:T(8,128)(2,1)}) custom-call(s32[1]{0:T(128)} %bitcast.place_ref, f32[2,1152,128]{2,1,0:T(8,128)} %get-tuple-element.84.part_send.part_keep, f32[2,1152,128]{2,1,0:T(8,128)} %get-tuple-element.84.part_send.part_keep, s16[2,3,400,128]{3,2,1,0:T(8,128)(2,1)} %copy-done.1, ...), custom_call_target="tpu_custom_call" | custom-call | flops 1179648 | bytes 2359296 | tf_op jit(solution)/shard_map/hop/pallas_call | solution.py:164
  159.8 0.5 collective-permute-start.14
  160.3 18.5 %collective-permute-done.11.got_send.got_keep = s16[2,3,400,128]{3,2,1,0:T(8,128)(2,1)S(1)} collective-permute-done((s16[2,3,400,128]{3,2,1,0:T(8,128)(2,1)}, s16[2,3,400,128]{3,2,1,0:T(8,128)(2,1)S(1)}, u32[]{:S(2)}, u32[]{:S(2)}) %collective-permute-start.11) | collective-permute-done | bytes 614432 | tf_op jit(solution)/shard_map/ppermute | solution.py:294
  178.9 0.8 copy-done.2
  179.7 3.4 %hop.4 = (f32[1,1152,128]{2,1,0:T(8,128)}, s16[1,3,400,128]{3,2,1,0:T(8,128)(2,1)}) custom-call(s32[1]{0:T(128)} %bitcast.place_ref, f32[2,1152,128]{2,1,0:T(8,128)} %get-tuple-element.80.part_send.part_keep, f32[2,1152,128]{2,1,0:T(8,128)} %get-tuple-element.80.part_send.part_keep, s16[2,3,400,128]{3,2,1,0:T(8,128)(2,1)} %copy-done.2, ...), custom_call_target="tpu_custom_call" | custom-call | flops 1179648 | bytes 2359296 | tf_op jit(solution)/shard_map/hop/pallas_call | solution.py:164
  183.5 0.2 bitcast_add_fusion
  183.8 0.7 copy-done.12
  184.5 2.5 %finish.3.refs_0_ = f32[192,2304]{1,0:T(8,128)} custom-call(f32[1,1152,128]{2,1,0:T(8,128)} %get-tuple-element.89.part, s16[1,3,400,128]{3,2,1,0:T(8,128)(2,1)} %copy-done.12, f32[3,1,128]{2,1,0:T(1,128)S(1)} %pad_maximum_fusion.pair_ref, f32[1152,2]{1,0:T(8,128)S(1)} %bitcast.15), custom_call_target="tpu_custom_call" | custom-call | flops 2359296 | bytes 2359296 | tf_op jit(solution)/shard_map/finish/pallas_call | solution.py:164
  187.0 0.7 copy-done.4
  187.7 2.5 %finish.4.refs_0_ = f32[192,2304]{1,0:T(8,128)} custom-call(f32[1,1152,128]{2,1,0:T(8,128)} %get-tuple-element.86.part, s16[1,3,400,128]{3,2,1,0:T(8,128)(2,1)} %copy-done.4, f32[3,1,128]{2,1,0:T(1,128)S(1)} %pad_maximum_fusion.pair_ref, f32[1152,2]{1,0:T(8,128)S(1)} %bitcast.16, f32[192,2304]{1,0:T(8,128)} %finish.3.refs_0_), custom_call_target="tpu_custom_call", output_to_operand_aliasing={{}: (4, {})} | custom-call | flops 2359296 | bytes 2359296 | tf_op jit(solution)/shard_map/finish/pallas_call | solution.py:164
  190.2 7.6 %collective-permute-done.12.got = s16[1,3,400,128]{3,2,1,0:T(8,128)(2,1)S(1)} collective-permute-done((s16[1,3,400,128]{3,2,1,0:T(8,128)(2,1)}, s16[1,3,400,128]{3,2,1,0:T(8,128)(2,1)S(1)}, u32[]{:S(2)}, u32[]{:S(2)}) %collective-permute-start.12) | collective-permute-done | bytes 307232 | tf_op jit(solution)/shard_map/ppermute | solution.py:294
  197.9 0.7 copy-done.5
  198.6 2.5 %finish.5 = f32[192,2304]{1,0:T(8,128)} custom-call(f32[1,1152,128]{2,1,0:T(8,128)} %get-tuple-element.82.part, s16[1,3,400,128]{3,2,1,0:T(8,128)(2,1)} %copy-done.5, f32[3,1,128]{2,1,0:T(1,128)S(1)} %pad_maximum_fusion.pair_ref, f32[1152,2]{1,0:T(8,128)S(1)} %bitcast.17, f32[192,2304]{1,0:T(8,128)} %finish.4.refs_0_), custom_call_target="tpu_custom_call", output_to_operand_aliasing={{}: (4, {})} | custom-call | flops 2359296 | bytes 2359296 | tf_op jit(solution)/shard_map/finish/pallas_call | solution.py:164
  (57 shorter events, 1.0 us)
Async XLA Ops:
  6.5 9.1 %copy-start.3 = (bf16[192,2304]{1,0:T(8,128)(2,1)S(1)}, bf16[192,2304]{1,0:T(8,128)(2,1)}, u32[]{:S(2)}) copy-start(bf16[192,2304]{1,0:T(8,128)(2,1)} %param.5) | copy-start | bytes 2654212
  6.5 40.3 %all-gather.7.cloned.1.call-start = ((), (), s32[]{:S(2)}) async-start(), calls=%async_computation | async-start | bytes 1474560 | tf_op jit(solution)/shard_map/all_gather | solution.py:291
  15.2 61.4 %collective-permute-start = (bf16[1152,2304]{1,0:T(8,128)(2,1)}, bf16[1152,2304]{1,0:T(8,128)(2,1)}, u32[]{:S(2)}, u32[]{:S(2)}) collective-permute-start(bf16[1152,2304]{1,0:T(8,128)(2,1)} %bitcast.18), channel_id=1, source_target_pairs={{0,4},{4,0},{8,12},{12,8},{16,20},{20,16},{24,28},{28,24},{1,5},{5... | collective-permute-start | bytes 15925256 | tf_op jit(solution)/shard_map/ppermute | solution.py:271
  16.6 59.9 %all-gather.9.cloned.1.call-start = ((), (), s32[]{:S(2)}) async-start(), calls=%async_computation.1 | async-start | bytes 1474560 | tf_op jit(solution)/shard_map/all_gather | solution.py:291
  46.9 71.8 %all-gather.11.cloned.1.call-start = ((), (), s32[]{:S(2)}) async-start(), calls=%async_computation.2 | async-start | bytes 1474560 | tf_op jit(solution)/shard_map/all_gather | solution.py:291
  84.6 13.5 %collective-permute-start.1 = (s16[3,400,128]{2,1,0:T(8,128)(2,1)}, s16[3,400,128]{2,1,0:T(8,128)(2,1)S(1)}, u32[]{:S(2)}, u32[]{:S(2)}) collective-permute-start(s16[3,400,128]{2,1,0:T(8,128)(2,1)} %get-tuple-element.52), channel_id=1, source_target_pairs={{0,8},{4,12},{8,0},{12,4},{16,24},{20,28},{24,16},{28,20},{1,9},{5... | collective-permute-start | bytes 921608 | tf_op jit(solution)/shard_map/ppermute | solution.py:153
  86.1 18.2 %collective-permute-start.2 = (s16[3,400,128]{2,1,0:T(8,128)(2,1)}, s16[3,400,128]{2,1,0:T(8,128)(2,1)S(1)}, u32[]{:S(2)}, u32[]{:S(2)}) collective-permute-start(s16[3,400,128]{2,1,0:T(8,128)(2,1)} %get-tuple-element.53), channel_id=1, source_target_pairs={{0,16},{4,20},{8,24},{12,28},{16,0},{20,4},{24,8},{28,12},{1,17},{... | collective-permute-start | bytes 921608 | tf_op jit(solution)/shard_map/ppermute | solution.py:153
  86.6 19.8 %collective-permute-start.3 = (s16[3,400,128]{2,1,0:T(8,128)(2,1)}, s16[3,400,128]{2,1,0:T(8,128)(2,1)S(1)}, u32[]{:S(2)}, u32[]{:S(2)}) collective-permute-start(s16[3,400,128]{2,1,0:T(8,128)(2,1)} %get-tuple-element.54), channel_id=1, source_target_pairs={{0,24},{4,28},{8,16},{12,20},{16,8},{20,12},{24,0},{28,4},{1,25},{... | collective-permute-start | bytes 921608 | tf_op jit(solution)/shard_map/ppermute | solution.py:153
  98.2 8.3 %copy-start.13 = (s16[3,400,128]{2,1,0:T(8,128)(2,1)}, s16[3,400,128]{2,1,0:T(8,128)(2,1)S(1)}, u32[]{:S(2)}) copy-start(s16[3,400,128]{2,1,0:T(8,128)(2,1)S(1)} %collective-permute-done.1.refs_1_) | copy-start | bytes 921604
  104.3 2.2 %copy-start.14 = (s16[3,400,128]{2,1,0:T(8,128)(2,1)}, s16[3,400,128]{2,1,0:T(8,128)(2,1)S(1)}, u32[]{:S(2)}) copy-start(s16[3,400,128]{2,1,0:T(8,128)(2,1)S(1)} %collective-permute-done.2.refs_2_) | copy-start | bytes 921604
  106.5 0.7 copy-start.15
  113.8 26.6 %collective-permute-start.7 = (s16[2,3,400,128]{3,2,1,0:T(8,128)(2,1)}, s16[2,3,400,128]{3,2,1,0:T(8,128)(2,1)S(1)}, u32[]{:S(2)}, u32[]{:S(2)}) collective-permute-start(s16[2,3,400,128]{3,2,1,0:T(8,128)(2,1)} %get-tuple-element.61), channel_id=1, source_target_pairs={{0,1},{1,0},{2,3},{3,2},{4,5},{5,4},{6,7},{7,6},{8,9},{9,8},{10,11... | collective-permute-start | bytes 1843208 | tf_op jit(solution)/shard_map/ppermute | solution.py:294
  115.2 12.0 %collective-permute-start.10 = (s16[3,400,128]{2,1,0:T(8,128)(2,1)}, s16[3,400,128]{2,1,0:T(8,128)(2,1)S(1)}, u32[]{:S(2)}, u32[]{:S(2)}) collective-permute-start(s16[3,400,128]{2,1,0:T(8,128)(2,1)} %get-tuple-element.57), channel_id=1, source_target_pairs={{0,24},{4,28},{8,16},{12,20},{16,8},{20,12},{24,0},{28,4},{1,25},{... | collective-permute-start | bytes 921608 | tf_op jit(solution)/shard_map/ppermute | solution.py:153
  117.0 14.6 %collective-permute-start.8 = (s16[3,400,128]{2,1,0:T(8,128)(2,1)}, s16[3,400,128]{2,1,0:T(8,128)(2,1)S(1)}, u32[]{:S(2)}, u32[]{:S(2)}) collective-permute-start(s16[3,400,128]{2,1,0:T(8,128)(2,1)} %get-tuple-element.69), channel_id=1, source_target_pairs={{0,8},{4,12},{8,0},{12,4},{16,24},{20,28},{24,16},{28,20},{1,9},{5... | collective-permute-start | bytes 921608 | tf_op jit(solution)/shard_map/ppermute | solution.py:153
  117.3 14.7 %collective-permute-start.9 = (s16[3,400,128]{2,1,0:T(8,128)(2,1)}, s16[3,400,128]{2,1,0:T(8,128)(2,1)S(1)}, u32[]{:S(2)}, u32[]{:S(2)}) collective-permute-start(s16[3,400,128]{2,1,0:T(8,128)(2,1)} %get-tuple-element.70), channel_id=1, source_target_pairs={{0,16},{4,20},{8,24},{12,28},{16,0},{20,4},{24,8},{28,12},{1,17},{... | collective-permute-start | bytes 921608 | tf_op jit(solution)/shard_map/ppermute | solution.py:153
  126.8 17.8 %collective-permute-start.4 = (s16[3,400,128]{2,1,0:T(8,128)(2,1)}, s16[3,400,128]{2,1,0:T(8,128)(2,1)S(1)}, u32[]{:S(2)}, u32[]{:S(2)}) collective-permute-start(s16[3,400,128]{2,1,0:T(8,128)(2,1)} %get-tuple-element.64), channel_id=1, source_target_pairs={{0,8},{4,12},{8,0},{12,4},{16,24},{20,28},{24,16},{28,20},{1,9},{5... | collective-permute-start | bytes 921608 | tf_op jit(solution)/shard_map/ppermute | solution.py:153
  127.3 4.7 %copy-start.8 = (s16[3,400,128]{2,1,0:T(8,128)(2,1)}, s16[3,400,128]{2,1,0:T(8,128)(2,1)S(1)}, u32[]{:S(2)}) copy-start(s16[3,400,128]{2,1,0:T(8,128)(2,1)S(1)} %collective-permute-done.10.refs_3_) | copy-start | bytes 921604
  127.3 17.3 %collective-permute-start.5 = (s16[3,400,128]{2,1,0:T(8,128)(2,1)}, s16[3,400,128]{2,1,0:T(8,128)(2,1)S(1)}, u32[]{:S(2)}, u32[]{:S(2)}) collective-permute-start(s16[3,400,128]{2,1,0:T(8,128)(2,1)} %get-tuple-element.65), channel_id=1, source_target_pairs={{0,16},{4,20},{8,24},{12,28},{16,0},{20,4},{24,8},{28,12},{1,17},{... | collective-permute-start | bytes 921608 | tf_op jit(solution)/shard_map/ppermute | solution.py:153
  131.6 0.7 copy-start.9
  131.6 13.0 %collective-permute-start.6 = (s16[3,400,128]{2,1,0:T(8,128)(2,1)}, s16[3,400,128]{2,1,0:T(8,128)(2,1)S(1)}, u32[]{:S(2)}, u32[]{:S(2)}) collective-permute-start(s16[3,400,128]{2,1,0:T(8,128)(2,1)} %get-tuple-element.66), channel_id=1, source_target_pairs={{0,24},{4,28},{8,16},{12,20},{16,8},{20,12},{24,0},{28,4},{1,25},{... | collective-permute-start | bytes 921608 | tf_op jit(solution)/shard_map/ppermute | solution.py:153
  132.0 0.7 copy-start.11
  139.3 16.4 %collective-permute-start.13 = (s16[2,3,400,128]{3,2,1,0:T(8,128)(2,1)}, s16[2,3,400,128]{3,2,1,0:T(8,128)(2,1)S(1)}, u32[]{:S(2)}, u32[]{:S(2)}) collective-permute-start(s16[2,3,400,128]{3,2,1,0:T(8,128)(2,1)} %get-tuple-element.74), channel_id=1, source_target_pairs={{0,1},{1,0},{2,3},{3,2},{4,5},{5,4},{6,7},{7,6},{8,9},{9,8},{10,11... | collective-permute-start | bytes 1843208 | tf_op jit(solution)/shard_map/ppermute | solution.py:294
  140.4 0.8 copy-start
  141.2 11.9 %copy-start.16 = (f32[96]{0:T(128)S(1)}, f32[96]{0:T(128)}, u32[]{:S(2)}) copy-start(f32[96]{0:T(128)} %param.9) | copy-start | bytes 1156
  141.2 12.0 %copy-start.17 = (s32[192,2]{0,1:T(2,128)S(1)}, s32[192,2]{0,1:T(2,128)}, u32[]{:S(2)}) copy-start(s32[192,2]{0,1:T(2,128)} %param.7) | copy-start | bytes 4612
  144.6 0.7 copy-start.6
  144.6 0.8 copy-start.7
  144.6 0.9 copy-start.10
  152.1 26.8 %collective-permute-start.11 = (s16[2,3,400,128]{3,2,1,0:T(8,128)(2,1)}, s16[2,3,400,128]{3,2,1,0:T(8,128)(2,1)S(1)}, u32[]{:S(2)}, u32[]{:S(2)}) collective-permute-start(s16[2,3,400,128]{3,2,1,0:T(8,128)(2,1)} %get-tuple-element.81), channel_id=1, source_target_pairs={{0,1},{1,0},{2,3},{3,2},{4,5},{5,4},{6,7},{7,6},{8,9},{9,8},{10,11... | collective-permute-start | bytes 1843208 | tf_op jit(solution)/shard_map/ppermute | solution.py:294
  153.2 30.6 %collective-permute-start.15 = (s16[1,3,400,128]{3,2,1,0:T(8,128)(2,1)}, s16[1,3,400,128]{3,2,1,0:T(8,128)(2,1)S(1)}, u32[]{:S(2)}, u32[]{:S(2)}) collective-permute-start(s16[1,3,400,128]{3,2,1,0:T(8,128)(2,1)} %get-tuple-element.76), channel_id=1, source_target_pairs={{0,2},{1,3},{2,0},{3,1},{4,6},{5,7},{6,4},{7,5},{8,10},{9,11},{10,... | collective-permute-start | bytes 921608 | tf_op jit(solution)/shard_map/ppermute | solution.py:294
  155.7 0.8 copy-start.1
  159.8 27.2 %collective-permute-start.14 = (s16[1,3,400,128]{3,2,1,0:T(8,128)(2,1)}, s16[1,3,400,128]{3,2,1,0:T(8,128)(2,1)S(1)}, u32[]{:S(2)}, u32[]{:S(2)}) collective-permute-start(s16[1,3,400,128]{3,2,1,0:T(8,128)(2,1)} %get-tuple-element.87), channel_id=1, source_target_pairs={{0,2},{1,3},{2,0},{3,1},{4,6},{5,7},{6,4},{7,5},{8,10},{9,11},{10,... | collective-permute-start | bytes 921608 | tf_op jit(solution)/shard_map/ppermute | solution.py:294
  178.9 0.8 copy-start.2
  179.7 3.6 %copy-start.18 = (f32[160]{0:T(256)S(1)}, f32[160]{0:T(256)}, u32[]{:S(2)}) copy-start(f32[160]{0:T(256)} %param.8) | copy-start | bytes 1924
  183.1 14.8 %collective-permute-start.12 = (s16[1,3,400,128]{3,2,1,0:T(8,128)(2,1)}, s16[1,3,400,128]{3,2,1,0:T(8,128)(2,1)S(1)}, u32[]{:S(2)}, u32[]{:S(2)}) collective-permute-start(s16[1,3,400,128]{3,2,1,0:T(8,128)(2,1)} %get-tuple-element.83), channel_id=1, source_target_pairs={{0,2},{1,3},{2,0},{3,1},{4,6},{5,7},{6,4},{7,5},{8,10},{9,11},{10,... | collective-permute-start | bytes 921608 | tf_op jit(solution)/shard_map/ppermute | solution.py:294
  183.8 0.7 copy-start.12
  187.0 0.7 copy-start.4
  197.9 0.7 copy-start.5
Sparse Core Ops, SparseCore 0:
  16.7 30.1 all-gather.6
  48.7 27.7 all-gather.8
  78.3 33.0 all-gather.10

commit v4 on v3

v4 whole, which is shorter than its diff:
```python
import functools

import jax
import jax.numpy as jnp
from jax import lax
from jax.experimental import pallas as pl
from jax.experimental.pallas import tpu as pltpu
from jax.sharding import PartitionSpec as P

CORES = 2
WIDTH = 64
LANES = 2 * WIDTH
TAIL = 16
NT = (((1,), (1,)), ((), ()))


def tile_of(rows, most):
    return max(t for t in range(16, most + 1, 16) if rows % t == 0)


def is_low(shape):
    return lax.broadcasted_iota(jnp.int32, shape, len(shape) - 1) < WIDTH


def turn(values):
    return pltpu.roll(values, WIDTH, 1)


def encode(values, out_ref):
    tile = values.shape[0]
    peak = jnp.max(jnp.abs(values), axis=0, keepdims=True)
    power = jnp.ceil(jnp.log2(jnp.maximum(peak, 1e-30) * (1.0 / 32760.0)))
    codes = jnp.round(values * jnp.exp2(-power)).astype(jnp.int32)
    out_ref[pl.ds(0, tile), :] = codes.astype(jnp.int16)
    wide = jnp.broadcast_to(power.astype(jnp.int32), (TAIL, LANES))
    out_ref[pl.ds(tile, TAIL), :] = wide.astype(jnp.int16)


def decode(ref):
    tile = ref.shape[0] - TAIL
    power = ref[pl.ds(tile, TAIL), :].astype(jnp.int32).astype(jnp.float32)[0:1, :]
    return ref[pl.ds(0, tile), :].astype(jnp.int32).astype(jnp.float32) * jnp.exp2(power)


def transpose_kernel(in_ref, out_ref):
    width = in_ref.shape[1]
    at = pl.ds(pl.multiple_of(pl.program_id(0) * width, width), width)
    out_ref[at, :] = in_ref[...].T


def ladder_kernel(chips, tile, own_ref, sib_ref, *refs):
    rows_in, outs, rhs = refs[:chips], refs[chips : 2 * chips], refs[-1]
    for d in range(chips):
        rhs[pl.ds(d * WIDTH, WIDTH), :] = rows_in[d][...]
    low = is_low((tile, LANES))
    group = min(4, chips)

    def step(i, carry):
        at = pl.ds(pl.multiple_of(i * tile, tile), tile)
        for first in range(0, chips, group):
            right = rhs[pl.ds(first * WIDTH, group * WIDTH), :]
            own = lax.dot_general(own_ref[at, :], right, NT, preferred_element_type=jnp.float32)
            sib = lax.dot_general(sib_ref[at, :], right, NT, preferred_element_type=jnp.float32)
            for k in range(0, group, 2):
                u = own[:, k * WIDTH : k * WIDTH + LANES]
                v = sib[:, k * WIDTH : k * WIDTH + LANES]
                encode(jnp.where(low, u, turn(v)), outs[first + k].at[i])
                encode(jnp.where(low, turn(u), v), outs[first + k + 1].at[i])
        return carry

    lax.fori_loop(0, own_ref.shape[0] // tile, step, 0)


def antisym_kernel(chips, slabs, vir, place_ref, *refs):
    arrived, (kept, away, cube, sent) = refs[:chips], refs[chips:]
    chip, core, z = place_ref[0], place_ref[1], place_ref[2]
    tiles, tile = arrived[0].shape[0], arrived[0].shape[1] - TAIL
    rows = tiles * tile
    low = is_low((tile, LANES))
    for d in range(chips):
        base = (chip ^ d) * (CORES * rows)
        for t in range(tiles):
            values = decode(arrived[d].at[t])
            turned = turn(values)
            at_own = pl.multiple_of(base + core * rows + t * tile, tile)
            at_sib = pl.multiple_of(base + (1 - core) * rows + t * tile, tile)
            cube[pl.ds(at_own, tile), :] = jnp.where(low, values, turned)
            cube[pl.ds(at_sib, tile), :] = jnp.where(low, turned, values)

    half = vir // slabs // 2
    low = is_low((vir, LANES))
    part_tile = away.shape[2] - TAIL

    def into(slab, out):
        def body(k, carry):
            a = slab * (2 * half) + k
            b = a + half
            here = cube[pl.ds(pl.multiple_of(a * vir, vir), vir), :]
            other = cube[pl.ds(pl.multiple_of(b * vir, vir), vir), :]
            lower = here - cube[pl.ds(a, vir, stride=vir), :]
            upper = other - cube[pl.ds(b, vir, stride=vir), :]
            out[pl.ds(pl.multiple_of(k * vir, vir), vir), :] = jnp.where(low, lower, upper)
            return carry

        lax.fori_loop(0, half, body, 0)

    for i in range(slabs // 2):
        into(2 * i + (z & 1), kept.at[i])
        into(2 * i + 1 - (z & 1), sent)
        for t in range(away.shape[1]):
            encode(sent[pl.ds(t * part_tile, part_tile), :], away.at[i, t])


def hop_kernel(bit_ref, part, got, kept, away):
    tiles, tile = got.shape[1], got.shape[2] - TAIL
    bit = bit_ref[0]
    for i in range(part.shape[0] // 2):
        keep, send = 2 * i + bit, 2 * i + 1 - bit
        for t in range(tiles):
            at = pl.ds(t * tile, tile)
            encode(part[send, at, :] + decode(got.at[send, t]), away.at[i, t])
            kept[i, at, :] = part[keep, at, :] + decode(got.at[keep, t])


def finish_kernel(part, got, pair_ref, vir_ref, *refs):
    out_ref = refs[-1]
    tiles, tile = got.shape[1], got.shape[2] - TAIL
    low = is_low((tile, LANES))
    pair = pair_ref[0]
    half = tiles * tile
    for t in range(tiles):
        at = pl.ds(t * tile, tile)
        total = part[0, at, :] + decode(got.at[0, t])
        virt = jnp.where(low, vir_ref[at, 0:1], vir_ref[at, 1:2])
        update = (total / (pair - virt)).T
        out_ref[:, pl.ds(t * tile, tile)] = update[:WIDTH]
        out_ref[:, pl.ds(half + t * tile, tile)] = update[WIDTH:]


def on_device(mesh, amplitudes, integrals, pair_index, eps_occ, eps_vir):
    devices, slabs = mesh.shape["pair"], mesh.shape["slab"]
    chips = devices // CORES
    num_pairs, depth = amplitudes.shape
    rows = integrals.shape[1]
    vir = eps_vir.shape[0]
    chunks = num_pairs // WIDTH
    half = vir // slabs // 2
    part_rows = half * vir
    tile, part_tile = tile_of(rows, 384), tile_of(part_rows, 384)
    tiles, part_tiles = rows // tile, part_rows // part_tile
    me, z = lax.axis_index("pair"), lax.axis_index("slab")
    chip, core = me // CORES, me % CORES

    def to_chip(x, d):
        return lax.ppermute(x, "pair", [(i, i ^ (d * CORES)) for i in range(devices)])

    def limit(mib):
        return pltpu.CompilerParams(vmem_limit_bytes=mib * 1024 * 1024)

    def cost(flops, moved):
        return pl.CostEstimate(flops=flops, bytes_accessed=moved, transcendentals=0)

    smem = pl.BlockSpec(memory_space=pltpu.SMEM)
    vmem = pl.BlockSpec(memory_space=pltpu.VMEM)
    message = jax.ShapeDtypeStruct((tiles, tile + TAIL, LANES), jnp.int16)

    def parcel(count):
        return (count, part_tiles, part_tile + TAIL, LANES)

    column = 128 if rows % 128 == 0 else rows
    transpose = pl.pallas_call(
        transpose_kernel,
        grid=(rows // column,),
        in_specs=[pl.BlockSpec((depth, column), lambda i: (0, i))],
        out_specs=vmem,
        out_shape=jax.ShapeDtypeStruct((rows, depth), jnp.bfloat16),
        compiler_params=limit(16),
        cost_estimate=cost(0, 4 * rows * depth),
        name="transpose",
    )
    ladder = pl.pallas_call(
        functools.partial(ladder_kernel, chips, tile),
        in_specs=[vmem] * (2 + chips),
        out_specs=[vmem] * chips,
        out_shape=[message] * chips,
        scratch_shapes=[pltpu.VMEM((chips * WIDTH, depth), jnp.bfloat16)],
        compiler_params=limit(16),
        cost_estimate=cost(
            4 * rows * depth * chips * WIDTH,
            4 * rows * depth + 2 * chips * WIDTH * depth + 2 * chips * rows * LANES,
        ),
        name="ladder",
    )
    antisym = pl.pallas_call(
        functools.partial(antisym_kernel, chips, slabs, vir),
        in_specs=[smem] + [vmem] * chips,
        out_specs=[vmem, vmem],
        out_shape=[
            jax.ShapeDtypeStruct((slabs // 2, part_rows, LANES), jnp.float32),
            jax.ShapeDtypeStruct(parcel(slabs // 2), jnp.int16),
        ],
        scratch_shapes=[
            pltpu.VMEM((vir * vir, LANES), jnp.float32),
            pltpu.VMEM((part_rows, LANES), jnp.float32),
        ],
        compiler_params=limit(16),
        cost_estimate=cost(8 * vir * vir * LANES, 4 * vir * vir * LANES),
        name="antisym",
    )

    def hop(place, part, got):
        count = part.shape[0] // 2
        return pl.pallas_call(
            hop_kernel,
            in_specs=[smem, vmem, vmem],
            out_specs=[vmem, vmem],
            out_shape=[
                jax.ShapeDtypeStruct((count, part_rows, LANES), jnp.float32),
                jax.ShapeDtypeStruct(parcel(count), jnp.int16),
            ],
            compiler_params=limit(8),
            cost_estimate=cost(8 * count * part_rows * LANES, 16 * count * part_rows * LANES),
            name="hop",
        )(place, part, got)

    def finish(r, part, got, pair, virt, so_far):
        given = [] if so_far is None else [so_far]
        call = pl.pallas_call(
            finish_kernel,
            grid=(1,),
            in_specs=[
                vmem,
                vmem,
                pl.BlockSpec((1, 1, LANES), lambda i: (r, 0, 0)),
                vmem,
            ]
            + [pl.BlockSpec(memory_space=pl.ANY)] * len(given),
            out_specs=pl.BlockSpec((WIDTH, 2 * part_rows), lambda i: (r, 0)),
            out_shape=jax.ShapeDtypeStruct((num_pairs, 2 * part_rows), jnp.float32),
            input_output_aliases={4: 0} if given else {},
            compiler_params=limit(8),
            cost_estimate=cost(16 * part_rows * LANES, 16 * part_rows * LANES),
            name="finish",
        )
        return call(part, got, pair, virt, *given)

    sib_t = transpose(lax.ppermute(integrals, "pair", [(i, i ^ 1) for i in range(devices)]))
    own_t = transpose(integrals)

    occ_ids = jnp.arange(eps_occ.shape[0], dtype=jnp.int32)

    def pick(ids):
        return jnp.sum(jnp.where(ids[:, None] == occ_ids[None, :], eps_occ[None, :], 0.0), axis=1)

    eps_pair = (pick(pair_index[:, 0]) + pick(pair_index[:, 1])).reshape(chunks, 1, WIDTH)
    eps_pair = jnp.concatenate([eps_pair, eps_pair], axis=2)
    eps_mine = lax.dynamic_slice(eps_vir.reshape(slabs, 2, half), (z, 0, 0), (1, 2, half))[0]
    eps_virt = (eps_mine[:, :, None] + eps_vir[None, None, :]).reshape(2, part_rows).T

    place = jnp.stack([chip, core, z]).astype(jnp.int32)

    gathered = []
    for r in range(chunks):
        mine = amplitudes[r * WIDTH : (r + 1) * WIDTH]
        if gathered:
            mine, *gathered[-1] = lax.optimization_barrier((mine, *gathered[-1]))
        gathered.append([mine] + [to_chip(mine, d) for d in range(1, chips)])
        if r == 0:
            own_t, *gathered[0] = lax.optimization_barrier((own_t, *gathered[0]))

    def across(x, level):
        return lax.ppermute(x, "slab", [(i, i ^ level) for i in range(slabs)])

    def stages(r):
        sums = yield functools.partial(ladder, own_t, sib_t), *gathered[r]
        arrived = [to_chip(sums[d], d) for d in range(1, chips)]
        kept, away = yield functools.partial(antisym, place, sums[0]), *arrived
        got, level = across(away, 1), 2
        while level < slabs:
            bit = (z // level % 2)[None].astype(jnp.int32)
            kept, away = yield functools.partial(hop, bit, kept), got
            got, level = across(away, level), 2 * level
        yield functools.partial(finish, r, kept), got

    length = 3 + max(0, (slabs - 1).bit_length() - 1)

    def when(stage):
        r, k = stage
        if k == 0:
            return 18 * r + 14
        return 18 * r + 38 + (k - 1) * (17 + 2 * r) + (12 if k == length - 1 else 0)

    order = sorted(((r, k) for r in range(chunks) for k in range(length)), key=when)

    running = [stages(r) for r in range(chunks)]
    results = [None] * chunks
    update = token = None
    for r, k in order:
        call, *inputs = running[r].send(results[r])
        if token is not None:
            *inputs, token = lax.optimization_barrier((*inputs, token))
        if k == length - 1:
            update = call(*inputs, eps_pair, eps_virt, update)
        else:
            results[r] = call(*inputs)
            token = results[r][-1]
    return update


def solution(mesh):
    in_specs = (P("pair", "slab"), P("slab", "pair"), P("pair", None), P(), P())
    out_specs = P("pair", "slab")
    return jax.shard_map(
        functools.partial(on_device, mesh),
        mesh=mesh,
        in_specs=in_specs,
        out_specs=out_specs,
        check_vma=False,
    )
```

time: 208 us -> 148 us (0.71)
  waiting for transfers between devices: 98.9 us -> 61.8 us
  Pallas kernels: 61.4 us -> 48 us
  between operations: 13.2 us -> 0.17 us
  starting transfers between devices: 16.7 us -> 28.5 us
  local copies, waits for them, and re-layouts: 16.9 us -> 8.71 us
    all_gather x3 -> x0, waiting for transfers between devices: 59.8 us -> none  [on_device(): gathered.append(lax.all_gather(mine, 'pair', axis_index_groups=same_core))]
    ppermute x9 -> x18, waiting for transfers between devices: 12.9 us -> 27.3 us  [to_chip(): return lax.ppermute(x, 'pair', [(i, i ^ d * CORES) for i in range(devices)])]
    pallas_call x12 -> x14, Pallas kernels: 61.4 us -> 48 us  [the longest x6 31.2 us: on_device(): results[r] = call(*inputs)]
    ppermute x9 -> x18, starting transfers between devices: 9.65 us -> 22.1 us  [to_chip(): return lax.ppermute(x, 'pair', [(i, i ^ d * CORES) for i in range(devices)])]
    unnamed x39 -> x32, local copies, waits for them, and re-layouts: 15.7 us -> 7.17 us
    ppermute x6, waiting for transfers between devices: 26.2 us -> 34.5 us  [across(): return lax.ppermute(x, 'slab', [(i, i ^ level) for i in range(slabs)])]
  transfers between devices with their start and end apart: 19 -> 25, of which waited for: 8 -> 12; matrix products, arithmetic and copies ran while one was open for 1% -> 1% of each run, Pallas kernels for 28% -> 28%
where the time goes in v4:
time: 148 us
  waiting for transfers between devices  61.8 us (42%)
  Pallas kernels  48 us (32%)
  starting transfers between devices  28.5 us (19%)
  local copies, waits for them, and re-layouts  8.71 us (6%)
    ppermute x6, waiting for transfers between devices, across(): return lax.ppermute(x, 'slab', [(i, i ^ level) for i in range(slabs)])  34.5 us
    pallas_call x6, Pallas kernels, on_device(): results[r] = call(*inputs)  31.2 us
    ppermute x18, waiting for transfers between devices, to_chip(): return lax.ppermute(x, 'pair', [(i, i ^ d * CORES) for i in range(devices)])  27.3 us
    ppermute x18, starting transfers between devices, to_chip(): return lax.ppermute(x, 'pair', [(i, i ^ d * CORES) for i in range(devices)])  22.1 us
    unnamed x32, local copies, waits for them, and re-layouts  7.17 us
    pallas_call x1, Pallas kernels, on_device(): transpose(lax.ppermute(integrals, 'pair', [(i, i ^ 1) for i in range(devi...  6.44 us
    ppermute x6, starting transfers between devices, across(): return lax.ppermute(x, 'slab', [(i, i ^ level) for i in range(slabs)])  5.91 us
    pallas_call x3, Pallas kernels, finish(): return call(part, got, pair, virt, *given)  4.13 us
  transfers between devices with their start and end apart: 25, of which 12 were waited for; matrix products, arithmetic and copies ran while one was open for 1% of the time, Pallas kernels for 28%

profile of v4, /device:TPU:0, one launch (start us, length us, event | category | flops | bytes accessed | tf_op | source)
XLA Modules:
  0.0 147.7 jit_solution(13262005378244433850)
XLA Ops:
  0.5 1.2 fusion
  1.7 2.6 %collective-permute-start = (bf16[64,2304]{1,0:T(8,128)(2,1)S(1)}, bf16[64,2304]{1,0:T(8,128)(2,1)S(1)}, u32[]{:S(2)}, u32[]{:S(2)}) collective-permute-start(bf16[64,2304]{1,0:T(8,128)(2,1)S(1)} %get-tuple-element.72.refs_0_), channel_id=1, source_target_pairs={{0,8},{4,12},{8,0},{12,4},{16,24},{20,28},{24,16},{28,20},{1,9},{5... | collective-permute-start | bytes 884744 | tf_op jit(solution)/shard_map/ppermute | solution.py:155
  4.2 1.5 %collective-permute-start.1 = (bf16[64,2304]{1,0:T(8,128)(2,1)S(1)}, bf16[64,2304]{1,0:T(8,128)(2,1)S(1)}, u32[]{:S(2)}, u32[]{:S(2)}) collective-permute-start(bf16[64,2304]{1,0:T(8,128)(2,1)S(1)} %get-tuple-element.72.refs_0_), channel_id=1, source_target_pairs={{0,16},{4,20},{8,24},{12,28},{16,0},{20,4},{24,8},{28,12},{1,17},{... | collective-permute-start | bytes 884744 | tf_op jit(solution)/shard_map/ppermute | solution.py:155
  5.8 2.5 %copy-done.1 = bf16[2304,1152]{1,0:T(8,128)(2,1)S(1)} copy-done((bf16[2304,1152]{1,0:T(8,128)(2,1)S(1)}, bf16[2304,1152]{1,0:T(8,128)(2,1)}, u32[]{:S(2)}) %copy-start.1) | copy-done | bytes 5308440
  8.3 2.9 %transpose.16.own_ref = bf16[1152,2304]{1,0:T(8,128)(2,1)S(1)} custom-call(bf16[2304,1152]{1,0:T(8,128)(2,1)S(1)} %copy-done.1), custom_call_target="tpu_custom_call" | custom-call | bytes 10616832 | tf_op jit(solution)/shard_map/transpose/pallas_call | solution.py:248
  11.1 2.4 %copy-done = bf16[1152,2304]{1,0:T(8,128)(2,1)} copy-done((bf16[1152,2304]{1,0:T(8,128)(2,1)}, bf16[1152,2304]{1,0:T(8,128)(2,1)S(1)}, u32[]{:S(2)}) %copy-start) | copy-done | bytes 5308440
  13.5 6.2 %collective-permute-done.1.refs_2_ = bf16[64,2304]{1,0:T(8,128)(2,1)S(1)} collective-permute-done((bf16[64,2304]{1,0:T(8,128)(2,1)S(1)}, bf16[64,2304]{1,0:T(8,128)(2,1)S(1)}, u32[]{:S(2)}, u32[]{:S(2)}) %collective-permute-start.1) | collective-permute-done | bytes 294944 | tf_op jit(solution)/shard_map/ppermute | solution.py:155
  19.7 1.2 collective-permute-start.4
  20.9 0.8 collective-permute-start.5
  21.7 1.4 collective-permute-start.6
  23.2 6.4 %transpose.17.sib_ref = bf16[1152,2304]{1,0:T(8,128)(2,1)S(1)} custom-call(bf16[2304,1152]{1,0:T(8,128)(2,1)} %collective-permute-done.3.in_ref), custom_call_target="tpu_custom_call" | custom-call | bytes 10616832 | tf_op jit(solution)/shard_map/transpose/pallas_call | solution.py:247
  29.6 4.2 %ladder.3 = (s16[3,400,128]{2,1,0:T(8,128)(2,1)S(1)}, s16[3,400,128]{2,1,0:T(8,128)(2,1)S(1)}, s16[3,400,128]{2,1,0:T(8,128)(2,1)S(1)}, s16[3,400,128]{2,1,0:T(8,128)(2,1)S(1)}) custom-call(bf16[1152,2304]{1,0:T(8,128)(2,1)S(1)} %bitcast.12, bf16[1152,2304]{1,0:T(8,128)(2,1)S(1)} %transpose.17.sib_ref, bf16[64,2304]{1,0:T(8,128)(2,1)S(1)} %get-tuple-element.72.refs_0_, ...), custom_call_target="tpu_custom_call" | custom-call | flops 2717908992 | bytes 12976128 | tf_op jit(solution)/shard_map/ladder/pallas_call | solution.py:305
  33.9 1.3 collective-permute-start.10
  35.2 0.8 collective-permute-start.11
  36.0 1.4 collective-permute-start.12
  37.5 5.0 %ladder.4 = (s16[3,400,128]{2,1,0:T(8,128)(2,1)S(1)}, s16[3,400,128]{2,1,0:T(8,128)(2,1)S(1)}, s16[3,400,128]{2,1,0:T(8,128)(2,1)}, s16[3,400,128]{2,1,0:T(8,128)(2,1)}) custom-call(bf16[1152,2304]{1,0:T(8,128)(2,1)S(1)} %bitcast.12, bf16[1152,2304]{1,0:T(8,128)(2,1)S(1)} %transpose.17.sib_ref, bf16[64,2304]{1,0:T(8,128)(2,1)S(1)} %get-tuple-element.84.refs_0_, ...), custom_call_target="tpu_custom_call" | custom-call | flops 2717908992 | bytes 12976128 | tf_op jit(solution)/shard_map/ladder/pallas_call | solution.py:305
  42.6 1.6 %collective-permute-done.10.refs_1_ = s16[3,400,128]{2,1,0:T(8,128)(2,1)S(1)} collective-permute-done((s16[3,400,128]{2,1,0:T(8,128)(2,1)S(1)}, s16[3,400,128]{2,1,0:T(8,128)(2,1)S(1)}, u32[]{:S(2)}, u32[]{:S(2)}) %collective-permute-start.10) | collective-permute-done | bytes 307232 | tf_op jit(solution)/shard_map/ppermute | solution.py:155
  44.2 5.4 %collective-permute-done.11.refs_2_ = s16[3,400,128]{2,1,0:T(8,128)(2,1)S(1)} collective-permute-done((s16[3,400,128]{2,1,0:T(8,128)(2,1)S(1)}, s16[3,400,128]{2,1,0:T(8,128)(2,1)S(1)}, u32[]{:S(2)}, u32[]{:S(2)}) %collective-permute-start.11) | collective-permute-done | bytes 307232 | tf_op jit(solution)/shard_map/ppermute | solution.py:155
  49.5 4.7 %antisym.3 = (f32[2,1152,128]{2,1,0:T(8,128)S(1)}, s16[2,3,400,128]{3,2,1,0:T(8,128)(2,1)S(1)}) custom-call(s32[3]{0:T(128)S(1)} %pad_add_fusion.place_ref, s16[3,400,128]{2,1,0:T(8,128)(2,1)S(1)} %get-tuple-element.76.refs_0_, s16[3,400,128]{2,1,0:T(8,128)(2,1)S(1)} %collective-permute-done.10.refs_1_, ...), custom_call_target="tpu_custom_call" | custom-call | flops 9437184 | bytes 4718592 | tf_op jit(solution)/shard_map/antisym/pallas_call | solution.py:305
  54.2 1.6 %collective-permute-start.19 = (s16[2,3,400,128]{3,2,1,0:T(8,128)(2,1)S(1)}, s16[2,3,400,128]{3,2,1,0:T(8,128)(2,1)S(1)}, u32[]{:S(2)}, u32[]{:S(2)}) collective-permute-start(s16[2,3,400,128]{3,2,1,0:T(8,128)(2,1)S(1)} %get-tuple-element.92), channel_id=1, source_target_pairs={{0,1},{1,0},{2,3},{3,2},{4,5},{5,4},{6,7},{7,6},{8,9},{9,8},{10,11... | collective-permute-start | bytes 1843208 | tf_op jit(solution)/shard_map/ppermute | solution.py:272
  56.6 1.3 collective-permute-start.8
  57.9 1.5 %collective-permute-start.9 = (bf16[64,2304]{1,0:T(8,128)(2,1)S(1)}, bf16[64,2304]{1,0:T(8,128)(2,1)S(1)}, u32[]{:S(2)}, u32[]{:S(2)}) collective-permute-start(bf16[64,2304]{1,0:T(8,128)(2,1)S(1)} %get-tuple-element.93.refs_0_), channel_id=1, source_target_pairs={{0,24},{4,28},{8,16},{12,20},{16,8},{20,12},{24,0},{28,4},{1,25},{... | collective-permute-start | bytes 884744 | tf_op jit(solution)/shard_map/ppermute | solution.py:155
  59.4 0.7 collective-permute-start.16
  60.0 5.8 %collective-permute-done.7.refs_1_ = bf16[64,2304]{1,0:T(8,128)(2,1)S(1)} collective-permute-done((bf16[64,2304]{1,0:T(8,128)(2,1)S(1)}, bf16[64,2304]{1,0:T(8,128)(2,1)S(1)}, u32[]{:S(2)}, u32[]{:S(2)}) %collective-permute-start.7) | collective-permute-done | bytes 294944 | tf_op jit(solution)/shard_map/ppermute | solution.py:155
  65.8 1.4 collective-permute-start.18
  67.6 1.9 %collective-permute-start.17 = (s16[3,400,128]{2,1,0:T(8,128)(2,1)}, s16[3,400,128]{2,1,0:T(8,128)(2,1)}, u32[]{:S(2)}, u32[]{:S(2)}) collective-permute-start(s16[3,400,128]{2,1,0:T(8,128)(2,1)} %get-tuple-element.103), channel_id=1, source_target_pairs={{0,16},{4,20},{8,24},{12,28},{16,0},{20,4},{24,8},{28,12},{1,17},{... | collective-permute-start | bytes 921608 | tf_op jit(solution)/shard_map/ppermute | solution.py:155
  69.6 2.8 %collective-permute-done.9.refs_3_ = bf16[64,2304]{1,0:T(8,128)(2,1)S(1)} collective-permute-done((bf16[64,2304]{1,0:T(8,128)(2,1)S(1)}, bf16[64,2304]{1,0:T(8,128)(2,1)S(1)}, u32[]{:S(2)}, u32[]{:S(2)}) %collective-permute-start.9) | collective-permute-done | bytes 294944 | tf_op jit(solution)/shard_map/ppermute | solution.py:155
  72.3 5.1 %ladder.5 = (s16[3,400,128]{2,1,0:T(8,128)(2,1)S(1)}, s16[3,400,128]{2,1,0:T(8,128)(2,1)}, s16[3,400,128]{2,1,0:T(8,128)(2,1)}, s16[3,400,128]{2,1,0:T(8,128)(2,1)}) custom-call(bf16[1152,2304]{1,0:T(8,128)(2,1)S(1)} %bitcast.12, bf16[1152,2304]{1,0:T(8,128)(2,1)S(1)} %transpose.17.sib_ref, bf16[64,2304]{1,0:T(8,128)(2,1)S(1)} %get-tuple-element.93.refs_0_, ...), custom_call_target="tpu_custom_call" | custom-call | flops 2717908992 | bytes 12976128 | tf_op jit(solution)/shard_map/ladder/pallas_call | solution.py:305
  77.4 0.7 copy-done.6
  78.2 1.4 collective-permute-start.13
  79.5 0.7 copy-done.8
  80.3 0.7 collective-permute-start.14
  81.0 1.4 collective-permute-start.15
  82.7 0.8 copy-done.4
  83.5 2.1 %collective-permute-done.18.refs_3_ = s16[3,400,128]{2,1,0:T(8,128)(2,1)} collective-permute-done((s16[3,400,128]{2,1,0:T(8,128)(2,1)}, s16[3,400,128]{2,1,0:T(8,128)(2,1)}, u32[]{:S(2)}, u32[]{:S(2)}) %collective-permute-start.18) | collective-permute-done | bytes 307232 | tf_op jit(solution)/shard_map/ppermute | solution.py:155
  85.6 6.0 %antisym.4 = (f32[2,1152,128]{2,1,0:T(8,128)S(1)}, s16[2,3,400,128]{3,2,1,0:T(8,128)(2,1)}) custom-call(s32[3]{0:T(128)S(1)} %pad_add_fusion.place_ref, s16[3,400,128]{2,1,0:T(8,128)(2,1)S(1)} %get-tuple-element.101.refs_0_, s16[3,400,128]{2,1,0:T(8,128)(2,1)S(1)} %copy-done.9, s16[3,400,128]{2,1,0:T(8,128)(2,1)} %collective-permute-done.17.refs_2_, ...), custom_call_target="tpu_custom_call" | custom-call | flops 9437184 | bytes 4718592 | tf_op jit(solution)/shard_map/antisym/pallas_call | solution.py:305
  92.1 3.2 %collective-permute-done.14.refs_2_ = s16[3,400,128]{2,1,0:T(8,128)(2,1)} collective-permute-done((s16[3,400,128]{2,1,0:T(8,128)(2,1)}, s16[3,400,128]{2,1,0:T(8,128)(2,1)}, u32[]{:S(2)}, u32[]{:S(2)}) %collective-permute-start.14) | collective-permute-done | bytes 307232 | tf_op jit(solution)/shard_map/ppermute | solution.py:155
  95.2 6.1 %antisym.5 = (f32[2,1152,128]{2,1,0:T(8,128)S(1)}, s16[2,3,400,128]{3,2,1,0:T(8,128)(2,1)}) custom-call(s32[3]{0:T(128)S(1)} %pad_add_fusion.place_ref, s16[3,400,128]{2,1,0:T(8,128)(2,1)S(1)} %copy-done.7, s16[3,400,128]{2,1,0:T(8,128)(2,1)} %collective-permute-done.13.refs_1_, s16[3,400,128]{2,1,0:T(8,128)(2,1)} %collective-permute-done.14.refs_2_, ...), custom_call_target="tpu_custom_call" | custom-call | flops 9437184 | bytes 4718592 | tf_op jit(solution)/shard_map/antisym/pallas_call | solution.py:305
  101.9 2.7 %collective-permute-start.24 = (s16[1,3,400,128]{3,2,1,0:T(8,128)(2,1)}, s16[1,3,400,128]{3,2,1,0:T(8,128)(2,1)S(1)}, u32[]{:S(2)}, u32[]{:S(2)}) collective-permute-start(s16[1,3,400,128]{3,2,1,0:T(8,128)(2,1)} %copy-done.10), channel_id=1, source_target_pairs={{0,2},{1,3},{2,0},{3,1},{4,6},{5,7},{6,4},{7,5},{8,10},{9,11},{10,... | collective-permute-start | bytes 921608 | tf_op jit(solution)/shard_map/ppermute | solution.py:272
  104.6 9.2 %collective-permute-done.22.got = s16[2,3,400,128]{3,2,1,0:T(8,128)(2,1)S(1)} collective-permute-done((s16[2,3,400,128]{3,2,1,0:T(8,128)(2,1)}, s16[2,3,400,128]{3,2,1,0:T(8,128)(2,1)S(1)}, u32[]{:S(2)}, u32[]{:S(2)}) %collective-permute-start.22) | collective-permute-done | bytes 614432 | tf_op jit(solution)/shard_map/ppermute | solution.py:272
  113.8 1.0 hop.5
  115.4 10.3 %collective-permute-done.20.got = s16[2,3,400,128]{3,2,1,0:T(8,128)(2,1)} collective-permute-done((s16[2,3,400,128]{3,2,1,0:T(8,128)(2,1)}, s16[2,3,400,128]{3,2,1,0:T(8,128)(2,1)}, u32[]{:S(2)}, u32[]{:S(2)}) %collective-permute-start.20) | collective-permute-done | bytes 614432 | tf_op jit(solution)/shard_map/ppermute | solution.py:272
  125.7 2.1 %hop.4 = (f32[1,1152,128]{2,1,0:T(8,128)S(1)}, s16[1,3,400,128]{3,2,1,0:T(8,128)(2,1)}) custom-call(s32[1]{0:T(128)} %bitcast.bit_ref, f32[2,1152,128]{2,1,0:T(8,128)S(1)} %get-tuple-element.114.part, s16[2,3,400,128]{3,2,1,0:T(8,128)(2,1)} %collective-permute-done.20.got), custom_call_target="tpu_custom_call" | custom-call | flops 1179648 | bytes 2359296 | tf_op jit(solution)/shard_map/hop/pallas_call | solution.py:213
  128.6 1.4 finish.3.refs_0_
  130.0 12.4 %collective-permute-done.23.got = s16[1,3,400,128]{3,2,1,0:T(8,128)(2,1)S(1)} collective-permute-done((s16[1,3,400,128]{3,2,1,0:T(8,128)(2,1)}, s16[1,3,400,128]{3,2,1,0:T(8,128)(2,1)S(1)}, u32[]{:S(2)}, u32[]{:S(2)}) %collective-permute-start.23) | collective-permute-done | bytes 307232 | tf_op jit(solution)/shard_map/ppermute | solution.py:272
  142.4 1.4 finish.4.refs_0_
  143.8 2.6 %collective-permute-done.21.got = s16[1,3,400,128]{3,2,1,0:T(8,128)(2,1)S(1)} collective-permute-done((s16[1,3,400,128]{3,2,1,0:T(8,128)(2,1)}, s16[1,3,400,128]{3,2,1,0:T(8,128)(2,1)S(1)}, u32[]{:S(2)}, u32[]{:S(2)}) %collective-permute-start.21) | collective-permute-done | bytes 307232 | tf_op jit(solution)/shard_map/ppermute | solution.py:272
  146.3 1.4 finish.5
  (62 shorter events, 4.3 us)
Async XLA Ops:
  0.0 23.2 %collective-permute-start.3 = (bf16[2304,1152]{1,0:T(8,128)(2,1)}, bf16[2304,1152]{1,0:T(8,128)(2,1)}, u32[]{:S(2)}, u32[]{:S(2)}) collective-permute-start(bf16[2304,1152]{1,0:T(8,128)(2,1)} %in_ref.1), channel_id=1, source_target_pairs={{0,4},{4,0},{8,12},{12,8},{16,20},{20,16},{24,28},{28,24},{1,5},{5... | collective-permute-start | bytes 15925256 | tf_op jit(solution)/shard_map/ppermute | solution.py:247
  1.7 11.8 %collective-permute-start = (bf16[64,2304]{1,0:T(8,128)(2,1)S(1)}, bf16[64,2304]{1,0:T(8,128)(2,1)S(1)}, u32[]{:S(2)}, u32[]{:S(2)}) collective-permute-start(bf16[64,2304]{1,0:T(8,128)(2,1)S(1)} %get-tuple-element.72.refs_0_), channel_id=1, source_target_pairs={{0,8},{4,12},{8,0},{12,4},{16,24},{20,28},{24,16},{28,20},{1,9},{5... | collective-permute-start | bytes 884744 | tf_op jit(solution)/shard_map/ppermute | solution.py:155
  4.2 15.5 %collective-permute-start.1 = (bf16[64,2304]{1,0:T(8,128)(2,1)S(1)}, bf16[64,2304]{1,0:T(8,128)(2,1)S(1)}, u32[]{:S(2)}, u32[]{:S(2)}) collective-permute-start(bf16[64,2304]{1,0:T(8,128)(2,1)S(1)} %get-tuple-element.72.refs_0_), channel_id=1, source_target_pairs={{0,16},{4,20},{8,24},{12,28},{16,0},{20,4},{24,8},{28,12},{1,17},{... | collective-permute-start | bytes 884744 | tf_op jit(solution)/shard_map/ppermute | solution.py:155
  5.7 13.9 %collective-permute-start.2 = (bf16[64,2304]{1,0:T(8,128)(2,1)S(1)}, bf16[64,2304]{1,0:T(8,128)(2,1)S(1)}, u32[]{:S(2)}, u32[]{:S(2)}) collective-permute-start(bf16[64,2304]{1,0:T(8,128)(2,1)S(1)} %get-tuple-element.72.refs_0_), channel_id=1, source_target_pairs={{0,24},{4,28},{8,16},{12,20},{16,8},{20,12},{24,0},{28,4},{1,25},{... | collective-permute-start | bytes 884744 | tf_op jit(solution)/shard_map/ppermute | solution.py:155
  5.7 2.5 %copy-start.1 = (bf16[2304,1152]{1,0:T(8,128)(2,1)S(1)}, bf16[2304,1152]{1,0:T(8,128)(2,1)}, u32[]{:S(2)}) copy-start(bf16[2304,1152]{1,0:T(8,128)(2,1)} %in_ref.1) | copy-start | bytes 15925252
  11.1 2.4 %copy-start = (bf16[1152,2304]{1,0:T(8,128)(2,1)}, bf16[1152,2304]{1,0:T(8,128)(2,1)S(1)}, u32[]{:S(2)}) copy-start(bf16[1152,2304]{1,0:T(8,128)(2,1)S(1)} %transpose.16.own_ref) | copy-start | bytes 15925252
  19.7 16.3 %collective-permute-start.4 = (bf16[64,2304]{1,0:T(8,128)(2,1)S(1)}, bf16[64,2304]{1,0:T(8,128)(2,1)S(1)}, u32[]{:S(2)}, u32[]{:S(2)}) collective-permute-start(bf16[64,2304]{1,0:T(8,128)(2,1)S(1)} %get-tuple-element.84.refs_0_), channel_id=1, source_target_pairs={{0,8},{4,12},{8,0},{12,4},{16,24},{20,28},{24,16},{28,20},{1,9},{5... | collective-permute-start | bytes 884744 | tf_op jit(solution)/shard_map/ppermute | solution.py:155
  20.9 8.7 %slice-start = ((s8[5308416]{0:T(1024)(128)(4,1)}), s8[1114112]{0:T(1024)(128)(4,1)S(1)}, s32[]{:S(2)}) async-start(s8[5308416]{0:T(1024)(128)(4,1)} %bitcast.11), calls=%async_computation | async-start | bytes 2228224
  20.9 8.7 %slice-start.1 = ((s8[5308416]{0:T(1024)(128)(4,1)}), s8[4194304]{0:T(1024)(128)(4,1)S(1)}, s32[]{:S(2)}) async-start(s8[5308416]{0:T(1024)(128)(4,1)} %bitcast.11), calls=%async_computation.1 | async-start | bytes 8388608
  20.9 16.6 %collective-permute-start.5 = (bf16[64,2304]{1,0:T(8,128)(2,1)S(1)}, bf16[64,2304]{1,0:T(8,128)(2,1)S(1)}, u32[]{:S(2)}, u32[]{:S(2)}) collective-permute-start(bf16[64,2304]{1,0:T(8,128)(2,1)S(1)} %get-tuple-element.84.refs_0_), channel_id=1, source_target_pairs={{0,16},{4,20},{8,24},{12,28},{16,0},{20,4},{24,8},{28,12},{1,17},{... | collective-permute-start | bytes 884744 | tf_op jit(solution)/shard_map/ppermute | solution.py:155
  21.7 15.8 %collective-permute-start.6 = (bf16[64,2304]{1,0:T(8,128)(2,1)S(1)}, bf16[64,2304]{1,0:T(8,128)(2,1)S(1)}, u32[]{:S(2)}, u32[]{:S(2)}) collective-permute-start(bf16[64,2304]{1,0:T(8,128)(2,1)S(1)} %get-tuple-element.84.refs_0_), channel_id=1, source_target_pairs={{0,24},{4,28},{8,16},{12,20},{16,8},{20,12},{24,0},{28,4},{1,25},{... | collective-permute-start | bytes 884744 | tf_op jit(solution)/shard_map/ppermute | solution.py:155
  33.9 10.3 %collective-permute-start.10 = (s16[3,400,128]{2,1,0:T(8,128)(2,1)S(1)}, s16[3,400,128]{2,1,0:T(8,128)(2,1)S(1)}, u32[]{:S(2)}, u32[]{:S(2)}) collective-permute-start(s16[3,400,128]{2,1,0:T(8,128)(2,1)S(1)} %get-tuple-element.77), channel_id=1, source_target_pairs={{0,8},{4,12},{8,0},{12,4},{16,24},{20,28},{24,16},{28,20},{1,9},{5... | collective-permute-start | bytes 921608 | tf_op jit(solution)/shard_map/ppermute | solution.py:155
  35.2 14.4 %collective-permute-start.11 = (s16[3,400,128]{2,1,0:T(8,128)(2,1)S(1)}, s16[3,400,128]{2,1,0:T(8,128)(2,1)S(1)}, u32[]{:S(2)}, u32[]{:S(2)}) collective-permute-start(s16[3,400,128]{2,1,0:T(8,128)(2,1)S(1)} %get-tuple-element.78), channel_id=1, source_target_pairs={{0,16},{4,20},{8,24},{12,28},{16,0},{20,4},{24,8},{28,12},{1,17},{... | collective-permute-start | bytes 921608 | tf_op jit(solution)/shard_map/ppermute | solution.py:155
  36.0 13.5 %collective-permute-start.12 = (s16[3,400,128]{2,1,0:T(8,128)(2,1)S(1)}, s16[3,400,128]{2,1,0:T(8,128)(2,1)S(1)}, u32[]{:S(2)}, u32[]{:S(2)}) collective-permute-start(s16[3,400,128]{2,1,0:T(8,128)(2,1)S(1)} %get-tuple-element.79), channel_id=1, source_target_pairs={{0,24},{4,28},{8,16},{12,20},{16,8},{20,12},{24,0},{28,4},{1,25},{... | collective-permute-start | bytes 921608 | tf_op jit(solution)/shard_map/ppermute | solution.py:155
  54.2 26.7 %collective-permute-start.19 = (s16[2,3,400,128]{3,2,1,0:T(8,128)(2,1)S(1)}, s16[2,3,400,128]{3,2,1,0:T(8,128)(2,1)S(1)}, u32[]{:S(2)}, u32[]{:S(2)}) collective-permute-start(s16[2,3,400,128]{3,2,1,0:T(8,128)(2,1)S(1)} %get-tuple-element.92), channel_id=1, source_target_pairs={{0,1},{1,0},{2,3},{3,2},{4,5},{5,4},{6,7},{7,6},{8,9},{9,8},{10,11... | collective-permute-start | bytes 1843208 | tf_op jit(solution)/shard_map/ppermute | solution.py:272
  55.9 9.9 %collective-permute-start.7 = (bf16[64,2304]{1,0:T(8,128)(2,1)S(1)}, bf16[64,2304]{1,0:T(8,128)(2,1)S(1)}, u32[]{:S(2)}, u32[]{:S(2)}) collective-permute-start(bf16[64,2304]{1,0:T(8,128)(2,1)S(1)} %get-tuple-element.93.refs_0_), channel_id=1, source_target_pairs={{0,8},{4,12},{8,0},{12,4},{16,24},{20,28},{24,16},{28,20},{1,9},{5... | collective-permute-start | bytes 884744 | tf_op jit(solution)/shard_map/ppermute | solution.py:155
  56.6 11.1 %collective-permute-start.8 = (bf16[64,2304]{1,0:T(8,128)(2,1)S(1)}, bf16[64,2304]{1,0:T(8,128)(2,1)S(1)}, u32[]{:S(2)}, u32[]{:S(2)}) collective-permute-start(bf16[64,2304]{1,0:T(8,128)(2,1)S(1)} %get-tuple-element.93.refs_0_), channel_id=1, source_target_pairs={{0,16},{4,20},{8,24},{12,28},{16,0},{20,4},{24,8},{28,12},{1,17},{... | collective-permute-start | bytes 884744 | tf_op jit(solution)/shard_map/ppermute | solution.py:155
  57.9 14.4 %collective-permute-start.9 = (bf16[64,2304]{1,0:T(8,128)(2,1)S(1)}, bf16[64,2304]{1,0:T(8,128)(2,1)S(1)}, u32[]{:S(2)}, u32[]{:S(2)}) collective-permute-start(bf16[64,2304]{1,0:T(8,128)(2,1)S(1)} %get-tuple-element.93.refs_0_), channel_id=1, source_target_pairs={{0,24},{4,28},{8,16},{12,20},{16,8},{20,12},{24,0},{28,4},{1,25},{... | collective-permute-start | bytes 884744 | tf_op jit(solution)/shard_map/ppermute | solution.py:155
  59.4 20.2 %collective-permute-start.16 = (s16[3,400,128]{2,1,0:T(8,128)(2,1)S(1)}, s16[3,400,128]{2,1,0:T(8,128)(2,1)S(1)}, u32[]{:S(2)}, u32[]{:S(2)}) collective-permute-start(s16[3,400,128]{2,1,0:T(8,128)(2,1)S(1)} %get-tuple-element.102), channel_id=1, source_target_pairs={{0,8},{4,12},{8,0},{12,4},{16,24},{20,28},{24,16},{28,20},{1,9},{5... | collective-permute-start | bytes 921608 | tf_op jit(solution)/shard_map/ppermute | solution.py:155
  65.8 19.8 %collective-permute-start.18 = (s16[3,400,128]{2,1,0:T(8,128)(2,1)}, s16[3,400,128]{2,1,0:T(8,128)(2,1)}, u32[]{:S(2)}, u32[]{:S(2)}) collective-permute-start(s16[3,400,128]{2,1,0:T(8,128)(2,1)} %get-tuple-element.88), channel_id=1, source_target_pairs={{0,24},{4,28},{8,16},{12,20},{16,8},{20,12},{24,0},{28,4},{1,25},{... | collective-permute-start | bytes 921608 | tf_op jit(solution)/shard_map/ppermute | solution.py:155
  67.6 15.9 %collective-permute-start.17 = (s16[3,400,128]{2,1,0:T(8,128)(2,1)}, s16[3,400,128]{2,1,0:T(8,128)(2,1)}, u32[]{:S(2)}, u32[]{:S(2)}) collective-permute-start(s16[3,400,128]{2,1,0:T(8,128)(2,1)} %get-tuple-element.103), channel_id=1, source_target_pairs={{0,16},{4,20},{8,24},{12,28},{16,0},{20,4},{24,8},{28,12},{1,17},{... | collective-permute-start | bytes 921608 | tf_op jit(solution)/shard_map/ppermute | solution.py:155
  77.4 0.7 copy-start.6
  78.2 13.9 %collective-permute-start.13 = (s16[3,400,128]{2,1,0:T(8,128)(2,1)}, s16[3,400,128]{2,1,0:T(8,128)(2,1)}, u32[]{:S(2)}, u32[]{:S(2)}) collective-permute-start(s16[3,400,128]{2,1,0:T(8,128)(2,1)} %get-tuple-element.98), channel_id=1, source_target_pairs={{0,8},{4,12},{8,0},{12,4},{16,24},{20,28},{24,16},{28,20},{1,9},{5... | collective-permute-start | bytes 921608 | tf_op jit(solution)/shard_map/ppermute | solution.py:155
  79.5 0.7 copy-start.8
  80.3 15.0 %collective-permute-start.14 = (s16[3,400,128]{2,1,0:T(8,128)(2,1)}, s16[3,400,128]{2,1,0:T(8,128)(2,1)}, u32[]{:S(2)}, u32[]{:S(2)}) collective-permute-start(s16[3,400,128]{2,1,0:T(8,128)(2,1)} %get-tuple-element.99), channel_id=1, source_target_pairs={{0,16},{4,20},{8,24},{12,28},{16,0},{20,4},{24,8},{28,12},{1,17},{... | collective-permute-start | bytes 921608 | tf_op jit(solution)/shard_map/ppermute | solution.py:155
  81.0 14.3 %collective-permute-start.15 = (s16[3,400,128]{2,1,0:T(8,128)(2,1)}, s16[3,400,128]{2,1,0:T(8,128)(2,1)}, u32[]{:S(2)}, u32[]{:S(2)}) collective-permute-start(s16[3,400,128]{2,1,0:T(8,128)(2,1)} %get-tuple-element.100), channel_id=1, source_target_pairs={{0,24},{4,28},{8,16},{12,20},{16,8},{20,12},{24,0},{28,4},{1,25},{... | collective-permute-start | bytes 921608 | tf_op jit(solution)/shard_map/ppermute | solution.py:155
  82.4 3.2 %copy-start.9 = (s16[3,400,128]{2,1,0:T(8,128)(2,1)S(1)}, s16[3,400,128]{2,1,0:T(8,128)(2,1)}, u32[]{:S(2)}) copy-start(s16[3,400,128]{2,1,0:T(8,128)(2,1)} %copy-done.8) | copy-start | bytes 921604
  82.4 12.9 %copy-start.7 = (s16[3,400,128]{2,1,0:T(8,128)(2,1)S(1)}, s16[3,400,128]{2,1,0:T(8,128)(2,1)}, u32[]{:S(2)}) copy-start(s16[3,400,128]{2,1,0:T(8,128)(2,1)} %copy-done.6) | copy-start | bytes 921604
  82.4 19.4 %copy-start.11 = (f32[96]{0:T(128)S(1)}, f32[96]{0:T(128)}, u32[]{:S(2)}) copy-start(f32[96]{0:T(128)} %param.9) | copy-start | bytes 1156
  82.4 19.5 %copy-start.12 = (s32[192,2]{0,1:T(2,128)S(1)}, s32[192,2]{0,1:T(2,128)}, u32[]{:S(2)}) copy-start(s32[192,2]{0,1:T(2,128)} %param.7) | copy-start | bytes 4612
  82.7 0.8 copy-start.4
  83.5 11.7 %copy-start.10 = (s16[1,3,400,128]{3,2,1,0:T(8,128)(2,1)}, s16[1,3,400,128]{3,2,1,0:T(8,128)(2,1)S(1)}, u32[]{:S(2)}) copy-start(s16[1,3,400,128]{3,2,1,0:T(8,128)(2,1)S(1)} %get-tuple-element.106) | copy-start | bytes 921604
  91.6 22.1 %collective-permute-start.22 = (s16[2,3,400,128]{3,2,1,0:T(8,128)(2,1)}, s16[2,3,400,128]{3,2,1,0:T(8,128)(2,1)S(1)}, u32[]{:S(2)}, u32[]{:S(2)}) collective-permute-start(s16[2,3,400,128]{3,2,1,0:T(8,128)(2,1)} %get-tuple-element.110), channel_id=1, source_target_pairs={{0,1},{1,0},{2,3},{3,2},{4,5},{5,4},{6,7},{7,6},{8,9},{9,8},{10,11... | collective-permute-start | bytes 1843208 | tf_op jit(solution)/shard_map/ppermute | solution.py:272
  101.3 24.4 %collective-permute-start.20 = (s16[2,3,400,128]{3,2,1,0:T(8,128)(2,1)}, s16[2,3,400,128]{3,2,1,0:T(8,128)(2,1)}, u32[]{:S(2)}, u32[]{:S(2)}) collective-permute-start(s16[2,3,400,128]{3,2,1,0:T(8,128)(2,1)} %get-tuple-element.115), channel_id=1, source_target_pairs={{0,1},{1,0},{2,3},{3,2},{4,5},{5,4},{6,7},{7,6},{8,9},{9,8},{10,11... | collective-permute-start | bytes 1843208 | tf_op jit(solution)/shard_map/ppermute | solution.py:272
  101.9 26.7 %collective-permute-start.24 = (s16[1,3,400,128]{3,2,1,0:T(8,128)(2,1)}, s16[1,3,400,128]{3,2,1,0:T(8,128)(2,1)S(1)}, u32[]{:S(2)}, u32[]{:S(2)}) collective-permute-start(s16[1,3,400,128]{3,2,1,0:T(8,128)(2,1)} %copy-done.10), channel_id=1, source_target_pairs={{0,2},{1,3},{2,0},{3,1},{4,6},{5,7},{6,4},{7,5},{8,10},{9,11},{10,... | collective-permute-start | bytes 921608 | tf_op jit(solution)/shard_map/ppermute | solution.py:272
  113.8 14.3 %copy-start.13 = (f32[160]{0:T(256)S(1)}, f32[160]{0:T(256)}, u32[]{:S(2)}) copy-start(f32[160]{0:T(256)} %param.8) | copy-start | bytes 1924
  114.7 13.1 %copy-start.2 = (f32[1,1152,128]{2,1,0:T(8,128)}, f32[1,1152,128]{2,1,0:T(8,128)S(1)}, u32[]{:S(2)}) copy-start(f32[1,1152,128]{2,1,0:T(8,128)S(1)} %get-tuple-element.120.part) | copy-start | bytes 1769476
  114.7 13.8 %copy-start.5 = (f32[1,1152,128]{2,1,0:T(8,128)S(1)}, f32[1,1152,128]{2,1,0:T(8,128)}, u32[]{:S(2)}) copy-start(f32[1,1152,128]{2,1,0:T(8,128)} %copy-done.4) | copy-start | bytes 1769476
  114.7 27.6 %collective-permute-start.23 = (s16[1,3,400,128]{3,2,1,0:T(8,128)(2,1)}, s16[1,3,400,128]{3,2,1,0:T(8,128)(2,1)S(1)}, u32[]{:S(2)}, u32[]{:S(2)}) collective-permute-start(s16[1,3,400,128]{3,2,1,0:T(8,128)(2,1)} %get-tuple-element.121), channel_id=1, source_target_pairs={{0,2},{1,3},{2,0},{3,1},{4,6},{5,7},{6,4},{7,5},{8,10},{9,11},{10,... | collective-permute-start | bytes 921608 | tf_op jit(solution)/shard_map/ppermute | solution.py:272
  127.8 18.5 %collective-permute-start.21 = (s16[1,3,400,128]{3,2,1,0:T(8,128)(2,1)}, s16[1,3,400,128]{3,2,1,0:T(8,128)(2,1)S(1)}, u32[]{:S(2)}, u32[]{:S(2)}) collective-permute-start(s16[1,3,400,128]{3,2,1,0:T(8,128)(2,1)} %get-tuple-element.117), channel_id=1, source_target_pairs={{0,2},{1,3},{2,0},{3,1},{4,6},{5,7},{6,4},{7,5},{8,10},{9,11},{10,... | collective-permute-start | bytes 921608 | tf_op jit(solution)/shard_map/ppermute | solution.py:272
  128.5 13.9 %copy-start.3 = (f32[1,1152,128]{2,1,0:T(8,128)S(1)}, f32[1,1152,128]{2,1,0:T(8,128)}, u32[]{:S(2)}) copy-start(f32[1,1152,128]{2,1,0:T(8,128)} %copy-done.2) | copy-start | bytes 1769476

commit v5 on v4

--- a/solution.py
+++ b/solution.py
@@ -48,10 +48,12 @@
     out_ref[at, :] = in_ref[...].T
 
 
-def ladder_kernel(chips, tile, own_ref, sib_ref, *refs):
-    rows_in, outs, rhs = refs[:chips], refs[chips : 2 * chips], refs[-1]
-    for d in range(chips):
-        rhs[pl.ds(d * WIDTH, WIDTH), :] = rows_in[d][...]
+def ladder_kernel(chips, tile, pieces, own_ref, sib_ref, *refs):
+    rows_in, outs, rhs = refs[: len(pieces)], refs[len(pieces) : -1], refs[-1]
+    at = 0
+    for ref, (start, count) in zip(rows_in, pieces):
+        rhs[pl.ds(at, count), :] = ref[pl.ds(start, count), :]
+        at += count
     low = is_low((tile, LANES))
     group = min(4, chips)
 
@@ -72,7 +74,7 @@
 
 
 def antisym_kernel(chips, slabs, vir, place_ref, *refs):
-    arrived, (kept, away, cube, sent) = refs[:chips], refs[chips:]
+    arrived, (parts, *away, cube, sent) = refs[:chips], refs[chips:]
     chip, core, z = place_ref[0], place_ref[1], place_ref[2]
     tiles, tile = arrived[0].shape[0], arrived[0].shape[1] - TAIL
     rows = tiles * tile
@@ -89,7 +91,7 @@
 
     half = vir // slabs // 2
     low = is_low((vir, LANES))
-    part_tile = away.shape[2] - TAIL
+    part_tile = away[0].shape[2] - TAIL
 
     def into(slab, out):
         def body(k, carry):
@@ -104,33 +106,37 @@
 
         lax.fori_loop(0, half, body, 0)
 
-    for i in range(slabs // 2):
-        into(2 * i + (z & 1), kept.at[i])
-        into(2 * i + 1 - (z & 1), sent)
-        for t in range(away.shape[1]):
-            encode(sent[pl.ds(t * part_tile, part_tile), :], away.at[i, t])
-
-
-def hop_kernel(bit_ref, part, got, kept, away):
-    tiles, tile = got.shape[1], got.shape[2] - TAIL
-    bit = bit_ref[0]
-    for i in range(part.shape[0] // 2):
-        keep, send = 2 * i + bit, 2 * i + 1 - bit
+    for e in reversed(range(1, slabs, 2)):
+        into(e ^ z, sent)
+        out = away[e // 2].at[0] if len(away) > 1 else away[0].at[e // 2]
+        for t in range(out.shape[0]):
+            encode(sent[pl.ds(t * part_tile, part_tile), :], out.at[t])
+    for e in range(0, slabs, 2):
+        into(e ^ z, parts.at[e // 2])
+
+
+def hop_kernel(slots, parts, *refs):
+    got, out = refs[:-1], refs[-1]
+    tiles, tile = out.shape[1], out.shape[2] - TAIL
+    for i, (part, places) in enumerate(slots):
         for t in range(tiles):
-            at = pl.ds(t * tile, tile)
-            encode(part[send, at, :] + decode(got.at[send, t]), away.at[i, t])
-            kept[i, at, :] = part[keep, at, :] + decode(got.at[keep, t])
-
-
-def finish_kernel(part, got, pair_ref, vir_ref, *refs):
-    out_ref = refs[-1]
-    tiles, tile = got.shape[1], got.shape[2] - TAIL
+            total = parts[part, pl.ds(t * tile, tile), :]
+            for k, slot in places:
+                total = total + decode(got[k].at[slot, t])
+            encode(total, out.at[i, t])
+
+
+def finish_kernel(places, pair_ref, vir_ref, parts, *refs):
+    got, out_ref = refs[:-1], refs[-1]
+    tiles, tile = got[0].shape[1], got[0].shape[2] - TAIL
     low = is_low((tile, LANES))
     pair = pair_ref[0]
     half = tiles * tile
     for t in range(tiles):
         at = pl.ds(t * tile, tile)
-        total = part[0, at, :] + decode(got.at[0, t])
+        total = parts[0, at, :]
+        for k, slot in places:
+            total = total + decode(got[k].at[slot, t])
         virt = jnp.where(low, vir_ref[at, 0:1], vir_ref[at, 1:2])
         update = (total / (pair - virt)).T
         out_ref[:, pl.ds(t * tile, tile)] = update[:WIDTH]
@@ -157,8 +163,7 @@
     def limit(mib):
         return pltpu.CompilerParams(vmem_limit_bytes=mib * 1024 * 1024)
 
-    def cost(flops, moved):
-        return pl.CostEstimate(flops=flops, bytes_accessed=moved, transcendentals=0)
+    cost = pl.CostEstimate(flops=1024, bytes_accessed=1024, transcendentals=0)
 
     smem = pl.BlockSpec(memory_space=pltpu.SMEM)
     vmem = pl.BlockSpec(memory_space=pltpu.VMEM)
@@ -175,74 +180,66 @@
         out_specs=vmem,
         out_shape=jax.ShapeDtypeStruct((rows, depth), jnp.bfloat16),
         compiler_params=limit(16),
-        cost_estimate=cost(0, 4 * rows * depth),
+        cost_estimate=cost,
         name="transpose",
     )
-    ladder = pl.pallas_call(
-        functools.partial(ladder_kernel, chips, tile),
-        in_specs=[vmem] * (2 + chips),
-        out_specs=[vmem] * chips,
-        out_shape=[message] * chips,
-        scratch_shapes=[pltpu.VMEM((chips * WIDTH, depth), jnp.bfloat16)],
-        compiler_params=limit(16),
-        cost_estimate=cost(
-            4 * rows * depth * chips * WIDTH,
-            4 * rows * depth + 2 * chips * WIDTH * depth + 2 * chips * rows * LANES,
-        ),
-        name="ladder",
-    )
-    antisym = pl.pallas_call(
-        functools.partial(antisym_kernel, chips, slabs, vir),
-        in_specs=[smem] + [vmem] * chips,
-        out_specs=[vmem, vmem],
-        out_shape=[
-            jax.ShapeDtypeStruct((slabs // 2, part_rows, LANES), jnp.float32),
-            jax.ShapeDtypeStruct(parcel(slabs // 2), jnp.int16),
-        ],
-        scratch_shapes=[
-            pltpu.VMEM((vir * vir, LANES), jnp.float32),
-            pltpu.VMEM((part_rows, LANES), jnp.float32),
-        ],
-        compiler_params=limit(16),
-        cost_estimate=cost(8 * vir * vir * LANES, 4 * vir * vir * LANES),
-        name="antisym",
-    )
-
-    def hop(place, part, got):
-        count = part.shape[0] // 2
+
+    def ladder(gathered):
+        arrays, pieces = zip(*[(x, (start, count)) for x, start, count in gathered])
+        call = pl.pallas_call(
+            functools.partial(ladder_kernel, chips, tile, pieces),
+            in_specs=[vmem] * (2 + len(arrays)),
+            out_specs=[vmem] * chips,
+            out_shape=[message] * chips,
+            scratch_shapes=[pltpu.VMEM((chips * WIDTH, depth), jnp.bfloat16)],
+            compiler_params=limit(16),
+            cost_estimate=cost,
+            name="ladder",
+        )
+        return functools.partial(call, own_t, sib_t), arrays
+
+    def antisym(parcels):
         return pl.pallas_call(
-            hop_kernel,
-            in_specs=[smem, vmem, vmem],
-            out_specs=[vmem, vmem],
-            out_shape=[
-                jax.ShapeDtypeStruct((count, part_rows, LANES), jnp.float32),
-                jax.ShapeDtypeStruct(parcel(count), jnp.int16),
+            functools.partial(antisym_kernel, chips, slabs, vir),
+            in_specs=[smem] + [vmem] * chips,
+            out_specs=[vmem] * (1 + parcels),
+            out_shape=[jax.ShapeDtypeStruct((slabs // 2, part_rows, LANES), jnp.float32)]
+            + [jax.ShapeDtypeStruct(parcel(slabs // 2 // parcels), jnp.int16)] * parcels,
+            scratch_shapes=[
+                pltpu.VMEM((vir * vir, LANES), jnp.float32),
+                pltpu.VMEM((part_rows, LANES), jnp.float32),
             ],
+            compiler_params=limit(16),
+            cost_estimate=cost,
+            name="antisym",
+        )
+
+    def hop(slots, got_count):
+        return pl.pallas_call(
+            functools.partial(hop_kernel, slots),
+            in_specs=[vmem] * (1 + got_count),
+            out_specs=vmem,
+            out_shape=jax.ShapeDtypeStruct(parcel(len(slots)), jnp.int16),
             compiler_params=limit(8),
-            cost_estimate=cost(8 * count * part_rows * LANES, 16 * count * part_rows * LANES),
+            cost_estimate=cost,
             name="hop",
-        )(place, part, got)
-
-    def finish(r, part, got, pair, virt, so_far):
+        )
+
+    def finish(r, parts, got, places, so_far):
         given = [] if so_far is None else [so_far]
-        call = pl.pallas_call(
-            finish_kernel,
+        return pl.pallas_call(
+            functools.partial(finish_kernel, places),
             grid=(1,),
-            in_specs=[
-                vmem,
-                vmem,
-                pl.BlockSpec((1, 1, LANES), lambda i: (r, 0, 0)),
-                vmem,
-            ]
+            in_specs=[pl.BlockSpec((1, 1, LANES), lambda i: (r, 0, 0))]
+            + [vmem] * (2 + len(got))
             + [pl.BlockSpec(memory_space=pl.ANY)] * len(given),
             out_specs=pl.BlockSpec((WIDTH, 2 * part_rows), lambda i: (r, 0)),
             out_shape=jax.ShapeDtypeStruct((num_pairs, 2 * part_rows), jnp.float32),
-            input_output_aliases={4: 0} if given else {},
+            input_output_aliases={3 + len(got): 0} if given else {},
             compiler_params=limit(8),
-            cost_estimate=cost(16 * part_rows * LANES, 16 * part_rows * LANES),
+            cost_estimate=cost,
             name="finish",
-        )
-        return call(part, got, pair, virt, *given)
+        )(eps_pair, eps_virt, parts, *got, *given)
 
     sib_t = transpose(lax.ppermute(integrals, "pair", [(i, i ^ 1) for i in range(devices)]))
     own_t = transpose(integrals)
@@ -259,36 +256,79 @@
 
     place = jnp.stack([chip, core, z]).astype(jnp.int32)
 
-    gathered = []
-    for r in range(chunks):
-        mine = amplitudes[r * WIDTH : (r + 1) * WIDTH]
-        if gathered:
-            mine, *gathered[-1] = lax.optimization_barrier((mine, *gathered[-1]))
-        gathered.append([mine] + [to_chip(mine, d) for d in range(1, chips)])
+    def gather(mine, beside=()):
+        count = mine.shape[0]
+        if chips != 4:
+            return [[(x, 0, count)] for x in [mine] + [to_chip(mine, d) for d in range(1, chips)]]
+        one, two = to_chip(mine, 1), to_chip(mine, 2)
+        if beside:
+            one, two, *_ = lax.optimization_barrier((one, two, *beside))
+        low, high = to_chip(two[: count // 2], 1), to_chip(one[count // 2 :], 2)
+        parts = [(low, 0, count // 2), (high, 0, count // 2)]
+        return [[(mine, 0, count)], [(one, 0, count)], [(two, 0, count)], parts]
+
+    def cut(pieces, start, count):
+        found, at = [], 0
+        for x, first, rows_of in pieces:
+            begin, end = max(start, at), min(start + count, at + rows_of)
+            if begin < end:
+                found.append((x, first + begin - at, end - begin))
+            at += rows_of
+        return found
+
+    head = gather(amplitudes[:WIDTH], (own_t,))
+    arrays = [x for pieces in head for x, _, _ in pieces]
+    rest = amplitudes[WIDTH:]
+    rest, own_t, sib_t, *arrays = lax.optimization_barrier((rest, own_t, sib_t, *arrays))
+    fresh = iter(arrays)
+    head = [[(next(fresh), start, count) for _, start, count in pieces] for pieces in head]
+    tail = gather(rest)
+
+    def rows_of(r):
         if r == 0:
-            own_t, *gathered[0] = lax.optimization_barrier((own_t, *gathered[0]))
+            return [piece for pieces in head for piece in pieces]
+        return [piece for pieces in tail for piece in cut(pieces, (r - 1) * WIDTH, WIDTH)]
 
     def across(x, level):
         return lax.ppermute(x, "slab", [(i, i ^ level) for i in range(slabs)])
 
     def stages(r):
-        sums = yield functools.partial(ladder, own_t, sib_t), *gathered[r]
+        sums = yield ladder(rows_of(r))
         arrived = [to_chip(sums[d], d) for d in range(1, chips)]
-        kept, away = yield functools.partial(antisym, place, sums[0]), *arrived
-        got, level = across(away, 1), 2
+        parcels = slabs // 2 if r == chunks - 1 else 1
+        parts, *away = yield functools.partial(antisym(parcels), place, sums[0]), arrived
+        away = [across(x, 1) for x in reversed(away)][::-1]
+        each = slabs // 2 // parcels
+        held = {e: [(away[e // 2 // each], e // 2 % each)] for e in range(0, slabs, 2)}
+
+        def listed(wanted):
+            arrays = []
+            for e in wanted:
+                arrays += [x for x, _ in held[e] if not any(x is y for y in arrays)]
+            index = {id(x): k for k, x in enumerate(arrays)}
+            return arrays, [(e // 2, [(index[id(x)], i) for x, i in held[e]]) for e in wanted]
+
+        level = 2
         while level < slabs:
-            bit = (z // level % 2)[None].astype(jnp.int32)
-            kept, away = yield functools.partial(hop, bit, kept), got
-            got, level = across(away, level), 2 * level
-        yield functools.partial(finish, r, kept), got
+            leave = [e for e in held if e & level]
+            got, slots = listed(leave)
+            call = hop(slots, len(got))
+            (out,) = yield (lambda *args, call=call: [call(parts, *args)]), got
+            out = across(out, level)
+            for i, e in enumerate(leave):
+                held[e ^ level].append((out, i))
+                del held[e]
+            level *= 2
+        got, ((_, places),) = listed([0])
+        yield (lambda *args: finish(r, parts, args, places, update)), got
 
     length = 3 + max(0, (slabs - 1).bit_length() - 1)
 
     def when(stage):
         r, k = stage
         if k == 0:
-            return 18 * r + 14
-        return 18 * r + 38 + (k - 1) * (17 + 2 * r) + (12 if k == length - 1 else 0)
+            return 38 + 7 * r if r else 14
+        return 18 * r + 40 + (k - 1) * (17 + 2 * r) + (12 if k == length - 1 else 0)
 
     order = sorted(((r, k) for r in range(chunks) for k in range(length)), key=when)
 
@@ -296,11 +336,11 @@
     results = [None] * chunks
     update = token = None
     for r, k in order:
-        call, *inputs = running[r].send(results[r])
+        call, inputs = running[r].send(results[r])
         if token is not None:
             *inputs, token = lax.optimization_barrier((*inputs, token))
         if k == length - 1:
-            update = call(*inputs, eps_pair, eps_virt, update)
+            update = call(*inputs)
         else:
             results[r] = call(*inputs)
             token = results[r][-1]

time: 148 us -> 168 us (1.14)
  local copies, waits for them, and re-layouts: 8.71 us -> 19.6 us
  waiting for transfers between devices: 61.8 us -> 66.3 us
  starting transfers between devices: 28.5 us -> 32.8 us
  other arithmetic: 0.49 us -> 2.47 us
  Pallas kernels: 48 us -> 46.3 us
    ppermute x18 -> x17, waiting for transfers between devices: 27.3 us -> 41.3 us  [to_chip(): return lax.ppermute(x, 'pair', [(i, i ^ d * CORES) for i in range(devices)])]
    ppermute x6 -> x7, waiting for transfers between devices: 34.5 us -> 25 us  [across(): return lax.ppermute(x, 'slab', [(i, i ^ level) for i in range(slabs)])]
    unnamed x32 -> x36, local copies, waits for them, and re-layouts: 7.17 us -> 15.1 us
    pallas_call x6, Pallas kernels: 7.5 us -> 11.3 us  [the longest x3 7.3 us: finish(): pl.pallas_call(functools.partial(finish_kernel, places), grid=(1,), in_sp...]
    pallas_call x1, Pallas kernels: 6.44 us -> 2.87 us  [on_device(): transpose(lax.ppermute(integrals, 'pair', [(i, i ^ 1) for i in range(devi...]
    ppermute x6 -> x7, starting transfers between devices: 5.91 us -> 9.33 us  [across(): return lax.ppermute(x, 'slab', [(i, i ^ level) for i in range(slabs)])]
    pallas_call x6, Pallas kernels: 31.2 us -> 29.3 us  [on_device(): results[r] = call(*inputs)]
    ppermute x18 -> x17, starting transfers between devices: 22.1 us -> 23.1 us  [to_chip(): return lax.ppermute(x, 'pair', [(i, i ^ d * CORES) for i in range(devices)])]
  transfers between devices with their start and end apart: 25 -> 25, of which waited for: 12 -> 11; matrix products, arithmetic and copies ran while one was open for 1% -> 4% of each run, Pallas kernels for 28% -> 25%
where the time goes in v5:
time: 168 us
  waiting for transfers between devices  66.3 us (39%)
  Pallas kernels  46.3 us (28%)
  starting transfers between devices  32.8 us (20%)
  local copies, waits for them, and re-layouts  19.6 us (12%)
  other arithmetic  2.47 us (1%)
    ppermute x17, waiting for transfers between devices, to_chip(): return lax.ppermute(x, 'pair', [(i, i ^ d * CORES) for i in range(devices)])  41.3 us
    pallas_call x6, Pallas kernels, on_device(): results[r] = call(*inputs)  29.3 us
    ppermute x7, waiting for transfers between devices, across(): return lax.ppermute(x, 'slab', [(i, i ^ level) for i in range(slabs)])  25 us
    ppermute x17, starting transfers between devices, to_chip(): return lax.ppermute(x, 'pair', [(i, i ^ d * CORES) for i in range(devices)])  23.1 us
    unnamed x36, local copies, waits for them, and re-layouts  15.1 us
    ppermute x7, starting transfers between devices, across(): return lax.ppermute(x, 'slab', [(i, i ^ level) for i in range(slabs)])  9.33 us
    pallas_call x3, Pallas kernels, finish(): pl.pallas_call(functools.partial(finish_kernel, places), grid=(1,), in_sp...  7.3 us
    pallas_call x3, Pallas kernels, stages(): out, = (yield (lambda *args, call=call: [call(parts, *args)], got))  4.02 us
  transfers between devices with their start and end apart: 25, of which 11 were waited for; matrix products, arithmetic and copies ran while one was open for 4% of the time, Pallas kernels for 25%

profile of v5, /device:TPU:0, one launch (start us, length us, event | category | flops | bytes accessed | tf_op | source)
XLA Modules:
  0.0 167.7 jit_solution(7100872216990167289)
XLA Ops:
  0.5 1.0 slice.27.refs_0_
  1.4 2.6 %collective-permute-start.1 = (bf16[64,2304]{1,0:T(8,128)(2,1)S(1)}, bf16[64,2304]{1,0:T(8,128)(2,1)S(1)}, u32[]{:S(2)}, u32[]{:S(2)}) collective-permute-start(bf16[64,2304]{1,0:T(8,128)(2,1)S(1)} %slice.27.refs_0_), channel_id=1, source_target_pairs={{0,8},{4,12},{8,0},{12,4},{16,24},{20,28},{24,16},{28,20},{1,9},{5... | collective-permute-start | bytes 884744 | tf_op jit(solution)/shard_map/ppermute | solution.py:161
  4.0 1.5 collective-permute-start.2
  5.5 2.5 %copy-done.4 = bf16[2304,1152]{1,0:T(8,128)(2,1)S(1)} copy-done((bf16[2304,1152]{1,0:T(8,128)(2,1)S(1)}, bf16[2304,1152]{1,0:T(8,128)(2,1)}, u32[]{:S(2)}) %copy-start.4) | copy-done | bytes 5308440
  8.0 2.9 %transpose.14.own_ref = bf16[1152,2304]{1,0:T(8,128)(2,1)S(1)} custom-call(bf16[2304,1152]{1,0:T(8,128)(2,1)S(1)} %copy-done.4), custom_call_target="tpu_custom_call" | custom-call | flops 1024 | bytes 1024 | tf_op jit(solution)/shard_map/transpose/pallas_call | solution.py:245
  11.7 1.5 collective-permute-done.2.refs_2_
  13.6 1.8 %collective-permute-start.4 = (bf16[32,2304]{1,0:T(8,128)(2,1)S(1)}, bf16[32,2304]{1,0:T(8,128)(2,1)S(1)}, u32[]{:S(2)}, u32[]{:S(2)}) collective-permute-start(bf16[32,2304]{1,0:T(8,128)(2,1)S(1)} %slice.29), channel_id=1, source_target_pairs={{0,16},{4,20},{8,24},{12,28},{16,0},{20,4},{24,8},{28,12},{1,17},{... | collective-permute-start | bytes 442376 | tf_op jit(solution)/shard_map/ppermute | solution.py:161
  15.4 2.9 %transpose.15.sib_ref = bf16[1152,2304]{1,0:T(8,128)(2,1)S(1)} custom-call(bf16[2304,1152]{1,0:T(8,128)(2,1)S(1)} %collective-permute-done.in_ref), custom_call_target="tpu_custom_call" | custom-call | flops 1024 | bytes 1024 | tf_op jit(solution)/shard_map/transpose/pallas_call | solution.py:244
  18.8 1.6 collective-permute-start.6
  20.5 5.1 %ladder.3 = (s16[3,400,128]{2,1,0:T(8,128)(2,1)S(1)}, s16[3,400,128]{2,1,0:T(8,128)(2,1)}, s16[3,400,128]{2,1,0:T(8,128)(2,1)}, s16[3,400,128]{2,1,0:T(8,128)(2,1)}) custom-call(bf16[1152,2304]{1,0:T(8,128)(2,1)S(1)} %transpose.14.own_ref, bf16[1152,2304]{1,0:T(8,128)(2,1)S(1)} %transpose.15.sib_ref, bf16[64,2304]{1,0:T(8,128)(2,1)S(1)} %slice.27.refs_0_, ...), custom_call_target="tpu_custom_call" | custom-call | flops 1024 | bytes 1024 | tf_op jit(solution)/shard_map/ladder/pallas_call | solution.py:345
  26.0 2.6 %collective-permute-start.11 = (s16[3,400,128]{2,1,0:T(8,128)(2,1)}, s16[3,400,128]{2,1,0:T(8,128)(2,1)S(1)}, u32[]{:S(2)}, u32[]{:S(2)}) collective-permute-start(s16[3,400,128]{2,1,0:T(8,128)(2,1)} %get-tuple-element.72), channel_id=1, source_target_pairs={{0,24},{4,28},{8,16},{12,20},{16,8},{20,12},{24,0},{28,4},{1,25},{... | collective-permute-start | bytes 921608 | tf_op jit(solution)/shard_map/ppermute | solution.py:161
  29.1 1.5 collective-permute-start.5
  30.7 15.1 %collective-permute-done.10.refs_2_ = s16[3,400,128]{2,1,0:T(8,128)(2,1)S(1)} collective-permute-done((s16[3,400,128]{2,1,0:T(8,128)(2,1)}, s16[3,400,128]{2,1,0:T(8,128)(2,1)S(1)}, u32[]{:S(2)}, u32[]{:S(2)}) %collective-permute-start.10) | collective-permute-done | bytes 307232 | tf_op jit(solution)/shard_map/ppermute | solution.py:161
  48.0 1.0 copy-done.8
  48.9 1.0 copy-done.10
  49.9 1.0 copy-done.12
  50.9 4.7 %antisym.3 = (f32[2,1152,128]{2,1,0:T(8,128)S(1)}, s16[2,3,400,128]{3,2,1,0:T(8,128)(2,1)S(1)}) custom-call(s32[3]{0:T(128)S(1)} %pad_add_fusion.place_ref, s16[3,400,128]{2,1,0:T(8,128)(2,1)S(1)} %get-tuple-element.69.refs_0_, s16[3,400,128]{2,1,0:T(8,128)(2,1)S(1)} %copy-done.12, s16[3,400,128]{2,1,0:T(8,128)(2,1)S(1)} %copy-done.8, ...), custom_call_target="tpu_custom_call" | custom-call | flops 1024 | bytes 1024 | tf_op jit(solution)/shard_map/antisym/pallas_call | solution.py:345
  55.6 1.6 collective-permute-start.18
  57.2 1.5 collective-permute-start.8
  58.7 5.3 %collective-permute-done.8.refs_3_ = bf16[64,2304]{1,0:T(8,128)(2,1)S(1)} collective-permute-done((bf16[64,2304]{1,0:T(8,128)(2,1)S(1)}, bf16[64,2304]{1,0:T(8,128)(2,1)S(1)}, u32[]{:S(2)}, u32[]{:S(2)}) %collective-permute-start.8) | collective-permute-done | bytes 294944 | tf_op jit(solution)/shard_map/ppermute | solution.py:161
  64.0 2.5 %copy-done.1 = bf16[1152,2304]{1,0:T(8,128)(2,1)S(1)} copy-done((bf16[1152,2304]{1,0:T(8,128)(2,1)S(1)}, bf16[1152,2304]{1,0:T(8,128)(2,1)}, u32[]{:S(2)}) %copy-start.1) | copy-done | bytes 5308440
  66.5 2.5 %copy-done.3 = bf16[1152,2304]{1,0:T(8,128)(2,1)S(1)} copy-done((bf16[1152,2304]{1,0:T(8,128)(2,1)S(1)}, bf16[1152,2304]{1,0:T(8,128)(2,1)}, u32[]{:S(2)}) %copy-start.3) | copy-done | bytes 5308440
  69.0 4.2 %ladder.4 = (s16[3,400,128]{2,1,0:T(8,128)(2,1)S(1)}, s16[3,400,128]{2,1,0:T(8,128)(2,1)S(1)}, s16[3,400,128]{2,1,0:T(8,128)(2,1)S(1)}, s16[3,400,128]{2,1,0:T(8,128)(2,1)S(1)}) custom-call(bf16[1152,2304]{1,0:T(8,128)(2,1)S(1)} %copy-done.1, bf16[1152,2304]{1,0:T(8,128)(2,1)S(1)} %copy-done.3, bf16[128,2304]{1,0:T(8,128)(2,1)S(1)} %slice.26.refs_0_, ...), custom_call_target="tpu_custom_call" | custom-call | flops 1024 | bytes 1024 | tf_op jit(solution)/shard_map/ladder/pallas_call | solution.py:345
  73.2 1.5 collective-permute-start.15
  74.7 1.5 collective-permute-start.16
  76.8 1.6 collective-permute-start.7
  78.4 14.3 %collective-permute-done.7.refs_3_ = bf16[64,2304]{1,0:T(8,128)(2,1)S(1)} collective-permute-done((bf16[64,2304]{1,0:T(8,128)(2,1)S(1)}, bf16[64,2304]{1,0:T(8,128)(2,1)S(1)}, u32[]{:S(2)}, u32[]{:S(2)}) %collective-permute-start.7) | collective-permute-done | bytes 294944 | tf_op jit(solution)/shard_map/ppermute | solution.py:161
  92.7 4.2 %ladder.5 = (s16[3,400,128]{2,1,0:T(8,128)(2,1)S(1)}, s16[3,400,128]{2,1,0:T(8,128)(2,1)S(1)}, s16[3,400,128]{2,1,0:T(8,128)(2,1)S(1)}, s16[3,400,128]{2,1,0:T(8,128)(2,1)S(1)}) custom-call(bf16[1152,2304]{1,0:T(8,128)(2,1)S(1)} %copy-done.1, bf16[1152,2304]{1,0:T(8,128)(2,1)S(1)} %copy-done.3, bf16[128,2304]{1,0:T(8,128)(2,1)S(1)} %slice.26.refs_0_, ...), custom_call_target="tpu_custom_call" | custom-call | flops 1024 | bytes 1024 | tf_op jit(solution)/shard_map/ladder/pallas_call | solution.py:345
  97.7 1.5 collective-permute-start.13
  99.2 1.3 collective-permute-start.14
  101.4 5.5 %antisym.4 = (f32[2,1152,128]{2,1,0:T(8,128)S(1)}, s16[2,3,400,128]{3,2,1,0:T(8,128)(2,1)}) custom-call(s32[3]{0:T(128)S(1)} %pad_add_fusion.place_ref, s16[3,400,128]{2,1,0:T(8,128)(2,1)S(1)} %get-tuple-element.90.refs_0_, s16[3,400,128]{2,1,0:T(8,128)(2,1)S(1)} %collective-permute-done.15.refs_1_, s16[3,400,128]{2,1,0:T(8,128)(2,1)S(1)} %collective-permute-done.16.refs_2_, ...), custom_call_target="tpu_custom_call" | custom-call | flops 1024 | bytes 1024 | tf_op jit(solution)/shard_map/antisym/pallas_call | solution.py:345
  107.1 2.0 %collective-permute-done.13.refs_2_ = s16[3,400,128]{2,1,0:T(8,128)(2,1)S(1)} collective-permute-done((s16[3,400,128]{2,1,0:T(8,128)(2,1)S(1)}, s16[3,400,128]{2,1,0:T(8,128)(2,1)S(1)}, u32[]{:S(2)}, u32[]{:S(2)}) %collective-permute-start.13) | collective-permute-done | bytes 307232 | tf_op jit(solution)/shard_map/ppermute | solution.py:161
  109.1 1.7 %collective-permute-done.14.refs_3_ = s16[3,400,128]{2,1,0:T(8,128)(2,1)S(1)} collective-permute-done((s16[3,400,128]{2,1,0:T(8,128)(2,1)S(1)}, s16[3,400,128]{2,1,0:T(8,128)(2,1)S(1)}, u32[]{:S(2)}, u32[]{:S(2)}) %collective-permute-start.14) | collective-permute-done | bytes 307232 | tf_op jit(solution)/shard_map/ppermute | solution.py:161
  110.8 5.4 %antisym.5 = (f32[2,1152,128]{2,1,0:T(8,128)S(1)}, s16[1,3,400,128]{3,2,1,0:T(8,128)(2,1)S(1)}, s16[1,3,400,128]{3,2,1,0:T(8,128)(2,1)}) custom-call(s32[3]{0:T(128)S(1)} %pad_add_fusion.place_ref, s16[3,400,128]{2,1,0:T(8,128)(2,1)S(1)} %get-tuple-element.86.refs_0_, s16[3,400,128]{2,1,0:T(8,128)(2,1)S(1)} %collective-permute-done.12.refs_1_, ...), custom_call_target="tpu_custom_call" | custom-call | flops 1024 | bytes 1024 | tf_op jit(solution)/shard_map/antisym/pallas_call | solution.py:345
  117.7 2.8 %collective-permute-start.24 = (s16[1,3,400,128]{3,2,1,0:T(8,128)(2,1)}, s16[1,3,400,128]{3,2,1,0:T(8,128)(2,1)}, u32[]{:S(2)}, u32[]{:S(2)}) collective-permute-start(s16[1,3,400,128]{3,2,1,0:T(8,128)(2,1)} %copy-done.13), channel_id=1, source_target_pairs={{0,2},{1,3},{2,0},{3,1},{4,6},{5,7},{6,4},{7,5},{8,10},{9,11},{10,... | collective-permute-start | bytes 921608 | tf_op jit(solution)/shard_map/ppermute | solution.py:293
  120.5 1.9 %collective-permute-start.19 = (s16[1,3,400,128]{3,2,1,0:T(8,128)(2,1)}, s16[1,3,400,128]{3,2,1,0:T(8,128)(2,1)}, u32[]{:S(2)}, u32[]{:S(2)}) collective-permute-start(s16[1,3,400,128]{3,2,1,0:T(8,128)(2,1)} %copy-done.14), channel_id=1, source_target_pairs={{0,1},{1,0},{2,3},{3,2},{4,5},{5,4},{6,7},{7,6},{8,9},{9,8},{10,11... | collective-permute-start | bytes 921608 | tf_op jit(solution)/shard_map/ppermute | solution.py:293
  122.3 14.0 %collective-permute-done.20.refs_0_ = s16[1,3,400,128]{3,2,1,0:T(8,128)(2,1)} collective-permute-done((s16[1,3,400,128]{3,2,1,0:T(8,128)(2,1)}, s16[1,3,400,128]{3,2,1,0:T(8,128)(2,1)}, u32[]{:S(2)}, u32[]{:S(2)}) %collective-permute-start.20) | collective-permute-done | bytes 307232 | tf_op jit(solution)/shard_map/ppermute | solution.py:293
  136.4 1.9 %hop.4 = s16[1,3,400,128]{3,2,1,0:T(8,128)(2,1)} custom-call(f32[2,1152,128]{2,1,0:T(8,128)S(1)} %get-tuple-element.102.parts, s16[1,3,400,128]{3,2,1,0:T(8,128)(2,1)} %collective-permute-done.20.refs_0_), custom_call_target="tpu_custom_call" | custom-call | flops 1024 | bytes 1024 | tf_op jit(solution)/shard_map/hop/pallas_call | solution.py:316
  138.2 1.6 collective-permute-start.21
  139.8 2.0 %hop.5 = s16[1,3,400,128]{3,2,1,0:T(8,128)(2,1)} custom-call(f32[2,1152,128]{2,1,0:T(8,128)S(1)} %get-tuple-element.107.parts, s16[2,3,400,128]{3,2,1,0:T(8,128)(2,1)} %collective-permute-done.22.refs_0_), custom_call_target="tpu_custom_call" | custom-call | flops 1024 | bytes 1024 | tf_op jit(solution)/shard_map/hop/pallas_call | solution.py:316
  141.8 1.4 collective-permute-start.23
  146.0 1.3 add.44
  147.5 0.8 pad_maximum_fusion.pair_ref
  148.3 11.0 %collective-permute-done.21.refs_1_ = s16[1,3,400,128]{3,2,1,0:T(8,128)(2,1)} collective-permute-done((s16[1,3,400,128]{3,2,1,0:T(8,128)(2,1)}, s16[1,3,400,128]{3,2,1,0:T(8,128)(2,1)}, u32[]{:S(2)}, u32[]{:S(2)}) %collective-permute-start.21) | collective-permute-done | bytes 307232 | tf_op jit(solution)/shard_map/ppermute | solution.py:293
  159.3 1.1 copy-done.6
  160.4 2.3 %finish.3.refs_2_ = f32[192,2304]{1,0:T(8,128)} custom-call(f32[3,1,128]{2,1,0:T(1,128)S(1)} %pad_maximum_fusion.pair_ref, f32[1152,2]{1,0:T(8,128)S(1)} %bitcast.10, f32[2,1152,128]{2,1,0:T(8,128)S(1)} %get-tuple-element.93.parts, s16[2,3,400,128]{3,2,1,0:T(8,128)(2,1)S(1)} %copy-done.6, s16[1,3,400,128]{3,2,1,0:T(8,128)(2,1)} %collective-permute-done.24.refs_1_), custom_call_target="tpu_custom_call" | custom-call | flops 1024 | bytes 1024 | tf_op jit(solution)/shard_map/finish/pallas_call | solution.py:230
  162.7 2.5 %finish.4.refs_2_ = f32[192,2304]{1,0:T(8,128)} custom-call(f32[3,1,128]{2,1,0:T(1,128)S(1)} %pad_maximum_fusion.pair_ref, f32[1152,2]{1,0:T(8,128)S(1)} %bitcast.11, f32[2,1152,128]{2,1,0:T(8,128)S(1)} %get-tuple-element.107.parts, s16[2,3,400,128]{3,2,1,0:T(8,128)(2,1)} %collective-permute-done.22.refs_0_, ...), custom_call_target="tpu_custom_call", output_to_operand_aliasing={{}: (5, {})} | custom-call | flops 1024 | bytes 1024 | tf_op jit(solution)/shard_map/finish/pallas_call | solution.py:230
  165.2 2.4 %finish.5 = f32[192,2304]{1,0:T(8,128)} custom-call(f32[3,1,128]{2,1,0:T(1,128)S(1)} %pad_maximum_fusion.pair_ref, f32[1152,2]{1,0:T(8,128)S(1)} %bitcast.12, f32[2,1152,128]{2,1,0:T(8,128)S(1)} %get-tuple-element.102.parts, s16[1,3,400,128]{3,2,1,0:T(8,128)(2,1)} %collective-permute-done.19.refs_0_, ...), custom_call_target="tpu_custom_call", output_to_operand_aliasing={{}: (5, {})} | custom-call | flops 1024 | bytes 1024 | tf_op jit(solution)/shard_map/finish/pallas_call | solution.py:230
  (70 shorter events, 12.2 us)
Async XLA Ops:
  0.0 15.4 %collective-permute-start = (bf16[2304,1152]{1,0:T(8,128)(2,1)}, bf16[2304,1152]{1,0:T(8,128)(2,1)S(1)}, u32[]{:S(2)}, u32[]{:S(2)}) collective-permute-start(bf16[2304,1152]{1,0:T(8,128)(2,1)} %in_ref.1), channel_id=1, source_target_pairs={{0,4},{4,0},{8,12},{12,8},{16,20},{20,16},{24,28},{28,24},{1,5},{5... | collective-permute-start | bytes 15925256 | tf_op jit(solution)/shard_map/ppermute | solution.py:244
  1.4 10.2 %collective-permute-start.1 = (bf16[64,2304]{1,0:T(8,128)(2,1)S(1)}, bf16[64,2304]{1,0:T(8,128)(2,1)S(1)}, u32[]{:S(2)}, u32[]{:S(2)}) collective-permute-start(bf16[64,2304]{1,0:T(8,128)(2,1)S(1)} %slice.27.refs_0_), channel_id=1, source_target_pairs={{0,8},{4,12},{8,0},{12,4},{16,24},{20,28},{24,16},{28,20},{1,9},{5... | collective-permute-start | bytes 884744 | tf_op jit(solution)/shard_map/ppermute | solution.py:161
  4.0 9.1 %collective-permute-start.2 = (bf16[64,2304]{1,0:T(8,128)(2,1)S(1)}, bf16[64,2304]{1,0:T(8,128)(2,1)S(1)}, u32[]{:S(2)}, u32[]{:S(2)}) collective-permute-start(bf16[64,2304]{1,0:T(8,128)(2,1)S(1)} %slice.27.refs_0_), channel_id=1, source_target_pairs={{0,16},{4,20},{8,24},{12,28},{16,0},{20,4},{24,8},{28,12},{1,17},{... | collective-permute-start | bytes 884744 | tf_op jit(solution)/shard_map/ppermute | solution.py:161
  5.5 2.5 %copy-start.4 = (bf16[2304,1152]{1,0:T(8,128)(2,1)S(1)}, bf16[2304,1152]{1,0:T(8,128)(2,1)}, u32[]{:S(2)}) copy-start(bf16[2304,1152]{1,0:T(8,128)(2,1)} %in_ref.1) | copy-start | bytes 15925252
  8.0 7.3 %copy-start.15 = (bf16[192,2304]{1,0:T(8,128)(2,1)S(1)}, bf16[192,2304]{1,0:T(8,128)(2,1)}, u32[]{:S(2)}) copy-start(bf16[192,2304]{1,0:T(8,128)(2,1)} %param.5) | copy-start | bytes 2654212
  10.9 9.6 %copy-start = (bf16[1152,2304]{1,0:T(8,128)(2,1)}, bf16[1152,2304]{1,0:T(8,128)(2,1)S(1)}, u32[]{:S(2)}) copy-start(bf16[1152,2304]{1,0:T(8,128)(2,1)S(1)} %transpose.14.own_ref) | copy-start | bytes 15925252
  13.1 5.2 %collective-permute-start.3 = (bf16[32,2304]{1,0:T(8,128)(2,1)S(1)}, bf16[32,2304]{1,0:T(8,128)(2,1)S(1)}, u32[]{:S(2)}, u32[]{:S(2)}) collective-permute-start(bf16[32,2304]{1,0:T(8,128)(2,1)S(1)} %slice.28), channel_id=1, source_target_pairs={{0,8},{4,12},{8,0},{12,4},{16,24},{20,28},{24,16},{28,20},{1,9},{5... | collective-permute-start | bytes 442376 | tf_op jit(solution)/shard_map/ppermute | solution.py:161
  13.6 5.3 %collective-permute-start.4 = (bf16[32,2304]{1,0:T(8,128)(2,1)S(1)}, bf16[32,2304]{1,0:T(8,128)(2,1)S(1)}, u32[]{:S(2)}, u32[]{:S(2)}) collective-permute-start(bf16[32,2304]{1,0:T(8,128)(2,1)S(1)} %slice.29), channel_id=1, source_target_pairs={{0,16},{4,20},{8,24},{12,28},{16,0},{20,4},{24,8},{28,12},{1,17},{... | collective-permute-start | bytes 442376 | tf_op jit(solution)/shard_map/ppermute | solution.py:161
  18.3 7.3 %copy-start.2 = (bf16[1152,2304]{1,0:T(8,128)(2,1)}, bf16[1152,2304]{1,0:T(8,128)(2,1)S(1)}, u32[]{:S(2)}) copy-start(bf16[1152,2304]{1,0:T(8,128)(2,1)S(1)} %transpose.15.sib_ref) | copy-start | bytes 15925252
  18.8 38.3 %collective-permute-start.6 = (bf16[128,2304]{1,0:T(8,128)(2,1)S(1)}, bf16[128,2304]{1,0:T(8,128)(2,1)S(1)}, u32[]{:S(2)}, u32[]{:S(2)}) collective-permute-start(bf16[128,2304]{1,0:T(8,128)(2,1)S(1)} %slice.26.refs_0_), channel_id=1, source_target_pairs={{0,16},{4,20},{8,24},{12,28},{16,0},{20,4},{24,8},{28,12},{1,17},{... | collective-permute-start | bytes 1769480 | tf_op jit(solution)/shard_map/ppermute | solution.py:161
  25.6 20.2 %collective-permute-start.10 = (s16[3,400,128]{2,1,0:T(8,128)(2,1)}, s16[3,400,128]{2,1,0:T(8,128)(2,1)S(1)}, u32[]{:S(2)}, u32[]{:S(2)}) collective-permute-start(s16[3,400,128]{2,1,0:T(8,128)(2,1)} %get-tuple-element.71), channel_id=1, source_target_pairs={{0,16},{4,20},{8,24},{12,28},{16,0},{20,4},{24,8},{28,12},{1,17},{... | collective-permute-start | bytes 921608 | tf_op jit(solution)/shard_map/ppermute | solution.py:161
  26.0 20.5 %collective-permute-start.11 = (s16[3,400,128]{2,1,0:T(8,128)(2,1)}, s16[3,400,128]{2,1,0:T(8,128)(2,1)S(1)}, u32[]{:S(2)}, u32[]{:S(2)}) collective-permute-start(s16[3,400,128]{2,1,0:T(8,128)(2,1)} %get-tuple-element.72), channel_id=1, source_target_pairs={{0,24},{4,28},{8,16},{12,20},{16,8},{20,12},{24,0},{28,4},{1,25},{... | collective-permute-start | bytes 921608 | tf_op jit(solution)/shard_map/ppermute | solution.py:161
  28.6 18.7 %collective-permute-start.9 = (s16[3,400,128]{2,1,0:T(8,128)(2,1)}, s16[3,400,128]{2,1,0:T(8,128)(2,1)S(1)}, u32[]{:S(2)}, u32[]{:S(2)}) collective-permute-start(s16[3,400,128]{2,1,0:T(8,128)(2,1)} %get-tuple-element.70), channel_id=1, source_target_pairs={{0,8},{4,12},{8,0},{12,4},{16,24},{20,28},{24,16},{28,20},{1,9},{5... | collective-permute-start | bytes 921608 | tf_op jit(solution)/shard_map/ppermute | solution.py:161
  29.1 29.6 %collective-permute-start.5 = (bf16[128,2304]{1,0:T(8,128)(2,1)S(1)}, bf16[128,2304]{1,0:T(8,128)(2,1)S(1)}, u32[]{:S(2)}, u32[]{:S(2)}) collective-permute-start(bf16[128,2304]{1,0:T(8,128)(2,1)S(1)} %slice.26.refs_0_), channel_id=1, source_target_pairs={{0,8},{4,12},{8,0},{12,4},{16,24},{20,28},{24,16},{28,20},{1,9},{5... | collective-permute-start | bytes 1769480 | tf_op jit(solution)/shard_map/ppermute | solution.py:161
  45.8 0.7 copy-start.7
  46.5 0.7 copy-start.9
  47.2 0.7 copy-start.11
  48.0 1.0 copy-start.8
  48.9 1.0 copy-start.10
  49.9 1.0 copy-start.12
  55.6 42.1 %collective-permute-start.18 = (s16[2,3,400,128]{3,2,1,0:T(8,128)(2,1)S(1)}, s16[2,3,400,128]{3,2,1,0:T(8,128)(2,1)S(1)}, u32[]{:S(2)}, u32[]{:S(2)}) collective-permute-start(s16[2,3,400,128]{3,2,1,0:T(8,128)(2,1)S(1)} %get-tuple-element.76), channel_id=1, source_target_pairs={{0,1},{1,0},{2,3},{3,2},{4,5},{5,4},{6,7},{7,6},{8,9},{9,8},{10,11... | collective-permute-start | bytes 1843208 | tf_op jit(solution)/shard_map/ppermute | solution.py:293
  57.2 6.8 %collective-permute-start.8 = (bf16[64,2304]{1,0:T(8,128)(2,1)S(1)}, bf16[64,2304]{1,0:T(8,128)(2,1)S(1)}, u32[]{:S(2)}, u32[]{:S(2)}) collective-permute-start(bf16[64,2304]{1,0:T(8,128)(2,1)S(1)} %slice.33), channel_id=1, source_target_pairs={{0,8},{4,12},{8,0},{12,4},{16,24},{20,28},{24,16},{28,20},{1,9},{5... | collective-permute-start | bytes 884744 | tf_op jit(solution)/shard_map/ppermute | solution.py:161
  63.9 2.5 %copy-start.1 = (bf16[1152,2304]{1,0:T(8,128)(2,1)S(1)}, bf16[1152,2304]{1,0:T(8,128)(2,1)}, u32[]{:S(2)}) copy-start(bf16[1152,2304]{1,0:T(8,128)(2,1)} %copy-done) | copy-start | bytes 15925252
  66.5 2.5 %copy-start.3 = (bf16[1152,2304]{1,0:T(8,128)(2,1)S(1)}, bf16[1152,2304]{1,0:T(8,128)(2,1)}, u32[]{:S(2)}) copy-start(bf16[1152,2304]{1,0:T(8,128)(2,1)} %copy-done.2) | copy-start | bytes 15925252
  73.2 26.0 %collective-permute-start.15 = (s16[3,400,128]{2,1,0:T(8,128)(2,1)S(1)}, s16[3,400,128]{2,1,0:T(8,128)(2,1)S(1)}, u32[]{:S(2)}, u32[]{:S(2)}) collective-permute-start(s16[3,400,128]{2,1,0:T(8,128)(2,1)S(1)} %get-tuple-element.91), channel_id=1, source_target_pairs={{0,8},{4,12},{8,0},{12,4},{16,24},{20,28},{24,16},{28,20},{1,9},{5... | collective-permute-start | bytes 921608 | tf_op jit(solution)/shard_map/ppermute | solution.py:161
  74.7 26.7 %collective-permute-start.16 = (s16[3,400,128]{2,1,0:T(8,128)(2,1)S(1)}, s16[3,400,128]{2,1,0:T(8,128)(2,1)S(1)}, u32[]{:S(2)}, u32[]{:S(2)}) collective-permute-start(s16[3,400,128]{2,1,0:T(8,128)(2,1)S(1)} %get-tuple-element.92), channel_id=1, source_target_pairs={{0,16},{4,20},{8,24},{12,28},{16,0},{20,4},{24,8},{28,12},{1,17},{... | collective-permute-start | bytes 921608 | tf_op jit(solution)/shard_map/ppermute | solution.py:161
  76.2 25.2 %collective-permute-start.17 = (s16[3,400,128]{2,1,0:T(8,128)(2,1)S(1)}, s16[3,400,128]{2,1,0:T(8,128)(2,1)S(1)}, u32[]{:S(2)}, u32[]{:S(2)}) collective-permute-start(s16[3,400,128]{2,1,0:T(8,128)(2,1)S(1)} %get-tuple-element.81), channel_id=1, source_target_pairs={{0,24},{4,28},{8,16},{12,20},{16,8},{20,12},{24,0},{28,4},{1,25},{... | collective-permute-start | bytes 921608 | tf_op jit(solution)/shard_map/ppermute | solution.py:161
  76.8 15.9 %collective-permute-start.7 = (bf16[64,2304]{1,0:T(8,128)(2,1)S(1)}, bf16[64,2304]{1,0:T(8,128)(2,1)S(1)}, u32[]{:S(2)}, u32[]{:S(2)}) collective-permute-start(bf16[64,2304]{1,0:T(8,128)(2,1)S(1)} %slice.32), channel_id=1, source_target_pairs={{0,16},{4,20},{8,24},{12,28},{16,0},{20,4},{24,8},{28,12},{1,17},{... | collective-permute-start | bytes 884744 | tf_op jit(solution)/shard_map/ppermute | solution.py:161
  97.0 10.2 %collective-permute-start.12 = (s16[3,400,128]{2,1,0:T(8,128)(2,1)S(1)}, s16[3,400,128]{2,1,0:T(8,128)(2,1)S(1)}, u32[]{:S(2)}, u32[]{:S(2)}) collective-permute-start(s16[3,400,128]{2,1,0:T(8,128)(2,1)S(1)} %get-tuple-element.87), channel_id=1, source_target_pairs={{0,8},{4,12},{8,0},{12,4},{16,24},{20,28},{24,16},{28,20},{1,9},{5... | collective-permute-start | bytes 921608 | tf_op jit(solution)/shard_map/ppermute | solution.py:161
  97.7 18.6 %copy-start.5 = (s16[2,3,400,128]{3,2,1,0:T(8,128)(2,1)}, s16[2,3,400,128]{3,2,1,0:T(8,128)(2,1)S(1)}, u32[]{:S(2)}) copy-start(s16[2,3,400,128]{3,2,1,0:T(8,128)(2,1)S(1)} %collective-permute-done.18.refs_0_) | copy-start | bytes 1843204
  97.7 11.4 %collective-permute-start.13 = (s16[3,400,128]{2,1,0:T(8,128)(2,1)S(1)}, s16[3,400,128]{2,1,0:T(8,128)(2,1)S(1)}, u32[]{:S(2)}, u32[]{:S(2)}) collective-permute-start(s16[3,400,128]{2,1,0:T(8,128)(2,1)S(1)} %get-tuple-element.88), channel_id=1, source_target_pairs={{0,16},{4,20},{8,24},{12,28},{16,0},{20,4},{24,8},{28,12},{1,17},{... | collective-permute-start | bytes 921608 | tf_op jit(solution)/shard_map/ppermute | solution.py:161
  99.2 11.6 %collective-permute-start.14 = (s16[3,400,128]{2,1,0:T(8,128)(2,1)S(1)}, s16[3,400,128]{2,1,0:T(8,128)(2,1)S(1)}, u32[]{:S(2)}, u32[]{:S(2)}) collective-permute-start(s16[3,400,128]{2,1,0:T(8,128)(2,1)S(1)} %get-tuple-element.89), channel_id=1, source_target_pairs={{0,24},{4,28},{8,16},{12,20},{16,8},{20,12},{24,0},{28,4},{1,25},{... | collective-permute-start | bytes 921608 | tf_op jit(solution)/shard_map/ppermute | solution.py:161
  100.5 16.5 %copy-start.16 = (f32[96]{0:T(128)S(1)}, f32[96]{0:T(128)}, u32[]{:S(2)}) copy-start(f32[96]{0:T(128)} %param.9) | copy-start | bytes 1156
  100.5 16.6 %copy-start.17 = (s32[192,2]{0,1:T(2,128)S(1)}, s32[192,2]{0,1:T(2,128)}, u32[]{:S(2)}) copy-start(s32[192,2]{0,1:T(2,128)} %param.7) | copy-start | bytes 4612
  100.7 0.7 copy-start.13
  107.0 32.8 %collective-permute-start.22 = (s16[2,3,400,128]{3,2,1,0:T(8,128)(2,1)}, s16[2,3,400,128]{3,2,1,0:T(8,128)(2,1)}, u32[]{:S(2)}, u32[]{:S(2)}) collective-permute-start(s16[2,3,400,128]{3,2,1,0:T(8,128)(2,1)} %get-tuple-element.98), channel_id=1, source_target_pairs={{0,1},{1,0},{2,3},{3,2},{4,5},{5,4},{6,7},{7,6},{8,9},{9,8},{10,11... | collective-permute-start | bytes 1843208 | tf_op jit(solution)/shard_map/ppermute | solution.py:293
  116.3 0.7 copy-start.14
  117.0 19.3 %collective-permute-start.20 = (s16[1,3,400,128]{3,2,1,0:T(8,128)(2,1)}, s16[1,3,400,128]{3,2,1,0:T(8,128)(2,1)}, u32[]{:S(2)}, u32[]{:S(2)}) collective-permute-start(s16[1,3,400,128]{3,2,1,0:T(8,128)(2,1)} %get-tuple-element.104), channel_id=1, source_target_pairs={{0,1},{1,0},{2,3},{3,2},{4,5},{5,4},{6,7},{7,6},{8,9},{9,8},{10,11... | collective-permute-start | bytes 921608 | tf_op jit(solution)/shard_map/ppermute | solution.py:293
  117.7 41.6 %collective-permute-start.24 = (s16[1,3,400,128]{3,2,1,0:T(8,128)(2,1)}, s16[1,3,400,128]{3,2,1,0:T(8,128)(2,1)}, u32[]{:S(2)}, u32[]{:S(2)}) collective-permute-start(s16[1,3,400,128]{3,2,1,0:T(8,128)(2,1)} %copy-done.13), channel_id=1, source_target_pairs={{0,2},{1,3},{2,0},{3,1},{4,6},{5,7},{6,4},{7,5},{8,10},{9,11},{10,... | collective-permute-start | bytes 921608 | tf_op jit(solution)/shard_map/ppermute | solution.py:293
  120.5 27.8 %collective-permute-start.19 = (s16[1,3,400,128]{3,2,1,0:T(8,128)(2,1)}, s16[1,3,400,128]{3,2,1,0:T(8,128)(2,1)}, u32[]{:S(2)}, u32[]{:S(2)}) collective-permute-start(s16[1,3,400,128]{3,2,1,0:T(8,128)(2,1)} %copy-done.14), channel_id=1, source_target_pairs={{0,1},{1,0},{2,3},{3,2},{4,5},{5,4},{6,7},{7,6},{8,9},{9,8},{10,11... | collective-permute-start | bytes 921608 | tf_op jit(solution)/shard_map/ppermute | solution.py:293
  138.2 21.1 %collective-permute-start.21 = (s16[1,3,400,128]{3,2,1,0:T(8,128)(2,1)}, s16[1,3,400,128]{3,2,1,0:T(8,128)(2,1)}, u32[]{:S(2)}, u32[]{:S(2)}) collective-permute-start(s16[1,3,400,128]{3,2,1,0:T(8,128)(2,1)} %hop.4), channel_id=1, source_target_pairs={{0,2},{1,3},{2,0},{3,1},{4,6},{5,7},{6,4},{7,5},{8,10},{9,11},{10,... | collective-permute-start | bytes 921608 | tf_op jit(solution)/shard_map/ppermute | solution.py:293
  141.8 20.9 %collective-permute-start.23 = (s16[1,3,400,128]{3,2,1,0:T(8,128)(2,1)}, s16[1,3,400,128]{3,2,1,0:T(8,128)(2,1)}, u32[]{:S(2)}, u32[]{:S(2)}) collective-permute-start(s16[1,3,400,128]{3,2,1,0:T(8,128)(2,1)} %hop.5), channel_id=1, source_target_pairs={{0,2},{1,3},{2,0},{3,1},{4,6},{5,7},{6,4},{7,5},{8,10},{9,11},{10,... | collective-permute-start | bytes 921608 | tf_op jit(solution)/shard_map/ppermute | solution.py:293
  159.3 1.1 copy-start.6

commit v6 on v5

--- a/solution.py
+++ b/solution.py
@@ -256,45 +256,38 @@
 
     place = jnp.stack([chip, core, z]).astype(jnp.int32)
 
-    def gather(mine, beside=()):
-        count = mine.shape[0]
-        if chips != 4:
-            return [[(x, 0, count)] for x in [mine] + [to_chip(mine, d) for d in range(1, chips)]]
+    mine = amplitudes
+    if chips == 4:
         one, two = to_chip(mine, 1), to_chip(mine, 2)
-        if beside:
-            one, two, *_ = lax.optimization_barrier((one, two, *beside))
-        low, high = to_chip(two[: count // 2], 1), to_chip(one[count // 2 :], 2)
-        parts = [(low, 0, count // 2), (high, 0, count // 2)]
-        return [[(mine, 0, count)], [(one, 0, count)], [(two, 0, count)], parts]
-
-    def cut(pieces, start, count):
-        found, at = [], 0
-        for x, first, rows_of in pieces:
-            begin, end = max(start, at), min(start + count, at + rows_of)
-            if begin < end:
-                found.append((x, first + begin - at, end - begin))
-            at += rows_of
+        one, two, own_t, sib_t, eps_pair, eps_virt = lax.optimization_barrier(
+            (one, two, own_t, sib_t, eps_pair, eps_virt)
+        )
+        middle = num_pairs // 2
+        low, high = to_chip(two[:middle], 1), to_chip(one[middle:], 2)
+        gathered = [[mine], [one], [two], [low, high]]
+    else:
+        gathered = [[mine]] + [[to_chip(mine, d)] for d in range(1, chips)]
+
+    def rows_of(r):
+        found = []
+        for arrays in gathered:
+            at = 0
+            for x in arrays:
+                begin = max(r * WIDTH, at)
+                end = min((r + 1) * WIDTH, at + x.shape[0])
+                if begin < end:
+                    found.append((x, begin - at, end - begin))
+                at += x.shape[0]
         return found
-
-    head = gather(amplitudes[:WIDTH], (own_t,))
-    arrays = [x for pieces in head for x, _, _ in pieces]
-    rest = amplitudes[WIDTH:]
-    rest, own_t, sib_t, *arrays = lax.optimization_barrier((rest, own_t, sib_t, *arrays))
-    fresh = iter(arrays)
-    head = [[(next(fresh), start, count) for _, start, count in pieces] for pieces in head]
-    tail = gather(rest)
-
-    def rows_of(r):
-        if r == 0:
-            return [piece for pieces in head for piece in pieces]
-        return [piece for pieces in tail for piece in cut(pieces, (r - 1) * WIDTH, WIDTH)]
 
     def across(x, level):
         return lax.ppermute(x, "slab", [(i, i ^ level) for i in range(slabs)])
 
     def stages(r):
         sums = yield ladder(rows_of(r))
+        sums, _ = lax.optimization_barrier((sums, turns[-1]))
         arrived = [to_chip(sums[d], d) for d in range(1, chips)]
+        turns.append(arrived)
         parcels = slabs // 2 if r == chunks - 1 else 1
         parts, *away = yield functools.partial(antisym(parcels), place, sums[0]), arrived
         away = [across(x, 1) for x in reversed(away)][::-1]
@@ -327,11 +320,12 @@
     def when(stage):
         r, k = stage
         if k == 0:
-            return 38 + 7 * r if r else 14
-        return 18 * r + 40 + (k - 1) * (17 + 2 * r) + (12 if k == length - 1 else 0)
+            return 30 + 5 * r
+        return 15 * r + 54 + (k - 1) * 17 + (12 if k == length - 1 else 0)
 
     order = sorted(((r, k) for r in range(chunks) for k in range(length)), key=when)
 
+    turns = [[]]
     running = [stages(r) for r in range(chunks)]
     results = [None] * chunks
     update = token = None

time: 168 us -> 144 us (0.86)
  local copies, waits for them, and re-layouts: 19.6 us -> 12.1 us
  starting transfers between devices: 32.8 us -> 25.5 us
  waiting for transfers between devices: 66.3 us -> 59.9 us
  other arithmetic: 2.47 us -> 0.49 us
    ppermute x17 -> x13, waiting for transfers between devices: 41.3 us -> 23.7 us  [to_chip(): return lax.ppermute(x, 'pair', [(i, i ^ d * CORES) for i in range(devices)])]
    ppermute x7, waiting for transfers between devices: 25 us -> 36.1 us  [across(): return lax.ppermute(x, 'slab', [(i, i ^ level) for i in range(slabs)])]
    ppermute x17 -> x13, starting transfers between devices: 23.1 us -> 16.7 us  [to_chip(): return lax.ppermute(x, 'pair', [(i, i ^ d * CORES) for i in range(devices)])]
    unnamed x36 -> x26, local copies, waits for them, and re-layouts: 15.1 us -> 10.9 us
    pallas_call x1, Pallas kernels: 2.87 us -> 7.02 us  [on_device(): transpose(lax.ppermute(integrals, 'pair', [(i, i ^ 1) for i in range(devi...]
    pallas_call x3, Pallas kernels: 4.02 us -> 0.54 us  [stages(): out, = (yield (lambda *args, call=call: [call(parts, *args)], got))]
    pallas_call x3, Pallas kernels: 7.3 us -> 4.18 us  [finish(): pl.pallas_call(functools.partial(finish_kernel, places), grid=(1,), in_sp...]
  transfers between devices with their start and end apart: 25 -> 21, of which waited for: 11 -> 11; matrix products, arithmetic and copies ran while one was open for 4% -> 1% of each run, Pallas kernels for 25% -> 29%
where the time goes in v6:
time: 144 us; the launch traced here: 143 us
  waiting for transfers between devices  59.9 us (42%)
  Pallas kernels  44.9 us (31%)
  starting transfers between devices  25.5 us (18%)
  local copies, waits for them, and re-layouts  12.1 us (8%)
    ppermute x7, waiting for transfers between devices, across(): return lax.ppermute(x, 'slab', [(i, i ^ level) for i in range(slabs)])  36.1 us
    pallas_call x6, Pallas kernels, on_device(): results[r] = call(*inputs)  30.3 us
    ppermute x13, waiting for transfers between devices, to_chip(): return lax.ppermute(x, 'pair', [(i, i ^ d * CORES) for i in range(devices)])  23.7 us
    ppermute x13, starting transfers between devices, to_chip(): return lax.ppermute(x, 'pair', [(i, i ^ d * CORES) for i in range(devices)])  16.7 us
    unnamed x26, local copies, waits for them, and re-layouts  10.9 us
    ppermute x7, starting transfers between devices, across(): return lax.ppermute(x, 'slab', [(i, i ^ level) for i in range(slabs)])  8.44 us
    pallas_call x1, Pallas kernels, on_device(): transpose(lax.ppermute(integrals, 'pair', [(i, i ^ 1) for i in range(devi...  7.02 us
    pallas_call x3, Pallas kernels, finish(): pl.pallas_call(functools.partial(finish_kernel, places), grid=(1,), in_sp...  4.18 us
  transfers between devices with their start and end apart: 21, of which 11 were waited for; matrix products, arithmetic and copies ran while one was open for 1% of the time, Pallas kernels for 29%

profile of v6, /device:TPU:0, one launch (start us, length us, event | category | flops | bytes accessed | tf_op | source)
XLA Modules:
  0.0 143.1 jit_solution(16085635197174470848)
XLA Ops:
  0.0 0.5 collective-permute-start.2
  0.5 2.5 %collective-permute-start = (bf16[192,2304]{1,0:T(8,128)(2,1)}, bf16[192,2304]{1,0:T(8,128)(2,1)S(1)}, u32[]{:S(2)}, u32[]{:S(2)}) collective-permute-start(bf16[192,2304]{1,0:T(8,128)(2,1)} %refs_0_.3), channel_id=1, source_target_pairs={{0,8},{4,12},{8,0},{12,4},{16,24},{20,28},{24,16},{28,20},{1,9},{5... | collective-permute-start | bytes 2654216 | tf_op jit(solution)/shard_map/ppermute | solution.py:161
  2.9 1.5 %collective-permute-start.1 = (bf16[192,2304]{1,0:T(8,128)(2,1)}, bf16[192,2304]{1,0:T(8,128)(2,1)S(1)}, u32[]{:S(2)}, u32[]{:S(2)}) collective-permute-start(bf16[192,2304]{1,0:T(8,128)(2,1)} %refs_0_.3), channel_id=1, source_target_pairs={{0,16},{4,20},{8,24},{12,28},{16,0},{20,4},{24,8},{28,12},{1,17},{... | collective-permute-start | bytes 2654216 | tf_op jit(solution)/shard_map/ppermute | solution.py:161
  4.5 2.5 %copy-done.5 = bf16[2304,1152]{1,0:T(8,128)(2,1)S(1)} copy-done((bf16[2304,1152]{1,0:T(8,128)(2,1)S(1)}, bf16[2304,1152]{1,0:T(8,128)(2,1)}, u32[]{:S(2)}) %copy-start.5) | copy-done | bytes 5308440
  7.0 2.9 %transpose.14.own_ref = bf16[1152,2304]{1,0:T(8,128)(2,1)S(1)} custom-call(bf16[2304,1152]{1,0:T(8,128)(2,1)S(1)} %copy-done.5), custom_call_target="tpu_custom_call" | custom-call | flops 1024 | bytes 1024 | tf_op jit(solution)/shard_map/transpose/pallas_call | solution.py:245
  9.8 2.3 %copy-done = bf16[1152,2304]{1,0:T(8,128)(2,1)} copy-done((bf16[1152,2304]{1,0:T(8,128)(2,1)}, bf16[1152,2304]{1,0:T(8,128)(2,1)S(1)}, u32[]{:S(2)}) %copy-start) | copy-done | bytes 5308440
  12.7 0.2 bitcast_add_fusion
  13.0 7.0 %transpose.15.sib_ref = bf16[1152,2304]{1,0:T(8,128)(2,1)S(1)} custom-call(bf16[2304,1152]{1,0:T(8,128)(2,1)} %collective-permute-done.2.in_ref), custom_call_target="tpu_custom_call" | custom-call | flops 1024 | bytes 1024 | tf_op jit(solution)/shard_map/transpose/pallas_call | solution.py:244
  20.1 3.4 %collective-permute-done.refs_1_ = bf16[192,2304]{1,0:T(8,128)(2,1)S(1)} collective-permute-done((bf16[192,2304]{1,0:T(8,128)(2,1)}, bf16[192,2304]{1,0:T(8,128)(2,1)S(1)}, u32[]{:S(2)}, u32[]{:S(2)}) %collective-permute-start) | collective-permute-done | bytes 884768 | tf_op jit(solution)/shard_map/ppermute | solution.py:161
  23.5 1.5 %collective-permute-done.1.refs_2_ = bf16[192,2304]{1,0:T(8,128)(2,1)S(1)} collective-permute-done((bf16[192,2304]{1,0:T(8,128)(2,1)}, bf16[192,2304]{1,0:T(8,128)(2,1)S(1)}, u32[]{:S(2)}, u32[]{:S(2)}) %collective-permute-start.1) | collective-permute-done | bytes 884768 | tf_op jit(solution)/shard_map/ppermute | solution.py:161
  25.0 0.4 collective-permute-start.4
  25.4 0.8 slice.14
  26.2 1.7 %collective-permute-start.3 = (bf16[96,2304]{1,0:T(8,128)(2,1)}, bf16[96,2304]{1,0:T(8,128)(2,1)}, u32[]{:S(2)}, u32[]{:S(2)}) collective-permute-start(bf16[96,2304]{1,0:T(8,128)(2,1)} %slice.14), channel_id=1, source_target_pairs={{0,16},{4,20},{8,24},{12,28},{16,0},{20,4},{24,8},{28,12},{1,17},{... | collective-permute-start | bytes 1327112 | tf_op jit(solution)/shard_map/ppermute | solution.py:161
  27.9 8.6 %collective-permute-done.4.refs_3_ = bf16[96,2304]{1,0:T(8,128)(2,1)S(1)} collective-permute-done((bf16[96,2304]{1,0:T(8,128)(2,1)S(1)}, bf16[96,2304]{1,0:T(8,128)(2,1)S(1)}, u32[]{:S(2)}, u32[]{:S(2)}) %collective-permute-start.4) | collective-permute-done | bytes 442400 | tf_op jit(solution)/shard_map/ppermute | solution.py:161
  36.5 5.1 %ladder.5 = (s16[3,400,128]{2,1,0:T(8,128)(2,1)S(1)}, s16[3,400,128]{2,1,0:T(8,128)(2,1)}, s16[3,400,128]{2,1,0:T(8,128)(2,1)}, s16[3,400,128]{2,1,0:T(8,128)(2,1)}) custom-call(bf16[1152,2304]{1,0:T(8,128)(2,1)S(1)} %bitcast.11, bf16[1152,2304]{1,0:T(8,128)(2,1)S(1)} %transpose.15.sib_ref, bf16[192,2304]{1,0:T(8,128)(2,1)S(1)} %copy-done.4, ...), custom_call_target="tpu_custom_call" | custom-call | flops 1024 | bytes 1024 | tf_op jit(solution)/shard_map/ladder/pallas_call | solution.py:339
  41.7 0.6 collective-permute-start.5
  42.3 1.5 %collective-permute-start.6 = (s16[3,400,128]{2,1,0:T(8,128)(2,1)}, s16[3,400,128]{2,1,0:T(8,128)(2,1)}, u32[]{:S(2)}, u32[]{:S(2)}) collective-permute-start(s16[3,400,128]{2,1,0:T(8,128)(2,1)} %get-tuple-element.88), channel_id=1, source_target_pairs={{0,16},{4,20},{8,24},{12,28},{16,0},{20,4},{24,8},{28,12},{1,17},{... | collective-permute-start | bytes 921608 | tf_op jit(solution)/shard_map/ppermute | solution.py:161
  43.8 1.4 collective-permute-start.7
  45.2 2.5 %copy-done.1 = bf16[1152,2304]{1,0:T(8,128)(2,1)S(1)} copy-done((bf16[1152,2304]{1,0:T(8,128)(2,1)S(1)}, bf16[1152,2304]{1,0:T(8,128)(2,1)}, u32[]{:S(2)}) %copy-start.1) | copy-done | bytes 5308440
  47.8 2.5 %copy-done.3 = bf16[1152,2304]{1,0:T(8,128)(2,1)S(1)} copy-done((bf16[1152,2304]{1,0:T(8,128)(2,1)S(1)}, bf16[1152,2304]{1,0:T(8,128)(2,1)}, u32[]{:S(2)}) %copy-start.3) | copy-done | bytes 5308440
  50.3 1.0 copy-done.7
  51.3 5.2 %ladder.3 = (s16[3,400,128]{2,1,0:T(8,128)(2,1)S(1)}, s16[3,400,128]{2,1,0:T(8,128)(2,1)S(1)}, s16[3,400,128]{2,1,0:T(8,128)(2,1)S(1)}, s16[3,400,128]{2,1,0:T(8,128)(2,1)S(1)}) custom-call(bf16[1152,2304]{1,0:T(8,128)(2,1)S(1)} %copy-done.1, bf16[1152,2304]{1,0:T(8,128)(2,1)S(1)} %copy-done.3, bf16[192,2304]{1,0:T(8,128)(2,1)S(1)} %copy-done.4, ...), custom_call_target="tpu_custom_call" | custom-call | flops 1024 | bytes 1024 | tf_op jit(solution)/shard_map/ladder/pallas_call | solution.py:339
  56.5 5.2 %ladder.4 = (s16[3,400,128]{2,1,0:T(8,128)(2,1)S(1)}, s16[3,400,128]{2,1,0:T(8,128)(2,1)S(1)}, s16[3,400,128]{2,1,0:T(8,128)(2,1)S(1)}, s16[3,400,128]{2,1,0:T(8,128)(2,1)S(1)}) custom-call(bf16[1152,2304]{1,0:T(8,128)(2,1)S(1)} %copy-done.1, bf16[1152,2304]{1,0:T(8,128)(2,1)S(1)} %copy-done.3, bf16[192,2304]{1,0:T(8,128)(2,1)S(1)} %copy-done.4, ...), custom_call_target="tpu_custom_call" | custom-call | flops 1024 | bytes 1024 | tf_op jit(solution)/shard_map/ladder/pallas_call | solution.py:339
  61.8 1.6 %collective-permute-start.10 = (s16[3,400,128]{2,1,0:T(8,128)(2,1)S(1)}, s16[3,400,128]{2,1,0:T(8,128)(2,1)S(1)}, u32[]{:S(2)}, u32[]{:S(2)}) collective-permute-start(s16[3,400,128]{2,1,0:T(8,128)(2,1)S(1)} %get-tuple-element.92), channel_id=1, source_target_pairs={{0,24},{4,28},{8,16},{12,20},{16,8},{20,12},{24,0},{28,4},{1,25},{... | collective-permute-start | bytes 921608 | tf_op jit(solution)/shard_map/ppermute | solution.py:161
  63.4 1.4 collective-permute-start.8
  64.9 0.5 collective-permute-start.9
  65.3 5.3 %antisym.3 = (f32[2,1152,128]{2,1,0:T(8,128)S(1)}, s16[2,3,400,128]{3,2,1,0:T(8,128)(2,1)S(1)}) custom-call(s32[3]{0:T(128)S(1)} %pad_add_fusion.place_ref, s16[3,400,128]{2,1,0:T(8,128)(2,1)S(1)} %get-tuple-element.97.refs_0_, s16[3,400,128]{2,1,0:T(8,128)(2,1)} %collective-permute-done.5.refs_1_, s16[3,400,128]{2,1,0:T(8,128)(2,1)} %collective-permute-done.6.refs_2_, ...), custom_call_target="tpu_custom_call" | custom-call | flops 1024 | bytes 1024 | tf_op jit(solution)/shard_map/antisym/pallas_call | solution.py:339
  70.7 1.7 %collective-permute-start.14 = (s16[2,3,400,128]{3,2,1,0:T(8,128)(2,1)S(1)}, s16[2,3,400,128]{3,2,1,0:T(8,128)(2,1)S(1)}, u32[]{:S(2)}, u32[]{:S(2)}) collective-permute-start(s16[2,3,400,128]{3,2,1,0:T(8,128)(2,1)S(1)} %get-tuple-element.102), channel_id=1, source_target_pairs={{0,1},{1,0},{2,3},{3,2},{4,5},{5,4},{6,7},{7,6},{8,9},{9,8},{10,11... | collective-permute-start | bytes 1843208 | tf_op jit(solution)/shard_map/ppermute | solution.py:284
  72.3 0.6 collective-permute-done.10.refs_3_
  73.0 3.4 %collective-permute-done.8.refs_1_ = s16[3,400,128]{2,1,0:T(8,128)(2,1)S(1)} collective-permute-done((s16[3,400,128]{2,1,0:T(8,128)(2,1)S(1)}, s16[3,400,128]{2,1,0:T(8,128)(2,1)S(1)}, u32[]{:S(2)}, u32[]{:S(2)}) %collective-permute-start.8) | collective-permute-done | bytes 307232 | tf_op jit(solution)/shard_map/ppermute | solution.py:161
  76.4 0.8 collective-permute-start.11
  77.2 1.3 collective-permute-start.12
  78.5 1.4 collective-permute-start.13
  79.9 4.7 %antisym.4 = (f32[2,1152,128]{2,1,0:T(8,128)S(1)}, s16[2,3,400,128]{3,2,1,0:T(8,128)(2,1)S(1)}) custom-call(s32[3]{0:T(128)S(1)} %pad_add_fusion.place_ref, s16[3,400,128]{2,1,0:T(8,128)(2,1)S(1)} %get-tuple-element.103.refs_0_, s16[3,400,128]{2,1,0:T(8,128)(2,1)S(1)} %collective-permute-done.8.refs_1_, ...), custom_call_target="tpu_custom_call" | custom-call | flops 1024 | bytes 1024 | tf_op jit(solution)/shard_map/antisym/pallas_call | solution.py:339
  84.6 1.6 %collective-permute-start.18 = (s16[2,3,400,128]{3,2,1,0:T(8,128)(2,1)S(1)}, s16[2,3,400,128]{3,2,1,0:T(8,128)(2,1)S(1)}, u32[]{:S(2)}, u32[]{:S(2)}) collective-permute-start(s16[2,3,400,128]{3,2,1,0:T(8,128)(2,1)S(1)} %get-tuple-element.107), channel_id=1, source_target_pairs={{0,1},{1,0},{2,3},{3,2},{4,5},{5,4},{6,7},{7,6},{8,9},{9,8},{10,11... | collective-permute-start | bytes 1843208 | tf_op jit(solution)/shard_map/ppermute | solution.py:284
  86.6 4.5 %collective-permute-done.12.refs_2_ = s16[3,400,128]{2,1,0:T(8,128)(2,1)S(1)} collective-permute-done((s16[3,400,128]{2,1,0:T(8,128)(2,1)S(1)}, s16[3,400,128]{2,1,0:T(8,128)(2,1)S(1)}, u32[]{:S(2)}, u32[]{:S(2)}) %collective-permute-start.12) | collective-permute-done | bytes 307232 | tf_op jit(solution)/shard_map/ppermute | solution.py:161
  91.1 1.5 %collective-permute-done.13.refs_3_ = s16[3,400,128]{2,1,0:T(8,128)(2,1)S(1)} collective-permute-done((s16[3,400,128]{2,1,0:T(8,128)(2,1)S(1)}, s16[3,400,128]{2,1,0:T(8,128)(2,1)S(1)}, u32[]{:S(2)}, u32[]{:S(2)}) %collective-permute-start.13) | collective-permute-done | bytes 307232 | tf_op jit(solution)/shard_map/ppermute | solution.py:161
  92.6 4.7 %antisym.5 = (f32[2,1152,128]{2,1,0:T(8,128)S(1)}, s16[1,3,400,128]{3,2,1,0:T(8,128)(2,1)S(1)}, s16[1,3,400,128]{3,2,1,0:T(8,128)(2,1)S(1)}) custom-call(s32[3]{0:T(128)S(1)} %pad_add_fusion.place_ref, s16[3,400,128]{2,1,0:T(8,128)(2,1)S(1)} %get-tuple-element.93.refs_0_, s16[3,400,128]{2,1,0:T(8,128)(2,1)S(1)} %collective-permute-done.11.refs_1_, ...), custom_call_target="tpu_custom_call" | custom-call | flops 1024 | bytes 1024 | tf_op jit(solution)/shard_map/antisym/pallas_call | solution.py:339
  97.3 1.6 %collective-permute-start.16 = (s16[1,3,400,128]{3,2,1,0:T(8,128)(2,1)S(1)}, s16[1,3,400,128]{3,2,1,0:T(8,128)(2,1)S(1)}, u32[]{:S(2)}, u32[]{:S(2)}) collective-permute-start(s16[1,3,400,128]{3,2,1,0:T(8,128)(2,1)S(1)} %get-tuple-element.114), channel_id=1, source_target_pairs={{0,1},{1,0},{2,3},{3,2},{4,5},{5,4},{6,7},{7,6},{8,9},{9,8},{10,11... | collective-permute-start | bytes 921608 | tf_op jit(solution)/shard_map/ppermute | solution.py:284
  98.9 2.6 %collective-permute-start.20 = (s16[1,3,400,128]{3,2,1,0:T(8,128)(2,1)S(1)}, s16[1,3,400,128]{3,2,1,0:T(8,128)(2,1)S(1)}, u32[]{:S(2)}, u32[]{:S(2)}) collective-permute-start(s16[1,3,400,128]{3,2,1,0:T(8,128)(2,1)S(1)} %hop.3), channel_id=1, source_target_pairs={{0,2},{1,3},{2,0},{3,1},{4,6},{5,7},{6,4},{7,5},{8,10},{9,11},{10,... | collective-permute-start | bytes 921608 | tf_op jit(solution)/shard_map/ppermute | solution.py:284
  101.5 0.5 collective-permute-start.15
  102.1 0.4 collective-permute-start.19
  102.6 16.1 %collective-permute-done.16.refs_0_ = s16[1,3,400,128]{3,2,1,0:T(8,128)(2,1)S(1)} collective-permute-done((s16[1,3,400,128]{3,2,1,0:T(8,128)(2,1)S(1)}, s16[1,3,400,128]{3,2,1,0:T(8,128)(2,1)S(1)}, u32[]{:S(2)}, u32[]{:S(2)}) %collective-permute-start.16) | collective-permute-done | bytes 307232 | tf_op jit(solution)/shard_map/ppermute | solution.py:284
  118.9 1.4 finish.3.refs_2_
  120.3 16.1 %collective-permute-done.19.refs_1_ = s16[1,3,400,128]{3,2,1,0:T(8,128)(2,1)S(1)} collective-permute-done((s16[1,3,400,128]{3,2,1,0:T(8,128)(2,1)S(1)}, s16[1,3,400,128]{3,2,1,0:T(8,128)(2,1)S(1)}, u32[]{:S(2)}, u32[]{:S(2)}) %collective-permute-start.19) | collective-permute-done | bytes 307232 | tf_op jit(solution)/shard_map/ppermute | solution.py:284
  136.4 4.0 %collective-permute-done.17.refs_1_ = s16[1,3,400,128]{3,2,1,0:T(8,128)(2,1)S(1)} collective-permute-done((s16[1,3,400,128]{3,2,1,0:T(8,128)(2,1)S(1)}, s16[1,3,400,128]{3,2,1,0:T(8,128)(2,1)S(1)}, u32[]{:S(2)}, u32[]{:S(2)}) %collective-permute-start.17) | collective-permute-done | bytes 307232 | tf_op jit(solution)/shard_map/ppermute | solution.py:284
  140.3 1.4 finish.4.refs_2_
  141.7 1.4 finish.5
  (49 shorter events, 1.5 us)
Async XLA Ops:
  0.0 13.0 %collective-permute-start.2 = (bf16[2304,1152]{1,0:T(8,128)(2,1)}, bf16[2304,1152]{1,0:T(8,128)(2,1)}, u32[]{:S(2)}, u32[]{:S(2)}) collective-permute-start(bf16[2304,1152]{1,0:T(8,128)(2,1)} %in_ref.1), channel_id=1, source_target_pairs={{0,4},{4,0},{8,12},{12,8},{16,20},{20,16},{24,28},{28,24},{1,5},{5... | collective-permute-start | bytes 15925256 | tf_op jit(solution)/shard_map/ppermute | solution.py:244
  0.5 23.0 %collective-permute-start = (bf16[192,2304]{1,0:T(8,128)(2,1)}, bf16[192,2304]{1,0:T(8,128)(2,1)S(1)}, u32[]{:S(2)}, u32[]{:S(2)}) collective-permute-start(bf16[192,2304]{1,0:T(8,128)(2,1)} %refs_0_.3), channel_id=1, source_target_pairs={{0,8},{4,12},{8,0},{12,4},{16,24},{20,28},{24,16},{28,20},{1,9},{5... | collective-permute-start | bytes 2654216 | tf_op jit(solution)/shard_map/ppermute | solution.py:161
  2.9 22.0 %collective-permute-start.1 = (bf16[192,2304]{1,0:T(8,128)(2,1)}, bf16[192,2304]{1,0:T(8,128)(2,1)S(1)}, u32[]{:S(2)}, u32[]{:S(2)}) collective-permute-start(bf16[192,2304]{1,0:T(8,128)(2,1)} %refs_0_.3), channel_id=1, source_target_pairs={{0,16},{4,20},{8,24},{12,28},{16,0},{20,4},{24,8},{28,12},{1,17},{... | collective-permute-start | bytes 2654216 | tf_op jit(solution)/shard_map/ppermute | solution.py:161
  4.5 2.5 %copy-start.5 = (bf16[2304,1152]{1,0:T(8,128)(2,1)S(1)}, bf16[2304,1152]{1,0:T(8,128)(2,1)}, u32[]{:S(2)}) copy-start(bf16[2304,1152]{1,0:T(8,128)(2,1)} %in_ref.1) | copy-start | bytes 15925252
  7.0 5.2 %copy-start.8 = (f32[96]{0:T(128)S(1)}, f32[96]{0:T(128)}, u32[]{:S(2)}) copy-start(f32[96]{0:T(128)} %param.9) | copy-start | bytes 1156
  7.0 5.5 %copy-start.9 = (s32[192,2]{0,1:T(2,128)S(1)}, s32[192,2]{0,1:T(2,128)}, u32[]{:S(2)}) copy-start(s32[192,2]{0,1:T(2,128)} %param.7) | copy-start | bytes 4612
  7.0 5.5 %copy-start.10 = (f32[160]{0:T(256)S(1)}, f32[160]{0:T(256)}, u32[]{:S(2)}) copy-start(f32[160]{0:T(256)} %param.8) | copy-start | bytes 1924
  9.8 2.3 %copy-start = (bf16[1152,2304]{1,0:T(8,128)(2,1)}, bf16[1152,2304]{1,0:T(8,128)(2,1)S(1)}, u32[]{:S(2)}) copy-start(bf16[1152,2304]{1,0:T(8,128)(2,1)S(1)} %transpose.14.own_ref) | copy-start | bytes 15925252
  12.9 23.6 %slice-start = ((s8[5308416]{0:T(1024)(128)(4,1)}), s8[4194304]{0:T(1024)(128)(4,1)S(1)}, s32[]{:S(2)}) async-start(s8[5308416]{0:T(1024)(128)(4,1)} %bitcast.10), calls=%async_computation | async-start | bytes 8388608
  13.0 23.5 %slice-start.1 = ((s8[5308416]{0:T(1024)(128)(4,1)}), s8[1114112]{0:T(1024)(128)(4,1)S(1)}, s32[]{:S(2)}) async-start(s8[5308416]{0:T(1024)(128)(4,1)} %bitcast.10), calls=%async_computation.1 | async-start | bytes 2228224
  20.0 21.6 %copy-start.2 = (bf16[1152,2304]{1,0:T(8,128)(2,1)}, bf16[1152,2304]{1,0:T(8,128)(2,1)S(1)}, u32[]{:S(2)}) copy-start(bf16[1152,2304]{1,0:T(8,128)(2,1)S(1)} %transpose.15.sib_ref) | copy-start | bytes 15925252
  20.0 16.5 %copy-start.4 = (bf16[192,2304]{1,0:T(8,128)(2,1)S(1)}, bf16[192,2304]{1,0:T(8,128)(2,1)}, u32[]{:S(2)}) copy-start(bf16[192,2304]{1,0:T(8,128)(2,1)} %refs_0_.3) | copy-start | bytes 2654212
  25.0 11.5 %collective-permute-start.4 = (bf16[96,2304]{1,0:T(8,128)(2,1)S(1)}, bf16[96,2304]{1,0:T(8,128)(2,1)S(1)}, u32[]{:S(2)}, u32[]{:S(2)}) collective-permute-start(bf16[96,2304]{1,0:T(8,128)(2,1)S(1)} %slice.15), channel_id=1, source_target_pairs={{0,8},{4,12},{8,0},{12,4},{16,24},{20,28},{24,16},{28,20},{1,9},{5... | collective-permute-start | bytes 1327112 | tf_op jit(solution)/shard_map/ppermute | solution.py:161
  26.2 19.1 %collective-permute-start.3 = (bf16[96,2304]{1,0:T(8,128)(2,1)}, bf16[96,2304]{1,0:T(8,128)(2,1)}, u32[]{:S(2)}, u32[]{:S(2)}) collective-permute-start(bf16[96,2304]{1,0:T(8,128)(2,1)} %slice.14), channel_id=1, source_target_pairs={{0,16},{4,20},{8,24},{12,28},{16,0},{20,4},{24,8},{28,12},{1,17},{... | collective-permute-start | bytes 1327112 | tf_op jit(solution)/shard_map/ppermute | solution.py:161
  36.5 5.1 %copy-start.6 = (bf16[96,2304]{1,0:T(8,128)(2,1)}, bf16[96,2304]{1,0:T(8,128)(2,1)S(1)}, u32[]{:S(2)}) copy-start(bf16[96,2304]{1,0:T(8,128)(2,1)S(1)} %collective-permute-done.4.refs_3_) | copy-start | bytes 1327108
  41.7 20.1 %collective-permute-start.5 = (s16[3,400,128]{2,1,0:T(8,128)(2,1)}, s16[3,400,128]{2,1,0:T(8,128)(2,1)}, u32[]{:S(2)}, u32[]{:S(2)}) collective-permute-start(s16[3,400,128]{2,1,0:T(8,128)(2,1)} %get-tuple-element.87), channel_id=1, source_target_pairs={{0,8},{4,12},{8,0},{12,4},{16,24},{20,28},{24,16},{28,20},{1,9},{5... | collective-permute-start | bytes 921608 | tf_op jit(solution)/shard_map/ppermute | solution.py:161
  42.3 19.5 %collective-permute-start.6 = (s16[3,400,128]{2,1,0:T(8,128)(2,1)}, s16[3,400,128]{2,1,0:T(8,128)(2,1)}, u32[]{:S(2)}, u32[]{:S(2)}) collective-permute-start(s16[3,400,128]{2,1,0:T(8,128)(2,1)} %get-tuple-element.88), channel_id=1, source_target_pairs={{0,16},{4,20},{8,24},{12,28},{16,0},{20,4},{24,8},{28,12},{1,17},{... | collective-permute-start | bytes 921608 | tf_op jit(solution)/shard_map/ppermute | solution.py:161
  43.8 18.0 %collective-permute-start.7 = (s16[3,400,128]{2,1,0:T(8,128)(2,1)}, s16[3,400,128]{2,1,0:T(8,128)(2,1)}, u32[]{:S(2)}, u32[]{:S(2)}) collective-permute-start(s16[3,400,128]{2,1,0:T(8,128)(2,1)} %get-tuple-element.89), channel_id=1, source_target_pairs={{0,24},{4,28},{8,16},{12,20},{16,8},{20,12},{24,0},{28,4},{1,25},{... | collective-permute-start | bytes 921608 | tf_op jit(solution)/shard_map/ppermute | solution.py:161
  45.2 2.5 %copy-start.1 = (bf16[1152,2304]{1,0:T(8,128)(2,1)S(1)}, bf16[1152,2304]{1,0:T(8,128)(2,1)}, u32[]{:S(2)}) copy-start(bf16[1152,2304]{1,0:T(8,128)(2,1)} %copy-done) | copy-start | bytes 15925252
  47.7 2.5 %copy-start.3 = (bf16[1152,2304]{1,0:T(8,128)(2,1)S(1)}, bf16[1152,2304]{1,0:T(8,128)(2,1)}, u32[]{:S(2)}) copy-start(bf16[1152,2304]{1,0:T(8,128)(2,1)} %copy-done.2) | copy-start | bytes 15925252
  50.3 1.0 copy-start.7
  61.8 11.2 %collective-permute-start.10 = (s16[3,400,128]{2,1,0:T(8,128)(2,1)S(1)}, s16[3,400,128]{2,1,0:T(8,128)(2,1)S(1)}, u32[]{:S(2)}, u32[]{:S(2)}) collective-permute-start(s16[3,400,128]{2,1,0:T(8,128)(2,1)S(1)} %get-tuple-element.92), channel_id=1, source_target_pairs={{0,24},{4,28},{8,16},{12,20},{16,8},{20,12},{24,0},{28,4},{1,25},{... | collective-permute-start | bytes 921608 | tf_op jit(solution)/shard_map/ppermute | solution.py:161
  63.4 13.0 %collective-permute-start.8 = (s16[3,400,128]{2,1,0:T(8,128)(2,1)S(1)}, s16[3,400,128]{2,1,0:T(8,128)(2,1)S(1)}, u32[]{:S(2)}, u32[]{:S(2)}) collective-permute-start(s16[3,400,128]{2,1,0:T(8,128)(2,1)S(1)} %get-tuple-element.90), channel_id=1, source_target_pairs={{0,8},{4,12},{8,0},{12,4},{16,24},{20,28},{24,16},{28,20},{1,9},{5... | collective-permute-start | bytes 921608 | tf_op jit(solution)/shard_map/ppermute | solution.py:161
  64.9 11.5 %collective-permute-start.9 = (s16[3,400,128]{2,1,0:T(8,128)(2,1)S(1)}, s16[3,400,128]{2,1,0:T(8,128)(2,1)S(1)}, u32[]{:S(2)}, u32[]{:S(2)}) collective-permute-start(s16[3,400,128]{2,1,0:T(8,128)(2,1)S(1)} %get-tuple-element.91), channel_id=1, source_target_pairs={{0,16},{4,20},{8,24},{12,28},{16,0},{20,4},{24,8},{28,12},{1,17},{... | collective-permute-start | bytes 921608 | tf_op jit(solution)/shard_map/ppermute | solution.py:161
  70.7 15.6 %collective-permute-start.14 = (s16[2,3,400,128]{3,2,1,0:T(8,128)(2,1)S(1)}, s16[2,3,400,128]{3,2,1,0:T(8,128)(2,1)S(1)}, u32[]{:S(2)}, u32[]{:S(2)}) collective-permute-start(s16[2,3,400,128]{3,2,1,0:T(8,128)(2,1)S(1)} %get-tuple-element.102), channel_id=1, source_target_pairs={{0,1},{1,0},{2,3},{3,2},{4,5},{5,4},{6,7},{7,6},{8,9},{9,8},{10,11... | collective-permute-start | bytes 1843208 | tf_op jit(solution)/shard_map/ppermute | solution.py:284
  76.4 10.2 %collective-permute-start.11 = (s16[3,400,128]{2,1,0:T(8,128)(2,1)S(1)}, s16[3,400,128]{2,1,0:T(8,128)(2,1)S(1)}, u32[]{:S(2)}, u32[]{:S(2)}) collective-permute-start(s16[3,400,128]{2,1,0:T(8,128)(2,1)S(1)} %get-tuple-element.94), channel_id=1, source_target_pairs={{0,8},{4,12},{8,0},{12,4},{16,24},{20,28},{24,16},{28,20},{1,9},{5... | collective-permute-start | bytes 921608 | tf_op jit(solution)/shard_map/ppermute | solution.py:161
  77.2 13.9 %collective-permute-start.12 = (s16[3,400,128]{2,1,0:T(8,128)(2,1)S(1)}, s16[3,400,128]{2,1,0:T(8,128)(2,1)S(1)}, u32[]{:S(2)}, u32[]{:S(2)}) collective-permute-start(s16[3,400,128]{2,1,0:T(8,128)(2,1)S(1)} %get-tuple-element.95), channel_id=1, source_target_pairs={{0,16},{4,20},{8,24},{12,28},{16,0},{20,4},{24,8},{28,12},{1,17},{... | collective-permute-start | bytes 921608 | tf_op jit(solution)/shard_map/ppermute | solution.py:161
  78.5 14.1 %collective-permute-start.13 = (s16[3,400,128]{2,1,0:T(8,128)(2,1)S(1)}, s16[3,400,128]{2,1,0:T(8,128)(2,1)S(1)}, u32[]{:S(2)}, u32[]{:S(2)}) collective-permute-start(s16[3,400,128]{2,1,0:T(8,128)(2,1)S(1)} %get-tuple-element.96), channel_id=1, source_target_pairs={{0,24},{4,28},{8,16},{12,20},{16,8},{20,12},{24,0},{28,4},{1,25},{... | collective-permute-start | bytes 921608 | tf_op jit(solution)/shard_map/ppermute | solution.py:161
  84.6 17.4 %collective-permute-start.18 = (s16[2,3,400,128]{3,2,1,0:T(8,128)(2,1)S(1)}, s16[2,3,400,128]{3,2,1,0:T(8,128)(2,1)S(1)}, u32[]{:S(2)}, u32[]{:S(2)}) collective-permute-start(s16[2,3,400,128]{3,2,1,0:T(8,128)(2,1)S(1)} %get-tuple-element.107), channel_id=1, source_target_pairs={{0,1},{1,0},{2,3},{3,2},{4,5},{5,4},{6,7},{7,6},{8,9},{9,8},{10,11... | collective-permute-start | bytes 1843208 | tf_op jit(solution)/shard_map/ppermute | solution.py:284
  97.3 21.3 %collective-permute-start.16 = (s16[1,3,400,128]{3,2,1,0:T(8,128)(2,1)S(1)}, s16[1,3,400,128]{3,2,1,0:T(8,128)(2,1)S(1)}, u32[]{:S(2)}, u32[]{:S(2)}) collective-permute-start(s16[1,3,400,128]{3,2,1,0:T(8,128)(2,1)S(1)} %get-tuple-element.114), channel_id=1, source_target_pairs={{0,1},{1,0},{2,3},{3,2},{4,5},{5,4},{6,7},{7,6},{8,9},{9,8},{10,11... | collective-permute-start | bytes 921608 | tf_op jit(solution)/shard_map/ppermute | solution.py:284
  98.9 20.0 %collective-permute-start.20 = (s16[1,3,400,128]{3,2,1,0:T(8,128)(2,1)S(1)}, s16[1,3,400,128]{3,2,1,0:T(8,128)(2,1)S(1)}, u32[]{:S(2)}, u32[]{:S(2)}) collective-permute-start(s16[1,3,400,128]{3,2,1,0:T(8,128)(2,1)S(1)} %hop.3), channel_id=1, source_target_pairs={{0,2},{1,3},{2,0},{3,1},{4,6},{5,7},{6,4},{7,5},{8,10},{9,11},{10,... | collective-permute-start | bytes 921608 | tf_op jit(solution)/shard_map/ppermute | solution.py:284
  101.5 34.9 %collective-permute-start.15 = (s16[1,3,400,128]{3,2,1,0:T(8,128)(2,1)S(1)}, s16[1,3,400,128]{3,2,1,0:T(8,128)(2,1)S(1)}, u32[]{:S(2)}, u32[]{:S(2)}) collective-permute-start(s16[1,3,400,128]{3,2,1,0:T(8,128)(2,1)S(1)} %get-tuple-element.113), channel_id=1, source_target_pairs={{0,1},{1,0},{2,3},{3,2},{4,5},{5,4},{6,7},{7,6},{8,9},{9,8},{10,11... | collective-permute-start | bytes 921608 | tf_op jit(solution)/shard_map/ppermute | solution.py:284
  102.1 34.2 %collective-permute-start.19 = (s16[1,3,400,128]{3,2,1,0:T(8,128)(2,1)S(1)}, s16[1,3,400,128]{3,2,1,0:T(8,128)(2,1)S(1)}, u32[]{:S(2)}, u32[]{:S(2)}) collective-permute-start(s16[1,3,400,128]{3,2,1,0:T(8,128)(2,1)S(1)} %hop.5), channel_id=1, source_target_pairs={{0,2},{1,3},{2,0},{3,1},{4,6},{5,7},{6,4},{7,5},{8,10},{9,11},{10,... | collective-permute-start | bytes 921608 | tf_op jit(solution)/shard_map/ppermute | solution.py:284
  118.8 21.5 %collective-permute-start.17 = (s16[1,3,400,128]{3,2,1,0:T(8,128)(2,1)S(1)}, s16[1,3,400,128]{3,2,1,0:T(8,128)(2,1)S(1)}, u32[]{:S(2)}, u32[]{:S(2)}) collective-permute-start(s16[1,3,400,128]{3,2,1,0:T(8,128)(2,1)S(1)} %hop.4), channel_id=1, source_target_pairs={{0,2},{1,3},{2,0},{3,1},{4,6},{5,7},{6,4},{7,5},{8,10},{9,11},{10,... | collective-permute-start | bytes 921608 | tf_op jit(solution)/shard_map/ppermute | solution.py:284

commit v7 on v6

--- a/solution.py
+++ b/solution.py
@@ -126,8 +126,8 @@
             encode(total, out.at[i, t])
 
 
-def finish_kernel(places, pair_ref, vir_ref, parts, *refs):
-    got, out_ref = refs[:-1], refs[-1]
+def finish_kernel(places, count, pair_ref, vir_ref, parts, *refs):
+    got, out_ref = refs[:count], refs[-1]
     tiles, tile = got[0].shape[1], got[0].shape[2] - TAIL
     low = is_low((tile, LANES))
     pair = pair_ref[0]
@@ -172,7 +172,7 @@
     def parcel(count):
         return (count, part_tiles, part_tile + TAIL, LANES)
 
-    column = 128 if rows % 128 == 0 else rows
+    column = max((c for c in (384, 256, 128) if rows % c == 0), default=rows)
     transpose = pl.pallas_call(
         transpose_kernel,
         grid=(rows // column,),
@@ -184,65 +184,90 @@
         name="transpose",
     )
 
+    def ordered(body, inputs, in_specs, out_specs, out_shape, mib, scratch=(), name=None, **more):
+        given, made = len(in_specs), len(out_specs)
+
+        def kernel(*refs):
+            token_in, token_out = refs[given], refs[given + 1 + made]
+            token_out[...] = token_in[...]
+            outs = refs[given + 1 : given + 1 + made]
+            body(*refs[:given], *outs, *refs[given + made + 2 :])
+
+        def call(token, *args):
+            return pl.pallas_call(
+                kernel,
+                in_specs=[*in_specs, vmem],
+                out_specs=[*out_specs, vmem],
+                out_shape=[*out_shape, jax.ShapeDtypeStruct(token.shape, token.dtype)],
+                scratch_shapes=scratch,
+                compiler_params=limit(mib),
+                cost_estimate=cost,
+                name=name,
+                **more,
+            )(*args, token)
+
+        return call, inputs
+
     def ladder(gathered):
         arrays, pieces = zip(*[(x, (start, count)) for x, start, count in gathered])
-        call = pl.pallas_call(
+        return ordered(
             functools.partial(ladder_kernel, chips, tile, pieces),
-            in_specs=[vmem] * (2 + len(arrays)),
-            out_specs=[vmem] * chips,
-            out_shape=[message] * chips,
-            scratch_shapes=[pltpu.VMEM((chips * WIDTH, depth), jnp.bfloat16)],
-            compiler_params=limit(16),
-            cost_estimate=cost,
+            [own_t, sib_t, *arrays],
+            [vmem] * (2 + len(arrays)),
+            [vmem] * chips,
+            [message] * chips,
+            16,
+            [pltpu.VMEM((chips * WIDTH, depth), jnp.bfloat16)],
             name="ladder",
         )
-        return functools.partial(call, own_t, sib_t), arrays
-
-    def antisym(parcels):
-        return pl.pallas_call(
+
+    def antisym(parcels, arrived):
+        return ordered(
             functools.partial(antisym_kernel, chips, slabs, vir),
-            in_specs=[smem] + [vmem] * chips,
-            out_specs=[vmem] * (1 + parcels),
-            out_shape=[jax.ShapeDtypeStruct((slabs // 2, part_rows, LANES), jnp.float32)]
+            [place, *arrived],
+            [smem] + [vmem] * chips,
+            [vmem] * (1 + parcels),
+            [jax.ShapeDtypeStruct((slabs // 2, part_rows, LANES), jnp.float32)]
             + [jax.ShapeDtypeStruct(parcel(slabs // 2 // parcels), jnp.int16)] * parcels,
-            scratch_shapes=[
+            16,
+            [
                 pltpu.VMEM((vir * vir, LANES), jnp.float32),
                 pltpu.VMEM((part_rows, LANES), jnp.float32),
             ],
-            compiler_params=limit(16),
-            cost_estimate=cost,
             name="antisym",
         )
 
-    def hop(slots, got_count):
-        return pl.pallas_call(
+    def hop(slots, parts, got):
+        return ordered(
             functools.partial(hop_kernel, slots),
-            in_specs=[vmem] * (1 + got_count),
-            out_specs=vmem,
-            out_shape=jax.ShapeDtypeStruct(parcel(len(slots)), jnp.int16),
-            compiler_params=limit(8),
-            cost_estimate=cost,
+            [parts, *got],
+            [vmem] * (1 + len(got)),
+            [vmem],
+            [jax.ShapeDtypeStruct(parcel(len(slots)), jnp.int16)],
+            8,
             name="hop",
         )
 
     def finish(r, parts, got, places, so_far):
         given = [] if so_far is None else [so_far]
-        return pl.pallas_call(
-            functools.partial(finish_kernel, places),
-            grid=(1,),
-            in_specs=[pl.BlockSpec((1, 1, LANES), lambda i: (r, 0, 0))]
+        return ordered(
+            functools.partial(finish_kernel, places, len(got)),
+            [eps_pair, eps_virt, parts, *got, *given],
+            [pl.BlockSpec((1, 1, LANES), lambda i: (r, 0, 0))]
             + [vmem] * (2 + len(got))
             + [pl.BlockSpec(memory_space=pl.ANY)] * len(given),
-            out_specs=pl.BlockSpec((WIDTH, 2 * part_rows), lambda i: (r, 0)),
-            out_shape=jax.ShapeDtypeStruct((num_pairs, 2 * part_rows), jnp.float32),
+            [pl.BlockSpec((WIDTH, 2 * part_rows), lambda i: (r, 0))],
+            [jax.ShapeDtypeStruct((num_pairs, 2 * part_rows), jnp.float32)],
+            8,
+            name="finish",
+            grid=(1,),
             input_output_aliases={3 + len(got): 0} if given else {},
-            compiler_params=limit(8),
-            cost_estimate=cost,
-            name="finish",
-        )(eps_pair, eps_virt, parts, *got, *given)
-
-    sib_t = transpose(lax.ppermute(integrals, "pair", [(i, i ^ 1) for i in range(devices)]))
-    own_t = transpose(integrals)
+        )
+
+    in_hbm = functools.partial(pltpu.with_memory_space_constraint, memory_space=pltpu.HBM)
+    own_t = transpose(in_hbm(integrals))
+    swapped = lax.ppermute(integrals, "pair", [(i, i ^ 1) for i in range(devices)])
+    sib_t = transpose(swapped)
 
     occ_ids = jnp.arange(eps_occ.shape[0], dtype=jnp.int32)
 
@@ -285,11 +310,12 @@
 
     def stages(r):
         sums = yield ladder(rows_of(r))
-        sums, _ = lax.optimization_barrier((sums, turns[-1]))
+        if r:
+            sums, _ = lax.optimization_barrier((sums, turns[-1] + results[-1][:1]))
         arrived = [to_chip(sums[d], d) for d in range(1, chips)]
         turns.append(arrived)
         parcels = slabs // 2 if r == chunks - 1 else 1
-        parts, *away = yield functools.partial(antisym(parcels), place, sums[0]), arrived
+        parts, *away = yield antisym(parcels, [sums[0], *arrived])
         away = [across(x, 1) for x in reversed(away)][::-1]
         each = slabs // 2 // parcels
         held = {e: [(away[e // 2 // each], e // 2 % each)] for e in range(0, slabs, 2)}
@@ -305,15 +331,14 @@
         while level < slabs:
             leave = [e for e in held if e & level]
             got, slots = listed(leave)
-            call = hop(slots, len(got))
-            (out,) = yield (lambda *args, call=call: [call(parts, *args)]), got
+            (out,) = yield hop(slots, parts, got)
             out = across(out, level)
             for i, e in enumerate(leave):
                 held[e ^ level].append((out, i))
                 del held[e]
             level *= 2
         got, ((_, places),) = listed([0])
-        yield (lambda *args: finish(r, parts, args, places, update)), got
+        yield finish(r, parts, got, places, update)
 
     length = 3 + max(0, (slabs - 1).bit_length() - 1)
 
@@ -321,23 +346,19 @@
         r, k = stage
         if k == 0:
             return 30 + 5 * r
-        return 15 * r + 54 + (k - 1) * 17 + (12 if k == length - 1 else 0)
+        return 15 * r + 54 + (k - 1) * 17 - (1 if k == length - 1 else 0)
 
     order = sorted(((r, k) for r in range(chunks) for k in range(length)), key=when)
 
     turns = [[]]
     running = [stages(r) for r in range(chunks)]
     results = [None] * chunks
-    update = token = None
+    update, token = None, jnp.zeros((8, LANES), jnp.float32)
     for r, k in order:
         call, inputs = running[r].send(results[r])
-        if token is not None:
-            *inputs, token = lax.optimization_barrier((*inputs, token))
+        *results[r], token = call(token, *inputs)
         if k == length - 1:
-            update = call(*inputs)
-        else:
-            results[r] = call(*inputs)
-            token = results[r][-1]
+            (update,) = results[r]
     return update
 
 

time: 144 us -> 140 us (0.972)
  waiting for transfers between devices: 59.9 us -> 56.6 us
  starting transfers between devices: 25.5 us -> 28 us
    ppermute x7, waiting for transfers between devices: 36.1 us -> 26 us  [across(): return lax.ppermute(x, 'slab', [(i, i ^ level) for i in range(slabs)])]
    ppermute x13, waiting for transfers between devices: 23.7 us -> 30.5 us  [to_chip(): return lax.ppermute(x, 'pair', [(i, i ^ d * CORES) for i in range(devices)])]
    ppermute x7, starting transfers between devices: 8.44 us -> 10.7 us  [across(): return lax.ppermute(x, 'slab', [(i, i ^ level) for i in range(slabs)])]
    unnamed x26 -> x28, local copies, waits for them, and re-layouts: 10.9 us -> 9.69 us
  transfers between devices with their start and end apart: 21 -> 21, of which waited for: 11 -> 11; matrix products, arithmetic and copies ran while one was open for 1% -> 1% of each run, Pallas kernels for 29% -> 30%
where the time goes in v7:
time: 140 us
  waiting for transfers between devices  56.6 us (40%)
  Pallas kernels  43.7 us (31%)
  starting transfers between devices  28 us (20%)
  local copies, waits for them, and re-layouts  10.9 us (8%)
    pallas_call x12, Pallas kernels, call(): pl.pallas_call(kernel, in_specs=[*in_specs, vmem], out_specs=[*out_specs,...  35.1 us
    ppermute x13, waiting for transfers between devices, to_chip(): return lax.ppermute(x, 'pair', [(i, i ^ d * CORES) for i in range(devices)])  30.5 us
    ppermute x7, waiting for transfers between devices, across(): return lax.ppermute(x, 'slab', [(i, i ^ level) for i in range(slabs)])  26 us
    ppermute x13, starting transfers between devices, to_chip(): return lax.ppermute(x, 'pair', [(i, i ^ d * CORES) for i in range(devices)])  16.7 us
    ppermute x7, starting transfers between devices, across(): return lax.ppermute(x, 'slab', [(i, i ^ level) for i in range(slabs)])  10.7 us
    unnamed x28, local copies, waits for them, and re-layouts  9.69 us
    pallas_call x1, Pallas kernels, on_device(): sib_t = transpose(swapped)  4.61 us
    pallas_call x1, Pallas kernels, on_device(): own_t = transpose(in_hbm(integrals))  4 us
  transfers between devices with their start and end apart: 21, of which 11 were waited for; matrix products, arithmetic and copies ran while one was open for 1% of the time, Pallas kernels for 30%

profile of v7, /device:TPU:0, one launch (start us, length us, event | category | flops | bytes accessed | tf_op | source)
XLA Modules:
  0.0 139.8 jit_solution(10235631514241953111)
XLA Ops:
  0.0 0.5 collective-permute-start.2
  0.5 2.6 %collective-permute-start = (bf16[192,2304]{1,0:T(8,128)(2,1)}, bf16[192,2304]{1,0:T(8,128)(2,1)S(1)}, u32[]{:S(2)}, u32[]{:S(2)}) collective-permute-start(bf16[192,2304]{1,0:T(8,128)(2,1)} %refs_2_.5), channel_id=1, source_target_pairs={{0,8},{4,12},{8,0},{12,4},{16,24},{20,28},{24,16},{28,20},{1,9},{5... | collective-permute-start | bytes 2654216 | tf_op jit(solution)/shard_map/ppermute | solution.py:161
  3.1 1.5 %collective-permute-start.1 = (bf16[192,2304]{1,0:T(8,128)(2,1)}, bf16[192,2304]{1,0:T(8,128)(2,1)S(1)}, u32[]{:S(2)}, u32[]{:S(2)}) collective-permute-start(bf16[192,2304]{1,0:T(8,128)(2,1)} %refs_2_.5), channel_id=1, source_target_pairs={{0,16},{4,20},{8,24},{12,28},{16,0},{20,4},{24,8},{28,12},{1,17},{... | collective-permute-start | bytes 2654216 | tf_op jit(solution)/shard_map/ppermute | solution.py:161
  4.6 4.0 %transpose.14.refs_0_ = bf16[1152,2304]{1,0:T(8,128)(2,1)S(1)} custom-call(bf16[2304,1152]{1,0:T(8,128)(2,1)} %in_ref.1), custom_call_target="tpu_custom_call" | custom-call | flops 1024 | bytes 1024 | tf_op jit(solution)/shard_map/transpose/pallas_call | solution.py:268
  8.6 2.4 %copy-done = bf16[1152,2304]{1,0:T(8,128)(2,1)} copy-done((bf16[1152,2304]{1,0:T(8,128)(2,1)}, bf16[1152,2304]{1,0:T(8,128)(2,1)S(1)}, u32[]{:S(2)}) %copy-start) | copy-done | bytes 5308440
  11.8 4.6 %transpose.15.refs_1_ = bf16[1152,2304]{1,0:T(8,128)(2,1)S(1)} custom-call(bf16[2304,1152]{1,0:T(8,128)(2,1)} %collective-permute-done.2.in_ref), custom_call_target="tpu_custom_call" | custom-call | flops 1024 | bytes 1024 | tf_op jit(solution)/shard_map/transpose/pallas_call | solution.py:270
  16.4 7.1 %collective-permute-done.refs_3_ = bf16[192,2304]{1,0:T(8,128)(2,1)S(1)} collective-permute-done((bf16[192,2304]{1,0:T(8,128)(2,1)}, bf16[192,2304]{1,0:T(8,128)(2,1)S(1)}, u32[]{:S(2)}, u32[]{:S(2)}) %collective-permute-start) | collective-permute-done | bytes 884768 | tf_op jit(solution)/shard_map/ppermute | solution.py:161
  23.5 1.5 %collective-permute-done.1.refs_4_ = bf16[192,2304]{1,0:T(8,128)(2,1)S(1)} collective-permute-done((bf16[192,2304]{1,0:T(8,128)(2,1)}, bf16[192,2304]{1,0:T(8,128)(2,1)S(1)}, u32[]{:S(2)}, u32[]{:S(2)}) %collective-permute-start.1) | collective-permute-done | bytes 884768 | tf_op jit(solution)/shard_map/ppermute | solution.py:161
  25.5 0.8 slice.14
  26.3 1.7 %collective-permute-start.3 = (bf16[96,2304]{1,0:T(8,128)(2,1)}, bf16[96,2304]{1,0:T(8,128)(2,1)}, u32[]{:S(2)}, u32[]{:S(2)}) collective-permute-start(bf16[96,2304]{1,0:T(8,128)(2,1)} %slice.14), channel_id=1, source_target_pairs={{0,16},{4,20},{8,24},{12,28},{16,0},{20,4},{24,8},{28,12},{1,17},{... | collective-permute-start | bytes 1327112 | tf_op jit(solution)/shard_map/ppermute | solution.py:161
  28.0 8.6 %collective-permute-done.4.refs_5_ = bf16[96,2304]{1,0:T(8,128)(2,1)S(1)} collective-permute-done((bf16[96,2304]{1,0:T(8,128)(2,1)S(1)}, bf16[96,2304]{1,0:T(8,128)(2,1)S(1)}, u32[]{:S(2)}, u32[]{:S(2)}) %collective-permute-start.4) | collective-permute-done | bytes 442400 | tf_op jit(solution)/shard_map/ppermute | solution.py:161
  36.6 5.2 %ladder.3 = (s16[3,400,128]{2,1,0:T(8,128)(2,1)S(1)}, s16[3,400,128]{2,1,0:T(8,128)(2,1)}, s16[3,400,128]{2,1,0:T(8,128)(2,1)}, s16[3,400,128]{2,1,0:T(8,128)(2,1)}, f32[8,128]{1,0:T(8,128)S(1)}) custom-call(bf16[1152,2304]{1,0:T(8,128)(2,1)S(1)} %bitcast.11, bf16[1152,2304]{1,0:T(8,128)(2,1)S(1)} %transpose.15.refs_1_, bf16[192,2304]{1,0:T(8,128)(2,1)S(1)} %copy-done.4, ...), custom_call_target="tpu_custom_call" | custom-call | flops 1024 | bytes 1024 | tf_op jit(solution)/shard_map/ladder/pallas_call | solution.py:197
  41.7 0.6 copy-done.7
  42.3 0.6 collective-permute-start.5
  42.9 1.5 %collective-permute-start.6 = (s16[3,400,128]{2,1,0:T(8,128)(2,1)}, s16[3,400,128]{2,1,0:T(8,128)(2,1)}, u32[]{:S(2)}, u32[]{:S(2)}) collective-permute-start(s16[3,400,128]{2,1,0:T(8,128)(2,1)} %get-tuple-element.72), channel_id=1, source_target_pairs={{0,16},{4,20},{8,24},{12,28},{16,0},{20,4},{24,8},{28,12},{1,17},{... | collective-permute-start | bytes 921608 | tf_op jit(solution)/shard_map/ppermute | solution.py:161
  44.4 1.4 collective-permute-start.7
  45.8 2.5 %copy-done.1 = bf16[1152,2304]{1,0:T(8,128)(2,1)S(1)} copy-done((bf16[1152,2304]{1,0:T(8,128)(2,1)S(1)}, bf16[1152,2304]{1,0:T(8,128)(2,1)}, u32[]{:S(2)}) %copy-start.1) | copy-done | bytes 5308440
  48.3 2.5 %copy-done.3 = bf16[1152,2304]{1,0:T(8,128)(2,1)S(1)} copy-done((bf16[1152,2304]{1,0:T(8,128)(2,1)S(1)}, bf16[1152,2304]{1,0:T(8,128)(2,1)}, u32[]{:S(2)}) %copy-start.3) | copy-done | bytes 5308440
  50.8 1.0 copy-done.6
  51.8 0.7 copy-done.8
  52.5 5.2 %ladder.4 = (s16[3,400,128]{2,1,0:T(8,128)(2,1)S(1)}, s16[3,400,128]{2,1,0:T(8,128)(2,1)S(1)}, s16[3,400,128]{2,1,0:T(8,128)(2,1)S(1)}, s16[3,400,128]{2,1,0:T(8,128)(2,1)S(1)}, f32[8,128]{1,0:T(8,128)S(1)}) custom-call(bf16[1152,2304]{1,0:T(8,128)(2,1)S(1)} %copy-done.1, bf16[1152,2304]{1,0:T(8,128)(2,1)S(1)} %copy-done.3, bf16[192,2304]{1,0:T(8,128)(2,1)S(1)} %copy-done.4, ...), custom_call_target="tpu_custom_call" | custom-call | flops 1024 | bytes 1024 | tf_op jit(solution)/shard_map/ladder/pallas_call | solution.py:197
  57.8 5.2 %ladder.5 = (s16[3,400,128]{2,1,0:T(8,128)(2,1)S(1)}, s16[3,400,128]{2,1,0:T(8,128)(2,1)S(1)}, s16[3,400,128]{2,1,0:T(8,128)(2,1)S(1)}, s16[3,400,128]{2,1,0:T(8,128)(2,1)S(1)}, f32[8,128]{1,0:T(8,128)S(1)}) custom-call(bf16[1152,2304]{1,0:T(8,128)(2,1)S(1)} %copy-done.1, bf16[1152,2304]{1,0:T(8,128)(2,1)S(1)} %copy-done.3, bf16[192,2304]{1,0:T(8,128)(2,1)S(1)} %copy-done.4, ...), custom_call_target="tpu_custom_call" | custom-call | flops 1024 | bytes 1024 | tf_op jit(solution)/shard_map/ladder/pallas_call | solution.py:197
  63.0 1.6 %collective-permute-start.10 = (s16[3,400,128]{2,1,0:T(8,128)(2,1)S(1)}, s16[3,400,128]{2,1,0:T(8,128)(2,1)S(1)}, u32[]{:S(2)}, u32[]{:S(2)}) collective-permute-start(s16[3,400,128]{2,1,0:T(8,128)(2,1)S(1)} %get-tuple-element.76), channel_id=1, source_target_pairs={{0,24},{4,28},{8,16},{12,20},{16,8},{20,12},{24,0},{28,4},{1,25},{... | collective-permute-start | bytes 921608 | tf_op jit(solution)/shard_map/ppermute | solution.py:161
  64.7 1.4 %collective-permute-start.8 = (s16[3,400,128]{2,1,0:T(8,128)(2,1)S(1)}, s16[3,400,128]{2,1,0:T(8,128)(2,1)S(1)}, u32[]{:S(2)}, u32[]{:S(2)}) collective-permute-start(s16[3,400,128]{2,1,0:T(8,128)(2,1)S(1)} %get-tuple-element.74), channel_id=1, source_target_pairs={{0,8},{4,12},{8,0},{12,4},{16,24},{20,28},{24,16},{28,20},{1,9},{5... | collective-permute-start | bytes 921608 | tf_op jit(solution)/shard_map/ppermute | solution.py:161
  66.1 0.5 collective-permute-start.9
  66.7 5.3 %antisym.3 = (f32[2,1152,128]{2,1,0:T(8,128)S(1)}, s16[2,3,400,128]{3,2,1,0:T(8,128)(2,1)S(1)}, f32[8,128]{1,0:T(8,128)S(1)}) custom-call(s32[3]{0:T(128)S(1)} %pad_add_fusion.refs_0_, s16[3,400,128]{2,1,0:T(8,128)(2,1)S(1)} %get-tuple-element.81.refs_1_, s16[3,400,128]{2,1,0:T(8,128)(2,1)} %collective-permute-done.5.refs_2_, ...), custom_call_target="tpu_custom_call" | custom-call | flops 1024 | bytes 1024 | tf_op jit(solution)/shard_map/antisym/pallas_call | solution.py:197
  72.0 1.7 %collective-permute-start.14 = (s16[2,3,400,128]{3,2,1,0:T(8,128)(2,1)S(1)}, s16[2,3,400,128]{3,2,1,0:T(8,128)(2,1)S(1)}, u32[]{:S(2)}, u32[]{:S(2)}) collective-permute-start(s16[2,3,400,128]{3,2,1,0:T(8,128)(2,1)S(1)} %get-tuple-element.84), channel_id=1, source_target_pairs={{0,1},{1,0},{2,3},{3,2},{4,5},{5,4},{6,7},{7,6},{8,9},{9,8},{10,11... | collective-permute-start | bytes 1843208 | tf_op jit(solution)/shard_map/ppermute | solution.py:309
  73.7 0.5 collective-permute-done.10.refs_4_
  74.2 3.4 %collective-permute-done.8.refs_2_ = s16[3,400,128]{2,1,0:T(8,128)(2,1)S(1)} collective-permute-done((s16[3,400,128]{2,1,0:T(8,128)(2,1)S(1)}, s16[3,400,128]{2,1,0:T(8,128)(2,1)S(1)}, u32[]{:S(2)}, u32[]{:S(2)}) %collective-permute-start.8) | collective-permute-done | bytes 307232 | tf_op jit(solution)/shard_map/ppermute | solution.py:161
  77.6 4.7 %antisym.4 = (f32[2,1152,128]{2,1,0:T(8,128)S(1)}, s16[2,3,400,128]{3,2,1,0:T(8,128)(2,1)S(1)}, f32[8,128]{1,0:T(8,128)S(1)}) custom-call(s32[3]{0:T(128)S(1)} %pad_add_fusion.refs_0_, s16[3,400,128]{2,1,0:T(8,128)(2,1)S(1)} %get-tuple-element.85.refs_1_, s16[3,400,128]{2,1,0:T(8,128)(2,1)S(1)} %collective-permute-done.8.refs_2_, ...), custom_call_target="tpu_custom_call" | custom-call | flops 1024 | bytes 1024 | tf_op jit(solution)/shard_map/antisym/pallas_call | solution.py:197
  82.3 1.6 %collective-permute-start.18 = (s16[2,3,400,128]{3,2,1,0:T(8,128)(2,1)S(1)}, s16[2,3,400,128]{3,2,1,0:T(8,128)(2,1)S(1)}, u32[]{:S(2)}, u32[]{:S(2)}) collective-permute-start(s16[2,3,400,128]{3,2,1,0:T(8,128)(2,1)S(1)} %get-tuple-element.94), channel_id=1, source_target_pairs={{0,1},{1,0},{2,3},{3,2},{4,5},{5,4},{6,7},{7,6},{8,9},{9,8},{10,11... | collective-permute-start | bytes 1843208 | tf_op jit(solution)/shard_map/ppermute | solution.py:309
  83.9 0.7 collective-permute-start.11
  84.6 1.4 %collective-permute-start.12 = (s16[3,400,128]{2,1,0:T(8,128)(2,1)S(1)}, s16[3,400,128]{2,1,0:T(8,128)(2,1)S(1)}, u32[]{:S(2)}, u32[]{:S(2)}) collective-permute-start(s16[3,400,128]{2,1,0:T(8,128)(2,1)S(1)} %get-tuple-element.79), channel_id=1, source_target_pairs={{0,16},{4,20},{8,24},{12,28},{16,0},{20,4},{24,8},{28,12},{1,17},{... | collective-permute-start | bytes 921608 | tf_op jit(solution)/shard_map/ppermute | solution.py:161
  86.0 1.4 %collective-permute-start.13 = (s16[3,400,128]{2,1,0:T(8,128)(2,1)S(1)}, s16[3,400,128]{2,1,0:T(8,128)(2,1)S(1)}, u32[]{:S(2)}, u32[]{:S(2)}) collective-permute-start(s16[3,400,128]{2,1,0:T(8,128)(2,1)S(1)} %get-tuple-element.80), channel_id=1, source_target_pairs={{0,24},{4,28},{8,16},{12,20},{16,8},{20,12},{24,0},{28,4},{1,25},{... | collective-permute-start | bytes 921608 | tf_op jit(solution)/shard_map/ppermute | solution.py:161
  87.6 2.6 %collective-permute-start.17 = (s16[1,3,400,128]{3,2,1,0:T(8,128)(2,1)S(1)}, s16[1,3,400,128]{3,2,1,0:T(8,128)(2,1)S(1)}, u32[]{:S(2)}, u32[]{:S(2)}) collective-permute-start(s16[1,3,400,128]{3,2,1,0:T(8,128)(2,1)S(1)} %get-tuple-element.92), channel_id=1, source_target_pairs={{0,2},{1,3},{2,0},{3,1},{4,6},{5,7},{6,4},{7,5},{8,10},{9,11},{10,... | collective-permute-start | bytes 921608 | tf_op jit(solution)/shard_map/ppermute | solution.py:309
  90.2 3.9 %collective-permute-done.11.refs_2_ = s16[3,400,128]{2,1,0:T(8,128)(2,1)S(1)} collective-permute-done((s16[3,400,128]{2,1,0:T(8,128)(2,1)S(1)}, s16[3,400,128]{2,1,0:T(8,128)(2,1)S(1)}, u32[]{:S(2)}, u32[]{:S(2)}) %collective-permute-start.11) | collective-permute-done | bytes 307232 | tf_op jit(solution)/shard_map/ppermute | solution.py:161
  94.1 4.1 %collective-permute-done.12.refs_3_ = s16[3,400,128]{2,1,0:T(8,128)(2,1)S(1)} collective-permute-done((s16[3,400,128]{2,1,0:T(8,128)(2,1)S(1)}, s16[3,400,128]{2,1,0:T(8,128)(2,1)S(1)}, u32[]{:S(2)}, u32[]{:S(2)}) %collective-permute-start.12) | collective-permute-done | bytes 307232 | tf_op jit(solution)/shard_map/ppermute | solution.py:161
  98.3 1.5 %collective-permute-done.13.refs_4_ = s16[3,400,128]{2,1,0:T(8,128)(2,1)S(1)} collective-permute-done((s16[3,400,128]{2,1,0:T(8,128)(2,1)S(1)}, s16[3,400,128]{2,1,0:T(8,128)(2,1)S(1)}, u32[]{:S(2)}, u32[]{:S(2)}) %collective-permute-start.13) | collective-permute-done | bytes 307232 | tf_op jit(solution)/shard_map/ppermute | solution.py:161
  99.7 4.7 %antisym.5 = (f32[2,1152,128]{2,1,0:T(8,128)S(1)}, s16[1,3,400,128]{3,2,1,0:T(8,128)(2,1)S(1)}, s16[1,3,400,128]{3,2,1,0:T(8,128)(2,1)S(1)}, f32[8,128]{1,0:T(8,128)S(1)}) custom-call(s32[3]{0:T(128)S(1)} %pad_add_fusion.refs_0_, s16[3,400,128]{2,1,0:T(8,128)(2,1)S(1)} %get-tuple-element.77.refs_1_, s16[3,400,128]{2,1,0:T(8,128)(2,1)S(1)} %collective-permute-done.11.refs_2_, ...), custom_call_target="tpu_custom_call" | custom-call | flops 1024 | bytes 1024 | tf_op jit(solution)/shard_map/antisym/pallas_call | solution.py:197
  104.4 0.5 collective-permute-start.16
  105.0 1.6 %collective-permute-start.15 = (s16[1,3,400,128]{3,2,1,0:T(8,128)(2,1)S(1)}, s16[1,3,400,128]{3,2,1,0:T(8,128)(2,1)S(1)}, u32[]{:S(2)}, u32[]{:S(2)}) collective-permute-start(s16[1,3,400,128]{3,2,1,0:T(8,128)(2,1)S(1)} %get-tuple-element.90), channel_id=1, source_target_pairs={{0,1},{1,0},{2,3},{3,2},{4,5},{5,4},{6,7},{7,6},{8,9},{9,8},{10,11... | collective-permute-start | bytes 921608 | tf_op jit(solution)/shard_map/ppermute | solution.py:309
  106.7 2.6 %collective-permute-start.20 = (s16[1,3,400,128]{3,2,1,0:T(8,128)(2,1)S(1)}, s16[1,3,400,128]{3,2,1,0:T(8,128)(2,1)S(1)}, u32[]{:S(2)}, u32[]{:S(2)}) collective-permute-start(s16[1,3,400,128]{3,2,1,0:T(8,128)(2,1)S(1)} %get-tuple-element.99), channel_id=1, source_target_pairs={{0,2},{1,3},{2,0},{3,1},{4,6},{5,7},{6,4},{7,5},{8,10},{9,11},{10,... | collective-permute-start | bytes 921608 | tf_op jit(solution)/shard_map/ppermute | solution.py:309
  109.3 1.4 finish.3
  110.7 12.2 %collective-permute-done.16.refs_1_ = s16[1,3,400,128]{3,2,1,0:T(8,128)(2,1)S(1)} collective-permute-done((s16[1,3,400,128]{3,2,1,0:T(8,128)(2,1)S(1)}, s16[1,3,400,128]{3,2,1,0:T(8,128)(2,1)S(1)}, u32[]{:S(2)}, u32[]{:S(2)}) %collective-permute-start.16) | collective-permute-done | bytes 307232 | tf_op jit(solution)/shard_map/ppermute | solution.py:309
  123.2 2.7 %collective-permute-done.20.refs_4_ = s16[1,3,400,128]{3,2,1,0:T(8,128)(2,1)S(1)} collective-permute-done((s16[1,3,400,128]{3,2,1,0:T(8,128)(2,1)S(1)}, s16[1,3,400,128]{3,2,1,0:T(8,128)(2,1)S(1)}, u32[]{:S(2)}, u32[]{:S(2)}) %collective-permute-start.20) | collective-permute-done | bytes 307232 | tf_op jit(solution)/shard_map/ppermute | solution.py:309
  125.9 1.4 finish.4
  127.3 11.1 %collective-permute-done.19.refs_4_ = s16[1,3,400,128]{3,2,1,0:T(8,128)(2,1)S(1)} collective-permute-done((s16[1,3,400,128]{3,2,1,0:T(8,128)(2,1)S(1)}, s16[1,3,400,128]{3,2,1,0:T(8,128)(2,1)S(1)}, u32[]{:S(2)}, u32[]{:S(2)}) %collective-permute-start.19) | collective-permute-done | bytes 307232 | tf_op jit(solution)/shard_map/ppermute | solution.py:309
  138.4 1.4 finish.5
  (52 shorter events, 1.9 us)
Async XLA Ops:
  0.0 11.0 %copy-start.9 = (f32[96]{0:T(128)S(1)}, f32[96]{0:T(128)}, u32[]{:S(2)}) copy-start(f32[96]{0:T(128)} %param.9) | copy-start | bytes 1156
  0.0 11.2 %copy-start.10 = (s32[192,2]{0,1:T(2,128)S(1)}, s32[192,2]{0,1:T(2,128)}, u32[]{:S(2)}) copy-start(s32[192,2]{0,1:T(2,128)} %param.7) | copy-start | bytes 4612
  0.0 11.3 %copy-start.11 = (f32[160]{0:T(256)S(1)}, f32[160]{0:T(256)}, u32[]{:S(2)}) copy-start(f32[160]{0:T(256)} %param.8) | copy-start | bytes 1924
  0.0 11.8 %collective-permute-start.2 = (bf16[2304,1152]{1,0:T(8,128)(2,1)}, bf16[2304,1152]{1,0:T(8,128)(2,1)}, u32[]{:S(2)}, u32[]{:S(2)}) collective-permute-start(bf16[2304,1152]{1,0:T(8,128)(2,1)} %in_ref.1), channel_id=1, source_target_pairs={{0,4},{4,0},{8,12},{12,8},{16,20},{20,16},{24,28},{28,24},{1,5},{5... | collective-permute-start | bytes 15925256 | tf_op jit(solution)/shard_map/ppermute | solution.py:269
  0.5 23.0 %collective-permute-start = (bf16[192,2304]{1,0:T(8,128)(2,1)}, bf16[192,2304]{1,0:T(8,128)(2,1)S(1)}, u32[]{:S(2)}, u32[]{:S(2)}) collective-permute-start(bf16[192,2304]{1,0:T(8,128)(2,1)} %refs_2_.5), channel_id=1, source_target_pairs={{0,8},{4,12},{8,0},{12,4},{16,24},{20,28},{24,16},{28,20},{1,9},{5... | collective-permute-start | bytes 2654216 | tf_op jit(solution)/shard_map/ppermute | solution.py:161
  3.1 21.9 %collective-permute-start.1 = (bf16[192,2304]{1,0:T(8,128)(2,1)}, bf16[192,2304]{1,0:T(8,128)(2,1)S(1)}, u32[]{:S(2)}, u32[]{:S(2)}) collective-permute-start(bf16[192,2304]{1,0:T(8,128)(2,1)} %refs_2_.5), channel_id=1, source_target_pairs={{0,16},{4,20},{8,24},{12,28},{16,0},{20,4},{24,8},{28,12},{1,17},{... | collective-permute-start | bytes 2654216 | tf_op jit(solution)/shard_map/ppermute | solution.py:161
  8.6 2.4 %copy-start = (bf16[1152,2304]{1,0:T(8,128)(2,1)}, bf16[1152,2304]{1,0:T(8,128)(2,1)S(1)}, u32[]{:S(2)}) copy-start(bf16[1152,2304]{1,0:T(8,128)(2,1)S(1)} %transpose.14.refs_0_) | copy-start | bytes 15925252
  11.7 24.8 %slice-start = ((s8[5308416]{0:T(1024)(128)(4,1)}), s8[4194304]{0:T(1024)(128)(4,1)S(1)}, s32[]{:S(2)}) async-start(s8[5308416]{0:T(1024)(128)(4,1)} %bitcast.10), calls=%async_computation | async-start | bytes 8388608
  11.8 24.7 %slice-start.1 = ((s8[5308416]{0:T(1024)(128)(4,1)}), s8[1114112]{0:T(1024)(128)(4,1)S(1)}, s32[]{:S(2)}) async-start(s8[5308416]{0:T(1024)(128)(4,1)} %bitcast.10), calls=%async_computation.1 | async-start | bytes 2228224
  16.4 25.3 %copy-start.2 = (bf16[1152,2304]{1,0:T(8,128)(2,1)}, bf16[1152,2304]{1,0:T(8,128)(2,1)S(1)}, u32[]{:S(2)}) copy-start(bf16[1152,2304]{1,0:T(8,128)(2,1)S(1)} %transpose.15.refs_1_) | copy-start | bytes 15925252
  16.4 20.1 %copy-start.4 = (bf16[192,2304]{1,0:T(8,128)(2,1)S(1)}, bf16[192,2304]{1,0:T(8,128)(2,1)}, u32[]{:S(2)}) copy-start(bf16[192,2304]{1,0:T(8,128)(2,1)} %refs_2_.5) | copy-start | bytes 2654212
  25.1 11.5 %collective-permute-start.4 = (bf16[96,2304]{1,0:T(8,128)(2,1)S(1)}, bf16[96,2304]{1,0:T(8,128)(2,1)S(1)}, u32[]{:S(2)}, u32[]{:S(2)}) collective-permute-start(bf16[96,2304]{1,0:T(8,128)(2,1)S(1)} %slice.15), channel_id=1, source_target_pairs={{0,8},{4,12},{8,0},{12,4},{16,24},{20,28},{24,16},{28,20},{1,9},{5... | collective-permute-start | bytes 1327112 | tf_op jit(solution)/shard_map/ppermute | solution.py:161
  26.3 19.6 %collective-permute-start.3 = (bf16[96,2304]{1,0:T(8,128)(2,1)}, bf16[96,2304]{1,0:T(8,128)(2,1)}, u32[]{:S(2)}, u32[]{:S(2)}) collective-permute-start(bf16[96,2304]{1,0:T(8,128)(2,1)} %slice.14), channel_id=1, source_target_pairs={{0,16},{4,20},{8,24},{12,28},{16,0},{20,4},{24,8},{28,12},{1,17},{... | collective-permute-start | bytes 1327112 | tf_op jit(solution)/shard_map/ppermute | solution.py:161
  36.5 5.2 %copy-start.5 = (bf16[96,2304]{1,0:T(8,128)(2,1)}, bf16[96,2304]{1,0:T(8,128)(2,1)S(1)}, u32[]{:S(2)}) copy-start(bf16[96,2304]{1,0:T(8,128)(2,1)S(1)} %collective-permute-done.4.refs_5_) | copy-start | bytes 1327108
  41.7 0.6 copy-start.7
  42.3 20.7 %collective-permute-start.5 = (s16[3,400,128]{2,1,0:T(8,128)(2,1)}, s16[3,400,128]{2,1,0:T(8,128)(2,1)}, u32[]{:S(2)}, u32[]{:S(2)}) collective-permute-start(s16[3,400,128]{2,1,0:T(8,128)(2,1)} %get-tuple-element.71), channel_id=1, source_target_pairs={{0,8},{4,12},{8,0},{12,4},{16,24},{20,28},{24,16},{28,20},{1,9},{5... | collective-permute-start | bytes 921608 | tf_op jit(solution)/shard_map/ppermute | solution.py:161
  42.9 20.1 %collective-permute-start.6 = (s16[3,400,128]{2,1,0:T(8,128)(2,1)}, s16[3,400,128]{2,1,0:T(8,128)(2,1)}, u32[]{:S(2)}, u32[]{:S(2)}) collective-permute-start(s16[3,400,128]{2,1,0:T(8,128)(2,1)} %get-tuple-element.72), channel_id=1, source_target_pairs={{0,16},{4,20},{8,24},{12,28},{16,0},{20,4},{24,8},{28,12},{1,17},{... | collective-permute-start | bytes 921608 | tf_op jit(solution)/shard_map/ppermute | solution.py:161
  44.4 18.6 %collective-permute-start.7 = (s16[3,400,128]{2,1,0:T(8,128)(2,1)}, s16[3,400,128]{2,1,0:T(8,128)(2,1)}, u32[]{:S(2)}, u32[]{:S(2)}) collective-permute-start(s16[3,400,128]{2,1,0:T(8,128)(2,1)} %get-tuple-element.73), channel_id=1, source_target_pairs={{0,24},{4,28},{8,16},{12,20},{16,8},{20,12},{24,0},{28,4},{1,25},{... | collective-permute-start | bytes 921608 | tf_op jit(solution)/shard_map/ppermute | solution.py:161
  45.8 2.5 %copy-start.1 = (bf16[1152,2304]{1,0:T(8,128)(2,1)S(1)}, bf16[1152,2304]{1,0:T(8,128)(2,1)}, u32[]{:S(2)}) copy-start(bf16[1152,2304]{1,0:T(8,128)(2,1)} %copy-done) | copy-start | bytes 15925252
  48.3 2.5 %copy-start.3 = (bf16[1152,2304]{1,0:T(8,128)(2,1)S(1)}, bf16[1152,2304]{1,0:T(8,128)(2,1)}, u32[]{:S(2)}) copy-start(bf16[1152,2304]{1,0:T(8,128)(2,1)} %copy-done.2) | copy-start | bytes 15925252
  50.8 1.0 copy-start.6
  51.8 0.7 copy-start.8
  63.0 11.2 %collective-permute-start.10 = (s16[3,400,128]{2,1,0:T(8,128)(2,1)S(1)}, s16[3,400,128]{2,1,0:T(8,128)(2,1)S(1)}, u32[]{:S(2)}, u32[]{:S(2)}) collective-permute-start(s16[3,400,128]{2,1,0:T(8,128)(2,1)S(1)} %get-tuple-element.76), channel_id=1, source_target_pairs={{0,24},{4,28},{8,16},{12,20},{16,8},{20,12},{24,0},{28,4},{1,25},{... | collective-permute-start | bytes 921608 | tf_op jit(solution)/shard_map/ppermute | solution.py:161
  64.7 12.9 %collective-permute-start.8 = (s16[3,400,128]{2,1,0:T(8,128)(2,1)S(1)}, s16[3,400,128]{2,1,0:T(8,128)(2,1)S(1)}, u32[]{:S(2)}, u32[]{:S(2)}) collective-permute-start(s16[3,400,128]{2,1,0:T(8,128)(2,1)S(1)} %get-tuple-element.74), channel_id=1, source_target_pairs={{0,8},{4,12},{8,0},{12,4},{16,24},{20,28},{24,16},{28,20},{1,9},{5... | collective-permute-start | bytes 921608 | tf_op jit(solution)/shard_map/ppermute | solution.py:161
  66.1 11.5 %collective-permute-start.9 = (s16[3,400,128]{2,1,0:T(8,128)(2,1)S(1)}, s16[3,400,128]{2,1,0:T(8,128)(2,1)S(1)}, u32[]{:S(2)}, u32[]{:S(2)}) collective-permute-start(s16[3,400,128]{2,1,0:T(8,128)(2,1)S(1)} %get-tuple-element.75), channel_id=1, source_target_pairs={{0,16},{4,20},{8,24},{12,28},{16,0},{20,4},{24,8},{28,12},{1,17},{... | collective-permute-start | bytes 921608 | tf_op jit(solution)/shard_map/ppermute | solution.py:161
  72.0 15.4 %collective-permute-start.14 = (s16[2,3,400,128]{3,2,1,0:T(8,128)(2,1)S(1)}, s16[2,3,400,128]{3,2,1,0:T(8,128)(2,1)S(1)}, u32[]{:S(2)}, u32[]{:S(2)}) collective-permute-start(s16[2,3,400,128]{3,2,1,0:T(8,128)(2,1)S(1)} %get-tuple-element.84), channel_id=1, source_target_pairs={{0,1},{1,0},{2,3},{3,2},{4,5},{5,4},{6,7},{7,6},{8,9},{9,8},{10,11... | collective-permute-start | bytes 1843208 | tf_op jit(solution)/shard_map/ppermute | solution.py:309
  82.3 24.3 %collective-permute-start.18 = (s16[2,3,400,128]{3,2,1,0:T(8,128)(2,1)S(1)}, s16[2,3,400,128]{3,2,1,0:T(8,128)(2,1)S(1)}, u32[]{:S(2)}, u32[]{:S(2)}) collective-permute-start(s16[2,3,400,128]{3,2,1,0:T(8,128)(2,1)S(1)} %get-tuple-element.94), channel_id=1, source_target_pairs={{0,1},{1,0},{2,3},{3,2},{4,5},{5,4},{6,7},{7,6},{8,9},{9,8},{10,11... | collective-permute-start | bytes 1843208 | tf_op jit(solution)/shard_map/ppermute | solution.py:309
  83.9 10.2 %collective-permute-start.11 = (s16[3,400,128]{2,1,0:T(8,128)(2,1)S(1)}, s16[3,400,128]{2,1,0:T(8,128)(2,1)S(1)}, u32[]{:S(2)}, u32[]{:S(2)}) collective-permute-start(s16[3,400,128]{2,1,0:T(8,128)(2,1)S(1)} %get-tuple-element.78), channel_id=1, source_target_pairs={{0,8},{4,12},{8,0},{12,4},{16,24},{20,28},{24,16},{28,20},{1,9},{5... | collective-permute-start | bytes 921608 | tf_op jit(solution)/shard_map/ppermute | solution.py:161
  84.6 13.7 %collective-permute-start.12 = (s16[3,400,128]{2,1,0:T(8,128)(2,1)S(1)}, s16[3,400,128]{2,1,0:T(8,128)(2,1)S(1)}, u32[]{:S(2)}, u32[]{:S(2)}) collective-permute-start(s16[3,400,128]{2,1,0:T(8,128)(2,1)S(1)} %get-tuple-element.79), channel_id=1, source_target_pairs={{0,16},{4,20},{8,24},{12,28},{16,0},{20,4},{24,8},{28,12},{1,17},{... | collective-permute-start | bytes 921608 | tf_op jit(solution)/shard_map/ppermute | solution.py:161
  86.0 13.7 %collective-permute-start.13 = (s16[3,400,128]{2,1,0:T(8,128)(2,1)S(1)}, s16[3,400,128]{2,1,0:T(8,128)(2,1)S(1)}, u32[]{:S(2)}, u32[]{:S(2)}) collective-permute-start(s16[3,400,128]{2,1,0:T(8,128)(2,1)S(1)} %get-tuple-element.80), channel_id=1, source_target_pairs={{0,24},{4,28},{8,16},{12,20},{16,8},{20,12},{24,0},{28,4},{1,25},{... | collective-permute-start | bytes 921608 | tf_op jit(solution)/shard_map/ppermute | solution.py:161
  87.6 21.7 %collective-permute-start.17 = (s16[1,3,400,128]{3,2,1,0:T(8,128)(2,1)S(1)}, s16[1,3,400,128]{3,2,1,0:T(8,128)(2,1)S(1)}, u32[]{:S(2)}, u32[]{:S(2)}) collective-permute-start(s16[1,3,400,128]{3,2,1,0:T(8,128)(2,1)S(1)} %get-tuple-element.92), channel_id=1, source_target_pairs={{0,2},{1,3},{2,0},{3,1},{4,6},{5,7},{6,4},{7,5},{8,10},{9,11},{10,... | collective-permute-start | bytes 921608 | tf_op jit(solution)/shard_map/ppermute | solution.py:309
  104.4 18.5 %collective-permute-start.16 = (s16[1,3,400,128]{3,2,1,0:T(8,128)(2,1)S(1)}, s16[1,3,400,128]{3,2,1,0:T(8,128)(2,1)S(1)}, u32[]{:S(2)}, u32[]{:S(2)}) collective-permute-start(s16[1,3,400,128]{3,2,1,0:T(8,128)(2,1)S(1)} %get-tuple-element.91), channel_id=1, source_target_pairs={{0,1},{1,0},{2,3},{3,2},{4,5},{5,4},{6,7},{7,6},{8,9},{9,8},{10,11... | collective-permute-start | bytes 921608 | tf_op jit(solution)/shard_map/ppermute | solution.py:309
  105.0 22.3 %collective-permute-start.15 = (s16[1,3,400,128]{3,2,1,0:T(8,128)(2,1)S(1)}, s16[1,3,400,128]{3,2,1,0:T(8,128)(2,1)S(1)}, u32[]{:S(2)}, u32[]{:S(2)}) collective-permute-start(s16[1,3,400,128]{3,2,1,0:T(8,128)(2,1)S(1)} %get-tuple-element.90), channel_id=1, source_target_pairs={{0,1},{1,0},{2,3},{3,2},{4,5},{5,4},{6,7},{7,6},{8,9},{9,8},{10,11... | collective-permute-start | bytes 921608 | tf_op jit(solution)/shard_map/ppermute | solution.py:309
  106.7 19.2 %collective-permute-start.20 = (s16[1,3,400,128]{3,2,1,0:T(8,128)(2,1)S(1)}, s16[1,3,400,128]{3,2,1,0:T(8,128)(2,1)S(1)}, u32[]{:S(2)}, u32[]{:S(2)}) collective-permute-start(s16[1,3,400,128]{3,2,1,0:T(8,128)(2,1)S(1)} %get-tuple-element.99), channel_id=1, source_target_pairs={{0,2},{1,3},{2,0},{3,1},{4,6},{5,7},{6,4},{7,5},{8,10},{9,11},{10,... | collective-permute-start | bytes 921608 | tf_op jit(solution)/shard_map/ppermute | solution.py:309
  123.1 15.3 %collective-permute-start.19 = (s16[1,3,400,128]{3,2,1,0:T(8,128)(2,1)S(1)}, s16[1,3,400,128]{3,2,1,0:T(8,128)(2,1)S(1)}, u32[]{:S(2)}, u32[]{:S(2)}) collective-permute-start(s16[1,3,400,128]{3,2,1,0:T(8,128)(2,1)S(1)} %get-tuple-element.98), channel_id=1, source_target_pairs={{0,2},{1,3},{2,0},{3,1},{4,6},{5,7},{6,4},{7,5},{8,10},{9,11},{10,... | collective-permute-start | bytes 921608 | tf_op jit(solution)/shard_map/ppermute | solution.py:309

commit v8 on v7

--- a/solution.py
+++ b/solution.py
@@ -163,7 +163,8 @@
     def limit(mib):
         return pltpu.CompilerParams(vmem_limit_bytes=mib * 1024 * 1024)
 
-    cost = pl.CostEstimate(flops=1024, bytes_accessed=1024, transcendentals=0)
+    def cost(flops, moved):
+        return pl.CostEstimate(flops=flops, bytes_accessed=moved, transcendentals=0)
 
     smem = pl.BlockSpec(memory_space=pltpu.SMEM)
     vmem = pl.BlockSpec(memory_space=pltpu.VMEM)
@@ -180,12 +181,15 @@
         out_specs=vmem,
         out_shape=jax.ShapeDtypeStruct((rows, depth), jnp.bfloat16),
         compiler_params=limit(16),
-        cost_estimate=cost,
+        cost_estimate=cost(0, 4 * rows * depth),
         name="transpose",
     )
 
-    def ordered(body, inputs, in_specs, out_specs, out_shape, mib, scratch=(), name=None, **more):
+    def ordered(
+        body, flops, inputs, in_specs, out_specs, out_shape, mib, scratch=(), name=None, **more
+    ):
         given, made = len(in_specs), len(out_specs)
+        moved = sum(x.size * x.dtype.itemsize for x in (*inputs, *out_shape))
 
         def kernel(*refs):
             token_in, token_out = refs[given], refs[given + 1 + made]
@@ -201,7 +205,7 @@
                 out_shape=[*out_shape, jax.ShapeDtypeStruct(token.shape, token.dtype)],
                 scratch_shapes=scratch,
                 compiler_params=limit(mib),
-                cost_estimate=cost,
+                cost_estimate=cost(flops, moved),
                 name=name,
                 **more,
             )(*args, token)
@@ -212,6 +216,7 @@
         arrays, pieces = zip(*[(x, (start, count)) for x, start, count in gathered])
         return ordered(
             functools.partial(ladder_kernel, chips, tile, pieces),
+            4 * rows * depth * chips * WIDTH,
             [own_t, sib_t, *arrays],
             [vmem] * (2 + len(arrays)),
             [vmem] * chips,
@@ -224,6 +229,7 @@
     def antisym(parcels, arrived):
         return ordered(
             functools.partial(antisym_kernel, chips, slabs, vir),
+            8 * vir * vir * LANES,
             [place, *arrived],
             [smem] + [vmem] * chips,
             [vmem] * (1 + parcels),
@@ -240,6 +246,7 @@
     def hop(slots, parts, got):
         return ordered(
             functools.partial(hop_kernel, slots),
+            8 * part_rows * LANES,
             [parts, *got],
             [vmem] * (1 + len(got)),
             [vmem],
@@ -252,6 +259,7 @@
         given = [] if so_far is None else [so_far]
         return ordered(
             functools.partial(finish_kernel, places, len(got)),
+            16 * part_rows * LANES,
             [eps_pair, eps_virt, parts, *got, *given],
             [pl.BlockSpec((1, 1, LANES), lambda i: (r, 0, 0))]
             + [vmem] * (2 + len(got))

time: 140 us -> 141 us (level)
  waiting for transfers between devices: 56.6 us -> 60.6 us
  starting transfers between devices: 28 us -> 25.2 us
    ppermute x7, waiting for transfers between devices: 26 us -> 37 us  [across(): return lax.ppermute(x, 'slab', [(i, i ^ level) for i in range(slabs)])]
    ppermute x13, waiting for transfers between devices: 30.5 us -> 23.6 us  [to_chip(): return lax.ppermute(x, 'pair', [(i, i ^ d * CORES) for i in range(devices)])]
    ppermute x7, starting transfers between devices: 10.7 us -> 8.2 us  [across(): return lax.ppermute(x, 'slab', [(i, i ^ level) for i in range(slabs)])]
    unnamed x28 -> x16, local copies, waits for them, and re-layouts: 9.69 us -> 9.74 us
  transfers between devices with their start and end apart: 21 -> 21, of which waited for: 11 -> 12; matrix products, arithmetic and copies ran while one was open for 1% -> 1% of each run, Pallas kernels for 30% -> 29%
where the time goes in v8:
time: 141 us
  waiting for transfers between devices  60.6 us (43%)
  Pallas kernels  42.7 us (30%)
  starting transfers between devices  25.2 us (18%)
  local copies, waits for them, and re-layouts  11.7 us (8%)
    ppermute x7, waiting for transfers between devices, across(): return lax.ppermute(x, 'slab', [(i, i ^ level) for i in range(slabs)])  37 us
    pallas_call x12, Pallas kernels, call(): pl.pallas_call(kernel, in_specs=[*in_specs, vmem], out_specs=[*out_specs,...  34.7 us
    ppermute x13, waiting for transfers between devices, to_chip(): return lax.ppermute(x, 'pair', [(i, i ^ d * CORES) for i in range(devices)])  23.6 us
    ppermute x13, starting transfers between devices, to_chip(): return lax.ppermute(x, 'pair', [(i, i ^ d * CORES) for i in range(devices)])  16.6 us
    unnamed x16, local copies, waits for them, and re-layouts  9.74 us
    ppermute x7, starting transfers between devices, across(): return lax.ppermute(x, 'slab', [(i, i ^ level) for i in range(slabs)])  8.2 us
    pallas_call x1, Pallas kernels, on_device(): own_t = transpose(in_hbm(integrals))  4.04 us
    pallas_call x1, Pallas kernels, on_device(): sib_t = transpose(swapped)  4 us
  transfers between devices with their start and end apart: 21, of which 12 were waited for; matrix products, arithmetic and copies ran while one was open for 1% of the time, Pallas kernels for 29%

profile of v8, /device:TPU:0, one launch (start us, length us, event | category | flops | bytes accessed | tf_op | source)
XLA Modules:
  0.0 140.9 jit_solution(7017381900529464903)
XLA Ops:
  0.0 0.5 collective-permute-start.2
  0.5 2.5 %collective-permute-start = (bf16[192,2304]{1,0:T(8,128)(2,1)}, bf16[192,2304]{1,0:T(8,128)(2,1)S(1)}, u32[]{:S(2)}, u32[]{:S(2)}) collective-permute-start(bf16[192,2304]{1,0:T(8,128)(2,1)} %refs_2_.5), channel_id=1, source_target_pairs={{0,8},{4,12},{8,0},{12,4},{16,24},{20,28},{24,16},{28,20},{1,9},{5... | collective-permute-start | bytes 2654216 | tf_op jit(solution)/shard_map/ppermute | solution.py:161
  2.9 1.5 %collective-permute-start.1 = (bf16[192,2304]{1,0:T(8,128)(2,1)}, bf16[192,2304]{1,0:T(8,128)(2,1)S(1)}, u32[]{:S(2)}, u32[]{:S(2)}) collective-permute-start(bf16[192,2304]{1,0:T(8,128)(2,1)} %refs_2_.5), channel_id=1, source_target_pairs={{0,16},{4,20},{8,24},{12,28},{16,0},{20,4},{24,8},{28,12},{1,17},{... | collective-permute-start | bytes 2654216 | tf_op jit(solution)/shard_map/ppermute | solution.py:161
  4.5 4.0 %transpose.14.refs_0_ = bf16[1152,2304]{1,0:T(8,128)(2,1)S(1)} custom-call(bf16[2304,1152]{1,0:T(8,128)(2,1)} %in_ref.1), custom_call_target="tpu_custom_call" | custom-call | bytes 10616832 | tf_op jit(solution)/shard_map/transpose/pallas_call | solution.py:276
  8.5 2.3 %copy-done = bf16[1152,2304]{1,0:T(8,128)(2,1)} copy-done((bf16[1152,2304]{1,0:T(8,128)(2,1)}, bf16[1152,2304]{1,0:T(8,128)(2,1)S(1)}, u32[]{:S(2)}) %copy-start) | copy-done | bytes 5308440
  11.7 4.0 %transpose.15.refs_1_ = bf16[1152,2304]{1,0:T(8,128)(2,1)S(1)} custom-call(bf16[2304,1152]{1,0:T(8,128)(2,1)} %collective-permute-done.2.in_ref), custom_call_target="tpu_custom_call" | custom-call | bytes 10616832 | tf_op jit(solution)/shard_map/transpose/pallas_call | solution.py:278
  15.7 2.4 %copy-done.2 = bf16[1152,2304]{1,0:T(8,128)(2,1)} copy-done((bf16[1152,2304]{1,0:T(8,128)(2,1)}, bf16[1152,2304]{1,0:T(8,128)(2,1)S(1)}, u32[]{:S(2)}) %copy-start.2) | copy-done | bytes 5308440
  18.1 5.4 %collective-permute-done.refs_3_ = bf16[192,2304]{1,0:T(8,128)(2,1)S(1)} collective-permute-done((bf16[192,2304]{1,0:T(8,128)(2,1)}, bf16[192,2304]{1,0:T(8,128)(2,1)S(1)}, u32[]{:S(2)}, u32[]{:S(2)}) %collective-permute-start) | collective-permute-done | bytes 884768 | tf_op jit(solution)/shard_map/ppermute | solution.py:161
  23.5 1.5 %collective-permute-done.1.refs_4_ = bf16[192,2304]{1,0:T(8,128)(2,1)S(1)} collective-permute-done((bf16[192,2304]{1,0:T(8,128)(2,1)}, bf16[192,2304]{1,0:T(8,128)(2,1)S(1)}, u32[]{:S(2)}, u32[]{:S(2)}) %collective-permute-start.1) | collective-permute-done | bytes 884768 | tf_op jit(solution)/shard_map/ppermute | solution.py:161
  24.9 0.8 slice.15
  25.7 0.3 collective-permute-start.4
  26.1 0.8 slice.14
  26.9 1.7 %collective-permute-start.3 = (bf16[96,2304]{1,0:T(8,128)(2,1)}, bf16[96,2304]{1,0:T(8,128)(2,1)}, u32[]{:S(2)}, u32[]{:S(2)}) collective-permute-start(bf16[96,2304]{1,0:T(8,128)(2,1)} %slice.14), channel_id=1, source_target_pairs={{0,16},{4,20},{8,24},{12,28},{16,0},{20,4},{24,8},{28,12},{1,17},{... | collective-permute-start | bytes 1327112 | tf_op jit(solution)/shard_map/ppermute | solution.py:161
  28.7 8.9 %collective-permute-done.4.refs_5_ = bf16[96,2304]{1,0:T(8,128)(2,1)} collective-permute-done((bf16[96,2304]{1,0:T(8,128)(2,1)}, bf16[96,2304]{1,0:T(8,128)(2,1)}, u32[]{:S(2)}, u32[]{:S(2)}) %collective-permute-start.4) | collective-permute-done | bytes 442400 | tf_op jit(solution)/shard_map/ppermute | solution.py:161
  37.5 2.5 %copy-done.1 = bf16[1152,2304]{1,0:T(8,128)(2,1)S(1)} copy-done((bf16[1152,2304]{1,0:T(8,128)(2,1)S(1)}, bf16[1152,2304]{1,0:T(8,128)(2,1)}, u32[]{:S(2)}) %copy-start.1) | copy-done | bytes 5308440
  40.1 2.5 %copy-done.3 = bf16[1152,2304]{1,0:T(8,128)(2,1)S(1)} copy-done((bf16[1152,2304]{1,0:T(8,128)(2,1)S(1)}, bf16[1152,2304]{1,0:T(8,128)(2,1)}, u32[]{:S(2)}) %copy-start.3) | copy-done | bytes 5308440
  42.6 5.2 %ladder.3 = (s16[3,400,128]{2,1,0:T(8,128)(2,1)S(1)}, s16[3,400,128]{2,1,0:T(8,128)(2,1)S(1)}, s16[3,400,128]{2,1,0:T(8,128)(2,1)S(1)}, s16[3,400,128]{2,1,0:T(8,128)(2,1)S(1)}, f32[8,128]{1,0:T(8,128)S(1)}) custom-call(bf16[1152,2304]{1,0:T(8,128)(2,1)S(1)} %copy-done.1, bf16[1152,2304]{1,0:T(8,128)(2,1)S(1)} %copy-done.3, bf16[192,2304]{1,0:T(8,128)(2,1)S(1)} %copy-done.4, ...), custom_call_target="tpu_custom_call" | custom-call | flops 2717908992 | bytes 14942208 | tf_op jit(solution)/shard_map/ladder/pallas_call | solution.py:201
  47.8 0.7 collective-permute-start.5
  48.5 1.5 %collective-permute-start.6 = (s16[3,400,128]{2,1,0:T(8,128)(2,1)S(1)}, s16[3,400,128]{2,1,0:T(8,128)(2,1)S(1)}, u32[]{:S(2)}, u32[]{:S(2)}) collective-permute-start(s16[3,400,128]{2,1,0:T(8,128)(2,1)S(1)} %get-tuple-element.72), channel_id=1, source_target_pairs={{0,16},{4,20},{8,24},{12,28},{16,0},{20,4},{24,8},{28,12},{1,17},{... | collective-permute-start | bytes 921608 | tf_op jit(solution)/shard_map/ppermute | solution.py:161
  50.0 1.4 collective-permute-start.7
  51.3 5.4 %ladder.4 = (s16[3,400,128]{2,1,0:T(8,128)(2,1)S(1)}, s16[3,400,128]{2,1,0:T(8,128)(2,1)S(1)}, s16[3,400,128]{2,1,0:T(8,128)(2,1)S(1)}, s16[3,400,128]{2,1,0:T(8,128)(2,1)S(1)}, f32[8,128]{1,0:T(8,128)S(1)}) custom-call(bf16[1152,2304]{1,0:T(8,128)(2,1)S(1)} %copy-done.1, bf16[1152,2304]{1,0:T(8,128)(2,1)S(1)} %copy-done.3, bf16[192,2304]{1,0:T(8,128)(2,1)S(1)} %copy-done.4, ...), custom_call_target="tpu_custom_call" | custom-call | flops 2717908992 | bytes 15384576 | tf_op jit(solution)/shard_map/ladder/pallas_call | solution.py:201
  56.7 5.2 %ladder.5 = (s16[3,400,128]{2,1,0:T(8,128)(2,1)S(1)}, s16[3,400,128]{2,1,0:T(8,128)(2,1)S(1)}, s16[3,400,128]{2,1,0:T(8,128)(2,1)S(1)}, s16[3,400,128]{2,1,0:T(8,128)(2,1)S(1)}, f32[8,128]{1,0:T(8,128)S(1)}) custom-call(bf16[1152,2304]{1,0:T(8,128)(2,1)S(1)} %copy-done.1, bf16[1152,2304]{1,0:T(8,128)(2,1)S(1)} %copy-done.3, bf16[192,2304]{1,0:T(8,128)(2,1)S(1)} %copy-done.4, ...), custom_call_target="tpu_custom_call" | custom-call | flops 2717908992 | bytes 14942208 | tf_op jit(solution)/shard_map/ladder/pallas_call | solution.py:201
  62.0 1.1 collective-permute-done.7.refs_4_
  63.1 1.8 %collective-permute-start.10 = (s16[3,400,128]{2,1,0:T(8,128)(2,1)S(1)}, s16[3,400,128]{2,1,0:T(8,128)(2,1)S(1)}, u32[]{:S(2)}, u32[]{:S(2)}) collective-permute-start(s16[3,400,128]{2,1,0:T(8,128)(2,1)S(1)} %get-tuple-element.76), channel_id=1, source_target_pairs={{0,24},{4,28},{8,16},{12,20},{16,8},{20,12},{24,0},{28,4},{1,25},{... | collective-permute-start | bytes 921608 | tf_op jit(solution)/shard_map/ppermute | solution.py:161
  64.8 0.7 collective-permute-start.8
  65.5 1.1 collective-permute-start.9
  66.6 4.7 %antisym.3 = (f32[2,1152,128]{2,1,0:T(8,128)S(1)}, s16[2,3,400,128]{3,2,1,0:T(8,128)(2,1)S(1)}, f32[8,128]{1,0:T(8,128)S(1)}) custom-call(s32[3]{0:T(128)S(1)} %pad_add_fusion.refs_0_, s16[3,400,128]{2,1,0:T(8,128)(2,1)S(1)} %get-tuple-element.81.refs_1_, s16[3,400,128]{2,1,0:T(8,128)(2,1)S(1)} %collective-permute-done.5.refs_2_, ...), custom_call_target="tpu_custom_call" | custom-call | flops 9437184 | bytes 3022860 | tf_op jit(solution)/shard_map/antisym/pallas_call | solution.py:201
  71.3 1.6 %collective-permute-start.14 = (s16[2,3,400,128]{3,2,1,0:T(8,128)(2,1)S(1)}, s16[2,3,400,128]{3,2,1,0:T(8,128)(2,1)S(1)}, u32[]{:S(2)}, u32[]{:S(2)}) collective-permute-start(s16[2,3,400,128]{3,2,1,0:T(8,128)(2,1)S(1)} %get-tuple-element.84), channel_id=1, source_target_pairs={{0,1},{1,0},{2,3},{3,2},{4,5},{5,4},{6,7},{7,6},{8,9},{9,8},{10,11... | collective-permute-start | bytes 1843208 | tf_op jit(solution)/shard_map/ppermute | solution.py:317
  72.9 1.1 collective-permute-done.10.refs_4_
  74.1 2.4 %collective-permute-done.8.refs_2_ = s16[3,400,128]{2,1,0:T(8,128)(2,1)S(1)} collective-permute-done((s16[3,400,128]{2,1,0:T(8,128)(2,1)S(1)}, s16[3,400,128]{2,1,0:T(8,128)(2,1)S(1)}, u32[]{:S(2)}, u32[]{:S(2)}) %collective-permute-start.8) | collective-permute-done | bytes 307232 | tf_op jit(solution)/shard_map/ppermute | solution.py:161
  76.5 0.8 collective-permute-done.9.refs_3_
  77.3 0.8 collective-permute-start.11
  78.1 1.0 collective-permute-start.12
  79.1 1.7 %collective-permute-start.13 = (s16[3,400,128]{2,1,0:T(8,128)(2,1)S(1)}, s16[3,400,128]{2,1,0:T(8,128)(2,1)S(1)}, u32[]{:S(2)}, u32[]{:S(2)}) collective-permute-start(s16[3,400,128]{2,1,0:T(8,128)(2,1)S(1)} %get-tuple-element.80), channel_id=1, source_target_pairs={{0,24},{4,28},{8,16},{12,20},{16,8},{20,12},{24,0},{28,4},{1,25},{... | collective-permute-start | bytes 921608 | tf_op jit(solution)/shard_map/ppermute | solution.py:161
  80.8 4.7 %antisym.4 = (f32[2,1152,128]{2,1,0:T(8,128)S(1)}, s16[2,3,400,128]{3,2,1,0:T(8,128)(2,1)S(1)}, f32[8,128]{1,0:T(8,128)S(1)}) custom-call(s32[3]{0:T(128)S(1)} %pad_add_fusion.refs_0_, s16[3,400,128]{2,1,0:T(8,128)(2,1)S(1)} %get-tuple-element.85.refs_1_, s16[3,400,128]{2,1,0:T(8,128)(2,1)S(1)} %collective-permute-done.8.refs_2_, ...), custom_call_target="tpu_custom_call" | custom-call | flops 9437184 | bytes 3022860 | tf_op jit(solution)/shard_map/antisym/pallas_call | solution.py:201
  85.5 1.7 %collective-permute-start.18 = (s16[2,3,400,128]{3,2,1,0:T(8,128)(2,1)S(1)}, s16[2,3,400,128]{3,2,1,0:T(8,128)(2,1)S(1)}, u32[]{:S(2)}, u32[]{:S(2)}) collective-permute-start(s16[2,3,400,128]{3,2,1,0:T(8,128)(2,1)S(1)} %get-tuple-element.94), channel_id=1, source_target_pairs={{0,1},{1,0},{2,3},{3,2},{4,5},{5,4},{6,7},{7,6},{8,9},{9,8},{10,11... | collective-permute-start | bytes 1843208 | tf_op jit(solution)/shard_map/ppermute | solution.py:317
  87.3 2.6 %collective-permute-start.17 = (s16[1,3,400,128]{3,2,1,0:T(8,128)(2,1)S(1)}, s16[1,3,400,128]{3,2,1,0:T(8,128)(2,1)S(1)}, u32[]{:S(2)}, u32[]{:S(2)}) collective-permute-start(s16[1,3,400,128]{3,2,1,0:T(8,128)(2,1)S(1)} %get-tuple-element.92), channel_id=1, source_target_pairs={{0,2},{1,3},{2,0},{3,1},{4,6},{5,7},{6,4},{7,5},{8,10},{9,11},{10,... | collective-permute-start | bytes 921608 | tf_op jit(solution)/shard_map/ppermute | solution.py:317
  90.0 2.4 %collective-permute-done.12.refs_3_ = s16[3,400,128]{2,1,0:T(8,128)(2,1)S(1)} collective-permute-done((s16[3,400,128]{2,1,0:T(8,128)(2,1)S(1)}, s16[3,400,128]{2,1,0:T(8,128)(2,1)S(1)}, u32[]{:S(2)}, u32[]{:S(2)}) %collective-permute-start.12) | collective-permute-done | bytes 307232 | tf_op jit(solution)/shard_map/ppermute | solution.py:161
  92.4 4.7 %antisym.5 = (f32[2,1152,128]{2,1,0:T(8,128)S(1)}, s16[1,3,400,128]{3,2,1,0:T(8,128)(2,1)S(1)}, s16[1,3,400,128]{3,2,1,0:T(8,128)(2,1)S(1)}, f32[8,128]{1,0:T(8,128)S(1)}) custom-call(s32[3]{0:T(128)S(1)} %pad_add_fusion.refs_0_, s16[3,400,128]{2,1,0:T(8,128)(2,1)S(1)} %get-tuple-element.77.refs_1_, s16[3,400,128]{2,1,0:T(8,128)(2,1)S(1)} %collective-permute-done.11.refs_2_, ...), custom_call_target="tpu_custom_call" | custom-call | flops 9437184 | bytes 3022860 | tf_op jit(solution)/shard_map/antisym/pallas_call | solution.py:201
  97.1 1.6 %collective-permute-start.16 = (s16[1,3,400,128]{3,2,1,0:T(8,128)(2,1)S(1)}, s16[1,3,400,128]{3,2,1,0:T(8,128)(2,1)S(1)}, u32[]{:S(2)}, u32[]{:S(2)}) collective-permute-start(s16[1,3,400,128]{3,2,1,0:T(8,128)(2,1)S(1)} %get-tuple-element.91), channel_id=1, source_target_pairs={{0,1},{1,0},{2,3},{3,2},{4,5},{5,4},{6,7},{7,6},{8,9},{9,8},{10,11... | collective-permute-start | bytes 921608 | tf_op jit(solution)/shard_map/ppermute | solution.py:317
  98.7 0.4 collective-permute-start.15
  99.2 10.9 %collective-permute-done.18.refs_1_.refs_3_ = s16[2,3,400,128]{3,2,1,0:T(8,128)(2,1)S(1)} collective-permute-done((s16[2,3,400,128]{3,2,1,0:T(8,128)(2,1)S(1)}, s16[2,3,400,128]{3,2,1,0:T(8,128)(2,1)S(1)}, u32[]{:S(2)}, u32[]{:S(2)}) %collective-permute-start.18) | collective-permute-done | bytes 614432 | tf_op jit(solution)/shard_map/ppermute | solution.py:317
  110.4 1.4 finish.3
  111.8 11.5 %collective-permute-done.16.refs_1_ = s16[1,3,400,128]{3,2,1,0:T(8,128)(2,1)S(1)} collective-permute-done((s16[1,3,400,128]{3,2,1,0:T(8,128)(2,1)S(1)}, s16[1,3,400,128]{3,2,1,0:T(8,128)(2,1)S(1)}, u32[]{:S(2)}, u32[]{:S(2)}) %collective-permute-start.16) | collective-permute-done | bytes 307232 | tf_op jit(solution)/shard_map/ppermute | solution.py:317
  123.5 4.3 %collective-permute-done.20.refs_4_ = s16[1,3,400,128]{3,2,1,0:T(8,128)(2,1)S(1)} collective-permute-done((s16[1,3,400,128]{3,2,1,0:T(8,128)(2,1)S(1)}, s16[1,3,400,128]{3,2,1,0:T(8,128)(2,1)S(1)}, u32[]{:S(2)}, u32[]{:S(2)}) %collective-permute-start.20) | collective-permute-done | bytes 307232 | tf_op jit(solution)/shard_map/ppermute | solution.py:317
  127.8 1.4 finish.4
  129.2 10.3 %collective-permute-done.19.refs_4_ = s16[1,3,400,128]{3,2,1,0:T(8,128)(2,1)S(1)} collective-permute-done((s16[1,3,400,128]{3,2,1,0:T(8,128)(2,1)S(1)}, s16[1,3,400,128]{3,2,1,0:T(8,128)(2,1)S(1)}, u32[]{:S(2)}, u32[]{:S(2)}) %collective-permute-start.19) | collective-permute-done | bytes 307232 | tf_op jit(solution)/shard_map/ppermute | solution.py:317
  139.5 1.4 finish.5
  (39 shorter events, 1.6 us)
Async XLA Ops:
  0.0 11.7 %collective-permute-start.2 = (bf16[2304,1152]{1,0:T(8,128)(2,1)}, bf16[2304,1152]{1,0:T(8,128)(2,1)}, u32[]{:S(2)}, u32[]{:S(2)}) collective-permute-start(bf16[2304,1152]{1,0:T(8,128)(2,1)} %in_ref.1), channel_id=1, source_target_pairs={{0,4},{4,0},{8,12},{12,8},{16,20},{20,16},{24,28},{28,24},{1,5},{5... | collective-permute-start | bytes 15925256 | tf_op jit(solution)/shard_map/ppermute | solution.py:277
  0.5 23.0 %collective-permute-start = (bf16[192,2304]{1,0:T(8,128)(2,1)}, bf16[192,2304]{1,0:T(8,128)(2,1)S(1)}, u32[]{:S(2)}, u32[]{:S(2)}) collective-permute-start(bf16[192,2304]{1,0:T(8,128)(2,1)} %refs_2_.5), channel_id=1, source_target_pairs={{0,8},{4,12},{8,0},{12,4},{16,24},{20,28},{24,16},{28,20},{1,9},{5... | collective-permute-start | bytes 2654216 | tf_op jit(solution)/shard_map/ppermute | solution.py:161
  2.9 22.0 %collective-permute-start.1 = (bf16[192,2304]{1,0:T(8,128)(2,1)}, bf16[192,2304]{1,0:T(8,128)(2,1)S(1)}, u32[]{:S(2)}, u32[]{:S(2)}) collective-permute-start(bf16[192,2304]{1,0:T(8,128)(2,1)} %refs_2_.5), channel_id=1, source_target_pairs={{0,16},{4,20},{8,24},{12,28},{16,0},{20,4},{24,8},{28,12},{1,17},{... | collective-permute-start | bytes 2654216 | tf_op jit(solution)/shard_map/ppermute | solution.py:161
  4.5 6.4 %copy-start.5 = (f32[96]{0:T(128)S(1)}, f32[96]{0:T(128)}, u32[]{:S(2)}) copy-start(f32[96]{0:T(128)} %param.9) | copy-start | bytes 1156
  4.5 6.6 %copy-start.6 = (s32[192,2]{0,1:T(2,128)S(1)}, s32[192,2]{0,1:T(2,128)}, u32[]{:S(2)}) copy-start(s32[192,2]{0,1:T(2,128)} %param.7) | copy-start | bytes 4612
  4.5 6.7 %copy-start.7 = (f32[160]{0:T(256)S(1)}, f32[160]{0:T(256)}, u32[]{:S(2)}) copy-start(f32[160]{0:T(256)} %param.8) | copy-start | bytes 1924
  8.5 2.3 %copy-start = (bf16[1152,2304]{1,0:T(8,128)(2,1)}, bf16[1152,2304]{1,0:T(8,128)(2,1)S(1)}, u32[]{:S(2)}) copy-start(bf16[1152,2304]{1,0:T(8,128)(2,1)S(1)} %transpose.14.refs_0_) | copy-start | bytes 15925252
  15.7 2.4 %copy-start.2 = (bf16[1152,2304]{1,0:T(8,128)(2,1)}, bf16[1152,2304]{1,0:T(8,128)(2,1)S(1)}, u32[]{:S(2)}) copy-start(bf16[1152,2304]{1,0:T(8,128)(2,1)S(1)} %transpose.15.refs_1_) | copy-start | bytes 15925252
  18.1 19.5 %copy-start.4 = (bf16[192,2304]{1,0:T(8,128)(2,1)S(1)}, bf16[192,2304]{1,0:T(8,128)(2,1)}, u32[]{:S(2)}) copy-start(bf16[192,2304]{1,0:T(8,128)(2,1)} %refs_2_.5) | copy-start | bytes 2654212
  25.7 11.8 %collective-permute-start.4 = (bf16[96,2304]{1,0:T(8,128)(2,1)}, bf16[96,2304]{1,0:T(8,128)(2,1)}, u32[]{:S(2)}, u32[]{:S(2)}) collective-permute-start(bf16[96,2304]{1,0:T(8,128)(2,1)} %slice.15), channel_id=1, source_target_pairs={{0,8},{4,12},{8,0},{12,4},{16,24},{20,28},{24,16},{28,20},{1,9},{5... | collective-permute-start | bytes 1327112 | tf_op jit(solution)/shard_map/ppermute | solution.py:161
  26.9 24.5 %collective-permute-start.3 = (bf16[96,2304]{1,0:T(8,128)(2,1)}, bf16[96,2304]{1,0:T(8,128)(2,1)}, u32[]{:S(2)}, u32[]{:S(2)}) collective-permute-start(bf16[96,2304]{1,0:T(8,128)(2,1)} %slice.14), channel_id=1, source_target_pairs={{0,16},{4,20},{8,24},{12,28},{16,0},{20,4},{24,8},{28,12},{1,17},{... | collective-permute-start | bytes 1327112 | tf_op jit(solution)/shard_map/ppermute | solution.py:161
  37.5 2.5 %copy-start.1 = (bf16[1152,2304]{1,0:T(8,128)(2,1)S(1)}, bf16[1152,2304]{1,0:T(8,128)(2,1)}, u32[]{:S(2)}) copy-start(bf16[1152,2304]{1,0:T(8,128)(2,1)} %copy-done) | copy-start | bytes 15925252
  40.1 2.5 %copy-start.3 = (bf16[1152,2304]{1,0:T(8,128)(2,1)S(1)}, bf16[1152,2304]{1,0:T(8,128)(2,1)}, u32[]{:S(2)}) copy-start(bf16[1152,2304]{1,0:T(8,128)(2,1)} %copy-done.2) | copy-start | bytes 15925252
  47.8 14.2 %collective-permute-start.5 = (s16[3,400,128]{2,1,0:T(8,128)(2,1)S(1)}, s16[3,400,128]{2,1,0:T(8,128)(2,1)S(1)}, u32[]{:S(2)}, u32[]{:S(2)}) collective-permute-start(s16[3,400,128]{2,1,0:T(8,128)(2,1)S(1)} %get-tuple-element.71), channel_id=1, source_target_pairs={{0,8},{4,12},{8,0},{12,4},{16,24},{20,28},{24,16},{28,20},{1,9},{5... | collective-permute-start | bytes 921608 | tf_op jit(solution)/shard_map/ppermute | solution.py:161
  48.5 13.5 %collective-permute-start.6 = (s16[3,400,128]{2,1,0:T(8,128)(2,1)S(1)}, s16[3,400,128]{2,1,0:T(8,128)(2,1)S(1)}, u32[]{:S(2)}, u32[]{:S(2)}) collective-permute-start(s16[3,400,128]{2,1,0:T(8,128)(2,1)S(1)} %get-tuple-element.72), channel_id=1, source_target_pairs={{0,16},{4,20},{8,24},{12,28},{16,0},{20,4},{24,8},{28,12},{1,17},{... | collective-permute-start | bytes 921608 | tf_op jit(solution)/shard_map/ppermute | solution.py:161
  50.0 13.1 %collective-permute-start.7 = (s16[3,400,128]{2,1,0:T(8,128)(2,1)S(1)}, s16[3,400,128]{2,1,0:T(8,128)(2,1)S(1)}, u32[]{:S(2)}, u32[]{:S(2)}) collective-permute-start(s16[3,400,128]{2,1,0:T(8,128)(2,1)S(1)} %get-tuple-element.73), channel_id=1, source_target_pairs={{0,24},{4,28},{8,16},{12,20},{16,8},{20,12},{24,0},{28,4},{1,25},{... | collective-permute-start | bytes 921608 | tf_op jit(solution)/shard_map/ppermute | solution.py:161
  63.1 11.0 %collective-permute-start.10 = (s16[3,400,128]{2,1,0:T(8,128)(2,1)S(1)}, s16[3,400,128]{2,1,0:T(8,128)(2,1)S(1)}, u32[]{:S(2)}, u32[]{:S(2)}) collective-permute-start(s16[3,400,128]{2,1,0:T(8,128)(2,1)S(1)} %get-tuple-element.76), channel_id=1, source_target_pairs={{0,24},{4,28},{8,16},{12,20},{16,8},{20,12},{24,0},{28,4},{1,25},{... | collective-permute-start | bytes 921608 | tf_op jit(solution)/shard_map/ppermute | solution.py:161
  64.8 11.7 %collective-permute-start.8 = (s16[3,400,128]{2,1,0:T(8,128)(2,1)S(1)}, s16[3,400,128]{2,1,0:T(8,128)(2,1)S(1)}, u32[]{:S(2)}, u32[]{:S(2)}) collective-permute-start(s16[3,400,128]{2,1,0:T(8,128)(2,1)S(1)} %get-tuple-element.74), channel_id=1, source_target_pairs={{0,8},{4,12},{8,0},{12,4},{16,24},{20,28},{24,16},{28,20},{1,9},{5... | collective-permute-start | bytes 921608 | tf_op jit(solution)/shard_map/ppermute | solution.py:161
  65.5 11.8 %collective-permute-start.9 = (s16[3,400,128]{2,1,0:T(8,128)(2,1)S(1)}, s16[3,400,128]{2,1,0:T(8,128)(2,1)S(1)}, u32[]{:S(2)}, u32[]{:S(2)}) collective-permute-start(s16[3,400,128]{2,1,0:T(8,128)(2,1)S(1)} %get-tuple-element.75), channel_id=1, source_target_pairs={{0,16},{4,20},{8,24},{12,28},{16,0},{20,4},{24,8},{28,12},{1,17},{... | collective-permute-start | bytes 921608 | tf_op jit(solution)/shard_map/ppermute | solution.py:161
  71.3 15.9 %collective-permute-start.14 = (s16[2,3,400,128]{3,2,1,0:T(8,128)(2,1)S(1)}, s16[2,3,400,128]{3,2,1,0:T(8,128)(2,1)S(1)}, u32[]{:S(2)}, u32[]{:S(2)}) collective-permute-start(s16[2,3,400,128]{3,2,1,0:T(8,128)(2,1)S(1)} %get-tuple-element.84), channel_id=1, source_target_pairs={{0,1},{1,0},{2,3},{3,2},{4,5},{5,4},{6,7},{7,6},{8,9},{9,8},{10,11... | collective-permute-start | bytes 1843208 | tf_op jit(solution)/shard_map/ppermute | solution.py:317
  77.3 12.7 %collective-permute-start.11 = (s16[3,400,128]{2,1,0:T(8,128)(2,1)S(1)}, s16[3,400,128]{2,1,0:T(8,128)(2,1)S(1)}, u32[]{:S(2)}, u32[]{:S(2)}) collective-permute-start(s16[3,400,128]{2,1,0:T(8,128)(2,1)S(1)} %get-tuple-element.78), channel_id=1, source_target_pairs={{0,8},{4,12},{8,0},{12,4},{16,24},{20,28},{24,16},{28,20},{1,9},{5... | collective-permute-start | bytes 921608 | tf_op jit(solution)/shard_map/ppermute | solution.py:161
  78.1 14.3 %collective-permute-start.12 = (s16[3,400,128]{2,1,0:T(8,128)(2,1)S(1)}, s16[3,400,128]{2,1,0:T(8,128)(2,1)S(1)}, u32[]{:S(2)}, u32[]{:S(2)}) collective-permute-start(s16[3,400,128]{2,1,0:T(8,128)(2,1)S(1)} %get-tuple-element.79), channel_id=1, source_target_pairs={{0,16},{4,20},{8,24},{12,28},{16,0},{20,4},{24,8},{28,12},{1,17},{... | collective-permute-start | bytes 921608 | tf_op jit(solution)/shard_map/ppermute | solution.py:161
  79.1 13.3 %collective-permute-start.13 = (s16[3,400,128]{2,1,0:T(8,128)(2,1)S(1)}, s16[3,400,128]{2,1,0:T(8,128)(2,1)S(1)}, u32[]{:S(2)}, u32[]{:S(2)}) collective-permute-start(s16[3,400,128]{2,1,0:T(8,128)(2,1)S(1)} %get-tuple-element.80), channel_id=1, source_target_pairs={{0,24},{4,28},{8,16},{12,20},{16,8},{20,12},{24,0},{28,4},{1,25},{... | collective-permute-start | bytes 921608 | tf_op jit(solution)/shard_map/ppermute | solution.py:161
  85.5 24.6 %collective-permute-start.18 = (s16[2,3,400,128]{3,2,1,0:T(8,128)(2,1)S(1)}, s16[2,3,400,128]{3,2,1,0:T(8,128)(2,1)S(1)}, u32[]{:S(2)}, u32[]{:S(2)}) collective-permute-start(s16[2,3,400,128]{3,2,1,0:T(8,128)(2,1)S(1)} %get-tuple-element.94), channel_id=1, source_target_pairs={{0,1},{1,0},{2,3},{3,2},{4,5},{5,4},{6,7},{7,6},{8,9},{9,8},{10,11... | collective-permute-start | bytes 1843208 | tf_op jit(solution)/shard_map/ppermute | solution.py:317
  87.3 23.0 %collective-permute-start.17 = (s16[1,3,400,128]{3,2,1,0:T(8,128)(2,1)S(1)}, s16[1,3,400,128]{3,2,1,0:T(8,128)(2,1)S(1)}, u32[]{:S(2)}, u32[]{:S(2)}) collective-permute-start(s16[1,3,400,128]{3,2,1,0:T(8,128)(2,1)S(1)} %get-tuple-element.92), channel_id=1, source_target_pairs={{0,2},{1,3},{2,0},{3,1},{4,6},{5,7},{6,4},{7,5},{8,10},{9,11},{10,... | collective-permute-start | bytes 921608 | tf_op jit(solution)/shard_map/ppermute | solution.py:317
  97.1 26.2 %collective-permute-start.16 = (s16[1,3,400,128]{3,2,1,0:T(8,128)(2,1)S(1)}, s16[1,3,400,128]{3,2,1,0:T(8,128)(2,1)S(1)}, u32[]{:S(2)}, u32[]{:S(2)}) collective-permute-start(s16[1,3,400,128]{3,2,1,0:T(8,128)(2,1)S(1)} %get-tuple-element.91), channel_id=1, source_target_pairs={{0,1},{1,0},{2,3},{3,2},{4,5},{5,4},{6,7},{7,6},{8,9},{9,8},{10,11... | collective-permute-start | bytes 921608 | tf_op jit(solution)/shard_map/ppermute | solution.py:317
  98.7 30.5 %collective-permute-start.15 = (s16[1,3,400,128]{3,2,1,0:T(8,128)(2,1)S(1)}, s16[1,3,400,128]{3,2,1,0:T(8,128)(2,1)S(1)}, u32[]{:S(2)}, u32[]{:S(2)}) collective-permute-start(s16[1,3,400,128]{3,2,1,0:T(8,128)(2,1)S(1)} %get-tuple-element.90), channel_id=1, source_target_pairs={{0,1},{1,0},{2,3},{3,2},{4,5},{5,4},{6,7},{7,6},{8,9},{9,8},{10,11... | collective-permute-start | bytes 921608 | tf_op jit(solution)/shard_map/ppermute | solution.py:317
  110.3 17.6 %collective-permute-start.20 = (s16[1,3,400,128]{3,2,1,0:T(8,128)(2,1)S(1)}, s16[1,3,400,128]{3,2,1,0:T(8,128)(2,1)S(1)}, u32[]{:S(2)}, u32[]{:S(2)}) collective-permute-start(s16[1,3,400,128]{3,2,1,0:T(8,128)(2,1)S(1)} %get-tuple-element.99), channel_id=1, source_target_pairs={{0,2},{1,3},{2,0},{3,1},{4,6},{5,7},{6,4},{7,5},{8,10},{9,11},{10,... | collective-permute-start | bytes 921608 | tf_op jit(solution)/shard_map/ppermute | solution.py:317
  123.4 16.1 %collective-permute-start.19 = (s16[1,3,400,128]{3,2,1,0:T(8,128)(2,1)S(1)}, s16[1,3,400,128]{3,2,1,0:T(8,128)(2,1)S(1)}, u32[]{:S(2)}, u32[]{:S(2)}) collective-permute-start(s16[1,3,400,128]{3,2,1,0:T(8,128)(2,1)S(1)} %get-tuple-element.98), channel_id=1, source_target_pairs={{0,2},{1,3},{2,0},{3,1},{4,6},{5,7},{6,4},{7,5},{8,10},{9,11},{10,... | collective-permute-start | bytes 921608 | tf_op jit(solution)/shard_map/ppermute | solution.py:317

commit v9 on v8

--- a/solution.py
+++ b/solution.py
@@ -71,6 +71,97 @@
         return carry
 
     lax.fori_loop(0, own_ref.shape[0] // tile, step, 0)
+
+
+def early_ladder_kernel(chips, tile, vir, pieces, place_ref, own_ref, sib_ref, *refs):
+    rows_in, (parts, away, rhs, work, sent) = refs[: len(pieces)], refs[len(pieces) :]
+    chip, z = place_ref[0], place_ref[2]
+    at = 0
+    for ref, (start, count) in zip(rows_in, pieces):
+        rhs[pl.ds(at, count), :] = ref[pl.ds(start, count), :]
+        at += count
+    low = is_low((tile, LANES))
+    block = vir // chips
+    group = own_ref.shape[0] // chips
+
+    def step(i, carry):
+        at = pl.ds(pl.multiple_of(i * tile, tile), tile)
+        own = lax.dot_general(own_ref[at, :], rhs[...], NT, preferred_element_type=jnp.float32)
+        sib = lax.dot_general(sib_ref[at, :], rhs[...], NT, preferred_element_type=jnp.float32)
+        for d in range(0, chips, 2):
+            u = own[:, d * WIDTH : d * WIDTH + LANES]
+            v = sib[:, d * WIDTH : d * WIDTH + LANES]
+            work[d] = jnp.where(low, u, turn(v))
+            work[d + 1] = jnp.where(low, turn(u), v)
+        for e in range(chips):
+            column = (chip ^ z ^ e) * block
+            out = sent if e % 2 else parts
+            for k in range(tile // vir):
+                source = pl.ds(pl.multiple_of(k * vir + column, 8), block)
+                line = (i * (tile // vir) + k) * block
+                for d in range(chips):
+                    target = pl.ds(pl.multiple_of(d * group + line, 8), block)
+                    out[e // 2, target, :] = work[d, source, :]
+        return carry
+
+    lax.fori_loop(0, own_ref.shape[0] // tile, step, 0)
+    for i in range(chips // 2):
+        for d in range(chips):
+            encode(sent[i, pl.ds(d * group, group), :], away.at[i, d])
+
+
+def sum_kernel(places, count, parts, *refs):
+    got, outs = refs[:count], refs[count:]
+    group = outs[0].shape[0] - TAIL
+    for d, out in enumerate(outs):
+        total = parts[0, pl.ds(d * group, group), :]
+        for k, slot in places:
+            total = total + decode(got[k].at[slot, d])
+        encode(total, out)
+
+
+def early_antisym_kernel(chips, side, place_ref, *refs):
+    arrived, own, outs = refs[:chips], refs[chips], refs[chips + 1 : 2 * chips]
+    cube, sent = refs[2 * chips :]
+    chip, core, z = place_ref[0], place_ref[1], place_ref[2]
+    group = own.shape[0]
+    size, held = CORES * group, side // CORES
+    low = is_low((group, LANES))
+    for d in range(chips):
+        values = decode(arrived[d])
+        turned = turn(values)
+        at_own = pl.multiple_of(d * size + core * group, group)
+        at_sib = pl.multiple_of(d * size + (1 - core) * group, group)
+        cube[pl.ds(at_own, group), :] = jnp.where(low, values, turned)
+        cube[pl.ds(at_sib, group), :] = jnp.where(low, turned, values)
+    low = is_low((side, LANES))
+    for e in range(chips):
+        this = (e ^ z ^ chip) * size
+        that = (e ^ chip) * size
+        out = sent if e else own
+        for a in range(held):
+            b = a + held
+            here = cube[pl.ds(pl.multiple_of(this + a * side, 8), side), :]
+            other = cube[pl.ds(pl.multiple_of(this + b * side, 8), side), :]
+            lower = here - cube[pl.ds(that + a, side, stride=side), :]
+            upper = other - cube[pl.ds(that + b, side, stride=side), :]
+            out[pl.ds(a * side, side), :] = jnp.where(low, lower, upper)
+        if e:
+            encode(sent[...], outs[e - 1])
+
+
+def early_finish_kernel(chips, side, pair_ref, vir_ref, own, *refs):
+    got, (out_ref, cube) = refs[: chips - 1], refs[-2:]
+    group, rows = own.shape[0], cube.shape[0]
+    for e in range(chips):
+        values = decode(got[e - 1]) if e else own[...]
+        for a in range(group // side):
+            target = pl.ds((a * chips + e) * side, side)
+            cube[target, :] = values[a * side : (a + 1) * side]
+    virt = jnp.where(is_low(cube.shape), vir_ref[:, 0:1], vir_ref[:, 1:2])
+    update = (cube[...] / (pair_ref[0] - virt)).T
+    out_ref[:, pl.ds(0, rows)] = update[:WIDTH]
+    out_ref[:, pl.ds(rows, rows)] = update[WIDTH:]
 
 
 def antisym_kernel(chips, slabs, vir, place_ref, *refs):
@@ -226,6 +317,60 @@
             name="ladder",
         )
 
+    early = chips == slabs and chips >= 4 and tile % vir == 0 and vir // chips % 8 == 0
+    side, group = vir // chips, rows // chips
+    small = jax.ShapeDtypeStruct((group + TAIL, LANES), jnp.int16)
+    grouped = (chips // 2, chips * group, LANES)
+
+    def early_ladder(gathered):
+        arrays, pieces = zip(*[(x, (start, count)) for x, start, count in gathered])
+        return ordered(
+            functools.partial(early_ladder_kernel, chips, tile, vir, pieces),
+            4 * rows * depth * chips * WIDTH,
+            [place, own_t, sib_t, *arrays],
+            [smem] + [vmem] * (2 + len(arrays)),
+            [vmem] * 2,
+            [
+                jax.ShapeDtypeStruct(grouped, jnp.float32),
+                jax.ShapeDtypeStruct((chips // 2, chips, *small.shape), jnp.int16),
+            ],
+            20,
+            [
+                pltpu.VMEM((chips * WIDTH, depth), jnp.bfloat16),
+                pltpu.VMEM((chips, tile, LANES), jnp.float32),
+                pltpu.VMEM(grouped, jnp.float32),
+            ],
+            name="early_ladder",
+        )
+
+    def early_sum(places, parts, got):
+        return ordered(
+            functools.partial(sum_kernel, places, len(got)),
+            8 * chips * group * LANES,
+            [parts, *got],
+            [vmem] * (1 + len(got)),
+            [vmem] * chips,
+            [small] * chips,
+            8,
+            name="early_sum",
+        )
+
+    def early_antisym(arrived):
+        return ordered(
+            functools.partial(early_antisym_kernel, chips, side),
+            8 * vir * side * LANES,
+            [place, *arrived],
+            [smem] + [vmem] * chips,
+            [vmem] * chips,
+            [jax.ShapeDtypeStruct((group, LANES), jnp.float32)] + [small] * (chips - 1),
+            12,
+            [
+                pltpu.VMEM((chips * side * side, LANES), jnp.float32),
+                pltpu.VMEM((group, LANES), jnp.float32),
+            ],
+            name="early_antisym",
+        )
+
     def antisym(parcels, arrived):
         return ordered(
             functools.partial(antisym_kernel, chips, slabs, vir),
@@ -246,19 +391,23 @@
     def hop(slots, parts, got):
         return ordered(
             functools.partial(hop_kernel, slots),
-            8 * part_rows * LANES,
+            8 * parts.size,
             [parts, *got],
             [vmem] * (1 + len(got)),
             [vmem],
-            [jax.ShapeDtypeStruct(parcel(len(slots)), jnp.int16)],
+            [jax.ShapeDtypeStruct((len(slots), *got[0].shape[1:]), jnp.int16)],
             8,
             name="hop",
         )
 
     def finish(r, parts, got, places, so_far):
         given = [] if so_far is None else [so_far]
-        return ordered(
-            functools.partial(finish_kernel, places, len(got)),
+        if places is None:
+            body = functools.partial(early_finish_kernel, chips, side)
+        else:
+            body = functools.partial(finish_kernel, places, len(got))
+        return ordered(
+            body,
             16 * part_rows * LANES,
             [eps_pair, eps_virt, parts, *got, *given],
             [pl.BlockSpec((1, 1, LANES), lambda i: (r, 0, 0))]
@@ -267,6 +416,7 @@
             [pl.BlockSpec((WIDTH, 2 * part_rows), lambda i: (r, 0))],
             [jax.ShapeDtypeStruct((num_pairs, 2 * part_rows), jnp.float32)],
             8,
+            [] if places else [pltpu.VMEM((part_rows, LANES), jnp.float32)],
             name="finish",
             grid=(1,),
             input_output_aliases={3 + len(got): 0} if given else {},
@@ -289,43 +439,45 @@
 
     place = jnp.stack([chip, core, z]).astype(jnp.int32)
 
-    mine = amplitudes
-    if chips == 4:
+    def gather(mine, beside):
+        count = mine.shape[0]
+        if chips != 4:
+            return [[mine]] + [[to_chip(mine, d)] for d in range(1, chips)], beside
         one, two = to_chip(mine, 1), to_chip(mine, 2)
-        one, two, own_t, sib_t, eps_pair, eps_virt = lax.optimization_barrier(
-            (one, two, own_t, sib_t, eps_pair, eps_virt)
-        )
-        middle = num_pairs // 2
-        low, high = to_chip(two[:middle], 1), to_chip(one[middle:], 2)
-        gathered = [[mine], [one], [two], [low, high]]
+        if beside:
+            one, two, *beside = lax.optimization_barrier((one, two, *beside))
+        low, high = to_chip(two[: count // 2], 1), to_chip(one[count // 2 :], 2)
+        return [[mine], [one], [two], [low, high]], beside
+
+    if early:
+        head, (eps_pair, eps_virt) = gather(amplitudes[:WIDTH], (eps_pair, eps_virt))
+        (head, own_t, sib_t, rest) = lax.optimization_barrier((head, own_t, sib_t, amplitudes[WIDTH:]))
+        tail, _ = gather(rest, ())
+        gathered = [(0, head), (WIDTH, tail)]
     else:
-        gathered = [[mine]] + [[to_chip(mine, d)] for d in range(1, chips)]
+        tail, (own_t, sib_t, eps_pair, eps_virt) = gather(
+            amplitudes, (own_t, sib_t, eps_pair, eps_virt)
+        )
+        gathered = [(0, tail)]
 
     def rows_of(r):
         found = []
-        for arrays in gathered:
-            at = 0
-            for x in arrays:
-                begin = max(r * WIDTH, at)
-                end = min((r + 1) * WIDTH, at + x.shape[0])
-                if begin < end:
-                    found.append((x, begin - at, end - begin))
-                at += x.shape[0]
+        for d in range(chips):
+            for base, parts in gathered:
+                at = base
+                for x in parts[d]:
+                    begin = max(r * WIDTH, at)
+                    end = min((r + 1) * WIDTH, at + x.shape[0])
+                    if begin < end:
+                        found.append((x, begin - at, end - begin))
+                    at += x.shape[0]
         return found
 
     def across(x, level):
         return lax.ppermute(x, "slab", [(i, i ^ level) for i in range(slabs)])
 
-    def stages(r):
-        sums = yield ladder(rows_of(r))
-        if r:
-            sums, _ = lax.optimization_barrier((sums, turns[-1] + results[-1][:1]))
-        arrived = [to_chip(sums[d], d) for d in range(1, chips)]
-        turns.append(arrived)
-        parcels = slabs // 2 if r == chunks - 1 else 1
-        parts, *away = yield antisym(parcels, [sums[0], *arrived])
-        away = [across(x, 1) for x in reversed(away)][::-1]
-        each = slabs // 2 // parcels
+    def halved(parts, away):
+        each = slabs // 2 // len(away)
         held = {e: [(away[e // 2 // each], e // 2 % each)] for e in range(0, slabs, 2)}
 
         def listed(wanted):
@@ -346,27 +498,54 @@
                 del held[e]
             level *= 2
         got, ((_, places),) = listed([0])
+        return got, places
+
+    def early_stages(r):
+        parts, away = yield early_ladder(rows_of(r))
+        got, places = yield from halved(parts, [across(away, 1)])
+        sums = yield early_sum(places, parts, got)
+        arrived = [sums[0]] + [to_chip(sums[d], d) for d in range(1, chips)]
+        own, *blocks = yield early_antisym(arrived)
+        got = [across(x, e + 1) for e, x in enumerate(blocks)]
+        yield finish(r, own, got, None, update)
+
+    def stages(r):
+        sums = yield ladder(rows_of(r))
+        if turns:
+            sums, _ = lax.optimization_barrier((sums, turns[-1] + results[-1][:1]))
+        arrived = [to_chip(sums[d], d) for d in range(1, chips)]
+        turns.append(arrived)
+        parcels = slabs // 2 if r == chunks - 1 else 1
+        parts, *away = yield antisym(parcels, [sums[0], *arrived])
+        if parcels > 1 and firsts:
+            away, _ = lax.optimization_barrier((away, firsts[-1]))
+        away = [across(x, 1) for x in reversed(away)][::-1]
+        firsts.append(away)
+        got, places = yield from halved(parts, away)
         yield finish(r, parts, got, places, update)
 
-    length = 3 + max(0, (slabs - 1).bit_length() - 1)
+    hops = max(0, (slabs - 1).bit_length() - 1)
 
     def when(stage):
         r, k = stage
+        if early and r == 0:
+            return (20, *[46] * hops, 54, 66, 83)[k]
         if k == 0:
-            return 30 + 5 * r
-        return 15 * r + 54 + (k - 1) * 17 - (1 if k == length - 1 else 0)
-
-    order = sorted(((r, k) for r in range(chunks) for k in range(length)), key=when)
-
-    turns = [[]]
-    running = [stages(r) for r in range(chunks)]
+            return 37 + 5 * r if early else 30 + 5 * r
+        return 15 * r + (45 if early else 54) + (k - 1) * 17 - (1 if k == 2 + hops else 0)
+
+    order = [(r, k) for r in range(chunks) for k in range(3 + hops + (early and r == 0))]
+    order = sorted(order, key=when)
+
+    turns, firsts = [], []
+    running = [early_stages(r) if early and r == 0 else stages(r) for r in range(chunks)]
     results = [None] * chunks
     update, token = None, jnp.zeros((8, LANES), jnp.float32)
     for r, k in order:
         call, inputs = running[r].send(results[r])
         *results[r], token = call(token, *inputs)
-        if k == length - 1:
-            (update,) = results[r]
+        if results[r][0].shape == (num_pairs, 2 * part_rows):
+            update = results[r][0]
     return update
 
 

time: 141 us -> 152 us (1.078)
  starting transfers between devices: 25.2 us -> 37.8 us
  Pallas kernels: 42.7 us -> 36.8 us
  local copies, waits for them, and re-layouts: 11.7 us -> 17.4 us
  waiting for transfers between devices: 60.6 us -> 58.1 us
    ppermute x7 -> x10, starting transfers between devices: 8.2 us -> 14.9 us  [across(): return lax.ppermute(x, 'slab', [(i, i ^ level) for i in range(slabs)])]
    pallas_call x12 -> x13, Pallas kernels: 34.7 us -> 28.7 us  [call(): pl.pallas_call(kernel, in_specs=[*in_specs, vmem], out_specs=[*out_specs,...]
    ppermute x13 -> x17, starting transfers between devices: 16.6 us -> 22.4 us  [to_chip(): return lax.ppermute(x, 'pair', [(i, i ^ d * CORES) for i in range(devices)])]
    ppermute x7 -> x10, waiting for transfers between devices: 37 us -> 31.8 us  [across(): return lax.ppermute(x, 'slab', [(i, i ^ level) for i in range(slabs)])]
    unnamed x16 -> x28, local copies, waits for them, and re-layouts: 9.74 us -> 13.9 us
    ppermute x13 -> x17, waiting for transfers between devices: 23.6 us -> 26.3 us  [to_chip(): return lax.ppermute(x, 'pair', [(i, i ^ d * CORES) for i in range(devices)])]
  transfers between devices with their start and end apart: 21 -> 28, of which waited for: 12 -> 13; matrix products, arithmetic and copies ran while one was open for 1% -> 3% of each run, Pallas kernels for 29% -> 20%
where the time goes in v9:
time: 152 us; the launch traced here: 151 us
  waiting for transfers between devices  58.1 us (38%)
  starting transfers between devices  37.8 us (25%)
  Pallas kernels  36.8 us (24%)
  local copies, waits for them, and re-layouts  17.4 us (11%)
    ppermute x10, waiting for transfers between devices, across(): return lax.ppermute(x, 'slab', [(i, i ^ level) for i in range(slabs)])  31.8 us
    pallas_call x13, Pallas kernels, call(): pl.pallas_call(kernel, in_specs=[*in_specs, vmem], out_specs=[*out_specs,...  28.7 us
    ppermute x17, waiting for transfers between devices, to_chip(): return lax.ppermute(x, 'pair', [(i, i ^ d * CORES) for i in range(devices)])  26.3 us
    ppermute x17, starting transfers between devices, to_chip(): return lax.ppermute(x, 'pair', [(i, i ^ d * CORES) for i in range(devices)])  22.4 us
    ppermute x10, starting transfers between devices, across(): return lax.ppermute(x, 'slab', [(i, i ^ level) for i in range(slabs)])  14.9 us
    unnamed x28, local copies, waits for them, and re-layouts  13.9 us
    pallas_call x1, Pallas kernels, on_device(): sib_t = transpose(swapped)  4.1 us
    pallas_call x1, Pallas kernels, on_device(): own_t = transpose(in_hbm(integrals))  4 us
  transfers between devices with their start and end apart: 28, of which 13 were waited for; matrix products, arithmetic and copies ran while one was open for 3% of the time, Pallas kernels for 20%

profile of v9, /device:TPU:0, one launch (start us, length us, event | category | flops | bytes accessed | tf_op | source)
XLA Modules:
  0.0 151.5 jit_solution(6873687681383433703)
XLA Ops:
  0.5 1.0 slice.24.refs_3_
  1.4 2.6 %collective-permute-start = (bf16[64,2304]{1,0:T(8,128)(2,1)S(1)}, bf16[64,2304]{1,0:T(8,128)(2,1)S(1)}, u32[]{:S(2)}, u32[]{:S(2)}) collective-permute-start(bf16[64,2304]{1,0:T(8,128)(2,1)S(1)} %slice.24.refs_3_), channel_id=1, source_target_pairs={{0,8},{4,12},{8,0},{12,4},{16,24},{20,28},{24,16},{28,20},{1,9},{5... | collective-permute-start | bytes 884744 | tf_op jit(solution)/shard_map/ppermute | solution.py:252
  4.0 1.5 %collective-permute-start.1 = (bf16[64,2304]{1,0:T(8,128)(2,1)S(1)}, bf16[64,2304]{1,0:T(8,128)(2,1)S(1)}, u32[]{:S(2)}, u32[]{:S(2)}) collective-permute-start(bf16[64,2304]{1,0:T(8,128)(2,1)S(1)} %slice.24.refs_3_), channel_id=1, source_target_pairs={{0,16},{4,20},{8,24},{12,28},{16,0},{20,4},{24,8},{28,12},{1,17},{... | collective-permute-start | bytes 884744 | tf_op jit(solution)/shard_map/ppermute | solution.py:252
  9.0 2.6 %collective-permute-done.refs_4_ = bf16[64,2304]{1,0:T(8,128)(2,1)S(1)} collective-permute-done((bf16[64,2304]{1,0:T(8,128)(2,1)S(1)}, bf16[64,2304]{1,0:T(8,128)(2,1)S(1)}, u32[]{:S(2)}, u32[]{:S(2)}) %collective-permute-start) | collective-permute-done | bytes 294944 | tf_op jit(solution)/shard_map/ppermute | solution.py:252
  11.7 1.5 collective-permute-done.1.refs_5_
  13.6 1.8 %collective-permute-start.3 = (bf16[32,2304]{1,0:T(8,128)(2,1)S(1)}, bf16[32,2304]{1,0:T(8,128)(2,1)S(1)}, u32[]{:S(2)}, u32[]{:S(2)}) collective-permute-start(bf16[32,2304]{1,0:T(8,128)(2,1)S(1)} %slice.28), channel_id=1, source_target_pairs={{0,16},{4,20},{8,24},{12,28},{16,0},{20,4},{24,8},{28,12},{1,17},{... | collective-permute-start | bytes 442376 | tf_op jit(solution)/shard_map/ppermute | solution.py:252
  15.4 4.0 %transpose.14.refs_1_.refs_0_ = bf16[1152,2304]{1,0:T(8,128)(2,1)S(1)} custom-call(bf16[2304,1152]{1,0:T(8,128)(2,1)} %in_ref.1), custom_call_target="tpu_custom_call" | custom-call | bytes 10616832 | tf_op jit(solution)/shard_map/transpose/pallas_call | solution.py:426
  19.4 2.3 %copy-done = bf16[1152,2304]{1,0:T(8,128)(2,1)} copy-done((bf16[1152,2304]{1,0:T(8,128)(2,1)}, bf16[1152,2304]{1,0:T(8,128)(2,1)S(1)}, u32[]{:S(2)}) %copy-start) | copy-done | bytes 5308440
  21.8 4.1 %transpose.15.refs_2_.refs_1_ = bf16[1152,2304]{1,0:T(8,128)(2,1)S(1)} custom-call(bf16[2304,1152]{1,0:T(8,128)(2,1)} %collective-permute-done.4.in_ref), custom_call_target="tpu_custom_call" | custom-call | bytes 10616832 | tf_op jit(solution)/shard_map/transpose/pallas_call | solution.py:428
  25.9 2.4 %copy-done.2 = bf16[1152,2304]{1,0:T(8,128)(2,1)} copy-done((bf16[1152,2304]{1,0:T(8,128)(2,1)}, bf16[1152,2304]{1,0:T(8,128)(2,1)S(1)}, u32[]{:S(2)}) %copy-start.2) | copy-done | bytes 5308440
  30.0 1.7 %collective-permute-start.5 = (bf16[128,2304]{1,0:T(8,128)(2,1)S(1)}, bf16[128,2304]{1,0:T(8,128)(2,1)S(1)}, u32[]{:S(2)}, u32[]{:S(2)}) collective-permute-start(bf16[128,2304]{1,0:T(8,128)(2,1)S(1)} %slice.29.refs_2_), channel_id=1, source_target_pairs={{0,8},{4,12},{8,0},{12,4},{16,24},{20,28},{24,16},{28,20},{1,9},{5... | collective-permute-start | bytes 1769480 | tf_op jit(solution)/shard_map/ppermute | solution.py:252
  31.7 2.5 %copy-done.1 = bf16[1152,2304]{1,0:T(8,128)(2,1)S(1)} copy-done((bf16[1152,2304]{1,0:T(8,128)(2,1)S(1)}, bf16[1152,2304]{1,0:T(8,128)(2,1)}, u32[]{:S(2)}) %copy-start.1) | copy-done | bytes 5308440
  34.2 2.5 %copy-done.3 = bf16[1152,2304]{1,0:T(8,128)(2,1)S(1)} copy-done((bf16[1152,2304]{1,0:T(8,128)(2,1)S(1)}, bf16[1152,2304]{1,0:T(8,128)(2,1)}, u32[]{:S(2)}) %copy-start.3) | copy-done | bytes 5308440
  36.7 1.0 copy-done.6
  37.7 0.9 copy-done.8
  38.6 0.9 copy-done.10
  39.5 4.8 %early_ladder.1 = (f32[2,1152,128]{2,1,0:T(8,128)S(1)}, s16[2,4,304,128]{3,2,1,0:T(8,128)(2,1)S(1)}, f32[8,128]{1,0:T(8,128)S(1)}) custom-call(s32[3]{0:T(128)S(1)} %pad_add_fusion.refs_0_, bf16[1152,2304]{1,0:T(8,128)(2,1)S(1)} %copy-done.1, bf16[1152,2304]{1,0:T(8,128)(2,1)S(1)} %copy-done.3, bf16[64,2304]{1,0:T(8,128)(2,1)S(1)} %slice.24.refs_3_, ...), custom_call_target="tpu_custom_call" | custom-call | flops 2717908992 | bytes 13598732 | tf_op jit(solution)/shard_map/early_ladder/pallas_call | solution.py:292
  44.3 1.6 %collective-permute-start.8 = (s16[2,4,304,128]{3,2,1,0:T(8,128)(2,1)S(1)}, s16[2,4,304,128]{3,2,1,0:T(8,128)(2,1)S(1)}, u32[]{:S(2)}, u32[]{:S(2)}) collective-permute-start(s16[2,4,304,128]{3,2,1,0:T(8,128)(2,1)S(1)} %get-tuple-element.77), channel_id=1, source_target_pairs={{0,1},{1,0},{2,3},{3,2},{4,5},{5,4},{6,7},{7,6},{8,9},{9,8},{10,11... | collective-permute-start | bytes 1867784 | tf_op jit(solution)/shard_map/ppermute | solution.py:477
  46.6 1.6 %collective-permute-start.7 = (bf16[64,2304]{1,0:T(8,128)(2,1)S(1)}, bf16[64,2304]{1,0:T(8,128)(2,1)S(1)}, u32[]{:S(2)}, u32[]{:S(2)}) collective-permute-start(bf16[64,2304]{1,0:T(8,128)(2,1)S(1)} %slice.32), channel_id=1, source_target_pairs={{0,16},{4,20},{8,24},{12,28},{16,0},{20,4},{24,8},{28,12},{1,17},{... | collective-permute-start | bytes 884744 | tf_op jit(solution)/shard_map/ppermute | solution.py:252
  48.2 4.8 %collective-permute-done.9.refs_5_ = bf16[64,2304]{1,0:T(8,128)(2,1)S(1)} collective-permute-done((bf16[64,2304]{1,0:T(8,128)(2,1)S(1)}, bf16[64,2304]{1,0:T(8,128)(2,1)S(1)}, u32[]{:S(2)}, u32[]{:S(2)}) %collective-permute-start.9) | collective-permute-done | bytes 294944 | tf_op jit(solution)/shard_map/ppermute | solution.py:252
  53.0 4.2 %ladder.2 = (s16[3,400,128]{2,1,0:T(8,128)(2,1)S(1)}, s16[3,400,128]{2,1,0:T(8,128)(2,1)S(1)}, s16[3,400,128]{2,1,0:T(8,128)(2,1)S(1)}, s16[3,400,128]{2,1,0:T(8,128)(2,1)S(1)}, f32[8,128]{1,0:T(8,128)S(1)}) custom-call(bf16[1152,2304]{1,0:T(8,128)(2,1)S(1)} %bitcast.11, bf16[1152,2304]{1,0:T(8,128)(2,1)S(1)} %copy-done.4, ...), custom_call_target="tpu_custom_call" | custom-call | flops 2717908992 | bytes 13910016 | tf_op jit(solution)/shard_map/ladder/pallas_call | solution.py:292
  57.2 1.3 collective-permute-done.8.refs_1_
  58.8 2.7 %collective-permute-start.16 = (s16[1,4,304,128]{3,2,1,0:T(8,128)(2,1)S(1)}, s16[1,4,304,128]{3,2,1,0:T(8,128)(2,1)S(1)}, u32[]{:S(2)}, u32[]{:S(2)}) collective-permute-start(s16[1,4,304,128]{3,2,1,0:T(8,128)(2,1)S(1)} %get-tuple-element.92), channel_id=1, source_target_pairs={{0,2},{1,3},{2,0},{3,1},{4,6},{5,7},{6,4},{7,5},{8,10},{9,11},{10,... | collective-permute-start | bytes 933896 | tf_op jit(solution)/shard_map/ppermute | solution.py:477
  62.0 1.5 %collective-permute-start.11 = (s16[3,400,128]{2,1,0:T(8,128)(2,1)S(1)}, s16[3,400,128]{2,1,0:T(8,128)(2,1)S(1)}, u32[]{:S(2)}, u32[]{:S(2)}) collective-permute-start(s16[3,400,128]{2,1,0:T(8,128)(2,1)S(1)} %get-tuple-element.86), channel_id=1, source_target_pairs={{0,16},{4,20},{8,24},{12,28},{16,0},{20,4},{24,8},{28,12},{1,17},{... | collective-permute-start | bytes 921608 | tf_op jit(solution)/shard_map/ppermute | solution.py:252
  63.5 1.4 collective-permute-start.12
  64.9 4.2 %ladder.3 = (s16[3,400,128]{2,1,0:T(8,128)(2,1)S(1)}, s16[3,400,128]{2,1,0:T(8,128)(2,1)S(1)}, s16[3,400,128]{2,1,0:T(8,128)(2,1)S(1)}, s16[3,400,128]{2,1,0:T(8,128)(2,1)S(1)}, f32[8,128]{1,0:T(8,128)S(1)}) custom-call(bf16[1152,2304]{1,0:T(8,128)(2,1)S(1)} %bitcast.11, bf16[1152,2304]{1,0:T(8,128)(2,1)S(1)} %copy-done.4, ...), custom_call_target="tpu_custom_call" | custom-call | flops 2717908992 | bytes 13910016 | tf_op jit(solution)/shard_map/ladder/pallas_call | solution.py:292
  69.1 3.9 %collective-permute-done.16.refs_2_ = s16[1,4,304,128]{3,2,1,0:T(8,128)(2,1)S(1)} collective-permute-done((s16[1,4,304,128]{3,2,1,0:T(8,128)(2,1)S(1)}, s16[1,4,304,128]{3,2,1,0:T(8,128)(2,1)S(1)}, u32[]{:S(2)}, u32[]{:S(2)}) %collective-permute-start.16) | collective-permute-done | bytes 311328 | tf_op jit(solution)/shard_map/ppermute | solution.py:477
  73.7 1.5 %collective-permute-done.12.refs_4_ = s16[3,400,128]{2,1,0:T(8,128)(2,1)S(1)} collective-permute-done((s16[3,400,128]{2,1,0:T(8,128)(2,1)S(1)}, s16[3,400,128]{2,1,0:T(8,128)(2,1)S(1)}, u32[]{:S(2)}, u32[]{:S(2)}) %collective-permute-start.12) | collective-permute-done | bytes 307232 | tf_op jit(solution)/shard_map/ppermute | solution.py:252
  75.3 4.7 %antisym.2 = (f32[2,1152,128]{2,1,0:T(8,128)S(1)}, s16[2,3,400,128]{3,2,1,0:T(8,128)(2,1)S(1)}, f32[8,128]{1,0:T(8,128)S(1)}) custom-call(s32[3]{0:T(128)S(1)} %pad_add_fusion.refs_0_, s16[3,400,128]{2,1,0:T(8,128)(2,1)S(1)} %get-tuple-element.98.refs_1_, s16[3,400,128]{2,1,0:T(8,128)(2,1)S(1)} %collective-permute-done.10.refs_2_, ...), custom_call_target="tpu_custom_call" | custom-call | flops 9437184 | bytes 3022860 | tf_op jit(solution)/shard_map/antisym/pallas_call | solution.py:292
  80.0 1.6 %collective-permute-start.20 = (s16[2,3,400,128]{3,2,1,0:T(8,128)(2,1)S(1)}, s16[2,3,400,128]{3,2,1,0:T(8,128)(2,1)S(1)}, u32[]{:S(2)}, u32[]{:S(2)}) collective-permute-start(s16[2,3,400,128]{3,2,1,0:T(8,128)(2,1)S(1)} %get-tuple-element.105), channel_id=1, source_target_pairs={{0,1},{1,0},{2,3},{3,2},{4,5},{5,4},{6,7},{7,6},{8,9},{9,8},{10,11... | collective-permute-start | bytes 1843208 | tf_op jit(solution)/shard_map/ppermute | solution.py:477
  82.4 1.4 collective-permute-start.14
  83.9 1.2 collective-permute-start.15
  85.9 9.8 %collective-permute-done.17.refs_2_ = s16[304,128]{1,0:T(8,128)(2,1)S(1)} collective-permute-done((s16[304,128]{1,0:T(8,128)(2,1)S(1)}, s16[304,128]{1,0:T(8,128)(2,1)S(1)}, u32[]{:S(2)}, u32[]{:S(2)}) %collective-permute-start.17) | collective-permute-done | bytes 77856 | tf_op jit(solution)/shard_map/ppermute | solution.py:252
  95.8 1.6 %collective-permute-start.18 = (s16[304,128]{1,0:T(8,128)(2,1)S(1)}, s16[304,128]{1,0:T(8,128)(2,1)S(1)}, u32[]{:S(2)}, u32[]{:S(2)}) collective-permute-start(s16[304,128]{1,0:T(8,128)(2,1)S(1)} %get-tuple-element.96), channel_id=1, source_target_pairs={{0,16},{4,20},{8,24},{12,28},{16,0},{20,4},{24,8},{28,12},{1,17},{... | collective-permute-start | bytes 233480 | tf_op jit(solution)/shard_map/ppermute | solution.py:252
  97.3 2.8 %collective-permute-done.18.refs_3_ = s16[304,128]{1,0:T(8,128)(2,1)S(1)} collective-permute-done((s16[304,128]{1,0:T(8,128)(2,1)S(1)}, s16[304,128]{1,0:T(8,128)(2,1)S(1)}, u32[]{:S(2)}, u32[]{:S(2)}) %collective-permute-start.18) | collective-permute-done | bytes 77856 | tf_op jit(solution)/shard_map/ppermute | solution.py:252
  100.2 2.5 %collective-permute-start.19 = (s16[304,128]{1,0:T(8,128)(2,1)S(1)}, s16[304,128]{1,0:T(8,128)(2,1)S(1)}, u32[]{:S(2)}, u32[]{:S(2)}) collective-permute-start(s16[304,128]{1,0:T(8,128)(2,1)S(1)} %get-tuple-element.97), channel_id=1, source_target_pairs={{0,24},{4,28},{8,16},{12,20},{16,8},{20,12},{24,0},{28,4},{1,25},{... | collective-permute-start | bytes 233480 | tf_op jit(solution)/shard_map/ppermute | solution.py:252
  102.7 2.8 %collective-permute-done.19.refs_4_ = s16[304,128]{1,0:T(8,128)(2,1)S(1)} collective-permute-done((s16[304,128]{1,0:T(8,128)(2,1)S(1)}, s16[304,128]{1,0:T(8,128)(2,1)S(1)}, u32[]{:S(2)}, u32[]{:S(2)}) %collective-permute-start.19) | collective-permute-done | bytes 77856 | tf_op jit(solution)/shard_map/ppermute | solution.py:252
  105.5 1.1 early_antisym.1
  106.6 4.7 %antisym.3 = (f32[2,1152,128]{2,1,0:T(8,128)S(1)}, s16[1,3,400,128]{3,2,1,0:T(8,128)(2,1)S(1)}, s16[1,3,400,128]{3,2,1,0:T(8,128)(2,1)S(1)}, f32[8,128]{1,0:T(8,128)S(1)}) custom-call(s32[3]{0:T(128)S(1)} %pad_add_fusion.refs_0_, s16[3,400,128]{2,1,0:T(8,128)(2,1)S(1)} %get-tuple-element.88.refs_1_, s16[3,400,128]{2,1,0:T(8,128)(2,1)S(1)} %collective-permute-done.13.refs_2_, ...), custom_call_target="tpu_custom_call" | custom-call | flops 9437184 | bytes 3022860 | tf_op jit(solution)/shard_map/antisym/pallas_call | solution.py:292
  111.8 1.6 %collective-permute-start.23 = (s16[304,128]{1,0:T(8,128)(2,1)S(1)}, s16[304,128]{1,0:T(8,128)(2,1)S(1)}, u32[]{:S(2)}, u32[]{:S(2)}) collective-permute-start(s16[304,128]{1,0:T(8,128)(2,1)S(1)} %get-tuple-element.109), channel_id=1, source_target_pairs={{0,1},{1,0},{2,3},{3,2},{4,5},{5,4},{6,7},{7,6},{8,9},{9,8},{10,11... | collective-permute-start | bytes 233480 | tf_op jit(solution)/shard_map/ppermute | solution.py:477
  113.4 3.4 %collective-permute-start.24 = (s16[304,128]{1,0:T(8,128)(2,1)S(1)}, s16[304,128]{1,0:T(8,128)(2,1)S(1)}, u32[]{:S(2)}, u32[]{:S(2)}) collective-permute-start(s16[304,128]{1,0:T(8,128)(2,1)S(1)} %get-tuple-element.110), channel_id=1, source_target_pairs={{0,2},{1,3},{2,0},{3,1},{4,6},{5,7},{6,4},{7,5},{8,10},{9,11},{10,... | collective-permute-start | bytes 233480 | tf_op jit(solution)/shard_map/ppermute | solution.py:477
  117.6 11.9 %collective-permute-done.23.refs_3_ = s16[304,128]{1,0:T(8,128)(2,1)S(1)} collective-permute-done((s16[304,128]{1,0:T(8,128)(2,1)S(1)}, s16[304,128]{1,0:T(8,128)(2,1)S(1)}, u32[]{:S(2)}, u32[]{:S(2)}) %collective-permute-start.23) | collective-permute-done | bytes 77856 | tf_op jit(solution)/shard_map/ppermute | solution.py:477
  129.5 2.3 %collective-permute-start.27 = (s16[1,3,400,128]{3,2,1,0:T(8,128)(2,1)S(1)}, s16[1,3,400,128]{3,2,1,0:T(8,128)(2,1)S(1)}, u32[]{:S(2)}, u32[]{:S(2)}) collective-permute-start(s16[1,3,400,128]{3,2,1,0:T(8,128)(2,1)S(1)} %get-tuple-element.117), channel_id=1, source_target_pairs={{0,2},{1,3},{2,0},{3,1},{4,6},{5,7},{6,4},{7,5},{8,10},{9,11},{10,... | collective-permute-start | bytes 921608 | tf_op jit(solution)/shard_map/ppermute | solution.py:477
  131.8 1.4 finish.3
  134.0 12.7 %collective-permute-done.27.refs_4_ = s16[1,3,400,128]{3,2,1,0:T(8,128)(2,1)S(1)} collective-permute-done((s16[1,3,400,128]{3,2,1,0:T(8,128)(2,1)S(1)}, s16[1,3,400,128]{3,2,1,0:T(8,128)(2,1)S(1)}, u32[]{:S(2)}, u32[]{:S(2)}) %collective-permute-start.27) | collective-permute-done | bytes 307232 | tf_op jit(solution)/shard_map/ppermute | solution.py:477
  146.8 1.4 finish.4
  148.2 1.9 %collective-permute-done.26.refs_4_ = s16[1,3,400,128]{3,2,1,0:T(8,128)(2,1)S(1)} collective-permute-done((s16[1,3,400,128]{3,2,1,0:T(8,128)(2,1)S(1)}, s16[1,3,400,128]{3,2,1,0:T(8,128)(2,1)S(1)}, u32[]{:S(2)}, u32[]{:S(2)}) %collective-permute-start.26) | collective-permute-done | bytes 307232 | tf_op jit(solution)/shard_map/ppermute | solution.py:477
  150.1 1.4 finish.5
  (71 shorter events, 12.2 us)
Async XLA Ops:
  0.0 21.8 %collective-permute-start.4 = (bf16[2304,1152]{1,0:T(8,128)(2,1)}, bf16[2304,1152]{1,0:T(8,128)(2,1)}, u32[]{:S(2)}, u32[]{:S(2)}) collective-permute-start(bf16[2304,1152]{1,0:T(8,128)(2,1)} %in_ref.1), channel_id=1, source_target_pairs={{0,4},{4,0},{8,12},{12,8},{16,20},{20,16},{24,28},{28,24},{1,5},{5... | collective-permute-start | bytes 15925256 | tf_op jit(solution)/shard_map/ppermute | solution.py:427
  1.4 10.2 %collective-permute-start = (bf16[64,2304]{1,0:T(8,128)(2,1)S(1)}, bf16[64,2304]{1,0:T(8,128)(2,1)S(1)}, u32[]{:S(2)}, u32[]{:S(2)}) collective-permute-start(bf16[64,2304]{1,0:T(8,128)(2,1)S(1)} %slice.24.refs_3_), channel_id=1, source_target_pairs={{0,8},{4,12},{8,0},{12,4},{16,24},{20,28},{24,16},{28,20},{1,9},{5... | collective-permute-start | bytes 884744 | tf_op jit(solution)/shard_map/ppermute | solution.py:252
  4.0 9.1 %collective-permute-start.1 = (bf16[64,2304]{1,0:T(8,128)(2,1)S(1)}, bf16[64,2304]{1,0:T(8,128)(2,1)S(1)}, u32[]{:S(2)}, u32[]{:S(2)}) collective-permute-start(bf16[64,2304]{1,0:T(8,128)(2,1)S(1)} %slice.24.refs_3_), channel_id=1, source_target_pairs={{0,16},{4,20},{8,24},{12,28},{16,0},{20,4},{24,8},{28,12},{1,17},{... | collective-permute-start | bytes 884744 | tf_op jit(solution)/shard_map/ppermute | solution.py:252
  13.1 6.2 %copy-start.5 = (bf16[64,2304]{1,0:T(8,128)(2,1)}, bf16[64,2304]{1,0:T(8,128)(2,1)S(1)}, u32[]{:S(2)}) copy-start(bf16[64,2304]{1,0:T(8,128)(2,1)S(1)} %collective-permute-done.1.refs_5_) | copy-start | bytes 884740
  13.1 15.2 %collective-permute-start.2 = (bf16[32,2304]{1,0:T(8,128)(2,1)S(1)}, bf16[32,2304]{1,0:T(8,128)(2,1)S(1)}, u32[]{:S(2)}, u32[]{:S(2)}) collective-permute-start(bf16[32,2304]{1,0:T(8,128)(2,1)S(1)} %slice.27), channel_id=1, source_target_pairs={{0,8},{4,12},{8,0},{12,4},{16,24},{20,28},{24,16},{28,20},{1,9},{5... | collective-permute-start | bytes 442376 | tf_op jit(solution)/shard_map/ppermute | solution.py:252
  13.6 8.1 %copy-start.11 = (bf16[192,2304]{1,0:T(8,128)(2,1)S(1)}, bf16[192,2304]{1,0:T(8,128)(2,1)}, u32[]{:S(2)}) copy-start(bf16[192,2304]{1,0:T(8,128)(2,1)} %param.5) | copy-start | bytes 2654212
  13.6 15.4 %collective-permute-start.3 = (bf16[32,2304]{1,0:T(8,128)(2,1)S(1)}, bf16[32,2304]{1,0:T(8,128)(2,1)S(1)}, u32[]{:S(2)}, u32[]{:S(2)}) collective-permute-start(bf16[32,2304]{1,0:T(8,128)(2,1)S(1)} %slice.28), channel_id=1, source_target_pairs={{0,16},{4,20},{8,24},{12,28},{16,0},{20,4},{24,8},{28,12},{1,17},{... | collective-permute-start | bytes 442376 | tf_op jit(solution)/shard_map/ppermute | solution.py:252
  19.4 2.3 %copy-start = (bf16[1152,2304]{1,0:T(8,128)(2,1)}, bf16[1152,2304]{1,0:T(8,128)(2,1)S(1)}, u32[]{:S(2)}) copy-start(bf16[1152,2304]{1,0:T(8,128)(2,1)S(1)} %transpose.14.refs_1_.refs_0_) | copy-start | bytes 15925252
  21.8 31.2 %slice-start = ((s8[5308416]{0:T(1024)(128)(4,1)}), s8[1114112]{0:T(1024)(128)(4,1)S(1)}, s32[]{:S(2)}) async-start(s8[5308416]{0:T(1024)(128)(4,1)} %bitcast.10), calls=%async_computation | async-start | bytes 2228224
  25.9 2.4 %copy-start.2 = (bf16[1152,2304]{1,0:T(8,128)(2,1)}, bf16[1152,2304]{1,0:T(8,128)(2,1)S(1)}, u32[]{:S(2)}) copy-start(bf16[1152,2304]{1,0:T(8,128)(2,1)S(1)} %transpose.15.refs_2_.refs_1_) | copy-start | bytes 15925252
  28.3 0.7 copy-start.7
  29.0 0.7 copy-start.9
  29.6 16.3 %collective-permute-start.6 = (bf16[128,2304]{1,0:T(8,128)(2,1)S(1)}, bf16[128,2304]{1,0:T(8,128)(2,1)S(1)}, u32[]{:S(2)}, u32[]{:S(2)}) collective-permute-start(bf16[128,2304]{1,0:T(8,128)(2,1)S(1)} %slice.29.refs_2_), channel_id=1, source_target_pairs={{0,16},{4,20},{8,24},{12,28},{16,0},{20,4},{24,8},{28,12},{1,17},{... | collective-permute-start | bytes 1769480 | tf_op jit(solution)/shard_map/ppermute | solution.py:252
  30.0 16.5 %collective-permute-start.5 = (bf16[128,2304]{1,0:T(8,128)(2,1)S(1)}, bf16[128,2304]{1,0:T(8,128)(2,1)S(1)}, u32[]{:S(2)}, u32[]{:S(2)}) collective-permute-start(bf16[128,2304]{1,0:T(8,128)(2,1)S(1)} %slice.29.refs_2_), channel_id=1, source_target_pairs={{0,8},{4,12},{8,0},{12,4},{16,24},{20,28},{24,16},{28,20},{1,9},{5... | collective-permute-start | bytes 1769480 | tf_op jit(solution)/shard_map/ppermute | solution.py:252
  31.7 2.5 %copy-start.1 = (bf16[1152,2304]{1,0:T(8,128)(2,1)S(1)}, bf16[1152,2304]{1,0:T(8,128)(2,1)}, u32[]{:S(2)}) copy-start(bf16[1152,2304]{1,0:T(8,128)(2,1)} %copy-done) | copy-start | bytes 15925252
  34.2 2.5 %copy-start.3 = (bf16[1152,2304]{1,0:T(8,128)(2,1)S(1)}, bf16[1152,2304]{1,0:T(8,128)(2,1)}, u32[]{:S(2)}) copy-start(bf16[1152,2304]{1,0:T(8,128)(2,1)} %copy-done.2) | copy-start | bytes 15925252
  36.7 1.0 copy-start.6
  37.7 0.9 copy-start.8
  38.6 0.9 copy-start.10
  39.5 13.5 %slice-start.1 = ((s8[5308416]{0:T(1024)(128)(4,1)}), s8[4194304]{0:T(1024)(128)(4,1)S(1)}, s32[]{:S(2)}) async-start(s8[5308416]{0:T(1024)(128)(4,1)} %bitcast.10), calls=%async_computation.1 | async-start | bytes 8388608
  39.5 13.5 %copy-start.4 = (bf16[1152,2304]{1,0:T(8,128)(2,1)S(1)}, bf16[1152,2304]{1,0:T(8,128)(2,1)}, u32[]{:S(2)}) copy-start(bf16[1152,2304]{1,0:T(8,128)(2,1)} %copy-done.2) | copy-start | bytes 15925252
  44.3 14.3 %collective-permute-start.8 = (s16[2,4,304,128]{3,2,1,0:T(8,128)(2,1)S(1)}, s16[2,4,304,128]{3,2,1,0:T(8,128)(2,1)S(1)}, u32[]{:S(2)}, u32[]{:S(2)}) collective-permute-start(s16[2,4,304,128]{3,2,1,0:T(8,128)(2,1)S(1)} %get-tuple-element.77), channel_id=1, source_target_pairs={{0,1},{1,0},{2,3},{3,2},{4,5},{5,4},{6,7},{7,6},{8,9},{9,8},{10,11... | collective-permute-start | bytes 1867784 | tf_op jit(solution)/shard_map/ppermute | solution.py:477
  46.0 7.0 %collective-permute-start.9 = (bf16[64,2304]{1,0:T(8,128)(2,1)S(1)}, bf16[64,2304]{1,0:T(8,128)(2,1)S(1)}, u32[]{:S(2)}, u32[]{:S(2)}) collective-permute-start(bf16[64,2304]{1,0:T(8,128)(2,1)S(1)} %slice.33), channel_id=1, source_target_pairs={{0,8},{4,12},{8,0},{12,4},{16,24},{20,28},{24,16},{28,20},{1,9},{5... | collective-permute-start | bytes 884744 | tf_op jit(solution)/shard_map/ppermute | solution.py:252
  46.6 18.3 %collective-permute-start.7 = (bf16[64,2304]{1,0:T(8,128)(2,1)S(1)}, bf16[64,2304]{1,0:T(8,128)(2,1)S(1)}, u32[]{:S(2)}, u32[]{:S(2)}) collective-permute-start(bf16[64,2304]{1,0:T(8,128)(2,1)S(1)} %slice.32), channel_id=1, source_target_pairs={{0,16},{4,20},{8,24},{12,28},{16,0},{20,4},{24,8},{28,12},{1,17},{... | collective-permute-start | bytes 884744 | tf_op jit(solution)/shard_map/ppermute | solution.py:252
  58.8 14.2 %collective-permute-start.16 = (s16[1,4,304,128]{3,2,1,0:T(8,128)(2,1)S(1)}, s16[1,4,304,128]{3,2,1,0:T(8,128)(2,1)S(1)}, u32[]{:S(2)}, u32[]{:S(2)}) collective-permute-start(s16[1,4,304,128]{3,2,1,0:T(8,128)(2,1)S(1)} %get-tuple-element.92), channel_id=1, source_target_pairs={{0,2},{1,3},{2,0},{3,1},{4,6},{5,7},{6,4},{7,5},{8,10},{9,11},{10,... | collective-permute-start | bytes 933896 | tf_op jit(solution)/shard_map/ppermute | solution.py:477
  61.4 11.9 %collective-permute-start.10 = (s16[3,400,128]{2,1,0:T(8,128)(2,1)S(1)}, s16[3,400,128]{2,1,0:T(8,128)(2,1)S(1)}, u32[]{:S(2)}, u32[]{:S(2)}) collective-permute-start(s16[3,400,128]{2,1,0:T(8,128)(2,1)S(1)} %get-tuple-element.85), channel_id=1, source_target_pairs={{0,8},{4,12},{8,0},{12,4},{16,24},{20,28},{24,16},{28,20},{1,9},{5... | collective-permute-start | bytes 921608 | tf_op jit(solution)/shard_map/ppermute | solution.py:252
  62.0 11.7 %collective-permute-start.11 = (s16[3,400,128]{2,1,0:T(8,128)(2,1)S(1)}, s16[3,400,128]{2,1,0:T(8,128)(2,1)S(1)}, u32[]{:S(2)}, u32[]{:S(2)}) collective-permute-start(s16[3,400,128]{2,1,0:T(8,128)(2,1)S(1)} %get-tuple-element.86), channel_id=1, source_target_pairs={{0,16},{4,20},{8,24},{12,28},{16,0},{20,4},{24,8},{28,12},{1,17},{... | collective-permute-start | bytes 921608 | tf_op jit(solution)/shard_map/ppermute | solution.py:252
  63.5 11.7 %collective-permute-start.12 = (s16[3,400,128]{2,1,0:T(8,128)(2,1)S(1)}, s16[3,400,128]{2,1,0:T(8,128)(2,1)S(1)}, u32[]{:S(2)}, u32[]{:S(2)}) collective-permute-start(s16[3,400,128]{2,1,0:T(8,128)(2,1)S(1)} %get-tuple-element.87), channel_id=1, source_target_pairs={{0,24},{4,28},{8,16},{12,20},{16,8},{20,12},{24,0},{28,4},{1,25},{... | collective-permute-start | bytes 921608 | tf_op jit(solution)/shard_map/ppermute | solution.py:252
  80.0 31.4 %collective-permute-start.20 = (s16[2,3,400,128]{3,2,1,0:T(8,128)(2,1)S(1)}, s16[2,3,400,128]{3,2,1,0:T(8,128)(2,1)S(1)}, u32[]{:S(2)}, u32[]{:S(2)}) collective-permute-start(s16[2,3,400,128]{3,2,1,0:T(8,128)(2,1)S(1)} %get-tuple-element.105), channel_id=1, source_target_pairs={{0,1},{1,0},{2,3},{3,2},{4,5},{5,4},{6,7},{7,6},{8,9},{9,8},{10,11... | collective-permute-start | bytes 1843208 | tf_op jit(solution)/shard_map/ppermute | solution.py:477
  81.6 25.0 %collective-permute-start.13 = (s16[3,400,128]{2,1,0:T(8,128)(2,1)S(1)}, s16[3,400,128]{2,1,0:T(8,128)(2,1)S(1)}, u32[]{:S(2)}, u32[]{:S(2)}) collective-permute-start(s16[3,400,128]{2,1,0:T(8,128)(2,1)S(1)} %get-tuple-element.89), channel_id=1, source_target_pairs={{0,8},{4,12},{8,0},{12,4},{16,24},{20,28},{24,16},{28,20},{1,9},{5... | collective-permute-start | bytes 921608 | tf_op jit(solution)/shard_map/ppermute | solution.py:252
  82.4 24.1 %collective-permute-start.14 = (s16[3,400,128]{2,1,0:T(8,128)(2,1)S(1)}, s16[3,400,128]{2,1,0:T(8,128)(2,1)S(1)}, u32[]{:S(2)}, u32[]{:S(2)}) collective-permute-start(s16[3,400,128]{2,1,0:T(8,128)(2,1)S(1)} %get-tuple-element.90), channel_id=1, source_target_pairs={{0,16},{4,20},{8,24},{12,28},{16,0},{20,4},{24,8},{28,12},{1,17},{... | collective-permute-start | bytes 921608 | tf_op jit(solution)/shard_map/ppermute | solution.py:252
  83.9 22.7 %collective-permute-start.15 = (s16[3,400,128]{2,1,0:T(8,128)(2,1)S(1)}, s16[3,400,128]{2,1,0:T(8,128)(2,1)S(1)}, u32[]{:S(2)}, u32[]{:S(2)}) collective-permute-start(s16[3,400,128]{2,1,0:T(8,128)(2,1)S(1)} %get-tuple-element.91), channel_id=1, source_target_pairs={{0,24},{4,28},{8,16},{12,20},{16,8},{20,12},{24,0},{28,4},{1,25},{... | collective-permute-start | bytes 921608 | tf_op jit(solution)/shard_map/ppermute | solution.py:252
  85.0 10.7 %collective-permute-start.17 = (s16[304,128]{1,0:T(8,128)(2,1)S(1)}, s16[304,128]{1,0:T(8,128)(2,1)S(1)}, u32[]{:S(2)}, u32[]{:S(2)}) collective-permute-start(s16[304,128]{1,0:T(8,128)(2,1)S(1)} %get-tuple-element.95), channel_id=1, source_target_pairs={{0,8},{4,12},{8,0},{12,4},{16,24},{20,28},{24,16},{28,20},{1,9},{5... | collective-permute-start | bytes 233480 | tf_op jit(solution)/shard_map/ppermute | solution.py:252
  95.8 4.4 %collective-permute-start.18 = (s16[304,128]{1,0:T(8,128)(2,1)S(1)}, s16[304,128]{1,0:T(8,128)(2,1)S(1)}, u32[]{:S(2)}, u32[]{:S(2)}) collective-permute-start(s16[304,128]{1,0:T(8,128)(2,1)S(1)} %get-tuple-element.96), channel_id=1, source_target_pairs={{0,16},{4,20},{8,24},{12,28},{16,0},{20,4},{24,8},{28,12},{1,17},{... | collective-permute-start | bytes 233480 | tf_op jit(solution)/shard_map/ppermute | solution.py:252
  100.2 5.3 %collective-permute-start.19 = (s16[304,128]{1,0:T(8,128)(2,1)S(1)}, s16[304,128]{1,0:T(8,128)(2,1)S(1)}, u32[]{:S(2)}, u32[]{:S(2)}) collective-permute-start(s16[304,128]{1,0:T(8,128)(2,1)S(1)} %get-tuple-element.97), channel_id=1, source_target_pairs={{0,24},{4,28},{8,16},{12,20},{16,8},{20,12},{24,0},{28,4},{1,25},{... | collective-permute-start | bytes 233480 | tf_op jit(solution)/shard_map/ppermute | solution.py:252
  111.3 21.8 %collective-permute-start.22 = (s16[1,3,400,128]{3,2,1,0:T(8,128)(2,1)S(1)}, s16[1,3,400,128]{3,2,1,0:T(8,128)(2,1)S(1)}, u32[]{:S(2)}, u32[]{:S(2)}) collective-permute-start(s16[1,3,400,128]{3,2,1,0:T(8,128)(2,1)S(1)} %get-tuple-element.107), channel_id=1, source_target_pairs={{0,1},{1,0},{2,3},{3,2},{4,5},{5,4},{6,7},{7,6},{8,9},{9,8},{10,11... | collective-permute-start | bytes 921608 | tf_op jit(solution)/shard_map/ppermute | solution.py:477
  111.8 17.7 %collective-permute-start.23 = (s16[304,128]{1,0:T(8,128)(2,1)S(1)}, s16[304,128]{1,0:T(8,128)(2,1)S(1)}, u32[]{:S(2)}, u32[]{:S(2)}) collective-permute-start(s16[304,128]{1,0:T(8,128)(2,1)S(1)} %get-tuple-element.109), channel_id=1, source_target_pairs={{0,1},{1,0},{2,3},{3,2},{4,5},{5,4},{6,7},{7,6},{8,9},{9,8},{10,11... | collective-permute-start | bytes 233480 | tf_op jit(solution)/shard_map/ppermute | solution.py:477
  113.4 18.4 %collective-permute-start.24 = (s16[304,128]{1,0:T(8,128)(2,1)S(1)}, s16[304,128]{1,0:T(8,128)(2,1)S(1)}, u32[]{:S(2)}, u32[]{:S(2)}) collective-permute-start(s16[304,128]{1,0:T(8,128)(2,1)S(1)} %get-tuple-element.110), channel_id=1, source_target_pairs={{0,2},{1,3},{2,0},{3,1},{4,6},{5,7},{6,4},{7,5},{8,10},{9,11},{10,... | collective-permute-start | bytes 233480 | tf_op jit(solution)/shard_map/ppermute | solution.py:477
  116.8 15.0 %collective-permute-start.25 = (s16[304,128]{1,0:T(8,128)(2,1)S(1)}, s16[304,128]{1,0:T(8,128)(2,1)S(1)}, u32[]{:S(2)}, u32[]{:S(2)}) collective-permute-start(s16[304,128]{1,0:T(8,128)(2,1)S(1)} %get-tuple-element.111), channel_id=1, source_target_pairs={{0,3},{1,2},{2,1},{3,0},{4,7},{5,6},{6,5},{7,4},{8,11},{9,10},{10,... | collective-permute-start | bytes 233480 | tf_op jit(solution)/shard_map/ppermute | solution.py:477
  116.8 31.3 %collective-permute-start.21 = (s16[1,3,400,128]{3,2,1,0:T(8,128)(2,1)S(1)}, s16[1,3,400,128]{3,2,1,0:T(8,128)(2,1)S(1)}, u32[]{:S(2)}, u32[]{:S(2)}) collective-permute-start(s16[1,3,400,128]{3,2,1,0:T(8,128)(2,1)S(1)} %get-tuple-element.106), channel_id=1, source_target_pairs={{0,1},{1,0},{2,3},{3,2},{4,5},{5,4},{6,7},{7,6},{8,9},{9,8},{10,11... | collective-permute-start | bytes 921608 | tf_op jit(solution)/shard_map/ppermute | solution.py:477
  129.5 17.3 %collective-permute-start.27 = (s16[1,3,400,128]{3,2,1,0:T(8,128)(2,1)S(1)}, s16[1,3,400,128]{3,2,1,0:T(8,128)(2,1)S(1)}, u32[]{:S(2)}, u32[]{:S(2)}) collective-permute-start(s16[1,3,400,128]{3,2,1,0:T(8,128)(2,1)S(1)} %get-tuple-element.117), channel_id=1, source_target_pairs={{0,2},{1,3},{2,0},{3,1},{4,6},{5,7},{6,4},{7,5},{8,10},{9,11},{10,... | collective-permute-start | bytes 921608 | tf_op jit(solution)/shard_map/ppermute | solution.py:477
  133.3 16.7 %collective-permute-start.26 = (s16[1,3,400,128]{3,2,1,0:T(8,128)(2,1)S(1)}, s16[1,3,400,128]{3,2,1,0:T(8,128)(2,1)S(1)}, u32[]{:S(2)}, u32[]{:S(2)}) collective-permute-start(s16[1,3,400,128]{3,2,1,0:T(8,128)(2,1)S(1)} %get-tuple-element.116), channel_id=1, source_target_pairs={{0,2},{1,3},{2,0},{3,1},{4,6},{5,7},{6,4},{7,5},{8,10},{9,11},{10,... | collective-permute-start | bytes 921608 | tf_op jit(solution)/shard_map/ppermute | solution.py:477

commit v10 on v9

--- a/solution.py
+++ b/solution.py
@@ -111,9 +111,9 @@
 
 
 def sum_kernel(places, count, parts, *refs):
-    got, outs = refs[:count], refs[count:]
-    group = outs[0].shape[0] - TAIL
-    for d, out in enumerate(outs):
+    got, (own, pair, single) = refs[:count], refs[count:]
+    group = own.shape[0] - TAIL
+    for d, out in enumerate((own, pair.at[0], single.at[0], pair.at[1])):
         total = parts[0, pl.ds(d * group, group), :]
         for k, slot in places:
             total = total + decode(got[k].at[slot, d])
@@ -121,8 +121,9 @@
 
 
 def early_antisym_kernel(chips, side, place_ref, *refs):
-    arrived, own, outs = refs[:chips], refs[chips], refs[chips + 1 : 2 * chips]
-    cube, sent = refs[2 * chips :]
+    mine, pair_in, single_in, own, pair, single, cube, sent = refs
+    arrived = (mine, pair_in.at[0], single_in.at[0], single_in.at[1])
+    outs = (None, pair.at[0], single.at[0], pair.at[1])
     chip, core, z = place_ref[0], place_ref[1], place_ref[2]
     group = own.shape[0]
     size, held = CORES * group, side // CORES
@@ -147,11 +148,11 @@
             upper = other - cube[pl.ds(that + b, side, stride=side), :]
             out[pl.ds(a * side, side), :] = jnp.where(low, lower, upper)
         if e:
-            encode(sent[...], outs[e - 1])
-
-
-def early_finish_kernel(chips, side, pair_ref, vir_ref, own, *refs):
-    got, (out_ref, cube) = refs[: chips - 1], refs[-2:]
+            encode(sent[...], outs[e])
+
+
+def early_finish_kernel(chips, side, pair_ref, vir_ref, own, pair, single, *refs):
+    got, (out_ref, cube) = (pair.at[0], single.at[0], single.at[1]), refs[-2:]
     group, rows = own.shape[0], cube.shape[0]
     for e in range(chips):
         values = decode(got[e - 1]) if e else own[...]
@@ -317,9 +318,11 @@
             name="ladder",
         )
 
-    early = chips == slabs and chips >= 4 and tile % vir == 0 and vir // chips % 8 == 0
+    early = chips == slabs == 4 and tile % vir == 0 and vir // chips % 8 == 0
     side, group = vir // chips, rows // chips
-    small = jax.ShapeDtypeStruct((group + TAIL, LANES), jnp.int16)
+    small, single, pair = (
+        jax.ShapeDtypeStruct((*lead, group + TAIL, LANES), jnp.int16) for lead in ((), (1,), (2,))
+    )
     grouped = (chips // 2, chips * group, LANES)
 
     def early_ladder(gathered):
@@ -349,8 +352,8 @@
             8 * chips * group * LANES,
             [parts, *got],
             [vmem] * (1 + len(got)),
-            [vmem] * chips,
-            [small] * chips,
+            [vmem] * 3,
+            [small, pair, single],
             8,
             name="early_sum",
         )
@@ -360,9 +363,9 @@
             functools.partial(early_antisym_kernel, chips, side),
             8 * vir * side * LANES,
             [place, *arrived],
-            [smem] + [vmem] * chips,
-            [vmem] * chips,
-            [jax.ShapeDtypeStruct((group, LANES), jnp.float32)] + [small] * (chips - 1),
+            [smem] + [vmem] * 3,
+            [vmem] * 3,
+            [jax.ShapeDtypeStruct((group, LANES), jnp.float32), pair, single],
             12,
             [
                 pltpu.VMEM((chips * side * side, LANES), jnp.float32),
@@ -450,8 +453,12 @@
         return [[mine], [one], [two], [low, high]], beside
 
     if early:
-        head, (eps_pair, eps_virt) = gather(amplitudes[:WIDTH], (eps_pair, eps_virt))
-        (head, own_t, sib_t, rest) = lax.optimization_barrier((head, own_t, sib_t, amplitudes[WIDTH:]))
+        head, (own_t, eps_pair, eps_virt) = gather(
+            amplitudes[:WIDTH], (own_t, eps_pair, eps_virt)
+        )
+        head, own_t, sib_t, rest = lax.optimization_barrier(
+            (head, own_t, sib_t, amplitudes[WIDTH:])
+        )
         tail, _ = gather(rest, ())
         gathered = [(0, head), (WIDTH, tail)]
     else:
@@ -500,14 +507,18 @@
         got, ((_, places),) = listed([0])
         return got, places
 
+    def by_steps(move, pair, single):
+        first = move(pair, 1)
+        return [first, move(jnp.concatenate([single, first[1:]]), 2)]
+
     def early_stages(r):
         parts, away = yield early_ladder(rows_of(r))
         got, places = yield from halved(parts, [across(away, 1)])
-        sums = yield early_sum(places, parts, got)
-        arrived = [sums[0]] + [to_chip(sums[d], d) for d in range(1, chips)]
-        own, *blocks = yield early_antisym(arrived)
-        got = [across(x, e + 1) for e, x in enumerate(blocks)]
-        yield finish(r, own, got, None, update)
+        mine, *sums = yield early_sum(places, parts, got)
+        arrived = by_steps(to_chip, *sums)
+        turns.append(turns[-1] + arrived)
+        own, *blocks = yield early_antisym([mine, *arrived])
+        yield finish(r, own, by_steps(across, *blocks), None, update)
 
     def stages(r):
         sums = yield ladder(rows_of(r))
@@ -529,7 +540,7 @@
     def when(stage):
         r, k = stage
         if early and r == 0:
-            return (20, *[46] * hops, 54, 66, 83)[k]
+            return (20, *[41] * hops, 54, 66, 83)[k]
         if k == 0:
             return 37 + 5 * r if early else 30 + 5 * r
         return 15 * r + (45 if early else 54) + (k - 1) * 17 - (1 if k == 2 + hops else 0)

time: 152 us -> 127 us (0.84)
  local copies, waits for them, and re-layouts: 17.4 us -> 5.14 us
  starting transfers between devices: 37.8 us -> 31 us
  waiting for transfers between devices: 58.1 us -> 52.5 us
    unnamed x28 -> x14, local copies, waits for them, and re-layouts: 13.9 us -> 2.38 us
    ppermute x10 -> x9, waiting for transfers between devices: 31.8 us -> 24.6 us  [across(): return lax.ppermute(x, 'slab', [(i, i ^ level) for i in range(slabs)])]
    ppermute x17 -> x16, starting transfers between devices: 22.4 us -> 18.9 us  [to_chip(): return lax.ppermute(x, 'pair', [(i, i ^ d * CORES) for i in range(devices)])]
    ppermute x10 -> x9, starting transfers between devices: 14.9 us -> 11.7 us  [across(): return lax.ppermute(x, 'slab', [(i, i ^ level) for i in range(slabs)])]
    ppermute x17 -> x16, waiting for transfers between devices: 26.3 us -> 27.9 us  [to_chip(): return lax.ppermute(x, 'pair', [(i, i ^ d * CORES) for i in range(devices)])]
  transfers between devices with their start and end apart: 28 -> 26, of which waited for: 13 -> 12; matrix products, arithmetic and copies ran while one was open for 3% -> 3% of each run, Pallas kernels for 20% -> 28%
where the time goes in v10:
time: 127 us
  waiting for transfers between devices  52.5 us (41%)
  Pallas kernels  37.4 us (29%)
  starting transfers between devices  31 us (24%)
  local copies, waits for them, and re-layouts  5.14 us (4%)
    pallas_call x13, Pallas kernels, call(): pl.pallas_call(kernel, in_specs=[*in_specs, vmem], out_specs=[*out_specs,...  28.7 us
    ppermute x16, waiting for transfers between devices, to_chip(): return lax.ppermute(x, 'pair', [(i, i ^ d * CORES) for i in range(devices)])  27.9 us
    ppermute x9, waiting for transfers between devices, across(): return lax.ppermute(x, 'slab', [(i, i ^ level) for i in range(slabs)])  24.6 us
    ppermute x16, starting transfers between devices, to_chip(): return lax.ppermute(x, 'pair', [(i, i ^ d * CORES) for i in range(devices)])  18.9 us
    ppermute x9, starting transfers between devices, across(): return lax.ppermute(x, 'slab', [(i, i ^ level) for i in range(slabs)])  11.7 us
    pallas_call x1, Pallas kernels, on_device(): sib_t = transpose(swapped)  4.65 us
    pallas_call x1, Pallas kernels, on_device(): own_t = transpose(in_hbm(integrals))  4 us
  transfers between devices with their start and end apart: 26, of which 12 were waited for; matrix products, arithmetic and copies ran while one was open for 3% of the time, Pallas kernels for 28%

profile of v10, /device:TPU:0, one launch (start us, length us, event | category | flops | bytes accessed | tf_op | source)
XLA Modules:
  0.0 126.8 jit_solution(2564755112802069332)
XLA Ops:
  0.5 1.0 slice.30.refs_3_
  1.5 2.6 %collective-permute-start = (bf16[64,2304]{1,0:T(8,128)(2,1)S(1)}, bf16[64,2304]{1,0:T(8,128)(2,1)S(1)}, u32[]{:S(2)}, u32[]{:S(2)}) collective-permute-start(bf16[64,2304]{1,0:T(8,128)(2,1)S(1)} %slice.30.refs_3_), channel_id=1, source_target_pairs={{0,8},{4,12},{8,0},{12,4},{16,24},{20,28},{24,16},{28,20},{1,9},{5... | collective-permute-start | bytes 884744 | tf_op jit(solution)/shard_map/ppermute | solution.py:253
  4.0 1.5 %collective-permute-start.1 = (bf16[64,2304]{1,0:T(8,128)(2,1)S(1)}, bf16[64,2304]{1,0:T(8,128)(2,1)S(1)}, u32[]{:S(2)}, u32[]{:S(2)}) collective-permute-start(bf16[64,2304]{1,0:T(8,128)(2,1)S(1)} %slice.30.refs_3_), channel_id=1, source_target_pairs={{0,16},{4,20},{8,24},{12,28},{16,0},{20,4},{24,8},{28,12},{1,17},{... | collective-permute-start | bytes 884744 | tf_op jit(solution)/shard_map/ppermute | solution.py:253
  5.6 4.0 %transpose.14.refs_1_.refs_0_ = bf16[1152,2304]{1,0:T(8,128)(2,1)S(1)} custom-call(bf16[2304,1152]{1,0:T(8,128)(2,1)} %in_ref.1), custom_call_target="tpu_custom_call" | custom-call | bytes 10616832 | tf_op jit(solution)/shard_map/transpose/pallas_call | solution.py:429
  9.6 2.3 %copy-done = bf16[1152,2304]{1,0:T(8,128)(2,1)} copy-done((bf16[1152,2304]{1,0:T(8,128)(2,1)}, bf16[1152,2304]{1,0:T(8,128)(2,1)S(1)}, u32[]{:S(2)}) %copy-start) | copy-done | bytes 5308440
  13.2 0.7 slice.33
  14.2 0.7 slice.34
  14.9 1.7 %collective-permute-start.3 = (bf16[32,2304]{1,0:T(8,128)(2,1)}, bf16[32,2304]{1,0:T(8,128)(2,1)S(1)}, u32[]{:S(2)}, u32[]{:S(2)}) collective-permute-start(bf16[32,2304]{1,0:T(8,128)(2,1)} %slice.34), channel_id=1, source_target_pairs={{0,16},{4,20},{8,24},{12,28},{16,0},{20,4},{24,8},{28,12},{1,17},{... | collective-permute-start | bytes 442376 | tf_op jit(solution)/shard_map/ppermute | solution.py:253
  16.7 4.7 %transpose.15.refs_2_.refs_1_ = bf16[1152,2304]{1,0:T(8,128)(2,1)S(1)} custom-call(bf16[2304,1152]{1,0:T(8,128)(2,1)} %collective-permute-done.4.in_ref), custom_call_target="tpu_custom_call" | custom-call | bytes 10616832 | tf_op jit(solution)/shard_map/transpose/pallas_call | solution.py:431
  21.4 0.6 collective-permute-start.6
  22.0 1.5 %collective-permute-start.5 = (bf16[128,2304]{1,0:T(8,128)(2,1)S(1)}, bf16[128,2304]{1,0:T(8,128)(2,1)S(1)}, u32[]{:S(2)}, u32[]{:S(2)}) collective-permute-start(bf16[128,2304]{1,0:T(8,128)(2,1)S(1)} %slice.35.refs_2_), channel_id=1, source_target_pairs={{0,8},{4,12},{8,0},{12,4},{16,24},{20,28},{24,16},{28,20},{1,9},{5... | collective-permute-start | bytes 1769480 | tf_op jit(solution)/shard_map/ppermute | solution.py:253
  23.5 4.8 %early_ladder.1 = (f32[2,1152,128]{2,1,0:T(8,128)S(1)}, s16[2,4,304,128]{3,2,1,0:T(8,128)(2,1)S(1)}, f32[8,128]{1,0:T(8,128)S(1)}) custom-call(s32[3]{0:T(128)S(1)} %pad_add_fusion.2.refs_0_, bf16[1152,2304]{1,0:T(8,128)(2,1)S(1)} %bitcast.11, bf16[1152,2304]{1,0:T(8,128)(2,1)S(1)} %transpose.15.refs_2_.refs_1_, bf16[64,2304]{1,0:T(8,128)(2,1)S(1)} %slice.30.refs_3_, ...), custom_call_target="tpu_custom_call" | custom-call | flops 2717908992 | bytes 13598732 | tf_op jit(solution)/shard_map/early_ladder/pallas_call | solution.py:293
  28.3 1.6 %collective-permute-start.9 = (s16[2,4,304,128]{3,2,1,0:T(8,128)(2,1)S(1)}, s16[2,4,304,128]{3,2,1,0:T(8,128)(2,1)S(1)}, u32[]{:S(2)}, u32[]{:S(2)}) collective-permute-start(s16[2,4,304,128]{3,2,1,0:T(8,128)(2,1)S(1)} %get-tuple-element.77), channel_id=1, source_target_pairs={{0,1},{1,0},{2,3},{3,2},{4,5},{5,4},{6,7},{7,6},{8,9},{9,8},{10,11... | collective-permute-start | bytes 1867784 | tf_op jit(solution)/shard_map/ppermute | solution.py:484
  30.0 5.6 %collective-permute-done.6.refs_4_ = bf16[128,2304]{1,0:T(8,128)(2,1)S(1)} collective-permute-done((bf16[128,2304]{1,0:T(8,128)(2,1)S(1)}, bf16[128,2304]{1,0:T(8,128)(2,1)S(1)}, u32[]{:S(2)}, u32[]{:S(2)}) %collective-permute-start.6) | collective-permute-done | bytes 589856 | tf_op jit(solution)/shard_map/ppermute | solution.py:253
  35.6 1.5 %collective-permute-start.8 = (bf16[64,2304]{1,0:T(8,128)(2,1)S(1)}, bf16[64,2304]{1,0:T(8,128)(2,1)S(1)}, u32[]{:S(2)}, u32[]{:S(2)}) collective-permute-start(bf16[64,2304]{1,0:T(8,128)(2,1)S(1)} %slice.41), channel_id=1, source_target_pairs={{0,8},{4,12},{8,0},{12,4},{16,24},{20,28},{24,16},{28,20},{1,9},{5... | collective-permute-start | bytes 884744 | tf_op jit(solution)/shard_map/ppermute | solution.py:253
  37.1 0.8 collective-permute-start.7
  37.9 4.8 %collective-permute-done.9.refs_1_ = s16[2,4,304,128]{3,2,1,0:T(8,128)(2,1)S(1)} collective-permute-done((s16[2,4,304,128]{3,2,1,0:T(8,128)(2,1)S(1)}, s16[2,4,304,128]{3,2,1,0:T(8,128)(2,1)S(1)}, u32[]{:S(2)}, u32[]{:S(2)}) %collective-permute-start.9) | collective-permute-done | bytes 622624 | tf_op jit(solution)/shard_map/ppermute | solution.py:484
  42.9 2.7 %collective-permute-start.13 = (s16[1,4,304,128]{3,2,1,0:T(8,128)(2,1)S(1)}, s16[1,4,304,128]{3,2,1,0:T(8,128)(2,1)S(1)}, u32[]{:S(2)}, u32[]{:S(2)}) collective-permute-start(s16[1,4,304,128]{3,2,1,0:T(8,128)(2,1)S(1)} %get-tuple-element.88), channel_id=1, source_target_pairs={{0,2},{1,3},{2,0},{3,1},{4,6},{5,7},{6,4},{7,5},{8,10},{9,11},{10,... | collective-permute-start | bytes 933896 | tf_op jit(solution)/shard_map/ppermute | solution.py:484
  45.5 4.2 %ladder.2 = (s16[3,400,128]{2,1,0:T(8,128)(2,1)S(1)}, s16[3,400,128]{2,1,0:T(8,128)(2,1)S(1)}, s16[3,400,128]{2,1,0:T(8,128)(2,1)S(1)}, s16[3,400,128]{2,1,0:T(8,128)(2,1)S(1)}, f32[8,128]{1,0:T(8,128)S(1)}) custom-call(bf16[1152,2304]{1,0:T(8,128)(2,1)S(1)} %bitcast.11, bf16[1152,2304]{1,0:T(8,128)(2,1)S(1)} %transpose.15.refs_2_.refs_1_, ...), custom_call_target="tpu_custom_call" | custom-call | flops 2717908992 | bytes 13910016 | tf_op jit(solution)/shard_map/ladder/pallas_call | solution.py:293
  49.8 0.6 collective-permute-start.10
  50.4 1.5 %collective-permute-start.11 = (s16[3,400,128]{2,1,0:T(8,128)(2,1)S(1)}, s16[3,400,128]{2,1,0:T(8,128)(2,1)S(1)}, u32[]{:S(2)}, u32[]{:S(2)}) collective-permute-start(s16[3,400,128]{2,1,0:T(8,128)(2,1)S(1)} %get-tuple-element.86), channel_id=1, source_target_pairs={{0,16},{4,20},{8,24},{12,28},{16,0},{20,4},{24,8},{28,12},{1,17},{... | collective-permute-start | bytes 921608 | tf_op jit(solution)/shard_map/ppermute | solution.py:253
  51.9 1.4 %collective-permute-start.12 = (s16[3,400,128]{2,1,0:T(8,128)(2,1)S(1)}, s16[3,400,128]{2,1,0:T(8,128)(2,1)S(1)}, u32[]{:S(2)}, u32[]{:S(2)}) collective-permute-start(s16[3,400,128]{2,1,0:T(8,128)(2,1)S(1)} %get-tuple-element.87), channel_id=1, source_target_pairs={{0,24},{4,28},{8,16},{12,20},{16,8},{20,12},{24,0},{28,4},{1,25},{... | collective-permute-start | bytes 921608 | tf_op jit(solution)/shard_map/ppermute | solution.py:253
  53.3 4.2 %ladder.3 = (s16[3,400,128]{2,1,0:T(8,128)(2,1)S(1)}, s16[3,400,128]{2,1,0:T(8,128)(2,1)S(1)}, s16[3,400,128]{2,1,0:T(8,128)(2,1)S(1)}, s16[3,400,128]{2,1,0:T(8,128)(2,1)S(1)}, f32[8,128]{1,0:T(8,128)S(1)}) custom-call(bf16[1152,2304]{1,0:T(8,128)(2,1)S(1)} %bitcast.11, bf16[1152,2304]{1,0:T(8,128)(2,1)S(1)} %transpose.15.refs_2_.refs_1_, ...), custom_call_target="tpu_custom_call" | custom-call | flops 2717908992 | bytes 13910016 | tf_op jit(solution)/shard_map/ladder/pallas_call | solution.py:293
  57.9 0.6 collective-permute-start.14
  58.5 1.4 %collective-permute-done.10.refs_2_ = s16[3,400,128]{2,1,0:T(8,128)(2,1)S(1)} collective-permute-done((s16[3,400,128]{2,1,0:T(8,128)(2,1)S(1)}, s16[3,400,128]{2,1,0:T(8,128)(2,1)S(1)}, u32[]{:S(2)}, u32[]{:S(2)}) %collective-permute-start.10) | collective-permute-done | bytes 307232 | tf_op jit(solution)/shard_map/ppermute | solution.py:253
  60.3 5.0 %collective-permute-done.12.refs_4_ = s16[3,400,128]{2,1,0:T(8,128)(2,1)S(1)} collective-permute-done((s16[3,400,128]{2,1,0:T(8,128)(2,1)S(1)}, s16[3,400,128]{2,1,0:T(8,128)(2,1)S(1)}, u32[]{:S(2)}, u32[]{:S(2)}) %collective-permute-start.12) | collective-permute-done | bytes 307232 | tf_op jit(solution)/shard_map/ppermute | solution.py:253
  65.3 4.7 %antisym.2 = (f32[2,1152,128]{2,1,0:T(8,128)S(1)}, s16[2,3,400,128]{3,2,1,0:T(8,128)(2,1)S(1)}, f32[8,128]{1,0:T(8,128)S(1)}) custom-call(s32[3]{0:T(128)S(1)} %pad_add_fusion.2.refs_0_, s16[3,400,128]{2,1,0:T(8,128)(2,1)S(1)} %get-tuple-element.97.refs_1_, s16[3,400,128]{2,1,0:T(8,128)(2,1)S(1)} %collective-permute-done.10.refs_2_, ...), custom_call_target="tpu_custom_call" | custom-call | flops 9437184 | bytes 3022860 | tf_op jit(solution)/shard_map/antisym/pallas_call | solution.py:293
  70.0 1.6 %collective-permute-start.19 = (s16[2,3,400,128]{3,2,1,0:T(8,128)(2,1)S(1)}, s16[2,3,400,128]{3,2,1,0:T(8,128)(2,1)S(1)}, u32[]{:S(2)}, u32[]{:S(2)}) collective-permute-start(s16[2,3,400,128]{3,2,1,0:T(8,128)(2,1)S(1)} %get-tuple-element.104), channel_id=1, source_target_pairs={{0,1},{1,0},{2,3},{3,2},{4,5},{5,4},{6,7},{7,6},{8,9},{9,8},{10,11... | collective-permute-start | bytes 1843208 | tf_op jit(solution)/shard_map/ppermute | solution.py:484
  71.6 0.7 collective-permute-start.15
  72.4 8.6 %collective-permute-done.15.refs_3_ = s16[2,304,128]{2,1,0:T(8,128)(2,1)S(1)} collective-permute-done((s16[2,304,128]{2,1,0:T(8,128)(2,1)S(1)}, s16[2,304,128]{2,1,0:T(8,128)(2,1)S(1)}, u32[]{:S(2)}, u32[]{:S(2)}) %collective-permute-start.15) | collective-permute-done | bytes 155680 | tf_op jit(solution)/shard_map/ppermute | solution.py:253
  81.0 1.4 %collective-permute-start.16 = (s16[3,400,128]{2,1,0:T(8,128)(2,1)S(1)}, s16[3,400,128]{2,1,0:T(8,128)(2,1)S(1)}, u32[]{:S(2)}, u32[]{:S(2)}) collective-permute-start(s16[3,400,128]{2,1,0:T(8,128)(2,1)S(1)} %get-tuple-element.93), channel_id=1, source_target_pairs={{0,8},{4,12},{8,0},{12,4},{16,24},{20,28},{24,16},{28,20},{1,9},{5... | collective-permute-start | bytes 921608 | tf_op jit(solution)/shard_map/ppermute | solution.py:253
  82.3 0.8 collective-permute-start.17
  83.1 1.4 %collective-permute-start.18 = (s16[3,400,128]{2,1,0:T(8,128)(2,1)S(1)}, s16[3,400,128]{2,1,0:T(8,128)(2,1)S(1)}, u32[]{:S(2)}, u32[]{:S(2)}) collective-permute-start(s16[3,400,128]{2,1,0:T(8,128)(2,1)S(1)} %get-tuple-element.95), channel_id=1, source_target_pairs={{0,24},{4,28},{8,16},{12,20},{16,8},{20,12},{24,0},{28,4},{1,25},{... | collective-permute-start | bytes 921608 | tf_op jit(solution)/shard_map/ppermute | solution.py:253
  84.5 1.1 early_antisym.1
  85.6 0.5 collective-permute-start.22
  86.1 1.8 %collective-permute-done.16.refs_2_ = s16[3,400,128]{2,1,0:T(8,128)(2,1)S(1)} collective-permute-done((s16[3,400,128]{2,1,0:T(8,128)(2,1)S(1)}, s16[3,400,128]{2,1,0:T(8,128)(2,1)S(1)}, u32[]{:S(2)}, u32[]{:S(2)}) %collective-permute-start.16) | collective-permute-done | bytes 307232 | tf_op jit(solution)/shard_map/ppermute | solution.py:253
  87.8 4.6 %collective-permute-done.17.refs_3_ = s16[3,400,128]{2,1,0:T(8,128)(2,1)S(1)} collective-permute-done((s16[3,400,128]{2,1,0:T(8,128)(2,1)S(1)}, s16[3,400,128]{2,1,0:T(8,128)(2,1)S(1)}, u32[]{:S(2)}, u32[]{:S(2)}) %collective-permute-start.17) | collective-permute-done | bytes 307232 | tf_op jit(solution)/shard_map/ppermute | solution.py:253
  92.5 4.7 %antisym.3 = (f32[2,1152,128]{2,1,0:T(8,128)S(1)}, s16[1,3,400,128]{3,2,1,0:T(8,128)(2,1)S(1)}, s16[1,3,400,128]{3,2,1,0:T(8,128)(2,1)S(1)}, f32[8,128]{1,0:T(8,128)S(1)}) custom-call(s32[3]{0:T(128)S(1)} %pad_add_fusion.2.refs_0_, s16[3,400,128]{2,1,0:T(8,128)(2,1)S(1)} %get-tuple-element.92.refs_1_, ...), custom_call_target="tpu_custom_call" | custom-call | flops 9437184 | bytes 3022860 | tf_op jit(solution)/shard_map/antisym/pallas_call | solution.py:293
  97.2 0.5 collective-permute-start.21
  97.7 0.9 collective-permute-start.23
  98.7 0.8 collective-permute-start.20
  99.7 2.9 %collective-permute-start.25 = (s16[1,3,400,128]{3,2,1,0:T(8,128)(2,1)S(1)}, s16[1,3,400,128]{3,2,1,0:T(8,128)(2,1)S(1)}, u32[]{:S(2)}, u32[]{:S(2)}) collective-permute-start(s16[1,3,400,128]{3,2,1,0:T(8,128)(2,1)S(1)} %get-tuple-element.115), channel_id=1, source_target_pairs={{0,2},{1,3},{2,0},{3,1},{4,6},{5,7},{6,4},{7,5},{8,10},{9,11},{10,... | collective-permute-start | bytes 921608 | tf_op jit(solution)/shard_map/ppermute | solution.py:484
  102.6 8.8 %collective-permute-done.23.refs_4_ = s16[2,304,128]{2,1,0:T(8,128)(2,1)S(1)} collective-permute-done((s16[2,304,128]{2,1,0:T(8,128)(2,1)S(1)}, s16[2,304,128]{2,1,0:T(8,128)(2,1)S(1)}, u32[]{:S(2)}, u32[]{:S(2)}) %collective-permute-start.23) | collective-permute-done | bytes 155680 | tf_op jit(solution)/shard_map/ppermute | solution.py:484
  111.4 1.4 %finish.3 = (f32[192,2304]{1,0:T(8,128)}, f32[8,128]{1,0:T(8,128)S(1)}) custom-call(f32[3,1,128]{2,1,0:T(1,128)S(1)} %pad_maximum_fusion.refs_0_, f32[1152,2]{1,0:T(8,128)S(1)} %bitcast.12, f32[288,128]{1,0:T(8,128)S(1)} %get-tuple-element.107.refs_2_, s16[2,304,128]{2,1,0:T(8,128)(2,1)S(1)} %collective-permute-done.22.refs_3_, ...), custom_call_target="tpu_custom_call" | custom-call | flops 2359296 | bytes 2238976 | tf_op jit(solution)/shard_map/finish/pallas_call | solution.py:293
  113.0 9.1 %collective-permute-done.25.refs_4_ = s16[1,3,400,128]{3,2,1,0:T(8,128)(2,1)S(1)} collective-permute-done((s16[1,3,400,128]{3,2,1,0:T(8,128)(2,1)S(1)}, s16[1,3,400,128]{3,2,1,0:T(8,128)(2,1)S(1)}, u32[]{:S(2)}, u32[]{:S(2)}) %collective-permute-start.25) | collective-permute-done | bytes 307232 | tf_op jit(solution)/shard_map/ppermute | solution.py:484
  122.2 1.4 %finish.4 = (f32[192,2304]{1,0:T(8,128)}, f32[8,128]{1,0:T(8,128)S(1)}) custom-call(f32[3,1,128]{2,1,0:T(1,128)S(1)} %pad_maximum_fusion.refs_0_, f32[1152,2]{1,0:T(8,128)S(1)} %bitcast.13, f32[2,1152,128]{2,1,0:T(8,128)S(1)} %get-tuple-element.110.refs_0_.refs_2_, ...), custom_call_target="tpu_custom_call", output_to_operand_aliasing={{0}: (5, {})} | custom-call | flops 2359296 | bytes 5650944 | tf_op jit(solution)/shard_map/finish/pallas_call | solution.py:293
  123.5 1.9 %collective-permute-done.24.refs_4_ = s16[1,3,400,128]{3,2,1,0:T(8,128)(2,1)S(1)} collective-permute-done((s16[1,3,400,128]{3,2,1,0:T(8,128)(2,1)S(1)}, s16[1,3,400,128]{3,2,1,0:T(8,128)(2,1)S(1)}, u32[]{:S(2)}, u32[]{:S(2)}) %collective-permute-start.24) | collective-permute-done | bytes 307232 | tf_op jit(solution)/shard_map/ppermute | solution.py:484
  125.4 1.4 %finish.5 = (f32[192,2304]{1,0:T(8,128)}, f32[8,128]{1,0:T(8,128)}) custom-call(f32[3,1,128]{2,1,0:T(1,128)S(1)} %pad_maximum_fusion.refs_0_, f32[1152,2]{1,0:T(8,128)S(1)} %bitcast.14, f32[2,1152,128]{2,1,0:T(8,128)S(1)} %get-tuple-element.101.refs_0_.refs_2_, ...), custom_call_target="tpu_custom_call", output_to_operand_aliasing={{0}: (5, {})} | custom-call | flops 2359296 | bytes 5343744 | tf_op jit(solution)/shard_map/finish/pallas_call | solution.py:293
  (57 shorter events, 3.6 us)
Async XLA Ops:
  0.0 16.7 %collective-permute-start.4 = (bf16[2304,1152]{1,0:T(8,128)(2,1)}, bf16[2304,1152]{1,0:T(8,128)(2,1)}, u32[]{:S(2)}, u32[]{:S(2)}) collective-permute-start(bf16[2304,1152]{1,0:T(8,128)(2,1)} %in_ref.1), channel_id=1, source_target_pairs={{0,4},{4,0},{8,12},{12,8},{16,20},{20,16},{24,28},{28,24},{1,5},{5... | collective-permute-start | bytes 15925256 | tf_op jit(solution)/shard_map/ppermute | solution.py:430
  1.4 10.5 %copy-start.3 = (s32[192,2]{0,1:T(2,128)S(1)}, s32[192,2]{0,1:T(2,128)}, u32[]{:S(2)}) copy-start(s32[192,2]{0,1:T(2,128)} %param.7) | copy-start | bytes 4612
  1.4 10.5 %copy-start.4 = (f32[160]{0:T(256)S(1)}, f32[160]{0:T(256)}, u32[]{:S(2)}) copy-start(f32[160]{0:T(256)} %param.8) | copy-start | bytes 1924
  1.5 10.7 %copy-start.2 = (f32[96]{0:T(128)S(1)}, f32[96]{0:T(128)}, u32[]{:S(2)}) copy-start(f32[96]{0:T(128)} %param.9) | copy-start | bytes 1156
  1.5 15.1 %copy-start.1 = (bf16[192,2304]{1,0:T(8,128)(2,1)S(1)}, bf16[192,2304]{1,0:T(8,128)(2,1)}, u32[]{:S(2)}) copy-start(bf16[192,2304]{1,0:T(8,128)(2,1)} %param.5) | copy-start | bytes 2654212
  1.5 11.2 %collective-permute-start = (bf16[64,2304]{1,0:T(8,128)(2,1)S(1)}, bf16[64,2304]{1,0:T(8,128)(2,1)S(1)}, u32[]{:S(2)}, u32[]{:S(2)}) collective-permute-start(bf16[64,2304]{1,0:T(8,128)(2,1)S(1)} %slice.30.refs_3_), channel_id=1, source_target_pairs={{0,8},{4,12},{8,0},{12,4},{16,24},{20,28},{24,16},{28,20},{1,9},{5... | collective-permute-start | bytes 884744 | tf_op jit(solution)/shard_map/ppermute | solution.py:253
  4.0 9.1 %collective-permute-start.1 = (bf16[64,2304]{1,0:T(8,128)(2,1)S(1)}, bf16[64,2304]{1,0:T(8,128)(2,1)S(1)}, u32[]{:S(2)}, u32[]{:S(2)}) collective-permute-start(bf16[64,2304]{1,0:T(8,128)(2,1)S(1)} %slice.30.refs_3_), channel_id=1, source_target_pairs={{0,16},{4,20},{8,24},{12,28},{16,0},{20,4},{24,8},{28,12},{1,17},{... | collective-permute-start | bytes 884744 | tf_op jit(solution)/shard_map/ppermute | solution.py:253
  9.6 2.3 %copy-start = (bf16[1152,2304]{1,0:T(8,128)(2,1)}, bf16[1152,2304]{1,0:T(8,128)(2,1)S(1)}, u32[]{:S(2)}) copy-start(bf16[1152,2304]{1,0:T(8,128)(2,1)S(1)} %transpose.14.refs_1_.refs_0_) | copy-start | bytes 15925252
  13.9 7.5 %collective-permute-start.2 = (bf16[32,2304]{1,0:T(8,128)(2,1)}, bf16[32,2304]{1,0:T(8,128)(2,1)S(1)}, u32[]{:S(2)}, u32[]{:S(2)}) collective-permute-start(bf16[32,2304]{1,0:T(8,128)(2,1)} %slice.33), channel_id=1, source_target_pairs={{0,8},{4,12},{8,0},{12,4},{16,24},{20,28},{24,16},{28,20},{1,9},{5... | collective-permute-start | bytes 442376 | tf_op jit(solution)/shard_map/ppermute | solution.py:253
  14.9 6.5 %collective-permute-start.3 = (bf16[32,2304]{1,0:T(8,128)(2,1)}, bf16[32,2304]{1,0:T(8,128)(2,1)S(1)}, u32[]{:S(2)}, u32[]{:S(2)}) collective-permute-start(bf16[32,2304]{1,0:T(8,128)(2,1)} %slice.34), channel_id=1, source_target_pairs={{0,16},{4,20},{8,24},{12,28},{16,0},{20,4},{24,8},{28,12},{1,17},{... | collective-permute-start | bytes 442376 | tf_op jit(solution)/shard_map/ppermute | solution.py:253
  16.6 6.9 %slice-start = ((s8[5308416]{0:T(1024)(128)(4,1)}), s8[1114112]{0:T(1024)(128)(4,1)S(1)}, s32[]{:S(2)}) async-start(s8[5308416]{0:T(1024)(128)(4,1)} %bitcast.10), calls=%async_computation | async-start | bytes 2228224
  16.7 6.8 %slice-start.1 = ((s8[5308416]{0:T(1024)(128)(4,1)}), s8[4194304]{0:T(1024)(128)(4,1)S(1)}, s32[]{:S(2)}) async-start(s8[5308416]{0:T(1024)(128)(4,1)} %bitcast.10), calls=%async_computation.1 | async-start | bytes 8388608
  21.4 14.2 %collective-permute-start.6 = (bf16[128,2304]{1,0:T(8,128)(2,1)S(1)}, bf16[128,2304]{1,0:T(8,128)(2,1)S(1)}, u32[]{:S(2)}, u32[]{:S(2)}) collective-permute-start(bf16[128,2304]{1,0:T(8,128)(2,1)S(1)} %slice.35.refs_2_), channel_id=1, source_target_pairs={{0,16},{4,20},{8,24},{12,28},{16,0},{20,4},{24,8},{28,12},{1,17},{... | collective-permute-start | bytes 1769480 | tf_op jit(solution)/shard_map/ppermute | solution.py:253
  22.0 15.1 %collective-permute-start.5 = (bf16[128,2304]{1,0:T(8,128)(2,1)S(1)}, bf16[128,2304]{1,0:T(8,128)(2,1)S(1)}, u32[]{:S(2)}, u32[]{:S(2)}) collective-permute-start(bf16[128,2304]{1,0:T(8,128)(2,1)S(1)} %slice.35.refs_2_), channel_id=1, source_target_pairs={{0,8},{4,12},{8,0},{12,4},{16,24},{20,28},{24,16},{28,20},{1,9},{5... | collective-permute-start | bytes 1769480 | tf_op jit(solution)/shard_map/ppermute | solution.py:253
  28.3 14.3 %collective-permute-start.9 = (s16[2,4,304,128]{3,2,1,0:T(8,128)(2,1)S(1)}, s16[2,4,304,128]{3,2,1,0:T(8,128)(2,1)S(1)}, u32[]{:S(2)}, u32[]{:S(2)}) collective-permute-start(s16[2,4,304,128]{3,2,1,0:T(8,128)(2,1)S(1)} %get-tuple-element.77), channel_id=1, source_target_pairs={{0,1},{1,0},{2,3},{3,2},{4,5},{5,4},{6,7},{7,6},{8,9},{9,8},{10,11... | collective-permute-start | bytes 1867784 | tf_op jit(solution)/shard_map/ppermute | solution.py:484
  35.6 9.9 %collective-permute-start.8 = (bf16[64,2304]{1,0:T(8,128)(2,1)S(1)}, bf16[64,2304]{1,0:T(8,128)(2,1)S(1)}, u32[]{:S(2)}, u32[]{:S(2)}) collective-permute-start(bf16[64,2304]{1,0:T(8,128)(2,1)S(1)} %slice.41), channel_id=1, source_target_pairs={{0,8},{4,12},{8,0},{12,4},{16,24},{20,28},{24,16},{28,20},{1,9},{5... | collective-permute-start | bytes 884744 | tf_op jit(solution)/shard_map/ppermute | solution.py:253
  37.1 16.2 %collective-permute-start.7 = (bf16[64,2304]{1,0:T(8,128)(2,1)S(1)}, bf16[64,2304]{1,0:T(8,128)(2,1)S(1)}, u32[]{:S(2)}, u32[]{:S(2)}) collective-permute-start(bf16[64,2304]{1,0:T(8,128)(2,1)S(1)} %slice.40), channel_id=1, source_target_pairs={{0,16},{4,20},{8,24},{12,28},{16,0},{20,4},{24,8},{28,12},{1,17},{... | collective-permute-start | bytes 884744 | tf_op jit(solution)/shard_map/ppermute | solution.py:253
  42.9 14.7 %collective-permute-start.13 = (s16[1,4,304,128]{3,2,1,0:T(8,128)(2,1)S(1)}, s16[1,4,304,128]{3,2,1,0:T(8,128)(2,1)S(1)}, u32[]{:S(2)}, u32[]{:S(2)}) collective-permute-start(s16[1,4,304,128]{3,2,1,0:T(8,128)(2,1)S(1)} %get-tuple-element.88), channel_id=1, source_target_pairs={{0,2},{1,3},{2,0},{3,1},{4,6},{5,7},{6,4},{7,5},{8,10},{9,11},{10,... | collective-permute-start | bytes 933896 | tf_op jit(solution)/shard_map/ppermute | solution.py:484
  49.8 10.1 %collective-permute-start.10 = (s16[3,400,128]{2,1,0:T(8,128)(2,1)S(1)}, s16[3,400,128]{2,1,0:T(8,128)(2,1)S(1)}, u32[]{:S(2)}, u32[]{:S(2)}) collective-permute-start(s16[3,400,128]{2,1,0:T(8,128)(2,1)S(1)} %get-tuple-element.85), channel_id=1, source_target_pairs={{0,8},{4,12},{8,0},{12,4},{16,24},{20,28},{24,16},{28,20},{1,9},{5... | collective-permute-start | bytes 921608 | tf_op jit(solution)/shard_map/ppermute | solution.py:253
  50.4 9.9 %collective-permute-start.11 = (s16[3,400,128]{2,1,0:T(8,128)(2,1)S(1)}, s16[3,400,128]{2,1,0:T(8,128)(2,1)S(1)}, u32[]{:S(2)}, u32[]{:S(2)}) collective-permute-start(s16[3,400,128]{2,1,0:T(8,128)(2,1)S(1)} %get-tuple-element.86), channel_id=1, source_target_pairs={{0,16},{4,20},{8,24},{12,28},{16,0},{20,4},{24,8},{28,12},{1,17},{... | collective-permute-start | bytes 921608 | tf_op jit(solution)/shard_map/ppermute | solution.py:253
  51.9 13.4 %collective-permute-start.12 = (s16[3,400,128]{2,1,0:T(8,128)(2,1)S(1)}, s16[3,400,128]{2,1,0:T(8,128)(2,1)S(1)}, u32[]{:S(2)}, u32[]{:S(2)}) collective-permute-start(s16[3,400,128]{2,1,0:T(8,128)(2,1)S(1)} %get-tuple-element.87), channel_id=1, source_target_pairs={{0,24},{4,28},{8,16},{12,20},{16,8},{20,12},{24,0},{28,4},{1,25},{... | collective-permute-start | bytes 921608 | tf_op jit(solution)/shard_map/ppermute | solution.py:253
  57.9 13.8 %collective-permute-start.14 = (s16[2,304,128]{2,1,0:T(8,128)(2,1)S(1)}, s16[2,304,128]{2,1,0:T(8,128)(2,1)S(1)}, u32[]{:S(2)}, u32[]{:S(2)}) collective-permute-start(s16[2,304,128]{2,1,0:T(8,128)(2,1)S(1)} %get-tuple-element.90), channel_id=1, source_target_pairs={{0,8},{4,12},{8,0},{12,4},{16,24},{20,28},{24,16},{28,20},{1,9},{5... | collective-permute-start | bytes 466952 | tf_op jit(solution)/shard_map/ppermute | solution.py:253
  70.0 27.2 %collective-permute-start.19 = (s16[2,3,400,128]{3,2,1,0:T(8,128)(2,1)S(1)}, s16[2,3,400,128]{3,2,1,0:T(8,128)(2,1)S(1)}, u32[]{:S(2)}, u32[]{:S(2)}) collective-permute-start(s16[2,3,400,128]{3,2,1,0:T(8,128)(2,1)S(1)} %get-tuple-element.104), channel_id=1, source_target_pairs={{0,1},{1,0},{2,3},{3,2},{4,5},{5,4},{6,7},{7,6},{8,9},{9,8},{10,11... | collective-permute-start | bytes 1843208 | tf_op jit(solution)/shard_map/ppermute | solution.py:484
  71.6 9.3 %collective-permute-start.15 = (s16[2,304,128]{2,1,0:T(8,128)(2,1)S(1)}, s16[2,304,128]{2,1,0:T(8,128)(2,1)S(1)}, u32[]{:S(2)}, u32[]{:S(2)}) collective-permute-start(s16[2,304,128]{2,1,0:T(8,128)(2,1)S(1)} %pad_add_fusion), channel_id=1, source_target_pairs={{0,16},{4,20},{8,24},{12,28},{16,0},{20,4},{24,8},{28,12},{1,17},{... | collective-permute-start | bytes 466952 | tf_op jit(solution)/shard_map/ppermute | solution.py:253
  81.0 6.9 %collective-permute-start.16 = (s16[3,400,128]{2,1,0:T(8,128)(2,1)S(1)}, s16[3,400,128]{2,1,0:T(8,128)(2,1)S(1)}, u32[]{:S(2)}, u32[]{:S(2)}) collective-permute-start(s16[3,400,128]{2,1,0:T(8,128)(2,1)S(1)} %get-tuple-element.93), channel_id=1, source_target_pairs={{0,8},{4,12},{8,0},{12,4},{16,24},{20,28},{24,16},{28,20},{1,9},{5... | collective-permute-start | bytes 921608 | tf_op jit(solution)/shard_map/ppermute | solution.py:253
  82.3 10.1 %collective-permute-start.17 = (s16[3,400,128]{2,1,0:T(8,128)(2,1)S(1)}, s16[3,400,128]{2,1,0:T(8,128)(2,1)S(1)}, u32[]{:S(2)}, u32[]{:S(2)}) collective-permute-start(s16[3,400,128]{2,1,0:T(8,128)(2,1)S(1)} %get-tuple-element.94), channel_id=1, source_target_pairs={{0,16},{4,20},{8,24},{12,28},{16,0},{20,4},{24,8},{28,12},{1,17},{... | collective-permute-start | bytes 921608 | tf_op jit(solution)/shard_map/ppermute | solution.py:253
  83.1 9.4 %collective-permute-start.18 = (s16[3,400,128]{2,1,0:T(8,128)(2,1)S(1)}, s16[3,400,128]{2,1,0:T(8,128)(2,1)S(1)}, u32[]{:S(2)}, u32[]{:S(2)}) collective-permute-start(s16[3,400,128]{2,1,0:T(8,128)(2,1)S(1)} %get-tuple-element.95), channel_id=1, source_target_pairs={{0,24},{4,28},{8,16},{12,20},{16,8},{20,12},{24,0},{28,4},{1,25},{... | collective-permute-start | bytes 921608 | tf_op jit(solution)/shard_map/ppermute | solution.py:253
  85.6 12.1 %collective-permute-start.22 = (s16[2,304,128]{2,1,0:T(8,128)(2,1)S(1)}, s16[2,304,128]{2,1,0:T(8,128)(2,1)S(1)}, u32[]{:S(2)}, u32[]{:S(2)}) collective-permute-start(s16[2,304,128]{2,1,0:T(8,128)(2,1)S(1)} %get-tuple-element.108), channel_id=1, source_target_pairs={{0,1},{1,0},{2,3},{3,2},{4,5},{5,4},{6,7},{7,6},{8,9},{9,8},{10,11... | collective-permute-start | bytes 466952 | tf_op jit(solution)/shard_map/ppermute | solution.py:484
  97.2 15.6 %collective-permute-start.21 = (s16[1,3,400,128]{3,2,1,0:T(8,128)(2,1)S(1)}, s16[1,3,400,128]{3,2,1,0:T(8,128)(2,1)S(1)}, u32[]{:S(2)}, u32[]{:S(2)}) collective-permute-start(s16[1,3,400,128]{3,2,1,0:T(8,128)(2,1)S(1)} %get-tuple-element.106), channel_id=1, source_target_pairs={{0,1},{1,0},{2,3},{3,2},{4,5},{5,4},{6,7},{7,6},{8,9},{9,8},{10,11... | collective-permute-start | bytes 921608 | tf_op jit(solution)/shard_map/ppermute | solution.py:484
  97.7 13.7 %collective-permute-start.23 = (s16[2,304,128]{2,1,0:T(8,128)(2,1)S(1)}, s16[2,304,128]{2,1,0:T(8,128)(2,1)S(1)}, u32[]{:S(2)}, u32[]{:S(2)}) collective-permute-start(s16[2,304,128]{2,1,0:T(8,128)(2,1)S(1)} %pad_add_fusion.1), channel_id=1, source_target_pairs={{0,2},{1,3},{2,0},{3,1},{4,6},{5,7},{6,4},{7,5},{8,10},{9,11},{10,... | collective-permute-start | bytes 466952 | tf_op jit(solution)/shard_map/ppermute | solution.py:484
  98.7 24.9 %collective-permute-start.20 = (s16[1,3,400,128]{3,2,1,0:T(8,128)(2,1)S(1)}, s16[1,3,400,128]{3,2,1,0:T(8,128)(2,1)S(1)}, u32[]{:S(2)}, u32[]{:S(2)}) collective-permute-start(s16[1,3,400,128]{3,2,1,0:T(8,128)(2,1)S(1)} %get-tuple-element.105), channel_id=1, source_target_pairs={{0,1},{1,0},{2,3},{3,2},{4,5},{5,4},{6,7},{7,6},{8,9},{9,8},{10,11... | collective-permute-start | bytes 921608 | tf_op jit(solution)/shard_map/ppermute | solution.py:484
  99.7 22.5 %collective-permute-start.25 = (s16[1,3,400,128]{3,2,1,0:T(8,128)(2,1)S(1)}, s16[1,3,400,128]{3,2,1,0:T(8,128)(2,1)S(1)}, u32[]{:S(2)}, u32[]{:S(2)}) collective-permute-start(s16[1,3,400,128]{3,2,1,0:T(8,128)(2,1)S(1)} %get-tuple-element.115), channel_id=1, source_target_pairs={{0,2},{1,3},{2,0},{3,1},{4,6},{5,7},{6,4},{7,5},{8,10},{9,11},{10,... | collective-permute-start | bytes 921608 | tf_op jit(solution)/shard_map/ppermute | solution.py:484
  112.9 12.5 %collective-permute-start.24 = (s16[1,3,400,128]{3,2,1,0:T(8,128)(2,1)S(1)}, s16[1,3,400,128]{3,2,1,0:T(8,128)(2,1)S(1)}, u32[]{:S(2)}, u32[]{:S(2)}) collective-permute-start(s16[1,3,400,128]{3,2,1,0:T(8,128)(2,1)S(1)} %get-tuple-element.114), channel_id=1, source_target_pairs={{0,2},{1,3},{2,0},{3,1},{4,6},{5,7},{6,4},{7,5},{8,10},{9,11},{10,... | collective-permute-start | bytes 921608 | tf_op jit(solution)/shard_map/ppermute | solution.py:484

commit v11 on v10

--- a/solution.py
+++ b/solution.py
@@ -453,11 +453,8 @@
         return [[mine], [one], [two], [low, high]], beside
 
     if early:
-        head, (own_t, eps_pair, eps_virt) = gather(
-            amplitudes[:WIDTH], (own_t, eps_pair, eps_virt)
-        )
-        head, own_t, sib_t, rest = lax.optimization_barrier(
-            (head, own_t, sib_t, amplitudes[WIDTH:])
+        head, (own_t, eps_pair, eps_virt, rest) = gather(
+            amplitudes[:WIDTH], (own_t, eps_pair, eps_virt, amplitudes[WIDTH:])
         )
         tail, _ = gather(rest, ())
         gathered = [(0, head), (WIDTH, tail)]
@@ -516,7 +513,6 @@
         got, places = yield from halved(parts, [across(away, 1)])
         mine, *sums = yield early_sum(places, parts, got)
         arrived = by_steps(to_chip, *sums)
-        turns.append(turns[-1] + arrived)
         own, *blocks = yield early_antisym([mine, *arrived])
         yield finish(r, own, by_steps(across, *blocks), None, update)
 
@@ -540,7 +536,7 @@
     def when(stage):
         r, k = stage
         if early and r == 0:
-            return (20, *[41] * hops, 54, 66, 83)[k]
+            return (20, *[44] * hops, 54, 66, 83)[k]
         if k == 0:
             return 37 + 5 * r if early else 30 + 5 * r
         return 15 * r + (45 if early else 54) + (k - 1) * 17 - (1 if k == 2 + hops else 0)

time: 127 us -> 136 us (1.071)
  waiting for transfers between devices: 52.5 us -> 60 us
  starting transfers between devices: 31 us -> 34 us
    ppermute x9, waiting for transfers between devices: 24.6 us -> 31.5 us  [across(): return lax.ppermute(x, 'slab', [(i, i ^ level) for i in range(slabs)])]
    ppermute x9, starting transfers between devices: 11.7 us -> 13.5 us  [across(): return lax.ppermute(x, 'slab', [(i, i ^ level) for i in range(slabs)])]
  transfers between devices with their start and end apart: 26 -> 26, of which waited for: 12 -> 13; matrix products, arithmetic and copies ran while one was open for 3% -> 1% of each run, Pallas kernels for 28% -> 23%
where the time goes in v11:
time: 136 us; the launch traced here: 135 us
  waiting for transfers between devices  60 us (44%)
  Pallas kernels  36.7 us (27%)
  starting transfers between devices  34 us (25%)
  local copies, waits for them, and re-layouts  3.82 us (3%)
    ppermute x9, waiting for transfers between devices, across(): return lax.ppermute(x, 'slab', [(i, i ^ level) for i in range(slabs)])  31.5 us
    pallas_call x13, Pallas kernels, call(): pl.pallas_call(kernel, in_specs=[*in_specs, vmem], out_specs=[*out_specs,...  28.7 us
    ppermute x16, waiting for transfers between devices, to_chip(): return lax.ppermute(x, 'pair', [(i, i ^ d * CORES) for i in range(devices)])  28.5 us
    ppermute x16, starting transfers between devices, to_chip(): return lax.ppermute(x, 'pair', [(i, i ^ d * CORES) for i in range(devices)])  20 us
    ppermute x9, starting transfers between devices, across(): return lax.ppermute(x, 'slab', [(i, i ^ level) for i in range(slabs)])  13.5 us
    pallas_call x1, Pallas kernels, on_device(): sib_t = transpose(swapped)  4 us
    pallas_call x1, Pallas kernels, on_device(): own_t = transpose(in_hbm(integrals))  4 us
  transfers between devices with their start and end apart: 26, of which 13 were waited for; matrix products, arithmetic and copies ran while one was open for 1% of the time, Pallas kernels for 23%

profile of v11, /device:TPU:0, one launch (start us, length us, event | category | flops | bytes accessed | tf_op | source)
XLA Modules:
  0.0 135.3 jit_solution(12911126177884458794)
XLA Ops:
  0.0 0.5 collective-permute-start.2
  0.5 1.0 slice.30.refs_3_
  1.5 2.6 %collective-permute-start = (bf16[64,2304]{1,0:T(8,128)(2,1)S(1)}, bf16[64,2304]{1,0:T(8,128)(2,1)S(1)}, u32[]{:S(2)}, u32[]{:S(2)}) collective-permute-start(bf16[64,2304]{1,0:T(8,128)(2,1)S(1)} %slice.30.refs_3_), channel_id=1, source_target_pairs={{0,8},{4,12},{8,0},{12,4},{16,24},{20,28},{24,16},{28,20},{1,9},{5... | collective-permute-start | bytes 884744 | tf_op jit(solution)/shard_map/ppermute | solution.py:253
  4.0 1.5 %collective-permute-start.1 = (bf16[64,2304]{1,0:T(8,128)(2,1)S(1)}, bf16[64,2304]{1,0:T(8,128)(2,1)S(1)}, u32[]{:S(2)}, u32[]{:S(2)}) collective-permute-start(bf16[64,2304]{1,0:T(8,128)(2,1)S(1)} %slice.30.refs_3_), channel_id=1, source_target_pairs={{0,16},{4,20},{8,24},{12,28},{16,0},{20,4},{24,8},{28,12},{1,17},{... | collective-permute-start | bytes 884744 | tf_op jit(solution)/shard_map/ppermute | solution.py:253
  5.6 4.0 %transpose.14.refs_1_.refs_0_ = bf16[1152,2304]{1,0:T(8,128)(2,1)S(1)} custom-call(bf16[2304,1152]{1,0:T(8,128)(2,1)} %in_ref.1), custom_call_target="tpu_custom_call" | custom-call | bytes 10616832 | tf_op jit(solution)/shard_map/transpose/pallas_call | solution.py:429
  9.6 2.3 %copy-done = bf16[1152,2304]{1,0:T(8,128)(2,1)} copy-done((bf16[1152,2304]{1,0:T(8,128)(2,1)}, bf16[1152,2304]{1,0:T(8,128)(2,1)S(1)}, u32[]{:S(2)}) %copy-start) | copy-done | bytes 5308440
  12.8 0.4 collective-permute-done.1.refs_5_
  13.2 1.5 %collective-permute-start.4 = (bf16[128,2304]{1,0:T(8,128)(2,1)S(1)}, bf16[128,2304]{1,0:T(8,128)(2,1)S(1)}, u32[]{:S(2)}, u32[]{:S(2)}) collective-permute-start(bf16[128,2304]{1,0:T(8,128)(2,1)S(1)} %slice.33.refs_2_), channel_id=1, source_target_pairs={{0,16},{4,20},{8,24},{12,28},{16,0},{20,4},{24,8},{28,12},{1,17},{... | collective-permute-start | bytes 1769480 | tf_op jit(solution)/shard_map/ppermute | solution.py:253
  14.7 0.6 collective-permute-start.6
  15.8 1.7 %collective-permute-start.3 = (bf16[128,2304]{1,0:T(8,128)(2,1)S(1)}, bf16[128,2304]{1,0:T(8,128)(2,1)S(1)}, u32[]{:S(2)}, u32[]{:S(2)}) collective-permute-start(bf16[128,2304]{1,0:T(8,128)(2,1)S(1)} %slice.33.refs_2_), channel_id=1, source_target_pairs={{0,8},{4,12},{8,0},{12,4},{16,24},{20,28},{24,16},{28,20},{1,9},{5... | collective-permute-start | bytes 1769480 | tf_op jit(solution)/shard_map/ppermute | solution.py:253
  17.5 4.0 %transpose.15.refs_2_.refs_1_ = bf16[1152,2304]{1,0:T(8,128)(2,1)S(1)} custom-call(bf16[2304,1152]{1,0:T(8,128)(2,1)} %collective-permute-done.2.in_ref), custom_call_target="tpu_custom_call" | custom-call | bytes 10616832 | tf_op jit(solution)/shard_map/transpose/pallas_call | solution.py:431
  21.6 9.6 %collective-permute-done.7.refs_7_ = bf16[32,2304]{1,0:T(8,128)(2,1)S(1)} collective-permute-done((bf16[32,2304]{1,0:T(8,128)(2,1)S(1)}, bf16[32,2304]{1,0:T(8,128)(2,1)S(1)}, u32[]{:S(2)}, u32[]{:S(2)}) %collective-permute-start.7) | collective-permute-done | bytes 147488 | tf_op jit(solution)/shard_map/ppermute | solution.py:253
  31.2 4.8 %early_ladder.1 = (f32[2,1152,128]{2,1,0:T(8,128)S(1)}, s16[2,4,304,128]{3,2,1,0:T(8,128)(2,1)S(1)}, f32[8,128]{1,0:T(8,128)S(1)}) custom-call(s32[3]{0:T(128)S(1)} %pad_add_fusion.2.refs_0_, bf16[1152,2304]{1,0:T(8,128)(2,1)S(1)} %bitcast.11, bf16[1152,2304]{1,0:T(8,128)(2,1)S(1)} %transpose.15.refs_2_.refs_1_, bf16[64,2304]{1,0:T(8,128)(2,1)S(1)} %slice.30.refs_3_, ...), custom_call_target="tpu_custom_call" | custom-call | flops 2717908992 | bytes 13598732 | tf_op jit(solution)/shard_map/early_ladder/pallas_call | solution.py:293
  36.0 1.6 %collective-permute-start.8 = (s16[2,4,304,128]{3,2,1,0:T(8,128)(2,1)S(1)}, s16[2,4,304,128]{3,2,1,0:T(8,128)(2,1)S(1)}, u32[]{:S(2)}, u32[]{:S(2)}) collective-permute-start(s16[2,4,304,128]{3,2,1,0:T(8,128)(2,1)S(1)} %get-tuple-element.63), channel_id=1, source_target_pairs={{0,1},{1,0},{2,3},{3,2},{4,5},{5,4},{6,7},{7,6},{8,9},{9,8},{10,11... | collective-permute-start | bytes 1867784 | tf_op jit(solution)/shard_map/ppermute | solution.py:481
  37.7 0.6 collective-permute-start.9
  38.3 1.4 %collective-permute-start.5 = (bf16[64,2304]{1,0:T(8,128)(2,1)S(1)}, bf16[64,2304]{1,0:T(8,128)(2,1)S(1)}, u32[]{:S(2)}, u32[]{:S(2)}) collective-permute-start(bf16[64,2304]{1,0:T(8,128)(2,1)S(1)} %slice.40), channel_id=1, source_target_pairs={{0,16},{4,20},{8,24},{12,28},{16,0},{20,4},{24,8},{28,12},{1,17},{... | collective-permute-start | bytes 884744 | tf_op jit(solution)/shard_map/ppermute | solution.py:253
  39.8 5.3 %collective-permute-done.9.refs_5_ = bf16[64,2304]{1,0:T(8,128)(2,1)S(1)} collective-permute-done((bf16[64,2304]{1,0:T(8,128)(2,1)S(1)}, bf16[64,2304]{1,0:T(8,128)(2,1)S(1)}, u32[]{:S(2)}, u32[]{:S(2)}) %collective-permute-start.9) | collective-permute-done | bytes 294944 | tf_op jit(solution)/shard_map/ppermute | solution.py:253
  45.1 4.2 %ladder.2 = (s16[3,400,128]{2,1,0:T(8,128)(2,1)S(1)}, s16[3,400,128]{2,1,0:T(8,128)(2,1)S(1)}, s16[3,400,128]{2,1,0:T(8,128)(2,1)S(1)}, s16[3,400,128]{2,1,0:T(8,128)(2,1)S(1)}, f32[8,128]{1,0:T(8,128)S(1)}) custom-call(bf16[1152,2304]{1,0:T(8,128)(2,1)S(1)} %bitcast.11, bf16[1152,2304]{1,0:T(8,128)(2,1)S(1)} %transpose.15.refs_2_.refs_1_, ...), custom_call_target="tpu_custom_call" | custom-call | flops 2717908992 | bytes 13910016 | tf_op jit(solution)/shard_map/ladder/pallas_call | solution.py:293
  49.3 1.4 %collective-permute-done.8.refs_1_ = s16[2,4,304,128]{3,2,1,0:T(8,128)(2,1)S(1)} collective-permute-done((s16[2,4,304,128]{3,2,1,0:T(8,128)(2,1)S(1)}, s16[2,4,304,128]{3,2,1,0:T(8,128)(2,1)S(1)}, u32[]{:S(2)}, u32[]{:S(2)}) %collective-permute-start.8) | collective-permute-done | bytes 622624 | tf_op jit(solution)/shard_map/ppermute | solution.py:481
  50.9 2.7 %collective-permute-start.16 = (s16[1,4,304,128]{3,2,1,0:T(8,128)(2,1)S(1)}, s16[1,4,304,128]{3,2,1,0:T(8,128)(2,1)S(1)}, u32[]{:S(2)}, u32[]{:S(2)}) collective-permute-start(s16[1,4,304,128]{3,2,1,0:T(8,128)(2,1)S(1)} %get-tuple-element.78), channel_id=1, source_target_pairs={{0,2},{1,3},{2,0},{3,1},{4,6},{5,7},{6,4},{7,5},{8,10},{9,11},{10,... | collective-permute-start | bytes 933896 | tf_op jit(solution)/shard_map/ppermute | solution.py:481
  53.6 0.5 collective-permute-start.10
  54.1 1.2 collective-permute-start.11
  55.3 1.7 %collective-permute-start.12 = (s16[3,400,128]{2,1,0:T(8,128)(2,1)S(1)}, s16[3,400,128]{2,1,0:T(8,128)(2,1)S(1)}, u32[]{:S(2)}, u32[]{:S(2)}) collective-permute-start(s16[3,400,128]{2,1,0:T(8,128)(2,1)S(1)} %get-tuple-element.73), channel_id=1, source_target_pairs={{0,24},{4,28},{8,16},{12,20},{16,8},{20,12},{24,0},{28,4},{1,25},{... | collective-permute-start | bytes 921608 | tf_op jit(solution)/shard_map/ppermute | solution.py:253
  57.1 4.2 %ladder.3 = (s16[3,400,128]{2,1,0:T(8,128)(2,1)S(1)}, s16[3,400,128]{2,1,0:T(8,128)(2,1)S(1)}, s16[3,400,128]{2,1,0:T(8,128)(2,1)S(1)}, s16[3,400,128]{2,1,0:T(8,128)(2,1)S(1)}, f32[8,128]{1,0:T(8,128)S(1)}) custom-call(bf16[1152,2304]{1,0:T(8,128)(2,1)S(1)} %bitcast.11, bf16[1152,2304]{1,0:T(8,128)(2,1)S(1)} %transpose.15.refs_2_.refs_1_, ...), custom_call_target="tpu_custom_call" | custom-call | flops 2717908992 | bytes 13910016 | tf_op jit(solution)/shard_map/ladder/pallas_call | solution.py:293
  61.3 4.3 %collective-permute-done.16.refs_2_ = s16[1,4,304,128]{3,2,1,0:T(8,128)(2,1)S(1)} collective-permute-done((s16[1,4,304,128]{3,2,1,0:T(8,128)(2,1)S(1)}, s16[1,4,304,128]{3,2,1,0:T(8,128)(2,1)S(1)}, u32[]{:S(2)}, u32[]{:S(2)}) %collective-permute-start.16) | collective-permute-done | bytes 311328 | tf_op jit(solution)/shard_map/ppermute | solution.py:481
  65.9 1.3 collective-permute-done.12.refs_4_
  67.1 4.7 %antisym.2 = (f32[2,1152,128]{2,1,0:T(8,128)S(1)}, s16[2,3,400,128]{3,2,1,0:T(8,128)(2,1)S(1)}, f32[8,128]{1,0:T(8,128)S(1)}) custom-call(s32[3]{0:T(128)S(1)} %pad_add_fusion.2.refs_0_, s16[3,400,128]{2,1,0:T(8,128)(2,1)S(1)} %get-tuple-element.83.refs_1_, s16[3,400,128]{2,1,0:T(8,128)(2,1)S(1)} %collective-permute-done.10.refs_2_, ...), custom_call_target="tpu_custom_call" | custom-call | flops 9437184 | bytes 3022860 | tf_op jit(solution)/shard_map/antisym/pallas_call | solution.py:293
  71.8 1.7 %collective-permute-start.19 = (s16[2,3,400,128]{3,2,1,0:T(8,128)(2,1)S(1)}, s16[2,3,400,128]{3,2,1,0:T(8,128)(2,1)S(1)}, u32[]{:S(2)}, u32[]{:S(2)}) collective-permute-start(s16[2,3,400,128]{3,2,1,0:T(8,128)(2,1)S(1)} %get-tuple-element.90), channel_id=1, source_target_pairs={{0,1},{1,0},{2,3},{3,2},{4,5},{5,4},{6,7},{7,6},{8,9},{9,8},{10,11... | collective-permute-start | bytes 1843208 | tf_op jit(solution)/shard_map/ppermute | solution.py:481
  73.5 1.4 %collective-permute-start.17 = (s16[2,304,128]{2,1,0:T(8,128)(2,1)S(1)}, s16[2,304,128]{2,1,0:T(8,128)(2,1)S(1)}, u32[]{:S(2)}, u32[]{:S(2)}) collective-permute-start(s16[2,304,128]{2,1,0:T(8,128)(2,1)S(1)} %get-tuple-element.81), channel_id=1, source_target_pairs={{0,8},{4,12},{8,0},{12,4},{16,24},{20,28},{24,16},{28,20},{1,9},{5... | collective-permute-start | bytes 466952 | tf_op jit(solution)/shard_map/ppermute | solution.py:253
  74.9 0.6 collective-permute-start.13
  75.5 1.3 collective-permute-start.14
  76.8 1.6 %collective-permute-start.15 = (s16[3,400,128]{2,1,0:T(8,128)(2,1)S(1)}, s16[3,400,128]{2,1,0:T(8,128)(2,1)S(1)}, u32[]{:S(2)}, u32[]{:S(2)}) collective-permute-start(s16[3,400,128]{2,1,0:T(8,128)(2,1)S(1)} %get-tuple-element.77), channel_id=1, source_target_pairs={{0,24},{4,28},{8,16},{12,20},{16,8},{20,12},{24,0},{28,4},{1,25},{... | collective-permute-start | bytes 921608 | tf_op jit(solution)/shard_map/ppermute | solution.py:253
  78.4 2.0 %collective-permute-done.17.refs_2_ = s16[2,304,128]{2,1,0:T(8,128)(2,1)S(1)} collective-permute-done((s16[2,304,128]{2,1,0:T(8,128)(2,1)S(1)}, s16[2,304,128]{2,1,0:T(8,128)(2,1)S(1)}, u32[]{:S(2)}, u32[]{:S(2)}) %collective-permute-start.17) | collective-permute-done | bytes 155680 | tf_op jit(solution)/shard_map/ppermute | solution.py:253
  80.5 1.3 collective-permute-start.18
  81.8 9.8 %collective-permute-done.18.refs_3_ = s16[2,304,128]{2,1,0:T(8,128)(2,1)S(1)} collective-permute-done((s16[2,304,128]{2,1,0:T(8,128)(2,1)S(1)}, s16[2,304,128]{2,1,0:T(8,128)(2,1)S(1)}, u32[]{:S(2)}, u32[]{:S(2)}) %collective-permute-start.18) | collective-permute-done | bytes 155680 | tf_op jit(solution)/shard_map/ppermute | solution.py:253
  91.6 1.1 early_antisym.1
  92.7 0.4 collective-permute-start.22
  93.2 4.7 %antisym.3 = (f32[2,1152,128]{2,1,0:T(8,128)S(1)}, s16[1,3,400,128]{3,2,1,0:T(8,128)(2,1)S(1)}, s16[1,3,400,128]{3,2,1,0:T(8,128)(2,1)S(1)}, f32[8,128]{1,0:T(8,128)S(1)}) custom-call(s32[3]{0:T(128)S(1)} %pad_add_fusion.2.refs_0_, s16[3,400,128]{2,1,0:T(8,128)(2,1)S(1)} %get-tuple-element.74.refs_1_, ...), custom_call_target="tpu_custom_call" | custom-call | flops 9437184 | bytes 3022860 | tf_op jit(solution)/shard_map/antisym/pallas_call | solution.py:293
  97.9 1.7 %collective-permute-start.21 = (s16[1,3,400,128]{3,2,1,0:T(8,128)(2,1)S(1)}, s16[1,3,400,128]{3,2,1,0:T(8,128)(2,1)S(1)}, u32[]{:S(2)}, u32[]{:S(2)}) collective-permute-start(s16[1,3,400,128]{3,2,1,0:T(8,128)(2,1)S(1)} %get-tuple-element.92), channel_id=1, source_target_pairs={{0,1},{1,0},{2,3},{3,2},{4,5},{5,4},{6,7},{7,6},{8,9},{9,8},{10,11... | collective-permute-start | bytes 921608 | tf_op jit(solution)/shard_map/ppermute | solution.py:481
  99.6 3.5 %collective-permute-start.23 = (s16[2,304,128]{2,1,0:T(8,128)(2,1)S(1)}, s16[2,304,128]{2,1,0:T(8,128)(2,1)S(1)}, u32[]{:S(2)}, u32[]{:S(2)}) collective-permute-start(s16[2,304,128]{2,1,0:T(8,128)(2,1)S(1)} %pad_add_fusion.1), channel_id=1, source_target_pairs={{0,2},{1,3},{2,0},{3,1},{4,6},{5,7},{6,4},{7,5},{8,10},{9,11},{10,... | collective-permute-start | bytes 466952 | tf_op jit(solution)/shard_map/ppermute | solution.py:481
  103.8 6.9 %collective-permute-done.23.refs_4_ = s16[2,304,128]{2,1,0:T(8,128)(2,1)S(1)} collective-permute-done((s16[2,304,128]{2,1,0:T(8,128)(2,1)S(1)}, s16[2,304,128]{2,1,0:T(8,128)(2,1)S(1)}, u32[]{:S(2)}, u32[]{:S(2)}) %collective-permute-start.23) | collective-permute-done | bytes 155680 | tf_op jit(solution)/shard_map/ppermute | solution.py:481
  110.7 1.4 %finish.3 = (f32[192,2304]{1,0:T(8,128)}, f32[8,128]{1,0:T(8,128)S(1)}) custom-call(f32[3,1,128]{2,1,0:T(1,128)S(1)} %pad_maximum_fusion.refs_0_, f32[1152,2]{1,0:T(8,128)S(1)} %bitcast.12, f32[288,128]{1,0:T(8,128)S(1)} %get-tuple-element.93.refs_2_, s16[2,304,128]{2,1,0:T(8,128)(2,1)S(1)} %collective-permute-done.22.refs_3_, ...), custom_call_target="tpu_custom_call" | custom-call | flops 2359296 | bytes 2238976 | tf_op jit(solution)/shard_map/finish/pallas_call | solution.py:293
  112.1 4.1 %collective-permute-done.21.refs_1_ = s16[1,3,400,128]{3,2,1,0:T(8,128)(2,1)S(1)} collective-permute-done((s16[1,3,400,128]{3,2,1,0:T(8,128)(2,1)S(1)}, s16[1,3,400,128]{3,2,1,0:T(8,128)(2,1)S(1)}, u32[]{:S(2)}, u32[]{:S(2)}) %collective-permute-start.21) | collective-permute-done | bytes 307232 | tf_op jit(solution)/shard_map/ppermute | solution.py:481
  116.4 1.4 %collective-permute-start.24 = (s16[1,3,400,128]{3,2,1,0:T(8,128)(2,1)S(1)}, s16[1,3,400,128]{3,2,1,0:T(8,128)(2,1)S(1)}, u32[]{:S(2)}, u32[]{:S(2)}) collective-permute-start(s16[1,3,400,128]{3,2,1,0:T(8,128)(2,1)S(1)} %get-tuple-element.100), channel_id=1, source_target_pairs={{0,2},{1,3},{2,0},{3,1},{4,6},{5,7},{6,4},{7,5},{8,10},{9,11},{10,... | collective-permute-start | bytes 921608 | tf_op jit(solution)/shard_map/ppermute | solution.py:481
  117.8 3.6 %collective-permute-done.25.refs_4_ = s16[1,3,400,128]{3,2,1,0:T(8,128)(2,1)S(1)} collective-permute-done((s16[1,3,400,128]{3,2,1,0:T(8,128)(2,1)S(1)}, s16[1,3,400,128]{3,2,1,0:T(8,128)(2,1)S(1)}, u32[]{:S(2)}, u32[]{:S(2)}) %collective-permute-start.25) | collective-permute-done | bytes 307232 | tf_op jit(solution)/shard_map/ppermute | solution.py:481
  121.3 1.4 %finish.4 = (f32[192,2304]{1,0:T(8,128)}, f32[8,128]{1,0:T(8,128)S(1)}) custom-call(f32[3,1,128]{2,1,0:T(1,128)S(1)} %pad_maximum_fusion.refs_0_, f32[1152,2]{1,0:T(8,128)S(1)} %bitcast.13, f32[2,1152,128]{2,1,0:T(8,128)S(1)} %get-tuple-element.96.refs_0_.refs_2_, ...), custom_call_target="tpu_custom_call", output_to_operand_aliasing={{0}: (5, {})} | custom-call | flops 2359296 | bytes 5650944 | tf_op jit(solution)/shard_map/finish/pallas_call | solution.py:293
  122.7 11.2 %collective-permute-done.24.refs_4_ = s16[1,3,400,128]{3,2,1,0:T(8,128)(2,1)S(1)} collective-permute-done((s16[1,3,400,128]{3,2,1,0:T(8,128)(2,1)S(1)}, s16[1,3,400,128]{3,2,1,0:T(8,128)(2,1)S(1)}, u32[]{:S(2)}, u32[]{:S(2)}) %collective-permute-start.24) | collective-permute-done | bytes 307232 | tf_op jit(solution)/shard_map/ppermute | solution.py:481
  133.9 1.4 %finish.5 = (f32[192,2304]{1,0:T(8,128)}, f32[8,128]{1,0:T(8,128)}) custom-call(f32[3,1,128]{2,1,0:T(1,128)S(1)} %pad_maximum_fusion.refs_0_, f32[1152,2]{1,0:T(8,128)S(1)} %bitcast.14, f32[2,1152,128]{2,1,0:T(8,128)S(1)} %get-tuple-element.87.refs_0_.refs_2_, ...), custom_call_target="tpu_custom_call", output_to_operand_aliasing={{0}: (5, {})} | custom-call | flops 2359296 | bytes 5343744 | tf_op jit(solution)/shard_map/finish/pallas_call | solution.py:293
  (57 shorter events, 2.8 us)
Async XLA Ops:
  0.0 17.5 %collective-permute-start.2 = (bf16[2304,1152]{1,0:T(8,128)(2,1)}, bf16[2304,1152]{1,0:T(8,128)(2,1)}, u32[]{:S(2)}, u32[]{:S(2)}) collective-permute-start(bf16[2304,1152]{1,0:T(8,128)(2,1)} %in_ref.1), channel_id=1, source_target_pairs={{0,4},{4,0},{8,12},{12,8},{16,20},{20,16},{24,28},{28,24},{1,5},{5... | collective-permute-start | bytes 15925256 | tf_op jit(solution)/shard_map/ppermute | solution.py:430
  1.4 10.5 %copy-start.1 = (bf16[192,2304]{1,0:T(8,128)(2,1)S(1)}, bf16[192,2304]{1,0:T(8,128)(2,1)}, u32[]{:S(2)}) copy-start(bf16[192,2304]{1,0:T(8,128)(2,1)} %param.5) | copy-start | bytes 2654212
  1.4 10.5 %copy-start.3 = (s32[192,2]{0,1:T(2,128)S(1)}, s32[192,2]{0,1:T(2,128)}, u32[]{:S(2)}) copy-start(s32[192,2]{0,1:T(2,128)} %param.7) | copy-start | bytes 4612
  1.5 10.5 %copy-start.4 = (f32[160]{0:T(256)S(1)}, f32[160]{0:T(256)}, u32[]{:S(2)}) copy-start(f32[160]{0:T(256)} %param.8) | copy-start | bytes 1924
  1.5 10.7 %copy-start.2 = (f32[96]{0:T(128)S(1)}, f32[96]{0:T(128)}, u32[]{:S(2)}) copy-start(f32[96]{0:T(128)} %param.9) | copy-start | bytes 1156
  1.5 11.3 %collective-permute-start = (bf16[64,2304]{1,0:T(8,128)(2,1)S(1)}, bf16[64,2304]{1,0:T(8,128)(2,1)S(1)}, u32[]{:S(2)}, u32[]{:S(2)}) collective-permute-start(bf16[64,2304]{1,0:T(8,128)(2,1)S(1)} %slice.30.refs_3_), channel_id=1, source_target_pairs={{0,8},{4,12},{8,0},{12,4},{16,24},{20,28},{24,16},{28,20},{1,9},{5... | collective-permute-start | bytes 884744 | tf_op jit(solution)/shard_map/ppermute | solution.py:253
  4.0 9.1 %collective-permute-start.1 = (bf16[64,2304]{1,0:T(8,128)(2,1)S(1)}, bf16[64,2304]{1,0:T(8,128)(2,1)S(1)}, u32[]{:S(2)}, u32[]{:S(2)}) collective-permute-start(bf16[64,2304]{1,0:T(8,128)(2,1)S(1)} %slice.30.refs_3_), channel_id=1, source_target_pairs={{0,16},{4,20},{8,24},{12,28},{16,0},{20,4},{24,8},{28,12},{1,17},{... | collective-permute-start | bytes 884744 | tf_op jit(solution)/shard_map/ppermute | solution.py:253
  9.6 2.3 %copy-start = (bf16[1152,2304]{1,0:T(8,128)(2,1)}, bf16[1152,2304]{1,0:T(8,128)(2,1)S(1)}, u32[]{:S(2)}) copy-start(bf16[1152,2304]{1,0:T(8,128)(2,1)S(1)} %transpose.14.refs_1_.refs_0_) | copy-start | bytes 15925252
  13.2 24.5 %collective-permute-start.4 = (bf16[128,2304]{1,0:T(8,128)(2,1)S(1)}, bf16[128,2304]{1,0:T(8,128)(2,1)S(1)}, u32[]{:S(2)}, u32[]{:S(2)}) collective-permute-start(bf16[128,2304]{1,0:T(8,128)(2,1)S(1)} %slice.33.refs_2_), channel_id=1, source_target_pairs={{0,16},{4,20},{8,24},{12,28},{16,0},{20,4},{24,8},{28,12},{1,17},{... | collective-permute-start | bytes 1769480 | tf_op jit(solution)/shard_map/ppermute | solution.py:253
  14.7 6.8 %collective-permute-start.6 = (bf16[32,2304]{1,0:T(8,128)(2,1)S(1)}, bf16[32,2304]{1,0:T(8,128)(2,1)S(1)}, u32[]{:S(2)}, u32[]{:S(2)}) collective-permute-start(bf16[32,2304]{1,0:T(8,128)(2,1)S(1)} %slice.35), channel_id=1, source_target_pairs={{0,8},{4,12},{8,0},{12,4},{16,24},{20,28},{24,16},{28,20},{1,9},{5... | collective-permute-start | bytes 442376 | tf_op jit(solution)/shard_map/ppermute | solution.py:253
  15.3 15.9 %collective-permute-start.7 = (bf16[32,2304]{1,0:T(8,128)(2,1)S(1)}, bf16[32,2304]{1,0:T(8,128)(2,1)S(1)}, u32[]{:S(2)}, u32[]{:S(2)}) collective-permute-start(bf16[32,2304]{1,0:T(8,128)(2,1)S(1)} %slice.36), channel_id=1, source_target_pairs={{0,16},{4,20},{8,24},{12,28},{16,0},{20,4},{24,8},{28,12},{1,17},{... | collective-permute-start | bytes 442376 | tf_op jit(solution)/shard_map/ppermute | solution.py:253
  15.7 15.5 %slice-start = ((s8[5308416]{0:T(1024)(128)(4,1)}), s8[4194304]{0:T(1024)(128)(4,1)S(1)}, s32[]{:S(2)}) async-start(s8[5308416]{0:T(1024)(128)(4,1)} %bitcast.10), calls=%async_computation | async-start | bytes 8388608
  15.8 15.4 %slice-start.1 = ((s8[5308416]{0:T(1024)(128)(4,1)}), s8[1114112]{0:T(1024)(128)(4,1)S(1)}, s32[]{:S(2)}) async-start(s8[5308416]{0:T(1024)(128)(4,1)} %bitcast.10), calls=%async_computation.1 | async-start | bytes 2228224
  15.8 22.5 %collective-permute-start.3 = (bf16[128,2304]{1,0:T(8,128)(2,1)S(1)}, bf16[128,2304]{1,0:T(8,128)(2,1)S(1)}, u32[]{:S(2)}, u32[]{:S(2)}) collective-permute-start(bf16[128,2304]{1,0:T(8,128)(2,1)S(1)} %slice.33.refs_2_), channel_id=1, source_target_pairs={{0,8},{4,12},{8,0},{12,4},{16,24},{20,28},{24,16},{28,20},{1,9},{5... | collective-permute-start | bytes 1769480 | tf_op jit(solution)/shard_map/ppermute | solution.py:253
  36.0 14.7 %collective-permute-start.8 = (s16[2,4,304,128]{3,2,1,0:T(8,128)(2,1)S(1)}, s16[2,4,304,128]{3,2,1,0:T(8,128)(2,1)S(1)}, u32[]{:S(2)}, u32[]{:S(2)}) collective-permute-start(s16[2,4,304,128]{3,2,1,0:T(8,128)(2,1)S(1)} %get-tuple-element.63), channel_id=1, source_target_pairs={{0,1},{1,0},{2,3},{3,2},{4,5},{5,4},{6,7},{7,6},{8,9},{9,8},{10,11... | collective-permute-start | bytes 1867784 | tf_op jit(solution)/shard_map/ppermute | solution.py:481
  37.7 7.4 %collective-permute-start.9 = (bf16[64,2304]{1,0:T(8,128)(2,1)S(1)}, bf16[64,2304]{1,0:T(8,128)(2,1)S(1)}, u32[]{:S(2)}, u32[]{:S(2)}) collective-permute-start(bf16[64,2304]{1,0:T(8,128)(2,1)S(1)} %slice.41), channel_id=1, source_target_pairs={{0,8},{4,12},{8,0},{12,4},{16,24},{20,28},{24,16},{28,20},{1,9},{5... | collective-permute-start | bytes 884744 | tf_op jit(solution)/shard_map/ppermute | solution.py:253
  38.3 18.7 %collective-permute-start.5 = (bf16[64,2304]{1,0:T(8,128)(2,1)S(1)}, bf16[64,2304]{1,0:T(8,128)(2,1)S(1)}, u32[]{:S(2)}, u32[]{:S(2)}) collective-permute-start(bf16[64,2304]{1,0:T(8,128)(2,1)S(1)} %slice.40), channel_id=1, source_target_pairs={{0,16},{4,20},{8,24},{12,28},{16,0},{20,4},{24,8},{28,12},{1,17},{... | collective-permute-start | bytes 884744 | tf_op jit(solution)/shard_map/ppermute | solution.py:253
  50.9 14.7 %collective-permute-start.16 = (s16[1,4,304,128]{3,2,1,0:T(8,128)(2,1)S(1)}, s16[1,4,304,128]{3,2,1,0:T(8,128)(2,1)S(1)}, u32[]{:S(2)}, u32[]{:S(2)}) collective-permute-start(s16[1,4,304,128]{3,2,1,0:T(8,128)(2,1)S(1)} %get-tuple-element.78), channel_id=1, source_target_pairs={{0,2},{1,3},{2,0},{3,1},{4,6},{5,7},{6,4},{7,5},{8,10},{9,11},{10,... | collective-permute-start | bytes 933896 | tf_op jit(solution)/shard_map/ppermute | solution.py:481
  53.6 12.3 %collective-permute-start.10 = (s16[3,400,128]{2,1,0:T(8,128)(2,1)S(1)}, s16[3,400,128]{2,1,0:T(8,128)(2,1)S(1)}, u32[]{:S(2)}, u32[]{:S(2)}) collective-permute-start(s16[3,400,128]{2,1,0:T(8,128)(2,1)S(1)} %get-tuple-element.71), channel_id=1, source_target_pairs={{0,8},{4,12},{8,0},{12,4},{16,24},{20,28},{24,16},{28,20},{1,9},{5... | collective-permute-start | bytes 921608 | tf_op jit(solution)/shard_map/ppermute | solution.py:253
  54.1 11.8 %collective-permute-start.11 = (s16[3,400,128]{2,1,0:T(8,128)(2,1)S(1)}, s16[3,400,128]{2,1,0:T(8,128)(2,1)S(1)}, u32[]{:S(2)}, u32[]{:S(2)}) collective-permute-start(s16[3,400,128]{2,1,0:T(8,128)(2,1)S(1)} %get-tuple-element.72), channel_id=1, source_target_pairs={{0,16},{4,20},{8,24},{12,28},{16,0},{20,4},{24,8},{28,12},{1,17},{... | collective-permute-start | bytes 921608 | tf_op jit(solution)/shard_map/ppermute | solution.py:253
  55.3 11.8 %collective-permute-start.12 = (s16[3,400,128]{2,1,0:T(8,128)(2,1)S(1)}, s16[3,400,128]{2,1,0:T(8,128)(2,1)S(1)}, u32[]{:S(2)}, u32[]{:S(2)}) collective-permute-start(s16[3,400,128]{2,1,0:T(8,128)(2,1)S(1)} %get-tuple-element.73), channel_id=1, source_target_pairs={{0,24},{4,28},{8,16},{12,20},{16,8},{20,12},{24,0},{28,4},{1,25},{... | collective-permute-start | bytes 921608 | tf_op jit(solution)/shard_map/ppermute | solution.py:253
  71.8 26.0 %collective-permute-start.19 = (s16[2,3,400,128]{3,2,1,0:T(8,128)(2,1)S(1)}, s16[2,3,400,128]{3,2,1,0:T(8,128)(2,1)S(1)}, u32[]{:S(2)}, u32[]{:S(2)}) collective-permute-start(s16[2,3,400,128]{3,2,1,0:T(8,128)(2,1)S(1)} %get-tuple-element.90), channel_id=1, source_target_pairs={{0,1},{1,0},{2,3},{3,2},{4,5},{5,4},{6,7},{7,6},{8,9},{9,8},{10,11... | collective-permute-start | bytes 1843208 | tf_op jit(solution)/shard_map/ppermute | solution.py:481
  73.5 7.0 %collective-permute-start.17 = (s16[2,304,128]{2,1,0:T(8,128)(2,1)S(1)}, s16[2,304,128]{2,1,0:T(8,128)(2,1)S(1)}, u32[]{:S(2)}, u32[]{:S(2)}) collective-permute-start(s16[2,304,128]{2,1,0:T(8,128)(2,1)S(1)} %get-tuple-element.81), channel_id=1, source_target_pairs={{0,8},{4,12},{8,0},{12,4},{16,24},{20,28},{24,16},{28,20},{1,9},{5... | collective-permute-start | bytes 466952 | tf_op jit(solution)/shard_map/ppermute | solution.py:253
  74.9 18.2 %collective-permute-start.13 = (s16[3,400,128]{2,1,0:T(8,128)(2,1)S(1)}, s16[3,400,128]{2,1,0:T(8,128)(2,1)S(1)}, u32[]{:S(2)}, u32[]{:S(2)}) collective-permute-start(s16[3,400,128]{2,1,0:T(8,128)(2,1)S(1)} %get-tuple-element.75), channel_id=1, source_target_pairs={{0,8},{4,12},{8,0},{12,4},{16,24},{20,28},{24,16},{28,20},{1,9},{5... | collective-permute-start | bytes 921608 | tf_op jit(solution)/shard_map/ppermute | solution.py:253
  75.5 17.6 %collective-permute-start.14 = (s16[3,400,128]{2,1,0:T(8,128)(2,1)S(1)}, s16[3,400,128]{2,1,0:T(8,128)(2,1)S(1)}, u32[]{:S(2)}, u32[]{:S(2)}) collective-permute-start(s16[3,400,128]{2,1,0:T(8,128)(2,1)S(1)} %get-tuple-element.76), channel_id=1, source_target_pairs={{0,16},{4,20},{8,24},{12,28},{16,0},{20,4},{24,8},{28,12},{1,17},{... | collective-permute-start | bytes 921608 | tf_op jit(solution)/shard_map/ppermute | solution.py:253
  76.8 16.3 %collective-permute-start.15 = (s16[3,400,128]{2,1,0:T(8,128)(2,1)S(1)}, s16[3,400,128]{2,1,0:T(8,128)(2,1)S(1)}, u32[]{:S(2)}, u32[]{:S(2)}) collective-permute-start(s16[3,400,128]{2,1,0:T(8,128)(2,1)S(1)} %get-tuple-element.77), channel_id=1, source_target_pairs={{0,24},{4,28},{8,16},{12,20},{16,8},{20,12},{24,0},{28,4},{1,25},{... | collective-permute-start | bytes 921608 | tf_op jit(solution)/shard_map/ppermute | solution.py:253
  80.5 11.1 %collective-permute-start.18 = (s16[2,304,128]{2,1,0:T(8,128)(2,1)S(1)}, s16[2,304,128]{2,1,0:T(8,128)(2,1)S(1)}, u32[]{:S(2)}, u32[]{:S(2)}) collective-permute-start(s16[2,304,128]{2,1,0:T(8,128)(2,1)S(1)} %pad_add_fusion), channel_id=1, source_target_pairs={{0,16},{4,20},{8,24},{12,28},{16,0},{20,4},{24,8},{28,12},{1,17},{... | collective-permute-start | bytes 466952 | tf_op jit(solution)/shard_map/ppermute | solution.py:253
  92.7 6.9 %collective-permute-start.22 = (s16[2,304,128]{2,1,0:T(8,128)(2,1)S(1)}, s16[2,304,128]{2,1,0:T(8,128)(2,1)S(1)}, u32[]{:S(2)}, u32[]{:S(2)}) collective-permute-start(s16[2,304,128]{2,1,0:T(8,128)(2,1)S(1)} %get-tuple-element.94), channel_id=1, source_target_pairs={{0,1},{1,0},{2,3},{3,2},{4,5},{5,4},{6,7},{7,6},{8,9},{9,8},{10,11... | collective-permute-start | bytes 466952 | tf_op jit(solution)/shard_map/ppermute | solution.py:481
  97.9 18.3 %collective-permute-start.21 = (s16[1,3,400,128]{3,2,1,0:T(8,128)(2,1)S(1)}, s16[1,3,400,128]{3,2,1,0:T(8,128)(2,1)S(1)}, u32[]{:S(2)}, u32[]{:S(2)}) collective-permute-start(s16[1,3,400,128]{3,2,1,0:T(8,128)(2,1)S(1)} %get-tuple-element.92), channel_id=1, source_target_pairs={{0,1},{1,0},{2,3},{3,2},{4,5},{5,4},{6,7},{7,6},{8,9},{9,8},{10,11... | collective-permute-start | bytes 921608 | tf_op jit(solution)/shard_map/ppermute | solution.py:481
  99.6 11.1 %collective-permute-start.23 = (s16[2,304,128]{2,1,0:T(8,128)(2,1)S(1)}, s16[2,304,128]{2,1,0:T(8,128)(2,1)S(1)}, u32[]{:S(2)}, u32[]{:S(2)}) collective-permute-start(s16[2,304,128]{2,1,0:T(8,128)(2,1)S(1)} %pad_add_fusion.1), channel_id=1, source_target_pairs={{0,2},{1,3},{2,0},{3,1},{4,6},{5,7},{6,4},{7,5},{8,10},{9,11},{10,... | collective-permute-start | bytes 466952 | tf_op jit(solution)/shard_map/ppermute | solution.py:481
  103.1 19.6 %collective-permute-start.20 = (s16[1,3,400,128]{3,2,1,0:T(8,128)(2,1)S(1)}, s16[1,3,400,128]{3,2,1,0:T(8,128)(2,1)S(1)}, u32[]{:S(2)}, u32[]{:S(2)}) collective-permute-start(s16[1,3,400,128]{3,2,1,0:T(8,128)(2,1)S(1)} %get-tuple-element.91), channel_id=1, source_target_pairs={{0,1},{1,0},{2,3},{3,2},{4,5},{5,4},{6,7},{7,6},{8,9},{9,8},{10,11... | collective-permute-start | bytes 921608 | tf_op jit(solution)/shard_map/ppermute | solution.py:481
  103.6 17.7 %collective-permute-start.25 = (s16[1,3,400,128]{3,2,1,0:T(8,128)(2,1)S(1)}, s16[1,3,400,128]{3,2,1,0:T(8,128)(2,1)S(1)}, u32[]{:S(2)}, u32[]{:S(2)}) collective-permute-start(s16[1,3,400,128]{3,2,1,0:T(8,128)(2,1)S(1)} %get-tuple-element.101), channel_id=1, source_target_pairs={{0,2},{1,3},{2,0},{3,1},{4,6},{5,7},{6,4},{7,5},{8,10},{9,11},{10,... | collective-permute-start | bytes 921608 | tf_op jit(solution)/shard_map/ppermute | solution.py:481
  116.4 17.6 %collective-permute-start.24 = (s16[1,3,400,128]{3,2,1,0:T(8,128)(2,1)S(1)}, s16[1,3,400,128]{3,2,1,0:T(8,128)(2,1)S(1)}, u32[]{:S(2)}, u32[]{:S(2)}) collective-permute-start(s16[1,3,400,128]{3,2,1,0:T(8,128)(2,1)S(1)} %get-tuple-element.100), channel_id=1, source_target_pairs={{0,2},{1,3},{2,0},{3,1},{4,6},{5,7},{6,4},{7,5},{8,10},{9,11},{10,... | collective-permute-start | bytes 921608 | tf_op jit(solution)/shard_map/ppermute | solution.py:481

commit v12 on v10

--- a/solution.py
+++ b/solution.py
@@ -516,7 +516,8 @@
         got, places = yield from halved(parts, [across(away, 1)])
         mine, *sums = yield early_sum(places, parts, got)
         arrived = by_steps(to_chip, *sums)
-        turns.append(turns[-1] + arrived)
+        steps.append(arrived[0])
+        yield None
         own, *blocks = yield early_antisym([mine, *arrived])
         yield finish(r, own, by_steps(across, *blocks), None, update)
 
@@ -525,6 +526,8 @@
         if turns:
             sums, _ = lax.optimization_barrier((sums, turns[-1] + results[-1][:1]))
         arrived = [to_chip(sums[d], d) for d in range(1, chips)]
+        if steps:
+            arrived, _ = lax.optimization_barrier((arrived, steps[:1]))
         turns.append(arrived)
         parcels = slabs // 2 if r == chunks - 1 else 1
         parts, *away = yield antisym(parcels, [sums[0], *arrived])
@@ -540,20 +543,24 @@
     def when(stage):
         r, k = stage
         if early and r == 0:
-            return (20, *[41] * hops, 54, 66, 83)[k]
+            return (20, *[41] * hops, 54, 55, 66, 90)[k]
         if k == 0:
             return 37 + 5 * r if early else 30 + 5 * r
-        return 15 * r + (45 if early else 54) + (k - 1) * 17 - (1 if k == 2 + hops else 0)
-
-    order = [(r, k) for r in range(chunks) for k in range(3 + hops + (early and r == 0))]
+        start = 15 * r + (45 if early else 54)
+        return start + (k - 1) * (14 if early else 17) - (1 if k == 2 + hops else 0)
+
+    order = [(r, k) for r in range(chunks) for k in range(3 + hops + 2 * (early and r == 0))]
     order = sorted(order, key=when)
 
-    turns, firsts = [], []
+    turns, firsts, steps = [], [], []
     running = [early_stages(r) if early and r == 0 else stages(r) for r in range(chunks)]
     results = [None] * chunks
     update, token = None, jnp.zeros((8, LANES), jnp.float32)
     for r, k in order:
-        call, inputs = running[r].send(results[r])
+        step = running[r].send(results[r])
+        if step is None:
+            continue
+        call, inputs = step
         *results[r], token = call(token, *inputs)
         if results[r][0].shape == (num_pairs, 2 * part_rows):
             update = results[r][0]

time: 127 us -> 137 us (1.079)
  waiting for transfers between devices: 52.5 us -> 57.9 us
  starting transfers between devices: 31 us -> 35.5 us
    ppermute x9, waiting for transfers between devices: 24.6 us -> 33.5 us  [across(): return lax.ppermute(x, 'slab', [(i, i ^ level) for i in range(slabs)])]
    ppermute x9, starting transfers between devices: 11.7 us -> 15.6 us  [across(): return lax.ppermute(x, 'slab', [(i, i ^ level) for i in range(slabs)])]
    ppermute x16, waiting for transfers between devices: 27.9 us -> 24.4 us  [to_chip(): return lax.ppermute(x, 'pair', [(i, i ^ d * CORES) for i in range(devices)])]
  transfers between devices with their start and end apart: 26 -> 26, of which waited for: 12 -> 9; matrix products, arithmetic and copies ran while one was open for 3% -> 2% of each run, Pallas kernels for 28% -> 23%
where the time goes in v12:
time: 137 us
  waiting for transfers between devices  57.9 us (42%)
  Pallas kernels  37.4 us (27%)
  starting transfers between devices  35.5 us (26%)
  local copies, waits for them, and re-layouts  5.14 us (4%)
    ppermute x9, waiting for transfers between devices, across(): return lax.ppermute(x, 'slab', [(i, i ^ level) for i in range(slabs)])  33.5 us
    pallas_call x13, Pallas kernels, call(): pl.pallas_call(kernel, in_specs=[*in_specs, vmem], out_specs=[*out_specs,...  28.8 us
    ppermute x16, waiting for transfers between devices, to_chip(): return lax.ppermute(x, 'pair', [(i, i ^ d * CORES) for i in range(devices)])  24.4 us
    ppermute x16, starting transfers between devices, to_chip(): return lax.ppermute(x, 'pair', [(i, i ^ d * CORES) for i in range(devices)])  19.5 us
    ppermute x9, starting transfers between devices, across(): return lax.ppermute(x, 'slab', [(i, i ^ level) for i in range(slabs)])  15.6 us
    pallas_call x1, Pallas kernels, on_device(): sib_t = transpose(swapped)  4.65 us
    pallas_call x1, Pallas kernels, on_device(): own_t = transpose(in_hbm(integrals))  4 us
  transfers between devices with their start and end apart: 26, of which 9 were waited for; matrix products, arithmetic and copies ran while one was open for 2% of the time, Pallas kernels for 23%

profile of v12, /device:TPU:0, one launch (start us, length us, event | category | flops | bytes accessed | tf_op | source)
XLA Modules:
  0.0 136.8 jit_solution(12150125097572881532)
XLA Ops:
  0.0 0.5 collective-permute-start.4
  0.5 1.0 slice.30.refs_3_
  1.5 2.6 %collective-permute-start = (bf16[64,2304]{1,0:T(8,128)(2,1)S(1)}, bf16[64,2304]{1,0:T(8,128)(2,1)S(1)}, u32[]{:S(2)}, u32[]{:S(2)}) collective-permute-start(bf16[64,2304]{1,0:T(8,128)(2,1)S(1)} %slice.30.refs_3_), channel_id=1, source_target_pairs={{0,8},{4,12},{8,0},{12,4},{16,24},{20,28},{24,16},{28,20},{1,9},{5... | collective-permute-start | bytes 884744 | tf_op jit(solution)/shard_map/ppermute | solution.py:253
  4.0 1.5 %collective-permute-start.1 = (bf16[64,2304]{1,0:T(8,128)(2,1)S(1)}, bf16[64,2304]{1,0:T(8,128)(2,1)S(1)}, u32[]{:S(2)}, u32[]{:S(2)}) collective-permute-start(bf16[64,2304]{1,0:T(8,128)(2,1)S(1)} %slice.30.refs_3_), channel_id=1, source_target_pairs={{0,16},{4,20},{8,24},{12,28},{16,0},{20,4},{24,8},{28,12},{1,17},{... | collective-permute-start | bytes 884744 | tf_op jit(solution)/shard_map/ppermute | solution.py:253
  5.6 4.0 %transpose.14.refs_1_.refs_0_ = bf16[1152,2304]{1,0:T(8,128)(2,1)S(1)} custom-call(bf16[2304,1152]{1,0:T(8,128)(2,1)} %in_ref.1), custom_call_target="tpu_custom_call" | custom-call | bytes 10616832 | tf_op jit(solution)/shard_map/transpose/pallas_call | solution.py:429
  9.6 2.3 %copy-done = bf16[1152,2304]{1,0:T(8,128)(2,1)} copy-done((bf16[1152,2304]{1,0:T(8,128)(2,1)}, bf16[1152,2304]{1,0:T(8,128)(2,1)S(1)}, u32[]{:S(2)}) %copy-start) | copy-done | bytes 5308440
  12.7 0.5 collective-permute-done.1.refs_5_
  13.2 0.7 slice.33
  14.2 0.7 slice.34
  14.9 1.7 %collective-permute-start.3 = (bf16[32,2304]{1,0:T(8,128)(2,1)}, bf16[32,2304]{1,0:T(8,128)(2,1)S(1)}, u32[]{:S(2)}, u32[]{:S(2)}) collective-permute-start(bf16[32,2304]{1,0:T(8,128)(2,1)} %slice.34), channel_id=1, source_target_pairs={{0,16},{4,20},{8,24},{12,28},{16,0},{20,4},{24,8},{28,12},{1,17},{... | collective-permute-start | bytes 442376 | tf_op jit(solution)/shard_map/ppermute | solution.py:253
  16.7 4.7 %transpose.15.refs_2_.refs_1_ = bf16[1152,2304]{1,0:T(8,128)(2,1)S(1)} custom-call(bf16[2304,1152]{1,0:T(8,128)(2,1)} %collective-permute-done.4.in_ref), custom_call_target="tpu_custom_call" | custom-call | bytes 10616832 | tf_op jit(solution)/shard_map/transpose/pallas_call | solution.py:431
  21.4 0.6 collective-permute-start.6
  22.0 1.5 %collective-permute-start.5 = (bf16[128,2304]{1,0:T(8,128)(2,1)S(1)}, bf16[128,2304]{1,0:T(8,128)(2,1)S(1)}, u32[]{:S(2)}, u32[]{:S(2)}) collective-permute-start(bf16[128,2304]{1,0:T(8,128)(2,1)S(1)} %slice.35.refs_2_), channel_id=1, source_target_pairs={{0,8},{4,12},{8,0},{12,4},{16,24},{20,28},{24,16},{28,20},{1,9},{5... | collective-permute-start | bytes 1769480 | tf_op jit(solution)/shard_map/ppermute | solution.py:253
  23.5 4.8 %early_ladder.1 = (f32[2,1152,128]{2,1,0:T(8,128)S(1)}, s16[2,4,304,128]{3,2,1,0:T(8,128)(2,1)S(1)}, f32[8,128]{1,0:T(8,128)S(1)}) custom-call(s32[3]{0:T(128)S(1)} %pad_add_fusion.2.refs_0_, bf16[1152,2304]{1,0:T(8,128)(2,1)S(1)} %bitcast.11, bf16[1152,2304]{1,0:T(8,128)(2,1)S(1)} %transpose.15.refs_2_.refs_1_, bf16[64,2304]{1,0:T(8,128)(2,1)S(1)} %slice.30.refs_3_, ...), custom_call_target="tpu_custom_call" | custom-call | flops 2717908992 | bytes 13598732 | tf_op jit(solution)/shard_map/early_ladder/pallas_call | solution.py:293
  28.3 1.6 %collective-permute-start.9 = (s16[2,4,304,128]{3,2,1,0:T(8,128)(2,1)S(1)}, s16[2,4,304,128]{3,2,1,0:T(8,128)(2,1)S(1)}, u32[]{:S(2)}, u32[]{:S(2)}) collective-permute-start(s16[2,4,304,128]{3,2,1,0:T(8,128)(2,1)S(1)} %get-tuple-element.83), channel_id=1, source_target_pairs={{0,1},{1,0},{2,3},{3,2},{4,5},{5,4},{6,7},{7,6},{8,9},{9,8},{10,11... | collective-permute-start | bytes 1867784 | tf_op jit(solution)/shard_map/ppermute | solution.py:484
  30.0 5.6 %collective-permute-done.6.refs_4_ = bf16[128,2304]{1,0:T(8,128)(2,1)S(1)} collective-permute-done((bf16[128,2304]{1,0:T(8,128)(2,1)S(1)}, bf16[128,2304]{1,0:T(8,128)(2,1)S(1)}, u32[]{:S(2)}, u32[]{:S(2)}) %collective-permute-start.6) | collective-permute-done | bytes 589856 | tf_op jit(solution)/shard_map/ppermute | solution.py:253
  35.6 1.5 %collective-permute-start.8 = (bf16[64,2304]{1,0:T(8,128)(2,1)S(1)}, bf16[64,2304]{1,0:T(8,128)(2,1)S(1)}, u32[]{:S(2)}, u32[]{:S(2)}) collective-permute-start(bf16[64,2304]{1,0:T(8,128)(2,1)S(1)} %slice.41), channel_id=1, source_target_pairs={{0,8},{4,12},{8,0},{12,4},{16,24},{20,28},{24,16},{28,20},{1,9},{5... | collective-permute-start | bytes 884744 | tf_op jit(solution)/shard_map/ppermute | solution.py:253
  37.1 0.8 collective-permute-start.7
  37.9 4.8 %collective-permute-done.9.refs_1_ = s16[2,4,304,128]{3,2,1,0:T(8,128)(2,1)S(1)} collective-permute-done((s16[2,4,304,128]{3,2,1,0:T(8,128)(2,1)S(1)}, s16[2,4,304,128]{3,2,1,0:T(8,128)(2,1)S(1)}, u32[]{:S(2)}, u32[]{:S(2)}) %collective-permute-start.9) | collective-permute-done | bytes 622624 | tf_op jit(solution)/shard_map/ppermute | solution.py:484
  42.9 2.7 %collective-permute-start.13 = (s16[1,4,304,128]{3,2,1,0:T(8,128)(2,1)S(1)}, s16[1,4,304,128]{3,2,1,0:T(8,128)(2,1)S(1)}, u32[]{:S(2)}, u32[]{:S(2)}) collective-permute-start(s16[1,4,304,128]{3,2,1,0:T(8,128)(2,1)S(1)} %get-tuple-element.94), channel_id=1, source_target_pairs={{0,2},{1,3},{2,0},{3,1},{4,6},{5,7},{6,4},{7,5},{8,10},{9,11},{10,... | collective-permute-start | bytes 933896 | tf_op jit(solution)/shard_map/ppermute | solution.py:484
  45.5 4.2 %ladder.2 = (s16[3,400,128]{2,1,0:T(8,128)(2,1)S(1)}, s16[3,400,128]{2,1,0:T(8,128)(2,1)S(1)}, s16[3,400,128]{2,1,0:T(8,128)(2,1)S(1)}, s16[3,400,128]{2,1,0:T(8,128)(2,1)S(1)}, f32[8,128]{1,0:T(8,128)S(1)}) custom-call(bf16[1152,2304]{1,0:T(8,128)(2,1)S(1)} %bitcast.11, bf16[1152,2304]{1,0:T(8,128)(2,1)S(1)} %transpose.15.refs_2_.refs_1_, ...), custom_call_target="tpu_custom_call" | custom-call | flops 2717908992 | bytes 13910016 | tf_op jit(solution)/shard_map/ladder/pallas_call | solution.py:293
  49.8 0.6 collective-permute-start.10
  50.4 1.5 %collective-permute-start.11 = (s16[3,400,128]{2,1,0:T(8,128)(2,1)S(1)}, s16[3,400,128]{2,1,0:T(8,128)(2,1)S(1)}, u32[]{:S(2)}, u32[]{:S(2)}) collective-permute-start(s16[3,400,128]{2,1,0:T(8,128)(2,1)S(1)} %get-tuple-element.92), channel_id=1, source_target_pairs={{0,16},{4,20},{8,24},{12,28},{16,0},{20,4},{24,8},{28,12},{1,17},{... | collective-permute-start | bytes 921608 | tf_op jit(solution)/shard_map/ppermute | solution.py:253
  51.9 1.4 %collective-permute-start.12 = (s16[3,400,128]{2,1,0:T(8,128)(2,1)S(1)}, s16[3,400,128]{2,1,0:T(8,128)(2,1)S(1)}, u32[]{:S(2)}, u32[]{:S(2)}) collective-permute-start(s16[3,400,128]{2,1,0:T(8,128)(2,1)S(1)} %get-tuple-element.93), channel_id=1, source_target_pairs={{0,24},{4,28},{8,16},{12,20},{16,8},{20,12},{24,0},{28,4},{1,25},{... | collective-permute-start | bytes 921608 | tf_op jit(solution)/shard_map/ppermute | solution.py:253
  53.3 4.2 %ladder.3 = (s16[3,400,128]{2,1,0:T(8,128)(2,1)S(1)}, s16[3,400,128]{2,1,0:T(8,128)(2,1)S(1)}, s16[3,400,128]{2,1,0:T(8,128)(2,1)S(1)}, s16[3,400,128]{2,1,0:T(8,128)(2,1)S(1)}, f32[8,128]{1,0:T(8,128)S(1)}) custom-call(bf16[1152,2304]{1,0:T(8,128)(2,1)S(1)} %bitcast.11, bf16[1152,2304]{1,0:T(8,128)(2,1)S(1)} %transpose.15.refs_2_.refs_1_, ...), custom_call_target="tpu_custom_call" | custom-call | flops 2717908992 | bytes 13910016 | tf_op jit(solution)/shard_map/ladder/pallas_call | solution.py:293
  57.9 0.6 collective-permute-start.14
  58.5 7.7 %collective-permute-done.14.refs_2_ = s16[2,304,128]{2,1,0:T(8,128)(2,1)S(1)} collective-permute-done((s16[2,304,128]{2,1,0:T(8,128)(2,1)S(1)}, s16[2,304,128]{2,1,0:T(8,128)(2,1)S(1)}, u32[]{:S(2)}, u32[]{:S(2)}) %collective-permute-start.14) | collective-permute-done | bytes 155680 | tf_op jit(solution)/shard_map/ppermute | solution.py:253
  66.1 4.7 %antisym.2 = (f32[2,1152,128]{2,1,0:T(8,128)S(1)}, s16[2,3,400,128]{3,2,1,0:T(8,128)(2,1)S(1)}, f32[8,128]{1,0:T(8,128)S(1)}) custom-call(s32[3]{0:T(128)S(1)} %pad_add_fusion.2.refs_0_, s16[3,400,128]{2,1,0:T(8,128)(2,1)S(1)} %get-tuple-element.107.refs_1_, s16[3,400,128]{2,1,0:T(8,128)(2,1)S(1)} %collective-permute-done.10.refs_2_, ...), custom_call_target="tpu_custom_call" | custom-call | flops 9437184 | bytes 3022860 | tf_op jit(solution)/shard_map/antisym/pallas_call | solution.py:293
  70.8 1.7 %collective-permute-start.18 = (s16[2,3,400,128]{3,2,1,0:T(8,128)(2,1)S(1)}, s16[2,3,400,128]{3,2,1,0:T(8,128)(2,1)S(1)}, u32[]{:S(2)}, u32[]{:S(2)}) collective-permute-start(s16[2,3,400,128]{3,2,1,0:T(8,128)(2,1)S(1)} %get-tuple-element.110), channel_id=1, source_target_pairs={{0,1},{1,0},{2,3},{3,2},{4,5},{5,4},{6,7},{7,6},{8,9},{9,8},{10,11... | collective-permute-start | bytes 1843208 | tf_op jit(solution)/shard_map/ppermute | solution.py:484
  72.5 0.5 collective-permute-start.15
  73.0 1.5 %collective-permute-start.16 = (s16[3,400,128]{2,1,0:T(8,128)(2,1)S(1)}, s16[3,400,128]{2,1,0:T(8,128)(2,1)S(1)}, u32[]{:S(2)}, u32[]{:S(2)}) collective-permute-start(s16[3,400,128]{2,1,0:T(8,128)(2,1)S(1)} %get-tuple-element.102), channel_id=1, source_target_pairs={{0,16},{4,20},{8,24},{12,28},{16,0},{20,4},{24,8},{28,12},{1,17},{... | collective-permute-start | bytes 921608 | tf_op jit(solution)/shard_map/ppermute | solution.py:253
  74.5 1.5 %collective-permute-start.17 = (s16[3,400,128]{2,1,0:T(8,128)(2,1)S(1)}, s16[3,400,128]{2,1,0:T(8,128)(2,1)S(1)}, u32[]{:S(2)}, u32[]{:S(2)}) collective-permute-start(s16[3,400,128]{2,1,0:T(8,128)(2,1)S(1)} %get-tuple-element.103), channel_id=1, source_target_pairs={{0,24},{4,28},{8,16},{12,20},{16,8},{20,12},{24,0},{28,4},{1,25},{... | collective-permute-start | bytes 921608 | tf_op jit(solution)/shard_map/ppermute | solution.py:253
  76.0 1.4 %collective-permute-start.19 = (s16[2,304,128]{2,1,0:T(8,128)(2,1)S(1)}, s16[2,304,128]{2,1,0:T(8,128)(2,1)S(1)}, u32[]{:S(2)}, u32[]{:S(2)}) collective-permute-start(s16[2,304,128]{2,1,0:T(8,128)(2,1)S(1)} %pad_add_fusion), channel_id=1, source_target_pairs={{0,16},{4,20},{8,24},{12,28},{16,0},{20,4},{24,8},{28,12},{1,17},{... | collective-permute-start | bytes 466952 | tf_op jit(solution)/shard_map/ppermute | solution.py:253
  77.4 10.7 %collective-permute-done.19.refs_3_ = s16[2,304,128]{2,1,0:T(8,128)(2,1)S(1)} collective-permute-done((s16[2,304,128]{2,1,0:T(8,128)(2,1)S(1)}, s16[2,304,128]{2,1,0:T(8,128)(2,1)S(1)}, u32[]{:S(2)}, u32[]{:S(2)}) %collective-permute-start.19) | collective-permute-done | bytes 155680 | tf_op jit(solution)/shard_map/ppermute | solution.py:253
  88.1 1.1 early_antisym.1
  89.4 3.5 %collective-permute-start.22 = (s16[1,3,400,128]{3,2,1,0:T(8,128)(2,1)S(1)}, s16[1,3,400,128]{3,2,1,0:T(8,128)(2,1)S(1)}, u32[]{:S(2)}, u32[]{:S(2)}) collective-permute-start(s16[1,3,400,128]{3,2,1,0:T(8,128)(2,1)S(1)} %get-tuple-element.121), channel_id=1, source_target_pairs={{0,2},{1,3},{2,0},{3,1},{4,6},{5,7},{6,4},{7,5},{8,10},{9,11},{10,... | collective-permute-start | bytes 921608 | tf_op jit(solution)/shard_map/ppermute | solution.py:484
  92.9 4.7 %antisym.3 = (f32[2,1152,128]{2,1,0:T(8,128)S(1)}, s16[1,3,400,128]{3,2,1,0:T(8,128)(2,1)S(1)}, s16[1,3,400,128]{3,2,1,0:T(8,128)(2,1)S(1)}, f32[8,128]{1,0:T(8,128)S(1)}) custom-call(s32[3]{0:T(128)S(1)} %pad_add_fusion.2.refs_0_, s16[3,400,128]{2,1,0:T(8,128)(2,1)S(1)} %get-tuple-element.100.refs_1_, ...), custom_call_target="tpu_custom_call" | custom-call | flops 9437184 | bytes 3022860 | tf_op jit(solution)/shard_map/antisym/pallas_call | solution.py:293
  97.6 0.4 collective-permute-start.21
  98.0 1.7 %collective-permute-start.24 = (s16[2,304,128]{2,1,0:T(8,128)(2,1)S(1)}, s16[2,304,128]{2,1,0:T(8,128)(2,1)S(1)}, u32[]{:S(2)}, u32[]{:S(2)}) collective-permute-start(s16[2,304,128]{2,1,0:T(8,128)(2,1)S(1)} %get-tuple-element.126), channel_id=1, source_target_pairs={{0,1},{1,0},{2,3},{3,2},{4,5},{5,4},{6,7},{7,6},{8,9},{9,8},{10,11... | collective-permute-start | bytes 466952 | tf_op jit(solution)/shard_map/ppermute | solution.py:484
  99.7 0.4 collective-permute-start.20
  100.0 4.7 %collective-permute-done.22.refs_4_ = s16[1,3,400,128]{3,2,1,0:T(8,128)(2,1)S(1)} collective-permute-done((s16[1,3,400,128]{3,2,1,0:T(8,128)(2,1)S(1)}, s16[1,3,400,128]{3,2,1,0:T(8,128)(2,1)S(1)}, u32[]{:S(2)}, u32[]{:S(2)}) %collective-permute-start.22) | collective-permute-done | bytes 307232 | tf_op jit(solution)/shard_map/ppermute | solution.py:484
  104.7 1.4 %finish.3 = (f32[192,2304]{1,0:T(8,128)}, f32[8,128]{1,0:T(8,128)S(1)}) custom-call(f32[3,1,128]{2,1,0:T(1,128)S(1)} %pad_maximum_fusion.refs_0_, f32[1152,2]{1,0:T(8,128)S(1)} %bitcast.12, f32[2,1152,128]{2,1,0:T(8,128)S(1)} %get-tuple-element.109.refs_0_.refs_2_, s16[2,3,400,128]{3,2,1,0:T(8,128)(2,1)S(1)} %collective-permute-done.18.refs_1_.refs_3_, ...), custom_call_target="tpu_custom_call" | custom-call | flops 2359296 | bytes 3881472 | tf_op jit(solution)/shard_map/finish/pallas_call | solution.py:293
  106.1 5.2 %collective-permute-done.21.refs_1_ = s16[1,3,400,128]{3,2,1,0:T(8,128)(2,1)S(1)} collective-permute-done((s16[1,3,400,128]{3,2,1,0:T(8,128)(2,1)S(1)}, s16[1,3,400,128]{3,2,1,0:T(8,128)(2,1)S(1)}, u32[]{:S(2)}, u32[]{:S(2)}) %collective-permute-start.21) | collective-permute-done | bytes 307232 | tf_op jit(solution)/shard_map/ppermute | solution.py:484
  111.6 3.1 %collective-permute-done.24.refs_3_ = s16[2,304,128]{2,1,0:T(8,128)(2,1)S(1)} collective-permute-done((s16[2,304,128]{2,1,0:T(8,128)(2,1)S(1)}, s16[2,304,128]{2,1,0:T(8,128)(2,1)S(1)}, u32[]{:S(2)}, u32[]{:S(2)}) %collective-permute-start.24) | collective-permute-done | bytes 155680 | tf_op jit(solution)/shard_map/ppermute | solution.py:484
  114.7 3.6 %collective-permute-start.25 = (s16[2,304,128]{2,1,0:T(8,128)(2,1)S(1)}, s16[2,304,128]{2,1,0:T(8,128)(2,1)S(1)}, u32[]{:S(2)}, u32[]{:S(2)}) collective-permute-start(s16[2,304,128]{2,1,0:T(8,128)(2,1)S(1)} %pad_add_fusion.1), channel_id=1, source_target_pairs={{0,2},{1,3},{2,0},{3,1},{4,6},{5,7},{6,4},{7,5},{8,10},{9,11},{10,... | collective-permute-start | bytes 466952 | tf_op jit(solution)/shard_map/ppermute | solution.py:484
  118.3 15.7 %collective-permute-done.25.refs_4_ = s16[2,304,128]{2,1,0:T(8,128)(2,1)S(1)} collective-permute-done((s16[2,304,128]{2,1,0:T(8,128)(2,1)S(1)}, s16[2,304,128]{2,1,0:T(8,128)(2,1)S(1)}, u32[]{:S(2)}, u32[]{:S(2)}) %collective-permute-start.25) | collective-permute-done | bytes 155680 | tf_op jit(solution)/shard_map/ppermute | solution.py:484
  134.0 1.4 %finish.4 = (f32[192,2304]{1,0:T(8,128)}, f32[8,128]{1,0:T(8,128)S(1)}) custom-call(f32[3,1,128]{2,1,0:T(1,128)S(1)} %pad_maximum_fusion.refs_0_, f32[1152,2]{1,0:T(8,128)S(1)} %bitcast.13, f32[288,128]{1,0:T(8,128)S(1)} %get-tuple-element.125.refs_2_, s16[2,304,128]{2,1,0:T(8,128)(2,1)S(1)} %collective-permute-done.24.refs_3_, ...), custom_call_target="tpu_custom_call", output_to_operand_aliasing={{0}: (5, {})} | custom-call | flops 2359296 | bytes 4008448 | tf_op jit(solution)/shard_map/finish/pallas_call | solution.py:293
  135.4 1.4 %finish.5 = (f32[192,2304]{1,0:T(8,128)}, f32[8,128]{1,0:T(8,128)}) custom-call(f32[3,1,128]{2,1,0:T(1,128)S(1)} %pad_maximum_fusion.refs_0_, f32[1152,2]{1,0:T(8,128)S(1)} %bitcast.14, f32[2,1152,128]{2,1,0:T(8,128)S(1)} %get-tuple-element.116.refs_0_.refs_2_, ...), custom_call_target="tpu_custom_call", output_to_operand_aliasing={{0}: (5, {})} | custom-call | flops 2359296 | bytes 5343744 | tf_op jit(solution)/shard_map/finish/pallas_call | solution.py:293
  (57 shorter events, 2.3 us)
Async XLA Ops:
  0.0 16.7 %collective-permute-start.4 = (bf16[2304,1152]{1,0:T(8,128)(2,1)}, bf16[2304,1152]{1,0:T(8,128)(2,1)}, u32[]{:S(2)}, u32[]{:S(2)}) collective-permute-start(bf16[2304,1152]{1,0:T(8,128)(2,1)} %in_ref.1), channel_id=1, source_target_pairs={{0,4},{4,0},{8,12},{12,8},{16,20},{20,16},{24,28},{28,24},{1,5},{5... | collective-permute-start | bytes 15925256 | tf_op jit(solution)/shard_map/ppermute | solution.py:430
  1.4 10.5 %copy-start.3 = (s32[192,2]{0,1:T(2,128)S(1)}, s32[192,2]{0,1:T(2,128)}, u32[]{:S(2)}) copy-start(s32[192,2]{0,1:T(2,128)} %param.7) | copy-start | bytes 4612
  1.4 10.5 %copy-start.4 = (f32[160]{0:T(256)S(1)}, f32[160]{0:T(256)}, u32[]{:S(2)}) copy-start(f32[160]{0:T(256)} %param.8) | copy-start | bytes 1924
  1.5 10.7 %copy-start.2 = (f32[96]{0:T(128)S(1)}, f32[96]{0:T(128)}, u32[]{:S(2)}) copy-start(f32[96]{0:T(128)} %param.9) | copy-start | bytes 1156
  1.5 15.1 %copy-start.1 = (bf16[192,2304]{1,0:T(8,128)(2,1)S(1)}, bf16[192,2304]{1,0:T(8,128)(2,1)}, u32[]{:S(2)}) copy-start(bf16[192,2304]{1,0:T(8,128)(2,1)} %param.5) | copy-start | bytes 2654212
  1.5 11.2 %collective-permute-start = (bf16[64,2304]{1,0:T(8,128)(2,1)S(1)}, bf16[64,2304]{1,0:T(8,128)(2,1)S(1)}, u32[]{:S(2)}, u32[]{:S(2)}) collective-permute-start(bf16[64,2304]{1,0:T(8,128)(2,1)S(1)} %slice.30.refs_3_), channel_id=1, source_target_pairs={{0,8},{4,12},{8,0},{12,4},{16,24},{20,28},{24,16},{28,20},{1,9},{5... | collective-permute-start | bytes 884744 | tf_op jit(solution)/shard_map/ppermute | solution.py:253
  4.0 9.1 %collective-permute-start.1 = (bf16[64,2304]{1,0:T(8,128)(2,1)S(1)}, bf16[64,2304]{1,0:T(8,128)(2,1)S(1)}, u32[]{:S(2)}, u32[]{:S(2)}) collective-permute-start(bf16[64,2304]{1,0:T(8,128)(2,1)S(1)} %slice.30.refs_3_), channel_id=1, source_target_pairs={{0,16},{4,20},{8,24},{12,28},{16,0},{20,4},{24,8},{28,12},{1,17},{... | collective-permute-start | bytes 884744 | tf_op jit(solution)/shard_map/ppermute | solution.py:253
  9.6 2.3 %copy-start = (bf16[1152,2304]{1,0:T(8,128)(2,1)}, bf16[1152,2304]{1,0:T(8,128)(2,1)S(1)}, u32[]{:S(2)}) copy-start(bf16[1152,2304]{1,0:T(8,128)(2,1)S(1)} %transpose.14.refs_1_.refs_0_) | copy-start | bytes 15925252
  13.9 7.5 %collective-permute-start.2 = (bf16[32,2304]{1,0:T(8,128)(2,1)}, bf16[32,2304]{1,0:T(8,128)(2,1)S(1)}, u32[]{:S(2)}, u32[]{:S(2)}) collective-permute-start(bf16[32,2304]{1,0:T(8,128)(2,1)} %slice.33), channel_id=1, source_target_pairs={{0,8},{4,12},{8,0},{12,4},{16,24},{20,28},{24,16},{28,20},{1,9},{5... | collective-permute-start | bytes 442376 | tf_op jit(solution)/shard_map/ppermute | solution.py:253
  14.9 6.5 %collective-permute-start.3 = (bf16[32,2304]{1,0:T(8,128)(2,1)}, bf16[32,2304]{1,0:T(8,128)(2,1)S(1)}, u32[]{:S(2)}, u32[]{:S(2)}) collective-permute-start(bf16[32,2304]{1,0:T(8,128)(2,1)} %slice.34), channel_id=1, source_target_pairs={{0,16},{4,20},{8,24},{12,28},{16,0},{20,4},{24,8},{28,12},{1,17},{... | collective-permute-start | bytes 442376 | tf_op jit(solution)/shard_map/ppermute | solution.py:253
  16.6 6.9 %slice-start = ((s8[5308416]{0:T(1024)(128)(4,1)}), s8[1114112]{0:T(1024)(128)(4,1)S(1)}, s32[]{:S(2)}) async-start(s8[5308416]{0:T(1024)(128)(4,1)} %bitcast.10), calls=%async_computation | async-start | bytes 2228224
  16.7 6.8 %slice-start.1 = ((s8[5308416]{0:T(1024)(128)(4,1)}), s8[4194304]{0:T(1024)(128)(4,1)S(1)}, s32[]{:S(2)}) async-start(s8[5308416]{0:T(1024)(128)(4,1)} %bitcast.10), calls=%async_computation.1 | async-start | bytes 8388608
  21.4 14.2 %collective-permute-start.6 = (bf16[128,2304]{1,0:T(8,128)(2,1)S(1)}, bf16[128,2304]{1,0:T(8,128)(2,1)S(1)}, u32[]{:S(2)}, u32[]{:S(2)}) collective-permute-start(bf16[128,2304]{1,0:T(8,128)(2,1)S(1)} %slice.35.refs_2_), channel_id=1, source_target_pairs={{0,16},{4,20},{8,24},{12,28},{16,0},{20,4},{24,8},{28,12},{1,17},{... | collective-permute-start | bytes 1769480 | tf_op jit(solution)/shard_map/ppermute | solution.py:253
  22.0 15.1 %collective-permute-start.5 = (bf16[128,2304]{1,0:T(8,128)(2,1)S(1)}, bf16[128,2304]{1,0:T(8,128)(2,1)S(1)}, u32[]{:S(2)}, u32[]{:S(2)}) collective-permute-start(bf16[128,2304]{1,0:T(8,128)(2,1)S(1)} %slice.35.refs_2_), channel_id=1, source_target_pairs={{0,8},{4,12},{8,0},{12,4},{16,24},{20,28},{24,16},{28,20},{1,9},{5... | collective-permute-start | bytes 1769480 | tf_op jit(solution)/shard_map/ppermute | solution.py:253
  28.3 14.3 %collective-permute-start.9 = (s16[2,4,304,128]{3,2,1,0:T(8,128)(2,1)S(1)}, s16[2,4,304,128]{3,2,1,0:T(8,128)(2,1)S(1)}, u32[]{:S(2)}, u32[]{:S(2)}) collective-permute-start(s16[2,4,304,128]{3,2,1,0:T(8,128)(2,1)S(1)} %get-tuple-element.83), channel_id=1, source_target_pairs={{0,1},{1,0},{2,3},{3,2},{4,5},{5,4},{6,7},{7,6},{8,9},{9,8},{10,11... | collective-permute-start | bytes 1867784 | tf_op jit(solution)/shard_map/ppermute | solution.py:484
  35.6 9.9 %collective-permute-start.8 = (bf16[64,2304]{1,0:T(8,128)(2,1)S(1)}, bf16[64,2304]{1,0:T(8,128)(2,1)S(1)}, u32[]{:S(2)}, u32[]{:S(2)}) collective-permute-start(bf16[64,2304]{1,0:T(8,128)(2,1)S(1)} %slice.41), channel_id=1, source_target_pairs={{0,8},{4,12},{8,0},{12,4},{16,24},{20,28},{24,16},{28,20},{1,9},{5... | collective-permute-start | bytes 884744 | tf_op jit(solution)/shard_map/ppermute | solution.py:253
  37.1 16.2 %collective-permute-start.7 = (bf16[64,2304]{1,0:T(8,128)(2,1)S(1)}, bf16[64,2304]{1,0:T(8,128)(2,1)S(1)}, u32[]{:S(2)}, u32[]{:S(2)}) collective-permute-start(bf16[64,2304]{1,0:T(8,128)(2,1)S(1)} %slice.40), channel_id=1, source_target_pairs={{0,16},{4,20},{8,24},{12,28},{16,0},{20,4},{24,8},{28,12},{1,17},{... | collective-permute-start | bytes 884744 | tf_op jit(solution)/shard_map/ppermute | solution.py:253
  42.9 14.7 %collective-permute-start.13 = (s16[1,4,304,128]{3,2,1,0:T(8,128)(2,1)S(1)}, s16[1,4,304,128]{3,2,1,0:T(8,128)(2,1)S(1)}, u32[]{:S(2)}, u32[]{:S(2)}) collective-permute-start(s16[1,4,304,128]{3,2,1,0:T(8,128)(2,1)S(1)} %get-tuple-element.94), channel_id=1, source_target_pairs={{0,2},{1,3},{2,0},{3,1},{4,6},{5,7},{6,4},{7,5},{8,10},{9,11},{10,... | collective-permute-start | bytes 933896 | tf_op jit(solution)/shard_map/ppermute | solution.py:484
  49.8 16.3 %collective-permute-start.10 = (s16[3,400,128]{2,1,0:T(8,128)(2,1)S(1)}, s16[3,400,128]{2,1,0:T(8,128)(2,1)S(1)}, u32[]{:S(2)}, u32[]{:S(2)}) collective-permute-start(s16[3,400,128]{2,1,0:T(8,128)(2,1)S(1)} %get-tuple-element.91), channel_id=1, source_target_pairs={{0,8},{4,12},{8,0},{12,4},{16,24},{20,28},{24,16},{28,20},{1,9},{5... | collective-permute-start | bytes 921608 | tf_op jit(solution)/shard_map/ppermute | solution.py:253
  50.4 15.7 %collective-permute-start.11 = (s16[3,400,128]{2,1,0:T(8,128)(2,1)S(1)}, s16[3,400,128]{2,1,0:T(8,128)(2,1)S(1)}, u32[]{:S(2)}, u32[]{:S(2)}) collective-permute-start(s16[3,400,128]{2,1,0:T(8,128)(2,1)S(1)} %get-tuple-element.92), channel_id=1, source_target_pairs={{0,16},{4,20},{8,24},{12,28},{16,0},{20,4},{24,8},{28,12},{1,17},{... | collective-permute-start | bytes 921608 | tf_op jit(solution)/shard_map/ppermute | solution.py:253
  51.9 14.2 %collective-permute-start.12 = (s16[3,400,128]{2,1,0:T(8,128)(2,1)S(1)}, s16[3,400,128]{2,1,0:T(8,128)(2,1)S(1)}, u32[]{:S(2)}, u32[]{:S(2)}) collective-permute-start(s16[3,400,128]{2,1,0:T(8,128)(2,1)S(1)} %get-tuple-element.93), channel_id=1, source_target_pairs={{0,24},{4,28},{8,16},{12,20},{16,8},{20,12},{24,0},{28,4},{1,25},{... | collective-permute-start | bytes 921608 | tf_op jit(solution)/shard_map/ppermute | solution.py:253
  57.9 8.2 %collective-permute-start.14 = (s16[2,304,128]{2,1,0:T(8,128)(2,1)S(1)}, s16[2,304,128]{2,1,0:T(8,128)(2,1)S(1)}, u32[]{:S(2)}, u32[]{:S(2)}) collective-permute-start(s16[2,304,128]{2,1,0:T(8,128)(2,1)S(1)} %get-tuple-element.96), channel_id=1, source_target_pairs={{0,8},{4,12},{8,0},{12,4},{16,24},{20,28},{24,16},{28,20},{1,9},{5... | collective-permute-start | bytes 466952 | tf_op jit(solution)/shard_map/ppermute | solution.py:253
  70.8 18.4 %collective-permute-start.18 = (s16[2,3,400,128]{3,2,1,0:T(8,128)(2,1)S(1)}, s16[2,3,400,128]{3,2,1,0:T(8,128)(2,1)S(1)}, u32[]{:S(2)}, u32[]{:S(2)}) collective-permute-start(s16[2,3,400,128]{3,2,1,0:T(8,128)(2,1)S(1)} %get-tuple-element.110), channel_id=1, source_target_pairs={{0,1},{1,0},{2,3},{3,2},{4,5},{5,4},{6,7},{7,6},{8,9},{9,8},{10,11... | collective-permute-start | bytes 1843208 | tf_op jit(solution)/shard_map/ppermute | solution.py:484
  72.5 16.7 %collective-permute-start.15 = (s16[3,400,128]{2,1,0:T(8,128)(2,1)S(1)}, s16[3,400,128]{2,1,0:T(8,128)(2,1)S(1)}, u32[]{:S(2)}, u32[]{:S(2)}) collective-permute-start(s16[3,400,128]{2,1,0:T(8,128)(2,1)S(1)} %get-tuple-element.101), channel_id=1, source_target_pairs={{0,8},{4,12},{8,0},{12,4},{16,24},{20,28},{24,16},{28,20},{1,9},{5... | collective-permute-start | bytes 921608 | tf_op jit(solution)/shard_map/ppermute | solution.py:253
  73.0 16.2 %collective-permute-start.16 = (s16[3,400,128]{2,1,0:T(8,128)(2,1)S(1)}, s16[3,400,128]{2,1,0:T(8,128)(2,1)S(1)}, u32[]{:S(2)}, u32[]{:S(2)}) collective-permute-start(s16[3,400,128]{2,1,0:T(8,128)(2,1)S(1)} %get-tuple-element.102), channel_id=1, source_target_pairs={{0,16},{4,20},{8,24},{12,28},{16,0},{20,4},{24,8},{28,12},{1,17},{... | collective-permute-start | bytes 921608 | tf_op jit(solution)/shard_map/ppermute | solution.py:253
  74.5 14.7 %collective-permute-start.17 = (s16[3,400,128]{2,1,0:T(8,128)(2,1)S(1)}, s16[3,400,128]{2,1,0:T(8,128)(2,1)S(1)}, u32[]{:S(2)}, u32[]{:S(2)}) collective-permute-start(s16[3,400,128]{2,1,0:T(8,128)(2,1)S(1)} %get-tuple-element.103), channel_id=1, source_target_pairs={{0,24},{4,28},{8,16},{12,20},{16,8},{20,12},{24,0},{28,4},{1,25},{... | collective-permute-start | bytes 921608 | tf_op jit(solution)/shard_map/ppermute | solution.py:253
  76.0 12.1 %collective-permute-start.19 = (s16[2,304,128]{2,1,0:T(8,128)(2,1)S(1)}, s16[2,304,128]{2,1,0:T(8,128)(2,1)S(1)}, u32[]{:S(2)}, u32[]{:S(2)}) collective-permute-start(s16[2,304,128]{2,1,0:T(8,128)(2,1)S(1)} %pad_add_fusion), channel_id=1, source_target_pairs={{0,16},{4,20},{8,24},{12,28},{16,0},{20,4},{24,8},{28,12},{1,17},{... | collective-permute-start | bytes 466952 | tf_op jit(solution)/shard_map/ppermute | solution.py:253
  89.4 15.3 %collective-permute-start.22 = (s16[1,3,400,128]{3,2,1,0:T(8,128)(2,1)S(1)}, s16[1,3,400,128]{3,2,1,0:T(8,128)(2,1)S(1)}, u32[]{:S(2)}, u32[]{:S(2)}) collective-permute-start(s16[1,3,400,128]{3,2,1,0:T(8,128)(2,1)S(1)} %get-tuple-element.121), channel_id=1, source_target_pairs={{0,2},{1,3},{2,0},{3,1},{4,6},{5,7},{6,4},{7,5},{8,10},{9,11},{10,... | collective-permute-start | bytes 921608 | tf_op jit(solution)/shard_map/ppermute | solution.py:484
  97.6 13.7 %collective-permute-start.21 = (s16[1,3,400,128]{3,2,1,0:T(8,128)(2,1)S(1)}, s16[1,3,400,128]{3,2,1,0:T(8,128)(2,1)S(1)}, u32[]{:S(2)}, u32[]{:S(2)}) collective-permute-start(s16[1,3,400,128]{3,2,1,0:T(8,128)(2,1)S(1)} %get-tuple-element.120), channel_id=1, source_target_pairs={{0,1},{1,0},{2,3},{3,2},{4,5},{5,4},{6,7},{7,6},{8,9},{9,8},{10,11... | collective-permute-start | bytes 921608 | tf_op jit(solution)/shard_map/ppermute | solution.py:484
  98.0 16.6 %collective-permute-start.24 = (s16[2,304,128]{2,1,0:T(8,128)(2,1)S(1)}, s16[2,304,128]{2,1,0:T(8,128)(2,1)S(1)}, u32[]{:S(2)}, u32[]{:S(2)}) collective-permute-start(s16[2,304,128]{2,1,0:T(8,128)(2,1)S(1)} %get-tuple-element.126), channel_id=1, source_target_pairs={{0,1},{1,0},{2,3},{3,2},{4,5},{5,4},{6,7},{7,6},{8,9},{9,8},{10,11... | collective-permute-start | bytes 466952 | tf_op jit(solution)/shard_map/ppermute | solution.py:484
  99.7 35.7 %collective-permute-start.20 = (s16[1,3,400,128]{3,2,1,0:T(8,128)(2,1)S(1)}, s16[1,3,400,128]{3,2,1,0:T(8,128)(2,1)S(1)}, u32[]{:S(2)}, u32[]{:S(2)}) collective-permute-start(s16[1,3,400,128]{3,2,1,0:T(8,128)(2,1)S(1)} %get-tuple-element.119), channel_id=1, source_target_pairs={{0,1},{1,0},{2,3},{3,2},{4,5},{5,4},{6,7},{7,6},{8,9},{9,8},{10,11... | collective-permute-start | bytes 921608 | tf_op jit(solution)/shard_map/ppermute | solution.py:484
  111.5 23.9 %collective-permute-start.23 = (s16[1,3,400,128]{3,2,1,0:T(8,128)(2,1)S(1)}, s16[1,3,400,128]{3,2,1,0:T(8,128)(2,1)S(1)}, u32[]{:S(2)}, u32[]{:S(2)}) collective-permute-start(s16[1,3,400,128]{3,2,1,0:T(8,128)(2,1)S(1)} %get-tuple-element.124), channel_id=1, source_target_pairs={{0,2},{1,3},{2,0},{3,1},{4,6},{5,7},{6,4},{7,5},{8,10},{9,11},{10,... | collective-permute-start | bytes 921608 | tf_op jit(solution)/shard_map/ppermute | solution.py:484
  114.7 19.3 %collective-permute-start.25 = (s16[2,304,128]{2,1,0:T(8,128)(2,1)S(1)}, s16[2,304,128]{2,1,0:T(8,128)(2,1)S(1)}, u32[]{:S(2)}, u32[]{:S(2)}) collective-permute-start(s16[2,304,128]{2,1,0:T(8,128)(2,1)S(1)} %pad_add_fusion.1), channel_id=1, source_target_pairs={{0,2},{1,3},{2,0},{3,1},{4,6},{5,7},{6,4},{7,5},{8,10},{9,11},{10,... | collective-permute-start | bytes 466952 | tf_op jit(solution)/shard_map/ppermute | solution.py:484

commit v13 on v12

--- a/solution.py
+++ b/solution.py
@@ -74,7 +74,7 @@
 
 
 def early_ladder_kernel(chips, tile, vir, pieces, place_ref, own_ref, sib_ref, *refs):
-    rows_in, (parts, away, rhs, work, sent) = refs[: len(pieces)], refs[len(pieces) :]
+    rows_in, (parts, *away, rhs, work, sent) = refs[: len(pieces)], refs[len(pieces) :]
     chip, z = place_ref[0], place_ref[2]
     at = 0
     for ref, (start, count) in zip(rows_in, pieces):
@@ -107,7 +107,7 @@
     lax.fori_loop(0, own_ref.shape[0] // tile, step, 0)
     for i in range(chips // 2):
         for d in range(chips):
-            encode(sent[i, pl.ds(d * group, group), :], away.at[i, d])
+            encode(sent[i, pl.ds(d * group, group), :], away[i].at[0, d])
 
 
 def sum_kernel(places, count, parts, *refs):
@@ -332,11 +332,9 @@
             4 * rows * depth * chips * WIDTH,
             [place, own_t, sib_t, *arrays],
             [smem] + [vmem] * (2 + len(arrays)),
-            [vmem] * 2,
-            [
-                jax.ShapeDtypeStruct(grouped, jnp.float32),
-                jax.ShapeDtypeStruct((chips // 2, chips, *small.shape), jnp.int16),
-            ],
+            [vmem] * (1 + chips // 2),
+            [jax.ShapeDtypeStruct(grouped, jnp.float32)]
+            + [jax.ShapeDtypeStruct((1, chips, *small.shape), jnp.int16)] * (chips // 2),
             20,
             [
                 pltpu.VMEM((chips * WIDTH, depth), jnp.bfloat16),
@@ -512,27 +510,29 @@
         return [first, move(jnp.concatenate([single, first[1:]]), 2)]
 
     def early_stages(r):
-        parts, away = yield early_ladder(rows_of(r))
-        got, places = yield from halved(parts, [across(away, 1)])
+        parts, *away = yield early_ladder(rows_of(r))
+        away = [across(x, 1) for x in reversed(away)][::-1]
+        got, places = yield from halved(parts, away)
         mine, *sums = yield early_sum(places, parts, got)
         arrived = by_steps(to_chip, *sums)
-        steps.append(arrived[0])
+        steps.extend(arrived)
+        own, *blocks = yield early_antisym([mine, *arrived])
+        blocks = by_steps(across, *blocks)
+        firsts.append(blocks[:1])
+        seconds.extend(blocks[1:])
         yield None
-        own, *blocks = yield early_antisym([mine, *arrived])
-        yield finish(r, own, by_steps(across, *blocks), None, update)
+        yield finish(r, own, blocks, None, update)
 
     def stages(r):
         sums = yield ladder(rows_of(r))
         if turns:
-            sums, _ = lax.optimization_barrier((sums, turns[-1] + results[-1][:1]))
+            sums, _ = lax.optimization_barrier((sums, turns[-1] + steps + results[-1][:1]))
         arrived = [to_chip(sums[d], d) for d in range(1, chips)]
-        if steps:
-            arrived, _ = lax.optimization_barrier((arrived, steps[:1]))
         turns.append(arrived)
         parcels = slabs // 2 if r == chunks - 1 else 1
         parts, *away = yield antisym(parcels, [sums[0], *arrived])
-        if parcels > 1 and firsts:
-            away, _ = lax.optimization_barrier((away, firsts[-1]))
+        if firsts and (early or parcels > 1):
+            away, _ = lax.optimization_barrier((away, firsts[-1] + (seconds if parcels > 1 else [])))
         away = [across(x, 1) for x in reversed(away)][::-1]
         firsts.append(away)
         got, places = yield from halved(parts, away)
@@ -543,16 +543,15 @@
     def when(stage):
         r, k = stage
         if early and r == 0:
-            return (20, *[41] * hops, 54, 55, 66, 90)[k]
+            return (20, *[41] * hops, 44, 58, 59, 83)[k]
         if k == 0:
             return 37 + 5 * r if early else 30 + 5 * r
-        start = 15 * r + (45 if early else 54)
-        return start + (k - 1) * (14 if early else 17) - (1 if k == 2 + hops else 0)
+        return 15 * r + (45 if early else 54) + (k - 1) * 17 - (1 if k == 2 + hops else 0)
 
     order = [(r, k) for r in range(chunks) for k in range(3 + hops + 2 * (early and r == 0))]
     order = sorted(order, key=when)
 
-    turns, firsts, steps = [], [], []
+    turns, firsts, seconds, steps = [], [], [], []
     running = [early_stages(r) if early and r == 0 else stages(r) for r in range(chunks)]
     results = [None] * chunks
     update, token = None, jnp.zeros((8, LANES), jnp.float32)

time: 137 us -> 133 us (0.971)
  local copies, waits for them, and re-layouts: 5.14 us -> 16.4 us
  waiting for transfers between devices: 57.9 us -> 46.7 us
  starting transfers between devices: 35.5 us -> 32 us
    ppermute x16, waiting for transfers between devices: 24.4 us -> 9.82 us  [to_chip(): return lax.ppermute(x, 'pair', [(i, i ^ d * CORES) for i in range(devices)])]
    unnamed x14 -> x32, local copies, waits for them, and re-layouts: 2.38 us -> 13.9 us
    ppermute x9 -> x10, starting transfers between devices: 15.6 us -> 12.1 us  [across(): return lax.ppermute(x, 'slab', [(i, i ^ level) for i in range(slabs)])]
    ppermute x9 -> x10, waiting for transfers between devices: 33.5 us -> 36.9 us  [across(): return lax.ppermute(x, 'slab', [(i, i ^ level) for i in range(slabs)])]
  transfers between devices with their start and end apart: 26 -> 27, of which waited for: 9 -> 14; matrix products, arithmetic and copies ran while one was open for 2% -> 2% of each run, Pallas kernels for 23% -> 27%
where the time goes in v13:
time: 133 us
  waiting for transfers between devices  46.7 us (35%)
  Pallas kernels  36.8 us (28%)
  starting transfers between devices  32 us (24%)
  local copies, waits for them, and re-layouts  16.4 us (12%)
    ppermute x10, waiting for transfers between devices, across(): return lax.ppermute(x, 'slab', [(i, i ^ level) for i in range(slabs)])  36.9 us
    pallas_call x13, Pallas kernels, call(): pl.pallas_call(kernel, in_specs=[*in_specs, vmem], out_specs=[*out_specs,...  28.7 us
    ppermute x16, starting transfers between devices, to_chip(): return lax.ppermute(x, 'pair', [(i, i ^ d * CORES) for i in range(devices)])  19.4 us
    unnamed x32, local copies, waits for them, and re-layouts  13.9 us
    ppermute x10, starting transfers between devices, across(): return lax.ppermute(x, 'slab', [(i, i ^ level) for i in range(slabs)])  12.1 us
    ppermute x16, waiting for transfers between devices, to_chip(): return lax.ppermute(x, 'pair', [(i, i ^ d * CORES) for i in range(devices)])  9.82 us
    pallas_call x1, Pallas kernels, on_device(): sib_t = transpose(swapped)  4.1 us
    pallas_call x1, Pallas kernels, on_device(): own_t = transpose(in_hbm(integrals))  4 us
  transfers between devices with their start and end apart: 27, of which 14 were waited for; matrix products, arithmetic and copies ran while one was open for 2% of the time, Pallas kernels for 27%

profile of v13, /device:TPU:0, one launch (start us, length us, event | category | flops | bytes accessed | tf_op | source)
XLA Modules:
  0.0 132.7 jit_solution(9737512565334403378)
XLA Ops:
  0.5 1.0 slice.30.refs_3_
  1.5 2.6 %collective-permute-start = (bf16[64,2304]{1,0:T(8,128)(2,1)S(1)}, bf16[64,2304]{1,0:T(8,128)(2,1)S(1)}, u32[]{:S(2)}, u32[]{:S(2)}) collective-permute-start(bf16[64,2304]{1,0:T(8,128)(2,1)S(1)} %slice.30.refs_3_), channel_id=1, source_target_pairs={{0,8},{4,12},{8,0},{12,4},{16,24},{20,28},{24,16},{28,20},{1,9},{5... | collective-permute-start | bytes 884744 | tf_op jit(solution)/shard_map/ppermute | solution.py:253
  4.0 1.5 %collective-permute-start.1 = (bf16[64,2304]{1,0:T(8,128)(2,1)S(1)}, bf16[64,2304]{1,0:T(8,128)(2,1)S(1)}, u32[]{:S(2)}, u32[]{:S(2)}) collective-permute-start(bf16[64,2304]{1,0:T(8,128)(2,1)S(1)} %slice.30.refs_3_), channel_id=1, source_target_pairs={{0,16},{4,20},{8,24},{12,28},{16,0},{20,4},{24,8},{28,12},{1,17},{... | collective-permute-start | bytes 884744 | tf_op jit(solution)/shard_map/ppermute | solution.py:253
  5.5 4.0 %transpose.14.refs_1_.refs_0_ = bf16[1152,2304]{1,0:T(8,128)(2,1)S(1)} custom-call(bf16[2304,1152]{1,0:T(8,128)(2,1)} %in_ref.1), custom_call_target="tpu_custom_call" | custom-call | bytes 10616832 | tf_op jit(solution)/shard_map/transpose/pallas_call | solution.py:427
  9.6 2.3 %copy-done = bf16[1152,2304]{1,0:T(8,128)(2,1)} copy-done((bf16[1152,2304]{1,0:T(8,128)(2,1)}, bf16[1152,2304]{1,0:T(8,128)(2,1)S(1)}, u32[]{:S(2)}) %copy-start) | copy-done | bytes 5308440
  13.6 1.8 %collective-permute-start.3 = (bf16[32,2304]{1,0:T(8,128)(2,1)S(1)}, bf16[32,2304]{1,0:T(8,128)(2,1)S(1)}, u32[]{:S(2)}, u32[]{:S(2)}) collective-permute-start(bf16[32,2304]{1,0:T(8,128)(2,1)S(1)} %slice.34), channel_id=1, source_target_pairs={{0,16},{4,20},{8,24},{12,28},{16,0},{20,4},{24,8},{28,12},{1,17},{... | collective-permute-start | bytes 442376 | tf_op jit(solution)/shard_map/ppermute | solution.py:253
  15.4 1.1 slice.35.refs_2_
  16.5 4.1 %transpose.15.refs_2_.refs_1_ = bf16[1152,2304]{1,0:T(8,128)(2,1)S(1)} custom-call(bf16[2304,1152]{1,0:T(8,128)(2,1)} %collective-permute-done.4.in_ref), custom_call_target="tpu_custom_call" | custom-call | bytes 10616832 | tf_op jit(solution)/shard_map/transpose/pallas_call | solution.py:429
  20.6 2.4 %copy-done.2 = bf16[1152,2304]{1,0:T(8,128)(2,1)} copy-done((bf16[1152,2304]{1,0:T(8,128)(2,1)}, bf16[1152,2304]{1,0:T(8,128)(2,1)S(1)}, u32[]{:S(2)}) %copy-start.2) | copy-done | bytes 5308440
  24.8 1.7 %collective-permute-start.5 = (bf16[128,2304]{1,0:T(8,128)(2,1)S(1)}, bf16[128,2304]{1,0:T(8,128)(2,1)S(1)}, u32[]{:S(2)}, u32[]{:S(2)}) collective-permute-start(bf16[128,2304]{1,0:T(8,128)(2,1)S(1)} %slice.35.refs_2_), channel_id=1, source_target_pairs={{0,8},{4,12},{8,0},{12,4},{16,24},{20,28},{24,16},{28,20},{1,9},{5... | collective-permute-start | bytes 1769480 | tf_op jit(solution)/shard_map/ppermute | solution.py:253
  26.5 2.5 %copy-done.1 = bf16[1152,2304]{1,0:T(8,128)(2,1)S(1)} copy-done((bf16[1152,2304]{1,0:T(8,128)(2,1)S(1)}, bf16[1152,2304]{1,0:T(8,128)(2,1)}, u32[]{:S(2)}) %copy-start.1) | copy-done | bytes 5308440
  29.0 2.5 %copy-done.3 = bf16[1152,2304]{1,0:T(8,128)(2,1)S(1)} copy-done((bf16[1152,2304]{1,0:T(8,128)(2,1)S(1)}, bf16[1152,2304]{1,0:T(8,128)(2,1)}, u32[]{:S(2)}) %copy-start.3) | copy-done | bytes 5308440
  31.5 1.0 copy-done.6
  32.4 0.9 copy-done.8
  33.3 0.9 copy-done.10
  34.3 4.8 %early_ladder.1 = (f32[2,1152,128]{2,1,0:T(8,128)S(1)}, s16[1,4,304,128]{3,2,1,0:T(8,128)(2,1)S(1)}, s16[1,4,304,128]{3,2,1,0:T(8,128)(2,1)S(1)}, f32[8,128]{1,0:T(8,128)S(1)}) custom-call(s32[3]{0:T(128)S(1)} %pad_add_fusion.2.refs_0_, bf16[1152,2304]{1,0:T(8,128)(2,1)S(1)} %copy-done.1, bf16[1152,2304]{1,0:T(8,128)(2,1)S(1)} %copy-done.3, ...), custom_call_target="tpu_custom_call" | custom-call | flops 2717908992 | bytes 13598732 | tf_op jit(solution)/shard_map/early_ladder/pallas_call | solution.py:293
  39.1 1.7 %collective-permute-start.9 = (s16[1,4,304,128]{3,2,1,0:T(8,128)(2,1)S(1)}, s16[1,4,304,128]{3,2,1,0:T(8,128)(2,1)S(1)}, u32[]{:S(2)}, u32[]{:S(2)}) collective-permute-start(s16[1,4,304,128]{3,2,1,0:T(8,128)(2,1)S(1)} %get-tuple-element.80), channel_id=1, source_target_pairs={{0,1},{1,0},{2,3},{3,2},{4,5},{5,4},{6,7},{7,6},{8,9},{9,8},{10,11... | collective-permute-start | bytes 933896 | tf_op jit(solution)/shard_map/ppermute | solution.py:482
  41.6 11.1 %collective-permute-done.9.refs_1_ = s16[1,4,304,128]{3,2,1,0:T(8,128)(2,1)S(1)} collective-permute-done((s16[1,4,304,128]{3,2,1,0:T(8,128)(2,1)S(1)}, s16[1,4,304,128]{3,2,1,0:T(8,128)(2,1)S(1)}, u32[]{:S(2)}, u32[]{:S(2)}) %collective-permute-start.9) | collective-permute-done | bytes 311328 | tf_op jit(solution)/shard_map/ppermute | solution.py:482
  52.9 1.6 %collective-permute-start.10 = (s16[1,4,304,128]{3,2,1,0:T(8,128)(2,1)S(1)}, s16[1,4,304,128]{3,2,1,0:T(8,128)(2,1)S(1)}, u32[]{:S(2)}, u32[]{:S(2)}) collective-permute-start(s16[1,4,304,128]{3,2,1,0:T(8,128)(2,1)S(1)} %get-tuple-element.82), channel_id=1, source_target_pairs={{0,2},{1,3},{2,0},{3,1},{4,6},{5,7},{6,4},{7,5},{8,10},{9,11},{10,... | collective-permute-start | bytes 933896 | tf_op jit(solution)/shard_map/ppermute | solution.py:482
  54.6 1.6 %collective-permute-start.7 = (bf16[64,2304]{1,0:T(8,128)(2,1)S(1)}, bf16[64,2304]{1,0:T(8,128)(2,1)S(1)}, u32[]{:S(2)}, u32[]{:S(2)}) collective-permute-start(bf16[64,2304]{1,0:T(8,128)(2,1)S(1)} %slice.40), channel_id=1, source_target_pairs={{0,16},{4,20},{8,24},{12,28},{16,0},{20,4},{24,8},{28,12},{1,17},{... | collective-permute-start | bytes 884744 | tf_op jit(solution)/shard_map/ppermute | solution.py:253
  56.2 4.2 %ladder.2 = (s16[3,400,128]{2,1,0:T(8,128)(2,1)S(1)}, s16[3,400,128]{2,1,0:T(8,128)(2,1)S(1)}, s16[3,400,128]{2,1,0:T(8,128)(2,1)S(1)}, s16[3,400,128]{2,1,0:T(8,128)(2,1)S(1)}, f32[8,128]{1,0:T(8,128)S(1)}) custom-call(bf16[1152,2304]{1,0:T(8,128)(2,1)S(1)} %bitcast.11, bf16[1152,2304]{1,0:T(8,128)(2,1)S(1)} %copy-done.4, ...), custom_call_target="tpu_custom_call" | custom-call | flops 2717908992 | bytes 13910016 | tf_op jit(solution)/shard_map/ladder/pallas_call | solution.py:293
  60.4 4.7 %collective-permute-done.10.refs_2_ = s16[1,4,304,128]{3,2,1,0:T(8,128)(2,1)S(1)} collective-permute-done((s16[1,4,304,128]{3,2,1,0:T(8,128)(2,1)S(1)}, s16[1,4,304,128]{3,2,1,0:T(8,128)(2,1)S(1)}, u32[]{:S(2)}, u32[]{:S(2)}) %collective-permute-start.10) | collective-permute-done | bytes 311328 | tf_op jit(solution)/shard_map/ppermute | solution.py:482
  65.9 1.6 %collective-permute-start.12 = (s16[3,400,128]{2,1,0:T(8,128)(2,1)S(1)}, s16[3,400,128]{2,1,0:T(8,128)(2,1)S(1)}, u32[]{:S(2)}, u32[]{:S(2)}) collective-permute-start(s16[3,400,128]{2,1,0:T(8,128)(2,1)S(1)} %get-tuple-element.90), channel_id=1, source_target_pairs={{0,8},{4,12},{8,0},{12,4},{16,24},{20,28},{24,16},{28,20},{1,9},{5... | collective-permute-start | bytes 921608 | tf_op jit(solution)/shard_map/ppermute | solution.py:253
  67.5 1.4 %collective-permute-start.13 = (s16[3,400,128]{2,1,0:T(8,128)(2,1)S(1)}, s16[3,400,128]{2,1,0:T(8,128)(2,1)S(1)}, u32[]{:S(2)}, u32[]{:S(2)}) collective-permute-start(s16[3,400,128]{2,1,0:T(8,128)(2,1)S(1)} %get-tuple-element.91), channel_id=1, source_target_pairs={{0,16},{4,20},{8,24},{12,28},{16,0},{20,4},{24,8},{28,12},{1,17},{... | collective-permute-start | bytes 921608 | tf_op jit(solution)/shard_map/ppermute | solution.py:253
  69.4 1.3 collective-permute-done.15.refs_2_
  70.7 1.5 %collective-permute-start.16 = (s16[2,304,128]{2,1,0:T(8,128)(2,1)S(1)}, s16[2,304,128]{2,1,0:T(8,128)(2,1)S(1)}, u32[]{:S(2)}, u32[]{:S(2)}) collective-permute-start(s16[2,304,128]{2,1,0:T(8,128)(2,1)S(1)} %pad_add_fusion), channel_id=1, source_target_pairs={{0,16},{4,20},{8,24},{12,28},{16,0},{20,4},{24,8},{28,12},{1,17},{... | collective-permute-start | bytes 466952 | tf_op jit(solution)/shard_map/ppermute | solution.py:253
  72.2 4.2 %ladder.3 = (s16[3,400,128]{2,1,0:T(8,128)(2,1)S(1)}, s16[3,400,128]{2,1,0:T(8,128)(2,1)S(1)}, s16[3,400,128]{2,1,0:T(8,128)(2,1)S(1)}, s16[3,400,128]{2,1,0:T(8,128)(2,1)S(1)}, f32[8,128]{1,0:T(8,128)S(1)}) custom-call(bf16[1152,2304]{1,0:T(8,128)(2,1)S(1)} %bitcast.11, bf16[1152,2304]{1,0:T(8,128)(2,1)S(1)} %copy-done.4, ...), custom_call_target="tpu_custom_call" | custom-call | flops 2717908992 | bytes 13910016 | tf_op jit(solution)/shard_map/ladder/pallas_call | solution.py:293
  76.4 2.9 %collective-permute-done.16.refs_3_ = s16[2,304,128]{2,1,0:T(8,128)(2,1)S(1)} collective-permute-done((s16[2,304,128]{2,1,0:T(8,128)(2,1)S(1)}, s16[2,304,128]{2,1,0:T(8,128)(2,1)S(1)}, u32[]{:S(2)}, u32[]{:S(2)}) %collective-permute-start.16) | collective-permute-done | bytes 155680 | tf_op jit(solution)/shard_map/ppermute | solution.py:253
  79.3 1.1 early_antisym.1
  80.4 1.8 %collective-permute-start.20 = (s16[2,304,128]{2,1,0:T(8,128)(2,1)S(1)}, s16[2,304,128]{2,1,0:T(8,128)(2,1)S(1)}, u32[]{:S(2)}, u32[]{:S(2)}) collective-permute-start(s16[2,304,128]{2,1,0:T(8,128)(2,1)S(1)} %get-tuple-element.108), channel_id=1, source_target_pairs={{0,1},{1,0},{2,3},{3,2},{4,5},{5,4},{6,7},{7,6},{8,9},{9,8},{10,11... | collective-permute-start | bytes 466952 | tf_op jit(solution)/shard_map/ppermute | solution.py:482
  82.2 4.7 %antisym.2 = (f32[2,1152,128]{2,1,0:T(8,128)S(1)}, s16[2,3,400,128]{3,2,1,0:T(8,128)(2,1)S(1)}, f32[8,128]{1,0:T(8,128)S(1)}) custom-call(s32[3]{0:T(128)S(1)} %pad_add_fusion.2.refs_0_, s16[3,400,128]{2,1,0:T(8,128)(2,1)S(1)} %get-tuple-element.99.refs_1_, s16[3,400,128]{2,1,0:T(8,128)(2,1)S(1)} %collective-permute-done.12.refs_2_, ...), custom_call_target="tpu_custom_call" | custom-call | flops 9437184 | bytes 3022860 | tf_op jit(solution)/shard_map/antisym/pallas_call | solution.py:293
  86.9 2.2 %collective-permute-done.20.refs_3_ = s16[2,304,128]{2,1,0:T(8,128)(2,1)S(1)} collective-permute-done((s16[2,304,128]{2,1,0:T(8,128)(2,1)S(1)}, s16[2,304,128]{2,1,0:T(8,128)(2,1)S(1)}, u32[]{:S(2)}, u32[]{:S(2)}) %collective-permute-start.20) | collective-permute-done | bytes 155680 | tf_op jit(solution)/shard_map/ppermute | solution.py:482
  89.7 1.5 %collective-permute-start.18 = (s16[3,400,128]{2,1,0:T(8,128)(2,1)S(1)}, s16[3,400,128]{2,1,0:T(8,128)(2,1)S(1)}, u32[]{:S(2)}, u32[]{:S(2)}) collective-permute-start(s16[3,400,128]{2,1,0:T(8,128)(2,1)S(1)} %get-tuple-element.97), channel_id=1, source_target_pairs={{0,16},{4,20},{8,24},{12,28},{16,0},{20,4},{24,8},{28,12},{1,17},{... | collective-permute-start | bytes 921608 | tf_op jit(solution)/shard_map/ppermute | solution.py:253
  91.1 1.5 %collective-permute-start.19 = (s16[3,400,128]{2,1,0:T(8,128)(2,1)S(1)}, s16[3,400,128]{2,1,0:T(8,128)(2,1)S(1)}, u32[]{:S(2)}, u32[]{:S(2)}) collective-permute-start(s16[3,400,128]{2,1,0:T(8,128)(2,1)S(1)} %get-tuple-element.98), channel_id=1, source_target_pairs={{0,24},{4,28},{8,16},{12,20},{16,8},{20,12},{24,0},{28,4},{1,25},{... | collective-permute-start | bytes 921608 | tf_op jit(solution)/shard_map/ppermute | solution.py:253
  92.6 2.3 %collective-permute-start.22 = (s16[2,304,128]{2,1,0:T(8,128)(2,1)S(1)}, s16[2,304,128]{2,1,0:T(8,128)(2,1)S(1)}, u32[]{:S(2)}, u32[]{:S(2)}) collective-permute-start(s16[2,304,128]{2,1,0:T(8,128)(2,1)S(1)} %pad_add_fusion.1), channel_id=1, source_target_pairs={{0,2},{1,3},{2,0},{3,1},{4,6},{5,7},{6,4},{7,5},{8,10},{9,11},{10,... | collective-permute-start | bytes 466952 | tf_op jit(solution)/shard_map/ppermute | solution.py:482
  94.9 1.1 collective-permute-done.17.refs_2_
  96.0 2.8 %collective-permute-done.18.refs_3_ = s16[3,400,128]{2,1,0:T(8,128)(2,1)S(1)} collective-permute-done((s16[3,400,128]{2,1,0:T(8,128)(2,1)S(1)}, s16[3,400,128]{2,1,0:T(8,128)(2,1)S(1)}, u32[]{:S(2)}, u32[]{:S(2)}) %collective-permute-start.18) | collective-permute-done | bytes 307232 | tf_op jit(solution)/shard_map/ppermute | solution.py:253
  98.8 1.3 collective-permute-done.19.refs_4_
  100.1 4.7 %antisym.3 = (f32[2,1152,128]{2,1,0:T(8,128)S(1)}, s16[1,3,400,128]{3,2,1,0:T(8,128)(2,1)S(1)}, s16[1,3,400,128]{3,2,1,0:T(8,128)(2,1)S(1)}, f32[8,128]{1,0:T(8,128)S(1)}) custom-call(s32[3]{0:T(128)S(1)} %pad_add_fusion.2.refs_0_, s16[3,400,128]{2,1,0:T(8,128)(2,1)S(1)} %get-tuple-element.95.refs_1_, ...), custom_call_target="tpu_custom_call" | custom-call | flops 9437184 | bytes 3022860 | tf_op jit(solution)/shard_map/antisym/pallas_call | solution.py:293
  104.8 1.9 %collective-permute-done.21.refs_1_.refs_3_ = s16[2,3,400,128]{3,2,1,0:T(8,128)(2,1)S(1)} collective-permute-done((s16[2,3,400,128]{3,2,1,0:T(8,128)(2,1)S(1)}, s16[2,3,400,128]{3,2,1,0:T(8,128)(2,1)S(1)}, u32[]{:S(2)}, u32[]{:S(2)}) %collective-permute-start.21) | collective-permute-done | bytes 614432 | tf_op jit(solution)/shard_map/ppermute | solution.py:482
  106.9 1.9 %collective-permute-start.23 = (s16[1,3,400,128]{3,2,1,0:T(8,128)(2,1)S(1)}, s16[1,3,400,128]{3,2,1,0:T(8,128)(2,1)S(1)}, u32[]{:S(2)}, u32[]{:S(2)}) collective-permute-start(s16[1,3,400,128]{3,2,1,0:T(8,128)(2,1)S(1)} %get-tuple-element.111), channel_id=1, source_target_pairs={{0,1},{1,0},{2,3},{3,2},{4,5},{5,4},{6,7},{7,6},{8,9},{9,8},{10,11... | collective-permute-start | bytes 921608 | tf_op jit(solution)/shard_map/ppermute | solution.py:482
  109.0 2.0 %collective-permute-start.26 = (s16[1,3,400,128]{3,2,1,0:T(8,128)(2,1)S(1)}, s16[1,3,400,128]{3,2,1,0:T(8,128)(2,1)S(1)}, u32[]{:S(2)}, u32[]{:S(2)}) collective-permute-start(s16[1,3,400,128]{3,2,1,0:T(8,128)(2,1)S(1)} %get-tuple-element.119), channel_id=1, source_target_pairs={{0,2},{1,3},{2,0},{3,1},{4,6},{5,7},{6,4},{7,5},{8,10},{9,11},{10,... | collective-permute-start | bytes 921608 | tf_op jit(solution)/shard_map/ppermute | solution.py:482
  111.0 1.4 %finish.3 = (f32[192,2304]{1,0:T(8,128)}, f32[8,128]{1,0:T(8,128)S(1)}) custom-call(f32[3,1,128]{2,1,0:T(1,128)S(1)} %pad_maximum_fusion.refs_0_, f32[1152,2]{1,0:T(8,128)S(1)} %bitcast.12, f32[288,128]{1,0:T(8,128)S(1)} %get-tuple-element.113.refs_2_, s16[2,304,128]{2,1,0:T(8,128)(2,1)S(1)} %collective-permute-done.20.refs_3_, ...), custom_call_target="tpu_custom_call" | custom-call | flops 2359296 | bytes 2238976 | tf_op jit(solution)/shard_map/finish/pallas_call | solution.py:293
  112.3 8.3 %collective-permute-done.24.refs_1_ = s16[1,3,400,128]{3,2,1,0:T(8,128)(2,1)S(1)} collective-permute-done((s16[1,3,400,128]{3,2,1,0:T(8,128)(2,1)S(1)}, s16[1,3,400,128]{3,2,1,0:T(8,128)(2,1)S(1)}, u32[]{:S(2)}, u32[]{:S(2)}) %collective-permute-start.24) | collective-permute-done | bytes 307232 | tf_op jit(solution)/shard_map/ppermute | solution.py:482
  121.5 1.4 %finish.4 = (f32[192,2304]{1,0:T(8,128)}, f32[8,128]{1,0:T(8,128)S(1)}) custom-call(f32[3,1,128]{2,1,0:T(1,128)S(1)} %pad_maximum_fusion.refs_0_, f32[1152,2]{1,0:T(8,128)S(1)} %bitcast.13, f32[2,1152,128]{2,1,0:T(8,128)S(1)} %get-tuple-element.114.refs_0_.refs_2_, ...), custom_call_target="tpu_custom_call", output_to_operand_aliasing={{0}: (5, {})} | custom-call | flops 2359296 | bytes 5650944 | tf_op jit(solution)/shard_map/finish/pallas_call | solution.py:293
  122.9 1.1 collective-permute-done.23.refs_3_
  123.9 7.3 %collective-permute-done.25.refs_4_ = s16[1,3,400,128]{3,2,1,0:T(8,128)(2,1)S(1)} collective-permute-done((s16[1,3,400,128]{3,2,1,0:T(8,128)(2,1)S(1)}, s16[1,3,400,128]{3,2,1,0:T(8,128)(2,1)S(1)}, u32[]{:S(2)}, u32[]{:S(2)}) %collective-permute-start.25) | collective-permute-done | bytes 307232 | tf_op jit(solution)/shard_map/ppermute | solution.py:482
  131.3 1.4 %finish.5 = (f32[192,2304]{1,0:T(8,128)}, f32[8,128]{1,0:T(8,128)}) custom-call(f32[3,1,128]{2,1,0:T(1,128)S(1)} %pad_maximum_fusion.refs_0_, f32[1152,2]{1,0:T(8,128)S(1)} %bitcast.14, f32[2,1152,128]{2,1,0:T(8,128)S(1)} %get-tuple-element.104.refs_0_.refs_2_, ...), custom_call_target="tpu_custom_call", output_to_operand_aliasing={{0}: (5, {})} | custom-call | flops 2359296 | bytes 5343744 | tf_op jit(solution)/shard_map/finish/pallas_call | solution.py:293
  (77 shorter events, 8.1 us)
Async XLA Ops:
  0.0 16.5 %collective-permute-start.4 = (bf16[2304,1152]{1,0:T(8,128)(2,1)}, bf16[2304,1152]{1,0:T(8,128)(2,1)}, u32[]{:S(2)}, u32[]{:S(2)}) collective-permute-start(bf16[2304,1152]{1,0:T(8,128)(2,1)} %in_ref.1), channel_id=1, source_target_pairs={{0,4},{4,0},{8,12},{12,8},{16,20},{20,16},{24,28},{28,24},{1,5},{5... | collective-permute-start | bytes 15925256 | tf_op jit(solution)/shard_map/ppermute | solution.py:428
  1.4 10.5 %copy-start.12 = (s32[192,2]{0,1:T(2,128)S(1)}, s32[192,2]{0,1:T(2,128)}, u32[]{:S(2)}) copy-start(s32[192,2]{0,1:T(2,128)} %param.7) | copy-start | bytes 4612
  1.4 10.5 %copy-start.13 = (f32[160]{0:T(256)S(1)}, f32[160]{0:T(256)}, u32[]{:S(2)}) copy-start(f32[160]{0:T(256)} %param.8) | copy-start | bytes 1924
  1.5 10.7 %copy-start.11 = (f32[96]{0:T(128)S(1)}, f32[96]{0:T(128)}, u32[]{:S(2)}) copy-start(f32[96]{0:T(128)} %param.9) | copy-start | bytes 1156
  1.5 11.2 %collective-permute-start = (bf16[64,2304]{1,0:T(8,128)(2,1)S(1)}, bf16[64,2304]{1,0:T(8,128)(2,1)S(1)}, u32[]{:S(2)}, u32[]{:S(2)}) collective-permute-start(bf16[64,2304]{1,0:T(8,128)(2,1)S(1)} %slice.30.refs_3_), channel_id=1, source_target_pairs={{0,8},{4,12},{8,0},{12,4},{16,24},{20,28},{24,16},{28,20},{1,9},{5... | collective-permute-start | bytes 884744 | tf_op jit(solution)/shard_map/ppermute | solution.py:253
  4.0 9.1 %collective-permute-start.1 = (bf16[64,2304]{1,0:T(8,128)(2,1)S(1)}, bf16[64,2304]{1,0:T(8,128)(2,1)S(1)}, u32[]{:S(2)}, u32[]{:S(2)}) collective-permute-start(bf16[64,2304]{1,0:T(8,128)(2,1)S(1)} %slice.30.refs_3_), channel_id=1, source_target_pairs={{0,16},{4,20},{8,24},{12,28},{16,0},{20,4},{24,8},{28,12},{1,17},{... | collective-permute-start | bytes 884744 | tf_op jit(solution)/shard_map/ppermute | solution.py:253
  9.6 2.4 %copy-start = (bf16[1152,2304]{1,0:T(8,128)(2,1)}, bf16[1152,2304]{1,0:T(8,128)(2,1)S(1)}, u32[]{:S(2)}) copy-start(bf16[1152,2304]{1,0:T(8,128)(2,1)S(1)} %transpose.14.refs_1_.refs_0_) | copy-start | bytes 15925252
  13.2 3.3 %copy-start.5 = (bf16[64,2304]{1,0:T(8,128)(2,1)}, bf16[64,2304]{1,0:T(8,128)(2,1)S(1)}, u32[]{:S(2)}) copy-start(bf16[64,2304]{1,0:T(8,128)(2,1)S(1)} %collective-permute-done.1.refs_5_) | copy-start | bytes 884740
  13.2 9.9 %collective-permute-start.2 = (bf16[32,2304]{1,0:T(8,128)(2,1)S(1)}, bf16[32,2304]{1,0:T(8,128)(2,1)S(1)}, u32[]{:S(2)}, u32[]{:S(2)}) collective-permute-start(bf16[32,2304]{1,0:T(8,128)(2,1)S(1)} %slice.33), channel_id=1, source_target_pairs={{0,8},{4,12},{8,0},{12,4},{16,24},{20,28},{24,16},{28,20},{1,9},{5... | collective-permute-start | bytes 442376 | tf_op jit(solution)/shard_map/ppermute | solution.py:253
  13.6 10.1 %collective-permute-start.3 = (bf16[32,2304]{1,0:T(8,128)(2,1)S(1)}, bf16[32,2304]{1,0:T(8,128)(2,1)S(1)}, u32[]{:S(2)}, u32[]{:S(2)}) collective-permute-start(bf16[32,2304]{1,0:T(8,128)(2,1)S(1)} %slice.34), channel_id=1, source_target_pairs={{0,16},{4,20},{8,24},{12,28},{16,0},{20,4},{24,8},{28,12},{1,17},{... | collective-permute-start | bytes 442376 | tf_op jit(solution)/shard_map/ppermute | solution.py:253
  16.5 39.7 %slice-start = ((s8[5308416]{0:T(1024)(128)(4,1)}), s8[1114112]{0:T(1024)(128)(4,1)S(1)}, s32[]{:S(2)}) async-start(s8[5308416]{0:T(1024)(128)(4,1)} %bitcast.10), calls=%async_computation | async-start | bytes 2228224
  20.6 2.4 %copy-start.2 = (bf16[1152,2304]{1,0:T(8,128)(2,1)}, bf16[1152,2304]{1,0:T(8,128)(2,1)S(1)}, u32[]{:S(2)}) copy-start(bf16[1152,2304]{1,0:T(8,128)(2,1)S(1)} %transpose.15.refs_2_.refs_1_) | copy-start | bytes 15925252
  23.1 0.7 copy-start.7
  23.7 0.7 copy-start.9
  24.4 16.3 %collective-permute-start.6 = (bf16[128,2304]{1,0:T(8,128)(2,1)S(1)}, bf16[128,2304]{1,0:T(8,128)(2,1)S(1)}, u32[]{:S(2)}, u32[]{:S(2)}) collective-permute-start(bf16[128,2304]{1,0:T(8,128)(2,1)S(1)} %slice.35.refs_2_), channel_id=1, source_target_pairs={{0,16},{4,20},{8,24},{12,28},{16,0},{20,4},{24,8},{28,12},{1,17},{... | collective-permute-start | bytes 1769480 | tf_op jit(solution)/shard_map/ppermute | solution.py:253
  24.8 29.8 %collective-permute-start.5 = (bf16[128,2304]{1,0:T(8,128)(2,1)S(1)}, bf16[128,2304]{1,0:T(8,128)(2,1)S(1)}, u32[]{:S(2)}, u32[]{:S(2)}) collective-permute-start(bf16[128,2304]{1,0:T(8,128)(2,1)S(1)} %slice.35.refs_2_), channel_id=1, source_target_pairs={{0,8},{4,12},{8,0},{12,4},{16,24},{20,28},{24,16},{28,20},{1,9},{5... | collective-permute-start | bytes 1769480 | tf_op jit(solution)/shard_map/ppermute | solution.py:253
  26.5 2.5 %copy-start.1 = (bf16[1152,2304]{1,0:T(8,128)(2,1)S(1)}, bf16[1152,2304]{1,0:T(8,128)(2,1)}, u32[]{:S(2)}) copy-start(bf16[1152,2304]{1,0:T(8,128)(2,1)} %copy-done) | copy-start | bytes 15925252
  29.0 2.5 %copy-start.3 = (bf16[1152,2304]{1,0:T(8,128)(2,1)S(1)}, bf16[1152,2304]{1,0:T(8,128)(2,1)}, u32[]{:S(2)}) copy-start(bf16[1152,2304]{1,0:T(8,128)(2,1)} %copy-done.2) | copy-start | bytes 15925252
  31.5 1.0 copy-start.6
  32.4 0.9 copy-start.8
  33.3 0.9 copy-start.10
  34.2 21.9 %slice-start.1 = ((s8[5308416]{0:T(1024)(128)(4,1)}), s8[4194304]{0:T(1024)(128)(4,1)S(1)}, s32[]{:S(2)}) async-start(s8[5308416]{0:T(1024)(128)(4,1)} %bitcast.10), calls=%async_computation.1 | async-start | bytes 8388608
  34.2 21.9 %copy-start.4 = (bf16[1152,2304]{1,0:T(8,128)(2,1)S(1)}, bf16[1152,2304]{1,0:T(8,128)(2,1)}, u32[]{:S(2)}) copy-start(bf16[1152,2304]{1,0:T(8,128)(2,1)} %copy-done.2) | copy-start | bytes 15925252
  39.1 13.7 %collective-permute-start.9 = (s16[1,4,304,128]{3,2,1,0:T(8,128)(2,1)S(1)}, s16[1,4,304,128]{3,2,1,0:T(8,128)(2,1)S(1)}, u32[]{:S(2)}, u32[]{:S(2)}) collective-permute-start(s16[1,4,304,128]{3,2,1,0:T(8,128)(2,1)S(1)} %get-tuple-element.80), channel_id=1, source_target_pairs={{0,1},{1,0},{2,3},{3,2},{4,5},{5,4},{6,7},{7,6},{8,9},{9,8},{10,11... | collective-permute-start | bytes 933896 | tf_op jit(solution)/shard_map/ppermute | solution.py:482
  40.7 15.4 %collective-permute-start.11 = (bf16[64,2304]{1,0:T(8,128)(2,1)S(1)}, bf16[64,2304]{1,0:T(8,128)(2,1)S(1)}, u32[]{:S(2)}, u32[]{:S(2)}) collective-permute-start(bf16[64,2304]{1,0:T(8,128)(2,1)S(1)} %slice.41), channel_id=1, source_target_pairs={{0,8},{4,12},{8,0},{12,4},{16,24},{20,28},{24,16},{28,20},{1,9},{5... | collective-permute-start | bytes 884744 | tf_op jit(solution)/shard_map/ppermute | solution.py:253
  41.3 19.1 %collective-permute-start.8 = (s16[1,4,304,128]{3,2,1,0:T(8,128)(2,1)S(1)}, s16[1,4,304,128]{3,2,1,0:T(8,128)(2,1)S(1)}, u32[]{:S(2)}, u32[]{:S(2)}) collective-permute-start(s16[1,4,304,128]{3,2,1,0:T(8,128)(2,1)S(1)} %get-tuple-element.79), channel_id=1, source_target_pairs={{0,1},{1,0},{2,3},{3,2},{4,5},{5,4},{6,7},{7,6},{8,9},{9,8},{10,11... | collective-permute-start | bytes 933896 | tf_op jit(solution)/shard_map/ppermute | solution.py:482
  52.9 12.2 %collective-permute-start.10 = (s16[1,4,304,128]{3,2,1,0:T(8,128)(2,1)S(1)}, s16[1,4,304,128]{3,2,1,0:T(8,128)(2,1)S(1)}, u32[]{:S(2)}, u32[]{:S(2)}) collective-permute-start(s16[1,4,304,128]{3,2,1,0:T(8,128)(2,1)S(1)} %get-tuple-element.82), channel_id=1, source_target_pairs={{0,2},{1,3},{2,0},{3,1},{4,6},{5,7},{6,4},{7,5},{8,10},{9,11},{10,... | collective-permute-start | bytes 933896 | tf_op jit(solution)/shard_map/ppermute | solution.py:482
  54.6 17.6 %collective-permute-start.7 = (bf16[64,2304]{1,0:T(8,128)(2,1)S(1)}, bf16[64,2304]{1,0:T(8,128)(2,1)S(1)}, u32[]{:S(2)}, u32[]{:S(2)}) collective-permute-start(bf16[64,2304]{1,0:T(8,128)(2,1)S(1)} %slice.40), channel_id=1, source_target_pairs={{0,16},{4,20},{8,24},{12,28},{16,0},{20,4},{24,8},{28,12},{1,17},{... | collective-permute-start | bytes 884744 | tf_op jit(solution)/shard_map/ppermute | solution.py:253
  65.4 5.3 %collective-permute-start.15 = (s16[2,304,128]{2,1,0:T(8,128)(2,1)S(1)}, s16[2,304,128]{2,1,0:T(8,128)(2,1)S(1)}, u32[]{:S(2)}, u32[]{:S(2)}) collective-permute-start(s16[2,304,128]{2,1,0:T(8,128)(2,1)S(1)} %get-tuple-element.93), channel_id=1, source_target_pairs={{0,8},{4,12},{8,0},{12,4},{16,24},{20,28},{24,16},{28,20},{1,9},{5... | collective-permute-start | bytes 466952 | tf_op jit(solution)/shard_map/ppermute | solution.py:253
  65.9 16.2 %collective-permute-start.12 = (s16[3,400,128]{2,1,0:T(8,128)(2,1)S(1)}, s16[3,400,128]{2,1,0:T(8,128)(2,1)S(1)}, u32[]{:S(2)}, u32[]{:S(2)}) collective-permute-start(s16[3,400,128]{2,1,0:T(8,128)(2,1)S(1)} %get-tuple-element.90), channel_id=1, source_target_pairs={{0,8},{4,12},{8,0},{12,4},{16,24},{20,28},{24,16},{28,20},{1,9},{5... | collective-permute-start | bytes 921608 | tf_op jit(solution)/shard_map/ppermute | solution.py:253
  67.5 14.7 %collective-permute-start.13 = (s16[3,400,128]{2,1,0:T(8,128)(2,1)S(1)}, s16[3,400,128]{2,1,0:T(8,128)(2,1)S(1)}, u32[]{:S(2)}, u32[]{:S(2)}) collective-permute-start(s16[3,400,128]{2,1,0:T(8,128)(2,1)S(1)} %get-tuple-element.91), channel_id=1, source_target_pairs={{0,16},{4,20},{8,24},{12,28},{16,0},{20,4},{24,8},{28,12},{1,17},{... | collective-permute-start | bytes 921608 | tf_op jit(solution)/shard_map/ppermute | solution.py:253
  68.9 13.3 %collective-permute-start.14 = (s16[3,400,128]{2,1,0:T(8,128)(2,1)S(1)}, s16[3,400,128]{2,1,0:T(8,128)(2,1)S(1)}, u32[]{:S(2)}, u32[]{:S(2)}) collective-permute-start(s16[3,400,128]{2,1,0:T(8,128)(2,1)S(1)} %get-tuple-element.92), channel_id=1, source_target_pairs={{0,24},{4,28},{8,16},{12,20},{16,8},{20,12},{24,0},{28,4},{1,25},{... | collective-permute-start | bytes 921608 | tf_op jit(solution)/shard_map/ppermute | solution.py:253
  70.7 8.6 %collective-permute-start.16 = (s16[2,304,128]{2,1,0:T(8,128)(2,1)S(1)}, s16[2,304,128]{2,1,0:T(8,128)(2,1)S(1)}, u32[]{:S(2)}, u32[]{:S(2)}) collective-permute-start(s16[2,304,128]{2,1,0:T(8,128)(2,1)S(1)} %pad_add_fusion), channel_id=1, source_target_pairs={{0,16},{4,20},{8,24},{12,28},{16,0},{20,4},{24,8},{28,12},{1,17},{... | collective-permute-start | bytes 466952 | tf_op jit(solution)/shard_map/ppermute | solution.py:253
  80.4 8.7 %collective-permute-start.20 = (s16[2,304,128]{2,1,0:T(8,128)(2,1)S(1)}, s16[2,304,128]{2,1,0:T(8,128)(2,1)S(1)}, u32[]{:S(2)}, u32[]{:S(2)}) collective-permute-start(s16[2,304,128]{2,1,0:T(8,128)(2,1)S(1)} %get-tuple-element.108), channel_id=1, source_target_pairs={{0,1},{1,0},{2,3},{3,2},{4,5},{5,4},{6,7},{7,6},{8,9},{9,8},{10,11... | collective-permute-start | bytes 466952 | tf_op jit(solution)/shard_map/ppermute | solution.py:482
  89.1 17.7 %collective-permute-start.21 = (s16[2,3,400,128]{3,2,1,0:T(8,128)(2,1)S(1)}, s16[2,3,400,128]{3,2,1,0:T(8,128)(2,1)S(1)}, u32[]{:S(2)}, u32[]{:S(2)}) collective-permute-start(s16[2,3,400,128]{3,2,1,0:T(8,128)(2,1)S(1)} %get-tuple-element.109), channel_id=1, source_target_pairs={{0,1},{1,0},{2,3},{3,2},{4,5},{5,4},{6,7},{7,6},{8,9},{9,8},{10,11... | collective-permute-start | bytes 1843208 | tf_op jit(solution)/shard_map/ppermute | solution.py:482
  89.1 6.9 %collective-permute-start.17 = (s16[3,400,128]{2,1,0:T(8,128)(2,1)S(1)}, s16[3,400,128]{2,1,0:T(8,128)(2,1)S(1)}, u32[]{:S(2)}, u32[]{:S(2)}) collective-permute-start(s16[3,400,128]{2,1,0:T(8,128)(2,1)S(1)} %get-tuple-element.96), channel_id=1, source_target_pairs={{0,8},{4,12},{8,0},{12,4},{16,24},{20,28},{24,16},{28,20},{1,9},{5... | collective-permute-start | bytes 921608 | tf_op jit(solution)/shard_map/ppermute | solution.py:253
  89.7 9.2 %collective-permute-start.18 = (s16[3,400,128]{2,1,0:T(8,128)(2,1)S(1)}, s16[3,400,128]{2,1,0:T(8,128)(2,1)S(1)}, u32[]{:S(2)}, u32[]{:S(2)}) collective-permute-start(s16[3,400,128]{2,1,0:T(8,128)(2,1)S(1)} %get-tuple-element.97), channel_id=1, source_target_pairs={{0,16},{4,20},{8,24},{12,28},{16,0},{20,4},{24,8},{28,12},{1,17},{... | collective-permute-start | bytes 921608 | tf_op jit(solution)/shard_map/ppermute | solution.py:253
  91.1 9.0 %collective-permute-start.19 = (s16[3,400,128]{2,1,0:T(8,128)(2,1)S(1)}, s16[3,400,128]{2,1,0:T(8,128)(2,1)S(1)}, u32[]{:S(2)}, u32[]{:S(2)}) collective-permute-start(s16[3,400,128]{2,1,0:T(8,128)(2,1)S(1)} %get-tuple-element.98), channel_id=1, source_target_pairs={{0,24},{4,28},{8,16},{12,20},{16,8},{20,12},{24,0},{28,4},{1,25},{... | collective-permute-start | bytes 921608 | tf_op jit(solution)/shard_map/ppermute | solution.py:253
  92.6 12.2 %collective-permute-start.22 = (s16[2,304,128]{2,1,0:T(8,128)(2,1)S(1)}, s16[2,304,128]{2,1,0:T(8,128)(2,1)S(1)}, u32[]{:S(2)}, u32[]{:S(2)}) collective-permute-start(s16[2,304,128]{2,1,0:T(8,128)(2,1)S(1)} %pad_add_fusion.1), channel_id=1, source_target_pairs={{0,2},{1,3},{2,0},{3,1},{4,6},{5,7},{6,4},{7,5},{8,10},{9,11},{10,... | collective-permute-start | bytes 466952 | tf_op jit(solution)/shard_map/ppermute | solution.py:482
  106.8 13.9 %collective-permute-start.24 = (s16[1,3,400,128]{3,2,1,0:T(8,128)(2,1)S(1)}, s16[1,3,400,128]{3,2,1,0:T(8,128)(2,1)S(1)}, u32[]{:S(2)}, u32[]{:S(2)}) collective-permute-start(s16[1,3,400,128]{3,2,1,0:T(8,128)(2,1)S(1)} %get-tuple-element.112), channel_id=1, source_target_pairs={{0,1},{1,0},{2,3},{3,2},{4,5},{5,4},{6,7},{7,6},{8,9},{9,8},{10,11... | collective-permute-start | bytes 921608 | tf_op jit(solution)/shard_map/ppermute | solution.py:482
  106.9 17.0 %collective-permute-start.23 = (s16[1,3,400,128]{3,2,1,0:T(8,128)(2,1)S(1)}, s16[1,3,400,128]{3,2,1,0:T(8,128)(2,1)S(1)}, u32[]{:S(2)}, u32[]{:S(2)}) collective-permute-start(s16[1,3,400,128]{3,2,1,0:T(8,128)(2,1)S(1)} %get-tuple-element.111), channel_id=1, source_target_pairs={{0,1},{1,0},{2,3},{3,2},{4,5},{5,4},{6,7},{7,6},{8,9},{9,8},{10,11... | collective-permute-start | bytes 921608 | tf_op jit(solution)/shard_map/ppermute | solution.py:482
  109.0 12.5 %collective-permute-start.26 = (s16[1,3,400,128]{3,2,1,0:T(8,128)(2,1)S(1)}, s16[1,3,400,128]{3,2,1,0:T(8,128)(2,1)S(1)}, u32[]{:S(2)}, u32[]{:S(2)}) collective-permute-start(s16[1,3,400,128]{3,2,1,0:T(8,128)(2,1)S(1)} %get-tuple-element.119), channel_id=1, source_target_pairs={{0,2},{1,3},{2,0},{3,1},{4,6},{5,7},{6,4},{7,5},{8,10},{9,11},{10,... | collective-permute-start | bytes 921608 | tf_op jit(solution)/shard_map/ppermute | solution.py:482
  120.8 10.4 %collective-permute-start.25 = (s16[1,3,400,128]{3,2,1,0:T(8,128)(2,1)S(1)}, s16[1,3,400,128]{3,2,1,0:T(8,128)(2,1)S(1)}, u32[]{:S(2)}, u32[]{:S(2)}) collective-permute-start(s16[1,3,400,128]{3,2,1,0:T(8,128)(2,1)S(1)} %get-tuple-element.118), channel_id=1, source_target_pairs={{0,2},{1,3},{2,0},{3,1},{4,6},{5,7},{6,4},{7,5},{8,10},{9,11},{10,... | collective-permute-start | bytes 921608 | tf_op jit(solution)/shard_map/ppermute | solution.py:482

commit v14 on v13

--- a/solution.py
+++ b/solution.py
@@ -271,7 +271,7 @@
         grid=(rows // column,),
         in_specs=[pl.BlockSpec((depth, column), lambda i: (0, i))],
         out_specs=vmem,
-        out_shape=jax.ShapeDtypeStruct((rows, depth), jnp.bfloat16),
+        out_shape=pltpu.VMEM((rows, depth), jnp.bfloat16),
         compiler_params=limit(16),
         cost_estimate=cost(0, 4 * rows * depth),
         name="transpose",
@@ -294,13 +294,16 @@
                 kernel,
                 in_specs=[*in_specs, vmem],
                 out_specs=[*out_specs, vmem],
-                out_shape=[*out_shape, jax.ShapeDtypeStruct(token.shape, token.dtype)],
+                out_shape=[
+                    pltpu.VMEM(x.shape, x.dtype) if spec is vmem else x
+                    for x, spec in zip((*out_shape, token), (*out_specs, vmem))
+                ],
                 scratch_shapes=scratch,
                 compiler_params=limit(mib),
                 cost_estimate=cost(flops, moved),
                 name=name,
                 **more,
-            )(*args, token)
+            )(*(in_vmem(x) if spec is vmem else x for x, spec in zip((*args, token), (*in_specs, vmem))))
 
         return call, inputs
 
@@ -423,6 +426,7 @@
             input_output_aliases={3 + len(got): 0} if given else {},
         )
 
+    in_vmem = functools.partial(pltpu.with_memory_space_constraint, memory_space=pltpu.VMEM)
     in_hbm = functools.partial(pltpu.with_memory_space_constraint, memory_space=pltpu.HBM)
     own_t = transpose(in_hbm(integrals))
     swapped = lax.ppermute(integrals, "pair", [(i, i ^ 1) for i in range(devices)])

time: 133 us -> 133 us (level)
  no operation moved by 1% of the time
where the time goes in v14:
time: 133 us
  waiting for transfers between devices  46.7 us (35%)
  Pallas kernels  36.8 us (28%)
  starting transfers between devices  32 us (24%)
  local copies, waits for them, and re-layouts  16.4 us (12%)
    ppermute x10, waiting for transfers between devices, across(): return lax.ppermute(x, 'slab', [(i, i ^ level) for i in range(slabs)])  36.9 us
    pallas_call x13, Pallas kernels, call(): pl.pallas_call(kernel, in_specs=[*in_specs, vmem], out_specs=[*out_specs,...  28.7 us
    ppermute x16, starting transfers between devices, to_chip(): return lax.ppermute(x, 'pair', [(i, i ^ d * CORES) for i in range(devices)])  19.4 us
    unnamed x32, local copies, waits for them, and re-layouts  13.9 us
    ppermute x10, starting transfers between devices, across(): return lax.ppermute(x, 'slab', [(i, i ^ level) for i in range(slabs)])  12.1 us
    ppermute x16, waiting for transfers between devices, to_chip(): return lax.ppermute(x, 'pair', [(i, i ^ d * CORES) for i in range(devices)])  9.82 us
    pallas_call x1, Pallas kernels, on_device(): sib_t = transpose(swapped)  4.1 us
    pallas_call x1, Pallas kernels, on_device(): own_t = transpose(in_hbm(integrals))  4 us
  transfers between devices with their start and end apart: 27, of which 14 were waited for; matrix products, arithmetic and copies ran while one was open for 2% of the time, Pallas kernels for 27%

profile of v14, /device:TPU:0, one launch (start us, length us, event | category | flops | bytes accessed | tf_op | source)
XLA Modules:
  0.0 132.7 jit_solution(9737512565334403378)
XLA Ops:
  0.5 1.0 slice.30.refs_3_
  1.5 2.6 %collective-permute-start = (bf16[64,2304]{1,0:T(8,128)(2,1)S(1)}, bf16[64,2304]{1,0:T(8,128)(2,1)S(1)}, u32[]{:S(2)}, u32[]{:S(2)}) collective-permute-start(bf16[64,2304]{1,0:T(8,128)(2,1)S(1)} %slice.30.refs_3_), channel_id=1, source_target_pairs={{0,8},{4,12},{8,0},{12,4},{16,24},{20,28},{24,16},{28,20},{1,9},{5... | collective-permute-start | bytes 884744 | tf_op jit(solution)/shard_map/ppermute | solution.py:253
  4.0 1.5 %collective-permute-start.1 = (bf16[64,2304]{1,0:T(8,128)(2,1)S(1)}, bf16[64,2304]{1,0:T(8,128)(2,1)S(1)}, u32[]{:S(2)}, u32[]{:S(2)}) collective-permute-start(bf16[64,2304]{1,0:T(8,128)(2,1)S(1)} %slice.30.refs_3_), channel_id=1, source_target_pairs={{0,16},{4,20},{8,24},{12,28},{16,0},{20,4},{24,8},{28,12},{1,17},{... | collective-permute-start | bytes 884744 | tf_op jit(solution)/shard_map/ppermute | solution.py:253
  5.5 4.0 %transpose.14.refs_1_.refs_0_ = bf16[1152,2304]{1,0:T(8,128)(2,1)S(1)} custom-call(bf16[2304,1152]{1,0:T(8,128)(2,1)} %in_ref.1), custom_call_target="tpu_custom_call" | custom-call | bytes 10616832 | tf_op jit(solution)/shard_map/transpose/pallas_call | solution.py:431
  9.6 2.3 %copy-done = bf16[1152,2304]{1,0:T(8,128)(2,1)} copy-done((bf16[1152,2304]{1,0:T(8,128)(2,1)}, bf16[1152,2304]{1,0:T(8,128)(2,1)S(1)}, u32[]{:S(2)}) %copy-start) | copy-done | bytes 5308440
  13.6 1.8 %collective-permute-start.3 = (bf16[32,2304]{1,0:T(8,128)(2,1)S(1)}, bf16[32,2304]{1,0:T(8,128)(2,1)S(1)}, u32[]{:S(2)}, u32[]{:S(2)}) collective-permute-start(bf16[32,2304]{1,0:T(8,128)(2,1)S(1)} %slice.34), channel_id=1, source_target_pairs={{0,16},{4,20},{8,24},{12,28},{16,0},{20,4},{24,8},{28,12},{1,17},{... | collective-permute-start | bytes 442376 | tf_op jit(solution)/shard_map/ppermute | solution.py:253
  15.4 1.1 slice.35.refs_2_
  16.5 4.1 %transpose.15.refs_2_.refs_1_ = bf16[1152,2304]{1,0:T(8,128)(2,1)S(1)} custom-call(bf16[2304,1152]{1,0:T(8,128)(2,1)} %collective-permute-done.4.in_ref), custom_call_target="tpu_custom_call" | custom-call | bytes 10616832 | tf_op jit(solution)/shard_map/transpose/pallas_call | solution.py:433
  20.6 2.4 %copy-done.2 = bf16[1152,2304]{1,0:T(8,128)(2,1)} copy-done((bf16[1152,2304]{1,0:T(8,128)(2,1)}, bf16[1152,2304]{1,0:T(8,128)(2,1)S(1)}, u32[]{:S(2)}) %copy-start.2) | copy-done | bytes 5308440
  24.8 1.7 %collective-permute-start.5 = (bf16[128,2304]{1,0:T(8,128)(2,1)S(1)}, bf16[128,2304]{1,0:T(8,128)(2,1)S(1)}, u32[]{:S(2)}, u32[]{:S(2)}) collective-permute-start(bf16[128,2304]{1,0:T(8,128)(2,1)S(1)} %slice.35.refs_2_), channel_id=1, source_target_pairs={{0,8},{4,12},{8,0},{12,4},{16,24},{20,28},{24,16},{28,20},{1,9},{5... | collective-permute-start | bytes 1769480 | tf_op jit(solution)/shard_map/ppermute | solution.py:253
  26.5 2.5 %copy-done.1 = bf16[1152,2304]{1,0:T(8,128)(2,1)S(1)} copy-done((bf16[1152,2304]{1,0:T(8,128)(2,1)S(1)}, bf16[1152,2304]{1,0:T(8,128)(2,1)}, u32[]{:S(2)}) %copy-start.1) | copy-done | bytes 5308440
  29.0 2.5 %copy-done.3 = bf16[1152,2304]{1,0:T(8,128)(2,1)S(1)} copy-done((bf16[1152,2304]{1,0:T(8,128)(2,1)S(1)}, bf16[1152,2304]{1,0:T(8,128)(2,1)}, u32[]{:S(2)}) %copy-start.3) | copy-done | bytes 5308440
  31.5 1.0 copy-done.6
  32.4 0.9 copy-done.8
  33.3 0.9 copy-done.10
  34.3 4.8 %early_ladder.1 = (f32[2,1152,128]{2,1,0:T(8,128)S(1)}, s16[1,4,304,128]{3,2,1,0:T(8,128)(2,1)S(1)}, s16[1,4,304,128]{3,2,1,0:T(8,128)(2,1)S(1)}, f32[8,128]{1,0:T(8,128)S(1)}) custom-call(s32[3]{0:T(128)S(1)} %pad_add_fusion.2.refs_0_, bf16[1152,2304]{1,0:T(8,128)(2,1)S(1)} %copy-done.1, bf16[1152,2304]{1,0:T(8,128)(2,1)S(1)} %copy-done.3, ...), custom_call_target="tpu_custom_call" | custom-call | flops 2717908992 | bytes 13598732 | tf_op jit(solution)/shard_map/early_ladder/pallas_call | solution.py:293
  39.1 1.7 %collective-permute-start.9 = (s16[1,4,304,128]{3,2,1,0:T(8,128)(2,1)S(1)}, s16[1,4,304,128]{3,2,1,0:T(8,128)(2,1)S(1)}, u32[]{:S(2)}, u32[]{:S(2)}) collective-permute-start(s16[1,4,304,128]{3,2,1,0:T(8,128)(2,1)S(1)} %get-tuple-element.80), channel_id=1, source_target_pairs={{0,1},{1,0},{2,3},{3,2},{4,5},{5,4},{6,7},{7,6},{8,9},{9,8},{10,11... | collective-permute-start | bytes 933896 | tf_op jit(solution)/shard_map/ppermute | solution.py:486
  41.6 11.1 %collective-permute-done.9.refs_1_ = s16[1,4,304,128]{3,2,1,0:T(8,128)(2,1)S(1)} collective-permute-done((s16[1,4,304,128]{3,2,1,0:T(8,128)(2,1)S(1)}, s16[1,4,304,128]{3,2,1,0:T(8,128)(2,1)S(1)}, u32[]{:S(2)}, u32[]{:S(2)}) %collective-permute-start.9) | collective-permute-done | bytes 311328 | tf_op jit(solution)/shard_map/ppermute | solution.py:486
  52.9 1.6 %collective-permute-start.10 = (s16[1,4,304,128]{3,2,1,0:T(8,128)(2,1)S(1)}, s16[1,4,304,128]{3,2,1,0:T(8,128)(2,1)S(1)}, u32[]{:S(2)}, u32[]{:S(2)}) collective-permute-start(s16[1,4,304,128]{3,2,1,0:T(8,128)(2,1)S(1)} %get-tuple-element.82), channel_id=1, source_target_pairs={{0,2},{1,3},{2,0},{3,1},{4,6},{5,7},{6,4},{7,5},{8,10},{9,11},{10,... | collective-permute-start | bytes 933896 | tf_op jit(solution)/shard_map/ppermute | solution.py:486
  54.6 1.6 %collective-permute-start.7 = (bf16[64,2304]{1,0:T(8,128)(2,1)S(1)}, bf16[64,2304]{1,0:T(8,128)(2,1)S(1)}, u32[]{:S(2)}, u32[]{:S(2)}) collective-permute-start(bf16[64,2304]{1,0:T(8,128)(2,1)S(1)} %slice.40), channel_id=1, source_target_pairs={{0,16},{4,20},{8,24},{12,28},{16,0},{20,4},{24,8},{28,12},{1,17},{... | collective-permute-start | bytes 884744 | tf_op jit(solution)/shard_map/ppermute | solution.py:253
  56.2 4.2 %ladder.2 = (s16[3,400,128]{2,1,0:T(8,128)(2,1)S(1)}, s16[3,400,128]{2,1,0:T(8,128)(2,1)S(1)}, s16[3,400,128]{2,1,0:T(8,128)(2,1)S(1)}, s16[3,400,128]{2,1,0:T(8,128)(2,1)S(1)}, f32[8,128]{1,0:T(8,128)S(1)}) custom-call(bf16[1152,2304]{1,0:T(8,128)(2,1)S(1)} %bitcast.11, bf16[1152,2304]{1,0:T(8,128)(2,1)S(1)} %copy-done.4, ...), custom_call_target="tpu_custom_call" | custom-call | flops 2717908992 | bytes 13910016 | tf_op jit(solution)/shard_map/ladder/pallas_call | solution.py:293
  60.4 4.7 %collective-permute-done.10.refs_2_ = s16[1,4,304,128]{3,2,1,0:T(8,128)(2,1)S(1)} collective-permute-done((s16[1,4,304,128]{3,2,1,0:T(8,128)(2,1)S(1)}, s16[1,4,304,128]{3,2,1,0:T(8,128)(2,1)S(1)}, u32[]{:S(2)}, u32[]{:S(2)}) %collective-permute-start.10) | collective-permute-done | bytes 311328 | tf_op jit(solution)/shard_map/ppermute | solution.py:486
  65.9 1.6 %collective-permute-start.12 = (s16[3,400,128]{2,1,0:T(8,128)(2,1)S(1)}, s16[3,400,128]{2,1,0:T(8,128)(2,1)S(1)}, u32[]{:S(2)}, u32[]{:S(2)}) collective-permute-start(s16[3,400,128]{2,1,0:T(8,128)(2,1)S(1)} %get-tuple-element.90), channel_id=1, source_target_pairs={{0,8},{4,12},{8,0},{12,4},{16,24},{20,28},{24,16},{28,20},{1,9},{5... | collective-permute-start | bytes 921608 | tf_op jit(solution)/shard_map/ppermute | solution.py:253
  67.5 1.4 %collective-permute-start.13 = (s16[3,400,128]{2,1,0:T(8,128)(2,1)S(1)}, s16[3,400,128]{2,1,0:T(8,128)(2,1)S(1)}, u32[]{:S(2)}, u32[]{:S(2)}) collective-permute-start(s16[3,400,128]{2,1,0:T(8,128)(2,1)S(1)} %get-tuple-element.91), channel_id=1, source_target_pairs={{0,16},{4,20},{8,24},{12,28},{16,0},{20,4},{24,8},{28,12},{1,17},{... | collective-permute-start | bytes 921608 | tf_op jit(solution)/shard_map/ppermute | solution.py:253
  69.4 1.3 collective-permute-done.15.refs_2_
  70.7 1.5 %collective-permute-start.16 = (s16[2,304,128]{2,1,0:T(8,128)(2,1)S(1)}, s16[2,304,128]{2,1,0:T(8,128)(2,1)S(1)}, u32[]{:S(2)}, u32[]{:S(2)}) collective-permute-start(s16[2,304,128]{2,1,0:T(8,128)(2,1)S(1)} %pad_add_fusion), channel_id=1, source_target_pairs={{0,16},{4,20},{8,24},{12,28},{16,0},{20,4},{24,8},{28,12},{1,17},{... | collective-permute-start | bytes 466952 | tf_op jit(solution)/shard_map/ppermute | solution.py:253
  72.2 4.2 %ladder.3 = (s16[3,400,128]{2,1,0:T(8,128)(2,1)S(1)}, s16[3,400,128]{2,1,0:T(8,128)(2,1)S(1)}, s16[3,400,128]{2,1,0:T(8,128)(2,1)S(1)}, s16[3,400,128]{2,1,0:T(8,128)(2,1)S(1)}, f32[8,128]{1,0:T(8,128)S(1)}) custom-call(bf16[1152,2304]{1,0:T(8,128)(2,1)S(1)} %bitcast.11, bf16[1152,2304]{1,0:T(8,128)(2,1)S(1)} %copy-done.4, ...), custom_call_target="tpu_custom_call" | custom-call | flops 2717908992 | bytes 13910016 | tf_op jit(solution)/shard_map/ladder/pallas_call | solution.py:293
  76.4 2.9 %collective-permute-done.16.refs_3_ = s16[2,304,128]{2,1,0:T(8,128)(2,1)S(1)} collective-permute-done((s16[2,304,128]{2,1,0:T(8,128)(2,1)S(1)}, s16[2,304,128]{2,1,0:T(8,128)(2,1)S(1)}, u32[]{:S(2)}, u32[]{:S(2)}) %collective-permute-start.16) | collective-permute-done | bytes 155680 | tf_op jit(solution)/shard_map/ppermute | solution.py:253
  79.3 1.1 early_antisym.1
  80.4 1.8 %collective-permute-start.20 = (s16[2,304,128]{2,1,0:T(8,128)(2,1)S(1)}, s16[2,304,128]{2,1,0:T(8,128)(2,1)S(1)}, u32[]{:S(2)}, u32[]{:S(2)}) collective-permute-start(s16[2,304,128]{2,1,0:T(8,128)(2,1)S(1)} %get-tuple-element.108), channel_id=1, source_target_pairs={{0,1},{1,0},{2,3},{3,2},{4,5},{5,4},{6,7},{7,6},{8,9},{9,8},{10,11... | collective-permute-start | bytes 466952 | tf_op jit(solution)/shard_map/ppermute | solution.py:486
  82.2 4.7 %antisym.2 = (f32[2,1152,128]{2,1,0:T(8,128)S(1)}, s16[2,3,400,128]{3,2,1,0:T(8,128)(2,1)S(1)}, f32[8,128]{1,0:T(8,128)S(1)}) custom-call(s32[3]{0:T(128)S(1)} %pad_add_fusion.2.refs_0_, s16[3,400,128]{2,1,0:T(8,128)(2,1)S(1)} %get-tuple-element.99.refs_1_, s16[3,400,128]{2,1,0:T(8,128)(2,1)S(1)} %collective-permute-done.12.refs_2_, ...), custom_call_target="tpu_custom_call" | custom-call | flops 9437184 | bytes 3022860 | tf_op jit(solution)/shard_map/antisym/pallas_call | solution.py:293
  86.9 2.2 %collective-permute-done.20.refs_3_ = s16[2,304,128]{2,1,0:T(8,128)(2,1)S(1)} collective-permute-done((s16[2,304,128]{2,1,0:T(8,128)(2,1)S(1)}, s16[2,304,128]{2,1,0:T(8,128)(2,1)S(1)}, u32[]{:S(2)}, u32[]{:S(2)}) %collective-permute-start.20) | collective-permute-done | bytes 155680 | tf_op jit(solution)/shard_map/ppermute | solution.py:486
  89.7 1.5 %collective-permute-start.18 = (s16[3,400,128]{2,1,0:T(8,128)(2,1)S(1)}, s16[3,400,128]{2,1,0:T(8,128)(2,1)S(1)}, u32[]{:S(2)}, u32[]{:S(2)}) collective-permute-start(s16[3,400,128]{2,1,0:T(8,128)(2,1)S(1)} %get-tuple-element.97), channel_id=1, source_target_pairs={{0,16},{4,20},{8,24},{12,28},{16,0},{20,4},{24,8},{28,12},{1,17},{... | collective-permute-start | bytes 921608 | tf_op jit(solution)/shard_map/ppermute | solution.py:253
  91.1 1.5 %collective-permute-start.19 = (s16[3,400,128]{2,1,0:T(8,128)(2,1)S(1)}, s16[3,400,128]{2,1,0:T(8,128)(2,1)S(1)}, u32[]{:S(2)}, u32[]{:S(2)}) collective-permute-start(s16[3,400,128]{2,1,0:T(8,128)(2,1)S(1)} %get-tuple-element.98), channel_id=1, source_target_pairs={{0,24},{4,28},{8,16},{12,20},{16,8},{20,12},{24,0},{28,4},{1,25},{... | collective-permute-start | bytes 921608 | tf_op jit(solution)/shard_map/ppermute | solution.py:253
  92.6 2.3 %collective-permute-start.22 = (s16[2,304,128]{2,1,0:T(8,128)(2,1)S(1)}, s16[2,304,128]{2,1,0:T(8,128)(2,1)S(1)}, u32[]{:S(2)}, u32[]{:S(2)}) collective-permute-start(s16[2,304,128]{2,1,0:T(8,128)(2,1)S(1)} %pad_add_fusion.1), channel_id=1, source_target_pairs={{0,2},{1,3},{2,0},{3,1},{4,6},{5,7},{6,4},{7,5},{8,10},{9,11},{10,... | collective-permute-start | bytes 466952 | tf_op jit(solution)/shard_map/ppermute | solution.py:486
  94.9 1.1 collective-permute-done.17.refs_2_
  96.0 2.8 %collective-permute-done.18.refs_3_ = s16[3,400,128]{2,1,0:T(8,128)(2,1)S(1)} collective-permute-done((s16[3,400,128]{2,1,0:T(8,128)(2,1)S(1)}, s16[3,400,128]{2,1,0:T(8,128)(2,1)S(1)}, u32[]{:S(2)}, u32[]{:S(2)}) %collective-permute-start.18) | collective-permute-done | bytes 307232 | tf_op jit(solution)/shard_map/ppermute | solution.py:253
  98.8 1.3 collective-permute-done.19.refs_4_
  100.1 4.7 %antisym.3 = (f32[2,1152,128]{2,1,0:T(8,128)S(1)}, s16[1,3,400,128]{3,2,1,0:T(8,128)(2,1)S(1)}, s16[1,3,400,128]{3,2,1,0:T(8,128)(2,1)S(1)}, f32[8,128]{1,0:T(8,128)S(1)}) custom-call(s32[3]{0:T(128)S(1)} %pad_add_fusion.2.refs_0_, s16[3,400,128]{2,1,0:T(8,128)(2,1)S(1)} %get-tuple-element.95.refs_1_, ...), custom_call_target="tpu_custom_call" | custom-call | flops 9437184 | bytes 3022860 | tf_op jit(solution)/shard_map/antisym/pallas_call | solution.py:293
  104.8 1.9 %collective-permute-done.21.refs_1_.refs_3_ = s16[2,3,400,128]{3,2,1,0:T(8,128)(2,1)S(1)} collective-permute-done((s16[2,3,400,128]{3,2,1,0:T(8,128)(2,1)S(1)}, s16[2,3,400,128]{3,2,1,0:T(8,128)(2,1)S(1)}, u32[]{:S(2)}, u32[]{:S(2)}) %collective-permute-start.21) | collective-permute-done | bytes 614432 | tf_op jit(solution)/shard_map/ppermute | solution.py:486
  106.9 1.9 %collective-permute-start.23 = (s16[1,3,400,128]{3,2,1,0:T(8,128)(2,1)S(1)}, s16[1,3,400,128]{3,2,1,0:T(8,128)(2,1)S(1)}, u32[]{:S(2)}, u32[]{:S(2)}) collective-permute-start(s16[1,3,400,128]{3,2,1,0:T(8,128)(2,1)S(1)} %get-tuple-element.111), channel_id=1, source_target_pairs={{0,1},{1,0},{2,3},{3,2},{4,5},{5,4},{6,7},{7,6},{8,9},{9,8},{10,11... | collective-permute-start | bytes 921608 | tf_op jit(solution)/shard_map/ppermute | solution.py:486
  109.0 2.0 %collective-permute-start.26 = (s16[1,3,400,128]{3,2,1,0:T(8,128)(2,1)S(1)}, s16[1,3,400,128]{3,2,1,0:T(8,128)(2,1)S(1)}, u32[]{:S(2)}, u32[]{:S(2)}) collective-permute-start(s16[1,3,400,128]{3,2,1,0:T(8,128)(2,1)S(1)} %get-tuple-element.119), channel_id=1, source_target_pairs={{0,2},{1,3},{2,0},{3,1},{4,6},{5,7},{6,4},{7,5},{8,10},{9,11},{10,... | collective-permute-start | bytes 921608 | tf_op jit(solution)/shard_map/ppermute | solution.py:486
  111.0 1.4 %finish.3 = (f32[192,2304]{1,0:T(8,128)}, f32[8,128]{1,0:T(8,128)S(1)}) custom-call(f32[3,1,128]{2,1,0:T(1,128)S(1)} %pad_maximum_fusion.refs_0_, f32[1152,2]{1,0:T(8,128)S(1)} %bitcast.12, f32[288,128]{1,0:T(8,128)S(1)} %get-tuple-element.113.refs_2_, s16[2,304,128]{2,1,0:T(8,128)(2,1)S(1)} %collective-permute-done.20.refs_3_, ...), custom_call_target="tpu_custom_call" | custom-call | flops 2359296 | bytes 2238976 | tf_op jit(solution)/shard_map/finish/pallas_call | solution.py:293
  112.3 8.3 %collective-permute-done.24.refs_1_ = s16[1,3,400,128]{3,2,1,0:T(8,128)(2,1)S(1)} collective-permute-done((s16[1,3,400,128]{3,2,1,0:T(8,128)(2,1)S(1)}, s16[1,3,400,128]{3,2,1,0:T(8,128)(2,1)S(1)}, u32[]{:S(2)}, u32[]{:S(2)}) %collective-permute-start.24) | collective-permute-done | bytes 307232 | tf_op jit(solution)/shard_map/ppermute | solution.py:486
  121.5 1.4 %finish.4 = (f32[192,2304]{1,0:T(8,128)}, f32[8,128]{1,0:T(8,128)S(1)}) custom-call(f32[3,1,128]{2,1,0:T(1,128)S(1)} %pad_maximum_fusion.refs_0_, f32[1152,2]{1,0:T(8,128)S(1)} %bitcast.13, f32[2,1152,128]{2,1,0:T(8,128)S(1)} %get-tuple-element.114.refs_0_.refs_2_, ...), custom_call_target="tpu_custom_call", output_to_operand_aliasing={{0}: (5, {})} | custom-call | flops 2359296 | bytes 5650944 | tf_op jit(solution)/shard_map/finish/pallas_call | solution.py:293
  122.9 1.1 collective-permute-done.23.refs_3_
  123.9 7.3 %collective-permute-done.25.refs_4_ = s16[1,3,400,128]{3,2,1,0:T(8,128)(2,1)S(1)} collective-permute-done((s16[1,3,400,128]{3,2,1,0:T(8,128)(2,1)S(1)}, s16[1,3,400,128]{3,2,1,0:T(8,128)(2,1)S(1)}, u32[]{:S(2)}, u32[]{:S(2)}) %collective-permute-start.25) | collective-permute-done | bytes 307232 | tf_op jit(solution)/shard_map/ppermute | solution.py:486
  131.3 1.4 %finish.5 = (f32[192,2304]{1,0:T(8,128)}, f32[8,128]{1,0:T(8,128)}) custom-call(f32[3,1,128]{2,1,0:T(1,128)S(1)} %pad_maximum_fusion.refs_0_, f32[1152,2]{1,0:T(8,128)S(1)} %bitcast.14, f32[2,1152,128]{2,1,0:T(8,128)S(1)} %get-tuple-element.104.refs_0_.refs_2_, ...), custom_call_target="tpu_custom_call", output_to_operand_aliasing={{0}: (5, {})} | custom-call | flops 2359296 | bytes 5343744 | tf_op jit(solution)/shard_map/finish/pallas_call | solution.py:293
  (77 shorter events, 8.1 us)
Async XLA Ops:
  0.0 16.5 %collective-permute-start.4 = (bf16[2304,1152]{1,0:T(8,128)(2,1)}, bf16[2304,1152]{1,0:T(8,128)(2,1)}, u32[]{:S(2)}, u32[]{:S(2)}) collective-permute-start(bf16[2304,1152]{1,0:T(8,128)(2,1)} %in_ref.1), channel_id=1, source_target_pairs={{0,4},{4,0},{8,12},{12,8},{16,20},{20,16},{24,28},{28,24},{1,5},{5... | collective-permute-start | bytes 15925256 | tf_op jit(solution)/shard_map/ppermute | solution.py:432
  1.4 10.5 %copy-start.12 = (s32[192,2]{0,1:T(2,128)S(1)}, s32[192,2]{0,1:T(2,128)}, u32[]{:S(2)}) copy-start(s32[192,2]{0,1:T(2,128)} %param.7) | copy-start | bytes 4612
  1.4 10.5 %copy-start.13 = (f32[160]{0:T(256)S(1)}, f32[160]{0:T(256)}, u32[]{:S(2)}) copy-start(f32[160]{0:T(256)} %param.8) | copy-start | bytes 1924
  1.5 10.7 %copy-start.11 = (f32[96]{0:T(128)S(1)}, f32[96]{0:T(128)}, u32[]{:S(2)}) copy-start(f32[96]{0:T(128)} %param.9) | copy-start | bytes 1156
  1.5 11.2 %collective-permute-start = (bf16[64,2304]{1,0:T(8,128)(2,1)S(1)}, bf16[64,2304]{1,0:T(8,128)(2,1)S(1)}, u32[]{:S(2)}, u32[]{:S(2)}) collective-permute-start(bf16[64,2304]{1,0:T(8,128)(2,1)S(1)} %slice.30.refs_3_), channel_id=1, source_target_pairs={{0,8},{4,12},{8,0},{12,4},{16,24},{20,28},{24,16},{28,20},{1,9},{5... | collective-permute-start | bytes 884744 | tf_op jit(solution)/shard_map/ppermute | solution.py:253
  4.0 9.1 %collective-permute-start.1 = (bf16[64,2304]{1,0:T(8,128)(2,1)S(1)}, bf16[64,2304]{1,0:T(8,128)(2,1)S(1)}, u32[]{:S(2)}, u32[]{:S(2)}) collective-permute-start(bf16[64,2304]{1,0:T(8,128)(2,1)S(1)} %slice.30.refs_3_), channel_id=1, source_target_pairs={{0,16},{4,20},{8,24},{12,28},{16,0},{20,4},{24,8},{28,12},{1,17},{... | collective-permute-start | bytes 884744 | tf_op jit(solution)/shard_map/ppermute | solution.py:253
  9.6 2.4 %copy-start = (bf16[1152,2304]{1,0:T(8,128)(2,1)}, bf16[1152,2304]{1,0:T(8,128)(2,1)S(1)}, u32[]{:S(2)}) copy-start(bf16[1152,2304]{1,0:T(8,128)(2,1)S(1)} %transpose.14.refs_1_.refs_0_) | copy-start | bytes 15925252
  13.2 3.3 %copy-start.5 = (bf16[64,2304]{1,0:T(8,128)(2,1)}, bf16[64,2304]{1,0:T(8,128)(2,1)S(1)}, u32[]{:S(2)}) copy-start(bf16[64,2304]{1,0:T(8,128)(2,1)S(1)} %collective-permute-done.1.refs_5_) | copy-start | bytes 884740
  13.2 9.9 %collective-permute-start.2 = (bf16[32,2304]{1,0:T(8,128)(2,1)S(1)}, bf16[32,2304]{1,0:T(8,128)(2,1)S(1)}, u32[]{:S(2)}, u32[]{:S(2)}) collective-permute-start(bf16[32,2304]{1,0:T(8,128)(2,1)S(1)} %slice.33), channel_id=1, source_target_pairs={{0,8},{4,12},{8,0},{12,4},{16,24},{20,28},{24,16},{28,20},{1,9},{5... | collective-permute-start | bytes 442376 | tf_op jit(solution)/shard_map/ppermute | solution.py:253
  13.6 10.1 %collective-permute-start.3 = (bf16[32,2304]{1,0:T(8,128)(2,1)S(1)}, bf16[32,2304]{1,0:T(8,128)(2,1)S(1)}, u32[]{:S(2)}, u32[]{:S(2)}) collective-permute-start(bf16[32,2304]{1,0:T(8,128)(2,1)S(1)} %slice.34), channel_id=1, source_target_pairs={{0,16},{4,20},{8,24},{12,28},{16,0},{20,4},{24,8},{28,12},{1,17},{... | collective-permute-start | bytes 442376 | tf_op jit(solution)/shard_map/ppermute | solution.py:253
  16.5 39.7 %slice-start = ((s8[5308416]{0:T(1024)(128)(4,1)}), s8[1114112]{0:T(1024)(128)(4,1)S(1)}, s32[]{:S(2)}) async-start(s8[5308416]{0:T(1024)(128)(4,1)} %bitcast.10), calls=%async_computation | async-start | bytes 2228224
  20.6 2.4 %copy-start.2 = (bf16[1152,2304]{1,0:T(8,128)(2,1)}, bf16[1152,2304]{1,0:T(8,128)(2,1)S(1)}, u32[]{:S(2)}) copy-start(bf16[1152,2304]{1,0:T(8,128)(2,1)S(1)} %transpose.15.refs_2_.refs_1_) | copy-start | bytes 15925252
  23.1 0.7 copy-start.7
  23.7 0.7 copy-start.9
  24.4 16.3 %collective-permute-start.6 = (bf16[128,2304]{1,0:T(8,128)(2,1)S(1)}, bf16[128,2304]{1,0:T(8,128)(2,1)S(1)}, u32[]{:S(2)}, u32[]{:S(2)}) collective-permute-start(bf16[128,2304]{1,0:T(8,128)(2,1)S(1)} %slice.35.refs_2_), channel_id=1, source_target_pairs={{0,16},{4,20},{8,24},{12,28},{16,0},{20,4},{24,8},{28,12},{1,17},{... | collective-permute-start | bytes 1769480 | tf_op jit(solution)/shard_map/ppermute | solution.py:253
  24.8 29.8 %collective-permute-start.5 = (bf16[128,2304]{1,0:T(8,128)(2,1)S(1)}, bf16[128,2304]{1,0:T(8,128)(2,1)S(1)}, u32[]{:S(2)}, u32[]{:S(2)}) collective-permute-start(bf16[128,2304]{1,0:T(8,128)(2,1)S(1)} %slice.35.refs_2_), channel_id=1, source_target_pairs={{0,8},{4,12},{8,0},{12,4},{16,24},{20,28},{24,16},{28,20},{1,9},{5... | collective-permute-start | bytes 1769480 | tf_op jit(solution)/shard_map/ppermute | solution.py:253
  26.5 2.5 %copy-start.1 = (bf16[1152,2304]{1,0:T(8,128)(2,1)S(1)}, bf16[1152,2304]{1,0:T(8,128)(2,1)}, u32[]{:S(2)}) copy-start(bf16[1152,2304]{1,0:T(8,128)(2,1)} %copy-done) | copy-start | bytes 15925252
  29.0 2.5 %copy-start.3 = (bf16[1152,2304]{1,0:T(8,128)(2,1)S(1)}, bf16[1152,2304]{1,0:T(8,128)(2,1)}, u32[]{:S(2)}) copy-start(bf16[1152,2304]{1,0:T(8,128)(2,1)} %copy-done.2) | copy-start | bytes 15925252
  31.5 1.0 copy-start.6
  32.4 0.9 copy-start.8
  33.3 0.9 copy-start.10
  34.2 21.9 %slice-start.1 = ((s8[5308416]{0:T(1024)(128)(4,1)}), s8[4194304]{0:T(1024)(128)(4,1)S(1)}, s32[]{:S(2)}) async-start(s8[5308416]{0:T(1024)(128)(4,1)} %bitcast.10), calls=%async_computation.1 | async-start | bytes 8388608
  34.2 21.9 %copy-start.4 = (bf16[1152,2304]{1,0:T(8,128)(2,1)S(1)}, bf16[1152,2304]{1,0:T(8,128)(2,1)}, u32[]{:S(2)}) copy-start(bf16[1152,2304]{1,0:T(8,128)(2,1)} %copy-done.2) | copy-start | bytes 15925252
  39.1 13.7 %collective-permute-start.9 = (s16[1,4,304,128]{3,2,1,0:T(8,128)(2,1)S(1)}, s16[1,4,304,128]{3,2,1,0:T(8,128)(2,1)S(1)}, u32[]{:S(2)}, u32[]{:S(2)}) collective-permute-start(s16[1,4,304,128]{3,2,1,0:T(8,128)(2,1)S(1)} %get-tuple-element.80), channel_id=1, source_target_pairs={{0,1},{1,0},{2,3},{3,2},{4,5},{5,4},{6,7},{7,6},{8,9},{9,8},{10,11... | collective-permute-start | bytes 933896 | tf_op jit(solution)/shard_map/ppermute | solution.py:486
  40.7 15.4 %collective-permute-start.11 = (bf16[64,2304]{1,0:T(8,128)(2,1)S(1)}, bf16[64,2304]{1,0:T(8,128)(2,1)S(1)}, u32[]{:S(2)}, u32[]{:S(2)}) collective-permute-start(bf16[64,2304]{1,0:T(8,128)(2,1)S(1)} %slice.41), channel_id=1, source_target_pairs={{0,8},{4,12},{8,0},{12,4},{16,24},{20,28},{24,16},{28,20},{1,9},{5... | collective-permute-start | bytes 884744 | tf_op jit(solution)/shard_map/ppermute | solution.py:253
  41.3 19.1 %collective-permute-start.8 = (s16[1,4,304,128]{3,2,1,0:T(8,128)(2,1)S(1)}, s16[1,4,304,128]{3,2,1,0:T(8,128)(2,1)S(1)}, u32[]{:S(2)}, u32[]{:S(2)}) collective-permute-start(s16[1,4,304,128]{3,2,1,0:T(8,128)(2,1)S(1)} %get-tuple-element.79), channel_id=1, source_target_pairs={{0,1},{1,0},{2,3},{3,2},{4,5},{5,4},{6,7},{7,6},{8,9},{9,8},{10,11... | collective-permute-start | bytes 933896 | tf_op jit(solution)/shard_map/ppermute | solution.py:486
  52.9 12.2 %collective-permute-start.10 = (s16[1,4,304,128]{3,2,1,0:T(8,128)(2,1)S(1)}, s16[1,4,304,128]{3,2,1,0:T(8,128)(2,1)S(1)}, u32[]{:S(2)}, u32[]{:S(2)}) collective-permute-start(s16[1,4,304,128]{3,2,1,0:T(8,128)(2,1)S(1)} %get-tuple-element.82), channel_id=1, source_target_pairs={{0,2},{1,3},{2,0},{3,1},{4,6},{5,7},{6,4},{7,5},{8,10},{9,11},{10,... | collective-permute-start | bytes 933896 | tf_op jit(solution)/shard_map/ppermute | solution.py:486
  54.6 17.6 %collective-permute-start.7 = (bf16[64,2304]{1,0:T(8,128)(2,1)S(1)}, bf16[64,2304]{1,0:T(8,128)(2,1)S(1)}, u32[]{:S(2)}, u32[]{:S(2)}) collective-permute-start(bf16[64,2304]{1,0:T(8,128)(2,1)S(1)} %slice.40), channel_id=1, source_target_pairs={{0,16},{4,20},{8,24},{12,28},{16,0},{20,4},{24,8},{28,12},{1,17},{... | collective-permute-start | bytes 884744 | tf_op jit(solution)/shard_map/ppermute | solution.py:253
  65.4 5.3 %collective-permute-start.15 = (s16[2,304,128]{2,1,0:T(8,128)(2,1)S(1)}, s16[2,304,128]{2,1,0:T(8,128)(2,1)S(1)}, u32[]{:S(2)}, u32[]{:S(2)}) collective-permute-start(s16[2,304,128]{2,1,0:T(8,128)(2,1)S(1)} %get-tuple-element.93), channel_id=1, source_target_pairs={{0,8},{4,12},{8,0},{12,4},{16,24},{20,28},{24,16},{28,20},{1,9},{5... | collective-permute-start | bytes 466952 | tf_op jit(solution)/shard_map/ppermute | solution.py:253
  65.9 16.2 %collective-permute-start.12 = (s16[3,400,128]{2,1,0:T(8,128)(2,1)S(1)}, s16[3,400,128]{2,1,0:T(8,128)(2,1)S(1)}, u32[]{:S(2)}, u32[]{:S(2)}) collective-permute-start(s16[3,400,128]{2,1,0:T(8,128)(2,1)S(1)} %get-tuple-element.90), channel_id=1, source_target_pairs={{0,8},{4,12},{8,0},{12,4},{16,24},{20,28},{24,16},{28,20},{1,9},{5... | collective-permute-start | bytes 921608 | tf_op jit(solution)/shard_map/ppermute | solution.py:253
  67.5 14.7 %collective-permute-start.13 = (s16[3,400,128]{2,1,0:T(8,128)(2,1)S(1)}, s16[3,400,128]{2,1,0:T(8,128)(2,1)S(1)}, u32[]{:S(2)}, u32[]{:S(2)}) collective-permute-start(s16[3,400,128]{2,1,0:T(8,128)(2,1)S(1)} %get-tuple-element.91), channel_id=1, source_target_pairs={{0,16},{4,20},{8,24},{12,28},{16,0},{20,4},{24,8},{28,12},{1,17},{... | collective-permute-start | bytes 921608 | tf_op jit(solution)/shard_map/ppermute | solution.py:253
  68.9 13.3 %collective-permute-start.14 = (s16[3,400,128]{2,1,0:T(8,128)(2,1)S(1)}, s16[3,400,128]{2,1,0:T(8,128)(2,1)S(1)}, u32[]{:S(2)}, u32[]{:S(2)}) collective-permute-start(s16[3,400,128]{2,1,0:T(8,128)(2,1)S(1)} %get-tuple-element.92), channel_id=1, source_target_pairs={{0,24},{4,28},{8,16},{12,20},{16,8},{20,12},{24,0},{28,4},{1,25},{... | collective-permute-start | bytes 921608 | tf_op jit(solution)/shard_map/ppermute | solution.py:253
  70.7 8.6 %collective-permute-start.16 = (s16[2,304,128]{2,1,0:T(8,128)(2,1)S(1)}, s16[2,304,128]{2,1,0:T(8,128)(2,1)S(1)}, u32[]{:S(2)}, u32[]{:S(2)}) collective-permute-start(s16[2,304,128]{2,1,0:T(8,128)(2,1)S(1)} %pad_add_fusion), channel_id=1, source_target_pairs={{0,16},{4,20},{8,24},{12,28},{16,0},{20,4},{24,8},{28,12},{1,17},{... | collective-permute-start | bytes 466952 | tf_op jit(solution)/shard_map/ppermute | solution.py:253
  80.4 8.7 %collective-permute-start.20 = (s16[2,304,128]{2,1,0:T(8,128)(2,1)S(1)}, s16[2,304,128]{2,1,0:T(8,128)(2,1)S(1)}, u32[]{:S(2)}, u32[]{:S(2)}) collective-permute-start(s16[2,304,128]{2,1,0:T(8,128)(2,1)S(1)} %get-tuple-element.108), channel_id=1, source_target_pairs={{0,1},{1,0},{2,3},{3,2},{4,5},{5,4},{6,7},{7,6},{8,9},{9,8},{10,11... | collective-permute-start | bytes 466952 | tf_op jit(solution)/shard_map/ppermute | solution.py:486
  89.1 17.7 %collective-permute-start.21 = (s16[2,3,400,128]{3,2,1,0:T(8,128)(2,1)S(1)}, s16[2,3,400,128]{3,2,1,0:T(8,128)(2,1)S(1)}, u32[]{:S(2)}, u32[]{:S(2)}) collective-permute-start(s16[2,3,400,128]{3,2,1,0:T(8,128)(2,1)S(1)} %get-tuple-element.109), channel_id=1, source_target_pairs={{0,1},{1,0},{2,3},{3,2},{4,5},{5,4},{6,7},{7,6},{8,9},{9,8},{10,11... | collective-permute-start | bytes 1843208 | tf_op jit(solution)/shard_map/ppermute | solution.py:486
  89.1 6.9 %collective-permute-start.17 = (s16[3,400,128]{2,1,0:T(8,128)(2,1)S(1)}, s16[3,400,128]{2,1,0:T(8,128)(2,1)S(1)}, u32[]{:S(2)}, u32[]{:S(2)}) collective-permute-start(s16[3,400,128]{2,1,0:T(8,128)(2,1)S(1)} %get-tuple-element.96), channel_id=1, source_target_pairs={{0,8},{4,12},{8,0},{12,4},{16,24},{20,28},{24,16},{28,20},{1,9},{5... | collective-permute-start | bytes 921608 | tf_op jit(solution)/shard_map/ppermute | solution.py:253
  89.7 9.2 %collective-permute-start.18 = (s16[3,400,128]{2,1,0:T(8,128)(2,1)S(1)}, s16[3,400,128]{2,1,0:T(8,128)(2,1)S(1)}, u32[]{:S(2)}, u32[]{:S(2)}) collective-permute-start(s16[3,400,128]{2,1,0:T(8,128)(2,1)S(1)} %get-tuple-element.97), channel_id=1, source_target_pairs={{0,16},{4,20},{8,24},{12,28},{16,0},{20,4},{24,8},{28,12},{1,17},{... | collective-permute-start | bytes 921608 | tf_op jit(solution)/shard_map/ppermute | solution.py:253
  91.1 9.0 %collective-permute-start.19 = (s16[3,400,128]{2,1,0:T(8,128)(2,1)S(1)}, s16[3,400,128]{2,1,0:T(8,128)(2,1)S(1)}, u32[]{:S(2)}, u32[]{:S(2)}) collective-permute-start(s16[3,400,128]{2,1,0:T(8,128)(2,1)S(1)} %get-tuple-element.98), channel_id=1, source_target_pairs={{0,24},{4,28},{8,16},{12,20},{16,8},{20,12},{24,0},{28,4},{1,25},{... | collective-permute-start | bytes 921608 | tf_op jit(solution)/shard_map/ppermute | solution.py:253
  92.6 12.2 %collective-permute-start.22 = (s16[2,304,128]{2,1,0:T(8,128)(2,1)S(1)}, s16[2,304,128]{2,1,0:T(8,128)(2,1)S(1)}, u32[]{:S(2)}, u32[]{:S(2)}) collective-permute-start(s16[2,304,128]{2,1,0:T(8,128)(2,1)S(1)} %pad_add_fusion.1), channel_id=1, source_target_pairs={{0,2},{1,3},{2,0},{3,1},{4,6},{5,7},{6,4},{7,5},{8,10},{9,11},{10,... | collective-permute-start | bytes 466952 | tf_op jit(solution)/shard_map/ppermute | solution.py:486
  106.8 13.9 %collective-permute-start.24 = (s16[1,3,400,128]{3,2,1,0:T(8,128)(2,1)S(1)}, s16[1,3,400,128]{3,2,1,0:T(8,128)(2,1)S(1)}, u32[]{:S(2)}, u32[]{:S(2)}) collective-permute-start(s16[1,3,400,128]{3,2,1,0:T(8,128)(2,1)S(1)} %get-tuple-element.112), channel_id=1, source_target_pairs={{0,1},{1,0},{2,3},{3,2},{4,5},{5,4},{6,7},{7,6},{8,9},{9,8},{10,11... | collective-permute-start | bytes 921608 | tf_op jit(solution)/shard_map/ppermute | solution.py:486
  106.9 17.0 %collective-permute-start.23 = (s16[1,3,400,128]{3,2,1,0:T(8,128)(2,1)S(1)}, s16[1,3,400,128]{3,2,1,0:T(8,128)(2,1)S(1)}, u32[]{:S(2)}, u32[]{:S(2)}) collective-permute-start(s16[1,3,400,128]{3,2,1,0:T(8,128)(2,1)S(1)} %get-tuple-element.111), channel_id=1, source_target_pairs={{0,1},{1,0},{2,3},{3,2},{4,5},{5,4},{6,7},{7,6},{8,9},{9,8},{10,11... | collective-permute-start | bytes 921608 | tf_op jit(solution)/shard_map/ppermute | solution.py:486
  109.0 12.5 %collective-permute-start.26 = (s16[1,3,400,128]{3,2,1,0:T(8,128)(2,1)S(1)}, s16[1,3,400,128]{3,2,1,0:T(8,128)(2,1)S(1)}, u32[]{:S(2)}, u32[]{:S(2)}) collective-permute-start(s16[1,3,400,128]{3,2,1,0:T(8,128)(2,1)S(1)} %get-tuple-element.119), channel_id=1, source_target_pairs={{0,2},{1,3},{2,0},{3,1},{4,6},{5,7},{6,4},{7,5},{8,10},{9,11},{10,... | collective-permute-start | bytes 921608 | tf_op jit(solution)/shard_map/ppermute | solution.py:486
  120.8 10.4 %collective-permute-start.25 = (s16[1,3,400,128]{3,2,1,0:T(8,128)(2,1)S(1)}, s16[1,3,400,128]{3,2,1,0:T(8,128)(2,1)S(1)}, u32[]{:S(2)}, u32[]{:S(2)}) collective-permute-start(s16[1,3,400,128]{3,2,1,0:T(8,128)(2,1)S(1)} %get-tuple-element.118), channel_id=1, source_target_pairs={{0,2},{1,3},{2,0},{3,1},{4,6},{5,7},{6,4},{7,5},{8,10},{9,11},{10,... | collective-permute-start | bytes 921608 | tf_op jit(solution)/shard_map/ppermute | solution.py:486

commit v15 on v13

--- a/solution.py
+++ b/solution.py
@@ -424,7 +424,6 @@
         )
 
     in_hbm = functools.partial(pltpu.with_memory_space_constraint, memory_space=pltpu.HBM)
-    own_t = transpose(in_hbm(integrals))
     swapped = lax.ppermute(integrals, "pair", [(i, i ^ 1) for i in range(devices)])
     sib_t = transpose(swapped)
 
@@ -439,6 +438,13 @@
     eps_virt = (eps_mine[:, :, None] + eps_vir[None, None, :]).reshape(2, part_rows).T
 
     place = jnp.stack([chip, core, z]).astype(jnp.int32)
+    token = jnp.zeros((8, LANES), jnp.float32)
+    rest = amplitudes[WIDTH:]
+
+    ready, eps_pair, eps_virt, place, token, rest = lax.optimization_barrier(
+        (integrals, eps_pair, eps_virt, place, token, rest)
+    )
+    own_t = transpose(in_hbm(ready))
 
     def gather(mine, beside):
         count = mine.shape[0]
@@ -451,12 +457,8 @@
         return [[mine], [one], [two], [low, high]], beside
 
     if early:
-        head, (own_t, eps_pair, eps_virt) = gather(
-            amplitudes[:WIDTH], (own_t, eps_pair, eps_virt)
-        )
-        head, own_t, sib_t, rest = lax.optimization_barrier(
-            (head, own_t, sib_t, amplitudes[WIDTH:])
-        )
+        head, (own_t,) = gather(amplitudes[:WIDTH], (own_t,))
+        head, own_t, sib_t, rest = lax.optimization_barrier((head, own_t, sib_t, rest))
         tail, _ = gather(rest, ())
         gathered = [(0, head), (WIDTH, tail)]
     else:
@@ -554,7 +556,7 @@
     turns, firsts, seconds, steps = [], [], [], []
     running = [early_stages(r) if early and r == 0 else stages(r) for r in range(chunks)]
     results = [None] * chunks
-    update, token = None, jnp.zeros((8, LANES), jnp.float32)
+    update = None
     for r, k in order:
         step = running[r].send(results[r])
         if step is None:

time: 133 us -> 119 us (0.89)
  local copies, waits for them, and re-layouts: 16.4 us -> 2.52 us
  waiting for transfers between devices: 46.7 us -> 36.7 us
  starting transfers between devices: 32 us -> 41.7 us
    ppermute x10, waiting for transfers between devices: 36.9 us -> 20.7 us  [across(): return lax.ppermute(x, 'slab', [(i, i ^ level) for i in range(slabs)])]
    unnamed x32 -> x6, local copies, waits for them, and re-layouts: 13.9 us -> 0.01 us
    ppermute x10, starting transfers between devices: 12.1 us -> 20.6 us  [across(): return lax.ppermute(x, 'slab', [(i, i ^ level) for i in range(slabs)])]
    ppermute x16, waiting for transfers between devices: 9.82 us -> 16 us  [to_chip(): return lax.ppermute(x, 'pair', [(i, i ^ d * CORES) for i in range(devices)])]
  transfers between devices with their start and end apart: 27 -> 27, of which waited for: 14 -> 14; matrix products, arithmetic and copies ran while one was open for 2% -> 3% of each run, Pallas kernels for 27% -> 30%
where the time goes in v15:
time: 119 us; the launch traced here: 118 us
  starting transfers between devices  41.7 us (35%)
  Pallas kernels  36.7 us (31%)
  waiting for transfers between devices  36.7 us (31%)
  local copies, waits for them, and re-layouts  2.52 us (2%)
    pallas_call x13, Pallas kernels, call(): pl.pallas_call(kernel, in_specs=[*in_specs, vmem], out_specs=[*out_specs,...  28.7 us
    ppermute x10, waiting for transfers between devices, across(): return lax.ppermute(x, 'slab', [(i, i ^ level) for i in range(slabs)])  20.7 us
    ppermute x10, starting transfers between devices, across(): return lax.ppermute(x, 'slab', [(i, i ^ level) for i in range(slabs)])  20.6 us
    ppermute x16, starting transfers between devices, to_chip(): return lax.ppermute(x, 'pair', [(i, i ^ d * CORES) for i in range(devices)])  20.6 us
    ppermute x16, waiting for transfers between devices, to_chip(): return lax.ppermute(x, 'pair', [(i, i ^ d * CORES) for i in range(devices)])  16 us
    pallas_call x1, Pallas kernels, on_device(): own_t = transpose(in_hbm(ready))  4 us
    pallas_call x1, Pallas kernels, on_device(): sib_t = transpose(swapped)  4 us
  transfers between devices with their start and end apart: 27, of which 14 were waited for; matrix products, arithmetic and copies ran while one was open for 3% of the time, Pallas kernels for 30%

profile of v15, /device:TPU:0, one launch (start us, length us, event | category | flops | bytes accessed | tf_op | source)
XLA Modules:
  0.0 118.4 jit_solution(11308675830636958302)
XLA Ops:
  0.5 1.0 slice.33.refs_3_
  1.5 2.6 %collective-permute-start.1 = (bf16[64,2304]{1,0:T(8,128)(2,1)S(1)}, bf16[64,2304]{1,0:T(8,128)(2,1)S(1)}, u32[]{:S(2)}, u32[]{:S(2)}) collective-permute-start(bf16[64,2304]{1,0:T(8,128)(2,1)S(1)} %slice.33.refs_3_), channel_id=1, source_target_pairs={{0,16},{4,20},{8,24},{12,28},{16,0},{20,4},{24,8},{28,12},{1,17},{... | collective-permute-start | bytes 884744 | tf_op jit(solution)/shard_map/ppermute | solution.py:253
  4.1 1.5 %collective-permute-start = (bf16[64,2304]{1,0:T(8,128)(2,1)S(1)}, bf16[64,2304]{1,0:T(8,128)(2,1)S(1)}, u32[]{:S(2)}, u32[]{:S(2)}) collective-permute-start(bf16[64,2304]{1,0:T(8,128)(2,1)S(1)} %slice.33.refs_3_), channel_id=1, source_target_pairs={{0,8},{4,12},{8,0},{12,4},{16,24},{20,28},{24,16},{28,20},{1,9},{5... | collective-permute-start | bytes 884744 | tf_op jit(solution)/shard_map/ppermute | solution.py:253
  5.6 1.1 slice.32.refs_2_
  7.6 4.0 %transpose.14.refs_1_.refs_0_ = bf16[1152,2304]{1,0:T(8,128)(2,1)S(1)} custom-call(bf16[2304,1152]{1,0:T(8,128)(2,1)} %in_ref), custom_call_target="tpu_custom_call" | custom-call | bytes 10616832 | tf_op jit(solution)/shard_map/transpose/pallas_call | solution.py:447
  11.8 1.5 %collective-permute-done.refs_4_ = bf16[64,2304]{1,0:T(8,128)(2,1)S(1)} collective-permute-done((bf16[64,2304]{1,0:T(8,128)(2,1)S(1)}, bf16[64,2304]{1,0:T(8,128)(2,1)S(1)}, u32[]{:S(2)}, u32[]{:S(2)}) %collective-permute-start) | collective-permute-done | bytes 294944 | tf_op jit(solution)/shard_map/ppermute | solution.py:253
  13.3 1.6 %collective-permute-start.2 = (bf16[32,2304]{1,0:T(8,128)(2,1)S(1)}, bf16[32,2304]{1,0:T(8,128)(2,1)S(1)}, u32[]{:S(2)}, u32[]{:S(2)}) collective-permute-start(bf16[32,2304]{1,0:T(8,128)(2,1)S(1)} %slice.34), channel_id=1, source_target_pairs={{0,8},{4,12},{8,0},{12,4},{16,24},{20,28},{24,16},{28,20},{1,9},{5... | collective-permute-start | bytes 442376 | tf_op jit(solution)/shard_map/ppermute | solution.py:253
  15.3 4.0 %transpose.15.refs_2_.refs_1_ = bf16[1152,2304]{1,0:T(8,128)(2,1)S(1)} custom-call(bf16[2304,1152]{1,0:T(8,128)(2,1)} %collective-permute-done.4.in_ref), custom_call_target="tpu_custom_call" | custom-call | bytes 10616832 | tf_op jit(solution)/shard_map/transpose/pallas_call | solution.py:428
  19.4 0.6 collective-permute-done.3.refs_7_
  20.0 1.0 collective-permute-start.6
  21.5 4.8 %early_ladder.1 = (f32[2,1152,128]{2,1,0:T(8,128)S(1)}, s16[1,4,304,128]{3,2,1,0:T(8,128)(2,1)S(1)}, s16[1,4,304,128]{3,2,1,0:T(8,128)(2,1)S(1)}, f32[8,128]{1,0:T(8,128)S(1)}) custom-call(s32[3]{0:T(128)S(1)} %pad_add_fusion.2.refs_0_, bf16[1152,2304]{1,0:T(8,128)(2,1)S(1)} %transpose.14.refs_1_.refs_0_, bf16[1152,2304]{1,0:T(8,128)(2,1)S(1)} %transpose.15.refs_2_.refs_1_, ...), custom_call_target="tpu_custom_call" | custom-call | flops 2717908992 | bytes 13598732 | tf_op jit(solution)/shard_map/early_ladder/pallas_call | solution.py:293
  26.3 1.7 %collective-permute-start.9 = (s16[1,4,304,128]{3,2,1,0:T(8,128)(2,1)S(1)}, s16[1,4,304,128]{3,2,1,0:T(8,128)(2,1)S(1)}, u32[]{:S(2)}, u32[]{:S(2)}) collective-permute-start(s16[1,4,304,128]{3,2,1,0:T(8,128)(2,1)S(1)} %get-tuple-element.88), channel_id=1, source_target_pairs={{0,1},{1,0},{2,3},{3,2},{4,5},{5,4},{6,7},{7,6},{8,9},{9,8},{10,11... | collective-permute-start | bytes 933896 | tf_op jit(solution)/shard_map/ppermute | solution.py:484
  28.0 5.6 %collective-permute-done.6.refs_4_ = bf16[128,2304]{1,0:T(8,128)(2,1)S(1)} collective-permute-done((bf16[128,2304]{1,0:T(8,128)(2,1)S(1)}, bf16[128,2304]{1,0:T(8,128)(2,1)S(1)}, u32[]{:S(2)}, u32[]{:S(2)}) %collective-permute-start.6) | collective-permute-done | bytes 589856 | tf_op jit(solution)/shard_map/ppermute | solution.py:253
  33.6 0.7 collective-permute-start.11
  34.3 1.5 %collective-permute-start.8 = (s16[1,4,304,128]{3,2,1,0:T(8,128)(2,1)S(1)}, s16[1,4,304,128]{3,2,1,0:T(8,128)(2,1)S(1)}, u32[]{:S(2)}, u32[]{:S(2)}) collective-permute-start(s16[1,4,304,128]{3,2,1,0:T(8,128)(2,1)S(1)} %get-tuple-element.87), channel_id=1, source_target_pairs={{0,1},{1,0},{2,3},{3,2},{4,5},{5,4},{6,7},{7,6},{8,9},{9,8},{10,11... | collective-permute-start | bytes 933896 | tf_op jit(solution)/shard_map/ppermute | solution.py:484
  36.0 2.7 %collective-permute-start.10 = (s16[1,4,304,128]{3,2,1,0:T(8,128)(2,1)S(1)}, s16[1,4,304,128]{3,2,1,0:T(8,128)(2,1)S(1)}, u32[]{:S(2)}, u32[]{:S(2)}) collective-permute-start(s16[1,4,304,128]{3,2,1,0:T(8,128)(2,1)S(1)} %get-tuple-element.90), channel_id=1, source_target_pairs={{0,2},{1,3},{2,0},{3,1},{4,6},{5,7},{6,4},{7,5},{8,10},{9,11},{10,... | collective-permute-start | bytes 933896 | tf_op jit(solution)/shard_map/ppermute | solution.py:484
  38.7 1.5 %collective-permute-start.7 = (bf16[64,2304]{1,0:T(8,128)(2,1)S(1)}, bf16[64,2304]{1,0:T(8,128)(2,1)S(1)}, u32[]{:S(2)}, u32[]{:S(2)}) collective-permute-start(bf16[64,2304]{1,0:T(8,128)(2,1)S(1)} %slice.40), channel_id=1, source_target_pairs={{0,16},{4,20},{8,24},{12,28},{16,0},{20,4},{24,8},{28,12},{1,17},{... | collective-permute-start | bytes 884744 | tf_op jit(solution)/shard_map/ppermute | solution.py:253
  40.1 0.9 collective-permute-done.11.refs_5_
  41.1 4.2 %ladder.2 = (s16[3,400,128]{2,1,0:T(8,128)(2,1)S(1)}, s16[3,400,128]{2,1,0:T(8,128)(2,1)S(1)}, s16[3,400,128]{2,1,0:T(8,128)(2,1)S(1)}, s16[3,400,128]{2,1,0:T(8,128)(2,1)S(1)}, f32[8,128]{1,0:T(8,128)S(1)}) custom-call(bf16[1152,2304]{1,0:T(8,128)(2,1)S(1)} %transpose.14.refs_1_.refs_0_, bf16[1152,2304]{1,0:T(8,128)(2,1)S(1)} %transpose.15.refs_2_.refs_1_, ...), custom_call_target="tpu_custom_call" | custom-call | flops 2717908992 | bytes 13910016 | tf_op jit(solution)/shard_map/ladder/pallas_call | solution.py:293
  45.3 1.8 %collective-permute-done.8.refs_1_ = s16[1,4,304,128]{3,2,1,0:T(8,128)(2,1)S(1)} collective-permute-done((s16[1,4,304,128]{3,2,1,0:T(8,128)(2,1)S(1)}, s16[1,4,304,128]{3,2,1,0:T(8,128)(2,1)S(1)}, u32[]{:S(2)}, u32[]{:S(2)}) %collective-permute-start.8) | collective-permute-done | bytes 311328 | tf_op jit(solution)/shard_map/ppermute | solution.py:484
  47.1 2.7 %collective-permute-done.10.refs_2_ = s16[1,4,304,128]{3,2,1,0:T(8,128)(2,1)S(1)} collective-permute-done((s16[1,4,304,128]{3,2,1,0:T(8,128)(2,1)S(1)}, s16[1,4,304,128]{3,2,1,0:T(8,128)(2,1)S(1)}, u32[]{:S(2)}, u32[]{:S(2)}) %collective-permute-start.10) | collective-permute-done | bytes 311328 | tf_op jit(solution)/shard_map/ppermute | solution.py:484
  50.1 1.6 %collective-permute-start.15 = (s16[2,304,128]{2,1,0:T(8,128)(2,1)S(1)}, s16[2,304,128]{2,1,0:T(8,128)(2,1)S(1)}, u32[]{:S(2)}, u32[]{:S(2)}) collective-permute-start(s16[2,304,128]{2,1,0:T(8,128)(2,1)S(1)} %get-tuple-element.101), channel_id=1, source_target_pairs={{0,8},{4,12},{8,0},{12,4},{16,24},{20,28},{24,16},{28,20},{1,9},{5... | collective-permute-start | bytes 466952 | tf_op jit(solution)/shard_map/ppermute | solution.py:253
  51.6 0.5 collective-permute-start.12
  52.2 1.9 %collective-permute-start.13 = (s16[3,400,128]{2,1,0:T(8,128)(2,1)S(1)}, s16[3,400,128]{2,1,0:T(8,128)(2,1)S(1)}, u32[]{:S(2)}, u32[]{:S(2)}) collective-permute-start(s16[3,400,128]{2,1,0:T(8,128)(2,1)S(1)} %get-tuple-element.99), channel_id=1, source_target_pairs={{0,16},{4,20},{8,24},{12,28},{16,0},{20,4},{24,8},{28,12},{1,17},{... | collective-permute-start | bytes 921608 | tf_op jit(solution)/shard_map/ppermute | solution.py:253
  54.0 1.1 collective-permute-start.14
  55.1 0.6 collective-permute-done.15.refs_2_
  55.8 2.2 %collective-permute-start.16 = (s16[2,304,128]{2,1,0:T(8,128)(2,1)S(1)}, s16[2,304,128]{2,1,0:T(8,128)(2,1)S(1)}, u32[]{:S(2)}, u32[]{:S(2)}) collective-permute-start(s16[2,304,128]{2,1,0:T(8,128)(2,1)S(1)} %pad_add_fusion), channel_id=1, source_target_pairs={{0,16},{4,20},{8,24},{12,28},{16,0},{20,4},{24,8},{28,12},{1,17},{... | collective-permute-start | bytes 466952 | tf_op jit(solution)/shard_map/ppermute | solution.py:253
  58.0 4.2 %ladder.3 = (s16[3,400,128]{2,1,0:T(8,128)(2,1)S(1)}, s16[3,400,128]{2,1,0:T(8,128)(2,1)S(1)}, s16[3,400,128]{2,1,0:T(8,128)(2,1)S(1)}, s16[3,400,128]{2,1,0:T(8,128)(2,1)S(1)}, f32[8,128]{1,0:T(8,128)S(1)}) custom-call(bf16[1152,2304]{1,0:T(8,128)(2,1)S(1)} %transpose.14.refs_1_.refs_0_, bf16[1152,2304]{1,0:T(8,128)(2,1)S(1)} %transpose.15.refs_2_.refs_1_, ...), custom_call_target="tpu_custom_call" | custom-call | flops 2717908992 | bytes 13910016 | tf_op jit(solution)/shard_map/ladder/pallas_call | solution.py:293
  62.2 2.3 %collective-permute-done.16.refs_3_ = s16[2,304,128]{2,1,0:T(8,128)(2,1)S(1)} collective-permute-done((s16[2,304,128]{2,1,0:T(8,128)(2,1)S(1)}, s16[2,304,128]{2,1,0:T(8,128)(2,1)S(1)}, u32[]{:S(2)}, u32[]{:S(2)}) %collective-permute-start.16) | collective-permute-done | bytes 155680 | tf_op jit(solution)/shard_map/ppermute | solution.py:253
  64.5 1.1 early_antisym.1
  65.6 3.0 %collective-permute-start.20 = (s16[2,304,128]{2,1,0:T(8,128)(2,1)S(1)}, s16[2,304,128]{2,1,0:T(8,128)(2,1)S(1)}, u32[]{:S(2)}, u32[]{:S(2)}) collective-permute-start(s16[2,304,128]{2,1,0:T(8,128)(2,1)S(1)} %get-tuple-element.116), channel_id=1, source_target_pairs={{0,1},{1,0},{2,3},{3,2},{4,5},{5,4},{6,7},{7,6},{8,9},{9,8},{10,11... | collective-permute-start | bytes 466952 | tf_op jit(solution)/shard_map/ppermute | solution.py:484
  68.6 4.7 %antisym.2 = (f32[2,1152,128]{2,1,0:T(8,128)S(1)}, s16[2,3,400,128]{3,2,1,0:T(8,128)(2,1)S(1)}, f32[8,128]{1,0:T(8,128)S(1)}) custom-call(s32[3]{0:T(128)S(1)} %pad_add_fusion.2.refs_0_, s16[3,400,128]{2,1,0:T(8,128)(2,1)S(1)} %get-tuple-element.107.refs_1_, s16[3,400,128]{2,1,0:T(8,128)(2,1)S(1)} %collective-permute-done.12.refs_2_, ...), custom_call_target="tpu_custom_call" | custom-call | flops 9437184 | bytes 3022860 | tf_op jit(solution)/shard_map/antisym/pallas_call | solution.py:293
  73.3 1.9 %collective-permute-done.20.refs_3_ = s16[2,304,128]{2,1,0:T(8,128)(2,1)S(1)} collective-permute-done((s16[2,304,128]{2,1,0:T(8,128)(2,1)S(1)}, s16[2,304,128]{2,1,0:T(8,128)(2,1)S(1)}, u32[]{:S(2)}, u32[]{:S(2)}) %collective-permute-start.20) | collective-permute-done | bytes 155680 | tf_op jit(solution)/shard_map/ppermute | solution.py:484
  75.6 1.5 %collective-permute-start.17 = (s16[3,400,128]{2,1,0:T(8,128)(2,1)S(1)}, s16[3,400,128]{2,1,0:T(8,128)(2,1)S(1)}, u32[]{:S(2)}, u32[]{:S(2)}) collective-permute-start(s16[3,400,128]{2,1,0:T(8,128)(2,1)S(1)} %get-tuple-element.104), channel_id=1, source_target_pairs={{0,8},{4,12},{8,0},{12,4},{16,24},{20,28},{24,16},{28,20},{1,9},{5... | collective-permute-start | bytes 921608 | tf_op jit(solution)/shard_map/ppermute | solution.py:253
  77.1 1.7 %collective-permute-start.18 = (s16[3,400,128]{2,1,0:T(8,128)(2,1)S(1)}, s16[3,400,128]{2,1,0:T(8,128)(2,1)S(1)}, u32[]{:S(2)}, u32[]{:S(2)}) collective-permute-start(s16[3,400,128]{2,1,0:T(8,128)(2,1)S(1)} %get-tuple-element.105), channel_id=1, source_target_pairs={{0,16},{4,20},{8,24},{12,28},{16,0},{20,4},{24,8},{28,12},{1,17},{... | collective-permute-start | bytes 921608 | tf_op jit(solution)/shard_map/ppermute | solution.py:253
  79.1 3.8 %collective-permute-start.22 = (s16[2,304,128]{2,1,0:T(8,128)(2,1)S(1)}, s16[2,304,128]{2,1,0:T(8,128)(2,1)S(1)}, u32[]{:S(2)}, u32[]{:S(2)}) collective-permute-start(s16[2,304,128]{2,1,0:T(8,128)(2,1)S(1)} %pad_add_fusion.1), channel_id=1, source_target_pairs={{0,2},{1,3},{2,0},{3,1},{4,6},{5,7},{6,4},{7,5},{8,10},{9,11},{10,... | collective-permute-start | bytes 466952 | tf_op jit(solution)/shard_map/ppermute | solution.py:484
  82.9 4.3 %collective-permute-done.18.refs_3_ = s16[3,400,128]{2,1,0:T(8,128)(2,1)S(1)} collective-permute-done((s16[3,400,128]{2,1,0:T(8,128)(2,1)S(1)}, s16[3,400,128]{2,1,0:T(8,128)(2,1)S(1)}, u32[]{:S(2)}, u32[]{:S(2)}) %collective-permute-start.18) | collective-permute-done | bytes 307232 | tf_op jit(solution)/shard_map/ppermute | solution.py:253
  87.2 4.7 %antisym.3 = (f32[2,1152,128]{2,1,0:T(8,128)S(1)}, s16[1,3,400,128]{3,2,1,0:T(8,128)(2,1)S(1)}, s16[1,3,400,128]{3,2,1,0:T(8,128)(2,1)S(1)}, f32[8,128]{1,0:T(8,128)S(1)}) custom-call(s32[3]{0:T(128)S(1)} %pad_add_fusion.2.refs_0_, s16[3,400,128]{2,1,0:T(8,128)(2,1)S(1)} %get-tuple-element.103.refs_1_, ...), custom_call_target="tpu_custom_call" | custom-call | flops 9437184 | bytes 3022860 | tf_op jit(solution)/shard_map/antisym/pallas_call | solution.py:293
  91.9 1.7 %collective-permute-start.24 = (s16[1,3,400,128]{3,2,1,0:T(8,128)(2,1)S(1)}, s16[1,3,400,128]{3,2,1,0:T(8,128)(2,1)S(1)}, u32[]{:S(2)}, u32[]{:S(2)}) collective-permute-start(s16[1,3,400,128]{3,2,1,0:T(8,128)(2,1)S(1)} %get-tuple-element.120), channel_id=1, source_target_pairs={{0,1},{1,0},{2,3},{3,2},{4,5},{5,4},{6,7},{7,6},{8,9},{9,8},{10,11... | collective-permute-start | bytes 921608 | tf_op jit(solution)/shard_map/ppermute | solution.py:484
  93.9 2.2 %collective-permute-start.26 = (s16[1,3,400,128]{3,2,1,0:T(8,128)(2,1)S(1)}, s16[1,3,400,128]{3,2,1,0:T(8,128)(2,1)S(1)}, u32[]{:S(2)}, u32[]{:S(2)}) collective-permute-start(s16[1,3,400,128]{3,2,1,0:T(8,128)(2,1)S(1)} %get-tuple-element.127), channel_id=1, source_target_pairs={{0,2},{1,3},{2,0},{3,1},{4,6},{5,7},{6,4},{7,5},{8,10},{9,11},{10,... | collective-permute-start | bytes 921608 | tf_op jit(solution)/shard_map/ppermute | solution.py:484
  96.0 2.0 %collective-permute-start.23 = (s16[1,3,400,128]{3,2,1,0:T(8,128)(2,1)S(1)}, s16[1,3,400,128]{3,2,1,0:T(8,128)(2,1)S(1)}, u32[]{:S(2)}, u32[]{:S(2)}) collective-permute-start(s16[1,3,400,128]{3,2,1,0:T(8,128)(2,1)S(1)} %get-tuple-element.119), channel_id=1, source_target_pairs={{0,1},{1,0},{2,3},{3,2},{4,5},{5,4},{6,7},{7,6},{8,9},{9,8},{10,11... | collective-permute-start | bytes 921608 | tf_op jit(solution)/shard_map/ppermute | solution.py:484
  98.0 1.4 %finish.3 = (f32[192,2304]{1,0:T(8,128)}, f32[8,128]{1,0:T(8,128)S(1)}) custom-call(f32[3,1,128]{2,1,0:T(1,128)S(1)} %pad_maximum_fusion.refs_0_, f32[1152,2]{1,0:T(8,128)S(1)} %bitcast.10, f32[288,128]{1,0:T(8,128)S(1)} %get-tuple-element.121.refs_2_, s16[2,304,128]{2,1,0:T(8,128)(2,1)S(1)} %collective-permute-done.20.refs_3_, ...), custom_call_target="tpu_custom_call" | custom-call | flops 2359296 | bytes 2238976 | tf_op jit(solution)/shard_map/finish/pallas_call | solution.py:293
  99.4 4.5 %collective-permute-done.24.refs_1_ = s16[1,3,400,128]{3,2,1,0:T(8,128)(2,1)S(1)} collective-permute-done((s16[1,3,400,128]{3,2,1,0:T(8,128)(2,1)S(1)}, s16[1,3,400,128]{3,2,1,0:T(8,128)(2,1)S(1)}, u32[]{:S(2)}, u32[]{:S(2)}) %collective-permute-start.24) | collective-permute-done | bytes 307232 | tf_op jit(solution)/shard_map/ppermute | solution.py:484
  104.1 1.7 %collective-permute-start.25 = (s16[1,3,400,128]{3,2,1,0:T(8,128)(2,1)S(1)}, s16[1,3,400,128]{3,2,1,0:T(8,128)(2,1)S(1)}, u32[]{:S(2)}, u32[]{:S(2)}) collective-permute-start(s16[1,3,400,128]{3,2,1,0:T(8,128)(2,1)S(1)} %get-tuple-element.126), channel_id=1, source_target_pairs={{0,2},{1,3},{2,0},{3,1},{4,6},{5,7},{6,4},{7,5},{8,10},{9,11},{10,... | collective-permute-start | bytes 921608 | tf_op jit(solution)/shard_map/ppermute | solution.py:484
  105.8 4.6 %collective-permute-done.26.refs_4_ = s16[1,3,400,128]{3,2,1,0:T(8,128)(2,1)S(1)} collective-permute-done((s16[1,3,400,128]{3,2,1,0:T(8,128)(2,1)S(1)}, s16[1,3,400,128]{3,2,1,0:T(8,128)(2,1)S(1)}, u32[]{:S(2)}, u32[]{:S(2)}) %collective-permute-start.26) | collective-permute-done | bytes 307232 | tf_op jit(solution)/shard_map/ppermute | solution.py:484
  110.4 1.4 %finish.4 = (f32[192,2304]{1,0:T(8,128)}, f32[8,128]{1,0:T(8,128)S(1)}) custom-call(f32[3,1,128]{2,1,0:T(1,128)S(1)} %pad_maximum_fusion.refs_0_, f32[1152,2]{1,0:T(8,128)S(1)} %bitcast.11, f32[2,1152,128]{2,1,0:T(8,128)S(1)} %get-tuple-element.122.refs_0_.refs_2_, ...), custom_call_target="tpu_custom_call", output_to_operand_aliasing={{0}: (5, {})} | custom-call | flops 2359296 | bytes 5650944 | tf_op jit(solution)/shard_map/finish/pallas_call | solution.py:293
  111.8 5.2 %collective-permute-done.25.refs_4_ = s16[1,3,400,128]{3,2,1,0:T(8,128)(2,1)S(1)} collective-permute-done((s16[1,3,400,128]{3,2,1,0:T(8,128)(2,1)S(1)}, s16[1,3,400,128]{3,2,1,0:T(8,128)(2,1)S(1)}, u32[]{:S(2)}, u32[]{:S(2)}) %collective-permute-start.25) | collective-permute-done | bytes 307232 | tf_op jit(solution)/shard_map/ppermute | solution.py:484
  117.0 1.4 %finish.5 = (f32[192,2304]{1,0:T(8,128)}, f32[8,128]{1,0:T(8,128)}) custom-call(f32[3,1,128]{2,1,0:T(1,128)S(1)} %pad_maximum_fusion.refs_0_, f32[1152,2]{1,0:T(8,128)S(1)} %bitcast.12, f32[2,1152,128]{2,1,0:T(8,128)S(1)} %get-tuple-element.112.refs_0_.refs_2_, ...), custom_call_target="tpu_custom_call", output_to_operand_aliasing={{0}: (5, {})} | custom-call | flops 2359296 | bytes 5343744 | tf_op jit(solution)/shard_map/finish/pallas_call | solution.py:293
  (50 shorter events, 4.2 us)
Async XLA Ops:
  0.0 6.7 %copy-start.1 = (s32[192,2]{0,1:T(2,128)S(1)}, s32[192,2]{0,1:T(2,128)}, u32[]{:S(2)}) copy-start(s32[192,2]{0,1:T(2,128)} %param.7) | copy-start | bytes 4612
  0.0 6.7 %copy-start.2 = (f32[160]{0:T(256)S(1)}, f32[160]{0:T(256)}, u32[]{:S(2)}) copy-start(f32[160]{0:T(256)} %param.8) | copy-start | bytes 1924
  0.0 7.0 %copy-start = (f32[96]{0:T(128)S(1)}, f32[96]{0:T(128)}, u32[]{:S(2)}) copy-start(f32[96]{0:T(128)} %param.9) | copy-start | bytes 1156
  0.0 15.3 %collective-permute-start.4 = (bf16[2304,1152]{1,0:T(8,128)(2,1)}, bf16[2304,1152]{1,0:T(8,128)(2,1)}, u32[]{:S(2)}, u32[]{:S(2)}) collective-permute-start(bf16[2304,1152]{1,0:T(8,128)(2,1)} %in_ref), channel_id=1, source_target_pairs={{0,4},{4,0},{8,12},{12,8},{16,20},{20,16},{24,28},{28,24},{1,5},{5... | collective-permute-start | bytes 15925256 | tf_op jit(solution)/shard_map/ppermute | solution.py:427
  1.5 10.3 %collective-permute-start.1 = (bf16[64,2304]{1,0:T(8,128)(2,1)S(1)}, bf16[64,2304]{1,0:T(8,128)(2,1)S(1)}, u32[]{:S(2)}, u32[]{:S(2)}) collective-permute-start(bf16[64,2304]{1,0:T(8,128)(2,1)S(1)} %slice.33.refs_3_), channel_id=1, source_target_pairs={{0,16},{4,20},{8,24},{12,28},{16,0},{20,4},{24,8},{28,12},{1,17},{... | collective-permute-start | bytes 884744 | tf_op jit(solution)/shard_map/ppermute | solution.py:253
  4.1 9.1 %collective-permute-start = (bf16[64,2304]{1,0:T(8,128)(2,1)S(1)}, bf16[64,2304]{1,0:T(8,128)(2,1)S(1)}, u32[]{:S(2)}, u32[]{:S(2)}) collective-permute-start(bf16[64,2304]{1,0:T(8,128)(2,1)S(1)} %slice.33.refs_3_), channel_id=1, source_target_pairs={{0,8},{4,12},{8,0},{12,4},{16,24},{20,28},{24,16},{28,20},{1,9},{5... | collective-permute-start | bytes 884744 | tf_op jit(solution)/shard_map/ppermute | solution.py:253
  13.3 6.1 %collective-permute-start.2 = (bf16[32,2304]{1,0:T(8,128)(2,1)S(1)}, bf16[32,2304]{1,0:T(8,128)(2,1)S(1)}, u32[]{:S(2)}, u32[]{:S(2)}) collective-permute-start(bf16[32,2304]{1,0:T(8,128)(2,1)S(1)} %slice.34), channel_id=1, source_target_pairs={{0,8},{4,12},{8,0},{12,4},{16,24},{20,28},{24,16},{28,20},{1,9},{5... | collective-permute-start | bytes 442376 | tf_op jit(solution)/shard_map/ppermute | solution.py:253
  14.8 5.1 %collective-permute-start.3 = (bf16[32,2304]{1,0:T(8,128)(2,1)S(1)}, bf16[32,2304]{1,0:T(8,128)(2,1)S(1)}, u32[]{:S(2)}, u32[]{:S(2)}) collective-permute-start(bf16[32,2304]{1,0:T(8,128)(2,1)S(1)} %slice.35), channel_id=1, source_target_pairs={{0,16},{4,20},{8,24},{12,28},{16,0},{20,4},{24,8},{28,12},{1,17},{... | collective-permute-start | bytes 442376 | tf_op jit(solution)/shard_map/ppermute | solution.py:253
  20.0 13.6 %collective-permute-start.6 = (bf16[128,2304]{1,0:T(8,128)(2,1)S(1)}, bf16[128,2304]{1,0:T(8,128)(2,1)S(1)}, u32[]{:S(2)}, u32[]{:S(2)}) collective-permute-start(bf16[128,2304]{1,0:T(8,128)(2,1)S(1)} %slice.32.refs_2_), channel_id=1, source_target_pairs={{0,16},{4,20},{8,24},{12,28},{16,0},{20,4},{24,8},{28,12},{1,17},{... | collective-permute-start | bytes 1769480 | tf_op jit(solution)/shard_map/ppermute | solution.py:253
  20.9 17.7 %collective-permute-start.5 = (bf16[128,2304]{1,0:T(8,128)(2,1)S(1)}, bf16[128,2304]{1,0:T(8,128)(2,1)S(1)}, u32[]{:S(2)}, u32[]{:S(2)}) collective-permute-start(bf16[128,2304]{1,0:T(8,128)(2,1)S(1)} %slice.32.refs_2_), channel_id=1, source_target_pairs={{0,8},{4,12},{8,0},{12,4},{16,24},{20,28},{24,16},{28,20},{1,9},{5... | collective-permute-start | bytes 1769480 | tf_op jit(solution)/shard_map/ppermute | solution.py:253
  26.3 9.5 %collective-permute-start.9 = (s16[1,4,304,128]{3,2,1,0:T(8,128)(2,1)S(1)}, s16[1,4,304,128]{3,2,1,0:T(8,128)(2,1)S(1)}, u32[]{:S(2)}, u32[]{:S(2)}) collective-permute-start(s16[1,4,304,128]{3,2,1,0:T(8,128)(2,1)S(1)} %get-tuple-element.88), channel_id=1, source_target_pairs={{0,1},{1,0},{2,3},{3,2},{4,5},{5,4},{6,7},{7,6},{8,9},{9,8},{10,11... | collective-permute-start | bytes 933896 | tf_op jit(solution)/shard_map/ppermute | solution.py:484
  33.6 7.4 %collective-permute-start.11 = (bf16[64,2304]{1,0:T(8,128)(2,1)S(1)}, bf16[64,2304]{1,0:T(8,128)(2,1)S(1)}, u32[]{:S(2)}, u32[]{:S(2)}) collective-permute-start(bf16[64,2304]{1,0:T(8,128)(2,1)S(1)} %slice.41), channel_id=1, source_target_pairs={{0,8},{4,12},{8,0},{12,4},{16,24},{20,28},{24,16},{28,20},{1,9},{5... | collective-permute-start | bytes 884744 | tf_op jit(solution)/shard_map/ppermute | solution.py:253
  34.3 12.8 %collective-permute-start.8 = (s16[1,4,304,128]{3,2,1,0:T(8,128)(2,1)S(1)}, s16[1,4,304,128]{3,2,1,0:T(8,128)(2,1)S(1)}, u32[]{:S(2)}, u32[]{:S(2)}) collective-permute-start(s16[1,4,304,128]{3,2,1,0:T(8,128)(2,1)S(1)} %get-tuple-element.87), channel_id=1, source_target_pairs={{0,1},{1,0},{2,3},{3,2},{4,5},{5,4},{6,7},{7,6},{8,9},{9,8},{10,11... | collective-permute-start | bytes 933896 | tf_op jit(solution)/shard_map/ppermute | solution.py:484
  36.0 13.9 %collective-permute-start.10 = (s16[1,4,304,128]{3,2,1,0:T(8,128)(2,1)S(1)}, s16[1,4,304,128]{3,2,1,0:T(8,128)(2,1)S(1)}, u32[]{:S(2)}, u32[]{:S(2)}) collective-permute-start(s16[1,4,304,128]{3,2,1,0:T(8,128)(2,1)S(1)} %get-tuple-element.90), channel_id=1, source_target_pairs={{0,2},{1,3},{2,0},{3,1},{4,6},{5,7},{6,4},{7,5},{8,10},{9,11},{10,... | collective-permute-start | bytes 933896 | tf_op jit(solution)/shard_map/ppermute | solution.py:484
  38.7 19.3 %collective-permute-start.7 = (bf16[64,2304]{1,0:T(8,128)(2,1)S(1)}, bf16[64,2304]{1,0:T(8,128)(2,1)S(1)}, u32[]{:S(2)}, u32[]{:S(2)}) collective-permute-start(bf16[64,2304]{1,0:T(8,128)(2,1)S(1)} %slice.40), channel_id=1, source_target_pairs={{0,16},{4,20},{8,24},{12,28},{16,0},{20,4},{24,8},{28,12},{1,17},{... | collective-permute-start | bytes 884744 | tf_op jit(solution)/shard_map/ppermute | solution.py:253
  50.1 5.7 %collective-permute-start.15 = (s16[2,304,128]{2,1,0:T(8,128)(2,1)S(1)}, s16[2,304,128]{2,1,0:T(8,128)(2,1)S(1)}, u32[]{:S(2)}, u32[]{:S(2)}) collective-permute-start(s16[2,304,128]{2,1,0:T(8,128)(2,1)S(1)} %get-tuple-element.101), channel_id=1, source_target_pairs={{0,8},{4,12},{8,0},{12,4},{16,24},{20,28},{24,16},{28,20},{1,9},{5... | collective-permute-start | bytes 466952 | tf_op jit(solution)/shard_map/ppermute | solution.py:253
  51.6 17.0 %collective-permute-start.12 = (s16[3,400,128]{2,1,0:T(8,128)(2,1)S(1)}, s16[3,400,128]{2,1,0:T(8,128)(2,1)S(1)}, u32[]{:S(2)}, u32[]{:S(2)}) collective-permute-start(s16[3,400,128]{2,1,0:T(8,128)(2,1)S(1)} %get-tuple-element.98), channel_id=1, source_target_pairs={{0,8},{4,12},{8,0},{12,4},{16,24},{20,28},{24,16},{28,20},{1,9},{5... | collective-permute-start | bytes 921608 | tf_op jit(solution)/shard_map/ppermute | solution.py:253
  52.2 16.4 %collective-permute-start.13 = (s16[3,400,128]{2,1,0:T(8,128)(2,1)S(1)}, s16[3,400,128]{2,1,0:T(8,128)(2,1)S(1)}, u32[]{:S(2)}, u32[]{:S(2)}) collective-permute-start(s16[3,400,128]{2,1,0:T(8,128)(2,1)S(1)} %get-tuple-element.99), channel_id=1, source_target_pairs={{0,16},{4,20},{8,24},{12,28},{16,0},{20,4},{24,8},{28,12},{1,17},{... | collective-permute-start | bytes 921608 | tf_op jit(solution)/shard_map/ppermute | solution.py:253
  54.0 14.6 %collective-permute-start.14 = (s16[3,400,128]{2,1,0:T(8,128)(2,1)S(1)}, s16[3,400,128]{2,1,0:T(8,128)(2,1)S(1)}, u32[]{:S(2)}, u32[]{:S(2)}) collective-permute-start(s16[3,400,128]{2,1,0:T(8,128)(2,1)S(1)} %get-tuple-element.100), channel_id=1, source_target_pairs={{0,24},{4,28},{8,16},{12,20},{16,8},{20,12},{24,0},{28,4},{1,25},{... | collective-permute-start | bytes 921608 | tf_op jit(solution)/shard_map/ppermute | solution.py:253
  55.8 8.7 %collective-permute-start.16 = (s16[2,304,128]{2,1,0:T(8,128)(2,1)S(1)}, s16[2,304,128]{2,1,0:T(8,128)(2,1)S(1)}, u32[]{:S(2)}, u32[]{:S(2)}) collective-permute-start(s16[2,304,128]{2,1,0:T(8,128)(2,1)S(1)} %pad_add_fusion), channel_id=1, source_target_pairs={{0,16},{4,20},{8,24},{12,28},{16,0},{20,4},{24,8},{28,12},{1,17},{... | collective-permute-start | bytes 466952 | tf_op jit(solution)/shard_map/ppermute | solution.py:253
  65.6 9.6 %collective-permute-start.20 = (s16[2,304,128]{2,1,0:T(8,128)(2,1)S(1)}, s16[2,304,128]{2,1,0:T(8,128)(2,1)S(1)}, u32[]{:S(2)}, u32[]{:S(2)}) collective-permute-start(s16[2,304,128]{2,1,0:T(8,128)(2,1)S(1)} %get-tuple-element.116), channel_id=1, source_target_pairs={{0,1},{1,0},{2,3},{3,2},{4,5},{5,4},{6,7},{7,6},{8,9},{9,8},{10,11... | collective-permute-start | bytes 466952 | tf_op jit(solution)/shard_map/ppermute | solution.py:484
  75.2 16.7 %collective-permute-start.21 = (s16[2,3,400,128]{3,2,1,0:T(8,128)(2,1)S(1)}, s16[2,3,400,128]{3,2,1,0:T(8,128)(2,1)S(1)}, u32[]{:S(2)}, u32[]{:S(2)}) collective-permute-start(s16[2,3,400,128]{3,2,1,0:T(8,128)(2,1)S(1)} %get-tuple-element.117), channel_id=1, source_target_pairs={{0,1},{1,0},{2,3},{3,2},{4,5},{5,4},{6,7},{7,6},{8,9},{9,8},{10,11... | collective-permute-start | bytes 1843208 | tf_op jit(solution)/shard_map/ppermute | solution.py:484
  75.6 7.3 %collective-permute-start.17 = (s16[3,400,128]{2,1,0:T(8,128)(2,1)S(1)}, s16[3,400,128]{2,1,0:T(8,128)(2,1)S(1)}, u32[]{:S(2)}, u32[]{:S(2)}) collective-permute-start(s16[3,400,128]{2,1,0:T(8,128)(2,1)S(1)} %get-tuple-element.104), channel_id=1, source_target_pairs={{0,8},{4,12},{8,0},{12,4},{16,24},{20,28},{24,16},{28,20},{1,9},{5... | collective-permute-start | bytes 921608 | tf_op jit(solution)/shard_map/ppermute | solution.py:253
  77.1 10.1 %collective-permute-start.18 = (s16[3,400,128]{2,1,0:T(8,128)(2,1)S(1)}, s16[3,400,128]{2,1,0:T(8,128)(2,1)S(1)}, u32[]{:S(2)}, u32[]{:S(2)}) collective-permute-start(s16[3,400,128]{2,1,0:T(8,128)(2,1)S(1)} %get-tuple-element.105), channel_id=1, source_target_pairs={{0,16},{4,20},{8,24},{12,28},{16,0},{20,4},{24,8},{28,12},{1,17},{... | collective-permute-start | bytes 921608 | tf_op jit(solution)/shard_map/ppermute | solution.py:253
  78.7 8.5 %collective-permute-start.19 = (s16[3,400,128]{2,1,0:T(8,128)(2,1)S(1)}, s16[3,400,128]{2,1,0:T(8,128)(2,1)S(1)}, u32[]{:S(2)}, u32[]{:S(2)}) collective-permute-start(s16[3,400,128]{2,1,0:T(8,128)(2,1)S(1)} %get-tuple-element.106), channel_id=1, source_target_pairs={{0,24},{4,28},{8,16},{12,20},{16,8},{20,12},{24,0},{28,4},{1,25},{... | collective-permute-start | bytes 921608 | tf_op jit(solution)/shard_map/ppermute | solution.py:253
  79.1 12.8 %collective-permute-start.22 = (s16[2,304,128]{2,1,0:T(8,128)(2,1)S(1)}, s16[2,304,128]{2,1,0:T(8,128)(2,1)S(1)}, u32[]{:S(2)}, u32[]{:S(2)}) collective-permute-start(s16[2,304,128]{2,1,0:T(8,128)(2,1)S(1)} %pad_add_fusion.1), channel_id=1, source_target_pairs={{0,2},{1,3},{2,0},{3,1},{4,6},{5,7},{6,4},{7,5},{8,10},{9,11},{10,... | collective-permute-start | bytes 466952 | tf_op jit(solution)/shard_map/ppermute | solution.py:484
  91.9 12.0 %collective-permute-start.24 = (s16[1,3,400,128]{3,2,1,0:T(8,128)(2,1)S(1)}, s16[1,3,400,128]{3,2,1,0:T(8,128)(2,1)S(1)}, u32[]{:S(2)}, u32[]{:S(2)}) collective-permute-start(s16[1,3,400,128]{3,2,1,0:T(8,128)(2,1)S(1)} %get-tuple-element.120), channel_id=1, source_target_pairs={{0,1},{1,0},{2,3},{3,2},{4,5},{5,4},{6,7},{7,6},{8,9},{9,8},{10,11... | collective-permute-start | bytes 921608 | tf_op jit(solution)/shard_map/ppermute | solution.py:484
  93.9 16.5 %collective-permute-start.26 = (s16[1,3,400,128]{3,2,1,0:T(8,128)(2,1)S(1)}, s16[1,3,400,128]{3,2,1,0:T(8,128)(2,1)S(1)}, u32[]{:S(2)}, u32[]{:S(2)}) collective-permute-start(s16[1,3,400,128]{3,2,1,0:T(8,128)(2,1)S(1)} %get-tuple-element.127), channel_id=1, source_target_pairs={{0,2},{1,3},{2,0},{3,1},{4,6},{5,7},{6,4},{7,5},{8,10},{9,11},{10,... | collective-permute-start | bytes 921608 | tf_op jit(solution)/shard_map/ppermute | solution.py:484
  96.0 15.7 %collective-permute-start.23 = (s16[1,3,400,128]{3,2,1,0:T(8,128)(2,1)S(1)}, s16[1,3,400,128]{3,2,1,0:T(8,128)(2,1)S(1)}, u32[]{:S(2)}, u32[]{:S(2)}) collective-permute-start(s16[1,3,400,128]{3,2,1,0:T(8,128)(2,1)S(1)} %get-tuple-element.119), channel_id=1, source_target_pairs={{0,1},{1,0},{2,3},{3,2},{4,5},{5,4},{6,7},{7,6},{8,9},{9,8},{10,11... | collective-permute-start | bytes 921608 | tf_op jit(solution)/shard_map/ppermute | solution.py:484
  104.1 12.8 %collective-permute-start.25 = (s16[1,3,400,128]{3,2,1,0:T(8,128)(2,1)S(1)}, s16[1,3,400,128]{3,2,1,0:T(8,128)(2,1)S(1)}, u32[]{:S(2)}, u32[]{:S(2)}) collective-permute-start(s16[1,3,400,128]{3,2,1,0:T(8,128)(2,1)S(1)} %get-tuple-element.126), channel_id=1, source_target_pairs={{0,2},{1,3},{2,0},{3,1},{4,6},{5,7},{6,4},{7,5},{8,10},{9,11},{10,... | collective-permute-start | bytes 921608 | tf_op jit(solution)/shard_map/ppermute | solution.py:484

commit v16 on v15

--- a/solution.py
+++ b/solution.py
@@ -515,12 +515,13 @@
         parts, *away = yield early_ladder(rows_of(r))
         away = [across(x, 1) for x in reversed(away)][::-1]
         got, places = yield from halved(parts, away)
+        if turns:
+            got, _ = lax.optimization_barrier((got, turns[-1]))
         mine, *sums = yield early_sum(places, parts, got)
         arrived = by_steps(to_chip, *sums)
         steps.extend(arrived)
         own, *blocks = yield early_antisym([mine, *arrived])
         blocks = by_steps(across, *blocks)
-        firsts.append(blocks[:1])
         seconds.extend(blocks[1:])
         yield None
         yield finish(r, own, blocks, None, update)
@@ -531,6 +532,7 @@
             sums, _ = lax.optimization_barrier((sums, turns[-1] + steps + results[-1][:1]))
         arrived = [to_chip(sums[d], d) for d in range(1, chips)]
         turns.append(arrived)
+        yield None
         parcels = slabs // 2 if r == chunks - 1 else 1
         parts, *away = yield antisym(parcels, [sums[0], *arrived])
         if firsts and (early or parcels > 1):
@@ -545,12 +547,15 @@
     def when(stage):
         r, k = stage
         if early and r == 0:
-            return (20, *[41] * hops, 44, 58, 59, 83)[k]
+            return (20, *[41] * hops, 48, 62, 63, 83)[k]
         if k == 0:
             return 37 + 5 * r if early else 30 + 5 * r
-        return 15 * r + (45 if early else 54) + (k - 1) * 17 - (1 if k == 2 + hops else 0)
-
-    order = [(r, k) for r in range(chunks) for k in range(3 + hops + 2 * (early and r == 0))]
+        if k == 1:
+            return (47.5 if r == 1 else 64) if early else 53 + r / chunks
+        start = 15 * r + (45 if early else 54)
+        return start + (k - 2) * (14 if early and r == 1 else 17) - (1 if k == 3 + hops else 0)
+
+    order = [(r, k) for r in range(chunks) for k in range(4 + hops + (early and r == 0))]
     order = sorted(order, key=when)
 
     turns, firsts, seconds, steps = [], [], [], []

time: 119 us -> 119 us (level)
  starting transfers between devices: 41.7 us -> 36.2 us
  waiting for transfers between devices: 36.7 us -> 41.2 us
    ppermute x16, waiting for transfers between devices: 16 us -> 26.8 us  [to_chip(): return lax.ppermute(x, 'pair', [(i, i ^ d * CORES) for i in range(devices)])]
    ppermute x10, waiting for transfers between devices: 20.7 us -> 14.4 us  [across(): return lax.ppermute(x, 'slab', [(i, i ^ level) for i in range(slabs)])]
    ppermute x10, starting transfers between devices: 20.6 us -> 15.7 us  [across(): return lax.ppermute(x, 'slab', [(i, i ^ level) for i in range(slabs)])]
where the time goes in v16:
time: 119 us; the launch traced here: 117 us
  waiting for transfers between devices  41.2 us (35%)
  Pallas kernels  36.7 us (31%)
  starting transfers between devices  36.2 us (30%)
  local copies, waits for them, and re-layouts  2.52 us (2%)
    pallas_call x13, Pallas kernels, call(): pl.pallas_call(kernel, in_specs=[*in_specs, vmem], out_specs=[*out_specs,...  28.7 us
    ppermute x16, waiting for transfers between devices, to_chip(): return lax.ppermute(x, 'pair', [(i, i ^ d * CORES) for i in range(devices)])  26.8 us
    ppermute x16, starting transfers between devices, to_chip(): return lax.ppermute(x, 'pair', [(i, i ^ d * CORES) for i in range(devices)])  20 us
    ppermute x10, starting transfers between devices, across(): return lax.ppermute(x, 'slab', [(i, i ^ level) for i in range(slabs)])  15.7 us
    ppermute x10, waiting for transfers between devices, across(): return lax.ppermute(x, 'slab', [(i, i ^ level) for i in range(slabs)])  14.4 us
    pallas_call x1, Pallas kernels, on_device(): own_t = transpose(in_hbm(ready))  4 us
    pallas_call x1, Pallas kernels, on_device(): sib_t = transpose(swapped)  4 us
  transfers between devices with their start and end apart: 27, of which 14 were waited for; matrix products, arithmetic and copies ran while one was open for 3% of the time, Pallas kernels for 30%

profile of v16, /device:TPU:0, one launch (start us, length us, event | category | flops | bytes accessed | tf_op | source)
XLA Modules:
  0.0 117.5 jit_solution(15191272565482888670)
XLA Ops:
  0.0 0.5 collective-permute-start.4
  0.5 1.0 slice.33.refs_3_
  1.5 2.6 %collective-permute-start.1 = (bf16[64,2304]{1,0:T(8,128)(2,1)S(1)}, bf16[64,2304]{1,0:T(8,128)(2,1)S(1)}, u32[]{:S(2)}, u32[]{:S(2)}) collective-permute-start(bf16[64,2304]{1,0:T(8,128)(2,1)S(1)} %slice.33.refs_3_), channel_id=1, source_target_pairs={{0,16},{4,20},{8,24},{12,28},{16,0},{20,4},{24,8},{28,12},{1,17},{... | collective-permute-start | bytes 884744 | tf_op jit(solution)/shard_map/ppermute | solution.py:253
  4.1 1.5 %collective-permute-start = (bf16[64,2304]{1,0:T(8,128)(2,1)S(1)}, bf16[64,2304]{1,0:T(8,128)(2,1)S(1)}, u32[]{:S(2)}, u32[]{:S(2)}) collective-permute-start(bf16[64,2304]{1,0:T(8,128)(2,1)S(1)} %slice.33.refs_3_), channel_id=1, source_target_pairs={{0,8},{4,12},{8,0},{12,4},{16,24},{20,28},{24,16},{28,20},{1,9},{5... | collective-permute-start | bytes 884744 | tf_op jit(solution)/shard_map/ppermute | solution.py:253
  5.6 1.1 slice.32.refs_2_
  7.6 4.0 %transpose.14.refs_1_.refs_0_ = bf16[1152,2304]{1,0:T(8,128)(2,1)S(1)} custom-call(bf16[2304,1152]{1,0:T(8,128)(2,1)} %in_ref), custom_call_target="tpu_custom_call" | custom-call | bytes 10616832 | tf_op jit(solution)/shard_map/transpose/pallas_call | solution.py:447
  11.8 1.5 %collective-permute-done.refs_4_ = bf16[64,2304]{1,0:T(8,128)(2,1)S(1)} collective-permute-done((bf16[64,2304]{1,0:T(8,128)(2,1)S(1)}, bf16[64,2304]{1,0:T(8,128)(2,1)S(1)}, u32[]{:S(2)}, u32[]{:S(2)}) %collective-permute-start) | collective-permute-done | bytes 294944 | tf_op jit(solution)/shard_map/ppermute | solution.py:253
  13.3 1.6 %collective-permute-start.2 = (bf16[32,2304]{1,0:T(8,128)(2,1)S(1)}, bf16[32,2304]{1,0:T(8,128)(2,1)S(1)}, u32[]{:S(2)}, u32[]{:S(2)}) collective-permute-start(bf16[32,2304]{1,0:T(8,128)(2,1)S(1)} %slice.34), channel_id=1, source_target_pairs={{0,8},{4,12},{8,0},{12,4},{16,24},{20,28},{24,16},{28,20},{1,9},{5... | collective-permute-start | bytes 442376 | tf_op jit(solution)/shard_map/ppermute | solution.py:253
  14.8 0.5 collective-permute-start.3
  15.3 4.0 %transpose.15.refs_2_.refs_1_ = bf16[1152,2304]{1,0:T(8,128)(2,1)S(1)} custom-call(bf16[2304,1152]{1,0:T(8,128)(2,1)} %collective-permute-done.4.in_ref), custom_call_target="tpu_custom_call" | custom-call | bytes 10616832 | tf_op jit(solution)/shard_map/transpose/pallas_call | solution.py:428
  19.4 0.6 collective-permute-done.3.refs_7_
  20.0 1.0 collective-permute-start.6
  20.9 0.5 collective-permute-start.5
  21.5 4.8 %early_ladder.1 = (f32[2,1152,128]{2,1,0:T(8,128)S(1)}, s16[1,4,304,128]{3,2,1,0:T(8,128)(2,1)S(1)}, s16[1,4,304,128]{3,2,1,0:T(8,128)(2,1)S(1)}, f32[8,128]{1,0:T(8,128)S(1)}) custom-call(s32[3]{0:T(128)S(1)} %pad_add_fusion.2.refs_0_, bf16[1152,2304]{1,0:T(8,128)(2,1)S(1)} %transpose.14.refs_1_.refs_0_, bf16[1152,2304]{1,0:T(8,128)(2,1)S(1)} %transpose.15.refs_2_.refs_1_, ...), custom_call_target="tpu_custom_call" | custom-call | flops 2717908992 | bytes 13598732 | tf_op jit(solution)/shard_map/early_ladder/pallas_call | solution.py:293
  26.3 1.7 %collective-permute-start.9 = (s16[1,4,304,128]{3,2,1,0:T(8,128)(2,1)S(1)}, s16[1,4,304,128]{3,2,1,0:T(8,128)(2,1)S(1)}, u32[]{:S(2)}, u32[]{:S(2)}) collective-permute-start(s16[1,4,304,128]{3,2,1,0:T(8,128)(2,1)S(1)} %get-tuple-element.88), channel_id=1, source_target_pairs={{0,1},{1,0},{2,3},{3,2},{4,5},{5,4},{6,7},{7,6},{8,9},{9,8},{10,11... | collective-permute-start | bytes 933896 | tf_op jit(solution)/shard_map/ppermute | solution.py:484
  28.0 5.6 %collective-permute-done.6.refs_4_ = bf16[128,2304]{1,0:T(8,128)(2,1)S(1)} collective-permute-done((bf16[128,2304]{1,0:T(8,128)(2,1)S(1)}, bf16[128,2304]{1,0:T(8,128)(2,1)S(1)}, u32[]{:S(2)}, u32[]{:S(2)}) %collective-permute-start.6) | collective-permute-done | bytes 589856 | tf_op jit(solution)/shard_map/ppermute | solution.py:253
  33.6 0.7 collective-permute-start.8
  34.3 1.4 %collective-permute-done.5.refs_3_ = bf16[128,2304]{1,0:T(8,128)(2,1)S(1)} collective-permute-done((bf16[128,2304]{1,0:T(8,128)(2,1)S(1)}, bf16[128,2304]{1,0:T(8,128)(2,1)S(1)}, u32[]{:S(2)}, u32[]{:S(2)}) %collective-permute-start.5) | collective-permute-done | bytes 589856 | tf_op jit(solution)/shard_map/ppermute | solution.py:253
  35.8 1.6 %collective-permute-start.13 = (s16[1,4,304,128]{3,2,1,0:T(8,128)(2,1)S(1)}, s16[1,4,304,128]{3,2,1,0:T(8,128)(2,1)S(1)}, u32[]{:S(2)}, u32[]{:S(2)}) collective-permute-start(s16[1,4,304,128]{3,2,1,0:T(8,128)(2,1)S(1)} %get-tuple-element.99), channel_id=1, source_target_pairs={{0,1},{1,0},{2,3},{3,2},{4,5},{5,4},{6,7},{7,6},{8,9},{9,8},{10,11... | collective-permute-start | bytes 933896 | tf_op jit(solution)/shard_map/ppermute | solution.py:484
  37.6 2.7 %collective-permute-start.14 = (s16[1,4,304,128]{3,2,1,0:T(8,128)(2,1)S(1)}, s16[1,4,304,128]{3,2,1,0:T(8,128)(2,1)S(1)}, u32[]{:S(2)}, u32[]{:S(2)}) collective-permute-start(s16[1,4,304,128]{3,2,1,0:T(8,128)(2,1)S(1)} %get-tuple-element.100), channel_id=1, source_target_pairs={{0,2},{1,3},{2,0},{3,1},{4,6},{5,7},{6,4},{7,5},{8,10},{9,11},{10,... | collective-permute-start | bytes 933896 | tf_op jit(solution)/shard_map/ppermute | solution.py:484
  40.2 0.8 collective-permute-done.8.refs_5_
  41.1 4.2 %ladder.2 = (s16[3,400,128]{2,1,0:T(8,128)(2,1)S(1)}, s16[3,400,128]{2,1,0:T(8,128)(2,1)S(1)}, s16[3,400,128]{2,1,0:T(8,128)(2,1)S(1)}, s16[3,400,128]{2,1,0:T(8,128)(2,1)S(1)}, f32[8,128]{1,0:T(8,128)S(1)}) custom-call(bf16[1152,2304]{1,0:T(8,128)(2,1)S(1)} %transpose.14.refs_1_.refs_0_, bf16[1152,2304]{1,0:T(8,128)(2,1)S(1)} %transpose.15.refs_2_.refs_1_, ...), custom_call_target="tpu_custom_call" | custom-call | flops 2717908992 | bytes 13910016 | tf_op jit(solution)/shard_map/ladder/pallas_call | solution.py:293
  45.3 0.7 collective-permute-start.10
  46.0 1.1 collective-permute-start.11
  47.0 1.8 %collective-permute-start.12 = (s16[3,400,128]{2,1,0:T(8,128)(2,1)S(1)}, s16[3,400,128]{2,1,0:T(8,128)(2,1)S(1)}, u32[]{:S(2)}, u32[]{:S(2)}) collective-permute-start(s16[3,400,128]{2,1,0:T(8,128)(2,1)S(1)} %get-tuple-element.98), channel_id=1, source_target_pairs={{0,24},{4,28},{8,16},{12,20},{16,8},{20,12},{24,0},{28,4},{1,25},{... | collective-permute-start | bytes 921608 | tf_op jit(solution)/shard_map/ppermute | solution.py:253
  48.9 4.2 %ladder.3 = (s16[3,400,128]{2,1,0:T(8,128)(2,1)S(1)}, s16[3,400,128]{2,1,0:T(8,128)(2,1)S(1)}, s16[3,400,128]{2,1,0:T(8,128)(2,1)S(1)}, s16[3,400,128]{2,1,0:T(8,128)(2,1)S(1)}, f32[8,128]{1,0:T(8,128)S(1)}) custom-call(bf16[1152,2304]{1,0:T(8,128)(2,1)S(1)} %transpose.14.refs_1_.refs_0_, bf16[1152,2304]{1,0:T(8,128)(2,1)S(1)} %transpose.15.refs_2_.refs_1_, ...), custom_call_target="tpu_custom_call" | custom-call | flops 2717908992 | bytes 13910016 | tf_op jit(solution)/shard_map/ladder/pallas_call | solution.py:293
  53.1 2.3 %collective-permute-done.10.refs_2_ = s16[3,400,128]{2,1,0:T(8,128)(2,1)S(1)} collective-permute-done((s16[3,400,128]{2,1,0:T(8,128)(2,1)S(1)}, s16[3,400,128]{2,1,0:T(8,128)(2,1)S(1)}, u32[]{:S(2)}, u32[]{:S(2)}) %collective-permute-start.10) | collective-permute-done | bytes 307232 | tf_op jit(solution)/shard_map/ppermute | solution.py:253
  55.4 3.5 %collective-permute-done.11.refs_3_ = s16[3,400,128]{2,1,0:T(8,128)(2,1)S(1)} collective-permute-done((s16[3,400,128]{2,1,0:T(8,128)(2,1)S(1)}, s16[3,400,128]{2,1,0:T(8,128)(2,1)S(1)}, u32[]{:S(2)}, u32[]{:S(2)}) %collective-permute-start.11) | collective-permute-done | bytes 307232 | tf_op jit(solution)/shard_map/ppermute | solution.py:253
  59.1 1.6 %collective-permute-start.15 = (s16[2,304,128]{2,1,0:T(8,128)(2,1)S(1)}, s16[2,304,128]{2,1,0:T(8,128)(2,1)S(1)}, u32[]{:S(2)}, u32[]{:S(2)}) collective-permute-start(s16[2,304,128]{2,1,0:T(8,128)(2,1)S(1)} %get-tuple-element.104), channel_id=1, source_target_pairs={{0,8},{4,12},{8,0},{12,4},{16,24},{20,28},{24,16},{28,20},{1,9},{5... | collective-permute-start | bytes 466952 | tf_op jit(solution)/shard_map/ppermute | solution.py:253
  60.7 4.7 %antisym.2 = (f32[2,1152,128]{2,1,0:T(8,128)S(1)}, s16[2,3,400,128]{3,2,1,0:T(8,128)(2,1)S(1)}, f32[8,128]{1,0:T(8,128)S(1)}) custom-call(s32[3]{0:T(128)S(1)} %pad_add_fusion.2.refs_0_, s16[3,400,128]{2,1,0:T(8,128)(2,1)S(1)} %get-tuple-element.110.refs_1_, s16[3,400,128]{2,1,0:T(8,128)(2,1)S(1)} %collective-permute-done.10.refs_2_, ...), custom_call_target="tpu_custom_call" | custom-call | flops 9437184 | bytes 3022860 | tf_op jit(solution)/shard_map/antisym/pallas_call | solution.py:293
  65.5 1.7 %collective-permute-start.20 = (s16[2,3,400,128]{3,2,1,0:T(8,128)(2,1)S(1)}, s16[2,3,400,128]{3,2,1,0:T(8,128)(2,1)S(1)}, u32[]{:S(2)}, u32[]{:S(2)}) collective-permute-start(s16[2,3,400,128]{3,2,1,0:T(8,128)(2,1)S(1)} %get-tuple-element.113), channel_id=1, source_target_pairs={{0,1},{1,0},{2,3},{3,2},{4,5},{5,4},{6,7},{7,6},{8,9},{9,8},{10,11... | collective-permute-start | bytes 1843208 | tf_op jit(solution)/shard_map/ppermute | solution.py:484
  67.1 1.7 %collective-permute-start.16 = (s16[2,304,128]{2,1,0:T(8,128)(2,1)S(1)}, s16[2,304,128]{2,1,0:T(8,128)(2,1)S(1)}, u32[]{:S(2)}, u32[]{:S(2)}) collective-permute-start(s16[2,304,128]{2,1,0:T(8,128)(2,1)S(1)} %pad_add_fusion), channel_id=1, source_target_pairs={{0,16},{4,20},{8,24},{12,28},{16,0},{20,4},{24,8},{28,12},{1,17},{... | collective-permute-start | bytes 466952 | tf_op jit(solution)/shard_map/ppermute | solution.py:253
  68.8 7.6 %collective-permute-done.16.refs_3_ = s16[2,304,128]{2,1,0:T(8,128)(2,1)S(1)} collective-permute-done((s16[2,304,128]{2,1,0:T(8,128)(2,1)S(1)}, s16[2,304,128]{2,1,0:T(8,128)(2,1)S(1)}, u32[]{:S(2)}, u32[]{:S(2)}) %collective-permute-start.16) | collective-permute-done | bytes 155680 | tf_op jit(solution)/shard_map/ppermute | solution.py:253
  76.4 1.1 early_antisym.1
  77.6 2.1 %collective-permute-start.17 = (s16[3,400,128]{2,1,0:T(8,128)(2,1)S(1)}, s16[3,400,128]{2,1,0:T(8,128)(2,1)S(1)}, u32[]{:S(2)}, u32[]{:S(2)}) collective-permute-start(s16[3,400,128]{2,1,0:T(8,128)(2,1)S(1)} %get-tuple-element.107), channel_id=1, source_target_pairs={{0,8},{4,12},{8,0},{12,4},{16,24},{20,28},{24,16},{28,20},{1,9},{5... | collective-permute-start | bytes 921608 | tf_op jit(solution)/shard_map/ppermute | solution.py:253
  79.7 2.6 %collective-permute-start.18 = (s16[3,400,128]{2,1,0:T(8,128)(2,1)S(1)}, s16[3,400,128]{2,1,0:T(8,128)(2,1)S(1)}, u32[]{:S(2)}, u32[]{:S(2)}) collective-permute-start(s16[3,400,128]{2,1,0:T(8,128)(2,1)S(1)} %get-tuple-element.108), channel_id=1, source_target_pairs={{0,16},{4,20},{8,24},{12,28},{16,0},{20,4},{24,8},{28,12},{1,17},{... | collective-permute-start | bytes 921608 | tf_op jit(solution)/shard_map/ppermute | solution.py:253
  82.3 1.1 collective-permute-done.21.refs_3_
  83.5 3.2 %collective-permute-start.22 = (s16[2,304,128]{2,1,0:T(8,128)(2,1)S(1)}, s16[2,304,128]{2,1,0:T(8,128)(2,1)S(1)}, u32[]{:S(2)}, u32[]{:S(2)}) collective-permute-start(s16[2,304,128]{2,1,0:T(8,128)(2,1)S(1)} %pad_add_fusion.1), channel_id=1, source_target_pairs={{0,2},{1,3},{2,0},{3,1},{4,6},{5,7},{6,4},{7,5},{8,10},{9,11},{10,... | collective-permute-start | bytes 466952 | tf_op jit(solution)/shard_map/ppermute | solution.py:484
  87.0 3.5 %collective-permute-done.18.refs_3_ = s16[3,400,128]{2,1,0:T(8,128)(2,1)S(1)} collective-permute-done((s16[3,400,128]{2,1,0:T(8,128)(2,1)S(1)}, s16[3,400,128]{2,1,0:T(8,128)(2,1)S(1)}, u32[]{:S(2)}, u32[]{:S(2)}) %collective-permute-start.18) | collective-permute-done | bytes 307232 | tf_op jit(solution)/shard_map/ppermute | solution.py:253
  90.4 4.7 %antisym.3 = (f32[2,1152,128]{2,1,0:T(8,128)S(1)}, s16[1,3,400,128]{3,2,1,0:T(8,128)(2,1)S(1)}, s16[1,3,400,128]{3,2,1,0:T(8,128)(2,1)S(1)}, f32[8,128]{1,0:T(8,128)S(1)}) custom-call(s32[3]{0:T(128)S(1)} %pad_add_fusion.2.refs_0_, s16[3,400,128]{2,1,0:T(8,128)(2,1)S(1)} %get-tuple-element.106.refs_1_, ...), custom_call_target="tpu_custom_call" | custom-call | flops 9437184 | bytes 3022860 | tf_op jit(solution)/shard_map/antisym/pallas_call | solution.py:293
  95.2 1.5 %collective-permute-start.24 = (s16[1,3,400,128]{3,2,1,0:T(8,128)(2,1)S(1)}, s16[1,3,400,128]{3,2,1,0:T(8,128)(2,1)S(1)}, u32[]{:S(2)}, u32[]{:S(2)}) collective-permute-start(s16[1,3,400,128]{3,2,1,0:T(8,128)(2,1)S(1)} %get-tuple-element.124), channel_id=1, source_target_pairs={{0,1},{1,0},{2,3},{3,2},{4,5},{5,4},{6,7},{7,6},{8,9},{9,8},{10,11... | collective-permute-start | bytes 921608 | tf_op jit(solution)/shard_map/ppermute | solution.py:484
  96.7 0.6 collective-permute-start.23
  97.3 1.4 %finish.3 = (f32[192,2304]{1,0:T(8,128)}, f32[8,128]{1,0:T(8,128)S(1)}) custom-call(f32[3,1,128]{2,1,0:T(1,128)S(1)} %pad_maximum_fusion.refs_0_, f32[1152,2]{1,0:T(8,128)S(1)} %bitcast.10, f32[288,128]{1,0:T(8,128)S(1)} %get-tuple-element.126.refs_2_, s16[2,304,128]{2,1,0:T(8,128)(2,1)S(1)} %collective-permute-done.21.refs_3_, ...), custom_call_target="tpu_custom_call" | custom-call | flops 2359296 | bytes 2238976 | tf_op jit(solution)/shard_map/finish/pallas_call | solution.py:293
  98.7 1.4 %finish.4 = (f32[192,2304]{1,0:T(8,128)}, f32[8,128]{1,0:T(8,128)S(1)}) custom-call(f32[3,1,128]{2,1,0:T(1,128)S(1)} %pad_maximum_fusion.refs_0_, f32[1152,2]{1,0:T(8,128)S(1)} %bitcast.11, f32[2,1152,128]{2,1,0:T(8,128)S(1)} %get-tuple-element.112.refs_0_.refs_2_, ...), custom_call_target="tpu_custom_call", output_to_operand_aliasing={{0}: (5, {})} | custom-call | flops 2359296 | bytes 5650944 | tf_op jit(solution)/shard_map/finish/pallas_call | solution.py:293
  100.1 4.7 %collective-permute-done.24.refs_1_ = s16[1,3,400,128]{3,2,1,0:T(8,128)(2,1)S(1)} collective-permute-done((s16[1,3,400,128]{3,2,1,0:T(8,128)(2,1)S(1)}, s16[1,3,400,128]{3,2,1,0:T(8,128)(2,1)S(1)}, u32[]{:S(2)}, u32[]{:S(2)}) %collective-permute-start.24) | collective-permute-done | bytes 307232 | tf_op jit(solution)/shard_map/ppermute | solution.py:484
  105.0 2.6 %collective-permute-start.26 = (s16[1,3,400,128]{3,2,1,0:T(8,128)(2,1)S(1)}, s16[1,3,400,128]{3,2,1,0:T(8,128)(2,1)S(1)}, u32[]{:S(2)}, u32[]{:S(2)}) collective-permute-start(s16[1,3,400,128]{3,2,1,0:T(8,128)(2,1)S(1)} %get-tuple-element.131), channel_id=1, source_target_pairs={{0,2},{1,3},{2,0},{3,1},{4,6},{5,7},{6,4},{7,5},{8,10},{9,11},{10,... | collective-permute-start | bytes 921608 | tf_op jit(solution)/shard_map/ppermute | solution.py:484
  108.1 8.0 %collective-permute-done.26.refs_4_ = s16[1,3,400,128]{3,2,1,0:T(8,128)(2,1)S(1)} collective-permute-done((s16[1,3,400,128]{3,2,1,0:T(8,128)(2,1)S(1)}, s16[1,3,400,128]{3,2,1,0:T(8,128)(2,1)S(1)}, u32[]{:S(2)}, u32[]{:S(2)}) %collective-permute-start.26) | collective-permute-done | bytes 307232 | tf_op jit(solution)/shard_map/ppermute | solution.py:484
  116.1 1.4 %finish.5 = (f32[192,2304]{1,0:T(8,128)}, f32[8,128]{1,0:T(8,128)}) custom-call(f32[3,1,128]{2,1,0:T(1,128)S(1)} %pad_maximum_fusion.refs_0_, f32[1152,2]{1,0:T(8,128)S(1)} %bitcast.12, f32[2,1152,128]{2,1,0:T(8,128)S(1)} %get-tuple-element.118.refs_0_.refs_2_, ...), custom_call_target="tpu_custom_call", output_to_operand_aliasing={{0}: (5, {})} | custom-call | flops 2359296 | bytes 5343744 | tf_op jit(solution)/shard_map/finish/pallas_call | solution.py:293
  (50 shorter events, 2.7 us)
Async XLA Ops:
  0.0 6.7 %copy-start.1 = (s32[192,2]{0,1:T(2,128)S(1)}, s32[192,2]{0,1:T(2,128)}, u32[]{:S(2)}) copy-start(s32[192,2]{0,1:T(2,128)} %param.7) | copy-start | bytes 4612
  0.0 6.7 %copy-start.2 = (f32[160]{0:T(256)S(1)}, f32[160]{0:T(256)}, u32[]{:S(2)}) copy-start(f32[160]{0:T(256)} %param.8) | copy-start | bytes 1924
  0.0 7.0 %copy-start = (f32[96]{0:T(128)S(1)}, f32[96]{0:T(128)}, u32[]{:S(2)}) copy-start(f32[96]{0:T(128)} %param.9) | copy-start | bytes 1156
  0.0 15.3 %collective-permute-start.4 = (bf16[2304,1152]{1,0:T(8,128)(2,1)}, bf16[2304,1152]{1,0:T(8,128)(2,1)}, u32[]{:S(2)}, u32[]{:S(2)}) collective-permute-start(bf16[2304,1152]{1,0:T(8,128)(2,1)} %in_ref), channel_id=1, source_target_pairs={{0,4},{4,0},{8,12},{12,8},{16,20},{20,16},{24,28},{28,24},{1,5},{5... | collective-permute-start | bytes 15925256 | tf_op jit(solution)/shard_map/ppermute | solution.py:427
  1.5 10.3 %collective-permute-start.1 = (bf16[64,2304]{1,0:T(8,128)(2,1)S(1)}, bf16[64,2304]{1,0:T(8,128)(2,1)S(1)}, u32[]{:S(2)}, u32[]{:S(2)}) collective-permute-start(bf16[64,2304]{1,0:T(8,128)(2,1)S(1)} %slice.33.refs_3_), channel_id=1, source_target_pairs={{0,16},{4,20},{8,24},{12,28},{16,0},{20,4},{24,8},{28,12},{1,17},{... | collective-permute-start | bytes 884744 | tf_op jit(solution)/shard_map/ppermute | solution.py:253
  4.1 9.1 %collective-permute-start = (bf16[64,2304]{1,0:T(8,128)(2,1)S(1)}, bf16[64,2304]{1,0:T(8,128)(2,1)S(1)}, u32[]{:S(2)}, u32[]{:S(2)}) collective-permute-start(bf16[64,2304]{1,0:T(8,128)(2,1)S(1)} %slice.33.refs_3_), channel_id=1, source_target_pairs={{0,8},{4,12},{8,0},{12,4},{16,24},{20,28},{24,16},{28,20},{1,9},{5... | collective-permute-start | bytes 884744 | tf_op jit(solution)/shard_map/ppermute | solution.py:253
  13.3 6.1 %collective-permute-start.2 = (bf16[32,2304]{1,0:T(8,128)(2,1)S(1)}, bf16[32,2304]{1,0:T(8,128)(2,1)S(1)}, u32[]{:S(2)}, u32[]{:S(2)}) collective-permute-start(bf16[32,2304]{1,0:T(8,128)(2,1)S(1)} %slice.34), channel_id=1, source_target_pairs={{0,8},{4,12},{8,0},{12,4},{16,24},{20,28},{24,16},{28,20},{1,9},{5... | collective-permute-start | bytes 442376 | tf_op jit(solution)/shard_map/ppermute | solution.py:253
  14.8 5.1 %collective-permute-start.3 = (bf16[32,2304]{1,0:T(8,128)(2,1)S(1)}, bf16[32,2304]{1,0:T(8,128)(2,1)S(1)}, u32[]{:S(2)}, u32[]{:S(2)}) collective-permute-start(bf16[32,2304]{1,0:T(8,128)(2,1)S(1)} %slice.35), channel_id=1, source_target_pairs={{0,16},{4,20},{8,24},{12,28},{16,0},{20,4},{24,8},{28,12},{1,17},{... | collective-permute-start | bytes 442376 | tf_op jit(solution)/shard_map/ppermute | solution.py:253
  20.0 13.6 %collective-permute-start.6 = (bf16[128,2304]{1,0:T(8,128)(2,1)S(1)}, bf16[128,2304]{1,0:T(8,128)(2,1)S(1)}, u32[]{:S(2)}, u32[]{:S(2)}) collective-permute-start(bf16[128,2304]{1,0:T(8,128)(2,1)S(1)} %slice.32.refs_2_), channel_id=1, source_target_pairs={{0,16},{4,20},{8,24},{12,28},{16,0},{20,4},{24,8},{28,12},{1,17},{... | collective-permute-start | bytes 1769480 | tf_op jit(solution)/shard_map/ppermute | solution.py:253
  20.9 14.7 %collective-permute-start.5 = (bf16[128,2304]{1,0:T(8,128)(2,1)S(1)}, bf16[128,2304]{1,0:T(8,128)(2,1)S(1)}, u32[]{:S(2)}, u32[]{:S(2)}) collective-permute-start(bf16[128,2304]{1,0:T(8,128)(2,1)S(1)} %slice.32.refs_2_), channel_id=1, source_target_pairs={{0,8},{4,12},{8,0},{12,4},{16,24},{20,28},{24,16},{28,20},{1,9},{5... | collective-permute-start | bytes 1769480 | tf_op jit(solution)/shard_map/ppermute | solution.py:253
  26.3 11.1 %collective-permute-start.9 = (s16[1,4,304,128]{3,2,1,0:T(8,128)(2,1)S(1)}, s16[1,4,304,128]{3,2,1,0:T(8,128)(2,1)S(1)}, u32[]{:S(2)}, u32[]{:S(2)}) collective-permute-start(s16[1,4,304,128]{3,2,1,0:T(8,128)(2,1)S(1)} %get-tuple-element.88), channel_id=1, source_target_pairs={{0,1},{1,0},{2,3},{3,2},{4,5},{5,4},{6,7},{7,6},{8,9},{9,8},{10,11... | collective-permute-start | bytes 933896 | tf_op jit(solution)/shard_map/ppermute | solution.py:484
  33.6 7.4 %collective-permute-start.8 = (bf16[64,2304]{1,0:T(8,128)(2,1)S(1)}, bf16[64,2304]{1,0:T(8,128)(2,1)S(1)}, u32[]{:S(2)}, u32[]{:S(2)}) collective-permute-start(bf16[64,2304]{1,0:T(8,128)(2,1)S(1)} %slice.41), channel_id=1, source_target_pairs={{0,8},{4,12},{8,0},{12,4},{16,24},{20,28},{24,16},{28,20},{1,9},{5... | collective-permute-start | bytes 884744 | tf_op jit(solution)/shard_map/ppermute | solution.py:253
  35.7 11.4 %collective-permute-start.7 = (bf16[64,2304]{1,0:T(8,128)(2,1)S(1)}, bf16[64,2304]{1,0:T(8,128)(2,1)S(1)}, u32[]{:S(2)}, u32[]{:S(2)}) collective-permute-start(bf16[64,2304]{1,0:T(8,128)(2,1)S(1)} %slice.40), channel_id=1, source_target_pairs={{0,16},{4,20},{8,24},{12,28},{16,0},{20,4},{24,8},{28,12},{1,17},{... | collective-permute-start | bytes 884744 | tf_op jit(solution)/shard_map/ppermute | solution.py:253
  35.8 17.3 %collective-permute-start.13 = (s16[1,4,304,128]{3,2,1,0:T(8,128)(2,1)S(1)}, s16[1,4,304,128]{3,2,1,0:T(8,128)(2,1)S(1)}, u32[]{:S(2)}, u32[]{:S(2)}) collective-permute-start(s16[1,4,304,128]{3,2,1,0:T(8,128)(2,1)S(1)} %get-tuple-element.99), channel_id=1, source_target_pairs={{0,1},{1,0},{2,3},{3,2},{4,5},{5,4},{6,7},{7,6},{8,9},{9,8},{10,11... | collective-permute-start | bytes 933896 | tf_op jit(solution)/shard_map/ppermute | solution.py:484
  37.6 15.5 %collective-permute-start.14 = (s16[1,4,304,128]{3,2,1,0:T(8,128)(2,1)S(1)}, s16[1,4,304,128]{3,2,1,0:T(8,128)(2,1)S(1)}, u32[]{:S(2)}, u32[]{:S(2)}) collective-permute-start(s16[1,4,304,128]{3,2,1,0:T(8,128)(2,1)S(1)} %get-tuple-element.100), channel_id=1, source_target_pairs={{0,2},{1,3},{2,0},{3,1},{4,6},{5,7},{6,4},{7,5},{8,10},{9,11},{10,... | collective-permute-start | bytes 933896 | tf_op jit(solution)/shard_map/ppermute | solution.py:484
  45.3 10.1 %collective-permute-start.10 = (s16[3,400,128]{2,1,0:T(8,128)(2,1)S(1)}, s16[3,400,128]{2,1,0:T(8,128)(2,1)S(1)}, u32[]{:S(2)}, u32[]{:S(2)}) collective-permute-start(s16[3,400,128]{2,1,0:T(8,128)(2,1)S(1)} %get-tuple-element.96), channel_id=1, source_target_pairs={{0,8},{4,12},{8,0},{12,4},{16,24},{20,28},{24,16},{28,20},{1,9},{5... | collective-permute-start | bytes 921608 | tf_op jit(solution)/shard_map/ppermute | solution.py:253
  46.0 12.9 %collective-permute-start.11 = (s16[3,400,128]{2,1,0:T(8,128)(2,1)S(1)}, s16[3,400,128]{2,1,0:T(8,128)(2,1)S(1)}, u32[]{:S(2)}, u32[]{:S(2)}) collective-permute-start(s16[3,400,128]{2,1,0:T(8,128)(2,1)S(1)} %get-tuple-element.97), channel_id=1, source_target_pairs={{0,16},{4,20},{8,24},{12,28},{16,0},{20,4},{24,8},{28,12},{1,17},{... | collective-permute-start | bytes 921608 | tf_op jit(solution)/shard_map/ppermute | solution.py:253
  47.0 11.8 %collective-permute-start.12 = (s16[3,400,128]{2,1,0:T(8,128)(2,1)S(1)}, s16[3,400,128]{2,1,0:T(8,128)(2,1)S(1)}, u32[]{:S(2)}, u32[]{:S(2)}) collective-permute-start(s16[3,400,128]{2,1,0:T(8,128)(2,1)S(1)} %get-tuple-element.98), channel_id=1, source_target_pairs={{0,24},{4,28},{8,16},{12,20},{16,8},{20,12},{24,0},{28,4},{1,25},{... | collective-permute-start | bytes 921608 | tf_op jit(solution)/shard_map/ppermute | solution.py:253
  59.1 8.0 %collective-permute-start.15 = (s16[2,304,128]{2,1,0:T(8,128)(2,1)S(1)}, s16[2,304,128]{2,1,0:T(8,128)(2,1)S(1)}, u32[]{:S(2)}, u32[]{:S(2)}) collective-permute-start(s16[2,304,128]{2,1,0:T(8,128)(2,1)S(1)} %get-tuple-element.104), channel_id=1, source_target_pairs={{0,8},{4,12},{8,0},{12,4},{16,24},{20,28},{24,16},{28,20},{1,9},{5... | collective-permute-start | bytes 466952 | tf_op jit(solution)/shard_map/ppermute | solution.py:253
  65.5 21.2 %collective-permute-start.20 = (s16[2,3,400,128]{3,2,1,0:T(8,128)(2,1)S(1)}, s16[2,3,400,128]{3,2,1,0:T(8,128)(2,1)S(1)}, u32[]{:S(2)}, u32[]{:S(2)}) collective-permute-start(s16[2,3,400,128]{3,2,1,0:T(8,128)(2,1)S(1)} %get-tuple-element.113), channel_id=1, source_target_pairs={{0,1},{1,0},{2,3},{3,2},{4,5},{5,4},{6,7},{7,6},{8,9},{9,8},{10,11... | collective-permute-start | bytes 1843208 | tf_op jit(solution)/shard_map/ppermute | solution.py:484
  67.1 9.3 %collective-permute-start.16 = (s16[2,304,128]{2,1,0:T(8,128)(2,1)S(1)}, s16[2,304,128]{2,1,0:T(8,128)(2,1)S(1)}, u32[]{:S(2)}, u32[]{:S(2)}) collective-permute-start(s16[2,304,128]{2,1,0:T(8,128)(2,1)S(1)} %pad_add_fusion), channel_id=1, source_target_pairs={{0,16},{4,20},{8,24},{12,28},{16,0},{20,4},{24,8},{28,12},{1,17},{... | collective-permute-start | bytes 466952 | tf_op jit(solution)/shard_map/ppermute | solution.py:253
  77.5 5.9 %collective-permute-start.21 = (s16[2,304,128]{2,1,0:T(8,128)(2,1)S(1)}, s16[2,304,128]{2,1,0:T(8,128)(2,1)S(1)}, u32[]{:S(2)}, u32[]{:S(2)}) collective-permute-start(s16[2,304,128]{2,1,0:T(8,128)(2,1)S(1)} %get-tuple-element.122), channel_id=1, source_target_pairs={{0,1},{1,0},{2,3},{3,2},{4,5},{5,4},{6,7},{7,6},{8,9},{9,8},{10,11... | collective-permute-start | bytes 466952 | tf_op jit(solution)/shard_map/ppermute | solution.py:484
  77.6 9.4 %collective-permute-start.17 = (s16[3,400,128]{2,1,0:T(8,128)(2,1)S(1)}, s16[3,400,128]{2,1,0:T(8,128)(2,1)S(1)}, u32[]{:S(2)}, u32[]{:S(2)}) collective-permute-start(s16[3,400,128]{2,1,0:T(8,128)(2,1)S(1)} %get-tuple-element.107), channel_id=1, source_target_pairs={{0,8},{4,12},{8,0},{12,4},{16,24},{20,28},{24,16},{28,20},{1,9},{5... | collective-permute-start | bytes 921608 | tf_op jit(solution)/shard_map/ppermute | solution.py:253
  79.7 10.7 %collective-permute-start.18 = (s16[3,400,128]{2,1,0:T(8,128)(2,1)S(1)}, s16[3,400,128]{2,1,0:T(8,128)(2,1)S(1)}, u32[]{:S(2)}, u32[]{:S(2)}) collective-permute-start(s16[3,400,128]{2,1,0:T(8,128)(2,1)S(1)} %get-tuple-element.108), channel_id=1, source_target_pairs={{0,16},{4,20},{8,24},{12,28},{16,0},{20,4},{24,8},{28,12},{1,17},{... | collective-permute-start | bytes 921608 | tf_op jit(solution)/shard_map/ppermute | solution.py:253
  82.3 8.1 %collective-permute-start.19 = (s16[3,400,128]{2,1,0:T(8,128)(2,1)S(1)}, s16[3,400,128]{2,1,0:T(8,128)(2,1)S(1)}, u32[]{:S(2)}, u32[]{:S(2)}) collective-permute-start(s16[3,400,128]{2,1,0:T(8,128)(2,1)S(1)} %get-tuple-element.109), channel_id=1, source_target_pairs={{0,24},{4,28},{8,16},{12,20},{16,8},{20,12},{24,0},{28,4},{1,25},{... | collective-permute-start | bytes 921608 | tf_op jit(solution)/shard_map/ppermute | solution.py:253
  83.5 11.7 %collective-permute-start.22 = (s16[2,304,128]{2,1,0:T(8,128)(2,1)S(1)}, s16[2,304,128]{2,1,0:T(8,128)(2,1)S(1)}, u32[]{:S(2)}, u32[]{:S(2)}) collective-permute-start(s16[2,304,128]{2,1,0:T(8,128)(2,1)S(1)} %pad_add_fusion.1), channel_id=1, source_target_pairs={{0,2},{1,3},{2,0},{3,1},{4,6},{5,7},{6,4},{7,5},{8,10},{9,11},{10,... | collective-permute-start | bytes 466952 | tf_op jit(solution)/shard_map/ppermute | solution.py:484
  86.9 11.8 %collective-permute-start.25 = (s16[1,3,400,128]{3,2,1,0:T(8,128)(2,1)S(1)}, s16[1,3,400,128]{3,2,1,0:T(8,128)(2,1)S(1)}, u32[]{:S(2)}, u32[]{:S(2)}) collective-permute-start(s16[1,3,400,128]{3,2,1,0:T(8,128)(2,1)S(1)} %get-tuple-element.125), channel_id=1, source_target_pairs={{0,2},{1,3},{2,0},{3,1},{4,6},{5,7},{6,4},{7,5},{8,10},{9,11},{10,... | collective-permute-start | bytes 921608 | tf_op jit(solution)/shard_map/ppermute | solution.py:484
  95.2 9.6 %collective-permute-start.24 = (s16[1,3,400,128]{3,2,1,0:T(8,128)(2,1)S(1)}, s16[1,3,400,128]{3,2,1,0:T(8,128)(2,1)S(1)}, u32[]{:S(2)}, u32[]{:S(2)}) collective-permute-start(s16[1,3,400,128]{3,2,1,0:T(8,128)(2,1)S(1)} %get-tuple-element.124), channel_id=1, source_target_pairs={{0,1},{1,0},{2,3},{3,2},{4,5},{5,4},{6,7},{7,6},{8,9},{9,8},{10,11... | collective-permute-start | bytes 921608 | tf_op jit(solution)/shard_map/ppermute | solution.py:484
  96.7 11.4 %collective-permute-start.23 = (s16[1,3,400,128]{3,2,1,0:T(8,128)(2,1)S(1)}, s16[1,3,400,128]{3,2,1,0:T(8,128)(2,1)S(1)}, u32[]{:S(2)}, u32[]{:S(2)}) collective-permute-start(s16[1,3,400,128]{3,2,1,0:T(8,128)(2,1)S(1)} %get-tuple-element.123), channel_id=1, source_target_pairs={{0,1},{1,0},{2,3},{3,2},{4,5},{5,4},{6,7},{7,6},{8,9},{9,8},{10,11... | collective-permute-start | bytes 921608 | tf_op jit(solution)/shard_map/ppermute | solution.py:484
  105.0 11.1 %collective-permute-start.26 = (s16[1,3,400,128]{3,2,1,0:T(8,128)(2,1)S(1)}, s16[1,3,400,128]{3,2,1,0:T(8,128)(2,1)S(1)}, u32[]{:S(2)}, u32[]{:S(2)}) collective-permute-start(s16[1,3,400,128]{3,2,1,0:T(8,128)(2,1)S(1)} %get-tuple-element.131), channel_id=1, source_target_pairs={{0,2},{1,3},{2,0},{3,1},{4,6},{5,7},{6,4},{7,5},{8,10},{9,11},{10,... | collective-permute-start | bytes 921608 | tf_op jit(solution)/shard_map/ppermute | solution.py:484
